TPU v7x, 32 devices: a whole 2x2x4 slice. The times are simulated.
32 devices in a mesh: parts: 2 (over y), gz: 16 (over z, x, core).
Axes of the slice: x: 2, y: 2, z: 4, core: 2. Of those that a mesh axis runs over, the one named last changes fastest.
Arguments:
- state: float32 [16, 64, 16, 512], P('parts', 'gz'), parts along dimension 0, may hold values from -6 to 6
- target: float32 [128, 16, 512], P(('parts', 'gz')), parts along dimension 0, may hold values from -6 to 6
- rock_type: int32 [16, 64, 16, 512], P('parts', 'gz'), parts along dimension 0, may hold values from 0 to 7
- log_table: float32 [16, 8], P('parts'), parts along dimension 0, may hold values from -1.5 to 1.5
- obs_scale: float32 [16], P('parts'), parts along dimension 0, may hold values from 0.25 to 1
Outputs:
- adjoint: float32 [16, 64, 16, 512], P('parts', 'gz'), parts along dimension 0
- control_gradient: float32 [1024, 512], P(('parts', 'gz')), parts along dimension 0
- moments: float32 [4], P('parts'), parts along dimension 0
There are 2 independent parts, one for each index of `parts`. A program takes and returns all parts, laid end to end along the dimension named above; each array names one. Nothing has to cross between parts.
All inputs are finite; a program needn't handle non-finite values.
Results may differ from a plain program's by a relative error of at most 0.0003.
Values sent between devices are 32-bit elements; how exact they have to be, the bound alone decides.
No kernel may reach another device: no remote copies, remote signals or barrier semaphores. Data moves between devices by JAX's collectives and lax.ppermute only.
A program may use at most 64 MiB of HBM per device.

v0:
```python
import math

import jax
import jax.numpy as jnp
from jax import lax
from jax.sharding import PartitionSpec as P

NR = 8
DEGREE = 4
SWEEPS = 2
MA = 512
MB = 512

STORAGE = 0.05
BETA_RISK = 0.5
LOWER_EIGEN = 0.05
UPPER_EIGEN = 2.0

HALO = DEGREE * SWEEPS


def harmonic(left_side, right_side):
    summed = left_side + right_side
    guarded = jnp.where(summed > 0, summed, 1.0)
    return jnp.where(summed > 0, 2.0 * left_side * right_side / guarded, 0.0)


def shift_ahead(values, dimension):
    length_dim = values.shape[dimension]
    zero_plane = jnp.zeros_like(lax.slice_in_dim(values, 0, 1, axis=dimension))
    return jnp.concatenate(
        [lax.slice_in_dim(values, 1, length_dim, axis=dimension), zero_plane], axis=dimension
    )


def shift_behind(values, dimension):
    length_dim = values.shape[dimension]
    zero_plane = jnp.zeros_like(lax.slice_in_dim(values, 0, 1, axis=dimension))
    return jnp.concatenate(
        [zero_plane, lax.slice_in_dim(values, 0, length_dim - 1, axis=dimension)], axis=dimension
    )


def face_weights(conduct):
    return tuple(harmonic(conduct, shift_ahead(conduct, dim)) for dim in range(3))


def diagonal_of(weights):
    summed = weights[0] + shift_behind(weights[0], 0)
    summed = summed + (weights[1] + shift_behind(weights[1], 1))
    summed = summed + (weights[2] + shift_behind(weights[2], 2))
    return summed + STORAGE


def apply_operator(values, weights):
    result = STORAGE * values
    for dim in range(3):
        flux_term = weights[dim] * (shift_ahead(values, dim) - values)
        result = result + (shift_behind(flux_term, dim) - flux_term)
    return result


def chebyshev_constants(number_steps):
    centre = (UPPER_EIGEN + LOWER_EIGEN) / 2
    spread = (UPPER_EIGEN - LOWER_EIGEN) / 2
    quotient = centre / spread
    rho_now = 1.0 / quotient
    coefficients = []
    for position in range(number_steps):
        rho_next = 1.0 / (2.0 * quotient - rho_now)
        coefficients.append((rho_next * rho_now, 2.0 * rho_next / spread))
        rho_now = rho_next
    return (centre, coefficients)


def cosine_basis(positions, mode_index, length_total):
    product_index = jnp.remainder(
        (2 * positions[:, None] + 1) * (2 * mode_index[None, :] + 1), 8 * length_total
    )
    angle = product_index.astype(jnp.float32) * (math.pi / (4 * length_total))
    return math.sqrt(2.0 / length_total) * jnp.cos(angle)


def on_device(state, target, rock_type, log_table, obs_scale):
    samples, planes, rows_y, columns = state.shape
    slabs = lax.axis_size("gz")
    teams = slabs // samples
    depth = samples * planes
    groups = [[team * samples + i for i in range(samples)] for team in range(teams)]
    rank = lax.axis_index("gz")
    sample = lax.rem(rank, samples)
    depth_total = planes * slabs
    plane_index = rank * planes + jnp.arange(planes, dtype=jnp.int32)
    depth_weight = 1.0 + 2.0 * plane_index.astype(jnp.float32) / (depth_total - 1)

    def deal(field):
        return lax.all_to_all(
            field, "gz", split_axis=0, concat_axis=0, axis_index_groups=groups, tiled=True
        )

    def widen(field):
        ahead = [(i, i + samples) for i in range(slabs - samples)]
        behind = [(i + samples, i) for i in range(slabs - samples)]
        before = lax.ppermute(field[depth - HALO :], "gz", ahead)
        after = lax.ppermute(field[:HALO], "gz", behind)
        return jnp.concatenate([before, field, after], axis=0)

    codes = deal(rock_type).reshape(depth, rows_y, columns)

    misfit_gap = state - target[None]
    weighted = depth_weight[None, :, None, None] * misfit_gap
    local_sums = jnp.sum(weighted * misfit_gap, axis=(1, 2, 3))
    all_sums = lax.all_gather(local_sums, "gz")
    source = deal(obs_scale[:, None, None, None] * weighted).reshape(depth, rows_y, columns)

    table_row = jnp.exp(lax.dynamic_index_in_dim(log_table, sample, 0, keepdims=False))
    conduct = jnp.zeros(codes.shape, jnp.float32)
    for code_index in range(NR):
        conduct = conduct + jnp.where(codes == code_index, table_row[code_index], 0.0)
    weights = face_weights(widen(conduct))
    diagonal = diagonal_of(weights)
    residual = widen(source)
    iterate = jnp.zeros(residual.shape, jnp.float32)
    centre, coefficients = chebyshev_constants(DEGREE)
    for sweep_index in range(SWEEPS):
        search = residual / diagonal / centre
        for position in range(DEGREE):
            iterate = iterate + search
            residual = residual - apply_operator(search, weights)
            if position + 1 < DEGREE:
                first_mix, second_mix = coefficients[position]
                search = first_mix * search + second_mix * (residual / diagonal)
    own = iterate[HALO : HALO + depth]
    adjoint = deal(own.reshape(samples, planes, rows_y, columns))

    misfit = obs_scale * jnp.sum(all_sums, axis=0) / (2.0 * depth_total * rows_y * columns)
    mean_value = jnp.mean(misfit)
    deviation = misfit - mean_value
    variance = jnp.mean(deviation * deviation)
    risk_weight = 1.0 + 2.0 * BETA_RISK * deviation
    own_face = lax.dynamic_index_in_dim(risk_weight, sample, 0, keepdims=False) * own[:, 0, :]
    faces = lax.all_gather(own_face, "gz")
    face_values = jnp.sum(faces.reshape(teams, samples, depth, columns), axis=1)
    face_values = face_values.reshape(depth_total, columns)
    basis_x = cosine_basis(
        jnp.arange(columns, dtype=jnp.int32), jnp.arange(MB, dtype=jnp.int32), columns
    )
    own_count = MA // slabs
    mode_index = rank * own_count + jnp.arange(own_count, dtype=jnp.int32)
    basis_z = cosine_basis(jnp.arange(depth_total, dtype=jnp.int32), mode_index, depth_total)
    along_z = jnp.dot(basis_z.T, face_values, precision=lax.Precision.HIGHEST)
    gradient = jnp.dot(along_z, basis_x, precision=lax.Precision.HIGHEST)
    moments = jnp.stack([mean_value, variance])
    return (adjoint, gradient, moments)


def solution(mesh):
    return jax.shard_map(
        on_device,
        mesh=mesh,
        in_specs=(
            P("parts", "gz", None, None),
            P(("parts", "gz"), None, None),
            P("parts", "gz", None, None),
            P("parts", None),
            P("parts"),
        ),
        out_specs=(P("parts", "gz", None, None), P(("parts", "gz"), None), P("parts")),
        check_vma=False,
    )
```

profile of v0, /device:TPU:0, one launch (start us, length us, event | category | flops | bytes accessed | tf_op | source)
XLA Modules:
  0.0 232.3 jit_solution(6766836866994161318)
XLA Ops:
  7.2 5.4 %all-to-all-start.1 = ((s32[8,4,16,512]{3,2,1,0:T(8,128)}), s32[8,4,16,512]{3,2,1,0:T(8,128)S(1)}, u32[]{:S(2)}, u32[]{:S(2)}) async-start(s32[8,4,16,512]{3,2,1,0:T(8,128)} %param.7), calls=%async_computation.1 | async-start | bytes 2097152 | tf_op jit(solution)/shard_map/all_to_all | solution.py:97
  12.6 1.3 fusion.4
  13.9 13.1 %all-to-all-done.1 = s32[8,4,16,512]{3,2,1,0:T(8,128)S(1)} async-done(((s32[8,4,16,512]{3,2,1,0:T(8,128)}), s32[8,4,16,512]{3,2,1,0:T(8,128)S(1)}, u32[]{:S(2)}, u32[]{:S(2)}) %all-to-all-start.1) | async-done | bytes 1048608 | tf_op jit(solution)/shard_map/all_to_all | solution.py:97
  27.0 3.6 %all-to-all-start = ((f32[8,4,16,512]{3,2,1,0:T(8,128)}), f32[8,4,16,512]{3,2,1,0:T(8,128)S(1)}, u32[]{:S(2)}, u32[]{:S(2)}) async-start(f32[8,4,16,512]{3,2,1,0:T(8,128)} %get-tuple-element.42), calls=%async_computation | async-start | bytes 2097152 | tf_op jit(solution)/shard_map/all_to_all | solution.py:97
  32.2 37.9 %all-reduce.48 = f32[128]{0:T(128)S(1)} all-reduce(f32[128]{0:T(128)S(1)} %dynamic-update-slice), channel_id=2, replica_groups=mesh['parts'=2,'gz'=16] {'gz'}, use_global_device_ids=true, to_apply=%add.48 | all-reduce | flops 128 | bytes 1024
  70.2 0.6 fusion.49
  71.5 0.7 dynamic-slice_exponential_fusion
  72.2 0.7 fusion.53
  72.9 7.0 %add_add_fusion.2 = f32[8,4,16,512]{3,2,1,0:T(8,128)S(1)} fusion(s32[8,4,16,512]{3,2,1,0:T(8,128)} %copy-done.13, f32[]{:T(128)} %bitcast.10, f32[]{:T(128)} %bitcast.9, f32[]{:T(128)} %bitcast.8, f32[]{:T(128)} %bitcast.7, f32[]{:T(128)} %bitcast.6, f32[]{:T(128)} %bitcast.5, f32[]{:T(128)} %bitcast.4, f32[]{:T(128)} %bitcast.3), kind=kLoop, calls=%fused_computation.60 | loop fusion | flops 6029312 | bytes 2097184 | tf_op jit(solution)/shard_map/add | solution.py:119
  79.9 0.9 fusion.51
  80.8 1.3 collective-permute-start.3
  82.0 5.5 %collective-permute-start.2 = (f32[8,16,512]{2,1,0:T(8,128)}, f32[8,16,512]{2,1,0:T(8,128)S(1)}, u32[]{:S(2)}, u32[]{:S(2)}) collective-permute-start(f32[8,16,512]{2,1,0:T(8,128)} %bitcast.11), channel_id=1, source_target_pairs={{0,8},{1,9},{2,10},{3,11},{4,12},{5,13},{6,14},{7,15},{16,24},{17,... | collective-permute-start | bytes 786440 | tf_op jit(solution)/shard_map/ppermute | solution.py:104
  87.5 0.6 multiply_reduce_fusion
  88.1 0.7 dynamic_slice.9
  88.8 1.3 collective-permute-start.1
  90.1 5.6 %collective-permute-start = (f32[8,16,512]{2,1,0:T(8,128)S(1)}, f32[8,16,512]{2,1,0:T(8,128)S(1)}, u32[]{:S(2)}, u32[]{:S(2)}) collective-permute-start(f32[8,16,512]{2,1,0:T(8,128)S(1)} %bitcast.63), channel_id=1, source_target_pairs={{0,8},{1,9},{2,10},{3,11},{4,12},{5,13},{6,14},{7,15},{16,24},{17,... | collective-permute-start | bytes 786440 | tf_op jit(solution)/shard_map/ppermute | solution.py:104
  95.8 2.0 collective-permute-done.3
  98.9 1.4 compare_select_fusion.4
  100.3 2.6 %collective-permute-done.1 = f32[8,16,512]{2,1,0:T(8,128)S(1)} collective-permute-done((f32[8,16,512]{2,1,0:T(8,128)S(1)}, f32[8,16,512]{2,1,0:T(8,128)S(1)}, u32[]{:S(2)}, u32[]{:S(2)}) %collective-permute-start.1) | collective-permute-done | bytes 262176 | tf_op jit(solution)/shard_map/ppermute | solution.py:105
  103.0 1.5 broadcast_multiply_fusion.1
  105.4 1.5 subtract_multiply_fusion.20
  106.9 1.3 slice.278
  108.2 4.5 %multiply_add_fusion.4 = (f32[48,16,512]{2,1,0:T(8,128)S(1)}, f32[48,16,512]{2,1,0:T(8,128)}) fusion(f32[48,16,512]{2,1,0:T(8,128)S(1)} %get-tuple-element.16, f32[48,16,512]{2,1,0:T(8,128)S(1)} %get-tuple-element.15, f32[48,16,512]{2,1,0:T(8,128)S(1)} %get-tuple-element.36, f32[48,16,511]{2,1,0:T(8,128)S(1)} %bitcast.45, ...), kind=kLoop, calls=%fused_computation.44 | loop fusion | flops 5505024 | bytes 17167360 | tf_op jit(solution)/shard_map/add | solution.py:132
  113.6 1.4 subtract_multiply_fusion.17
  115.1 1.3 copy-done.12
  116.4 2.1 multiply_add_fusion.3
  119.5 1.4 subtract_multiply_fusion.14
  121.0 3.1 %multiply_add_fusion.2 = (f32[48,16,512]{2,1,0:T(8,128)S(1)}, f32[48,16,512]{2,1,0:T(8,128)}) fusion(f32[48,16,512]{2,1,0:T(8,128)S(1)} %get-tuple-element.16, f32[48,16,512]{2,1,0:T(8,128)S(1)} %get-tuple-element.10, f32[48,16,512]{2,1,0:T(8,128)S(1)} %get-tuple-element.11, f32[48,16,512]{2,1,0:T(8,128)S(1)} %get-tuple-element.31, ...), kind=kLoop, calls=%fused_computation.34 | loop fusion | flops 4718592 | bytes 17167360 | tf_op jit(solution)/shard_map/add | solution.py:132
  125.0 3.0 %subtract_multiply_fusion.11 = (f32[48,16,512]{2,1,0:T(8,128)S(1)}, f32[48,16,512]{2,1,0:T(8,128)S(1)}, f32[48,16,512]{2,1,0:T(8,128)}) fusion(f32[48,16,512]{2,1,0:T(8,128)S(1)} %get-tuple-element.38, f32[48,16,512]{2,1,0:T(8,128)S(1)} %get-tuple-element.8, f32[47,16,512]{2,1,0:T(8,128)S(1)} %slice.295, f32[48,16,512]{2,1,0:T(8,128)S(1)} %get-tuple-element.39, ...), kind=kLoop, calls=%fused_computation.33 | loop fusion | flops 2359296 | bytes 15594496 | tf_op jit(solution)/shard_map/mul | solution.py:58
  128.0 1.5 slice.296
  129.6 6.3 %broadcast_multiply_fusion = (f32[48,16,512]{2,1,0:T(8,128)S(1)}, f32[48,16,512]{2,1,0:T(8,128)S(1)}, f32[48,16,512]{2,1,0:T(8,128)}) fusion(f32[48,16,512]{2,1,0:T(8,128)S(1)} %get-tuple-element.16, f32[48,16,512]{2,1,0:T(8,128)} %get-tuple-element.9, f32[48,16,512]{2,1,0:T(8,128)S(1)} %get-tuple-element.27, f32[48,16,511]{2,1,0:T(8,128)S(1)} %bitcast.47, ...), kind=kLoop, calls=%fused_computation.64 | loop fusion | flops 3932160 | bytes 18740224 | tf_op jit(solution)/shard_map/div | solution.py:126
  137.0 2.8 %subtract_multiply_fusion.8 = (f32[48,16,512]{2,1,0:T(8,128)S(1)}, f32[48,16,512]{2,1,0:T(8,128)S(1)}, f32[48,16,512]{2,1,0:T(8,128)}) fusion(f32[48,16,512]{2,1,0:T(8,128)S(1)} %get-tuple-element.38, f32[47,16,512]{2,1,0:T(8,128)S(1)} %slice.301, f32[48,16,512]{2,1,0:T(8,128)S(1)} %get-tuple-element.6, f32[48,16,512]{2,1,0:T(8,128)S(1)} %get-tuple-element.40, ...), kind=kLoop, calls=%fused_computation.29 | loop fusion | flops 2752512 | bytes 15594496 | tf_op jit(solution)/shard_map/mul | solution.py:58
  139.8 1.0 copy-done.9
  140.9 5.1 %multiply_add_fusion.1 = (f32[48,16,512]{2,1,0:T(8,128)S(1)}, f32[48,16,512]{2,1,0:T(8,128)S(1)}) fusion(f32[48,16,512]{2,1,0:T(8,128)S(1)} %get-tuple-element.16, f32[48,16,512]{2,1,0:T(8,128)S(1)} %get-tuple-element.6, f32[48,16,512]{2,1,0:T(8,128)} %get-tuple-element.7, f32[48,16,512]{2,1,0:T(8,128)} %get-tuple-element.25, f32[48,16,511]{2,1,0:T(8,128)} %bitcast.54, ...), kind=kLoop, calls=%fused_computation.25 | loop fusion | flops 4718592 | bytes 17167360 | tf_op jit(solution)/shard_map/add | solution.py:132
  146.9 1.4 subtract_multiply_fusion.5
  148.5 1.9 multiply_add_fusion
  152.6 3.0 %subtract_multiply_fusion.2 = (f32[48,16,512]{2,1,0:T(8,128)S(1)}, f32[48,16,512]{2,1,0:T(8,128)}, f32[48,16,512]{2,1,0:T(8,128)}) fusion(f32[48,16,512]{2,1,0:T(8,128)S(1)} %get-tuple-element.38, f32[48,16,512]{2,1,0:T(8,128)S(1)} %multiply_add_fusion, f32[47,16,512]{2,1,0:T(8,128)S(1)} %slice.313, f32[48,16,512]{2,1,0:T(8,128)S(1)} %get-tuple-element.40, ...), kind=kLoop, calls=%fused_computation.19 | loop fusion | flops 2359296 | bytes 15594496 | tf_op jit(solution)/shard_map/mul | solution.py:58
  155.6 1.3 slice.314
  157.0 11.3 %add_add_fusion = f32[48,16,512]{2,1,0:T(8,128)} fusion(f32[48,16,512]{2,1,0:T(8,128)S(1)} %get-tuple-element.16, f32[48,16,511]{2,1,0:T(8,128)} %bitcast.60, f32[48,15,512]{2,1,0:T(8,128)} %bitcast.59, f32[47,16,512]{2,1,0:T(8,128)} %slice.314, f32[48,16,512]{2,1,0:T(8,128)S(1)} %multiply_add_fusion, f32[48,16,512]{2,1,0:T(8,128)S(1)} %get-tuple-element.3, ...), kind=kLoop, calls=%fused_computation.16 | loop fusion | flops 13762560 | bytes 38919168 | tf_op jit(solution)/shard_map/add | solution.py:128
  168.3 2.4 %slice_multiply_fusion = f32[32,1,512]{2,1,0:T(1,128)} fusion(f32[48,16,512]{2,1,0:T(8,128)} %add_add_fusion, f32[]{:T(128)} %bitcast.16), kind=kLoop, calls=%fused_computation.73 | loop fusion | flops 16384 | bytes 131076 | tf_op jit(solution)/shard_map/mul | solution.py:141
  170.7 2.3 slice.319
  173.0 5.7 %all-to-all-start.2 = ((f32[8,4,16,512]{3,2,1,0:T(8,128)}), f32[8,4,16,512]{3,2,1,0:T(8,128)S(1)}, u32[]{:S(2)}, u32[]{:S(2)}) async-start(f32[8,4,16,512]{3,2,1,0:T(8,128)} %bitcast.14), calls=%async_computation.2 | async-start | bytes 2097152 | tf_op jit(solution)/shard_map/all_to_all | solution.py:97
  179.4 0.6 pad_maximum_fusion.2
  180.0 14.6 %all-to-all-done.2 = f32[8,4,16,512]{3,2,1,0:T(8,128)S(1)} async-done(((f32[8,4,16,512]{3,2,1,0:T(8,128)}), f32[8,4,16,512]{3,2,1,0:T(8,128)S(1)}, u32[]{:S(2)}, u32[]{:S(2)}) %all-to-all-start.2) | async-done | bytes 1048608 | tf_op jit(solution)/shard_map/all_to_all | solution.py:97
  194.6 22.7 %all-gather.4.cloned.1.call-done = f32[512,1,512]{2,1,0:T(1,128)} async-done(((f32[32,1,512]{2,1,0:T(1,128)}), f32[512,1,512]{2,1,0:T(1,128)}) %all-gather.4.cloned.1.call-update) | async-done | bytes 1048592 | tf_op jit(solution)/shard_map/all_gather | solution.py:142
  217.3 1.3 copy.8
  219.1 5.2 %fusion.9 = f32[32,512]{1,0:T(8,128)} fusion(f32[32,512]{1,0:T(8,128)S(1)} %fusion.26, s32[512]{0:T(512)S(1)} %multiply_add_fusion.5), kind=kOutput, calls=%fused_computation.58 | convolution fusion | flops 104595456 | bytes 133120 | tf_op jit(solution)/shard_map/dot_general | solution.py:152
  224.3 1.0 copy.11
  (81 shorter events, 11.1 us)
Async XLA Ops:
  7.2 5.4 %copy-start.14 = (f32[8,4,16,512]{3,2,1,0:T(8,128)S(1)}, f32[8,4,16,512]{3,2,1,0:T(8,128)}, u32[]{:S(2)}) copy-start(f32[8,4,16,512]{3,2,1,0:T(8,128)} %param.5) | copy-start | bytes 3145732
  7.2 5.4 %copy-start.15 = (f32[4,16,512]{2,1,0:T(8,128)S(1)}, f32[4,16,512]{2,1,0:T(8,128)}, u32[]{:S(2)}) copy-start(f32[4,16,512]{2,1,0:T(8,128)} %param.6) | copy-start | bytes 393220
  7.2 5.4 %copy-start.16 = (f32[8]{0:T(128)S(1)}, f32[8]{0:T(128)}, u32[]{:S(2)}) copy-start(f32[8]{0:T(128)} %param.9) | copy-start | bytes 100
  7.2 19.8 %all-to-all-start.1 = ((s32[8,4,16,512]{3,2,1,0:T(8,128)}), s32[8,4,16,512]{3,2,1,0:T(8,128)S(1)}, u32[]{:S(2)}, u32[]{:S(2)}) async-start(s32[8,4,16,512]{3,2,1,0:T(8,128)} %param.7), calls=%async_computation.1 | async-start | bytes 2097152 | tf_op jit(solution)/shard_map/all_to_all | solution.py:97
  13.9 16.7 %copy-start.17 = (u32[32]{0:T(128)S(1)}, u32[32]{0:T(128)}, u32[]{:S(2)}) copy-start(u32[32]{0:T(128)} %constant.227) | copy-start | bytes 388
  27.0 45.8 %copy-start.13 = (s32[8,4,16,512]{3,2,1,0:T(8,128)}, s32[8,4,16,512]{3,2,1,0:T(8,128)S(1)}, u32[]{:S(2)}) copy-start(s32[8,4,16,512]{3,2,1,0:T(8,128)S(1)} %all-to-all-done.1) | copy-start | bytes 3145732
  27.0 61.8 %all-to-all-start = ((f32[8,4,16,512]{3,2,1,0:T(8,128)}), f32[8,4,16,512]{3,2,1,0:T(8,128)S(1)}, u32[]{:S(2)}, u32[]{:S(2)}) async-start(f32[8,4,16,512]{3,2,1,0:T(8,128)} %get-tuple-element.42), calls=%async_computation | async-start | bytes 2097152 | tf_op jit(solution)/shard_map/all_to_all | solution.py:97
  30.6 186.7 %all-gather.4.cloned.1.call-start = ((), (), s32[]{:S(2)}) async-start(), calls=%async_computation.3 | async-start | bytes 1114112 | tf_op jit(solution)/shard_map/all_gather | solution.py:142
  80.8 17.1 %collective-permute-start.3 = (f32[8,16,512]{2,1,0:T(8,128)}, f32[8,16,512]{2,1,0:T(8,128)S(1)}, u32[]{:S(2)}, u32[]{:S(2)}) collective-permute-start(f32[8,16,512]{2,1,0:T(8,128)} %bitcast.13), channel_id=1, source_target_pairs={{8,0},{9,1},{10,2},{11,3},{12,4},{13,5},{14,6},{15,7},{24,16},{25,... | collective-permute-start | bytes 786440 | tf_op jit(solution)/shard_map/ppermute | solution.py:105
  82.0 15.8 %collective-permute-start.2 = (f32[8,16,512]{2,1,0:T(8,128)}, f32[8,16,512]{2,1,0:T(8,128)S(1)}, u32[]{:S(2)}, u32[]{:S(2)}) collective-permute-start(f32[8,16,512]{2,1,0:T(8,128)} %bitcast.11), channel_id=1, source_target_pairs={{0,8},{1,9},{2,10},{3,11},{4,12},{5,13},{6,14},{7,15},{16,24},{17,... | collective-permute-start | bytes 786440 | tf_op jit(solution)/shard_map/ppermute | solution.py:104
  88.8 14.2 %collective-permute-start.1 = (f32[8,16,512]{2,1,0:T(8,128)S(1)}, f32[8,16,512]{2,1,0:T(8,128)S(1)}, u32[]{:S(2)}, u32[]{:S(2)}) collective-permute-start(f32[8,16,512]{2,1,0:T(8,128)S(1)} %bitcast.64), channel_id=1, source_target_pairs={{8,0},{9,1},{10,2},{11,3},{12,4},{13,5},{14,6},{15,7},{24,16},{25,... | collective-permute-start | bytes 786440 | tf_op jit(solution)/shard_map/ppermute | solution.py:105
  90.1 12.9 %collective-permute-start = (f32[8,16,512]{2,1,0:T(8,128)S(1)}, f32[8,16,512]{2,1,0:T(8,128)S(1)}, u32[]{:S(2)}, u32[]{:S(2)}) collective-permute-start(f32[8,16,512]{2,1,0:T(8,128)S(1)} %bitcast.63), channel_id=1, source_target_pairs={{0,8},{1,9},{2,10},{3,11},{4,12},{5,13},{6,14},{7,15},{16,24},{17,... | collective-permute-start | bytes 786440 | tf_op jit(solution)/shard_map/ppermute | solution.py:104
  104.5 3.7 %copy-start.3 = (f32[48,16,512]{2,1,0:T(8,128)}, f32[48,16,512]{2,1,0:T(8,128)S(1)}, u32[]{:S(2)}) copy-start(f32[48,16,512]{2,1,0:T(8,128)S(1)} %get-tuple-element.15) | copy-start | bytes 4718596
  115.0 1.4 copy-start.12
  128.0 1.7 copy-start.8
  136.0 4.9 %copy-start.2 = (f32[48,16,512]{2,1,0:T(8,128)}, f32[48,16,512]{2,1,0:T(8,128)S(1)}, u32[]{:S(2)}) copy-start(f32[48,16,512]{2,1,0:T(8,128)S(1)} %get-tuple-element.6) | copy-start | bytes 4718596
  139.7 1.1 copy-start.9
  145.9 2.6 %copy-start.5 = (f32[48,16,512]{2,1,0:T(8,128)}, f32[48,16,512]{2,1,0:T(8,128)S(1)}, u32[]{:S(2)}) copy-start(f32[48,16,512]{2,1,0:T(8,128)S(1)} %get-tuple-element.4) | copy-start | bytes 4718596
  148.3 2.2 copy-start
  148.3 2.2 copy-start.1
  148.3 2.2 copy-start.4
  148.5 2.3 copy-start.10
  150.9 1.2 copy-start.11
  151.2 1.4 copy-start.6
  152.6 3.0 %copy-start.7 = (f32[48,16,511]{2,1,0:T(8,128)}, f32[48,16,511]{2,1,0:T(8,128)S(1)}, u32[]{:S(2)}) copy-start(f32[48,16,511]{2,1,0:T(8,128)S(1)} %slice.317) | copy-start | bytes 4709380
  173.0 21.6 %all-to-all-start.2 = ((f32[8,4,16,512]{3,2,1,0:T(8,128)}), f32[8,4,16,512]{3,2,1,0:T(8,128)S(1)}, u32[]{:S(2)}, u32[]{:S(2)}) async-start(f32[8,4,16,512]{3,2,1,0:T(8,128)} %bitcast.14), calls=%async_computation.2 | async-start | bytes 2097152 | tf_op jit(solution)/shard_map/all_to_all | solution.py:97
Sparse Core Ops, SparseCore 0:
  170.9 46.3 all-gather.3
where the time goes:
time: 235 us; the launch traced here: 232 us
  other arithmetic  64.4 us (27%)
  waiting for transfers between devices  55.1 us (23%)
  blocking collectives  37.9 us (16%)
  starting transfers between devices  28.3 us (12%)
  local copies, waits for them, and re-layouts  24.2 us (10%)
  between operations  16.7 us (7%)
  matrix products  5.65 us (2%)
    unnamed x1, blocking collectives  37.9 us
    all_to_all x3, waiting for transfers between devices, deal(): lax.all_to_all(field, 'gz', split_axis=0, concat_axis=0, axis_index_group...  27.8 us
    all_gather x1, waiting for transfers between devices, on_device(): faces = lax.all_gather(own_face, 'gz')  22.7 us
    add x5, other arithmetic, on_device(): search = first_mix * search + second_mix * (residual / diagonal)  16.7 us
    all_to_all x3, starting transfers between devices, deal(): lax.all_to_all(field, 'gz', split_axis=0, concat_axis=0, axis_index_group...  14.6 us
    mul x7, other arithmetic, apply_operator(): flux_term = weights[dim] * (shift_ahead(values, dim) - values)  14.4 us
    add x1, other arithmetic, on_device(): iterate = iterate + search  11.3 us
    ppermute x2, starting transfers between devices, widen(): before = lax.ppermute(field[depth - HALO:], 'gz', ahead)  11.1 us
  transfers between devices with their start and end apart: 8, of which 5 were waited for; matrix products, arithmetic and copies ran while one was open for 8% of the time, Pallas kernels for 0%

commit v1 on v0

v1 whole, which is shorter than its diff:
```python
import math

import jax
import jax.numpy as jnp
import numpy as np
from jax import lax
from jax.experimental import pallas as pl
from jax.experimental.pallas import tpu as pltpu
from jax.sharding import PartitionSpec as P

NR = 8
DEGREE = 4
SWEEPS = 2
MA = 512
MB = 512

STORAGE = 0.05
BETA_RISK = 0.5
LOWER_EIGEN = 0.05
UPPER_EIGEN = 2.0

TEAM = 4
STEPS = DEGREE * SWEEPS
F32 = jnp.float32
MIB = 1024 * 1024


def chebyshev_constants(number_steps):
    centre = (UPPER_EIGEN + LOWER_EIGEN) / 2
    spread = (UPPER_EIGEN - LOWER_EIGEN) / 2
    quotient = centre / spread
    rho_now = 1.0 / quotient
    coefficients = []
    for position in range(number_steps):
        rho_next = 1.0 / (2.0 * quotient - rho_now)
        coefficients.append((rho_next * rho_now, 2.0 * rho_next / spread))
        rho_now = rho_next
    return (centre, coefficients)


def cosine_basis(length_total, modes):
    positions = np.arange(length_total, dtype=np.int64)
    mode_index = np.arange(modes, dtype=np.int64)
    product_index = ((2 * positions[:, None] + 1) * (2 * mode_index[None, :] + 1)) % (
        8 * length_total
    )
    angle = product_index.astype(np.float64) * (math.pi / (4 * length_total))
    return (math.sqrt(2.0 / length_total) * np.cos(angle)).astype(np.float32)


def team_place():
    return lax.rem(lax.axis_index("gz"), TEAM)


def prepare(slot, state, target, rock_type, log_table, obs_scale, depth_total):
    samples, planes, rows_y, columns = state.shape
    slots = samples // TEAM
    block = (planes, rows_y, columns)
    order = (2, 3, 1, 0)

    def kernel(table, scale, state_ref, target_ref, rock_ref, *rest):
        outs, sums_ref = rest[:TEAM], rest[TEAM]
        state_buf, rock_buf, target_buf, sems = rest[TEAM + 1 :]
        place = team_place()
        first_plane = lax.axis_index("gz") * planes
        members = [slots * (place ^ m) + slot for m in range(TEAM)]
        target_copy = pltpu.make_async_copy(target_ref, target_buf, sems.at[2, 0])
        target_copy.start()
        copies = {}
        for m in order:
            copies[m] = (
                pltpu.make_async_copy(state_ref.at[members[m]], state_buf.at[m], sems.at[0, m]),
                pltpu.make_async_copy(rock_ref.at[members[m]], rock_buf.at[m], sems.at[1, m]),
            )
            for copy in copies[m]:
                copy.start()
        sums_ref[...] = jnp.zeros(sums_ref.shape, F32)
        target_copy.wait()
        for m in order:
            for copy in copies[m]:
                copy.wait()
            values = [
                jnp.exp(jnp.full((1, columns), table[members[m], code], F32))
                for code in range(NR)
            ]
            own_scale = scale[members[m]]

            def one_plane(p, total):
                codes = rock_buf[m, p]
                low, mid, high = ((codes & bit) != 0 for bit in (1, 2, 4))
                pairs = [
                    jnp.where(low, values[2 * i + 1], values[2 * i]) for i in range(NR // 2)
                ]
                halves = [jnp.where(mid, pairs[2 * i + 1], pairs[2 * i]) for i in range(2)]
                outs[m][0, p] = jnp.where(high, halves[1], halves[0])
                depth_weight = 1.0 + (2.0 / (depth_total - 1)) * (first_plane + p).astype(F32)
                gap = state_buf[m, p] - target_buf[p]
                source = (own_scale * depth_weight) * gap
                outs[m][1, p] = source
                return total + source * gap

            total = lax.fori_loop(0, planes, one_plane, jnp.zeros((rows_y, columns), F32))
            summed = jnp.sum(total, keepdims=True)
            sums_ref[pl.ds(members[m], 1), :] = jnp.broadcast_to(summed, (1, 128))

    any_space = pl.BlockSpec(memory_space=pl.ANY)
    smem = pl.BlockSpec(memory_space=pltpu.SMEM)
    vmem = pl.BlockSpec(memory_space=pltpu.VMEM)
    results = pl.pallas_call(
        kernel,
        out_shape=[jax.ShapeDtypeStruct((2,) + block, F32)] * TEAM
        + [jax.ShapeDtypeStruct((samples, 128), F32)],
        in_specs=[smem, smem, any_space, any_space, any_space],
        out_specs=[vmem] * (TEAM + 1),
        scratch_shapes=[
            pltpu.VMEM((TEAM,) + block, F32),
            pltpu.VMEM((TEAM,) + block, jnp.int32),
            pltpu.VMEM(block, F32),
            pltpu.SemaphoreType.DMA((3, TEAM)),
        ],
        compiler_params=pltpu.CompilerParams(vmem_limit_bytes=16 * MIB),
        name=f"prepare{slot}",
    )(log_table, obs_scale, state, target, rock_type)
    return results[:TEAM], results[TEAM]


def solve(slot, blocks, near, far):
    _, planes, rows_y, columns = blocks[0].shape
    halo = 2 * planes
    own = TEAM * planes
    span = own + 2 * halo
    plane_shape = (rows_y, columns)
    centre, coefficients = chebyshev_constants(DEGREE)
    assert halo >= STEPS

    def kernel(*refs):
        inputs, outs = refs[:8], refs[8:12]
        cond, u, s_a, s_b, zp, zm, yp, ym, xp, xm, total, sems = refs[12:]
        place = team_place()
        column, side = lax.rem(place, 2), place // 2
        copies = []
        for m in range(TEAM):
            copies.append((inputs[m], halo + planes * (place ^ m)))
        upper, lower = halo + own, 0
        near_base = jnp.where(side == 0, upper, lower)
        far_base = jnp.where(side == 0, lower, upper)
        copies.append((inputs[4], near_base + planes * column))
        copies.append((inputs[5], near_base + planes * (1 - column)))
        copies.append((inputs[6], far_base + planes * column))
        copies.append((inputs[7], far_base + planes * (1 - column)))
        started = []
        for i, (source, place_at) in enumerate(copies):
            for j, held in enumerate((cond, u)):
                copy = pltpu.make_async_copy(
                    source.at[j], held.at[pl.ds(place_at, planes)], sems.at[i, j]
                )
                copy.start()
                started.append(copy)
        for copy in started:
            copy.wait()

        row_index = lax.broadcasted_iota(jnp.int32, plane_shape, 0)
        column_index = lax.broadcasted_iota(jnp.int32, plane_shape, 1)
        last_row = row_index == rows_y - 1
        last_column = column_index == columns - 1

        def ahead_y(v):
            return pltpu.roll(v, rows_y - 1, 0)

        def behind_y(v):
            return pltpu.roll(v, 1, 0)

        def ahead_x(v):
            return pltpu.roll(v, columns - 1, 1)

        def behind_x(v):
            return pltpu.roll(v, 1, 1)

        def harmonic(a, b):
            return 2.0 * a * b / jnp.maximum(a + b, 1e-30)

        def setup(p, w_behind):
            here = cond[p]
            w_z = harmonic(here, cond[p + 1])
            w_y = jnp.where(last_row, 0.0, harmonic(here, ahead_y(here)))
            w_x = jnp.where(last_column, 0.0, harmonic(here, ahead_x(here)))
            w_y_behind, w_x_behind = behind_y(w_y), behind_x(w_x)
            diagonal = (w_z + w_behind) + (w_y + w_y_behind) + (w_x + w_x_behind) + STORAGE
            inverse = 1.0 / diagonal
            zp[p] = w_z * inverse
            zm[p] = w_behind * inverse
            yp[p] = w_y * inverse
            ym[p] = w_y_behind * inverse
            xp[p] = w_x * inverse
            xm[p] = w_x_behind * inverse
            scaled = u[p] * inverse
            u[p] = scaled
            s_a[p] = scaled * (1.0 / centre)
            return w_z

        lax.fori_loop(1, span - 1, setup, harmonic(cond[0], cond[1]))

        here, there = s_a, s_b
        for step in range(STEPS - 1):
            position = step % DEGREE
            if position + 1 < DEGREE:
                keep, mix = coefficients[position]
            else:
                keep, mix = 0.0, 1.0 / centre
            last = step == STEPS - 2

            def advance(p, inside, here=here, there=there, step=step, keep=keep, mix=mix, last=last):
                s = here[p]
                moved = zp[p] * here[p + 1] + zm[p] * here[p - 1]
                moved += yp[p] * ahead_y(s) + ym[p] * behind_y(s)
                moved += xp[p] * ahead_x(s) + xm[p] * behind_x(s)
                new_u = (u[p] - s) + moved
                new_s = mix * new_u if keep == 0.0 else keep * s + mix * new_u
                if last:
                    total[p - halo] = (total[p - halo] + s) + new_s
                else:
                    u[p] = new_u
                    there[p] = new_s
                    if inside:
                        total[p - halo] = s if step == 0 else total[p - halo] + s
                return inside

            def run(start, stop, inside):
                if start < stop:
                    lax.fori_loop(
                        start, stop, lambda p, c: (advance(p, inside), c)[1], 0, unroll=2
                    )

            margin = halo - (STEPS - 2 - step)
            run(margin, halo, False)
            run(halo, halo + own, True)
            run(halo + own, span - margin, False)
            here, there = there, here

        for m in range(TEAM):
            outs[m][...] = total[pl.ds(planes * (place ^ m), planes)]

    any_space = pl.BlockSpec(memory_space=pl.ANY)
    vmem = pl.BlockSpec(memory_space=pltpu.VMEM)
    field = pltpu.VMEM((span,) + plane_shape, F32)
    return pl.pallas_call(
        kernel,
        out_shape=[jax.ShapeDtypeStruct((planes,) + plane_shape, F32)] * TEAM,
        in_specs=[any_space] * 8,
        out_specs=[vmem] * TEAM,
        scratch_shapes=[field] * 10
        + [pltpu.VMEM((own,) + plane_shape, F32), pltpu.SemaphoreType.DMA((8, 2))],
        compiler_params=pltpu.CompilerParams(vmem_limit_bytes=32 * MIB),
        name=f"solve{slot}",
    )(*blocks, *near, *far)


def weigh_faces(pieces, sums, cells):
    slots = len(pieces)
    planes, rows_y, columns = pieces[0][0].shape
    slabs, samples, _ = sums.shape

    def kernel(sums_ref, *refs):
        faces = refs[: slots * TEAM]
        face_ref, moments_ref, buf, weights, sems = refs[slots * TEAM :]
        place = team_place()
        copies = []
        for i, piece in enumerate(faces):
            copy = pltpu.make_async_copy(
                piece.at[:, pl.ds(0, 8), :], buf.at[i], sems.at[i]
            )
            copy.start()
            copies.append(copy)
        misfit = jnp.sum(sums_ref[...], axis=0) * (1.0 / (2.0 * cells))
        mean = jnp.sum(misfit, axis=0, keepdims=True) * (1.0 / samples)
        deviation = misfit - mean
        variance = jnp.sum(deviation * deviation, axis=0, keepdims=True) * (1.0 / samples)
        moments_ref[0:1, :] = mean
        moments_ref[1:2, :] = variance
        weights[...] = 1.0 + 2.0 * BETA_RISK * deviation
        for copy in copies:
            copy.wait()
        face = jnp.zeros((planes, columns), F32)
        for slot in range(slots):
            for m in range(TEAM):
                row = weights[pl.ds(slots * (place ^ m) + slot, 1), :]
                wide = jnp.concatenate([row] * (columns // 128), axis=1)
                face = face + wide * buf[slot * TEAM + m, :, 0, :]
        face_ref[...] = jnp.broadcast_to(face[None], face_ref.shape)

    any_space = pl.BlockSpec(memory_space=pl.ANY)
    vmem = pl.BlockSpec(memory_space=pltpu.VMEM)
    return pl.pallas_call(
        kernel,
        out_shape=[
            jax.ShapeDtypeStruct((slabs, planes, columns), F32),
            jax.ShapeDtypeStruct((2, 128), F32),
        ],
        in_specs=[vmem] + [any_space] * (slots * TEAM),
        out_specs=[vmem, vmem],
        scratch_shapes=[
            pltpu.VMEM((slots * TEAM, planes, 8, columns), F32),
            pltpu.VMEM((samples, 128), F32),
            pltpu.SemaphoreType.DMA((slots * TEAM,)),
        ],
        name="weigh_faces",
    )(sums, *[piece for group in pieces for piece in group])


def gather_adjoint(pieces):
    slots = len(pieces)
    block = pieces[0][0].shape

    def kernel(*refs):
        blocks, out, sems = refs[: slots * TEAM], refs[slots * TEAM], refs[slots * TEAM + 1]
        place = team_place()
        copies = []
        for slot in range(slots):
            for m in range(TEAM):
                i = slot * TEAM + m
                copy = pltpu.make_async_copy(
                    blocks[i], out.at[slots * (place ^ m) + slot], sems.at[i]
                )
                copy.start()
                copies.append(copy)
        for copy in copies:
            copy.wait()

    any_space = pl.BlockSpec(memory_space=pl.ANY)
    return pl.pallas_call(
        kernel,
        out_shape=jax.ShapeDtypeStruct((slots * TEAM,) + block, F32),
        in_specs=[any_space] * (slots * TEAM),
        out_specs=any_space,
        scratch_shapes=[pltpu.SemaphoreType.DMA((slots * TEAM,))],
        name="gather_adjoint",
    )(*[piece for group in pieces for piece in group])


def control(faces, basis_z, basis_x, own_count):
    depth_total, columns = faces.shape

    def kernel(face_ref, z_ref, x_ref, out_ref):
        own_modes = z_ref[lax.axis_index("gz")]
        along_z = jnp.dot(
            own_modes, face_ref[...], precision=lax.Precision.HIGHEST, preferred_element_type=F32
        )
        out_ref[...] = jnp.dot(
            along_z, x_ref[...], precision=lax.Precision.HIGHEST, preferred_element_type=F32
        )

    vmem = pl.BlockSpec(memory_space=pltpu.VMEM)
    return pl.pallas_call(
        kernel,
        out_shape=jax.ShapeDtypeStruct((own_count, basis_x.shape[1]), F32),
        in_specs=[vmem] * 3,
        out_specs=vmem,
        compiler_params=pltpu.CompilerParams(vmem_limit_bytes=16 * MIB),
        name="control",
    )(faces, basis_z, basis_x)


def on_device(state, target, rock_type, log_table, obs_scale):
    samples, planes, rows_y, columns = state.shape
    slabs = lax.axis_size("gz")
    slots = samples // TEAM
    depth_total = planes * slabs

    def swap(value, m):
        return lax.ppermute(value, "gz", [(i, i ^ m) for i in range(slabs)])

    def along(value, outward):
        pairs = []
        for i in range(slabs):
            side = (i % TEAM) // 2
            to = i + TEAM if (side == 1) == outward else i - TEAM
            if 0 <= to < slabs:
                pairs.append((i, to))
        return lax.ppermute(value, "gz", pairs)

    received, sums = [], []
    for slot in range(slots):
        blocks, slot_sums = prepare(
            slot, state, target, rock_type, log_table, obs_scale, depth_total
        )
        sums.append(slot_sums)
        far = [swap(blocks[m], m) for m in (2, 3)]
        received.append([blocks[0], swap(blocks[1], 1)] + far)
    pieces = []
    for slot in range(slots):
        blocks = received[slot]
        near = [along(blocks[m], True) for m in (0, 1)]
        far = [along(blocks[m], False) for m in (2, 3)]
        solved = solve(slot, blocks, near, far)
        pieces.append([solved[0]] + [swap(solved[m], m) for m in (1, 2, 3)])

    local_sums = sum(sums[1:], sums[0])
    spread_sums = jnp.broadcast_to(local_sums[None], (slabs,) + local_sums.shape)
    all_sums = lax.all_to_all(spread_sums, "gz", split_axis=0, concat_axis=0, tiled=True)

    faces, moments = weigh_faces(pieces, all_sums, depth_total * rows_y * columns)
    faces = lax.all_to_all(faces, "gz", split_axis=0, concat_axis=0, tiled=True)
    adjoint = gather_adjoint(pieces)
    gradient = control(
        faces.reshape(depth_total, columns),
        jnp.asarray(cosine_basis(depth_total, MA).T.reshape(slabs, MA // slabs, depth_total)),
        jnp.asarray(cosine_basis(columns, MB)),
        MA // slabs,
    )
    return (adjoint, gradient, moments[:, 0])


def solution(mesh):
    return jax.shard_map(
        on_device,
        mesh=mesh,
        in_specs=(
            P("parts", "gz", None, None),
            P(("parts", "gz"), None, None),
            P("parts", "gz", None, None),
            P("parts", None),
            P("parts"),
        ),
        out_specs=(P("parts", "gz", None, None), P(("parts", "gz"), None), P("parts")),
        check_vma=False,
    )
```

time: 235 us -> 138 us (0.59); the launches traced: 232 us -> 138 us
  Pallas kernels: 0 us -> 76.8 us
  other arithmetic: 64.4 us -> 0.01 us
  waiting for transfers between devices: 55.1 us -> 4.08 us
  blocking collectives: 37.9 us -> 11.7 us
  local copies, waits for them, and re-layouts: 24.2 us -> 7.69 us
  between operations: 16.7 us -> 0.96 us
  starting transfers between devices: 28.3 us -> 36.5 us
  matrix products: 5.65 us -> 0 us
    pallas_call x0 -> x7, Pallas kernels: none -> 76.8 us  [the longest x2 33.4 us: solve(): pl.pallas_call(kernel, out_shape=[jax.ShapeDtypeStruct((planes,) + plane_...]
    unnamed x1 -> x0, blocking collectives: 37.9 us -> none
    add x11 -> x1, other arithmetic: 35.1 us -> 0.01 us  [on_device(): local_sums = sum(sums[1:], sums[0])]
    all_to_all x3 -> x1, waiting for transfers between devices: 27.8 us -> 0.01 us  [on_device(): faces = lax.all_to_all(faces, 'gz', split_axis=0, concat_axis=0, tiled=True)]
    all_gather x1 -> x0, waiting for transfers between devices: 22.7 us -> none  [on_device(): faces = lax.all_gather(own_face, 'gz')]
    ppermute x4 -> x20, starting transfers between devices: 13.7 us -> 33 us  [the longest x8 21.9 us: along(): return lax.ppermute(value, 'gz', pairs)]
    mul x8 -> x0, other arithmetic: 16.8 us -> none  [the longest x7 14.4 us: apply_operator(): flux_term = weights[dim] * (shift_ahead(values, dim) - values)]
    slice x36 -> x1, local copies, waits for them, and re-layouts: 16 us -> 0.63 us  [on_device(): return (adjoint, gradient, moments[:, 0])]
  transfers between devices with their start and end apart: 8 -> 21, of which waited for: 5 -> 2; matrix products, arithmetic and copies ran while one was open for 8% -> 0% of each run, Pallas kernels for 0% -> 50%
where the time goes in v1:
time: 138 us
  Pallas kernels  76.8 us (56%)
  starting transfers between devices  36.5 us (26%)
  blocking collectives  11.7 us (8%)
  local copies, waits for them, and re-layouts  7.69 us (6%)
  waiting for transfers between devices  4.08 us (3%)
    pallas_call x2, Pallas kernels, solve(): pl.pallas_call(kernel, out_shape=[jax.ShapeDtypeStruct((planes,) + plane_...  33.4 us
    pallas_call x1, Pallas kernels, gather_adjoint(): pl.pallas_call(kernel, out_shape=jax.ShapeDtypeStruct((slots * TEAM,) + b...  32.9 us
    ppermute x8, starting transfers between devices, along(): return lax.ppermute(value, 'gz', pairs)  21.9 us
    all_to_all x1, blocking collectives, on_device(): lax.all_to_all(spread_sums, 'gz', split_axis=0, concat_axis=0, tiled=True)  11.7 us
    ppermute x12, starting transfers between devices, swap(): return lax.ppermute(value, 'gz', [(i, i ^ m) for i in range(slabs)])  11.1 us
    unnamed x32, local copies, waits for them, and re-layouts  7.01 us
    pallas_call x2, Pallas kernels, prepare(): pl.pallas_call(kernel, out_shape=[jax.ShapeDtypeStruct((2,) + block, F32)...  6.29 us
    ppermute x12, waiting for transfers between devices, swap(): return lax.ppermute(value, 'gz', [(i, i ^ m) for i in range(slabs)])  4.06 us
  transfers between devices with their start and end apart: 21, of which 2 were waited for; matrix products, arithmetic and copies ran while one was open for 0% of the time, Pallas kernels for 50%

profile of v1, /device:TPU:0, one launch (start us, length us, event | category | flops | bytes accessed | tf_op | source)
XLA Modules:
  0.0 137.7 jit_solution(11869903558185543711)
XLA Ops:
  0.6 1.2 copy-done
  1.9 1.2 copy-done.1
  3.1 0.9 copy-done.3
  4.0 0.7 copy-done.7
  4.7 0.7 copy-done.8
  5.3 3.1 %prepare1.1 = (f32[2,4,16,512]{3,2,1,0:T(8,128)S(1)}, f32[2,4,16,512]{3,2,1,0:T(8,128)S(1)}, f32[2,4,16,512]{3,2,1,0:T(8,128)S(1)}, f32[2,4,16,512]{3,2,1,0:T(8,128)S(1)}, f32[8,128]{1,0:T(8,128)S(1)}) custom-call(f32[8,8]{1,0:T(8,128)S(1)} %copy-done.7, f32[8]{0:T(128)S(1)} %copy-done.8, f32[8,4,16,512]{3,2,1,0:T(8,128)S(1)} %copy-done, ...), custom_call_target="tpu_custom_call" | custom-call | tf_op jit(solution)/shard_map/prepare1/pallas_call | solution.py:109
  8.5 0.5 collective-permute-start.10
  9.0 2.6 %collective-permute-start.11 = (f32[2,4,16,512]{3,2,1,0:T(8,128)S(1)}, f32[2,4,16,512]{3,2,1,0:T(8,128)S(1)}, u32[]{:S(2)}, u32[]{:S(2)}) collective-permute-start(f32[2,4,16,512]{3,2,1,0:T(8,128)S(1)} %get-tuple-element.33), channel_id=1, source_target_pairs={{0,2},{1,3},{2,0},{3,1},{4,6},{5,7},{6,4},{7,5},{8,10},{9,11},{10,... | collective-permute-start | bytes 786440 | tf_op jit(solution)/shard_map/ppermute | solution.py:370
  11.6 0.1 collective-permute-start.12
  11.6 1.3 collective-permute-start.13
  12.9 3.1 %prepare0.1 = (f32[2,4,16,512]{3,2,1,0:T(8,128)S(1)}, f32[2,4,16,512]{3,2,1,0:T(8,128)S(1)}, f32[2,4,16,512]{3,2,1,0:T(8,128)S(1)}, f32[2,4,16,512]{3,2,1,0:T(8,128)S(1)}, f32[8,128]{1,0:T(8,128)S(1)}) custom-call(f32[8,8]{1,0:T(8,128)S(1)} %copy-done.7, f32[8]{0:T(128)S(1)} %copy-done.8, f32[8,4,16,512]{3,2,1,0:T(8,128)S(1)} %copy-done, ...), custom_call_target="tpu_custom_call" | custom-call | tf_op jit(solution)/shard_map/prepare0/pallas_call | solution.py:109
  16.1 0.2 collective-permute-start
  16.3 3.9 %collective-permute-start.1 = (f32[2,4,16,512]{3,2,1,0:T(8,128)S(1)}, f32[2,4,16,512]{3,2,1,0:T(8,128)S(1)}, u32[]{:S(2)}, u32[]{:S(2)}) collective-permute-start(f32[2,4,16,512]{3,2,1,0:T(8,128)S(1)} %get-tuple-element.25), channel_id=1, source_target_pairs={{0,2},{1,3},{2,0},{3,1},{4,6},{5,7},{6,4},{7,5},{8,10},{9,11},{10,... | collective-permute-start | bytes 786440 | tf_op jit(solution)/shard_map/ppermute | solution.py:370
  20.2 0.0 collective-permute-done.11.refs_2_
  20.2 0.1 collective-permute-start.2
  20.3 3.6 %collective-permute-done.12.refs_3_ = f32[2,4,16,512]{3,2,1,0:T(8,128)S(1)} collective-permute-done((f32[2,4,16,512]{3,2,1,0:T(8,128)S(1)}, f32[2,4,16,512]{3,2,1,0:T(8,128)S(1)}, u32[]{:S(2)}, u32[]{:S(2)}) %collective-permute-start.12) | collective-permute-done | bytes 262176 | tf_op jit(solution)/shard_map/ppermute | solution.py:370
  23.8 1.3 collective-permute-start.14
  25.1 4.6 %collective-permute-start.15 = (f32[2,4,16,512]{3,2,1,0:T(8,128)S(1)}, f32[2,4,16,512]{3,2,1,0:T(8,128)S(1)}, u32[]{:S(2)}, u32[]{:S(2)}) collective-permute-start(f32[2,4,16,512]{3,2,1,0:T(8,128)S(1)} %collective-permute-done.11.refs_2_), channel_id=1, source_target_pairs={{0,4},{1,5},{4,8},{5,9},{6,2},{7,3},{8,12},{9,13},{10,6},{11,7},{1... | collective-permute-start | bytes 786440 | tf_op jit(solution)/shard_map/ppermute | solution.py:379
  29.7 3.5 %collective-permute-start.16 = (f32[2,4,16,512]{3,2,1,0:T(8,128)S(1)}, f32[2,4,16,512]{3,2,1,0:T(8,128)S(1)}, u32[]{:S(2)}, u32[]{:S(2)}) collective-permute-start(f32[2,4,16,512]{3,2,1,0:T(8,128)S(1)} %collective-permute-done.12.refs_3_), channel_id=1, source_target_pairs={{0,4},{1,5},{4,8},{5,9},{6,2},{7,3},{8,12},{9,13},{10,6},{11,7},{1... | collective-permute-start | bytes 786440 | tf_op jit(solution)/shard_map/ppermute | solution.py:379
  33.3 1.3 collective-permute-start.3
  34.6 0.5 collective-permute-done.2.refs_3_
  35.1 1.3 collective-permute-start.4
  36.4 4.7 %collective-permute-start.5 = (f32[2,4,16,512]{3,2,1,0:T(8,128)S(1)}, f32[2,4,16,512]{3,2,1,0:T(8,128)S(1)}, u32[]{:S(2)}, u32[]{:S(2)}) collective-permute-start(f32[2,4,16,512]{3,2,1,0:T(8,128)S(1)} %collective-permute-done.1.refs_2_), channel_id=1, source_target_pairs={{0,4},{1,5},{4,8},{5,9},{6,2},{7,3},{8,12},{9,13},{10,6},{11,7},{1... | collective-permute-start | bytes 786440 | tf_op jit(solution)/shard_map/ppermute | solution.py:379
  41.1 3.9 %collective-permute-start.6 = (f32[2,4,16,512]{3,2,1,0:T(8,128)S(1)}, f32[2,4,16,512]{3,2,1,0:T(8,128)S(1)}, u32[]{:S(2)}, u32[]{:S(2)}) collective-permute-start(f32[2,4,16,512]{3,2,1,0:T(8,128)S(1)} %collective-permute-done.2.refs_3_), channel_id=1, source_target_pairs={{0,4},{1,5},{4,8},{5,9},{6,2},{7,3},{8,12},{9,13},{10,6},{11,7},{1... | collective-permute-start | bytes 786440 | tf_op jit(solution)/shard_map/ppermute | solution.py:379
  45.0 16.7 %solve1.1 = (f32[4,16,512]{2,1,0:T(8,128)S(1)}, f32[4,16,512]{2,1,0:T(8,128)S(1)}, f32[4,16,512]{2,1,0:T(8,128)S(1)}, f32[4,16,512]{2,1,0:T(8,128)S(1)}) custom-call(f32[2,4,16,512]{3,2,1,0:T(8,128)S(1)} %get-tuple-element.31.refs_0_, f32[2,4,16,512]{3,2,1,0:T(8,128)S(1)} %collective-permute-done.10.refs_1_, ...), custom_call_target="tpu_custom_call" | custom-call | tf_op jit(solution)/shard_map/solve1/pallas_call | solution.py:246
  61.8 0.7 copy-done.4
  62.5 0.0 collective-permute-start.18
  62.5 1.8 %collective-permute-start.19 = (f32[4,16,512]{2,1,0:T(8,128)S(1)}, f32[4,16,512]{2,1,0:T(8,128)S(1)}, u32[]{:S(2)}, u32[]{:S(2)}) collective-permute-start(f32[4,16,512]{2,1,0:T(8,128)S(1)} %get-tuple-element.38), channel_id=1, source_target_pairs={{0,3},{1,2},{2,1},{3,0},{4,7},{5,6},{6,5},{7,4},{8,11},{9,10},{10,... | collective-permute-start | bytes 393224 | tf_op jit(solution)/shard_map/ppermute | solution.py:370
  64.3 16.7 %solve0.1 = (f32[4,16,512]{2,1,0:T(8,128)S(1)}, f32[4,16,512]{2,1,0:T(8,128)S(1)}, f32[4,16,512]{2,1,0:T(8,128)S(1)}, f32[4,16,512]{2,1,0:T(8,128)S(1)}) custom-call(f32[2,4,16,512]{3,2,1,0:T(8,128)S(1)} %get-tuple-element.23.refs_0_, f32[2,4,16,512]{3,2,1,0:T(8,128)S(1)} %collective-permute-done.refs_1_, ...), custom_call_target="tpu_custom_call" | custom-call | tf_op jit(solution)/shard_map/solve0/pallas_call | solution.py:246
  81.0 0.6 copy-done.5
  81.7 0.3 collective-permute-start.7
  82.0 0.2 collective-permute-start.8
  82.1 1.4 %collective-permute-start.9 = (f32[4,16,512]{2,1,0:T(8,128)S(1)}, f32[4,16,512]{2,1,0:T(8,128)S(1)}, u32[]{:S(2)}, u32[]{:S(2)}) collective-permute-start(f32[4,16,512]{2,1,0:T(8,128)S(1)} %get-tuple-element.30), channel_id=1, source_target_pairs={{0,3},{1,2},{2,1},{3,0},{4,7},{5,6},{6,5},{7,4},{8,11},{9,10},{10,... | collective-permute-start | bytes 393224 | tf_op jit(solution)/shard_map/ppermute | solution.py:370
  83.6 11.7 %all_to_all.10.sums_ref = f32[16,8,128]{2,1,0:T(8,128)} all-to-all(f32[16,8,128]{2,1,0:T(8,128)S(1)} %broadcast_in_dim.2), channel_id=1, replica_groups=mesh['parts'=2,'gz'=16] {'gz'}, dimensions={0} | all-to-all | bytes 131072 | tf_op jit(solution)/shard_map/all_to_all | solution.py:399
  95.4 0.6 copy-done.10
  96.0 0.0 copy-done.11
  96.0 0.0 copy-done.12
  96.1 0.0 copy-done.13
  96.1 0.0 copy-done.14
  96.2 2.7 %weigh_faces.1 = (f32[16,4,512]{2,1,0:T(4,128)}, f32[2,128]{1,0:T(2,128)}) custom-call(f32[16,8,128]{2,1,0:T(8,128)} %all_to_all.10.sums_ref, f32[4,16,512]{2,1,0:T(8,128)} %copy-done.5, f32[4,16,512]{2,1,0:T(8,128)} %copy-done.12, f32[4,16,512]{2,1,0:T(8,128)} %copy-done.13, f32[4,16,512]{2,1,0:T(8,128)} %copy-done.14, f32[4,16,512]{2,1,0:T(8,128)} %copy-done.4, ...), custom_call_target="tpu_custom_call" | custom-call | tf_op jit(solution)/shard_map/weigh_faces/pallas_call | solution.py:293
  98.8 3.5 %all-to-all-start.1 = ((f32[16,4,512]{2,1,0:T(4,128)}), f32[16,4,512]{2,1,0:T(4,128)S(1)}, u32[]{:S(2)}, u32[]{:S(2)}) async-start(f32[16,4,512]{2,1,0:T(4,128)} %get-tuple-element.41), calls=%async_computation.1 | async-start | bytes 262144 | tf_op jit(solution)/shard_map/all_to_all | solution.py:402
  102.4 0.0 copy-start.15
  102.4 0.0 copy-start.2
  102.4 32.9 %gather_adjoint.1 = f32[8,4,16,512]{3,2,1,0:T(8,128)} custom-call(f32[4,16,512]{2,1,0:T(8,128)} %copy-done.5, f32[4,16,512]{2,1,0:T(8,128)} %copy-done.12, f32[4,16,512]{2,1,0:T(8,128)} %copy-done.13, f32[4,16,512]{2,1,0:T(8,128)} %copy-done.14, f32[4,16,512]{2,1,0:T(8,128)} %copy-done.4, f32[4,16,512]{2,1,0:T(8,128)} %copy-done.9, ...), custom_call_target="tpu_custom_call" | custom-call | tf_op jit(solution)/shard_map/gather_adjoint/pallas_call | solution.py:330
  135.3 0.0 copy-start.6
  135.4 0.6 slice_reduce_fusion
  136.1 0.2 copy-done.6
  136.3 1.4 %control.1 = f32[32,512]{1,0:T(8,128)} custom-call(f32[64,512]{1,0:T(8,128)S(1)} %reshape.10.face_ref, f32[16,32,64]{2,1,0:T(8,128)S(1)} %copy-done.6, f32[512,512]{1,0:T(8,128)S(1)} %copy-done.2), custom_call_target="tpu_custom_call" | custom-call | tf_op jit(solution)/shard_map/control/pallas_call | solution.py:353
  (38 shorter events, 0.1 us)
Async XLA Ops:
  0.6 1.2 copy-start
  1.9 1.2 copy-start.1
  3.1 0.9 copy-start.3
  4.0 0.7 copy-start.7
  4.7 0.7 copy-start.8
  8.5 7.8 %collective-permute-start.10 = (f32[2,4,16,512]{3,2,1,0:T(8,128)S(1)}, f32[2,4,16,512]{3,2,1,0:T(8,128)S(1)}, u32[]{:S(2)}, u32[]{:S(2)}) collective-permute-start(f32[2,4,16,512]{3,2,1,0:T(8,128)S(1)} %get-tuple-element.32), channel_id=1, source_target_pairs={{0,1},{1,0},{2,3},{3,2},{4,5},{5,4},{6,7},{7,6},{8,9},{9,8},{10,11... | collective-permute-start | bytes 786440 | tf_op jit(solution)/shard_map/ppermute | solution.py:370
  9.0 11.2 %collective-permute-start.11 = (f32[2,4,16,512]{3,2,1,0:T(8,128)S(1)}, f32[2,4,16,512]{3,2,1,0:T(8,128)S(1)}, u32[]{:S(2)}, u32[]{:S(2)}) collective-permute-start(f32[2,4,16,512]{3,2,1,0:T(8,128)S(1)} %get-tuple-element.33), channel_id=1, source_target_pairs={{0,2},{1,3},{2,0},{3,1},{4,6},{5,7},{6,4},{7,5},{8,10},{9,11},{10,... | collective-permute-start | bytes 786440 | tf_op jit(solution)/shard_map/ppermute | solution.py:370
  11.6 12.3 %collective-permute-start.12 = (f32[2,4,16,512]{3,2,1,0:T(8,128)S(1)}, f32[2,4,16,512]{3,2,1,0:T(8,128)S(1)}, u32[]{:S(2)}, u32[]{:S(2)}) collective-permute-start(f32[2,4,16,512]{3,2,1,0:T(8,128)S(1)} %get-tuple-element.34), channel_id=1, source_target_pairs={{0,3},{1,2},{2,1},{3,0},{4,7},{5,6},{6,5},{7,4},{8,11},{9,10},{10,... | collective-permute-start | bytes 786440 | tf_op jit(solution)/shard_map/ppermute | solution.py:370
  11.6 13.5 %collective-permute-start.13 = (f32[2,4,16,512]{3,2,1,0:T(8,128)S(1)}, f32[2,4,16,512]{3,2,1,0:T(8,128)S(1)}, u32[]{:S(2)}, u32[]{:S(2)}) collective-permute-start(f32[2,4,16,512]{3,2,1,0:T(8,128)S(1)} %get-tuple-element.31.refs_0_), channel_id=1, source_target_pairs={{2,6},{3,7},{4,0},{5,1},{6,10},{7,11},{8,4},{9,5},{10,14},{11,15},... | collective-permute-start | bytes 786440 | tf_op jit(solution)/shard_map/ppermute | solution.py:379
  16.1 13.6 %collective-permute-start = (f32[2,4,16,512]{3,2,1,0:T(8,128)S(1)}, f32[2,4,16,512]{3,2,1,0:T(8,128)S(1)}, u32[]{:S(2)}, u32[]{:S(2)}) collective-permute-start(f32[2,4,16,512]{3,2,1,0:T(8,128)S(1)} %get-tuple-element.24), channel_id=1, source_target_pairs={{0,1},{1,0},{2,3},{3,2},{4,5},{5,4},{6,7},{7,6},{8,9},{9,8},{10,11... | collective-permute-start | bytes 786440 | tf_op jit(solution)/shard_map/ppermute | solution.py:370
  16.3 17.0 %collective-permute-start.1 = (f32[2,4,16,512]{3,2,1,0:T(8,128)S(1)}, f32[2,4,16,512]{3,2,1,0:T(8,128)S(1)}, u32[]{:S(2)}, u32[]{:S(2)}) collective-permute-start(f32[2,4,16,512]{3,2,1,0:T(8,128)S(1)} %get-tuple-element.25), channel_id=1, source_target_pairs={{0,2},{1,3},{2,0},{3,1},{4,6},{5,7},{6,4},{7,5},{8,10},{9,11},{10,... | collective-permute-start | bytes 786440 | tf_op jit(solution)/shard_map/ppermute | solution.py:370
  20.2 14.9 %collective-permute-start.2 = (f32[2,4,16,512]{3,2,1,0:T(8,128)S(1)}, f32[2,4,16,512]{3,2,1,0:T(8,128)S(1)}, u32[]{:S(2)}, u32[]{:S(2)}) collective-permute-start(f32[2,4,16,512]{3,2,1,0:T(8,128)S(1)} %get-tuple-element.26), channel_id=1, source_target_pairs={{0,3},{1,2},{2,1},{3,0},{4,7},{5,6},{6,5},{7,4},{8,11},{9,10},{10,... | collective-permute-start | bytes 786440 | tf_op jit(solution)/shard_map/ppermute | solution.py:370
  23.8 12.5 %collective-permute-start.14 = (f32[2,4,16,512]{3,2,1,0:T(8,128)S(1)}, f32[2,4,16,512]{3,2,1,0:T(8,128)S(1)}, u32[]{:S(2)}, u32[]{:S(2)}) collective-permute-start(f32[2,4,16,512]{3,2,1,0:T(8,128)S(1)} %collective-permute-done.10.refs_1_), channel_id=1, source_target_pairs={{2,6},{3,7},{4,0},{5,1},{6,10},{7,11},{8,4},{9,5},{10,14},{11,15},... | collective-permute-start | bytes 786440 | tf_op jit(solution)/shard_map/ppermute | solution.py:379
  25.1 16.0 %collective-permute-start.15 = (f32[2,4,16,512]{3,2,1,0:T(8,128)S(1)}, f32[2,4,16,512]{3,2,1,0:T(8,128)S(1)}, u32[]{:S(2)}, u32[]{:S(2)}) collective-permute-start(f32[2,4,16,512]{3,2,1,0:T(8,128)S(1)} %collective-permute-done.11.refs_2_), channel_id=1, source_target_pairs={{0,4},{1,5},{4,8},{5,9},{6,2},{7,3},{8,12},{9,13},{10,6},{11,7},{1... | collective-permute-start | bytes 786440 | tf_op jit(solution)/shard_map/ppermute | solution.py:379
  29.7 15.3 %collective-permute-start.16 = (f32[2,4,16,512]{3,2,1,0:T(8,128)S(1)}, f32[2,4,16,512]{3,2,1,0:T(8,128)S(1)}, u32[]{:S(2)}, u32[]{:S(2)}) collective-permute-start(f32[2,4,16,512]{3,2,1,0:T(8,128)S(1)} %collective-permute-done.12.refs_3_), channel_id=1, source_target_pairs={{0,4},{1,5},{4,8},{5,9},{6,2},{7,3},{8,12},{9,13},{10,6},{11,7},{1... | collective-permute-start | bytes 786440 | tf_op jit(solution)/shard_map/ppermute | solution.py:379
  33.3 29.2 %collective-permute-start.3 = (f32[2,4,16,512]{3,2,1,0:T(8,128)S(1)}, f32[2,4,16,512]{3,2,1,0:T(8,128)S(1)}, u32[]{:S(2)}, u32[]{:S(2)}) collective-permute-start(f32[2,4,16,512]{3,2,1,0:T(8,128)S(1)} %get-tuple-element.23.refs_0_), channel_id=1, source_target_pairs={{2,6},{3,7},{4,0},{5,1},{6,10},{7,11},{8,4},{9,5},{10,14},{11,15},... | collective-permute-start | bytes 786440 | tf_op jit(solution)/shard_map/ppermute | solution.py:379
  35.1 27.4 %collective-permute-start.4 = (f32[2,4,16,512]{3,2,1,0:T(8,128)S(1)}, f32[2,4,16,512]{3,2,1,0:T(8,128)S(1)}, u32[]{:S(2)}, u32[]{:S(2)}) collective-permute-start(f32[2,4,16,512]{3,2,1,0:T(8,128)S(1)} %collective-permute-done.refs_1_), channel_id=1, source_target_pairs={{2,6},{3,7},{4,0},{5,1},{6,10},{7,11},{8,4},{9,5},{10,14},{11,15},... | collective-permute-start | bytes 786440 | tf_op jit(solution)/shard_map/ppermute | solution.py:379
  36.4 28.0 %collective-permute-start.5 = (f32[2,4,16,512]{3,2,1,0:T(8,128)S(1)}, f32[2,4,16,512]{3,2,1,0:T(8,128)S(1)}, u32[]{:S(2)}, u32[]{:S(2)}) collective-permute-start(f32[2,4,16,512]{3,2,1,0:T(8,128)S(1)} %collective-permute-done.1.refs_2_), channel_id=1, source_target_pairs={{0,4},{1,5},{4,8},{5,9},{6,2},{7,3},{8,12},{9,13},{10,6},{11,7},{1... | collective-permute-start | bytes 786440 | tf_op jit(solution)/shard_map/ppermute | solution.py:379
  41.1 23.2 %collective-permute-start.6 = (f32[2,4,16,512]{3,2,1,0:T(8,128)S(1)}, f32[2,4,16,512]{3,2,1,0:T(8,128)S(1)}, u32[]{:S(2)}, u32[]{:S(2)}) collective-permute-start(f32[2,4,16,512]{3,2,1,0:T(8,128)S(1)} %collective-permute-done.2.refs_3_), channel_id=1, source_target_pairs={{0,4},{1,5},{4,8},{5,9},{6,2},{7,3},{8,12},{9,13},{10,6},{11,7},{1... | collective-permute-start | bytes 786440 | tf_op jit(solution)/shard_map/ppermute | solution.py:379
  61.8 0.7 copy-start.4
  62.4 19.7 %collective-permute-start.17 = (f32[4,16,512]{2,1,0:T(8,128)S(1)}, f32[4,16,512]{2,1,0:T(8,128)S(1)}, u32[]{:S(2)}, u32[]{:S(2)}) collective-permute-start(f32[4,16,512]{2,1,0:T(8,128)S(1)} %get-tuple-element.36), channel_id=1, source_target_pairs={{0,1},{1,0},{2,3},{3,2},{4,5},{5,4},{6,7},{7,6},{8,9},{9,8},{10,11... | collective-permute-start | bytes 393224 | tf_op jit(solution)/shard_map/ppermute | solution.py:370
  62.5 32.9 %collective-permute-start.18 = (f32[4,16,512]{2,1,0:T(8,128)S(1)}, f32[4,16,512]{2,1,0:T(8,128)S(1)}, u32[]{:S(2)}, u32[]{:S(2)}) collective-permute-start(f32[4,16,512]{2,1,0:T(8,128)S(1)} %get-tuple-element.37), channel_id=1, source_target_pairs={{0,2},{1,3},{2,0},{3,1},{4,6},{5,7},{6,4},{7,5},{8,10},{9,11},{10,... | collective-permute-start | bytes 393224 | tf_op jit(solution)/shard_map/ppermute | solution.py:370
  62.5 32.8 %collective-permute-start.19 = (f32[4,16,512]{2,1,0:T(8,128)S(1)}, f32[4,16,512]{2,1,0:T(8,128)S(1)}, u32[]{:S(2)}, u32[]{:S(2)}) collective-permute-start(f32[4,16,512]{2,1,0:T(8,128)S(1)} %get-tuple-element.38), channel_id=1, source_target_pairs={{0,3},{1,2},{2,1},{3,0},{4,7},{5,6},{6,5},{7,4},{8,11},{9,10},{10,... | collective-permute-start | bytes 393224 | tf_op jit(solution)/shard_map/ppermute | solution.py:370
  81.0 0.7 copy-start.5
  81.7 13.6 %collective-permute-start.7 = (f32[4,16,512]{2,1,0:T(8,128)S(1)}, f32[4,16,512]{2,1,0:T(8,128)S(1)}, u32[]{:S(2)}, u32[]{:S(2)}) collective-permute-start(f32[4,16,512]{2,1,0:T(8,128)S(1)} %get-tuple-element.28), channel_id=1, source_target_pairs={{0,1},{1,0},{2,3},{3,2},{4,5},{5,4},{6,7},{7,6},{8,9},{9,8},{10,11... | collective-permute-start | bytes 393224 | tf_op jit(solution)/shard_map/ppermute | solution.py:370
  82.0 13.4 %collective-permute-start.8 = (f32[4,16,512]{2,1,0:T(8,128)S(1)}, f32[4,16,512]{2,1,0:T(8,128)S(1)}, u32[]{:S(2)}, u32[]{:S(2)}) collective-permute-start(f32[4,16,512]{2,1,0:T(8,128)S(1)} %get-tuple-element.29), channel_id=1, source_target_pairs={{0,2},{1,3},{2,0},{3,1},{4,6},{5,7},{6,4},{7,5},{8,10},{9,11},{10,... | collective-permute-start | bytes 393224 | tf_op jit(solution)/shard_map/ppermute | solution.py:370
  82.1 13.3 %copy-start.9 = (f32[4,16,512]{2,1,0:T(8,128)}, f32[4,16,512]{2,1,0:T(8,128)S(1)}, u32[]{:S(2)}) copy-start(f32[4,16,512]{2,1,0:T(8,128)S(1)} %collective-permute-done.17.refs_5_) | copy-start | bytes 393220
  82.1 13.2 %collective-permute-start.9 = (f32[4,16,512]{2,1,0:T(8,128)S(1)}, f32[4,16,512]{2,1,0:T(8,128)S(1)}, u32[]{:S(2)}, u32[]{:S(2)}) collective-permute-start(f32[4,16,512]{2,1,0:T(8,128)S(1)} %get-tuple-element.30), channel_id=1, source_target_pairs={{0,3},{1,2},{2,1},{3,0},{4,7},{5,6},{6,5},{7,4},{8,11},{9,10},{10,... | collective-permute-start | bytes 393224 | tf_op jit(solution)/shard_map/ppermute | solution.py:370
  95.3 0.7 copy-start.10
  95.3 0.7 copy-start.11
  95.3 0.7 copy-start.12
  95.4 0.7 copy-start.13
  95.4 0.8 copy-start.14
  98.8 37.2 %all-to-all-start.1 = ((f32[16,4,512]{2,1,0:T(4,128)}), f32[16,4,512]{2,1,0:T(4,128)S(1)}, u32[]{:S(2)}, u32[]{:S(2)}) async-start(f32[16,4,512]{2,1,0:T(4,128)} %get-tuple-element.41), calls=%async_computation.1 | async-start | bytes 262144 | tf_op jit(solution)/shard_map/all_to_all | solution.py:402
  102.4 33.0 %copy-start.15 = (f32[2,128]{1,0:T(2,128)S(1)}, f32[2,128]{1,0:T(2,128)}, u32[]{:S(2)}) copy-start(f32[2,128]{1,0:T(2,128)} %get-tuple-element.42) | copy-start | bytes 3076
  102.4 33.7 %copy-start.2 = (f32[512,512]{1,0:T(8,128)S(1)}, f32[512,512]{1,0:T(8,128)}, u32[]{:S(2)}) copy-start(f32[512,512]{1,0:T(8,128)} %constant.5.clone.x_ref) | copy-start | bytes 3145732
  135.3 1.0 copy-start.6

commit v2 on v1

v2 whole, which is shorter than its diff:
```python
import math

import jax
import jax.numpy as jnp
import numpy as np
from jax import lax
from jax.experimental import pallas as pl
from jax.experimental.pallas import tpu as pltpu
from jax.sharding import PartitionSpec as P

NR = 8
DEGREE = 4
SWEEPS = 2
MA = 512
MB = 512

STORAGE = 0.05
BETA_RISK = 0.5
LOWER_EIGEN = 0.05
UPPER_EIGEN = 2.0

TEAM = 4
STEPS = DEGREE * SWEEPS
F32 = jnp.float32
MIB = 1024 * 1024
SUM_LANES = 256


def chebyshev_constants(number_steps):
    centre = (UPPER_EIGEN + LOWER_EIGEN) / 2
    spread = (UPPER_EIGEN - LOWER_EIGEN) / 2
    quotient = centre / spread
    rho_now = 1.0 / quotient
    coefficients = []
    for position in range(number_steps):
        rho_next = 1.0 / (2.0 * quotient - rho_now)
        coefficients.append((rho_next * rho_now, 2.0 * rho_next / spread))
        rho_now = rho_next
    return (centre, coefficients)


def cosine_basis(length_total, modes):
    positions = np.arange(length_total, dtype=np.int64)
    mode_index = np.arange(modes, dtype=np.int64)
    product_index = ((2 * positions[:, None] + 1) * (2 * mode_index[None, :] + 1)) % (
        8 * length_total
    )
    angle = product_index.astype(np.float64) * (math.pi / (4 * length_total))
    return (math.sqrt(2.0 / length_total) * np.cos(angle)).astype(np.float32)


def team_place():
    return lax.rem(lax.axis_index("gz"), TEAM)


def prepare(jobs, fields):
    state, target, rock_type, log_table, obs_scale, depth_total = fields
    samples, planes, rows_y, columns = state.shape
    slots = samples // TEAM
    block = (planes, rows_y, columns)
    half, tiles = rows_y // 2, columns // 128
    flat = [(o, i, job) for o, group in enumerate(jobs) for i, job in enumerate(group)]
    count = len(flat)

    def kernel(table_ref, scale_ref, state_ref, target_ref, rock_ref, *rest):
        outs, sums_ref = rest[: len(jobs)], rest[len(jobs)]
        table, scale, state_buf, rock_buf, target_buf, mixed, sems = rest[len(jobs) + 1 :]
        place = team_place()
        first_plane = lax.axis_index("gz") * planes
        members = [slots * (place ^ m) + slot for _, _, (slot, m) in flat]
        small = [
            pltpu.make_async_copy(table_ref, table, sems.at[2, 0]),
            pltpu.make_async_copy(scale_ref, scale, sems.at[2, 1]),
            pltpu.make_async_copy(target_ref, target_buf, sems.at[2, 2]),
        ]
        for copy in small:
            copy.start()
        copies = []
        for n, member in enumerate(members):
            pair = (
                pltpu.make_async_copy(rock_ref.at[member], rock_buf.at[n], sems.at[1, n]),
                pltpu.make_async_copy(state_ref.at[member], state_buf.at[n], sems.at[0, n]),
            )
            for copy in pair:
                copy.start()
            copies.append(pair)
        sums_ref[...] = jnp.zeros(sums_ref.shape, F32)
        for copy in small:
            copy.wait()
        for n, (o, i, _) in enumerate(flat):
            for copy in copies[n]:
                copy.wait()
            member = members[n]
            values = [
                jnp.exp(jnp.full((8, columns), table[member, code], F32)) for code in range(NR)
            ]
            own_scale = scale[member]
            total = jnp.zeros((8, columns), F32)
            for p in range(planes):
                depth_weight = 1.0 + (2.0 / (depth_total - 1)) * (first_plane + p).astype(F32)
                factor = own_scale * depth_weight
                for first in range(0, rows_y, 8):
                    rows = slice(first, first + 8)
                    codes = rock_buf[n, p, rows]
                    low, mid, high = ((codes & bit) != 0 for bit in (1, 2, 4))
                    pairs = [
                        jnp.where(low, values[2 * k + 1], values[2 * k]) for k in range(NR // 2)
                    ]
                    halves = [jnp.where(mid, pairs[2 * k + 1], pairs[2 * k]) for k in range(2)]
                    gap = state_buf[n, p, rows] - target_buf[p, rows]
                    source = factor * gap
                    total = total + source * gap
                    made = (jnp.where(high, halves[1], halves[0]), source)
                    for a in range(2):
                        for c in range(tiles):
                            mixed[n % 2, p, a, c, rows] = made[a][:, c * 128 : (c + 1) * 128]
                for a in range(2):
                    for t in range(2):
                        for c in range(tiles):
                            outs[o][i, a, p, t, :, c * 128 : (c + 1) * 128] = mixed[
                                n % 2, p, a, c, pl.ds(t, half, stride=2), :
                            ]
            summed = jnp.sum(total, keepdims=True)
            sums_ref[pl.ds(member, 1), :] = jnp.broadcast_to(summed, (1, sums_ref.shape[1]))

    hbm = pl.BlockSpec(memory_space=pltpu.HBM)
    vmem = pl.BlockSpec(memory_space=pltpu.VMEM)
    results = pl.pallas_call(
        kernel,
        out_shape=[jax.ShapeDtypeStruct((len(group), 2, planes, 2, half, columns), F32) for group in jobs]
        + [jax.ShapeDtypeStruct((samples, SUM_LANES), F32)],
        in_specs=[hbm] * 5,
        out_specs=[vmem] * (len(jobs) + 1),
        scratch_shapes=[
            pltpu.SMEM(log_table.shape, F32),
            pltpu.SMEM(obs_scale.shape, F32),
            pltpu.VMEM((count,) + block, F32),
            pltpu.VMEM((count,) + block, jnp.int32),
            pltpu.VMEM(block, F32),
            pltpu.VMEM((2, planes, 2, tiles, rows_y, 128), F32),
            pltpu.SemaphoreType.DMA((3, max(count, 3))),
        ],
        compiler_params=pltpu.CompilerParams(vmem_limit_bytes=16 * MIB),
        cost_estimate=pl.CostEstimate(flops=0, bytes_accessed=count * MIB, transcendentals=0),
        name="prepare",
    )(log_table, obs_scale, state, target, rock_type)
    return results[:-1], results[-1]


def reciprocal(x):
    guess = pl.reciprocal(x, approx=True)
    return guess * (2.0 - x * guess)


def harmonic(a, b):
    return (a * b) * (2.0 * reciprocal(a + b))


def each(start, stop, body, width):
    whole = (stop - start) // width

    def group(n, carry):
        for k in range(width):
            body(start + n * width + k)
        return carry

    lax.fori_loop(0, whole, group, 0)
    for p in range(start + whole * width, stop):
        body(p)


def solve(slot, blocks, halos):
    inputs = list(blocks) + list(halos)
    planes, _, half, columns = blocks[0].shape[2:]
    near = [0, 1, 4, 5]
    halo = 2 * planes
    own = TEAM * planes
    span = own + 2 * halo
    centre, coefficients = chebyshev_constants(DEGREE)
    assert halo >= STEPS

    def kernel(*refs):
        ins, outs = refs[:8], refs[8:12]
        cond, u_a, u_b, s_a, s_b, zp, zm, yp, ym, xp, xm, t_a, t_b = refs[12:]
        place = team_place()
        column, side = lax.rem(place, 2), place // 2
        upper, lower = halo + own, 0
        near_base = jnp.where(side == 0, upper, lower)
        far_base = jnp.where(side == 0, lower, upper)
        bases = [halo + planes * (place ^ m) for m in range(TEAM)]
        bases += [near_base + planes * column, near_base + planes * (1 - column)]
        bases += [far_base + planes * column, far_base + planes * (1 - column)]
        for n, base in enumerate(bases):
            item = slot if n in near else 0
            for j in range(planes):
                for t in range(2):
                    cond[base + j, t] = jnp.maximum(ins[n][item, 0, j, t], 1e-30)
                    t_a[base + j, t] = ins[n][item, 1, j, t]

        last_row = lax.broadcasted_iota(jnp.int32, (half, columns), 0) == half - 1
        last_column = lax.broadcasted_iota(jnp.int32, (half, columns), 1) == columns - 1

        def ahead_x(v):
            return pltpu.roll(v, columns - 1, 1)

        def behind_x(v):
            return pltpu.roll(v, 1, 1)

        def ahead_y(v):
            return pltpu.roll(v, half - 1, 0)

        def behind_y(v):
            return pltpu.roll(v, 1, 0)

        def setup(p):
            even, odd = cond[p, 0], cond[p, 1]
            w_pair = harmonic(even, odd)
            w_next = jnp.where(last_row, 0.0, harmonic(odd, ahead_y(even)))
            for t, here in enumerate((even, odd)):
                w_z = harmonic(here, cond[p + 1, t])
                w_z_behind = harmonic(here, cond[p - 1, t])
                w_y = w_next if t else w_pair
                w_y_behind = w_pair if t else behind_y(w_next)
                w_x = jnp.where(last_column, 0.0, harmonic(here, ahead_x(here)))
                w_x_behind = behind_x(w_x)
                diagonal = (w_z + w_z_behind) + (w_y + w_y_behind) + (w_x + w_x_behind) + STORAGE
                inverse = reciprocal(diagonal)
                zp[p, t] = w_z * inverse
                zm[p, t] = w_z_behind * inverse
                yp[p, t] = w_y * inverse
                ym[p, t] = w_y_behind * inverse
                xp[p, t] = w_x * inverse
                xm[p, t] = w_x_behind * inverse
                scaled = t_a[p, t] * inverse
                u_a[p, t] = scaled
                s_a[p, t] = scaled * (1.0 / centre)

        each(1, span - 1, setup, 2)

        s_now, s_next, u_now, u_next, t_now, t_next = s_a, s_b, u_a, u_b, t_a, t_b
        for step in range(STEPS - 1):
            position = step % DEGREE
            if position + 1 < DEGREE:
                keep, mix = coefficients[position]
            else:
                keep, mix = 0.0, 1.0 / centre
            last = step == STEPS - 2

            def advance(p):
                even, odd = s_now[p, 0], s_now[p, 1]
                for t, s in enumerate((even, odd)):
                    ahead = ahead_y(even) if t else odd
                    behind = even if t else behind_y(odd)
                    moved = zp[p, t] * s_now[p + 1, t] + zm[p, t] * s_now[p - 1, t]
                    moved += yp[p, t] * ahead + ym[p, t] * behind
                    moved += xp[p, t] * ahead_x(s) + xm[p, t] * behind_x(s)
                    new_u = (u_now[p, t] - s) + moved
                    new_s = mix * new_u if keep == 0.0 else keep * s + mix * new_u
                    if not last:
                        u_next[p, t] = new_u
                        s_next[p, t] = new_s
                    if step == 0:
                        t_next[p, t] = s + new_s
                    elif step % 2 == 0:
                        t_next[p, t] = t_now[p, t] + (s + new_s)

            margin = halo - (STEPS - 2 - step)
            each(margin, span - margin, advance, 4)
            s_now, s_next, u_now, u_next = s_next, s_now, u_next, u_now
            if step % 2 == 0:
                t_now, t_next = t_next, t_now

        for m in range(TEAM):
            base = halo + planes * (place ^ m)
            for j in range(planes):
                for t in range(2):
                    outs[m][j, t] = t_now[base + j, t]

    vmem = pl.BlockSpec(memory_space=pltpu.VMEM)
    field = pltpu.VMEM((span, 2, half, columns), F32)
    return pl.pallas_call(
        kernel,
        out_shape=[jax.ShapeDtypeStruct((planes, 2, half, columns), F32)] * TEAM,
        in_specs=[vmem] * 8,
        out_specs=[vmem] * TEAM,
        scratch_shapes=[field] * 13,
        compiler_params=pltpu.CompilerParams(vmem_limit_bytes=32 * MIB),
        cost_estimate=pl.CostEstimate(flops=0, bytes_accessed=22 * MIB, transcendentals=0),
        name=f"solve{slot}",
    )(*inputs)


def weigh_faces(pieces, sums, cells):
    slots = len(pieces)
    planes, _, _, columns = pieces[0][0].shape
    slabs, samples, _ = sums.shape

    def kernel(sums_ref, *refs):
        faces = refs[: slots * TEAM]
        face_ref, moments_ref, weights = refs[slots * TEAM :]
        place = team_place()
        misfit = jnp.sum(sums_ref[...], axis=0)[:, :128] * (1.0 / (2.0 * cells))
        mean = jnp.sum(misfit, axis=0, keepdims=True) * (1.0 / samples)
        deviation = misfit - mean
        variance = jnp.sum(deviation * deviation, axis=0, keepdims=True) * (1.0 / samples)
        lane = lax.broadcasted_iota(jnp.int32, (1, 128), 1)
        moments_ref[...] = jnp.where(lane == 0, mean, variance)
        weights[...] = 1.0 + 2.0 * BETA_RISK * deviation
        for j in range(planes):
            face = jnp.zeros((1, columns), F32)
            for slot in range(slots):
                for m in range(TEAM):
                    row = weights[pl.ds(slots * (place ^ m) + slot, 1), :]
                    wide = jnp.concatenate([row] * (columns // 128), axis=1)
                    face = face + wide * faces[slot * TEAM + m][j, 0, 0:1, :]
            for d in range(slabs):
                face_ref[d, j : j + 1, :] = face

    vmem = pl.BlockSpec(memory_space=pltpu.VMEM)
    return pl.pallas_call(
        kernel,
        out_shape=[
            jax.ShapeDtypeStruct((slabs, planes, columns), F32),
            jax.ShapeDtypeStruct((1, 128), F32),
        ],
        in_specs=[vmem] * (1 + slots * TEAM),
        out_specs=[vmem, vmem],
        scratch_shapes=[pltpu.VMEM((samples, 128), F32)],
        compiler_params=pltpu.CompilerParams(vmem_limit_bytes=24 * MIB),
        name="weigh_faces",
    )(sums, *[piece for group in pieces for piece in group])


def gather_adjoint(pieces):
    slots = len(pieces)
    planes, _, half, columns = pieces[0][0].shape
    tiles = columns // 128
    block = (planes, 2 * half, columns)

    def kernel(*refs):
        blocks, out, held, mixed, sems = refs[: slots * TEAM], *refs[slots * TEAM :]
        place = team_place()
        copies = []
        for slot in range(slots):
            for m in range(TEAM):
                i = slot * TEAM + m
                for j in range(planes):
                    for t in range(2):
                        for c in range(tiles):
                            mixed[i % 2, j, c, pl.ds(t, half, stride=2), :] = blocks[i][
                                j, t, :, c * 128 : (c + 1) * 128
                            ]
                    for c in range(tiles):
                        held[i, j, :, c * 128 : (c + 1) * 128] = mixed[i % 2, j, c]
                copy = pltpu.make_async_copy(
                    held.at[i], out.at[slots * (place ^ m) + slot], sems.at[i]
                )
                copy.start()
                copies.append(copy)
        for copy in copies:
            copy.wait()

    return pl.pallas_call(
        kernel,
        out_shape=jax.ShapeDtypeStruct((slots * TEAM,) + block, F32),
        in_specs=[pl.BlockSpec(memory_space=pltpu.VMEM)] * (slots * TEAM),
        out_specs=pl.BlockSpec(memory_space=pltpu.HBM),
        scratch_shapes=[
            pltpu.VMEM((slots * TEAM,) + block, F32),
            pltpu.VMEM((2, planes, tiles, 2 * half, 128), F32),
            pltpu.SemaphoreType.DMA((slots * TEAM,)),
        ],
        compiler_params=pltpu.CompilerParams(vmem_limit_bytes=16 * MIB),
        cost_estimate=pl.CostEstimate(flops=0, bytes_accessed=4 * MIB, transcendentals=0),
        name="gather_adjoint",
    )(*[piece for group in pieces for piece in group])


def control(faces, basis_z, basis_x, own_count):
    depth_total, columns = faces.shape

    def kernel(face_ref, z_ref, x_ref, out_ref):
        own_modes = z_ref[lax.axis_index("gz")]
        along_z = jnp.dot(
            own_modes, face_ref[...], precision=lax.Precision.HIGHEST, preferred_element_type=F32
        )
        out_ref[...] = jnp.dot(
            along_z, x_ref[...], precision=lax.Precision.HIGHEST, preferred_element_type=F32
        )

    vmem = pl.BlockSpec(memory_space=pltpu.VMEM)
    return pl.pallas_call(
        kernel,
        out_shape=jax.ShapeDtypeStruct((own_count, basis_x.shape[1]), F32),
        in_specs=[vmem] * 3,
        out_specs=vmem,
        compiler_params=pltpu.CompilerParams(vmem_limit_bytes=16 * MIB),
        name="control",
    )(faces, basis_z, basis_x)


def on_device(state, target, rock_type, log_table, obs_scale):
    samples, planes, rows_y, columns = state.shape
    slabs = lax.axis_size("gz")
    slots = samples // TEAM
    depth_total = planes * slabs

    def swap(value, m):
        return lax.ppermute(value, "gz", [(i, i ^ m) for i in range(slabs)])

    def along(value, outward):
        pairs = []
        for i in range(slabs):
            side = (i % TEAM) // 2
            to = i + TEAM if (side == 1) == outward else i - TEAM
            if 0 <= to < slabs:
                pairs.append((i, to))
        return lax.ppermute(value, "gz", pairs)

    fields = (state, target, rock_type, log_table, obs_scale, depth_total)
    sums, far = [], []
    for slot in range(slots):
        blocks, slot_sums = prepare([[(slot, 2)], [(slot, 3)]], fields)
        sums.append(slot_sums)
        far.append([swap(blocks[0], 2), swap(blocks[1], 3)])
    blocks, near_sums = prepare(
        [[(slot, m) for slot in range(slots)] for m in range(2)], fields
    )
    sums.append(near_sums)
    near = [blocks[0], swap(blocks[1], 1)]
    near_halo = [along(block, True) for block in near]
    pieces = []
    for slot in range(slots):
        far_halo = [along(block, False) for block in far[slot]]
        solved = solve(slot, near + far[slot], near_halo + far_halo)
        pieces.append([solved[0]] + [swap(solved[m], m) for m in (1, 2, 3)])

    local_sums = sum(sums[1:], sums[0])
    spread_sums = jnp.broadcast_to(local_sums[None], (slabs,) + local_sums.shape)
    all_sums = lax.all_to_all(spread_sums, "gz", split_axis=0, concat_axis=0, tiled=True)

    faces, moments = weigh_faces(pieces, all_sums, depth_total * rows_y * columns)
    faces = lax.all_to_all(faces, "gz", split_axis=0, concat_axis=0, tiled=True)
    adjoint = gather_adjoint(pieces)
    gradient = control(
        faces.reshape(depth_total, columns),
        jnp.asarray(cosine_basis(depth_total, MA).T.reshape(slabs, MA // slabs, depth_total)),
        jnp.asarray(cosine_basis(columns, MB)),
        MA // slabs,
    )
    return (adjoint, gradient, moments[0, :2])


def solution(mesh):
    return jax.shard_map(
        on_device,
        mesh=mesh,
        in_specs=(
            P("parts", "gz", None, None),
            P(("parts", "gz"), None, None),
            P("parts", "gz", None, None),
            P("parts", None),
            P("parts"),
        ),
        out_specs=(P("parts", "gz", None, None), P(("parts", "gz"), None), P("parts")),
        check_vma=False,
    )
```

time: 138 us -> 95.3 us (0.69)
  Pallas kernels: 76.8 us -> 28.9 us
  waiting for transfers between devices: 4.08 us -> 18.5 us
  blocking collectives: 11.7 us -> 0 us
  starting transfers between devices: 36.5 us -> 40.6 us
  local copies, waits for them, and re-layouts: 7.69 us -> 5.92 us
    pallas_call x1, Pallas kernels: 32.9 us -> 1.05 us  [gather_adjoint(): pl.pallas_call(kernel, out_shape=jax.ShapeDtypeStruct((slots * TEAM,) + b...]
    pallas_call x4 -> x5, Pallas kernels: 39.7 us -> 25.7 us  [the longest x2 20.5 us: solve(): pl.pallas_call(kernel, out_shape=[jax.ShapeDtypeStruct((planes, 2, half,...]
    all_to_all x1 -> x0, blocking collectives: 11.7 us -> none  [on_device(): lax.all_to_all(spread_sums, 'gz', split_axis=0, concat_axis=0, tiled=True)]
    ppermute x12 -> x11, waiting for transfers between devices: 4.06 us -> 12.2 us  [swap(): return lax.ppermute(value, 'gz', [(i, i ^ m) for i in range(slabs)])]
    all_to_all x1, waiting for transfers between devices: 0.01 us -> 6.34 us  [on_device(): faces = lax.all_to_all(faces, 'gz', split_axis=0, concat_axis=0, tiled=True)]
    ppermute x8 -> x6, starting transfers between devices: 21.9 us -> 17.7 us  [along(): return lax.ppermute(value, 'gz', pairs)]
    all_to_all x0 -> x1, starting transfers between devices: none -> 3.77 us  [on_device(): lax.all_to_all(spread_sums, 'gz', split_axis=0, concat_axis=0, tiled=True)]
    unnamed x32 -> x14, local copies, waits for them, and re-layouts: 7.01 us -> 4.7 us
  transfers between devices with their start and end apart: 21 -> 19, of which waited for: 2 -> 7; matrix products, arithmetic and copies ran while one was open for 0% -> 1% of each run, Pallas kernels for 50% -> 26%
where the time goes in v2:
time: 95.3 us; the launch traced here: 94.7 us
  starting transfers between devices  40.6 us (43%)
  Pallas kernels  28.9 us (30%)
  waiting for transfers between devices  18.5 us (19%)
  local copies, waits for them, and re-layouts  5.92 us (6%)
    pallas_call x2, Pallas kernels, solve(): pl.pallas_call(kernel, out_shape=[jax.ShapeDtypeStruct((planes, 2, half,...  20.5 us
    ppermute x6, starting transfers between devices, along(): return lax.ppermute(value, 'gz', pairs)  17.7 us
    ppermute x11, starting transfers between devices, swap(): return lax.ppermute(value, 'gz', [(i, i ^ m) for i in range(slabs)])  13.2 us
    ppermute x11, waiting for transfers between devices, swap(): return lax.ppermute(value, 'gz', [(i, i ^ m) for i in range(slabs)])  12.2 us
    all_to_all x1, waiting for transfers between devices, on_device(): faces = lax.all_to_all(faces, 'gz', split_axis=0, concat_axis=0, tiled=True)  6.34 us
    all_to_all x1, starting transfers between devices, on_device(): faces = lax.all_to_all(faces, 'gz', split_axis=0, concat_axis=0, tiled=True)  5.83 us
    pallas_call x3, Pallas kernels, prepare(): pl.pallas_call(kernel, out_shape=[jax.ShapeDtypeStruct((len(group), 2, pl...  5.12 us
    unnamed x14, local copies, waits for them, and re-layouts  4.7 us
  transfers between devices with their start and end apart: 19, of which 7 were waited for; matrix products, arithmetic and copies ran while one was open for 1% of the time, Pallas kernels for 26%

profile of v2, /device:TPU:0, one launch (start us, length us, event | category | flops | bytes accessed | tf_op | source)
XLA Modules:
  0.0 94.7 jit_solution(17142282697408850799)
XLA Ops:
  0.6 1.2 %copy-done = f32[8,4,16,512]{3,2,1,0:T(8,128)S(1)} copy-done((f32[8,4,16,512]{3,2,1,0:T(8,128)S(1)}, f32[8,4,16,512]{3,2,1,0:T(8,128)}, u32[]{:S(2)}) %copy-start) | copy-done | bytes 1048600
  1.9 1.2 %copy-done.1 = s32[8,4,16,512]{3,2,1,0:T(8,128)S(1)} copy-done((s32[8,4,16,512]{3,2,1,0:T(8,128)S(1)}, s32[8,4,16,512]{3,2,1,0:T(8,128)}, u32[]{:S(2)}) %copy-start.1) | copy-done | bytes 1048600
  3.1 0.9 copy-done.2
  4.0 0.7 copy-done.5
  4.7 0.7 copy-done.6
  5.3 2.5 %prepare.3 = (f32[2,2,4,2,8,512]{5,4,3,2,1,0:T(8,128)S(1)}, f32[2,2,4,2,8,512]{5,4,3,2,1,0:T(8,128)S(1)}, f32[8,256]{1,0:T(8,128)S(1)}) custom-call(f32[8,8]{1,0:T(8,128)S(1)} %copy-done.5, f32[8]{0:T(128)S(1)} %copy-done.6, f32[8,4,16,512]{3,2,1,0:T(8,128)S(1)} %copy-done, f32[4,16,512]{2,1,0:T(8,128)S(1)} %copy-done.2, s32[8,4,16,512]{3,2,1,0:T(8,128)S(1)} %copy-done.1), custom_call_target="tpu_custom_call" | custom-call | bytes 4194304 | tf_op jit(solution)/shard_map/prepare/pallas_call | solution.py:128
  7.8 0.5 collective-permute-start
  8.3 1.3 %prepare.5 = (f32[1,2,4,2,8,512]{5,4,3,2,1,0:T(8,128)S(1)}, f32[1,2,4,2,8,512]{5,4,3,2,1,0:T(8,128)S(1)}, f32[8,256]{1,0:T(8,128)S(1)}) custom-call(f32[8,8]{1,0:T(8,128)S(1)} %copy-done.5, f32[8]{0:T(128)S(1)} %copy-done.6, f32[8,4,16,512]{3,2,1,0:T(8,128)S(1)} %copy-done, f32[4,16,512]{2,1,0:T(8,128)S(1)} %copy-done.2, s32[8,4,16,512]{3,2,1,0:T(8,128)S(1)} %copy-done.1), custom_call_target="tpu_custom_call" | custom-call | bytes 2097152 | tf_op jit(solution)/shard_map/prepare/pallas_call | solution.py:128
  9.7 2.6 %collective-permute-start.10 = (f32[1,2,4,2,8,512]{5,4,3,2,1,0:T(8,128)S(1)}, f32[1,2,4,2,8,512]{5,4,3,2,1,0:T(8,128)S(1)}, u32[]{:S(2)}, u32[]{:S(2)}) collective-permute-start(f32[1,2,4,2,8,512]{5,4,3,2,1,0:T(8,128)S(1)} %get-tuple-element.30), channel_id=1, source_target_pairs={{0,2},{1,3},{2,0},{3,1},{4,6},{5,7},{6,4},{7,5},{8,10},{9,11},{10,... | collective-permute-start | bytes 786440 | tf_op jit(solution)/shard_map/ppermute | solution.py:409
  12.3 1.3 %collective-permute-start.3 = (f32[2,2,4,2,8,512]{5,4,3,2,1,0:T(8,128)S(1)}, f32[2,2,4,2,8,512]{5,4,3,2,1,0:T(8,128)S(1)}, u32[]{:S(2)}, u32[]{:S(2)}) collective-permute-start(f32[2,2,4,2,8,512]{5,4,3,2,1,0:T(8,128)S(1)} %get-tuple-element.22.refs_0_), channel_id=1, source_target_pairs={{2,6},{3,7},{4,0},{5,1},{6,10},{7,11},{8,4},{9,5},{10,14},{11,15},... | collective-permute-start | bytes 1572872 | tf_op jit(solution)/shard_map/ppermute | solution.py:418
  13.5 2.3 %collective-permute-start.11 = (f32[1,2,4,2,8,512]{5,4,3,2,1,0:T(8,128)S(1)}, f32[1,2,4,2,8,512]{5,4,3,2,1,0:T(8,128)S(1)}, u32[]{:S(2)}, u32[]{:S(2)}) collective-permute-start(f32[1,2,4,2,8,512]{5,4,3,2,1,0:T(8,128)S(1)} %get-tuple-element.31), channel_id=1, source_target_pairs={{0,3},{1,2},{2,1},{3,0},{4,7},{5,6},{6,5},{7,4},{8,11},{9,10},{10,... | collective-permute-start | bytes 786440 | tf_op jit(solution)/shard_map/ppermute | solution.py:409
  15.9 1.3 %prepare.4 = (f32[1,2,4,2,8,512]{5,4,3,2,1,0:T(8,128)S(1)}, f32[1,2,4,2,8,512]{5,4,3,2,1,0:T(8,128)S(1)}, f32[8,256]{1,0:T(8,128)S(1)}) custom-call(f32[8,8]{1,0:T(8,128)S(1)} %copy-done.5, f32[8]{0:T(128)S(1)} %copy-done.6, f32[8,4,16,512]{3,2,1,0:T(8,128)S(1)} %copy-done, f32[4,16,512]{2,1,0:T(8,128)S(1)} %copy-done.2, s32[8,4,16,512]{3,2,1,0:T(8,128)S(1)} %copy-done.1), custom_call_target="tpu_custom_call" | custom-call | bytes 2097152 | tf_op jit(solution)/shard_map/prepare/pallas_call | solution.py:128
  17.2 0.6 collective-permute-start.1
  17.8 0.0 collective-permute-done.refs_1_
  17.8 1.3 %collective-permute-start.4 = (f32[2,2,4,2,8,512]{5,4,3,2,1,0:T(8,128)S(1)}, f32[2,2,4,2,8,512]{5,4,3,2,1,0:T(8,128)S(1)}, u32[]{:S(2)}, u32[]{:S(2)}) collective-permute-start(f32[2,2,4,2,8,512]{5,4,3,2,1,0:T(8,128)S(1)} %collective-permute-done.refs_1_), channel_id=1, source_target_pairs={{2,6},{3,7},{4,0},{5,1},{6,10},{7,11},{8,4},{9,5},{10,14},{11,15},... | collective-permute-start | bytes 1572872 | tf_op jit(solution)/shard_map/ppermute | solution.py:418
  19.1 0.3 collective-permute-done.10.refs_2_
  19.4 3.1 %collective-permute-start.2 = (f32[1,2,4,2,8,512]{5,4,3,2,1,0:T(8,128)S(1)}, f32[1,2,4,2,8,512]{5,4,3,2,1,0:T(8,128)S(1)}, u32[]{:S(2)}, u32[]{:S(2)}) collective-permute-start(f32[1,2,4,2,8,512]{5,4,3,2,1,0:T(8,128)S(1)} %get-tuple-element.25), channel_id=1, source_target_pairs={{0,3},{1,2},{2,1},{3,0},{4,7},{5,6},{6,5},{7,4},{8,11},{9,10},{10,... | collective-permute-start | bytes 786440 | tf_op jit(solution)/shard_map/ppermute | solution.py:409
  22.5 2.0 %collective-permute-done.11.refs_3_ = f32[1,2,4,2,8,512]{5,4,3,2,1,0:T(8,128)S(1)} collective-permute-done((f32[1,2,4,2,8,512]{5,4,3,2,1,0:T(8,128)S(1)}, f32[1,2,4,2,8,512]{5,4,3,2,1,0:T(8,128)S(1)}, u32[]{:S(2)}, u32[]{:S(2)}) %collective-permute-start.11) | collective-permute-done | bytes 262176 | tf_op jit(solution)/shard_map/ppermute | solution.py:409
  24.6 3.5 %collective-permute-start.12 = (f32[1,2,4,2,8,512]{5,4,3,2,1,0:T(8,128)S(1)}, f32[1,2,4,2,8,512]{5,4,3,2,1,0:T(8,128)S(1)}, u32[]{:S(2)}, u32[]{:S(2)}) collective-permute-start(f32[1,2,4,2,8,512]{5,4,3,2,1,0:T(8,128)S(1)} %collective-permute-done.10.refs_2_), channel_id=1, source_target_pairs={{0,4},{1,5},{4,8},{5,9},{6,2},{7,3},{8,12},{9,13},{10,6},{11,7},{1... | collective-permute-start | bytes 786440 | tf_op jit(solution)/shard_map/ppermute | solution.py:418
  28.1 2.6 %collective-permute-done.1.refs_2_ = f32[1,2,4,2,8,512]{5,4,3,2,1,0:T(8,128)S(1)} collective-permute-done((f32[1,2,4,2,8,512]{5,4,3,2,1,0:T(8,128)S(1)}, f32[1,2,4,2,8,512]{5,4,3,2,1,0:T(8,128)S(1)}, u32[]{:S(2)}, u32[]{:S(2)}) %collective-permute-start.1) | collective-permute-done | bytes 262176 | tf_op jit(solution)/shard_map/ppermute | solution.py:409
  30.7 3.9 %collective-permute-start.13 = (f32[1,2,4,2,8,512]{5,4,3,2,1,0:T(8,128)S(1)}, f32[1,2,4,2,8,512]{5,4,3,2,1,0:T(8,128)S(1)}, u32[]{:S(2)}, u32[]{:S(2)}) collective-permute-start(f32[1,2,4,2,8,512]{5,4,3,2,1,0:T(8,128)S(1)} %collective-permute-done.11.refs_3_), channel_id=1, source_target_pairs={{0,4},{1,5},{4,8},{5,9},{6,2},{7,3},{8,12},{9,13},{10,6},{11,7},{1... | collective-permute-start | bytes 786440 | tf_op jit(solution)/shard_map/ppermute | solution.py:418
  34.6 1.2 %collective-permute-done.2.refs_3_ = f32[1,2,4,2,8,512]{5,4,3,2,1,0:T(8,128)S(1)} collective-permute-done((f32[1,2,4,2,8,512]{5,4,3,2,1,0:T(8,128)S(1)}, f32[1,2,4,2,8,512]{5,4,3,2,1,0:T(8,128)S(1)}, u32[]{:S(2)}, u32[]{:S(2)}) %collective-permute-start.2) | collective-permute-done | bytes 262176 | tf_op jit(solution)/shard_map/ppermute | solution.py:409
  35.8 4.2 %collective-permute-start.5 = (f32[1,2,4,2,8,512]{5,4,3,2,1,0:T(8,128)S(1)}, f32[1,2,4,2,8,512]{5,4,3,2,1,0:T(8,128)}, u32[]{:S(2)}, u32[]{:S(2)}) collective-permute-start(f32[1,2,4,2,8,512]{5,4,3,2,1,0:T(8,128)S(1)} %collective-permute-done.1.refs_2_), channel_id=1, source_target_pairs={{0,4},{1,5},{4,8},{5,9},{6,2},{7,3},{8,12},{9,13},{10,6},{11,7},{1... | collective-permute-start | bytes 786440 | tf_op jit(solution)/shard_map/ppermute | solution.py:418
  40.0 0.0 collective-permute-done.3.refs_4_
  40.0 3.5 %collective-permute-start.6 = (f32[1,2,4,2,8,512]{5,4,3,2,1,0:T(8,128)S(1)}, f32[1,2,4,2,8,512]{5,4,3,2,1,0:T(8,128)}, u32[]{:S(2)}, u32[]{:S(2)}) collective-permute-start(f32[1,2,4,2,8,512]{5,4,3,2,1,0:T(8,128)S(1)} %collective-permute-done.2.refs_3_), channel_id=1, source_target_pairs={{0,4},{1,5},{4,8},{5,9},{6,2},{7,3},{8,12},{9,13},{10,6},{11,7},{1... | collective-permute-start | bytes 786440 | tf_op jit(solution)/shard_map/ppermute | solution.py:418
  43.5 0.0 collective-permute-done.12.refs_6_
  43.5 0.0 collective-permute-done.13.refs_7_
  43.5 0.0 collective-permute-done.4.refs_5_
  43.5 9.8 %solve1.1 = (f32[4,2,8,512]{3,2,1,0:T(8,128)S(1)}, f32[4,2,8,512]{3,2,1,0:T(8,128)}, f32[4,2,8,512]{3,2,1,0:T(8,128)}, f32[4,2,8,512]{3,2,1,0:T(8,128)S(1)}) custom-call(f32[2,2,4,2,8,512]{5,4,3,2,1,0:T(8,128)S(1)} %get-tuple-element.22.refs_0_, f32[2,2,4,2,8,512]{5,4,3,2,1,0:T(8,128)S(1)} %collective-permute-done.refs_1_, ...), custom_call_target="tpu_custom_call" | custom-call | bytes 23068672 | tf_op jit(solution)/shard_map/solve1/pallas_call | solution.py:281
  53.3 0.7 broadcast_in_dim.2
  54.0 3.8 %all-to-all-start = ((f32[16,8,256]{2,1,0:T(8,128)}), f32[16,8,256]{2,1,0:T(8,128)S(1)}, u32[]{:S(2)}, u32[]{:S(2)}) async-start(f32[16,8,256]{2,1,0:T(8,128)} %broadcast_in_dim.2), calls=%async_computation | async-start | bytes 262144 | tf_op jit(solution)/shard_map/all_to_all | solution.py:440
  57.7 1.9 %collective-permute-start.15 = (f32[4,2,8,512]{3,2,1,0:T(8,128)}, f32[4,2,8,512]{3,2,1,0:T(8,128)S(1)}, u32[]{:S(2)}, u32[]{:S(2)}) collective-permute-start(f32[4,2,8,512]{3,2,1,0:T(8,128)} %get-tuple-element.34), channel_id=1, source_target_pairs={{0,2},{1,3},{2,0},{3,1},{4,6},{5,7},{6,4},{7,5},{8,10},{9,11},{10,... | collective-permute-start | bytes 393224 | tf_op jit(solution)/shard_map/ppermute | solution.py:409
  59.7 0.0 collective-permute-start.16
  59.7 0.0 collective-permute-done.5.refs_6_
  59.7 0.0 collective-permute-done.6.refs_7_
  59.7 10.8 %solve0.1 = (f32[4,2,8,512]{3,2,1,0:T(8,128)S(1)}, f32[4,2,8,512]{3,2,1,0:T(8,128)}, f32[4,2,8,512]{3,2,1,0:T(8,128)}, f32[4,2,8,512]{3,2,1,0:T(8,128)}) custom-call(f32[2,2,4,2,8,512]{5,4,3,2,1,0:T(8,128)S(1)} %get-tuple-element.22.refs_0_, f32[2,2,4,2,8,512]{5,4,3,2,1,0:T(8,128)S(1)} %collective-permute-done.refs_1_, ...), custom_call_target="tpu_custom_call" | custom-call | bytes 23068672 | tf_op jit(solution)/shard_map/solve0/pallas_call | solution.py:281
  70.5 0.3 collective-permute-start.7
  70.7 1.9 %collective-permute-start.8 = (f32[4,2,8,512]{3,2,1,0:T(8,128)}, f32[4,2,8,512]{3,2,1,0:T(8,128)S(1)}, u32[]{:S(2)}, u32[]{:S(2)}) collective-permute-start(f32[4,2,8,512]{3,2,1,0:T(8,128)} %get-tuple-element.28), channel_id=1, source_target_pairs={{0,2},{1,3},{2,0},{3,1},{4,6},{5,7},{6,4},{7,5},{8,10},{9,11},{10,... | collective-permute-start | bytes 393224 | tf_op jit(solution)/shard_map/ppermute | solution.py:409
  72.6 4.6 %collective-permute-done.8.refs_2_ = f32[4,2,8,512]{3,2,1,0:T(8,128)S(1)} collective-permute-done((f32[4,2,8,512]{3,2,1,0:T(8,128)}, f32[4,2,8,512]{3,2,1,0:T(8,128)S(1)}, u32[]{:S(2)}, u32[]{:S(2)}) %collective-permute-start.8) | collective-permute-done | bytes 131104 | tf_op jit(solution)/shard_map/ppermute | solution.py:409
  77.3 1.4 %collective-permute-done.9.refs_3_ = f32[4,2,8,512]{3,2,1,0:T(8,128)S(1)} collective-permute-done((f32[4,2,8,512]{3,2,1,0:T(8,128)}, f32[4,2,8,512]{3,2,1,0:T(8,128)S(1)}, u32[]{:S(2)}, u32[]{:S(2)}) %collective-permute-start.9) | collective-permute-done | bytes 131104 | tf_op jit(solution)/shard_map/ppermute | solution.py:409
  78.7 0.7 weigh_faces.1
  79.4 5.8 %all-to-all-start.1 = ((f32[16,4,512]{2,1,0:T(4,128)}), f32[16,4,512]{2,1,0:T(4,128)S(1)}, u32[]{:S(2)}, u32[]{:S(2)}) async-start(f32[16,4,512]{2,1,0:T(4,128)} %get-tuple-element.39), calls=%async_computation.1 | async-start | bytes 262144 | tf_op jit(solution)/shard_map/all_to_all | solution.py:443
  85.3 0.0 copy-start.3
  85.3 1.1 %gather_adjoint.1 = f32[8,4,16,512]{3,2,1,0:T(8,128)} custom-call(f32[4,2,8,512]{3,2,1,0:T(8,128)S(1)} %get-tuple-element.26.refs_0_, f32[4,2,8,512]{3,2,1,0:T(8,128)S(1)} %collective-permute-done.7.refs_1_, f32[4,2,8,512]{3,2,1,0:T(8,128)S(1)} %collective-permute-done.8.refs_2_, f32[4,2,8,512]{3,2,1,0:T(8,128)S(1)} %collective-permute-done.9.refs_3_, ...), custom_call_target="tpu_custom_call" | custom-call | bytes 4194304 | tf_op jit(solution)/shard_map/gather_adjoint/pallas_call | solution.py:363
  86.3 0.0 copy-start.4
  86.4 0.5 slice_bitcast_fusion
  86.9 6.3 %all-to-all-done.1 = f32[16,4,512]{2,1,0:T(4,128)S(1)} async-done(((f32[16,4,512]{2,1,0:T(4,128)}), f32[16,4,512]{2,1,0:T(4,128)S(1)}, u32[]{:S(2)}, u32[]{:S(2)}) %all-to-all-start.1) | async-done | bytes 131104 | tf_op jit(solution)/shard_map/all_to_all | solution.py:443
  93.3 1.4 %control.1 = f32[32,512]{1,0:T(8,128)} custom-call(f32[64,512]{1,0:T(8,128)S(1)} %reshape.10.face_ref, f32[16,32,64]{2,1,0:T(8,128)S(1)} %copy-done.4, f32[512,512]{1,0:T(8,128)S(1)} %copy-done.3), custom_call_target="tpu_custom_call" | custom-call | tf_op jit(solution)/shard_map/control/pallas_call | solution.py:392
  (16 shorter events, 0.1 us)
Async XLA Ops:
  0.6 1.2 %copy-start = (f32[8,4,16,512]{3,2,1,0:T(8,128)S(1)}, f32[8,4,16,512]{3,2,1,0:T(8,128)}, u32[]{:S(2)}) copy-start(f32[8,4,16,512]{3,2,1,0:T(8,128)} %state_ref.5) | copy-start | bytes 3145732
  1.9 1.2 %copy-start.1 = (s32[8,4,16,512]{3,2,1,0:T(8,128)S(1)}, s32[8,4,16,512]{3,2,1,0:T(8,128)}, u32[]{:S(2)}) copy-start(s32[8,4,16,512]{3,2,1,0:T(8,128)} %rock_ref.5) | copy-start | bytes 3145732
  3.1 0.9 copy-start.2
  4.0 0.7 copy-start.5
  4.7 0.7 copy-start.6
  7.8 10.0 %collective-permute-start = (f32[2,2,4,2,8,512]{5,4,3,2,1,0:T(8,128)S(1)}, f32[2,2,4,2,8,512]{5,4,3,2,1,0:T(8,128)S(1)}, u32[]{:S(2)}, u32[]{:S(2)}) collective-permute-start(f32[2,2,4,2,8,512]{5,4,3,2,1,0:T(8,128)S(1)} %get-tuple-element.23), channel_id=1, source_target_pairs={{0,1},{1,0},{2,3},{3,2},{4,5},{5,4},{6,7},{7,6},{8,9},{9,8},{10,11... | collective-permute-start | bytes 1572872 | tf_op jit(solution)/shard_map/ppermute | solution.py:409
  9.7 9.8 %collective-permute-start.10 = (f32[1,2,4,2,8,512]{5,4,3,2,1,0:T(8,128)S(1)}, f32[1,2,4,2,8,512]{5,4,3,2,1,0:T(8,128)S(1)}, u32[]{:S(2)}, u32[]{:S(2)}) collective-permute-start(f32[1,2,4,2,8,512]{5,4,3,2,1,0:T(8,128)S(1)} %get-tuple-element.30), channel_id=1, source_target_pairs={{0,2},{1,3},{2,0},{3,1},{4,6},{5,7},{6,4},{7,5},{8,10},{9,11},{10,... | collective-permute-start | bytes 786440 | tf_op jit(solution)/shard_map/ppermute | solution.py:409
  12.3 27.8 %collective-permute-start.3 = (f32[2,2,4,2,8,512]{5,4,3,2,1,0:T(8,128)S(1)}, f32[2,2,4,2,8,512]{5,4,3,2,1,0:T(8,128)S(1)}, u32[]{:S(2)}, u32[]{:S(2)}) collective-permute-start(f32[2,2,4,2,8,512]{5,4,3,2,1,0:T(8,128)S(1)} %get-tuple-element.22.refs_0_), channel_id=1, source_target_pairs={{2,6},{3,7},{4,0},{5,1},{6,10},{7,11},{8,4},{9,5},{10,14},{11,15},... | collective-permute-start | bytes 1572872 | tf_op jit(solution)/shard_map/ppermute | solution.py:418
  13.5 11.0 %collective-permute-start.11 = (f32[1,2,4,2,8,512]{5,4,3,2,1,0:T(8,128)S(1)}, f32[1,2,4,2,8,512]{5,4,3,2,1,0:T(8,128)S(1)}, u32[]{:S(2)}, u32[]{:S(2)}) collective-permute-start(f32[1,2,4,2,8,512]{5,4,3,2,1,0:T(8,128)S(1)} %get-tuple-element.31), channel_id=1, source_target_pairs={{0,3},{1,2},{2,1},{3,0},{4,7},{5,6},{6,5},{7,4},{8,11},{9,10},{10,... | collective-permute-start | bytes 786440 | tf_op jit(solution)/shard_map/ppermute | solution.py:409
  17.2 13.4 %collective-permute-start.1 = (f32[1,2,4,2,8,512]{5,4,3,2,1,0:T(8,128)S(1)}, f32[1,2,4,2,8,512]{5,4,3,2,1,0:T(8,128)S(1)}, u32[]{:S(2)}, u32[]{:S(2)}) collective-permute-start(f32[1,2,4,2,8,512]{5,4,3,2,1,0:T(8,128)S(1)} %get-tuple-element.24), channel_id=1, source_target_pairs={{0,2},{1,3},{2,0},{3,1},{4,6},{5,7},{6,4},{7,5},{8,10},{9,11},{10,... | collective-permute-start | bytes 786440 | tf_op jit(solution)/shard_map/ppermute | solution.py:409
  17.8 25.7 %collective-permute-start.4 = (f32[2,2,4,2,8,512]{5,4,3,2,1,0:T(8,128)S(1)}, f32[2,2,4,2,8,512]{5,4,3,2,1,0:T(8,128)S(1)}, u32[]{:S(2)}, u32[]{:S(2)}) collective-permute-start(f32[2,2,4,2,8,512]{5,4,3,2,1,0:T(8,128)S(1)} %collective-permute-done.refs_1_), channel_id=1, source_target_pairs={{2,6},{3,7},{4,0},{5,1},{6,10},{7,11},{8,4},{9,5},{10,14},{11,15},... | collective-permute-start | bytes 1572872 | tf_op jit(solution)/shard_map/ppermute | solution.py:418
  19.4 16.4 %collective-permute-start.2 = (f32[1,2,4,2,8,512]{5,4,3,2,1,0:T(8,128)S(1)}, f32[1,2,4,2,8,512]{5,4,3,2,1,0:T(8,128)S(1)}, u32[]{:S(2)}, u32[]{:S(2)}) collective-permute-start(f32[1,2,4,2,8,512]{5,4,3,2,1,0:T(8,128)S(1)} %get-tuple-element.25), channel_id=1, source_target_pairs={{0,3},{1,2},{2,1},{3,0},{4,7},{5,6},{6,5},{7,4},{8,11},{9,10},{10,... | collective-permute-start | bytes 786440 | tf_op jit(solution)/shard_map/ppermute | solution.py:409
  24.6 19.0 %collective-permute-start.12 = (f32[1,2,4,2,8,512]{5,4,3,2,1,0:T(8,128)S(1)}, f32[1,2,4,2,8,512]{5,4,3,2,1,0:T(8,128)S(1)}, u32[]{:S(2)}, u32[]{:S(2)}) collective-permute-start(f32[1,2,4,2,8,512]{5,4,3,2,1,0:T(8,128)S(1)} %collective-permute-done.10.refs_2_), channel_id=1, source_target_pairs={{0,4},{1,5},{4,8},{5,9},{6,2},{7,3},{8,12},{9,13},{10,6},{11,7},{1... | collective-permute-start | bytes 786440 | tf_op jit(solution)/shard_map/ppermute | solution.py:418
  30.7 12.9 %collective-permute-start.13 = (f32[1,2,4,2,8,512]{5,4,3,2,1,0:T(8,128)S(1)}, f32[1,2,4,2,8,512]{5,4,3,2,1,0:T(8,128)S(1)}, u32[]{:S(2)}, u32[]{:S(2)}) collective-permute-start(f32[1,2,4,2,8,512]{5,4,3,2,1,0:T(8,128)S(1)} %collective-permute-done.11.refs_3_), channel_id=1, source_target_pairs={{0,4},{1,5},{4,8},{5,9},{6,2},{7,3},{8,12},{9,13},{10,6},{11,7},{1... | collective-permute-start | bytes 786440 | tf_op jit(solution)/shard_map/ppermute | solution.py:418
  35.8 23.9 %collective-permute-start.5 = (f32[1,2,4,2,8,512]{5,4,3,2,1,0:T(8,128)S(1)}, f32[1,2,4,2,8,512]{5,4,3,2,1,0:T(8,128)}, u32[]{:S(2)}, u32[]{:S(2)}) collective-permute-start(f32[1,2,4,2,8,512]{5,4,3,2,1,0:T(8,128)S(1)} %collective-permute-done.1.refs_2_), channel_id=1, source_target_pairs={{0,4},{1,5},{4,8},{5,9},{6,2},{7,3},{8,12},{9,13},{10,6},{11,7},{1... | collective-permute-start | bytes 786440 | tf_op jit(solution)/shard_map/ppermute | solution.py:418
  40.0 19.7 %collective-permute-start.6 = (f32[1,2,4,2,8,512]{5,4,3,2,1,0:T(8,128)S(1)}, f32[1,2,4,2,8,512]{5,4,3,2,1,0:T(8,128)}, u32[]{:S(2)}, u32[]{:S(2)}) collective-permute-start(f32[1,2,4,2,8,512]{5,4,3,2,1,0:T(8,128)S(1)} %collective-permute-done.2.refs_3_), channel_id=1, source_target_pairs={{0,4},{1,5},{4,8},{5,9},{6,2},{7,3},{8,12},{9,13},{10,6},{11,7},{1... | collective-permute-start | bytes 786440 | tf_op jit(solution)/shard_map/ppermute | solution.py:418
  53.3 19.3 %collective-permute-start.14 = (f32[4,2,8,512]{3,2,1,0:T(8,128)}, f32[4,2,8,512]{3,2,1,0:T(8,128)S(1)}, u32[]{:S(2)}, u32[]{:S(2)}) collective-permute-start(f32[4,2,8,512]{3,2,1,0:T(8,128)} %get-tuple-element.33), channel_id=1, source_target_pairs={{0,1},{1,0},{2,3},{3,2},{4,5},{5,4},{6,7},{7,6},{8,9},{9,8},{10,11... | collective-permute-start | bytes 393224 | tf_op jit(solution)/shard_map/ppermute | solution.py:409
  54.0 18.6 %all-to-all-start = ((f32[16,8,256]{2,1,0:T(8,128)}), f32[16,8,256]{2,1,0:T(8,128)S(1)}, u32[]{:S(2)}, u32[]{:S(2)}) async-start(f32[16,8,256]{2,1,0:T(8,128)} %broadcast_in_dim.2), calls=%async_computation | async-start | bytes 262144 | tf_op jit(solution)/shard_map/all_to_all | solution.py:440
  57.7 14.9 %collective-permute-start.15 = (f32[4,2,8,512]{3,2,1,0:T(8,128)}, f32[4,2,8,512]{3,2,1,0:T(8,128)S(1)}, u32[]{:S(2)}, u32[]{:S(2)}) collective-permute-start(f32[4,2,8,512]{3,2,1,0:T(8,128)} %get-tuple-element.34), channel_id=1, source_target_pairs={{0,2},{1,3},{2,0},{3,1},{4,6},{5,7},{6,4},{7,5},{8,10},{9,11},{10,... | collective-permute-start | bytes 393224 | tf_op jit(solution)/shard_map/ppermute | solution.py:409
  59.7 13.0 %collective-permute-start.16 = (f32[4,2,8,512]{3,2,1,0:T(8,128)S(1)}, f32[4,2,8,512]{3,2,1,0:T(8,128)S(1)}, u32[]{:S(2)}, u32[]{:S(2)}) collective-permute-start(f32[4,2,8,512]{3,2,1,0:T(8,128)S(1)} %get-tuple-element.35), channel_id=1, source_target_pairs={{0,3},{1,2},{2,1},{3,0},{4,7},{5,6},{6,5},{7,4},{8,11},{9,10},{10,... | collective-permute-start | bytes 393224 | tf_op jit(solution)/shard_map/ppermute | solution.py:409
  70.5 2.2 %collective-permute-start.7 = (f32[4,2,8,512]{3,2,1,0:T(8,128)}, f32[4,2,8,512]{3,2,1,0:T(8,128)S(1)}, u32[]{:S(2)}, u32[]{:S(2)}) collective-permute-start(f32[4,2,8,512]{3,2,1,0:T(8,128)} %get-tuple-element.27), channel_id=1, source_target_pairs={{0,1},{1,0},{2,3},{3,2},{4,5},{5,4},{6,7},{7,6},{8,9},{9,8},{10,11... | collective-permute-start | bytes 393224 | tf_op jit(solution)/shard_map/ppermute | solution.py:409
  70.7 6.5 %collective-permute-start.8 = (f32[4,2,8,512]{3,2,1,0:T(8,128)}, f32[4,2,8,512]{3,2,1,0:T(8,128)S(1)}, u32[]{:S(2)}, u32[]{:S(2)}) collective-permute-start(f32[4,2,8,512]{3,2,1,0:T(8,128)} %get-tuple-element.28), channel_id=1, source_target_pairs={{0,2},{1,3},{2,0},{3,1},{4,6},{5,7},{6,4},{7,5},{8,10},{9,11},{10,... | collective-permute-start | bytes 393224 | tf_op jit(solution)/shard_map/ppermute | solution.py:409
  72.6 6.1 %collective-permute-start.9 = (f32[4,2,8,512]{3,2,1,0:T(8,128)}, f32[4,2,8,512]{3,2,1,0:T(8,128)S(1)}, u32[]{:S(2)}, u32[]{:S(2)}) collective-permute-start(f32[4,2,8,512]{3,2,1,0:T(8,128)} %get-tuple-element.29), channel_id=1, source_target_pairs={{0,3},{1,2},{2,1},{3,0},{4,7},{5,6},{6,5},{7,4},{8,11},{9,10},{10,... | collective-permute-start | bytes 393224 | tf_op jit(solution)/shard_map/ppermute | solution.py:409
  79.4 13.8 %all-to-all-start.1 = ((f32[16,4,512]{2,1,0:T(4,128)}), f32[16,4,512]{2,1,0:T(4,128)S(1)}, u32[]{:S(2)}, u32[]{:S(2)}) async-start(f32[16,4,512]{2,1,0:T(4,128)} %get-tuple-element.39), calls=%async_computation.1 | async-start | bytes 262144 | tf_op jit(solution)/shard_map/all_to_all | solution.py:443
  85.3 8.0 %copy-start.3 = (f32[512,512]{1,0:T(8,128)S(1)}, f32[512,512]{1,0:T(8,128)}, u32[]{:S(2)}) copy-start(f32[512,512]{1,0:T(8,128)} %constant.5.clone.x_ref) | copy-start | bytes 3145732
  86.3 6.9 %copy-start.4 = (f32[16,32,64]{2,1,0:T(8,128)S(1)}, f32[16,32,64]{2,1,0:T(8,128)}, u32[]{:S(2)}) copy-start(f32[16,32,64]{2,1,0:T(8,128)} %constant.4.clone.z_ref) | copy-start | bytes 393220

commit v3 on v2

--- a/solution.py
+++ b/solution.py
@@ -23,7 +23,7 @@
 STEPS = DEGREE * SWEEPS
 F32 = jnp.float32
 MIB = 1024 * 1024
-SUM_LANES = 256
+LANES = 128
 
 
 def chebyshev_constants(number_steps):
@@ -53,16 +53,17 @@
     return lax.rem(lax.axis_index("gz"), TEAM)
 
 
-def prepare(jobs, fields):
-    state, target, rock_type, log_table, obs_scale, depth_total = fields
+def prepare(jobs, fields, sums_before):
+    state, target, rock_type, log_table, obs_scale = fields
     samples, planes, rows_y, columns = state.shape
     slots = samples // TEAM
     block = (planes, rows_y, columns)
     half, tiles = rows_y // 2, columns // 128
+    depth_total = planes * lax.axis_size("gz")
     flat = [(o, i, job) for o, group in enumerate(jobs) for i, job in enumerate(group)]
     count = len(flat)
 
-    def kernel(table_ref, scale_ref, state_ref, target_ref, rock_ref, *rest):
+    def kernel(before_ref, table_ref, scale_ref, state_ref, target_ref, rock_ref, *rest):
         outs, sums_ref = rest[: len(jobs)], rest[len(jobs)]
         table, scale, state_buf, rock_buf, target_buf, mixed, sems = rest[len(jobs) + 1 :]
         place = team_place()
@@ -84,7 +85,7 @@
             for copy in pair:
                 copy.start()
             copies.append(pair)
-        sums_ref[...] = jnp.zeros(sums_ref.shape, F32)
+        sums_ref[...] = before_ref[...]
         for copy in small:
             copy.wait()
         for n, (o, i, _) in enumerate(flat):
@@ -128,8 +129,8 @@
     results = pl.pallas_call(
         kernel,
         out_shape=[jax.ShapeDtypeStruct((len(group), 2, planes, 2, half, columns), F32) for group in jobs]
-        + [jax.ShapeDtypeStruct((samples, SUM_LANES), F32)],
-        in_specs=[hbm] * 5,
+        + [jax.ShapeDtypeStruct((samples, LANES), F32)],
+        in_specs=[vmem] + [hbm] * 5,
         out_specs=[vmem] * (len(jobs) + 1),
         scratch_shapes=[
             pltpu.SMEM(log_table.shape, F32),
@@ -143,7 +144,7 @@
         compiler_params=pltpu.CompilerParams(vmem_limit_bytes=16 * MIB),
         cost_estimate=pl.CostEstimate(flops=0, bytes_accessed=count * MIB, transcendentals=0),
         name="prepare",
-    )(log_table, obs_scale, state, target, rock_type)
+    )(sums_before, log_table, obs_scale, state, target, rock_type)
     return results[:-1], results[-1]
 
 
@@ -169,19 +170,35 @@
         body(p)
 
 
-def solve(slot, blocks, halos):
+def risk(sums, cells):
+    misfit = sums * (1.0 / (2.0 * cells))
+    mean = jnp.mean(misfit, axis=0, keepdims=True)
+    deviation = misfit - mean
+    variance = jnp.mean(deviation * deviation, axis=0, keepdims=True)
+    return 1.0 + 2.0 * BETA_RISK * deviation, mean, variance
+
+
+def solve(slot, blocks, halos, sums=None, faces=()):
     inputs = list(blocks) + list(halos)
+    weigh = sums is not None
+    extra = [sums, *faces] if weigh else []
+    slots = len(faces) + 1
     planes, _, half, columns = blocks[0].shape[2:]
     near = [0, 1, 4, 5]
     halo = 2 * planes
     own = TEAM * planes
     span = own + 2 * halo
+    cells = planes * lax.axis_size("gz") * 2 * half * columns
     centre, coefficients = chebyshev_constants(DEGREE)
     assert halo >= STEPS
 
     def kernel(*refs):
-        ins, outs = refs[:8], refs[8:12]
-        cond, u_a, u_b, s_a, s_b, zp, zm, yp, ym, xp, xm, t_a, t_b = refs[12:]
+        ins, refs = refs[:8], refs[8:]
+        given, refs = refs[: len(extra)], refs[len(extra) :]
+        outs, face_ref, refs = refs[:TEAM], refs[TEAM], refs[TEAM + 1 :]
+        if weigh:
+            moments_ref, weights, refs = refs[0], refs[-1], refs[1:-1]
+        cond, u_a, u_b, s_a, s_b, zp, zm, yp, ym, xp, xm, t_a, t_b = refs
         place = team_place()
         column, side = lax.rem(place, 2), place // 2
         upper, lower = halo + own, 0
@@ -275,60 +292,33 @@
             for j in range(planes):
                 for t in range(2):
                     outs[m][j, t] = t_now[base + j, t]
+        face = jnp.concatenate([t_now[halo + p, 0, 0:1, :] for p in range(own)], axis=0)
+        if weigh:
+            weights[...], mean, variance = risk(given[0][...], cells)
+            lane = lax.broadcasted_iota(jnp.int32, (1, LANES), 1)
+            moments_ref[...] = jnp.where(lane == 0, mean, variance)
+            total = jnp.zeros((own, columns), F32)
+            for n, values in enumerate([ref[...] for ref in given[1:]] + [face]):
+                row = weights[pl.ds(slots * place + n, 1), :]
+                total = total + values * jnp.concatenate([row] * (columns // LANES), axis=1)
+            face_ref[...] = total
+        else:
+            face_ref[...] = face
 
     vmem = pl.BlockSpec(memory_space=pltpu.VMEM)
     field = pltpu.VMEM((span, 2, half, columns), F32)
     return pl.pallas_call(
         kernel,
-        out_shape=[jax.ShapeDtypeStruct((planes, 2, half, columns), F32)] * TEAM,
-        in_specs=[vmem] * 8,
-        out_specs=[vmem] * TEAM,
-        scratch_shapes=[field] * 13,
+        out_shape=[jax.ShapeDtypeStruct((planes, 2, half, columns), F32)] * TEAM
+        + [jax.ShapeDtypeStruct((own, columns), F32)]
+        + [jax.ShapeDtypeStruct((1, LANES), F32)] * weigh,
+        in_specs=[vmem] * (8 + len(extra)),
+        out_specs=[vmem] * (TEAM + 1 + weigh),
+        scratch_shapes=[field] * 13 + ([pltpu.VMEM(sums.shape, F32)] if weigh else []),
         compiler_params=pltpu.CompilerParams(vmem_limit_bytes=32 * MIB),
         cost_estimate=pl.CostEstimate(flops=0, bytes_accessed=22 * MIB, transcendentals=0),
         name=f"solve{slot}",
-    )(*inputs)
-
-
-def weigh_faces(pieces, sums, cells):
-    slots = len(pieces)
-    planes, _, _, columns = pieces[0][0].shape
-    slabs, samples, _ = sums.shape
-
-    def kernel(sums_ref, *refs):
-        faces = refs[: slots * TEAM]
-        face_ref, moments_ref, weights = refs[slots * TEAM :]
-        place = team_place()
-        misfit = jnp.sum(sums_ref[...], axis=0)[:, :128] * (1.0 / (2.0 * cells))
-        mean = jnp.sum(misfit, axis=0, keepdims=True) * (1.0 / samples)
-        deviation = misfit - mean
-        variance = jnp.sum(deviation * deviation, axis=0, keepdims=True) * (1.0 / samples)
-        lane = lax.broadcasted_iota(jnp.int32, (1, 128), 1)
-        moments_ref[...] = jnp.where(lane == 0, mean, variance)
-        weights[...] = 1.0 + 2.0 * BETA_RISK * deviation
-        for j in range(planes):
-            face = jnp.zeros((1, columns), F32)
-            for slot in range(slots):
-                for m in range(TEAM):
-                    row = weights[pl.ds(slots * (place ^ m) + slot, 1), :]
-                    wide = jnp.concatenate([row] * (columns // 128), axis=1)
-                    face = face + wide * faces[slot * TEAM + m][j, 0, 0:1, :]
-            for d in range(slabs):
-                face_ref[d, j : j + 1, :] = face
-
-    vmem = pl.BlockSpec(memory_space=pltpu.VMEM)
-    return pl.pallas_call(
-        kernel,
-        out_shape=[
-            jax.ShapeDtypeStruct((slabs, planes, columns), F32),
-            jax.ShapeDtypeStruct((1, 128), F32),
-        ],
-        in_specs=[vmem] * (1 + slots * TEAM),
-        out_specs=[vmem, vmem],
-        scratch_shapes=[pltpu.VMEM((samples, 128), F32)],
-        compiler_params=pltpu.CompilerParams(vmem_limit_bytes=24 * MIB),
-        name="weigh_faces",
-    )(sums, *[piece for group in pieces for piece in group])
+    )(*inputs, *extra)
 
 
 def gather_adjoint(pieces):
@@ -376,13 +366,27 @@
     )(*[piece for group in pieces for piece in group])
 
 
-def control(faces, basis_z, basis_x, own_count):
-    depth_total, columns = faces.shape
-
-    def kernel(face_ref, z_ref, x_ref, out_ref):
-        own_modes = z_ref[lax.axis_index("gz")]
+def control(faces, radices, basis_z, basis_x):
+    slabs, own_count, depth_total = basis_z.shape
+    own, columns = faces[0].shape[1:]
+    teams = depth_total // own
+
+    def kernel(*refs):
+        parts, (z_ref, x_ref, out_ref, whole) = refs[: len(faces)], refs[len(faces) :]
+        rank = lax.axis_index("gz")
+        team = rank // TEAM
+        for n in range(teams):
+            at, left, stride = 0, n, 1
+            for radix in radices:
+                digit = lax.rem(team // stride + left % radix, radix)
+                at, left, stride = at + digit * stride, left // radix, stride * radix
+            inner = teams // len(faces)
+            whole[at] = parts[n // inner][n % inner]
         along_z = jnp.dot(
-            own_modes, face_ref[...], precision=lax.Precision.HIGHEST, preferred_element_type=F32
+            z_ref[rank],
+            whole[...].reshape(depth_total, columns),
+            precision=lax.Precision.HIGHEST,
+            preferred_element_type=F32,
         )
         out_ref[...] = jnp.dot(
             along_z, x_ref[...], precision=lax.Precision.HIGHEST, preferred_element_type=F32
@@ -392,11 +396,21 @@
     return pl.pallas_call(
         kernel,
         out_shape=jax.ShapeDtypeStruct((own_count, basis_x.shape[1]), F32),
-        in_specs=[vmem] * 3,
+        in_specs=[vmem] * (len(faces) + 2),
         out_specs=vmem,
+        scratch_shapes=[pltpu.VMEM((teams, own, columns), F32)],
         compiler_params=pltpu.CompilerParams(vmem_limit_bytes=16 * MIB),
         name="control",
-    )(faces, basis_z, basis_x)
+    )(*faces, basis_z, basis_x)
+
+
+def radices_of(teams):
+    radices = []
+    while teams > 1:
+        radix = next(r for r in (4, 2, 3, *range(5, teams + 1)) if teams % r == 0)
+        radices.append(radix)
+        teams //= radix
+    return radices
 
 
 def on_device(state, target, rock_type, log_table, obs_scale):
@@ -404,6 +418,7 @@
     slabs = lax.axis_size("gz")
     slots = samples // TEAM
     depth_total = planes * slabs
+    radices = radices_of(slabs // TEAM)
 
     def swap(value, m):
         return lax.ppermute(value, "gz", [(i, i ^ m) for i in range(slabs)])
@@ -417,36 +432,62 @@
                 pairs.append((i, to))
         return lax.ppermute(value, "gz", pairs)
 
-    fields = (state, target, rock_type, log_table, obs_scale, depth_total)
-    sums, far = [], []
+    def from_teams(value, stride, radix):
+        heard = []
+        for k in range(1, radix):
+            pairs = []
+            for i in range(slabs):
+                digit = i // (TEAM * stride) % radix
+                pairs.append((i + ((digit + k) % radix - digit) * stride * TEAM, i))
+            heard.append(lax.ppermute(value, "gz", pairs))
+        return heard
+
+    def team_sum(value):
+        return sum((swap(value, m) for m in (2, 3, 1)), value)
+
+    fields = [
+        pltpu.with_memory_space_constraint(field, pltpu.HBM)
+        for field in (state, target, rock_type, log_table, obs_scale)
+    ]
+    sums = jnp.zeros((samples, LANES), F32)
+    far = []
     for slot in range(slots):
-        blocks, slot_sums = prepare([[(slot, 2)], [(slot, 3)]], fields)
-        sums.append(slot_sums)
+        blocks, sums = prepare([[(slot, 2)], [(slot, 3)]], fields, sums)
         far.append([swap(blocks[0], 2), swap(blocks[1], 3)])
-    blocks, near_sums = prepare(
-        [[(slot, m) for slot in range(slots)] for m in range(2)], fields
-    )
-    sums.append(near_sums)
+    blocks, sums = prepare([[(slot, m) for slot in range(slots)] for m in range(2)], fields, sums)
     near = [blocks[0], swap(blocks[1], 1)]
     near_halo = [along(block, True) for block in near]
-    pieces = []
+
+    sums = team_sum(sums)
+    stride = 1
+    for radix in radices:
+        sums = sum(from_teams(sums, stride, radix), sums)
+        stride *= radix
+
+    pieces, faces = [], []
     for slot in range(slots):
+        last = slot == slots - 1
         far_halo = [along(block, False) for block in far[slot]]
-        solved = solve(slot, near + far[slot], near_halo + far_halo)
+        solved = solve(
+            slot, near + far[slot], near_halo + far_halo, *((sums, faces) if last else ())
+        )
         pieces.append([solved[0]] + [swap(solved[m], m) for m in (1, 2, 3)])
-
-    local_sums = sum(sums[1:], sums[0])
-    spread_sums = jnp.broadcast_to(local_sums[None], (slabs,) + local_sums.shape)
-    all_sums = lax.all_to_all(spread_sums, "gz", split_axis=0, concat_axis=0, tiled=True)
-
-    faces, moments = weigh_faces(pieces, all_sums, depth_total * rows_y * columns)
-    faces = lax.all_to_all(faces, "gz", split_axis=0, concat_axis=0, tiled=True)
+        faces.append(solved[TEAM])
+    moments = solved[TEAM + 1]
+
+    heard = [team_sum(faces[-1])[None]]
+    stride = 1
+    for radix in radices:
+        held = heard[0] if len(heard) == 1 else jnp.concatenate(heard)
+        heard = [held] + from_teams(held, stride, radix)
+        stride *= radix
     adjoint = gather_adjoint(pieces)
+    own_count = MA // slabs
     gradient = control(
-        faces.reshape(depth_total, columns),
-        jnp.asarray(cosine_basis(depth_total, MA).T.reshape(slabs, MA // slabs, depth_total)),
+        heard,
+        radices,
+        jnp.asarray(cosine_basis(depth_total, MA).T.reshape(slabs, own_count, depth_total)),
         jnp.asarray(cosine_basis(columns, MB)),
-        MA // slabs,
     )
     return (adjoint, gradient, moments[0, :2])
 

time: 95.3 us -> 94 us (0.986)
  waiting for transfers between devices: 18.5 us -> 32.9 us
  starting transfers between devices: 40.6 us -> 33.7 us
  local copies, waits for them, and re-layouts: 5.92 us -> 0.52 us
  Pallas kernels: 28.9 us -> 25.7 us
    ppermute x0 -> x6, waiting for transfers between devices: none -> 13.2 us  [from_teams(): heard.append(lax.ppermute(value, 'gz', pairs))]
    all_to_all x2 -> x0, starting transfers between devices: 9.6 us -> none  [the longest x1 5.83 us: on_device(): faces = lax.all_to_all(faces, 'gz', split_axis=0, concat_axis=0, tiled=True)]
    ppermute x11 -> x17, waiting for transfers between devices: 12.2 us -> 19.2 us  [swap(): return lax.ppermute(value, 'gz', [(i, i ^ m) for i in range(slabs)])]
    all_to_all x2 -> x0, waiting for transfers between devices: 6.34 us -> none  [the longest x1 6.34 us: on_device(): faces = lax.all_to_all(faces, 'gz', split_axis=0, concat_axis=0, tiled=True)]
    ppermute x0 -> x6, starting transfers between devices: none -> 6.18 us  [from_teams(): heard.append(lax.ppermute(value, 'gz', pairs))]
    unnamed x14 -> x4, local copies, waits for them, and re-layouts: 4.7 us -> 0.01 us
    ppermute x6, starting transfers between devices: 17.7 us -> 13.9 us  [along(): return lax.ppermute(value, 'gz', pairs)]
    pallas_call x2, Pallas kernels: 20.5 us -> 18.1 us  [solve(): pl.pallas_call(kernel, out_shape=[jax.ShapeDtypeStruct((planes, 2, half,...]
  transfers between devices with their start and end apart: 19 -> 29, of which waited for: 7 -> 15; matrix products, arithmetic and copies ran while one was open for 1% -> 1% of each run, Pallas kernels for 26% -> 11%
where the time goes in v3:
time: 94 us; the launch traced here: 93.6 us
  starting transfers between devices  33.7 us (36%)
  waiting for transfers between devices  32.9 us (35%)
  Pallas kernels  25.7 us (27%)
    ppermute x17, waiting for transfers between devices, swap(): return lax.ppermute(value, 'gz', [(i, i ^ m) for i in range(slabs)])  19.2 us
    pallas_call x2, Pallas kernels, solve(): pl.pallas_call(kernel, out_shape=[jax.ShapeDtypeStruct((planes, 2, half,...  18.1 us
    ppermute x6, starting transfers between devices, along(): return lax.ppermute(value, 'gz', pairs)  13.9 us
    ppermute x17, starting transfers between devices, swap(): return lax.ppermute(value, 'gz', [(i, i ^ m) for i in range(slabs)])  13.6 us
    ppermute x6, waiting for transfers between devices, from_teams(): heard.append(lax.ppermute(value, 'gz', pairs))  13.2 us
    ppermute x6, starting transfers between devices, from_teams(): heard.append(lax.ppermute(value, 'gz', pairs))  6.18 us
    pallas_call x3, Pallas kernels, prepare(): pl.pallas_call(kernel, out_shape=[jax.ShapeDtypeStruct((len(group), 2, pl...  5.05 us
  transfers between devices with their start and end apart: 29, of which 15 were waited for; matrix products, arithmetic and copies ran while one was open for 1% of the time, Pallas kernels for 11%

profile of v3, /device:TPU:0, one launch (start us, length us, event | category | flops | bytes accessed | tf_op | source)
XLA Modules:
  0.0 93.6 jit_solution(211010185707085409)
XLA Ops:
  0.6 1.5 %prepare.3 = (f32[1,2,4,2,8,512]{5,4,3,2,1,0:T(8,128)S(1)}, f32[1,2,4,2,8,512]{5,4,3,2,1,0:T(8,128)S(1)}, f32[8,128]{1,0:T(8,128)S(1)}) custom-call(f32[8,128]{1,0:T(8,128)S(1)} %broadcast_in_dim.6.before_ref, f32[8,8]{1,0:T(8,128)} %table_ref.5, f32[8]{0:T(128)} %scale_ref.5, f32[8,4,16,512]{3,2,1,0:T(8,128)} %state_ref.5, f32[4,16,512]{2,1,0:T(8,128)} %target_ref.5, ...), custom_call_target="tpu_custom_call" | custom-call | bytes 2097152 | tf_op jit(solution)/shard_map/prepare/pallas_call | solution.py:129
  2.2 1.5 %prepare.4 = (f32[1,2,4,2,8,512]{5,4,3,2,1,0:T(8,128)S(1)}, f32[1,2,4,2,8,512]{5,4,3,2,1,0:T(8,128)S(1)}, f32[8,128]{1,0:T(8,128)S(1)}) custom-call(f32[8,128]{1,0:T(8,128)S(1)} %get-tuple-element.23.before_ref, f32[8,8]{1,0:T(8,128)} %table_ref.5, f32[8]{0:T(128)} %scale_ref.5, f32[8,4,16,512]{3,2,1,0:T(8,128)} %state_ref.5, f32[4,16,512]{2,1,0:T(8,128)} %target_ref.5, ...), custom_call_target="tpu_custom_call" | custom-call | bytes 2097152 | tf_op jit(solution)/shard_map/prepare/pallas_call | solution.py:129
  3.7 2.0 %prepare.5 = (f32[2,2,4,2,8,512]{5,4,3,2,1,0:T(8,128)S(1)}, f32[2,2,4,2,8,512]{5,4,3,2,1,0:T(8,128)S(1)}, f32[8,128]{1,0:T(8,128)S(1)}) custom-call(f32[8,128]{1,0:T(8,128)S(1)} %get-tuple-element.24.before_ref, f32[8,8]{1,0:T(8,128)} %table_ref.5, f32[8]{0:T(128)} %scale_ref.5, f32[8,4,16,512]{3,2,1,0:T(8,128)} %state_ref.5, f32[4,16,512]{2,1,0:T(8,128)} %target_ref.5, ...), custom_call_target="tpu_custom_call" | custom-call | bytes 4194304 | tf_op jit(solution)/shard_map/prepare/pallas_call | solution.py:129
  5.7 0.5 collective-permute-start
  6.2 2.6 %collective-permute-start.1 = (f32[1,2,4,2,8,512]{5,4,3,2,1,0:T(8,128)S(1)}, f32[1,2,4,2,8,512]{5,4,3,2,1,0:T(8,128)S(1)}, u32[]{:S(2)}, u32[]{:S(2)}) collective-permute-start(f32[1,2,4,2,8,512]{5,4,3,2,1,0:T(8,128)S(1)} %get-tuple-element.27), channel_id=1, source_target_pairs={{0,2},{1,3},{2,0},{3,1},{4,6},{5,7},{6,4},{7,5},{8,10},{9,11},{10,... | collective-permute-start | bytes 786440 | tf_op jit(solution)/shard_map/ppermute | solution.py:424
  8.8 1.3 %collective-permute-start.3 = (f32[2,2,4,2,8,512]{5,4,3,2,1,0:T(8,128)S(1)}, f32[2,2,4,2,8,512]{5,4,3,2,1,0:T(8,128)S(1)}, u32[]{:S(2)}, u32[]{:S(2)}) collective-permute-start(f32[2,2,4,2,8,512]{5,4,3,2,1,0:T(8,128)S(1)} %get-tuple-element.25.refs_0_), channel_id=1, source_target_pairs={{2,6},{3,7},{4,0},{5,1},{6,10},{7,11},{8,4},{9,5},{10,14},{11,15},... | collective-permute-start | bytes 1572872 | tf_op jit(solution)/shard_map/ppermute | solution.py:433
  10.1 0.2 collective-permute-start.16
  10.3 2.7 %collective-permute-start.15 = (f32[8,128]{1,0:T(8,128)S(1)}, f32[8,128]{1,0:T(8,128)S(1)}, u32[]{:S(2)}, u32[]{:S(2)}) collective-permute-start(f32[8,128]{1,0:T(8,128)S(1)} %get-tuple-element.35), channel_id=1, source_target_pairs={{0,3},{1,2},{2,1},{3,0},{4,7},{5,6},{6,5},{7,4},{8,11},{9,10},{10,... | collective-permute-start | bytes 12296 | tf_op jit(solution)/shard_map/ppermute | solution.py:424
  13.0 0.0 collective-permute-done.16
  13.0 1.0 %collective-permute-start.14 = (f32[8,128]{1,0:T(8,128)S(1)}, f32[8,128]{1,0:T(8,128)S(1)}, u32[]{:S(2)}, u32[]{:S(2)}) collective-permute-start(f32[8,128]{1,0:T(8,128)S(1)} %get-tuple-element.35), channel_id=1, source_target_pairs={{0,2},{1,3},{2,0},{3,1},{4,6},{5,7},{6,4},{7,5},{8,10},{9,11},{10,... | collective-permute-start | bytes 12296 | tf_op jit(solution)/shard_map/ppermute | solution.py:424
  14.1 1.4 %collective-permute-done.15 = f32[8,128]{1,0:T(8,128)S(1)} collective-permute-done((f32[8,128]{1,0:T(8,128)S(1)}, f32[8,128]{1,0:T(8,128)S(1)}, u32[]{:S(2)}, u32[]{:S(2)}) %collective-permute-start.15) | collective-permute-done | bytes 4128 | tf_op jit(solution)/shard_map/ppermute | solution.py:424
  15.5 1.1 %collective-permute-done.14 = f32[8,128]{1,0:T(8,128)S(1)} collective-permute-done((f32[8,128]{1,0:T(8,128)S(1)}, f32[8,128]{1,0:T(8,128)S(1)}, u32[]{:S(2)}, u32[]{:S(2)}) %collective-permute-start.14) | collective-permute-done | bytes 4128 | tf_op jit(solution)/shard_map/ppermute | solution.py:424
  16.7 1.5 %collective-permute-start.19 = (f32[8,128]{1,0:T(8,128)S(1)}, f32[8,128]{1,0:T(8,128)S(1)}, u32[]{:S(2)}, u32[]{:S(2)}) collective-permute-start(f32[8,128]{1,0:T(8,128)S(1)} %add_add_fusion.1), channel_id=1, source_target_pairs={{12,0},{13,1},{14,2},{15,3},{0,4},{1,5},{2,6},{3,7},{4,8},{5,9},{6... | collective-permute-start | bytes 12296 | tf_op jit(solution)/shard_map/ppermute | solution.py:442
  18.2 2.1 %collective-permute-start.18 = (f32[8,128]{1,0:T(8,128)S(1)}, f32[8,128]{1,0:T(8,128)S(1)}, u32[]{:S(2)}, u32[]{:S(2)}) collective-permute-start(f32[8,128]{1,0:T(8,128)S(1)} %add_add_fusion.1), channel_id=1, source_target_pairs={{8,0},{9,1},{10,2},{11,3},{12,4},{13,5},{14,6},{15,7},{0,8},{1,9},... | collective-permute-start | bytes 12296 | tf_op jit(solution)/shard_map/ppermute | solution.py:442
  20.3 6.6 %collective-permute-done.19 = f32[8,128]{1,0:T(8,128)S(1)} collective-permute-done((f32[8,128]{1,0:T(8,128)S(1)}, f32[8,128]{1,0:T(8,128)S(1)}, u32[]{:S(2)}, u32[]{:S(2)}) %collective-permute-start.19) | collective-permute-done | bytes 4128 | tf_op jit(solution)/shard_map/ppermute | solution.py:442
  26.9 0.0 collective-permute-start.17
  26.9 0.7 collective-permute-start.2
  27.6 2.9 %collective-permute-done.17 = f32[8,128]{1,0:T(8,128)S(1)} collective-permute-done((f32[8,128]{1,0:T(8,128)S(1)}, f32[8,128]{1,0:T(8,128)S(1)}, u32[]{:S(2)}, u32[]{:S(2)}) %collective-permute-start.17) | collective-permute-done | bytes 4128 | tf_op jit(solution)/shard_map/ppermute | solution.py:442
  30.5 1.3 %collective-permute-start.4 = (f32[2,2,4,2,8,512]{5,4,3,2,1,0:T(8,128)S(1)}, f32[2,2,4,2,8,512]{5,4,3,2,1,0:T(8,128)S(1)}, u32[]{:S(2)}, u32[]{:S(2)}) collective-permute-start(f32[2,2,4,2,8,512]{5,4,3,2,1,0:T(8,128)S(1)} %collective-permute-done.refs_1_), channel_id=1, source_target_pairs={{2,6},{3,7},{4,0},{5,1},{6,10},{7,11},{8,4},{9,5},{10,14},{11,15},... | collective-permute-start | bytes 1572872 | tf_op jit(solution)/shard_map/ppermute | solution.py:433
  31.8 3.1 %collective-permute-done.2.refs_3_ = f32[1,2,4,2,8,512]{5,4,3,2,1,0:T(8,128)S(1)} collective-permute-done((f32[1,2,4,2,8,512]{5,4,3,2,1,0:T(8,128)S(1)}, f32[1,2,4,2,8,512]{5,4,3,2,1,0:T(8,128)S(1)}, u32[]{:S(2)}, u32[]{:S(2)}) %collective-permute-start.2) | collective-permute-done | bytes 262176 | tf_op jit(solution)/shard_map/ppermute | solution.py:424
  34.9 4.5 %collective-permute-start.5 = (f32[1,2,4,2,8,512]{5,4,3,2,1,0:T(8,128)S(1)}, f32[1,2,4,2,8,512]{5,4,3,2,1,0:T(8,128)S(1)}, u32[]{:S(2)}, u32[]{:S(2)}) collective-permute-start(f32[1,2,4,2,8,512]{5,4,3,2,1,0:T(8,128)S(1)} %collective-permute-done.1.refs_2_), channel_id=1, source_target_pairs={{0,4},{1,5},{4,8},{5,9},{6,2},{7,3},{8,12},{9,13},{10,6},{11,7},{1... | collective-permute-start | bytes 786440 | tf_op jit(solution)/shard_map/ppermute | solution.py:433
  39.4 2.2 %collective-permute-done.10.refs_2_ = f32[1,2,4,2,8,512]{5,4,3,2,1,0:T(8,128)S(1)} collective-permute-done((f32[1,2,4,2,8,512]{5,4,3,2,1,0:T(8,128)S(1)}, f32[1,2,4,2,8,512]{5,4,3,2,1,0:T(8,128)S(1)}, u32[]{:S(2)}, u32[]{:S(2)}) %collective-permute-start.10) | collective-permute-done | bytes 262176 | tf_op jit(solution)/shard_map/ppermute | solution.py:424
  41.7 1.5 %collective-permute-start.6 = (f32[1,2,4,2,8,512]{5,4,3,2,1,0:T(8,128)S(1)}, f32[1,2,4,2,8,512]{5,4,3,2,1,0:T(8,128)S(1)}, u32[]{:S(2)}, u32[]{:S(2)}) collective-permute-start(f32[1,2,4,2,8,512]{5,4,3,2,1,0:T(8,128)S(1)} %collective-permute-done.2.refs_3_), channel_id=1, source_target_pairs={{0,4},{1,5},{4,8},{5,9},{6,2},{7,3},{8,12},{9,13},{10,6},{11,7},{1... | collective-permute-start | bytes 786440 | tf_op jit(solution)/shard_map/ppermute | solution.py:433
  43.2 2.9 %collective-permute-done.11.refs_3_ = f32[1,2,4,2,8,512]{5,4,3,2,1,0:T(8,128)S(1)} collective-permute-done((f32[1,2,4,2,8,512]{5,4,3,2,1,0:T(8,128)S(1)}, f32[1,2,4,2,8,512]{5,4,3,2,1,0:T(8,128)S(1)}, u32[]{:S(2)}, u32[]{:S(2)}) %collective-permute-start.11) | collective-permute-done | bytes 262176 | tf_op jit(solution)/shard_map/ppermute | solution.py:424
  46.1 3.4 %collective-permute-start.12 = (f32[1,2,4,2,8,512]{5,4,3,2,1,0:T(8,128)S(1)}, f32[1,2,4,2,8,512]{5,4,3,2,1,0:T(8,128)S(1)}, u32[]{:S(2)}, u32[]{:S(2)}) collective-permute-start(f32[1,2,4,2,8,512]{5,4,3,2,1,0:T(8,128)S(1)} %collective-permute-done.10.refs_2_), channel_id=1, source_target_pairs={{0,4},{1,5},{4,8},{5,9},{6,2},{7,3},{8,12},{9,13},{10,6},{11,7},{1... | collective-permute-start | bytes 786440 | tf_op jit(solution)/shard_map/ppermute | solution.py:433
  49.5 1.9 %collective-permute-start.13 = (f32[1,2,4,2,8,512]{5,4,3,2,1,0:T(8,128)S(1)}, f32[1,2,4,2,8,512]{5,4,3,2,1,0:T(8,128)S(1)}, u32[]{:S(2)}, u32[]{:S(2)}) collective-permute-start(f32[1,2,4,2,8,512]{5,4,3,2,1,0:T(8,128)S(1)} %collective-permute-done.11.refs_3_), channel_id=1, source_target_pairs={{0,4},{1,5},{4,8},{5,9},{6,2},{7,3},{8,12},{9,13},{10,6},{11,7},{1... | collective-permute-start | bytes 786440 | tf_op jit(solution)/shard_map/ppermute | solution.py:433
  51.5 9.1 %solve0.1 = (f32[4,2,8,512]{3,2,1,0:T(8,128)S(1)}, f32[4,2,8,512]{3,2,1,0:T(8,128)S(1)}, f32[4,2,8,512]{3,2,1,0:T(8,128)S(1)}, f32[4,2,8,512]{3,2,1,0:T(8,128)S(1)}, f32[16,512]{1,0:T(8,128)S(1)}) custom-call(f32[2,2,4,2,8,512]{5,4,3,2,1,0:T(8,128)S(1)} %get-tuple-element.25.refs_0_, f32[2,2,4,2,8,512]{5,4,3,2,1,0:T(8,128)S(1)} %collective-permute-done.refs_1_, ...), custom_call_target="tpu_custom_call" | custom-call | bytes 23068672 | tf_op jit(solution)/shard_map/solve0/pallas_call | solution.py:310
  60.6 0.5 collective-permute-done.13.refs_7_
  61.1 9.1 %solve1.1 = (f32[4,2,8,512]{3,2,1,0:T(8,128)S(1)}, f32[4,2,8,512]{3,2,1,0:T(8,128)S(1)}, f32[4,2,8,512]{3,2,1,0:T(8,128)S(1)}, f32[4,2,8,512]{3,2,1,0:T(8,128)S(...) custom-call(f32[2,2,4,2,8,512]{5,4,3,2,1,0:T(8,128)S(1)} %get-tuple-element.25.refs_0_, ...), custom_call_target="tpu_custom_call" | custom-call | bytes 23068672 | tf_op jit(solution)/shard_map/solve1/pallas_call | solution.py:310
  70.2 0.1 collective-permute-start.25
  70.3 3.1 %collective-permute-start.24 = (f32[16,512]{1,0:T(8,128)S(1)}, f32[16,512]{1,0:T(8,128)S(1)}, u32[]{:S(2)}, u32[]{:S(2)}) collective-permute-start(f32[16,512]{1,0:T(8,128)S(1)} %get-tuple-element.41), channel_id=1, source_target_pairs={{0,3},{1,2},{2,1},{3,0},{4,7},{5,6},{6,5},{7,4},{8,11},{9,10},{10,... | collective-permute-start | bytes 98312 | tf_op jit(solution)/shard_map/ppermute | solution.py:424
  73.3 0.0 collective-permute-start.23
  73.4 0.1 collective-permute-start.7
  73.5 1.5 %collective-permute-done.24 = f32[16,512]{1,0:T(8,128)S(1)} collective-permute-done((f32[16,512]{1,0:T(8,128)S(1)}, f32[16,512]{1,0:T(8,128)S(1)}, u32[]{:S(2)}, u32[]{:S(2)}) %collective-permute-start.24) | collective-permute-done | bytes 32800 | tf_op jit(solution)/shard_map/ppermute | solution.py:424
  75.0 2.2 %collective-permute-done.23 = f32[16,512]{1,0:T(8,128)S(1)} collective-permute-done((f32[16,512]{1,0:T(8,128)S(1)}, f32[16,512]{1,0:T(8,128)S(1)}, u32[]{:S(2)}, u32[]{:S(2)}) %collective-permute-start.23) | collective-permute-done | bytes 32800 | tf_op jit(solution)/shard_map/ppermute | solution.py:424
  77.3 0.1 collective-permute-start.26
  77.3 1.5 %collective-permute-start.27 = (f32[1,16,512]{2,1,0:T(8,128)S(1)}, f32[1,16,512]{2,1,0:T(8,128)S(1)}, u32[]{:S(2)}, u32[]{:S(2)}) collective-permute-start(f32[1,16,512]{2,1,0:T(8,128)S(1)} %add_bitcast_fusion.refs_0_), channel_id=1, source_target_pairs={{8,0},{9,1},{10,2},{11,3},{12,4},{13,5},{14,6},{15,7},{0,8},{1,9},... | collective-permute-start | bytes 98312 | tf_op jit(solution)/shard_map/ppermute | solution.py:442
  78.8 0.9 collective-permute-start.28
  79.8 1.0 %collective-permute-start.8 = (f32[4,2,8,512]{3,2,1,0:T(8,128)S(1)}, f32[4,2,8,512]{3,2,1,0:T(8,128)S(1)}, u32[]{:S(2)}, u32[]{:S(2)}) collective-permute-start(f32[4,2,8,512]{3,2,1,0:T(8,128)S(1)} %get-tuple-element.31), channel_id=1, source_target_pairs={{0,2},{1,3},{2,0},{3,1},{4,6},{5,7},{6,4},{7,5},{8,10},{9,11},{10,... | collective-permute-start | bytes 393224 | tf_op jit(solution)/shard_map/ppermute | solution.py:424
  80.8 0.4 collective-permute-done.26.refs_1_
  81.2 1.3 %collective-permute-done.27.refs_2_ = f32[1,16,512]{2,1,0:T(8,128)S(1)} collective-permute-done((f32[1,16,512]{2,1,0:T(8,128)S(1)}, f32[1,16,512]{2,1,0:T(8,128)S(1)}, u32[]{:S(2)}, u32[]{:S(2)}) %collective-permute-start.27) | collective-permute-done | bytes 32800 | tf_op jit(solution)/shard_map/ppermute | solution.py:442
  82.6 2.0 %collective-permute-done.28.refs_3_ = f32[1,16,512]{2,1,0:T(8,128)S(1)} collective-permute-done((f32[1,16,512]{2,1,0:T(8,128)S(1)}, f32[1,16,512]{2,1,0:T(8,128)S(1)}, u32[]{:S(2)}, u32[]{:S(2)}) %collective-permute-start.28) | collective-permute-done | bytes 32800 | tf_op jit(solution)/shard_map/ppermute | solution.py:442
  84.6 1.5 %collective-permute-start.21 = (f32[4,2,8,512]{3,2,1,0:T(8,128)S(1)}, f32[4,2,8,512]{3,2,1,0:T(8,128)S(1)}, u32[]{:S(2)}, u32[]{:S(2)}) collective-permute-start(f32[4,2,8,512]{3,2,1,0:T(8,128)S(1)} %get-tuple-element.39), channel_id=1, source_target_pairs={{0,2},{1,3},{2,0},{3,1},{4,6},{5,7},{6,4},{7,5},{8,10},{9,11},{10,... | collective-permute-start | bytes 393224 | tf_op jit(solution)/shard_map/ppermute | solution.py:424
  86.0 0.5 slice_bitcast_fusion
  86.6 1.4 %control.1 = f32[32,512]{1,0:T(8,128)} custom-call(f32[1,16,512]{2,1,0:T(8,128)S(1)} %add_bitcast_fusion.refs_0_, f32[1,16,512]{2,1,0:T(8,128)S(1)} %collective-permute-done.26.refs_1_, f32[1,16,512]{2,1,0:T(8,128)S(1)} %collective-permute-done.27.refs_2_, f32[1,16,512]{2,1,0:T(8,128)S(1)} %collective-permute-done.28.refs_3_, f32[16,32,64]{2,1,0:T(8,128)S(1)} %copy-done.1, ...), custom_call_target="tpu_custom_call" | custom-call | tf_op jit(solution)/shard_map/control/pallas_call | solution.py:396
  88.0 3.0 %collective-permute-done.21.refs_6_ = f32[4,2,8,512]{3,2,1,0:T(8,128)S(1)} collective-permute-done((f32[4,2,8,512]{3,2,1,0:T(8,128)S(1)}, f32[4,2,8,512]{3,2,1,0:T(8,128)S(1)}, u32[]{:S(2)}, u32[]{:S(2)}) %collective-permute-start.21) | collective-permute-done | bytes 131104 | tf_op jit(solution)/shard_map/ppermute | solution.py:424
  91.0 1.5 %collective-permute-done.22.refs_7_ = f32[4,2,8,512]{3,2,1,0:T(8,128)S(1)} collective-permute-done((f32[4,2,8,512]{3,2,1,0:T(8,128)S(1)}, f32[4,2,8,512]{3,2,1,0:T(8,128)S(1)}, u32[]{:S(2)}, u32[]{:S(2)}) %collective-permute-start.22) | collective-permute-done | bytes 131104 | tf_op jit(solution)/shard_map/ppermute | solution.py:424
  92.5 1.0 %gather_adjoint.1 = f32[8,4,16,512]{3,2,1,0:T(8,128)} custom-call(f32[4,2,8,512]{3,2,1,0:T(8,128)S(1)} %get-tuple-element.29.refs_0_, f32[4,2,8,512]{3,2,1,0:T(8,128)S(1)} %collective-permute-done.7.refs_1_, f32[4,2,8,512]{3,2,1,0:T(8,128)S(1)} %collective-permute-done.8.refs_2_, f32[4,2,8,512]{3,2,1,0:T(8,128)S(1)} %collective-permute-done.9.refs_3_, ...), custom_call_target="tpu_custom_call" | custom-call | bytes 4194304 | tf_op jit(solution)/shard_map/gather_adjoint/pallas_call | solution.py:353
  (26 shorter events, 0.1 us)
Async XLA Ops:
  5.7 24.8 %collective-permute-start = (f32[2,2,4,2,8,512]{5,4,3,2,1,0:T(8,128)S(1)}, f32[2,2,4,2,8,512]{5,4,3,2,1,0:T(8,128)S(1)}, u32[]{:S(2)}, u32[]{:S(2)}) collective-permute-start(f32[2,2,4,2,8,512]{5,4,3,2,1,0:T(8,128)S(1)} %get-tuple-element.26), channel_id=1, source_target_pairs={{0,1},{1,0},{2,3},{3,2},{4,5},{5,4},{6,7},{7,6},{8,9},{9,8},{10,11... | collective-permute-start | bytes 1572872 | tf_op jit(solution)/shard_map/ppermute | solution.py:424
  6.2 24.3 %collective-permute-start.1 = (f32[1,2,4,2,8,512]{5,4,3,2,1,0:T(8,128)S(1)}, f32[1,2,4,2,8,512]{5,4,3,2,1,0:T(8,128)S(1)}, u32[]{:S(2)}, u32[]{:S(2)}) collective-permute-start(f32[1,2,4,2,8,512]{5,4,3,2,1,0:T(8,128)S(1)} %get-tuple-element.27), channel_id=1, source_target_pairs={{0,2},{1,3},{2,0},{3,1},{4,6},{5,7},{6,4},{7,5},{8,10},{9,11},{10,... | collective-permute-start | bytes 786440 | tf_op jit(solution)/shard_map/ppermute | solution.py:424
  8.8 40.7 %collective-permute-start.3 = (f32[2,2,4,2,8,512]{5,4,3,2,1,0:T(8,128)S(1)}, f32[2,2,4,2,8,512]{5,4,3,2,1,0:T(8,128)S(1)}, u32[]{:S(2)}, u32[]{:S(2)}) collective-permute-start(f32[2,2,4,2,8,512]{5,4,3,2,1,0:T(8,128)S(1)} %get-tuple-element.25.refs_0_), channel_id=1, source_target_pairs={{2,6},{3,7},{4,0},{5,1},{6,10},{7,11},{8,4},{9,5},{10,14},{11,15},... | collective-permute-start | bytes 1572872 | tf_op jit(solution)/shard_map/ppermute | solution.py:433
  10.1 3.0 %collective-permute-start.16 = (f32[8,128]{1,0:T(8,128)S(1)}, f32[8,128]{1,0:T(8,128)S(1)}, u32[]{:S(2)}, u32[]{:S(2)}) collective-permute-start(f32[8,128]{1,0:T(8,128)S(1)} %get-tuple-element.35), channel_id=1, source_target_pairs={{0,1},{1,0},{2,3},{3,2},{4,5},{5,4},{6,7},{7,6},{8,9},{9,8},{10,11... | collective-permute-start | bytes 12296 | tf_op jit(solution)/shard_map/ppermute | solution.py:424
  10.3 5.2 %collective-permute-start.15 = (f32[8,128]{1,0:T(8,128)S(1)}, f32[8,128]{1,0:T(8,128)S(1)}, u32[]{:S(2)}, u32[]{:S(2)}) collective-permute-start(f32[8,128]{1,0:T(8,128)S(1)} %get-tuple-element.35), channel_id=1, source_target_pairs={{0,3},{1,2},{2,1},{3,0},{4,7},{5,6},{6,5},{7,4},{8,11},{9,10},{10,... | collective-permute-start | bytes 12296 | tf_op jit(solution)/shard_map/ppermute | solution.py:424
  13.0 3.6 %collective-permute-start.14 = (f32[8,128]{1,0:T(8,128)S(1)}, f32[8,128]{1,0:T(8,128)S(1)}, u32[]{:S(2)}, u32[]{:S(2)}) collective-permute-start(f32[8,128]{1,0:T(8,128)S(1)} %get-tuple-element.35), channel_id=1, source_target_pairs={{0,2},{1,3},{2,0},{3,1},{4,6},{5,7},{6,4},{7,5},{8,10},{9,11},{10,... | collective-permute-start | bytes 12296 | tf_op jit(solution)/shard_map/ppermute | solution.py:424
  16.7 10.2 %collective-permute-start.19 = (f32[8,128]{1,0:T(8,128)S(1)}, f32[8,128]{1,0:T(8,128)S(1)}, u32[]{:S(2)}, u32[]{:S(2)}) collective-permute-start(f32[8,128]{1,0:T(8,128)S(1)} %add_add_fusion.1), channel_id=1, source_target_pairs={{12,0},{13,1},{14,2},{15,3},{0,4},{1,5},{2,6},{3,7},{4,8},{5,9},{6... | collective-permute-start | bytes 12296 | tf_op jit(solution)/shard_map/ppermute | solution.py:442
  18.2 8.7 %collective-permute-start.18 = (f32[8,128]{1,0:T(8,128)S(1)}, f32[8,128]{1,0:T(8,128)S(1)}, u32[]{:S(2)}, u32[]{:S(2)}) collective-permute-start(f32[8,128]{1,0:T(8,128)S(1)} %add_add_fusion.1), channel_id=1, source_target_pairs={{8,0},{9,1},{10,2},{11,3},{12,4},{13,5},{14,6},{15,7},{0,8},{1,9},... | collective-permute-start | bytes 12296 | tf_op jit(solution)/shard_map/ppermute | solution.py:442
  26.9 3.6 %collective-permute-start.17 = (f32[8,128]{1,0:T(8,128)S(1)}, f32[8,128]{1,0:T(8,128)S(1)}, u32[]{:S(2)}, u32[]{:S(2)}) collective-permute-start(f32[8,128]{1,0:T(8,128)S(1)} %add_add_fusion.1), channel_id=1, source_target_pairs={{4,0},{5,1},{6,2},{7,3},{8,4},{9,5},{10,6},{11,7},{12,8},{13,9},{1... | collective-permute-start | bytes 12296 | tf_op jit(solution)/shard_map/ppermute | solution.py:442
  26.9 8.0 %collective-permute-start.2 = (f32[1,2,4,2,8,512]{5,4,3,2,1,0:T(8,128)S(1)}, f32[1,2,4,2,8,512]{5,4,3,2,1,0:T(8,128)S(1)}, u32[]{:S(2)}, u32[]{:S(2)}) collective-permute-start(f32[1,2,4,2,8,512]{5,4,3,2,1,0:T(8,128)S(1)} %get-tuple-element.28), channel_id=1, source_target_pairs={{0,3},{1,2},{2,1},{3,0},{4,7},{5,6},{6,5},{7,4},{8,11},{9,10},{10,... | collective-permute-start | bytes 786440 | tf_op jit(solution)/shard_map/ppermute | solution.py:424
  30.5 11.2 %collective-permute-start.10 = (f32[1,2,4,2,8,512]{5,4,3,2,1,0:T(8,128)S(1)}, f32[1,2,4,2,8,512]{5,4,3,2,1,0:T(8,128)S(1)}, u32[]{:S(2)}, u32[]{:S(2)}) collective-permute-start(f32[1,2,4,2,8,512]{5,4,3,2,1,0:T(8,128)S(1)} %get-tuple-element.33), channel_id=1, source_target_pairs={{0,2},{1,3},{2,0},{3,1},{4,6},{5,7},{6,4},{7,5},{8,10},{9,11},{10,... | collective-permute-start | bytes 786440 | tf_op jit(solution)/shard_map/ppermute | solution.py:424
  30.5 15.7 %collective-permute-start.11 = (f32[1,2,4,2,8,512]{5,4,3,2,1,0:T(8,128)S(1)}, f32[1,2,4,2,8,512]{5,4,3,2,1,0:T(8,128)S(1)}, u32[]{:S(2)}, u32[]{:S(2)}) collective-permute-start(f32[1,2,4,2,8,512]{5,4,3,2,1,0:T(8,128)S(1)} %get-tuple-element.34), channel_id=1, source_target_pairs={{0,3},{1,2},{2,1},{3,0},{4,7},{5,6},{6,5},{7,4},{8,11},{9,10},{10,... | collective-permute-start | bytes 786440 | tf_op jit(solution)/shard_map/ppermute | solution.py:424
  30.5 21.0 %collective-permute-start.4 = (f32[2,2,4,2,8,512]{5,4,3,2,1,0:T(8,128)S(1)}, f32[2,2,4,2,8,512]{5,4,3,2,1,0:T(8,128)S(1)}, u32[]{:S(2)}, u32[]{:S(2)}) collective-permute-start(f32[2,2,4,2,8,512]{5,4,3,2,1,0:T(8,128)S(1)} %collective-permute-done.refs_1_), channel_id=1, source_target_pairs={{2,6},{3,7},{4,0},{5,1},{6,10},{7,11},{8,4},{9,5},{10,14},{11,15},... | collective-permute-start | bytes 1572872 | tf_op jit(solution)/shard_map/ppermute | solution.py:433
  34.9 16.6 %collective-permute-start.5 = (f32[1,2,4,2,8,512]{5,4,3,2,1,0:T(8,128)S(1)}, f32[1,2,4,2,8,512]{5,4,3,2,1,0:T(8,128)S(1)}, u32[]{:S(2)}, u32[]{:S(2)}) collective-permute-start(f32[1,2,4,2,8,512]{5,4,3,2,1,0:T(8,128)S(1)} %collective-permute-done.1.refs_2_), channel_id=1, source_target_pairs={{0,4},{1,5},{4,8},{5,9},{6,2},{7,3},{8,12},{9,13},{10,6},{11,7},{1... | collective-permute-start | bytes 786440 | tf_op jit(solution)/shard_map/ppermute | solution.py:433
  41.7 9.8 %collective-permute-start.6 = (f32[1,2,4,2,8,512]{5,4,3,2,1,0:T(8,128)S(1)}, f32[1,2,4,2,8,512]{5,4,3,2,1,0:T(8,128)S(1)}, u32[]{:S(2)}, u32[]{:S(2)}) collective-permute-start(f32[1,2,4,2,8,512]{5,4,3,2,1,0:T(8,128)S(1)} %collective-permute-done.2.refs_3_), channel_id=1, source_target_pairs={{0,4},{1,5},{4,8},{5,9},{6,2},{7,3},{8,12},{9,13},{10,6},{11,7},{1... | collective-permute-start | bytes 786440 | tf_op jit(solution)/shard_map/ppermute | solution.py:433
  46.1 14.4 %collective-permute-start.12 = (f32[1,2,4,2,8,512]{5,4,3,2,1,0:T(8,128)S(1)}, f32[1,2,4,2,8,512]{5,4,3,2,1,0:T(8,128)S(1)}, u32[]{:S(2)}, u32[]{:S(2)}) collective-permute-start(f32[1,2,4,2,8,512]{5,4,3,2,1,0:T(8,128)S(1)} %collective-permute-done.10.refs_2_), channel_id=1, source_target_pairs={{0,4},{1,5},{4,8},{5,9},{6,2},{7,3},{8,12},{9,13},{10,6},{11,7},{1... | collective-permute-start | bytes 786440 | tf_op jit(solution)/shard_map/ppermute | solution.py:433
  49.5 11.6 %collective-permute-start.13 = (f32[1,2,4,2,8,512]{5,4,3,2,1,0:T(8,128)S(1)}, f32[1,2,4,2,8,512]{5,4,3,2,1,0:T(8,128)S(1)}, u32[]{:S(2)}, u32[]{:S(2)}) collective-permute-start(f32[1,2,4,2,8,512]{5,4,3,2,1,0:T(8,128)S(1)} %collective-permute-done.11.refs_3_), channel_id=1, source_target_pairs={{0,4},{1,5},{4,8},{5,9},{6,2},{7,3},{8,12},{9,13},{10,6},{11,7},{1... | collective-permute-start | bytes 786440 | tf_op jit(solution)/shard_map/ppermute | solution.py:433
  61.1 25.5 %copy-start = (f32[512,512]{1,0:T(8,128)S(1)}, f32[512,512]{1,0:T(8,128)}, u32[]{:S(2)}) copy-start(f32[512,512]{1,0:T(8,128)} %constant.7.clone.refs_5_) | copy-start | bytes 3145732
  61.1 25.5 %copy-start.1 = (f32[16,32,64]{2,1,0:T(8,128)S(1)}, f32[16,32,64]{2,1,0:T(8,128)}, u32[]{:S(2)}) copy-start(f32[16,32,64]{2,1,0:T(8,128)} %constant.6.clone.refs_4_) | copy-start | bytes 393220
  70.2 3.3 %collective-permute-start.25 = (f32[16,512]{1,0:T(8,128)S(1)}, f32[16,512]{1,0:T(8,128)S(1)}, u32[]{:S(2)}, u32[]{:S(2)}) collective-permute-start(f32[16,512]{1,0:T(8,128)S(1)} %get-tuple-element.41), channel_id=1, source_target_pairs={{0,1},{1,0},{2,3},{3,2},{4,5},{5,4},{6,7},{7,6},{8,9},{9,8},{10,11... | collective-permute-start | bytes 98312 | tf_op jit(solution)/shard_map/ppermute | solution.py:424
  70.3 4.7 %collective-permute-start.24 = (f32[16,512]{1,0:T(8,128)S(1)}, f32[16,512]{1,0:T(8,128)S(1)}, u32[]{:S(2)}, u32[]{:S(2)}) collective-permute-start(f32[16,512]{1,0:T(8,128)S(1)} %get-tuple-element.41), channel_id=1, source_target_pairs={{0,3},{1,2},{2,1},{3,0},{4,7},{5,6},{6,5},{7,4},{8,11},{9,10},{10,... | collective-permute-start | bytes 98312 | tf_op jit(solution)/shard_map/ppermute | solution.py:424
  73.3 3.9 %collective-permute-start.23 = (f32[16,512]{1,0:T(8,128)S(1)}, f32[16,512]{1,0:T(8,128)S(1)}, u32[]{:S(2)}, u32[]{:S(2)}) collective-permute-start(f32[16,512]{1,0:T(8,128)S(1)} %get-tuple-element.41), channel_id=1, source_target_pairs={{0,2},{1,3},{2,0},{3,1},{4,6},{5,7},{6,4},{7,5},{8,10},{9,11},{10,... | collective-permute-start | bytes 98312 | tf_op jit(solution)/shard_map/ppermute | solution.py:424
  73.4 12.7 %collective-permute-start.7 = (f32[4,2,8,512]{3,2,1,0:T(8,128)S(1)}, f32[4,2,8,512]{3,2,1,0:T(8,128)S(1)}, u32[]{:S(2)}, u32[]{:S(2)}) collective-permute-start(f32[4,2,8,512]{3,2,1,0:T(8,128)S(1)} %get-tuple-element.30), channel_id=1, source_target_pairs={{0,1},{1,0},{2,3},{3,2},{4,5},{5,4},{6,7},{7,6},{8,9},{9,8},{10,11... | collective-permute-start | bytes 393224 | tf_op jit(solution)/shard_map/ppermute | solution.py:424
  77.3 4.0 %collective-permute-start.26 = (f32[1,16,512]{2,1,0:T(8,128)S(1)}, f32[1,16,512]{2,1,0:T(8,128)S(1)}, u32[]{:S(2)}, u32[]{:S(2)}) collective-permute-start(f32[1,16,512]{2,1,0:T(8,128)S(1)} %add_bitcast_fusion.refs_0_), channel_id=1, source_target_pairs={{4,0},{5,1},{6,2},{7,3},{8,4},{9,5},{10,6},{11,7},{12,8},{13,9},{1... | collective-permute-start | bytes 98312 | tf_op jit(solution)/shard_map/ppermute | solution.py:442
  77.3 5.2 %collective-permute-start.27 = (f32[1,16,512]{2,1,0:T(8,128)S(1)}, f32[1,16,512]{2,1,0:T(8,128)S(1)}, u32[]{:S(2)}, u32[]{:S(2)}) collective-permute-start(f32[1,16,512]{2,1,0:T(8,128)S(1)} %add_bitcast_fusion.refs_0_), channel_id=1, source_target_pairs={{8,0},{9,1},{10,2},{11,3},{12,4},{13,5},{14,6},{15,7},{0,8},{1,9},... | collective-permute-start | bytes 98312 | tf_op jit(solution)/shard_map/ppermute | solution.py:442
  78.8 5.7 %collective-permute-start.28 = (f32[1,16,512]{2,1,0:T(8,128)S(1)}, f32[1,16,512]{2,1,0:T(8,128)S(1)}, u32[]{:S(2)}, u32[]{:S(2)}) collective-permute-start(f32[1,16,512]{2,1,0:T(8,128)S(1)} %add_bitcast_fusion.refs_0_), channel_id=1, source_target_pairs={{12,0},{13,1},{14,2},{15,3},{0,4},{1,5},{2,6},{3,7},{4,8},{5,9},{6... | collective-permute-start | bytes 98312 | tf_op jit(solution)/shard_map/ppermute | solution.py:442
  79.8 8.2 %collective-permute-start.8 = (f32[4,2,8,512]{3,2,1,0:T(8,128)S(1)}, f32[4,2,8,512]{3,2,1,0:T(8,128)S(1)}, u32[]{:S(2)}, u32[]{:S(2)}) collective-permute-start(f32[4,2,8,512]{3,2,1,0:T(8,128)S(1)} %get-tuple-element.31), channel_id=1, source_target_pairs={{0,2},{1,3},{2,0},{3,1},{4,6},{5,7},{6,4},{7,5},{8,10},{9,11},{10,... | collective-permute-start | bytes 393224 | tf_op jit(solution)/shard_map/ppermute | solution.py:424
  81.2 6.8 %collective-permute-start.9 = (f32[4,2,8,512]{3,2,1,0:T(8,128)S(1)}, f32[4,2,8,512]{3,2,1,0:T(8,128)S(1)}, u32[]{:S(2)}, u32[]{:S(2)}) collective-permute-start(f32[4,2,8,512]{3,2,1,0:T(8,128)S(1)} %get-tuple-element.32), channel_id=1, source_target_pairs={{0,3},{1,2},{2,1},{3,0},{4,7},{5,6},{6,5},{7,4},{8,11},{9,10},{10,... | collective-permute-start | bytes 393224 | tf_op jit(solution)/shard_map/ppermute | solution.py:424
  82.5 5.5 %collective-permute-start.20 = (f32[4,2,8,512]{3,2,1,0:T(8,128)S(1)}, f32[4,2,8,512]{3,2,1,0:T(8,128)S(1)}, u32[]{:S(2)}, u32[]{:S(2)}) collective-permute-start(f32[4,2,8,512]{3,2,1,0:T(8,128)S(1)} %get-tuple-element.38), channel_id=1, source_target_pairs={{0,1},{1,0},{2,3},{3,2},{4,5},{5,4},{6,7},{7,6},{8,9},{9,8},{10,11... | collective-permute-start | bytes 393224 | tf_op jit(solution)/shard_map/ppermute | solution.py:424
  84.6 6.4 %collective-permute-start.21 = (f32[4,2,8,512]{3,2,1,0:T(8,128)S(1)}, f32[4,2,8,512]{3,2,1,0:T(8,128)S(1)}, u32[]{:S(2)}, u32[]{:S(2)}) collective-permute-start(f32[4,2,8,512]{3,2,1,0:T(8,128)S(1)} %get-tuple-element.39), channel_id=1, source_target_pairs={{0,2},{1,3},{2,0},{3,1},{4,6},{5,7},{6,4},{7,5},{8,10},{9,11},{10,... | collective-permute-start | bytes 393224 | tf_op jit(solution)/shard_map/ppermute | solution.py:424
  86.0 6.5 %collective-permute-start.22 = (f32[4,2,8,512]{3,2,1,0:T(8,128)S(1)}, f32[4,2,8,512]{3,2,1,0:T(8,128)S(1)}, u32[]{:S(2)}, u32[]{:S(2)}) collective-permute-start(f32[4,2,8,512]{3,2,1,0:T(8,128)S(1)} %get-tuple-element.40), channel_id=1, source_target_pairs={{0,3},{1,2},{2,1},{3,0},{4,7},{5,6},{6,5},{7,4},{8,11},{9,10},{10,... | collective-permute-start | bytes 393224 | tf_op jit(solution)/shard_map/ppermute | solution.py:424

commit v4 on v3

--- a/solution.py
+++ b/solution.py
@@ -53,7 +53,7 @@
     return lax.rem(lax.axis_index("gz"), TEAM)
 
 
-def prepare(jobs, fields, sums_before):
+def prepare(jobs, fields, sums_before, by_core=False):
     state, target, rock_type, log_table, obs_scale = fields
     samples, planes, rows_y, columns = state.shape
     slots = samples // TEAM
@@ -62,10 +62,13 @@
     depth_total = planes * lax.axis_size("gz")
     flat = [(o, i, job) for o, group in enumerate(jobs) for i, job in enumerate(group)]
     count = len(flat)
+    shapes = [(len(group), 2, planes, 2, half, columns) for group in jobs]
+    if by_core:
+        shapes = [(len(jobs),) + shapes[0]]
 
     def kernel(before_ref, table_ref, scale_ref, state_ref, target_ref, rock_ref, *rest):
-        outs, sums_ref = rest[: len(jobs)], rest[len(jobs)]
-        table, scale, state_buf, rock_buf, target_buf, mixed, sems = rest[len(jobs) + 1 :]
+        outs, sums_ref = rest[: len(shapes)], rest[len(shapes)]
+        table, scale, state_buf, rock_buf, target_buf, mixed, sems = rest[len(shapes) + 1 :]
         place = team_place()
         first_plane = lax.axis_index("gz") * planes
         members = [slots * (place ^ m) + slot for _, _, (slot, m) in flat]
@@ -96,6 +99,8 @@
                 jnp.exp(jnp.full((8, columns), table[member, code], F32)) for code in range(NR)
             ]
             own_scale = scale[member]
+            at = (lax.rem(place, 2) ^ o, i) if by_core else (i,)
+            out_ref = outs[0 if by_core else o]
             total = jnp.zeros((8, columns), F32)
             for p in range(planes):
                 depth_weight = 1.0 + (2.0 / (depth_total - 1)) * (first_plane + p).astype(F32)
@@ -118,7 +123,7 @@
                 for a in range(2):
                     for t in range(2):
                         for c in range(tiles):
-                            outs[o][i, a, p, t, :, c * 128 : (c + 1) * 128] = mixed[
+                            out_ref[*at, a, p, t, :, c * 128 : (c + 1) * 128] = mixed[
                                 n % 2, p, a, c, pl.ds(t, half, stride=2), :
                             ]
             summed = jnp.sum(total, keepdims=True)
@@ -128,10 +133,10 @@
     vmem = pl.BlockSpec(memory_space=pltpu.VMEM)
     results = pl.pallas_call(
         kernel,
-        out_shape=[jax.ShapeDtypeStruct((len(group), 2, planes, 2, half, columns), F32) for group in jobs]
-        + [jax.ShapeDtypeStruct((samples, LANES), F32)],
+        out_shape=[jax.ShapeDtypeStruct(shape, F32) for shape in shapes]
+        + [jax.ShapeDtypeStruct(sums_before.shape, F32)],
         in_specs=[vmem] + [hbm] * 5,
-        out_specs=[vmem] * (len(jobs) + 1),
+        out_specs=[vmem] * (len(shapes) + 1),
         scratch_shapes=[
             pltpu.SMEM(log_table.shape, F32),
             pltpu.SMEM(obs_scale.shape, F32),
@@ -170,49 +175,101 @@
         body(p)
 
 
-def risk(sums, cells):
-    misfit = sums * (1.0 / (2.0 * cells))
-    mean = jnp.mean(misfit, axis=0, keepdims=True)
-    deviation = misfit - mean
-    variance = jnp.mean(deviation * deviation, axis=0, keepdims=True)
-    return 1.0 + 2.0 * BETA_RISK * deviation, mean, variance
-
-
-def solve(slot, blocks, halos, sums=None, faces=()):
-    inputs = list(blocks) + list(halos)
-    weigh = sums is not None
-    extra = [sums, *faces] if weigh else []
-    slots = len(faces) + 1
-    planes, _, half, columns = blocks[0].shape[2:]
-    near = [0, 1, 4, 5]
+def team_sums(first):
+    def kernel(*refs):
+        last = first[0].shape[0] - 1
+        total = refs[0][last]
+        for ref in refs[1:TEAM]:
+            total = total + ref[last]
+        refs[TEAM][...] = total[:, :LANES]
+
+    vmem = pl.BlockSpec(memory_space=pltpu.VMEM)
+    return pl.pallas_call(
+        kernel,
+        out_shape=jax.ShapeDtypeStruct((first[0].shape[1], LANES), F32),
+        in_specs=[vmem] * TEAM,
+        out_specs=vmem,
+        name="team_sums",
+    )(*first)
+
+
+def weigh(sums, first, faces, planes, cells):
+    own = TEAM * planes
+    half, columns = faces[0].shape[1:]
+    slots = 2
+    samples = sums[0].shape[0]
+
+    def kernel(*refs):
+        sum_refs, refs = refs[: len(sums)], refs[len(sums) :]
+        first_refs, face_refs, refs = refs[:TEAM], refs[TEAM : 2 * TEAM], refs[2 * TEAM :]
+        out_ref, moments_ref, weights = refs
+        place = team_place()
+        summed = sum_refs[0][...]
+        for ref in sum_refs[1:]:
+            summed = summed + ref[...]
+        misfit = summed * (1.0 / (2.0 * cells))
+        mean = jnp.sum(misfit, axis=0, keepdims=True) * (1.0 / samples)
+        deviation = misfit - mean
+        variance = jnp.sum(deviation * deviation, axis=0, keepdims=True) * (1.0 / samples)
+        lane = lax.broadcasted_iota(jnp.int32, (1, LANES), 1)
+        moments_ref[...] = jnp.where(lane == 0, mean, variance)
+        weights[...] = 1.0 + 2.0 * BETA_RISK * deviation
+        for tile in range(own // half):
+            total = jnp.zeros((half, columns), F32)
+            for slot in range(slots):
+                for m in range(TEAM):
+                    row = weights[pl.ds(slots * (place ^ m) + slot, 1), :]
+                    wide = jnp.concatenate([row] * (columns // LANES), axis=1)
+                    face = face_refs[m][tile] if slot else first_refs[m][2 * planes + tile]
+                    total = total + wide * face
+            out_ref[0, tile * half : (tile + 1) * half, :] = total
+
+    vmem = pl.BlockSpec(memory_space=pltpu.VMEM)
+    return pl.pallas_call(
+        kernel,
+        out_shape=[
+            jax.ShapeDtypeStruct((1, own, columns), F32),
+            jax.ShapeDtypeStruct((1, LANES), F32),
+        ],
+        in_specs=[vmem] * (len(sums) + 2 * TEAM),
+        out_specs=[vmem, vmem],
+        scratch_shapes=[pltpu.VMEM((samples, LANES), F32)],
+        compiler_params=pltpu.CompilerParams(vmem_limit_bytes=16 * MIB),
+        name="weigh",
+    )(*sums, *first, *faces)
+
+
+def solve(slot, near, far, near_halo, far_halo, sums=None):
+    inputs = [near, near_halo, *far, *far_halo]
+    extra = [] if sums is None else [sums]
+    planes, _, half, columns = far[0].shape[2:]
     halo = 2 * planes
     own = TEAM * planes
     span = own + 2 * halo
-    cells = planes * lax.axis_size("gz") * 2 * half * columns
     centre, coefficients = chebyshev_constants(DEGREE)
     assert halo >= STEPS
+    tail = (own + sums.shape[0]) // half if extra else 0
 
     def kernel(*refs):
-        ins, refs = refs[:8], refs[8:]
+        ins, refs = refs[:6], refs[6:]
         given, refs = refs[: len(extra)], refs[len(extra) :]
         outs, face_ref, refs = refs[:TEAM], refs[TEAM], refs[TEAM + 1 :]
-        if weigh:
-            moments_ref, weights, refs = refs[0], refs[-1], refs[1:-1]
         cond, u_a, u_b, s_a, s_b, zp, zm, yp, ym, xp, xm, t_a, t_b = refs
         place = team_place()
         column, side = lax.rem(place, 2), place // 2
         upper, lower = halo + own, 0
         near_base = jnp.where(side == 0, upper, lower)
         far_base = jnp.where(side == 0, lower, upper)
-        bases = [halo + planes * (place ^ m) for m in range(TEAM)]
-        bases += [near_base + planes * column, near_base + planes * (1 - column)]
-        bases += [far_base + planes * column, far_base + planes * (1 - column)]
-        for n, base in enumerate(bases):
-            item = slot if n in near else 0
+        blocks = [(ins[0].at[core, slot], halo + planes * (2 * side + core)) for core in range(2)]
+        blocks += [(ins[1].at[core, slot], near_base + planes * core) for core in range(2)]
+        blocks += [(ins[m].at[0], halo + planes * (place ^ m)) for m in (2, 3)]
+        blocks += [(ins[4].at[0], far_base + planes * column)]
+        blocks += [(ins[5].at[0], far_base + planes * (1 - column))]
+        for block, base in blocks:
             for j in range(planes):
                 for t in range(2):
-                    cond[base + j, t] = jnp.maximum(ins[n][item, 0, j, t], 1e-30)
-                    t_a[base + j, t] = ins[n][item, 1, j, t]
+                    cond[base + j, t] = jnp.maximum(block[0, j, t], 1e-30)
+                    t_a[base + j, t] = block[1, j, t]
 
         last_row = lax.broadcasted_iota(jnp.int32, (half, columns), 0) == half - 1
         last_column = lax.broadcasted_iota(jnp.int32, (half, columns), 1) == columns - 1
@@ -291,39 +348,31 @@
             base = halo + planes * (place ^ m)
             for j in range(planes):
                 for t in range(2):
-                    outs[m][j, t] = t_now[base + j, t]
-        face = jnp.concatenate([t_now[halo + p, 0, 0:1, :] for p in range(own)], axis=0)
-        if weigh:
-            weights[...], mean, variance = risk(given[0][...], cells)
-            lane = lax.broadcasted_iota(jnp.int32, (1, LANES), 1)
-            moments_ref[...] = jnp.where(lane == 0, mean, variance)
-            total = jnp.zeros((own, columns), F32)
-            for n, values in enumerate([ref[...] for ref in given[1:]] + [face]):
-                row = weights[pl.ds(slots * place + n, 1), :]
-                total = total + values * jnp.concatenate([row] * (columns // LANES), axis=1)
-            face_ref[...] = total
-        else:
-            face_ref[...] = face
+                    outs[m][2 * j + t] = t_now[base + j, t]
+        for p in range(own):
+            face_ref[p // half, p % half : p % half + 1, :] = t_now[halo + p, 0, 0:1, :]
+        for m in range(TEAM if extra else 0):
+            outs[m][2 * planes : 2 * planes + own // half] = face_ref[...]
+            outs[m][2 * planes + own // half] = given[0][...]
 
     vmem = pl.BlockSpec(memory_space=pltpu.VMEM)
     field = pltpu.VMEM((span, 2, half, columns), F32)
     return pl.pallas_call(
         kernel,
-        out_shape=[jax.ShapeDtypeStruct((planes, 2, half, columns), F32)] * TEAM
-        + [jax.ShapeDtypeStruct((own, columns), F32)]
-        + [jax.ShapeDtypeStruct((1, LANES), F32)] * weigh,
-        in_specs=[vmem] * (8 + len(extra)),
-        out_specs=[vmem] * (TEAM + 1 + weigh),
-        scratch_shapes=[field] * 13 + ([pltpu.VMEM(sums.shape, F32)] if weigh else []),
+        out_shape=[jax.ShapeDtypeStruct((2 * planes + tail, half, columns), F32)] * TEAM
+        + [jax.ShapeDtypeStruct((own // half, half, columns), F32)],
+        in_specs=[vmem] * (6 + len(extra)),
+        out_specs=[vmem] * (TEAM + 1),
+        scratch_shapes=[field] * 13,
         compiler_params=pltpu.CompilerParams(vmem_limit_bytes=32 * MIB),
         cost_estimate=pl.CostEstimate(flops=0, bytes_accessed=22 * MIB, transcendentals=0),
         name=f"solve{slot}",
     )(*inputs, *extra)
 
 
-def gather_adjoint(pieces):
+def gather_adjoint(pieces, planes):
     slots = len(pieces)
-    planes, _, half, columns = pieces[0][0].shape
+    _, half, columns = pieces[0][0].shape
     tiles = columns // 128
     block = (planes, 2 * half, columns)
 
@@ -338,7 +387,7 @@
                     for t in range(2):
                         for c in range(tiles):
                             mixed[i % 2, j, c, pl.ds(t, half, stride=2), :] = blocks[i][
-                                j, t, :, c * 128 : (c + 1) * 128
+                                2 * j + t, :, c * 128 : (c + 1) * 128
                             ]
                     for c in range(tiles):
                         held[i, j, :, c * 128 : (c + 1) * 128] = mixed[i % 2, j, c]
@@ -442,46 +491,47 @@
             heard.append(lax.ppermute(value, "gz", pairs))
         return heard
 
-    def team_sum(value):
-        return sum((swap(value, m) for m in (2, 3, 1)), value)
-
     fields = [
         pltpu.with_memory_space_constraint(field, pltpu.HBM)
         for field in (state, target, rock_type, log_table, obs_scale)
     ]
-    sums = jnp.zeros((samples, LANES), F32)
-    far = []
+    sums = jnp.zeros((samples, columns), F32)
+    jobs = [[(slot, m) for slot in range(slots)] for m in range(2)]
+    far = [None] * slots
+    blocks, sums = prepare([[(0, 2)], [(0, 3)]], fields, sums)
+    far[0] = [swap(blocks[0], 2), swap(blocks[1], 3)]
+    (near_blocks,), sums = prepare(jobs, fields, sums, by_core=True)
+    for slot in range(1, slots):
+        blocks, sums = prepare([[(slot, 2)], [(slot, 3)]], fields, sums)
+        far[slot] = [swap(blocks[0], 2), swap(blocks[1], 3)]
+    blocks = near_blocks
+    chips = [[i, i + 1] for i in range(0, slabs, 2)]
+    near = lax.all_to_all(
+        blocks, "gz", split_axis=0, concat_axis=0, axis_index_groups=chips, tiled=True
+    )
+    near_halo = along(near, True)
+
+    pieces = []
     for slot in range(slots):
-        blocks, sums = prepare([[(slot, 2)], [(slot, 3)]], fields, sums)
-        far.append([swap(blocks[0], 2), swap(blocks[1], 3)])
-    blocks, sums = prepare([[(slot, m) for slot in range(slots)] for m in range(2)], fields, sums)
-    near = [blocks[0], swap(blocks[1], 1)]
-    near_halo = [along(block, True) for block in near]
-
-    sums = team_sum(sums)
+        far_halo = [along(block, False) for block in far[slot]]
+        solved = solve(slot, near, far[slot], near_halo, far_halo, None if slot else sums)
+        pieces.append([solved[0]] + [swap(solved[m], m) for m in (1, 2, 3)])
+    faces = [solved[TEAM]] + [swap(solved[TEAM], m) for m in (1, 2, 3)]
+
+    sums = [team_sums(pieces[0])]
     stride = 1
     for radix in radices:
-        sums = sum(from_teams(sums, stride, radix), sums)
+        held = sum(sums[1:], sums[0])
+        sums = [held] + from_teams(held, stride, radix)
         stride *= radix
-
-    pieces, faces = [], []
-    for slot in range(slots):
-        last = slot == slots - 1
-        far_halo = [along(block, False) for block in far[slot]]
-        solved = solve(
-            slot, near + far[slot], near_halo + far_halo, *((sums, faces) if last else ())
-        )
-        pieces.append([solved[0]] + [swap(solved[m], m) for m in (1, 2, 3)])
-        faces.append(solved[TEAM])
-    moments = solved[TEAM + 1]
-
-    heard = [team_sum(faces[-1])[None]]
+    heard, moments = weigh(sums, pieces[0], faces, planes, depth_total * rows_y * columns)
+    heard = [heard]
     stride = 1
     for radix in radices:
         held = heard[0] if len(heard) == 1 else jnp.concatenate(heard)
         heard = [held] + from_teams(held, stride, radix)
         stride *= radix
-    adjoint = gather_adjoint(pieces)
+    adjoint = gather_adjoint(pieces, planes)
     own_count = MA // slabs
     gradient = control(
         heard,

time: 94 us -> 88.9 us (0.946)
  waiting for transfers between devices: 32.9 us -> 15.2 us
  blocking collectives: 0 us -> 4.58 us
  local copies, waits for them, and re-layouts: 0.52 us -> 3.98 us
  Pallas kernels: 25.7 us -> 28.1 us
  starting transfers between devices: 33.7 us -> 35.8 us
    ppermute x17 -> x13, waiting for transfers between devices: 19.2 us -> 9.52 us  [swap(): return lax.ppermute(value, 'gz', [(i, i ^ m) for i in range(slabs)])]
    ppermute x6, waiting for transfers between devices: 13.2 us -> 5.7 us  [from_teams(): heard.append(lax.ppermute(value, 'gz', pairs))]
    all_to_all x0 -> x1, blocking collectives: none -> 4.58 us  [on_device(): lax.all_to_all(blocks, 'gz', split_axis=0, concat_axis=0, axis_index_grou...]
    unnamed x4 -> x22, local copies, waits for them, and re-layouts: 0.01 us -> 3.46 us
    pallas_call x5 -> x7, Pallas kernels: 23.2 us -> 25.6 us  [the longest x2 18.7 us: solve(): pl.pallas_call(kernel, out_shape=[jax.ShapeDtypeStruct((2 * planes + tail...]
    ppermute x6, starting transfers between devices: 6.18 us -> 7.3 us  [from_teams(): heard.append(lax.ppermute(value, 'gz', pairs))]
    ppermute x6 -> x5, starting transfers between devices: 13.9 us -> 15 us  [along(): return lax.ppermute(value, 'gz', pairs)]
    ppermute x17 -> x13, starting transfers between devices: 13.6 us -> 13.5 us  [swap(): return lax.ppermute(value, 'gz', [(i, i ^ m) for i in range(slabs)])]
  transfers between devices with their start and end apart: 29 -> 24, of which waited for: 15 -> 9; matrix products, arithmetic and copies ran while one was open for 1% -> 1% of each run, Pallas kernels for 11% -> 26%
where the time goes in v4:
time: 88.9 us; the launch traced here: 88.5 us
  starting transfers between devices  35.8 us (40%)
  Pallas kernels  28.1 us (32%)
  waiting for transfers between devices  15.2 us (17%)
  blocking collectives  4.58 us (5%)
  local copies, waits for them, and re-layouts  3.98 us (4%)
    pallas_call x2, Pallas kernels, solve(): pl.pallas_call(kernel, out_shape=[jax.ShapeDtypeStruct((2 * planes + tail...  18.7 us
    ppermute x5, starting transfers between devices, along(): return lax.ppermute(value, 'gz', pairs)  15 us
    ppermute x13, starting transfers between devices, swap(): return lax.ppermute(value, 'gz', [(i, i ^ m) for i in range(slabs)])  13.5 us
    ppermute x13, waiting for transfers between devices, swap(): return lax.ppermute(value, 'gz', [(i, i ^ m) for i in range(slabs)])  9.52 us
    ppermute x6, starting transfers between devices, from_teams(): heard.append(lax.ppermute(value, 'gz', pairs))  7.3 us
    ppermute x6, waiting for transfers between devices, from_teams(): heard.append(lax.ppermute(value, 'gz', pairs))  5.7 us
    pallas_call x3, Pallas kernels, prepare(): pl.pallas_call(kernel, out_shape=[jax.ShapeDtypeStruct(shape, F32) for sh...  5.04 us
    all_to_all x1, blocking collectives, on_device(): lax.all_to_all(blocks, 'gz', split_axis=0, concat_axis=0, axis_index_grou...  4.58 us
  transfers between devices with their start and end apart: 24, of which 9 were waited for; matrix products, arithmetic and copies ran while one was open for 1% of the time, Pallas kernels for 26%

profile of v4, /device:TPU:0, one launch (start us, length us, event | category | flops | bytes accessed | tf_op | source)
XLA Modules:
  0.0 88.5 jit_solution(11012596245289408018)
XLA Ops:
  0.6 1.5 %prepare.3 = (f32[1,2,4,2,8,512]{5,4,3,2,1,0:T(8,128)S(1)}, f32[1,2,4,2,8,512]{5,4,3,2,1,0:T(8,128)S(1)}, f32[8,512]{1,0:T(8,128)S(1)}) custom-call(f32[8,512]{1,0:T(8,128)S(1)} %broadcast_in_dim.3.before_ref, f32[8,8]{1,0:T(8,128)} %table_ref.5, f32[8]{0:T(128)} %scale_ref.5, f32[8,4,16,512]{3,2,1,0:T(8,128)} %state_ref.5, f32[4,16,512]{2,1,0:T(8,128)} %target_ref.5, ...), custom_call_target="tpu_custom_call" | custom-call | bytes 2097152 | tf_op jit(solution)/shard_map/prepare/pallas_call | solution.py:134
  2.2 2.0 %prepare.4 = (f32[2,2,2,4,2,8,512]{6,5,4,3,2,1,0:T(8,128)S(1)}, f32[8,512]{1,0:T(8,128)S(1)}) custom-call(f32[8,512]{1,0:T(8,128)S(1)} %get-tuple-element.22.before_ref, f32[8,8]{1,0:T(8,128)} %table_ref.5, f32[8]{0:T(128)} %scale_ref.5, f32[8,4,16,512]{3,2,1,0:T(8,128)} %state_ref.5, f32[4,16,512]{2,1,0:T(8,128)} %target_ref.5, s32[8,4,16,512]{3,2,1,0:T(8,128)} %rock_ref.5), custom_call_target="tpu_custom_call" | custom-call | bytes 4194304 | tf_op jit(solution)/shard_map/prepare/pallas_call | solution.py:134
  4.2 4.6 %all_to_all.5.refs_0_ = f32[2,2,2,4,2,8,512]{6,5,4,3,2,1,0:T(8,128)S(1)} all-to-all(f32[2,2,2,4,2,8,512]{6,5,4,3,2,1,0:T(8,128)S(1)} %get-tuple-element.23), channel_id=1, replica_groups={{0,1},{2,3},{4,5},{6,7},{8,9},{10,11},{12,13},{14,15},{16,17},{18,19},{..., dimensions={0} | all-to-all | bytes 2097152 | tf_op jit(solution)/shard_map/all_to_all | solution.py:509
  8.7 1.3 %collective-permute-start = (f32[2,2,2,4,2,8,512]{6,5,4,3,2,1,0:T(8,128)S(1)}, f32[2,2,2,4,2,8,512]{6,5,4,3,2,1,0:T(8,128)S(1)}, u32[]{:S(2)}, u32[]{:S(2)}) collective-permute-start(f32[2,2,2,4,2,8,512]{6,5,4,3,2,1,0:T(8,128)S(1)} %all_to_all.5.refs_0_), channel_id=1, source_target_pairs={{2,6},{3,7},{4,0},{5,1},{6,10},{7,11},{8,4},{9,5},{10,14},{11,15},... | collective-permute-start | bytes 3145736 | tf_op jit(solution)/shard_map/ppermute | solution.py:482
  10.0 5.3 %collective-permute-start.1 = (f32[1,2,4,2,8,512]{5,4,3,2,1,0:T(8,128)S(1)}, f32[1,2,4,2,8,512]{5,4,3,2,1,0:T(8,128)S(1)}, u32[]{:S(2)}, u32[]{:S(2)}) collective-permute-start(f32[1,2,4,2,8,512]{5,4,3,2,1,0:T(8,128)S(1)} %get-tuple-element.24), channel_id=1, source_target_pairs={{0,2},{1,3},{2,0},{3,1},{4,6},{5,7},{6,4},{7,5},{8,10},{9,11},{10,... | collective-permute-start | bytes 786440 | tf_op jit(solution)/shard_map/ppermute | solution.py:473
  15.3 1.5 %prepare.5 = (f32[1,2,4,2,8,512]{5,4,3,2,1,0:T(8,128)S(1)}, f32[1,2,4,2,8,512]{5,4,3,2,1,0:T(8,128)S(1)}, f32[8,512]{1,0:T(8,128)S(1)}) custom-call(f32[8,512]{1,0:T(8,128)S(1)} %get-tuple-element.26.before_ref, f32[8,8]{1,0:T(8,128)} %table_ref.5, f32[8]{0:T(128)} %scale_ref.5, f32[8,4,16,512]{3,2,1,0:T(8,128)} %state_ref.5, f32[4,16,512]{2,1,0:T(8,128)} %target_ref.5, ...), custom_call_target="tpu_custom_call" | custom-call | bytes 2097152 | tf_op jit(solution)/shard_map/prepare/pallas_call | solution.py:134
  16.8 1.3 %collective-permute-start.8 = (f32[1,2,4,2,8,512]{5,4,3,2,1,0:T(8,128)S(1)}, f32[1,2,4,2,8,512]{5,4,3,2,1,0:T(8,128)S(1)}, u32[]{:S(2)}, u32[]{:S(2)}) collective-permute-start(f32[1,2,4,2,8,512]{5,4,3,2,1,0:T(8,128)S(1)} %get-tuple-element.32), channel_id=1, source_target_pairs={{0,2},{1,3},{2,0},{3,1},{4,6},{5,7},{6,4},{7,5},{8,10},{9,11},{10,... | collective-permute-start | bytes 786440 | tf_op jit(solution)/shard_map/ppermute | solution.py:473
  18.1 0.6 collective-permute-start.9
  18.7 3.7 %collective-permute-done.1.refs_2_ = f32[1,2,4,2,8,512]{5,4,3,2,1,0:T(8,128)S(1)} collective-permute-done((f32[1,2,4,2,8,512]{5,4,3,2,1,0:T(8,128)S(1)}, f32[1,2,4,2,8,512]{5,4,3,2,1,0:T(8,128)S(1)}, u32[]{:S(2)}, u32[]{:S(2)}) %collective-permute-start.1) | collective-permute-done | bytes 262176 | tf_op jit(solution)/shard_map/ppermute | solution.py:473
  22.4 3.4 %collective-permute-start.3 = (f32[1,2,4,2,8,512]{5,4,3,2,1,0:T(8,128)S(1)}, f32[1,2,4,2,8,512]{5,4,3,2,1,0:T(8,128)S(1)}, u32[]{:S(2)}, u32[]{:S(2)}) collective-permute-start(f32[1,2,4,2,8,512]{5,4,3,2,1,0:T(8,128)S(1)} %collective-permute-done.1.refs_2_), channel_id=1, source_target_pairs={{0,4},{1,5},{4,8},{5,9},{6,2},{7,3},{8,12},{9,13},{10,6},{11,7},{1... | collective-permute-start | bytes 786440 | tf_op jit(solution)/shard_map/ppermute | solution.py:482
  25.9 1.8 %collective-permute-done.2.refs_3_ = f32[1,2,4,2,8,512]{5,4,3,2,1,0:T(8,128)S(1)} collective-permute-done((f32[1,2,4,2,8,512]{5,4,3,2,1,0:T(8,128)S(1)}, f32[1,2,4,2,8,512]{5,4,3,2,1,0:T(8,128)S(1)}, u32[]{:S(2)}, u32[]{:S(2)}) %collective-permute-start.2) | collective-permute-done | bytes 262176 | tf_op jit(solution)/shard_map/ppermute | solution.py:473
  27.6 3.4 %collective-permute-start.4 = (f32[1,2,4,2,8,512]{5,4,3,2,1,0:T(8,128)S(1)}, f32[1,2,4,2,8,512]{5,4,3,2,1,0:T(8,128)S(1)}, u32[]{:S(2)}, u32[]{:S(2)}) collective-permute-start(f32[1,2,4,2,8,512]{5,4,3,2,1,0:T(8,128)S(1)} %collective-permute-done.2.refs_3_), channel_id=1, source_target_pairs={{0,4},{1,5},{4,8},{5,9},{6,2},{7,3},{8,12},{9,13},{10,6},{11,7},{1... | collective-permute-start | bytes 786440 | tf_op jit(solution)/shard_map/ppermute | solution.py:482
  31.1 2.6 %collective-permute-done.8.refs_2_ = f32[1,2,4,2,8,512]{5,4,3,2,1,0:T(8,128)S(1)} collective-permute-done((f32[1,2,4,2,8,512]{5,4,3,2,1,0:T(8,128)S(1)}, f32[1,2,4,2,8,512]{5,4,3,2,1,0:T(8,128)S(1)}, u32[]{:S(2)}, u32[]{:S(2)}) %collective-permute-start.8) | collective-permute-done | bytes 262176 | tf_op jit(solution)/shard_map/ppermute | solution.py:473
  33.7 3.4 %collective-permute-start.10 = (f32[1,2,4,2,8,512]{5,4,3,2,1,0:T(8,128)S(1)}, f32[1,2,4,2,8,512]{5,4,3,2,1,0:T(8,128)S(1)}, u32[]{:S(2)}, u32[]{:S(2)}) collective-permute-start(f32[1,2,4,2,8,512]{5,4,3,2,1,0:T(8,128)S(1)} %collective-permute-done.8.refs_2_), channel_id=1, source_target_pairs={{0,4},{1,5},{4,8},{5,9},{6,2},{7,3},{8,12},{9,13},{10,6},{11,7},{1... | collective-permute-start | bytes 786440 | tf_op jit(solution)/shard_map/ppermute | solution.py:482
  37.1 0.6 collective-permute-done.9.refs_3_
  37.7 3.4 %collective-permute-start.11 = (f32[1,2,4,2,8,512]{5,4,3,2,1,0:T(8,128)S(1)}, f32[1,2,4,2,8,512]{5,4,3,2,1,0:T(8,128)S(1)}, u32[]{:S(2)}, u32[]{:S(2)}) collective-permute-start(f32[1,2,4,2,8,512]{5,4,3,2,1,0:T(8,128)S(1)} %collective-permute-done.9.refs_3_), channel_id=1, source_target_pairs={{0,4},{1,5},{4,8},{5,9},{6,2},{7,3},{8,12},{9,13},{10,6},{11,7},{1... | collective-permute-start | bytes 786440 | tf_op jit(solution)/shard_map/ppermute | solution.py:482
  41.2 0.0 collective-permute-done.3.refs_4_
  41.2 0.0 collective-permute-done.refs_1_
  41.2 9.7 %solve0.1 = (f32[11,8,512]{2,1,0:T(8,128)S(1)}, f32[11,8,512]{2,1,0:T(8,128)S(1)}, f32[11,8,512]{2,1,0:T(8,128)S(1)}, f32[11,8,512]{2,1,0:T(8,128)S(1)}, f32[2,8,512]{2,1,0:T(8,128)}) custom-call(f32[2,2,2,4,2,8,512]{6,5,4,3,2,1,0:T(8,128)S(1)} %all_to_all.5.refs_0_, f32[2,2,2,4,2,8,512]{6,5,4,3,2,1,0:T(8,128)S(1)} %collective-permute-done.refs_1_, ...), custom_call_target="tpu_custom_call" | custom-call | bytes 23068672 | tf_op jit(solution)/shard_map/solve0/pallas_call | solution.py:360
  50.9 0.7 copy-done
  51.5 0.6 collective-permute-start.5
  52.1 1.4 %collective-permute-start.7 = (f32[11,8,512]{2,1,0:T(8,128)S(1)}, f32[11,8,512]{2,1,0:T(8,128)S(1)}, u32[]{:S(2)}, u32[]{:S(2)}) collective-permute-start(f32[11,8,512]{2,1,0:T(8,128)S(1)} %get-tuple-element.31), channel_id=1, source_target_pairs={{0,3},{1,2},{2,1},{3,0},{4,7},{5,6},{6,5},{7,4},{8,11},{9,10},{10,... | collective-permute-start | bytes 540680 | tf_op jit(solution)/shard_map/ppermute | solution.py:473
  53.5 9.0 %solve1.1 = (f32[8,8,512]{2,1,0:T(8,128)S(1)}, f32[8,8,512]{2,1,0:T(8,128)S(1)}, f32[8,8,512]{2,1,0:T(8,128)S(1)}, f32[8,8,512]{2,1,0:T(8,128)S(1)}, f32[2,8,512]{2,1,0:T(8,128)S(1)}) custom-call(f32[2,2,2,4,2,8,512]{6,5,4,3,2,1,0:T(8,128)S(1)} %all_to_all.5.refs_0_, f32[2,2,2,4,2,8,512]{6,5,4,3,2,1,0:T(8,128)S(1)} %collective-permute-done.refs_1_, ...), custom_call_target="tpu_custom_call" | custom-call | bytes 23068672 | tf_op jit(solution)/shard_map/solve1/pallas_call | solution.py:360
  62.5 0.9 collective-permute-start.18
  63.4 0.1 collective-permute-start.12
  63.5 0.8 collective-permute-done.18.refs_9_
  64.2 0.2 collective-permute-start.13
  64.5 1.5 %collective-permute-start.14 = (f32[8,8,512]{2,1,0:T(8,128)S(1)}, f32[8,8,512]{2,1,0:T(8,128)S(1)}, u32[]{:S(2)}, u32[]{:S(2)}) collective-permute-start(f32[8,8,512]{2,1,0:T(8,128)S(1)} %get-tuple-element.37), channel_id=1, source_target_pairs={{0,3},{1,2},{2,1},{3,0},{4,7},{5,6},{6,5},{7,4},{8,11},{9,10},{10,... | collective-permute-start | bytes 393224 | tf_op jit(solution)/shard_map/ppermute | solution.py:473
  65.9 0.4 collective-permute-start.19
  66.4 1.4 %collective-permute-start.20 = (f32[2,8,512]{2,1,0:T(8,128)S(1)}, f32[2,8,512]{2,1,0:T(8,128)S(1)}, u32[]{:S(2)}, u32[]{:S(2)}) collective-permute-start(f32[2,8,512]{2,1,0:T(8,128)S(1)} %get-tuple-element.38.refs_8_), channel_id=1, source_target_pairs={{0,3},{1,2},{2,1},{3,0},{4,7},{5,6},{6,5},{7,4},{8,11},{9,10},{10,... | collective-permute-start | bytes 98312 | tf_op jit(solution)/shard_map/ppermute | solution.py:473
  67.8 1.8 %team_sums.1.refs_0_ = f32[8,128]{1,0:T(8,128)} custom-call(f32[11,8,512]{2,1,0:T(8,128)} %copy-done, f32[11,8,512]{2,1,0:T(8,128)} %copy-done.2, f32[11,8,512]{2,1,0:T(8,128)} %copy-done.4, f32[11,8,512]{2,1,0:T(8,128)} %copy-done.6), custom_call_target="tpu_custom_call" | custom-call | tf_op jit(solution)/shard_map/team_sums/pallas_call | solution.py:187
  69.6 2.8 %collective-permute-start.15 = (f32[8,128]{1,0:T(8,128)}, f32[8,128]{1,0:T(8,128)S(1)}, u32[]{:S(2)}, u32[]{:S(2)}) collective-permute-start(f32[8,128]{1,0:T(8,128)} %team_sums.1.refs_0_), channel_id=1, source_target_pairs={{4,0},{5,1},{6,2},{7,3},{8,4},{9,5},{10,6},{11,7},{12,8},{13,9},{1... | collective-permute-start | bytes 12296 | tf_op jit(solution)/shard_map/ppermute | solution.py:491
  72.4 0.3 collective-permute-start.16
  72.6 1.2 %collective-permute-start.17 = (f32[8,128]{1,0:T(8,128)}, f32[8,128]{1,0:T(8,128)S(1)}, u32[]{:S(2)}, u32[]{:S(2)}) collective-permute-start(f32[8,128]{1,0:T(8,128)} %team_sums.1.refs_0_), channel_id=1, source_target_pairs={{12,0},{13,1},{14,2},{15,3},{0,4},{1,5},{2,6},{3,7},{4,8},{5,9},{6... | collective-permute-start | bytes 12296 | tf_op jit(solution)/shard_map/ppermute | solution.py:491
  73.8 0.9 %copy-done.3 = f32[11,8,512]{2,1,0:T(8,128)S(1)} copy-done((f32[11,8,512]{2,1,0:T(8,128)S(1)}, f32[11,8,512]{2,1,0:T(8,128)}, u32[]{:S(2)}) %copy-start.3) | copy-done | bytes 180248
  74.7 0.9 %copy-done.5 = f32[11,8,512]{2,1,0:T(8,128)S(1)} copy-done((f32[11,8,512]{2,1,0:T(8,128)S(1)}, f32[11,8,512]{2,1,0:T(8,128)}, u32[]{:S(2)}) %copy-start.5) | copy-done | bytes 180248
  75.6 0.9 %copy-done.7 = f32[11,8,512]{2,1,0:T(8,128)S(1)} copy-done((f32[11,8,512]{2,1,0:T(8,128)S(1)}, f32[11,8,512]{2,1,0:T(8,128)}, u32[]{:S(2)}) %copy-start.7) | copy-done | bytes 180248
  76.6 1.0 %gather_adjoint.1 = f32[8,4,16,512]{3,2,1,0:T(8,128)} custom-call(f32[11,8,512]{2,1,0:T(8,128)S(1)} %copy-done.1, f32[11,8,512]{2,1,0:T(8,128)S(1)} %copy-done.3, f32[11,8,512]{2,1,0:T(8,128)S(1)} %copy-done.5, f32[11,8,512]{2,1,0:T(8,128)S(1)} %copy-done.7, f32[8,8,512]{2,1,0:T(8,128)S(1)} %get-tuple-element.34.refs_4_, ...), custom_call_target="tpu_custom_call" | custom-call | bytes 4194304 | tf_op jit(solution)/shard_map/gather_adjoint/pallas_call | solution.py:402
  77.6 0.0 copy-start.9
  77.7 0.6 collective-permute-done.17.refs_3_
  78.3 2.2 %collective-permute-start.21 = (f32[1,16,512]{2,1,0:T(8,128)S(1)}, f32[1,16,512]{2,1,0:T(8,128)S(1)}, u32[]{:S(2)}, u32[]{:S(2)}) collective-permute-start(f32[1,16,512]{2,1,0:T(8,128)S(1)} %get-tuple-element.39.refs_0_), channel_id=1, source_target_pairs={{4,0},{5,1},{6,2},{7,3},{8,4},{9,5},{10,6},{11,7},{12,8},{13,9},{1... | collective-permute-start | bytes 98312 | tf_op jit(solution)/shard_map/ppermute | solution.py:491
  80.4 0.9 collective-permute-start.22
  81.3 0.1 collective-permute-start.23
  81.4 0.5 slice_bitcast_fusion
  81.9 0.3 collective-permute-done.21.refs_1_
  82.2 3.4 %collective-permute-done.22.refs_2_ = f32[1,16,512]{2,1,0:T(8,128)S(1)} collective-permute-done((f32[1,16,512]{2,1,0:T(8,128)S(1)}, f32[1,16,512]{2,1,0:T(8,128)S(1)}, u32[]{:S(2)}, u32[]{:S(2)}) %collective-permute-start.22) | collective-permute-done | bytes 32800 | tf_op jit(solution)/shard_map/ppermute | solution.py:491
  85.6 1.4 %collective-permute-done.23.refs_3_ = f32[1,16,512]{2,1,0:T(8,128)S(1)} collective-permute-done((f32[1,16,512]{2,1,0:T(8,128)S(1)}, f32[1,16,512]{2,1,0:T(8,128)S(1)}, u32[]{:S(2)}, u32[]{:S(2)}) %collective-permute-start.23) | collective-permute-done | bytes 32800 | tf_op jit(solution)/shard_map/ppermute | solution.py:491
  87.0 1.4 %control.1 = f32[32,512]{1,0:T(8,128)} custom-call(f32[1,16,512]{2,1,0:T(8,128)S(1)} %get-tuple-element.39.refs_0_, f32[1,16,512]{2,1,0:T(8,128)S(1)} %collective-permute-done.21.refs_1_, f32[1,16,512]{2,1,0:T(8,128)S(1)} %collective-permute-done.22.refs_2_, f32[1,16,512]{2,1,0:T(8,128)S(1)} %collective-permute-done.23.refs_3_, f32[16,32,64]{2,1,0:T(8,128)S(1)} %copy-done.9, ...), custom_call_target="tpu_custom_call" | custom-call | tf_op jit(solution)/shard_map/control/pallas_call | solution.py:445
  (34 shorter events, 0.1 us)
Async XLA Ops:
  8.7 32.4 %collective-permute-start = (f32[2,2,2,4,2,8,512]{6,5,4,3,2,1,0:T(8,128)S(1)}, f32[2,2,2,4,2,8,512]{6,5,4,3,2,1,0:T(8,128)S(1)}, u32[]{:S(2)}, u32[]{:S(2)}) collective-permute-start(f32[2,2,2,4,2,8,512]{6,5,4,3,2,1,0:T(8,128)S(1)} %all_to_all.5.refs_0_), channel_id=1, source_target_pairs={{2,6},{3,7},{4,0},{5,1},{6,10},{7,11},{8,4},{9,5},{10,14},{11,15},... | collective-permute-start | bytes 3145736 | tf_op jit(solution)/shard_map/ppermute | solution.py:482
  10.0 12.4 %collective-permute-start.1 = (f32[1,2,4,2,8,512]{5,4,3,2,1,0:T(8,128)S(1)}, f32[1,2,4,2,8,512]{5,4,3,2,1,0:T(8,128)S(1)}, u32[]{:S(2)}, u32[]{:S(2)}) collective-permute-start(f32[1,2,4,2,8,512]{5,4,3,2,1,0:T(8,128)S(1)} %get-tuple-element.24), channel_id=1, source_target_pairs={{0,2},{1,3},{2,0},{3,1},{4,6},{5,7},{6,4},{7,5},{8,10},{9,11},{10,... | collective-permute-start | bytes 786440 | tf_op jit(solution)/shard_map/ppermute | solution.py:473
  15.3 12.3 %collective-permute-start.2 = (f32[1,2,4,2,8,512]{5,4,3,2,1,0:T(8,128)S(1)}, f32[1,2,4,2,8,512]{5,4,3,2,1,0:T(8,128)S(1)}, u32[]{:S(2)}, u32[]{:S(2)}) collective-permute-start(f32[1,2,4,2,8,512]{5,4,3,2,1,0:T(8,128)S(1)} %get-tuple-element.25), channel_id=1, source_target_pairs={{0,3},{1,2},{2,1},{3,0},{4,7},{5,6},{6,5},{7,4},{8,11},{9,10},{10,... | collective-permute-start | bytes 786440 | tf_op jit(solution)/shard_map/ppermute | solution.py:473
  16.8 16.8 %collective-permute-start.8 = (f32[1,2,4,2,8,512]{5,4,3,2,1,0:T(8,128)S(1)}, f32[1,2,4,2,8,512]{5,4,3,2,1,0:T(8,128)S(1)}, u32[]{:S(2)}, u32[]{:S(2)}) collective-permute-start(f32[1,2,4,2,8,512]{5,4,3,2,1,0:T(8,128)S(1)} %get-tuple-element.32), channel_id=1, source_target_pairs={{0,2},{1,3},{2,0},{3,1},{4,6},{5,7},{6,4},{7,5},{8,10},{9,11},{10,... | collective-permute-start | bytes 786440 | tf_op jit(solution)/shard_map/ppermute | solution.py:473
  18.1 19.6 %collective-permute-start.9 = (f32[1,2,4,2,8,512]{5,4,3,2,1,0:T(8,128)S(1)}, f32[1,2,4,2,8,512]{5,4,3,2,1,0:T(8,128)S(1)}, u32[]{:S(2)}, u32[]{:S(2)}) collective-permute-start(f32[1,2,4,2,8,512]{5,4,3,2,1,0:T(8,128)S(1)} %get-tuple-element.33), channel_id=1, source_target_pairs={{0,3},{1,2},{2,1},{3,0},{4,7},{5,6},{6,5},{7,4},{8,11},{9,10},{10,... | collective-permute-start | bytes 786440 | tf_op jit(solution)/shard_map/ppermute | solution.py:473
  22.4 18.7 %collective-permute-start.3 = (f32[1,2,4,2,8,512]{5,4,3,2,1,0:T(8,128)S(1)}, f32[1,2,4,2,8,512]{5,4,3,2,1,0:T(8,128)S(1)}, u32[]{:S(2)}, u32[]{:S(2)}) collective-permute-start(f32[1,2,4,2,8,512]{5,4,3,2,1,0:T(8,128)S(1)} %collective-permute-done.1.refs_2_), channel_id=1, source_target_pairs={{0,4},{1,5},{4,8},{5,9},{6,2},{7,3},{8,12},{9,13},{10,6},{11,7},{1... | collective-permute-start | bytes 786440 | tf_op jit(solution)/shard_map/ppermute | solution.py:482
  27.6 13.6 %collective-permute-start.4 = (f32[1,2,4,2,8,512]{5,4,3,2,1,0:T(8,128)S(1)}, f32[1,2,4,2,8,512]{5,4,3,2,1,0:T(8,128)S(1)}, u32[]{:S(2)}, u32[]{:S(2)}) collective-permute-start(f32[1,2,4,2,8,512]{5,4,3,2,1,0:T(8,128)S(1)} %collective-permute-done.2.refs_3_), channel_id=1, source_target_pairs={{0,4},{1,5},{4,8},{5,9},{6,2},{7,3},{8,12},{9,13},{10,6},{11,7},{1... | collective-permute-start | bytes 786440 | tf_op jit(solution)/shard_map/ppermute | solution.py:482
  33.7 19.8 %collective-permute-start.10 = (f32[1,2,4,2,8,512]{5,4,3,2,1,0:T(8,128)S(1)}, f32[1,2,4,2,8,512]{5,4,3,2,1,0:T(8,128)S(1)}, u32[]{:S(2)}, u32[]{:S(2)}) collective-permute-start(f32[1,2,4,2,8,512]{5,4,3,2,1,0:T(8,128)S(1)} %collective-permute-done.8.refs_2_), channel_id=1, source_target_pairs={{0,4},{1,5},{4,8},{5,9},{6,2},{7,3},{8,12},{9,13},{10,6},{11,7},{1... | collective-permute-start | bytes 786440 | tf_op jit(solution)/shard_map/ppermute | solution.py:482
  37.7 15.7 %collective-permute-start.11 = (f32[1,2,4,2,8,512]{5,4,3,2,1,0:T(8,128)S(1)}, f32[1,2,4,2,8,512]{5,4,3,2,1,0:T(8,128)S(1)}, u32[]{:S(2)}, u32[]{:S(2)}) collective-permute-start(f32[1,2,4,2,8,512]{5,4,3,2,1,0:T(8,128)S(1)} %collective-permute-done.9.refs_3_), channel_id=1, source_target_pairs={{0,4},{1,5},{4,8},{5,9},{6,2},{7,3},{8,12},{9,13},{10,6},{11,7},{1... | collective-permute-start | bytes 786440 | tf_op jit(solution)/shard_map/ppermute | solution.py:482
  50.9 0.7 copy-start
  51.5 12.9 %collective-permute-start.5 = (f32[11,8,512]{2,1,0:T(8,128)S(1)}, f32[11,8,512]{2,1,0:T(8,128)S(1)}, u32[]{:S(2)}, u32[]{:S(2)}) collective-permute-start(f32[11,8,512]{2,1,0:T(8,128)S(1)} %get-tuple-element.29), channel_id=1, source_target_pairs={{0,1},{1,0},{2,3},{3,2},{4,5},{5,4},{6,7},{7,6},{8,9},{9,8},{10,11... | collective-permute-start | bytes 540680 | tf_op jit(solution)/shard_map/ppermute | solution.py:473
  52.1 13.8 %collective-permute-start.6 = (f32[11,8,512]{2,1,0:T(8,128)S(1)}, f32[11,8,512]{2,1,0:T(8,128)S(1)}, u32[]{:S(2)}, u32[]{:S(2)}) collective-permute-start(f32[11,8,512]{2,1,0:T(8,128)S(1)} %get-tuple-element.30), channel_id=1, source_target_pairs={{0,2},{1,3},{2,0},{3,1},{4,6},{5,7},{6,4},{7,5},{8,10},{9,11},{10,... | collective-permute-start | bytes 540680 | tf_op jit(solution)/shard_map/ppermute | solution.py:473
  52.1 14.2 %collective-permute-start.7 = (f32[11,8,512]{2,1,0:T(8,128)S(1)}, f32[11,8,512]{2,1,0:T(8,128)S(1)}, u32[]{:S(2)}, u32[]{:S(2)}) collective-permute-start(f32[11,8,512]{2,1,0:T(8,128)S(1)} %get-tuple-element.31), channel_id=1, source_target_pairs={{0,3},{1,2},{2,1},{3,0},{4,7},{5,6},{6,5},{7,4},{8,11},{9,10},{10,... | collective-permute-start | bytes 540680 | tf_op jit(solution)/shard_map/ppermute | solution.py:473
  62.5 1.7 %collective-permute-start.18 = (f32[2,8,512]{2,1,0:T(8,128)S(1)}, f32[2,8,512]{2,1,0:T(8,128)S(1)}, u32[]{:S(2)}, u32[]{:S(2)}) collective-permute-start(f32[2,8,512]{2,1,0:T(8,128)S(1)} %get-tuple-element.38.refs_8_), channel_id=1, source_target_pairs={{0,1},{1,0},{2,3},{3,2},{4,5},{5,4},{6,7},{7,6},{8,9},{9,8},{10,11... | collective-permute-start | bytes 98312 | tf_op jit(solution)/shard_map/ppermute | solution.py:473
  63.4 6.2 %collective-permute-start.12 = (f32[8,8,512]{2,1,0:T(8,128)S(1)}, f32[8,8,512]{2,1,0:T(8,128)S(1)}, u32[]{:S(2)}, u32[]{:S(2)}) collective-permute-start(f32[8,8,512]{2,1,0:T(8,128)S(1)} %get-tuple-element.35), channel_id=1, source_target_pairs={{0,1},{1,0},{2,3},{3,2},{4,5},{5,4},{6,7},{7,6},{8,9},{9,8},{10,11... | collective-permute-start | bytes 393224 | tf_op jit(solution)/shard_map/ppermute | solution.py:473
  64.2 8.1 %collective-permute-start.13 = (f32[8,8,512]{2,1,0:T(8,128)S(1)}, f32[8,8,512]{2,1,0:T(8,128)S(1)}, u32[]{:S(2)}, u32[]{:S(2)}) collective-permute-start(f32[8,8,512]{2,1,0:T(8,128)S(1)} %get-tuple-element.36), channel_id=1, source_target_pairs={{0,2},{1,3},{2,0},{3,1},{4,6},{5,7},{6,4},{7,5},{8,10},{9,11},{10,... | collective-permute-start | bytes 393224 | tf_op jit(solution)/shard_map/ppermute | solution.py:473
  64.5 3.3 %copy-start.2 = (f32[11,8,512]{2,1,0:T(8,128)}, f32[11,8,512]{2,1,0:T(8,128)S(1)}, u32[]{:S(2)}) copy-start(f32[11,8,512]{2,1,0:T(8,128)S(1)} %collective-permute-done.5.refs_1_.refs_5_) | copy-start | bytes 540676
  64.5 8.1 %collective-permute-start.14 = (f32[8,8,512]{2,1,0:T(8,128)S(1)}, f32[8,8,512]{2,1,0:T(8,128)S(1)}, u32[]{:S(2)}, u32[]{:S(2)}) collective-permute-start(f32[8,8,512]{2,1,0:T(8,128)S(1)} %get-tuple-element.37), channel_id=1, source_target_pairs={{0,3},{1,2},{2,1},{3,0},{4,7},{5,6},{6,5},{7,4},{8,11},{9,10},{10,... | collective-permute-start | bytes 393224 | tf_op jit(solution)/shard_map/ppermute | solution.py:473
  65.9 1.8 %copy-start.4 = (f32[11,8,512]{2,1,0:T(8,128)}, f32[11,8,512]{2,1,0:T(8,128)S(1)}, u32[]{:S(2)}) copy-start(f32[11,8,512]{2,1,0:T(8,128)S(1)} %collective-permute-done.6.refs_2_.refs_6_) | copy-start | bytes 540676
  65.9 11.7 %collective-permute-start.19 = (f32[2,8,512]{2,1,0:T(8,128)S(1)}, f32[2,8,512]{2,1,0:T(8,128)S(1)}, u32[]{:S(2)}, u32[]{:S(2)}) collective-permute-start(f32[2,8,512]{2,1,0:T(8,128)S(1)} %get-tuple-element.38.refs_8_), channel_id=1, source_target_pairs={{0,2},{1,3},{2,0},{3,1},{4,6},{5,7},{6,4},{7,5},{8,10},{9,11},{10,... | collective-permute-start | bytes 98312 | tf_op jit(solution)/shard_map/ppermute | solution.py:473
  66.4 1.4 %copy-start.6 = (f32[11,8,512]{2,1,0:T(8,128)}, f32[11,8,512]{2,1,0:T(8,128)S(1)}, u32[]{:S(2)}) copy-start(f32[11,8,512]{2,1,0:T(8,128)S(1)} %collective-permute-done.7.refs_3_.refs_7_) | copy-start | bytes 540676
  66.4 11.3 %collective-permute-start.20 = (f32[2,8,512]{2,1,0:T(8,128)S(1)}, f32[2,8,512]{2,1,0:T(8,128)S(1)}, u32[]{:S(2)}, u32[]{:S(2)}) collective-permute-start(f32[2,8,512]{2,1,0:T(8,128)S(1)} %get-tuple-element.38.refs_8_), channel_id=1, source_target_pairs={{0,3},{1,2},{2,1},{3,0},{4,7},{5,6},{6,5},{7,4},{8,11},{9,10},{10,... | collective-permute-start | bytes 98312 | tf_op jit(solution)/shard_map/ppermute | solution.py:473
  67.8 6.0 %copy-start.1 = (f32[11,8,512]{2,1,0:T(8,128)S(1)}, f32[11,8,512]{2,1,0:T(8,128)}, u32[]{:S(2)}) copy-start(f32[11,8,512]{2,1,0:T(8,128)} %copy-done) | copy-start | bytes 540676
  69.6 8.1 %collective-permute-start.15 = (f32[8,128]{1,0:T(8,128)}, f32[8,128]{1,0:T(8,128)S(1)}, u32[]{:S(2)}, u32[]{:S(2)}) collective-permute-start(f32[8,128]{1,0:T(8,128)} %team_sums.1.refs_0_), channel_id=1, source_target_pairs={{4,0},{5,1},{6,2},{7,3},{8,4},{9,5},{10,6},{11,7},{12,8},{13,9},{1... | collective-permute-start | bytes 12296 | tf_op jit(solution)/shard_map/ppermute | solution.py:491
  72.4 5.3 %collective-permute-start.16 = (f32[8,128]{1,0:T(8,128)}, f32[8,128]{1,0:T(8,128)S(1)}, u32[]{:S(2)}, u32[]{:S(2)}) collective-permute-start(f32[8,128]{1,0:T(8,128)} %team_sums.1.refs_0_), channel_id=1, source_target_pairs={{8,0},{9,1},{10,2},{11,3},{12,4},{13,5},{14,6},{15,7},{0,8},{1,9},... | collective-permute-start | bytes 12296 | tf_op jit(solution)/shard_map/ppermute | solution.py:491
  72.6 5.6 %collective-permute-start.17 = (f32[8,128]{1,0:T(8,128)}, f32[8,128]{1,0:T(8,128)S(1)}, u32[]{:S(2)}, u32[]{:S(2)}) collective-permute-start(f32[8,128]{1,0:T(8,128)} %team_sums.1.refs_0_), channel_id=1, source_target_pairs={{12,0},{13,1},{14,2},{15,3},{0,4},{1,5},{2,6},{3,7},{4,8},{5,9},{6... | collective-permute-start | bytes 12296 | tf_op jit(solution)/shard_map/ppermute | solution.py:491
  73.8 0.9 %copy-start.3 = (f32[11,8,512]{2,1,0:T(8,128)S(1)}, f32[11,8,512]{2,1,0:T(8,128)}, u32[]{:S(2)}) copy-start(f32[11,8,512]{2,1,0:T(8,128)} %copy-done.2) | copy-start | bytes 540676
  74.7 0.9 %copy-start.5 = (f32[11,8,512]{2,1,0:T(8,128)S(1)}, f32[11,8,512]{2,1,0:T(8,128)}, u32[]{:S(2)}) copy-start(f32[11,8,512]{2,1,0:T(8,128)} %copy-done.4) | copy-start | bytes 540676
  75.6 0.9 %copy-start.7 = (f32[11,8,512]{2,1,0:T(8,128)S(1)}, f32[11,8,512]{2,1,0:T(8,128)}, u32[]{:S(2)}) copy-start(f32[11,8,512]{2,1,0:T(8,128)} %copy-done.6) | copy-start | bytes 540676
  76.6 1.7 %copy-start.10 = (f32[8,128]{1,0:T(8,128)S(1)}, f32[8,128]{1,0:T(8,128)}, u32[]{:S(2)}) copy-start(f32[8,128]{1,0:T(8,128)} %team_sums.1.refs_0_) | copy-start | bytes 12292
  76.6 10.5 %copy-start.8 = (f32[512,512]{1,0:T(8,128)S(1)}, f32[512,512]{1,0:T(8,128)}, u32[]{:S(2)}) copy-start(f32[512,512]{1,0:T(8,128)} %constant.7.clone.refs_5_) | copy-start | bytes 3145732
  77.6 9.4 %copy-start.9 = (f32[16,32,64]{2,1,0:T(8,128)S(1)}, f32[16,32,64]{2,1,0:T(8,128)}, u32[]{:S(2)}) copy-start(f32[16,32,64]{2,1,0:T(8,128)} %constant.6.clone.refs_4_) | copy-start | bytes 393220
  78.3 4.0 %collective-permute-start.21 = (f32[1,16,512]{2,1,0:T(8,128)S(1)}, f32[1,16,512]{2,1,0:T(8,128)S(1)}, u32[]{:S(2)}, u32[]{:S(2)}) collective-permute-start(f32[1,16,512]{2,1,0:T(8,128)S(1)} %get-tuple-element.39.refs_0_), channel_id=1, source_target_pairs={{4,0},{5,1},{6,2},{7,3},{8,4},{9,5},{10,6},{11,7},{12,8},{13,9},{1... | collective-permute-start | bytes 98312 | tf_op jit(solution)/shard_map/ppermute | solution.py:491
  80.4 5.2 %collective-permute-start.22 = (f32[1,16,512]{2,1,0:T(8,128)S(1)}, f32[1,16,512]{2,1,0:T(8,128)S(1)}, u32[]{:S(2)}, u32[]{:S(2)}) collective-permute-start(f32[1,16,512]{2,1,0:T(8,128)S(1)} %get-tuple-element.39.refs_0_), channel_id=1, source_target_pairs={{8,0},{9,1},{10,2},{11,3},{12,4},{13,5},{14,6},{15,7},{0,8},{1,9},... | collective-permute-start | bytes 98312 | tf_op jit(solution)/shard_map/ppermute | solution.py:491
  81.3 5.7 %collective-permute-start.23 = (f32[1,16,512]{2,1,0:T(8,128)S(1)}, f32[1,16,512]{2,1,0:T(8,128)S(1)}, u32[]{:S(2)}, u32[]{:S(2)}) collective-permute-start(f32[1,16,512]{2,1,0:T(8,128)S(1)} %get-tuple-element.39.refs_0_), channel_id=1, source_target_pairs={{12,0},{13,1},{14,2},{15,3},{0,4},{1,5},{2,6},{3,7},{4,8},{5,9},{6... | collective-permute-start | bytes 98312 | tf_op jit(solution)/shard_map/ppermute | solution.py:491

commit v5 on v3

--- a/solution.py
+++ b/solution.py
@@ -53,19 +53,27 @@
     return lax.rem(lax.axis_index("gz"), TEAM)
 
 
-def prepare(jobs, fields, sums_before):
+def prepare(jobs, fields, sums=None):
     state, target, rock_type, log_table, obs_scale = fields
     samples, planes, rows_y, columns = state.shape
     slots = samples // TEAM
     block = (planes, rows_y, columns)
     half, tiles = rows_y // 2, columns // 128
+    size = 2 * 2 * planes
     depth_total = planes * lax.axis_size("gz")
     flat = [(o, i, job) for o, group in enumerate(jobs) for i, job in enumerate(group)]
     count = len(flat)
-
-    def kernel(before_ref, table_ref, scale_ref, state_ref, target_ref, rock_ref, *rest):
-        outs, sums_ref = rest[: len(jobs)], rest[len(jobs)]
-        table, scale, state_buf, rock_buf, target_buf, mixed, sems = rest[len(jobs) + 1 :]
+    shapes = [(len(group) * size + 1, half, columns) for group in jobs]
+    given = [] if sums is None else [sums]
+    states = count if given else samples
+
+    def kernel(*refs):
+        before, refs = refs[: len(given)], refs[len(given) :]
+        (table_ref, scale_ref, state_ref, target_ref, rock_ref), refs = refs[:5], refs[5:]
+        outs, refs = refs[: len(jobs)], refs[len(jobs) :]
+        if not given:
+            sums_ref, refs = refs[0], refs[1:]
+        table, scale, state_buf, rock_buf, target_buf, mixed, sems = refs
         place = team_place()
         first_plane = lax.axis_index("gz") * planes
         members = [slots * (place ^ m) + slot for _, _, (slot, m) in flat]
@@ -76,30 +84,48 @@
         ]
         for copy in small:
             copy.start()
-        copies = []
-        for n, member in enumerate(members):
-            pair = (
-                pltpu.make_async_copy(rock_ref.at[member], rock_buf.at[n], sems.at[1, n]),
-                pltpu.make_async_copy(state_ref.at[member], state_buf.at[n], sems.at[0, n]),
+        rocks = [
+            pltpu.make_async_copy(rock_ref.at[member], rock_buf.at[n], sems.at[1, n])
+            for n, member in enumerate(members)
+        ]
+        loads = [
+            pltpu.make_async_copy(
+                state_ref.at[members[n] if given else n], state_buf.at[n], sems.at[0, n]
             )
-            for copy in pair:
-                copy.start()
-            copies.append(pair)
-        sums_ref[...] = before_ref[...]
+            for n in range(states)
+        ]
+        for copy in rocks + loads:
+            copy.start()
+        depth_weights = [
+            1.0 + (2.0 / (depth_total - 1)) * (first_plane + p).astype(F32) for p in range(planes)
+        ]
         for copy in small:
             copy.wait()
+        if not given:
+            for copy in loads:
+                copy.wait()
+            for n in range(samples):
+                total = jnp.zeros((8, columns), F32)
+                for p in range(planes):
+                    part = jnp.zeros((8, columns), F32)
+                    for first in range(0, rows_y, 8):
+                        rows = slice(first, first + 8)
+                        gap = state_buf[n, p, rows] - target_buf[p, rows]
+                        part = part + gap * gap
+                    total = total + (scale[n] * depth_weights[p]) * part
+                summed = jnp.sum(total, keepdims=True)
+                sums_ref[n : n + 1, :] = jnp.broadcast_to(summed, (1, columns))
         for n, (o, i, _) in enumerate(flat):
-            for copy in copies[n]:
-                copy.wait()
+            rocks[n].wait()
+            if given:
+                loads[n].wait()
             member = members[n]
+            own_state = n if given else member
             values = [
                 jnp.exp(jnp.full((8, columns), table[member, code], F32)) for code in range(NR)
             ]
-            own_scale = scale[member]
-            total = jnp.zeros((8, columns), F32)
             for p in range(planes):
-                depth_weight = 1.0 + (2.0 / (depth_total - 1)) * (first_plane + p).astype(F32)
-                factor = own_scale * depth_weight
+                factor = scale[member] * depth_weights[p]
                 for first in range(0, rows_y, 8):
                     rows = slice(first, first + 8)
                     codes = rock_buf[n, p, rows]
@@ -108,44 +134,64 @@
                         jnp.where(low, values[2 * k + 1], values[2 * k]) for k in range(NR // 2)
                     ]
                     halves = [jnp.where(mid, pairs[2 * k + 1], pairs[2 * k]) for k in range(2)]
-                    gap = state_buf[n, p, rows] - target_buf[p, rows]
-                    source = factor * gap
-                    total = total + source * gap
-                    made = (jnp.where(high, halves[1], halves[0]), source)
+                    gap = state_buf[own_state, p, rows] - target_buf[p, rows]
+                    made = (jnp.where(high, halves[1], halves[0]), factor * gap)
                     for a in range(2):
                         for c in range(tiles):
                             mixed[n % 2, p, a, c, rows] = made[a][:, c * 128 : (c + 1) * 128]
                 for a in range(2):
                     for t in range(2):
                         for c in range(tiles):
-                            outs[o][i, a, p, t, :, c * 128 : (c + 1) * 128] = mixed[
+                            at = i * size + (a * planes + p) * 2 + t
+                            outs[o][at, :, c * 128 : (c + 1) * 128] = mixed[
                                 n % 2, p, a, c, pl.ds(t, half, stride=2), :
                             ]
-            summed = jnp.sum(total, keepdims=True)
-            sums_ref[pl.ds(member, 1), :] = jnp.broadcast_to(summed, (1, sums_ref.shape[1]))
+        for o, group in enumerate(jobs):
+            outs[o][len(group) * size] = before[0][...] if given else sums_ref[...]
 
     hbm = pl.BlockSpec(memory_space=pltpu.HBM)
     vmem = pl.BlockSpec(memory_space=pltpu.VMEM)
-    results = pl.pallas_call(
+    sums_shape = (samples, columns)
+    return pl.pallas_call(
         kernel,
-        out_shape=[jax.ShapeDtypeStruct((len(group), 2, planes, 2, half, columns), F32) for group in jobs]
-        + [jax.ShapeDtypeStruct((samples, LANES), F32)],
-        in_specs=[vmem] + [hbm] * 5,
-        out_specs=[vmem] * (len(jobs) + 1),
+        out_shape=[jax.ShapeDtypeStruct(shape, F32) for shape in shapes]
+        + ([] if given else [jax.ShapeDtypeStruct(sums_shape, F32)]),
+        in_specs=[vmem] * len(given) + [hbm] * 5,
+        out_specs=[vmem] * (len(shapes) + 1 - len(given)),
         scratch_shapes=[
             pltpu.SMEM(log_table.shape, F32),
             pltpu.SMEM(obs_scale.shape, F32),
-            pltpu.VMEM((count,) + block, F32),
+            pltpu.VMEM((states,) + block, F32),
             pltpu.VMEM((count,) + block, jnp.int32),
             pltpu.VMEM(block, F32),
             pltpu.VMEM((2, planes, 2, tiles, rows_y, 128), F32),
-            pltpu.SemaphoreType.DMA((3, max(count, 3))),
+            pltpu.SemaphoreType.DMA((3, max(states, 3))),
         ],
-        compiler_params=pltpu.CompilerParams(vmem_limit_bytes=16 * MIB),
+        compiler_params=pltpu.CompilerParams(vmem_limit_bytes=6 * MIB),
         cost_estimate=pl.CostEstimate(flops=0, bytes_accessed=count * MIB, transcendentals=0),
         name="prepare",
-    )(sums_before, log_table, obs_scale, state, target, rock_type)
-    return results[:-1], results[-1]
+    )(*given, log_table, obs_scale, state, target, rock_type)
+
+
+def merge(mine, theirs, slots, after):
+    size = (mine.shape[0] - 1) // slots
+
+    def kernel(mine_ref, theirs_ref, _, out_ref):
+        core = lax.rem(team_place(), 2)
+        for ref, at in ((mine_ref, core), (theirs_ref, 1 - core)):
+            for slot in range(slots):
+                for n in range(size):
+                    out_ref[at, slot, n] = ref[slot * size + n]
+
+    vmem = pl.BlockSpec(memory_space=pltpu.VMEM)
+    return pl.pallas_call(
+        kernel,
+        out_shape=jax.ShapeDtypeStruct((2, slots, size) + mine.shape[1:], F32),
+        in_specs=[vmem] * 2 + [pl.BlockSpec(memory_space=pl.ANY)],
+        out_specs=vmem,
+        compiler_params=pltpu.CompilerParams(vmem_limit_bytes=4 * MIB),
+        name="merge",
+    )(mine, theirs, after)
 
 
 def reciprocal(x):
@@ -170,49 +216,41 @@
         body(p)
 
 
-def risk(sums, cells):
-    misfit = sums * (1.0 / (2.0 * cells))
-    mean = jnp.mean(misfit, axis=0, keepdims=True)
-    deviation = misfit - mean
-    variance = jnp.mean(deviation * deviation, axis=0, keepdims=True)
-    return 1.0 + 2.0 * BETA_RISK * deviation, mean, variance
-
-
-def solve(slot, blocks, halos, sums=None, faces=()):
-    inputs = list(blocks) + list(halos)
-    weigh = sums is not None
-    extra = [sums, *faces] if weigh else []
-    slots = len(faces) + 1
-    planes, _, half, columns = blocks[0].shape[2:]
-    near = [0, 1, 4, 5]
+def solve(slot, near, far, near_halo, far_halo, sums, planes):
+    inputs = [near, near_halo, *far, *far_halo, *sums]
+    half, columns = far[0].shape[1:]
     halo = 2 * planes
     own = TEAM * planes
     span = own + 2 * halo
-    cells = planes * lax.axis_size("gz") * 2 * half * columns
     centre, coefficients = chebyshev_constants(DEGREE)
     assert halo >= STEPS
 
     def kernel(*refs):
-        ins, refs = refs[:8], refs[8:]
-        given, refs = refs[: len(extra)], refs[len(extra) :]
+        ins, refs = refs[:6], refs[6:]
+        sum_refs, refs = refs[: len(sums)], refs[len(sums) :]
         outs, face_ref, refs = refs[:TEAM], refs[TEAM], refs[TEAM + 1 :]
-        if weigh:
-            moments_ref, weights, refs = refs[0], refs[-1], refs[1:-1]
+        if sums:
+            summed_ref, refs = refs[0], refs[1:]
+            summed = sum_refs[0][sums[0].shape[0] - 1]
+            for n, ref in enumerate(sum_refs[1:], 1):
+                summed = summed + ref[sums[n].shape[0] - 1]
+            summed_ref[...] = summed
         cond, u_a, u_b, s_a, s_b, zp, zm, yp, ym, xp, xm, t_a, t_b = refs
         place = team_place()
         column, side = lax.rem(place, 2), place // 2
         upper, lower = halo + own, 0
         near_base = jnp.where(side == 0, upper, lower)
         far_base = jnp.where(side == 0, lower, upper)
-        bases = [halo + planes * (place ^ m) for m in range(TEAM)]
-        bases += [near_base + planes * column, near_base + planes * (1 - column)]
-        bases += [far_base + planes * column, far_base + planes * (1 - column)]
-        for n, base in enumerate(bases):
-            item = slot if n in near else 0
+        blocks = [(ins[0].at[core, slot], halo + planes * (2 * side + core)) for core in range(2)]
+        blocks += [(ins[1].at[core, slot], near_base + planes * core) for core in range(2)]
+        blocks += [(ins[m], halo + planes * (place ^ m)) for m in (2, 3)]
+        blocks += [(ins[4], far_base + planes * column)]
+        blocks += [(ins[5], far_base + planes * (1 - column))]
+        for block, base in blocks:
             for j in range(planes):
                 for t in range(2):
-                    cond[base + j, t] = jnp.maximum(ins[n][item, 0, j, t], 1e-30)
-                    t_a[base + j, t] = ins[n][item, 1, j, t]
+                    cond[base + j, t] = jnp.maximum(block[2 * j + t], 1e-30)
+                    t_a[base + j, t] = block[2 * (planes + j) + t]
 
         last_row = lax.broadcasted_iota(jnp.int32, (half, columns), 0) == half - 1
         last_column = lax.broadcasted_iota(jnp.int32, (half, columns), 1) == columns - 1
@@ -291,39 +329,68 @@
             base = halo + planes * (place ^ m)
             for j in range(planes):
                 for t in range(2):
-                    outs[m][j, t] = t_now[base + j, t]
-        face = jnp.concatenate([t_now[halo + p, 0, 0:1, :] for p in range(own)], axis=0)
-        if weigh:
-            weights[...], mean, variance = risk(given[0][...], cells)
-            lane = lax.broadcasted_iota(jnp.int32, (1, LANES), 1)
-            moments_ref[...] = jnp.where(lane == 0, mean, variance)
-            total = jnp.zeros((own, columns), F32)
-            for n, values in enumerate([ref[...] for ref in given[1:]] + [face]):
-                row = weights[pl.ds(slots * place + n, 1), :]
-                total = total + values * jnp.concatenate([row] * (columns // LANES), axis=1)
-            face_ref[...] = total
-        else:
-            face_ref[...] = face
+                    outs[m][2 * j + t] = t_now[base + j, t]
+        for p in range(own):
+            face_ref[p : p + 1, :] = t_now[halo + p, 0, 0:1, :]
 
     vmem = pl.BlockSpec(memory_space=pltpu.VMEM)
     field = pltpu.VMEM((span, 2, half, columns), F32)
     return pl.pallas_call(
         kernel,
-        out_shape=[jax.ShapeDtypeStruct((planes, 2, half, columns), F32)] * TEAM
+        out_shape=[jax.ShapeDtypeStruct((2 * planes, half, columns), F32)] * TEAM
         + [jax.ShapeDtypeStruct((own, columns), F32)]
-        + [jax.ShapeDtypeStruct((1, LANES), F32)] * weigh,
-        in_specs=[vmem] * (8 + len(extra)),
-        out_specs=[vmem] * (TEAM + 1 + weigh),
-        scratch_shapes=[field] * 13 + ([pltpu.VMEM(sums.shape, F32)] if weigh else []),
-        compiler_params=pltpu.CompilerParams(vmem_limit_bytes=32 * MIB),
+        + [jax.ShapeDtypeStruct(sums[0].shape[1:], F32) for _ in sums[:1]],
+        in_specs=[vmem] * len(inputs),
+        out_specs=[vmem] * (TEAM + 1 + len(sums[:1])),
+        scratch_shapes=[field] * 13,
+        compiler_params=pltpu.CompilerParams(vmem_limit_bytes=16 * MIB),
         cost_estimate=pl.CostEstimate(flops=0, bytes_accessed=22 * MIB, transcendentals=0),
         name=f"solve{slot}",
-    )(*inputs, *extra)
-
-
-def gather_adjoint(pieces):
+    )(*inputs)
+
+
+def weigh(sums, faces, cells, after):
+    slots = len(faces)
+    samples, columns = sums[0].shape
+
+    def kernel(*refs):
+        sum_refs, refs = refs[: len(sums)], refs[len(sums) :]
+        face_refs, (out_ref, moments_ref, weights) = refs[:slots], refs[slots + len(after) :]
+        place = team_place()
+        summed = sum_refs[0][...]
+        for ref in sum_refs[1:]:
+            summed = summed + ref[...]
+        misfit = summed * (1.0 / (2.0 * cells))
+        mean = jnp.sum(misfit, axis=0, keepdims=True) * (1.0 / samples)
+        deviation = misfit - mean
+        variance = jnp.sum(deviation * deviation, axis=0, keepdims=True) * (1.0 / samples)
+        lane = lax.broadcasted_iota(jnp.int32, (1, columns), 1)
+        moments_ref[...] = jnp.where(lane == 0, mean, variance)
+        weights[...] = 1.0 + 2.0 * BETA_RISK * deviation
+        total = weights[pl.ds(slots * place, 1), :] * face_refs[0][...]
+        for n in range(1, slots):
+            total = total + weights[pl.ds(slots * place + n, 1), :] * face_refs[n][...]
+        out_ref[...] = total
+
+    vmem = pl.BlockSpec(memory_space=pltpu.VMEM)
+    return pl.pallas_call(
+        kernel,
+        out_shape=[
+            jax.ShapeDtypeStruct(faces[0].shape, F32),
+            jax.ShapeDtypeStruct((1, columns), F32),
+        ],
+        in_specs=[vmem] * (len(sums) + slots)
+        + [pl.BlockSpec(memory_space=pl.ANY)] * len(after),
+        out_specs=[vmem, vmem],
+        scratch_shapes=[pltpu.VMEM((samples, columns), F32)],
+        compiler_params=pltpu.CompilerParams(vmem_limit_bytes=2 * MIB),
+        name="weigh",
+    )(*sums, *faces, *after)
+
+
+def gather_adjoint(pieces, planes):
     slots = len(pieces)
-    planes, _, half, columns = pieces[0][0].shape
+    _, half, columns = pieces[0][0].shape
     tiles = columns // 128
     block = (planes, 2 * half, columns)
 
@@ -338,7 +405,7 @@
                     for t in range(2):
                         for c in range(tiles):
                             mixed[i % 2, j, c, pl.ds(t, half, stride=2), :] = blocks[i][
-                                j, t, :, c * 128 : (c + 1) * 128
+                                2 * j + t, :, c * 128 : (c + 1) * 128
                             ]
                     for c in range(tiles):
                         held[i, j, :, c * 128 : (c + 1) * 128] = mixed[i % 2, j, c]
@@ -360,7 +427,7 @@
             pltpu.VMEM((2, planes, tiles, 2 * half, 128), F32),
             pltpu.SemaphoreType.DMA((slots * TEAM,)),
         ],
-        compiler_params=pltpu.CompilerParams(vmem_limit_bytes=16 * MIB),
+        compiler_params=pltpu.CompilerParams(vmem_limit_bytes=4 * MIB),
         cost_estimate=pl.CostEstimate(flops=0, bytes_accessed=4 * MIB, transcendentals=0),
         name="gather_adjoint",
     )(*[piece for group in pieces for piece in group])
@@ -399,7 +466,7 @@
         in_specs=[vmem] * (len(faces) + 2),
         out_specs=vmem,
         scratch_shapes=[pltpu.VMEM((teams, own, columns), F32)],
-        compiler_params=pltpu.CompilerParams(vmem_limit_bytes=16 * MIB),
+        compiler_params=pltpu.CompilerParams(vmem_limit_bytes=8 * MIB),
         name="control",
     )(*faces, basis_z, basis_x)
 
@@ -442,46 +509,44 @@
             heard.append(lax.ppermute(value, "gz", pairs))
         return heard
 
-    def team_sum(value):
-        return sum((swap(value, m) for m in (2, 3, 1)), value)
-
     fields = [
         pltpu.with_memory_space_constraint(field, pltpu.HBM)
         for field in (state, target, rock_type, log_table, obs_scale)
     ]
-    sums = jnp.zeros((samples, LANES), F32)
+    jobs = [[(slot, m) for slot in range(slots)] for m in range(2)]
+    mine, theirs, sums = prepare(jobs, fields)
+    theirs = swap(theirs, 1)
     far = []
     for slot in range(slots):
-        blocks, sums = prepare([[(slot, 2)], [(slot, 3)]], fields, sums)
+        blocks = prepare([[(slot, 2)], [(slot, 3)]], fields, sums)
         far.append([swap(blocks[0], 2), swap(blocks[1], 3)])
-    blocks, sums = prepare([[(slot, m) for slot in range(slots)] for m in range(2)], fields, sums)
-    near = [blocks[0], swap(blocks[1], 1)]
-    near_halo = [along(block, True) for block in near]
-
-    sums = team_sum(sums)
-    stride = 1
-    for radix in radices:
-        sums = sum(from_teams(sums, stride, radix), sums)
-        stride *= radix
+        if slot == 0:
+            near = merge(mine, theirs, slots, blocks[0])
+    near_halo = along(near, True)
 
     pieces, faces = [], []
     for slot in range(slots):
-        last = slot == slots - 1
         far_halo = [along(block, False) for block in far[slot]]
-        solved = solve(
-            slot, near + far[slot], near_halo + far_halo, *((sums, faces) if last else ())
-        )
+        known = [mine, theirs, *far[0]] if slot == 0 else []
+        solved = solve(slot, near, far[slot], near_halo, far_halo, known, planes)
         pieces.append([solved[0]] + [swap(solved[m], m) for m in (1, 2, 3)])
         faces.append(solved[TEAM])
-    moments = solved[TEAM + 1]
-
-    heard = [team_sum(faces[-1])[None]]
+        if slot == 0:
+            sums = [solved[TEAM + 1]]
+            stride = 1
+            for radix in radices:
+                held = sum(sums[1:], sums[0])
+                sums = [held] + from_teams(held, stride, radix)
+                stride *= radix
+
+    face, moments = weigh(sums, faces, depth_total * rows_y * columns, pieces[0][1:])
+    heard = [sum((swap(face, m) for m in (2, 3, 1)), face)[None]]
     stride = 1
     for radix in radices:
         held = heard[0] if len(heard) == 1 else jnp.concatenate(heard)
         heard = [held] + from_teams(held, stride, radix)
         stride *= radix
-    adjoint = gather_adjoint(pieces)
+    adjoint = gather_adjoint(pieces, planes)
     own_count = MA // slabs
     gradient = control(
         heard,

time: 94 us -> 80.4 us (0.86)
  waiting for transfers between devices: 32.9 us -> 15.4 us
  starting transfers between devices: 33.7 us -> 37.6 us
    ppermute x6, waiting for transfers between devices: 13.2 us -> 3.3 us  [from_teams(): heard.append(lax.ppermute(value, 'gz', pairs))]
    ppermute x17 -> x14, waiting for transfers between devices: 19.2 us -> 12.1 us  [swap(): return lax.ppermute(value, 'gz', [(i, i ^ m) for i in range(slabs)])]
    ppermute x6, starting transfers between devices: 6.18 us -> 10.4 us  [from_teams(): heard.append(lax.ppermute(value, 'gz', pairs))]
    ppermute x17 -> x14, starting transfers between devices: 13.6 us -> 12.3 us  [swap(): return lax.ppermute(value, 'gz', [(i, i ^ m) for i in range(slabs)])]
    ppermute x6 -> x5, starting transfers between devices: 13.9 us -> 15 us  [along(): return lax.ppermute(value, 'gz', pairs)]
    pallas_call x5 -> x7, Pallas kernels: 23.2 us -> 23.2 us  [the longest x2 18.1 us: solve(): pl.pallas_call(kernel, out_shape=[jax.ShapeDtypeStruct((2 * planes, half,...]
  transfers between devices with their start and end apart: 29 -> 25, of which waited for: 15 -> 9; matrix products, arithmetic and copies ran while one was open for 1% -> 1% of each run, Pallas kernels for 11% -> 27%
where the time goes in v5:
time: 80.4 us; the launch traced here: 80.1 us
  starting transfers between devices  37.6 us (47%)
  Pallas kernels  25.7 us (32%)
  waiting for transfers between devices  15.4 us (19%)
  between operations  0.84 us (1%)
    pallas_call x2, Pallas kernels, solve(): pl.pallas_call(kernel, out_shape=[jax.ShapeDtypeStruct((2 * planes, half,...  18.1 us
    ppermute x5, starting transfers between devices, along(): return lax.ppermute(value, 'gz', pairs)  15 us
    ppermute x14, starting transfers between devices, swap(): return lax.ppermute(value, 'gz', [(i, i ^ m) for i in range(slabs)])  12.3 us
    ppermute x14, waiting for transfers between devices, swap(): return lax.ppermute(value, 'gz', [(i, i ^ m) for i in range(slabs)])  12.1 us
    ppermute x6, starting transfers between devices, from_teams(): heard.append(lax.ppermute(value, 'gz', pairs))  10.4 us
    pallas_call x3, Pallas kernels, prepare(): pl.pallas_call(kernel, out_shape=[jax.ShapeDtypeStruct(shape, F32) for sh...  4.99 us
    ppermute x6, waiting for transfers between devices, from_teams(): heard.append(lax.ppermute(value, 'gz', pairs))  3.3 us
  transfers between devices with their start and end apart: 25, of which 9 were waited for; matrix products, arithmetic and copies ran while one was open for 1% of the time, Pallas kernels for 27%

profile of v5, /device:TPU:0, one launch (start us, length us, event | category | flops | bytes accessed | tf_op | source)
XLA Modules:
  0.0 80.1 jit_solution(13405674283649021676)
XLA Ops:
  0.6 2.3 %prepare.3 = (f32[33,8,512]{2,1,0:T(8,128)S(1)}, f32[33,8,512]{2,1,0:T(8,128)S(1)}, f32[8,512]{1,0:T(8,128)S(1)}) custom-call(f32[8,8]{1,0:T(8,128)} %refs_1_.5, f32[8]{0:T(128)} %refs_2_.5, f32[8,4,16,512]{3,2,1,0:T(8,128)} %refs_3_.5, f32[4,16,512]{2,1,0:T(8,128)} %refs_4_.6, s32[8,4,16,512]{3,2,1,0:T(8,128)} %refs_5_.4), custom_call_target="tpu_custom_call" | custom-call | bytes 4194304 | tf_op jit(solution)/shard_map/prepare/pallas_call | solution.py:155
  2.9 0.5 collective-permute-start
  3.5 1.3 %prepare.4 = (f32[17,8,512]{2,1,0:T(8,128)S(1)}, f32[17,8,512]{2,1,0:T(8,128)S(1)}) custom-call(f32[8,512]{1,0:T(8,128)S(1)} %get-tuple-element.25.refs_0_, f32[8,8]{1,0:T(8,128)} %refs_1_.5, f32[8]{0:T(128)} %refs_2_.5, f32[8,4,16,512]{3,2,1,0:T(8,128)} %refs_3_.5, f32[4,16,512]{2,1,0:T(8,128)} %refs_4_.6, s32[8,4,16,512]{3,2,1,0:T(8,128)} %refs_5_.4), custom_call_target="tpu_custom_call" | custom-call | bytes 2097152 | tf_op jit(solution)/shard_map/prepare/pallas_call | solution.py:155
  4.8 0.2 collective-permute-done.theirs_ref.refs_7_
  5.0 0.1 merge.1.refs_0_
  5.1 1.3 %collective-permute-start.1 = (f32[2,2,16,8,512]{4,3,2,1,0:T(8,128)S(1)}, f32[2,2,16,8,512]{4,3,2,1,0:T(8,128)S(1)}, u32[]{:S(2)}, u32[]{:S(2)}) collective-permute-start(f32[2,2,16,8,512]{4,3,2,1,0:T(8,128)S(1)} %merge.1.refs_0_), channel_id=1, source_target_pairs={{2,6},{3,7},{4,0},{5,1},{6,10},{7,11},{8,4},{9,5},{10,14},{11,15},... | collective-permute-start | bytes 3145736 | tf_op jit(solution)/shard_map/ppermute | solution.py:500
  6.4 5.2 %collective-permute-start.2 = (f32[17,8,512]{2,1,0:T(8,128)S(1)}, f32[17,8,512]{2,1,0:T(8,128)S(1)}, u32[]{:S(2)}, u32[]{:S(2)}) collective-permute-start(f32[17,8,512]{2,1,0:T(8,128)S(1)} %get-tuple-element.26._), channel_id=1, source_target_pairs={{0,2},{1,3},{2,0},{3,1},{4,6},{5,7},{6,4},{7,5},{8,10},{9,11},{10,... | collective-permute-start | bytes 835592 | tf_op jit(solution)/shard_map/ppermute | solution.py:491
  11.6 1.3 %prepare.5 = (f32[17,8,512]{2,1,0:T(8,128)S(1)}, f32[17,8,512]{2,1,0:T(8,128)S(1)}) custom-call(f32[8,512]{1,0:T(8,128)S(1)} %get-tuple-element.25.refs_0_, f32[8,8]{1,0:T(8,128)} %refs_1_.5, f32[8]{0:T(128)} %refs_2_.5, f32[8,4,16,512]{3,2,1,0:T(8,128)} %refs_3_.5, f32[4,16,512]{2,1,0:T(8,128)} %refs_4_.6, s32[8,4,16,512]{3,2,1,0:T(8,128)} %refs_5_.4), custom_call_target="tpu_custom_call" | custom-call | bytes 2097152 | tf_op jit(solution)/shard_map/prepare/pallas_call | solution.py:155
  12.9 1.3 %collective-permute-start.9 = (f32[17,8,512]{2,1,0:T(8,128)S(1)}, f32[17,8,512]{2,1,0:T(8,128)S(1)}, u32[]{:S(2)}, u32[]{:S(2)}) collective-permute-start(f32[17,8,512]{2,1,0:T(8,128)S(1)} %get-tuple-element.32), channel_id=1, source_target_pairs={{0,2},{1,3},{2,0},{3,1},{4,6},{5,7},{6,4},{7,5},{8,10},{9,11},{10,... | collective-permute-start | bytes 835592 | tf_op jit(solution)/shard_map/ppermute | solution.py:491
  14.2 0.6 collective-permute-start.10
  14.8 4.2 %collective-permute-done.2.refs_2_.refs_8_ = f32[17,8,512]{2,1,0:T(8,128)S(1)} collective-permute-done((f32[17,8,512]{2,1,0:T(8,128)S(1)}, f32[17,8,512]{2,1,0:T(8,128)S(1)}, u32[]{:S(2)}, u32[]{:S(2)}) %collective-permute-start.2) | collective-permute-done | bytes 278560 | tf_op jit(solution)/shard_map/ppermute | solution.py:491
  19.1 3.4 %collective-permute-start.4 = (f32[17,8,512]{2,1,0:T(8,128)S(1)}, f32[17,8,512]{2,1,0:T(8,128)S(1)}, u32[]{:S(2)}, u32[]{:S(2)}) collective-permute-start(f32[17,8,512]{2,1,0:T(8,128)S(1)} %collective-permute-done.2.refs_2_.refs_8_), channel_id=1, source_target_pairs={{0,4},{1,5},{4,8},{5,9},{6,2},{7,3},{8,12},{9,13},{10,6},{11,7},{1... | collective-permute-start | bytes 835592 | tf_op jit(solution)/shard_map/ppermute | solution.py:500
  22.5 2.1 %collective-permute-done.3.refs_3_.refs_9_ = f32[17,8,512]{2,1,0:T(8,128)S(1)} collective-permute-done((f32[17,8,512]{2,1,0:T(8,128)S(1)}, f32[17,8,512]{2,1,0:T(8,128)S(1)}, u32[]{:S(2)}, u32[]{:S(2)}) %collective-permute-start.3) | collective-permute-done | bytes 278560 | tf_op jit(solution)/shard_map/ppermute | solution.py:491
  24.6 3.4 %collective-permute-start.5 = (f32[17,8,512]{2,1,0:T(8,128)S(1)}, f32[17,8,512]{2,1,0:T(8,128)S(1)}, u32[]{:S(2)}, u32[]{:S(2)}) collective-permute-start(f32[17,8,512]{2,1,0:T(8,128)S(1)} %collective-permute-done.3.refs_3_.refs_9_), channel_id=1, source_target_pairs={{0,4},{1,5},{4,8},{5,9},{6,2},{7,3},{8,12},{9,13},{10,6},{11,7},{1... | collective-permute-start | bytes 835592 | tf_op jit(solution)/shard_map/ppermute | solution.py:500
  28.0 3.0 %collective-permute-done.9.refs_2_ = f32[17,8,512]{2,1,0:T(8,128)S(1)} collective-permute-done((f32[17,8,512]{2,1,0:T(8,128)S(1)}, f32[17,8,512]{2,1,0:T(8,128)S(1)}, u32[]{:S(2)}, u32[]{:S(2)}) %collective-permute-start.9) | collective-permute-done | bytes 278560 | tf_op jit(solution)/shard_map/ppermute | solution.py:491
  31.0 3.4 %collective-permute-start.11 = (f32[17,8,512]{2,1,0:T(8,128)S(1)}, f32[17,8,512]{2,1,0:T(8,128)S(1)}, u32[]{:S(2)}, u32[]{:S(2)}) collective-permute-start(f32[17,8,512]{2,1,0:T(8,128)S(1)} %collective-permute-done.9.refs_2_), channel_id=1, source_target_pairs={{0,4},{1,5},{4,8},{5,9},{6,2},{7,3},{8,12},{9,13},{10,6},{11,7},{1... | collective-permute-start | bytes 835592 | tf_op jit(solution)/shard_map/ppermute | solution.py:500
  34.4 1.0 %collective-permute-done.10.refs_3_ = f32[17,8,512]{2,1,0:T(8,128)S(1)} collective-permute-done((f32[17,8,512]{2,1,0:T(8,128)S(1)}, f32[17,8,512]{2,1,0:T(8,128)S(1)}, u32[]{:S(2)}, u32[]{:S(2)}) %collective-permute-start.10) | collective-permute-done | bytes 278560 | tf_op jit(solution)/shard_map/ppermute | solution.py:491
  35.4 3.4 %collective-permute-start.12 = (f32[17,8,512]{2,1,0:T(8,128)S(1)}, f32[17,8,512]{2,1,0:T(8,128)S(1)}, u32[]{:S(2)}, u32[]{:S(2)}) collective-permute-start(f32[17,8,512]{2,1,0:T(8,128)S(1)} %collective-permute-done.10.refs_3_), channel_id=1, source_target_pairs={{0,4},{1,5},{4,8},{5,9},{6,2},{7,3},{8,12},{9,13},{10,6},{11,7},{1... | collective-permute-start | bytes 835592 | tf_op jit(solution)/shard_map/ppermute | solution.py:500
  38.9 0.0 collective-permute-done.1.refs_1_
  38.9 9.0 %solve0.1 = (f32[8,8,512]{2,1,0:T(8,128)S(1)}, f32[8,8,512]{2,1,0:T(8,128)S(1)}, f32[8,8,512]{2,1,0:T(8,128)S(1)}, f32[8,8,512]{2,1,0:T(8,128)S(1)}, f32[16,512]{1,0:T(8,128)S(1)}, /*index=5*/f32[8,512]{1,0:T(8,128)S(1)}) custom-call(f32[2,2,16,8,512]{4,3,2,1,0:T(8,128)S(1)} %merge.1.refs_0_, f32[2,2,16,8,512]{4,3,2,1,0:T(8,128)S(1)} %collective-permute-done.1.refs_1_, ...), custom_call_target="tpu_custom_call" | custom-call | bytes 23068672 | tf_op jit(solution)/shard_map/solve0/pallas_call | solution.py:338
  47.9 0.4 collective-permute-start.6
  48.4 0.0 collective-permute-start.7
  48.4 1.5 %collective-permute-start.8 = (f32[8,8,512]{2,1,0:T(8,128)S(1)}, f32[8,8,512]{2,1,0:T(8,128)S(1)}, u32[]{:S(2)}, u32[]{:S(2)}) collective-permute-start(f32[8,8,512]{2,1,0:T(8,128)S(1)} %get-tuple-element.31), channel_id=1, source_target_pairs={{0,3},{1,2},{2,1},{3,0},{4,7},{5,6},{6,5},{7,4},{8,11},{9,10},{10,... | collective-permute-start | bytes 393224 | tf_op jit(solution)/shard_map/ppermute | solution.py:491
  49.9 0.0 collective-permute-done.11.refs_4_
  49.9 2.6 %collective-permute-start.16 = (f32[8,512]{1,0:T(8,128)S(1)}, f32[8,512]{1,0:T(8,128)S(1)}, u32[]{:S(2)}, u32[]{:S(2)}) collective-permute-start(f32[8,512]{1,0:T(8,128)S(1)} %get-tuple-element.38.refs_0_), channel_id=1, source_target_pairs={{4,0},{5,1},{6,2},{7,3},{8,4},{9,5},{10,6},{11,7},{12,8},{13,9},{1... | collective-permute-start | bytes 49160 | tf_op jit(solution)/shard_map/ppermute | solution.py:509
  52.5 0.0 collective-permute-done.12.refs_5_
  52.5 0.4 collective-permute-start.17
  52.9 1.1 %collective-permute-done.16.refs_1_ = f32[8,512]{1,0:T(8,128)S(1)} collective-permute-done((f32[8,512]{1,0:T(8,128)S(1)}, f32[8,512]{1,0:T(8,128)S(1)}, u32[]{:S(2)}, u32[]{:S(2)}) %collective-permute-start.16) | collective-permute-done | bytes 16416 | tf_op jit(solution)/shard_map/ppermute | solution.py:509
  54.0 1.2 %collective-permute-start.18 = (f32[8,512]{1,0:T(8,128)S(1)}, f32[8,512]{1,0:T(8,128)S(1)}, u32[]{:S(2)}, u32[]{:S(2)}) collective-permute-start(f32[8,512]{1,0:T(8,128)S(1)} %get-tuple-element.38.refs_0_), channel_id=1, source_target_pairs={{12,0},{13,1},{14,2},{15,3},{0,4},{1,5},{2,6},{3,7},{4,8},{5,9},{6... | collective-permute-start | bytes 49160 | tf_op jit(solution)/shard_map/ppermute | solution.py:509
  55.2 9.0 %solve1.1 = (f32[8,8,512]{2,1,0:T(8,128)S(1)}, f32[8,8,512]{2,1,0:T(8,128)S(1)}, f32[8,8,512]{2,1,0:T(8,128)S(1)}, f32[8,8,512]{2,1,0:T(8,128)S(1)}, f32[16,512]{1,0:T(8,128)S(1)}) custom-call(f32[2,2,16,8,512]{4,3,2,1,0:T(8,128)S(1)} %merge.1.refs_0_, f32[2,2,16,8,512]{4,3,2,1,0:T(8,128)S(1)} %collective-permute-done.1.refs_1_, ...), custom_call_target="tpu_custom_call" | custom-call | bytes 23068672 | tf_op jit(solution)/shard_map/solve1/pallas_call | solution.py:338
  64.2 0.0 collective-permute-done.17.refs_2_
  64.2 0.0 collective-permute-done.6.refs_1_.refs_6_
  64.3 0.0 collective-permute-done.7.refs_2_.refs_7_
  64.3 0.6 collective-permute-start.19
  64.9 0.3 collective-permute-start.20
  65.2 1.3 %collective-permute-start.21 = (f32[16,512]{1,0:T(8,128)S(1)}, f32[16,512]{1,0:T(8,128)S(1)}, u32[]{:S(2)}, u32[]{:S(2)}) collective-permute-start(f32[16,512]{1,0:T(8,128)S(1)} %get-tuple-element.41), channel_id=1, source_target_pairs={{0,1},{1,0},{2,3},{3,2},{4,5},{5,4},{6,7},{7,6},{8,9},{9,8},{10,11... | collective-permute-start | bytes 98312 | tf_op jit(solution)/shard_map/ppermute | solution.py:491
  66.5 0.0 collective-permute-start.13
  66.5 0.6 collective-permute-start.14
  67.1 1.5 %collective-permute-done.19 = f32[16,512]{1,0:T(8,128)S(1)} collective-permute-done((f32[16,512]{1,0:T(8,128)S(1)}, f32[16,512]{1,0:T(8,128)S(1)}, u32[]{:S(2)}, u32[]{:S(2)}) %collective-permute-start.19) | collective-permute-done | bytes 32800 | tf_op jit(solution)/shard_map/ppermute | solution.py:491
  68.7 3.5 %collective-permute-start.22 = (f32[1,16,512]{2,1,0:T(8,128)S(1)}, f32[1,16,512]{2,1,0:T(8,128)S(1)}, u32[]{:S(2)}, u32[]{:S(2)}) collective-permute-start(f32[1,16,512]{2,1,0:T(8,128)S(1)} %add_bitcast_fusion.refs_0_), channel_id=1, source_target_pairs={{4,0},{5,1},{6,2},{7,3},{8,4},{9,5},{10,6},{11,7},{12,8},{13,9},{1... | collective-permute-start | bytes 98312 | tf_op jit(solution)/shard_map/ppermute | solution.py:509
  72.2 0.6 collective-permute-start.23
  72.8 1.9 %collective-permute-start.24 = (f32[1,16,512]{2,1,0:T(8,128)S(1)}, f32[1,16,512]{2,1,0:T(8,128)S(1)}, u32[]{:S(2)}, u32[]{:S(2)}) collective-permute-start(f32[1,16,512]{2,1,0:T(8,128)S(1)} %add_bitcast_fusion.refs_0_), channel_id=1, source_target_pairs={{12,0},{13,1},{14,2},{15,3},{0,4},{1,5},{2,6},{3,7},{4,8},{5,9},{6... | collective-permute-start | bytes 98312 | tf_op jit(solution)/shard_map/ppermute | solution.py:509
  74.8 0.5 slice_bitcast_fusion
  75.3 0.0 copy-start.1
  75.3 1.1 %gather_adjoint.1 = f32[8,4,16,512]{3,2,1,0:T(8,128)} custom-call(f32[8,8,512]{2,1,0:T(8,128)S(1)} %get-tuple-element.28.refs_0_, f32[8,8,512]{2,1,0:T(8,128)S(1)} %collective-permute-done.6.refs_1_.refs_6_, f32[8,8,512]{2,1,0:T(8,128)S(1)} %collective-permute-done.7.refs_2_.refs_7_, f32[8,8,512]{2,1,0:T(8,128)S(1)} %collective-permute-done.8.refs_3_.refs_8_, ...), custom_call_target="tpu_custom_call" | custom-call | bytes 4194304 | tf_op jit(solution)/shard_map/gather_adjoint/pallas_call | solution.py:420
  76.4 1.4 %collective-permute-done.23.refs_2_ = f32[1,16,512]{2,1,0:T(8,128)S(1)} collective-permute-done((f32[1,16,512]{2,1,0:T(8,128)S(1)}, f32[1,16,512]{2,1,0:T(8,128)S(1)}, u32[]{:S(2)}, u32[]{:S(2)}) %collective-permute-start.23) | collective-permute-done | bytes 32800 | tf_op jit(solution)/shard_map/ppermute | solution.py:509
  77.8 0.8 %collective-permute-done.24.refs_3_ = f32[1,16,512]{2,1,0:T(8,128)S(1)} collective-permute-done((f32[1,16,512]{2,1,0:T(8,128)S(1)}, f32[1,16,512]{2,1,0:T(8,128)S(1)}, u32[]{:S(2)}, u32[]{:S(2)}) %collective-permute-start.24) | collective-permute-done | bytes 32800 | tf_op jit(solution)/shard_map/ppermute | solution.py:509
  78.6 1.4 %control.1 = f32[32,512]{1,0:T(8,128)} custom-call(f32[1,16,512]{2,1,0:T(8,128)S(1)} %add_bitcast_fusion.refs_0_, f32[1,16,512]{2,1,0:T(8,128)S(1)} %collective-permute-done.22.refs_1_, f32[1,16,512]{2,1,0:T(8,128)S(1)} %collective-permute-done.23.refs_2_, f32[1,16,512]{2,1,0:T(8,128)S(1)} %collective-permute-done.24.refs_3_, f32[16,32,64]{2,1,0:T(8,128)S(1)} %copy-done.1, ...), custom_call_target="tpu_custom_call" | custom-call | tf_op jit(solution)/shard_map/control/pallas_call | solution.py:463
  (17 shorter events, 0.1 us)
Async XLA Ops:
  2.9 2.1 %collective-permute-start = (f32[33,8,512]{2,1,0:T(8,128)S(1)}, f32[33,8,512]{2,1,0:T(8,128)S(1)}, u32[]{:S(2)}, u32[]{:S(2)}) collective-permute-start(f32[33,8,512]{2,1,0:T(8,128)S(1)} %get-tuple-element.24), channel_id=1, source_target_pairs={{0,1},{1,0},{2,3},{3,2},{4,5},{5,4},{6,7},{7,6},{8,9},{9,8},{10,11... | collective-permute-start | bytes 1622024 | tf_op jit(solution)/shard_map/ppermute | solution.py:491
  5.1 33.8 %collective-permute-start.1 = (f32[2,2,16,8,512]{4,3,2,1,0:T(8,128)S(1)}, f32[2,2,16,8,512]{4,3,2,1,0:T(8,128)S(1)}, u32[]{:S(2)}, u32[]{:S(2)}) collective-permute-start(f32[2,2,16,8,512]{4,3,2,1,0:T(8,128)S(1)} %merge.1.refs_0_), channel_id=1, source_target_pairs={{2,6},{3,7},{4,0},{5,1},{6,10},{7,11},{8,4},{9,5},{10,14},{11,15},... | collective-permute-start | bytes 3145736 | tf_op jit(solution)/shard_map/ppermute | solution.py:500
  6.4 12.7 %collective-permute-start.2 = (f32[17,8,512]{2,1,0:T(8,128)S(1)}, f32[17,8,512]{2,1,0:T(8,128)S(1)}, u32[]{:S(2)}, u32[]{:S(2)}) collective-permute-start(f32[17,8,512]{2,1,0:T(8,128)S(1)} %get-tuple-element.26._), channel_id=1, source_target_pairs={{0,2},{1,3},{2,0},{3,1},{4,6},{5,7},{6,4},{7,5},{8,10},{9,11},{10,... | collective-permute-start | bytes 835592 | tf_op jit(solution)/shard_map/ppermute | solution.py:491
  11.6 13.0 %collective-permute-start.3 = (f32[17,8,512]{2,1,0:T(8,128)S(1)}, f32[17,8,512]{2,1,0:T(8,128)S(1)}, u32[]{:S(2)}, u32[]{:S(2)}) collective-permute-start(f32[17,8,512]{2,1,0:T(8,128)S(1)} %get-tuple-element.27), channel_id=1, source_target_pairs={{0,3},{1,2},{2,1},{3,0},{4,7},{5,6},{6,5},{7,4},{8,11},{9,10},{10,... | collective-permute-start | bytes 835592 | tf_op jit(solution)/shard_map/ppermute | solution.py:491
  12.9 18.1 %collective-permute-start.9 = (f32[17,8,512]{2,1,0:T(8,128)S(1)}, f32[17,8,512]{2,1,0:T(8,128)S(1)}, u32[]{:S(2)}, u32[]{:S(2)}) collective-permute-start(f32[17,8,512]{2,1,0:T(8,128)S(1)} %get-tuple-element.32), channel_id=1, source_target_pairs={{0,2},{1,3},{2,0},{3,1},{4,6},{5,7},{6,4},{7,5},{8,10},{9,11},{10,... | collective-permute-start | bytes 835592 | tf_op jit(solution)/shard_map/ppermute | solution.py:491
  14.2 21.2 %collective-permute-start.10 = (f32[17,8,512]{2,1,0:T(8,128)S(1)}, f32[17,8,512]{2,1,0:T(8,128)S(1)}, u32[]{:S(2)}, u32[]{:S(2)}) collective-permute-start(f32[17,8,512]{2,1,0:T(8,128)S(1)} %get-tuple-element.33), channel_id=1, source_target_pairs={{0,3},{1,2},{2,1},{3,0},{4,7},{5,6},{6,5},{7,4},{8,11},{9,10},{10,... | collective-permute-start | bytes 835592 | tf_op jit(solution)/shard_map/ppermute | solution.py:491
  19.1 19.8 %collective-permute-start.4 = (f32[17,8,512]{2,1,0:T(8,128)S(1)}, f32[17,8,512]{2,1,0:T(8,128)S(1)}, u32[]{:S(2)}, u32[]{:S(2)}) collective-permute-start(f32[17,8,512]{2,1,0:T(8,128)S(1)} %collective-permute-done.2.refs_2_.refs_8_), channel_id=1, source_target_pairs={{0,4},{1,5},{4,8},{5,9},{6,2},{7,3},{8,12},{9,13},{10,6},{11,7},{1... | collective-permute-start | bytes 835592 | tf_op jit(solution)/shard_map/ppermute | solution.py:500
  24.6 14.3 %collective-permute-start.5 = (f32[17,8,512]{2,1,0:T(8,128)S(1)}, f32[17,8,512]{2,1,0:T(8,128)S(1)}, u32[]{:S(2)}, u32[]{:S(2)}) collective-permute-start(f32[17,8,512]{2,1,0:T(8,128)S(1)} %collective-permute-done.3.refs_3_.refs_9_), channel_id=1, source_target_pairs={{0,4},{1,5},{4,8},{5,9},{6,2},{7,3},{8,12},{9,13},{10,6},{11,7},{1... | collective-permute-start | bytes 835592 | tf_op jit(solution)/shard_map/ppermute | solution.py:500
  31.0 18.9 %collective-permute-start.11 = (f32[17,8,512]{2,1,0:T(8,128)S(1)}, f32[17,8,512]{2,1,0:T(8,128)S(1)}, u32[]{:S(2)}, u32[]{:S(2)}) collective-permute-start(f32[17,8,512]{2,1,0:T(8,128)S(1)} %collective-permute-done.9.refs_2_), channel_id=1, source_target_pairs={{0,4},{1,5},{4,8},{5,9},{6,2},{7,3},{8,12},{9,13},{10,6},{11,7},{1... | collective-permute-start | bytes 835592 | tf_op jit(solution)/shard_map/ppermute | solution.py:500
  35.4 17.1 %collective-permute-start.12 = (f32[17,8,512]{2,1,0:T(8,128)S(1)}, f32[17,8,512]{2,1,0:T(8,128)S(1)}, u32[]{:S(2)}, u32[]{:S(2)}) collective-permute-start(f32[17,8,512]{2,1,0:T(8,128)S(1)} %collective-permute-done.10.refs_3_), channel_id=1, source_target_pairs={{0,4},{1,5},{4,8},{5,9},{6,2},{7,3},{8,12},{9,13},{10,6},{11,7},{1... | collective-permute-start | bytes 835592 | tf_op jit(solution)/shard_map/ppermute | solution.py:500
  47.9 16.3 %collective-permute-start.6 = (f32[8,8,512]{2,1,0:T(8,128)S(1)}, f32[8,8,512]{2,1,0:T(8,128)S(1)}, u32[]{:S(2)}, u32[]{:S(2)}) collective-permute-start(f32[8,8,512]{2,1,0:T(8,128)S(1)} %get-tuple-element.29), channel_id=1, source_target_pairs={{0,1},{1,0},{2,3},{3,2},{4,5},{5,4},{6,7},{7,6},{8,9},{9,8},{10,11... | collective-permute-start | bytes 393224 | tf_op jit(solution)/shard_map/ppermute | solution.py:491
  48.4 15.9 %collective-permute-start.7 = (f32[8,8,512]{2,1,0:T(8,128)S(1)}, f32[8,8,512]{2,1,0:T(8,128)S(1)}, u32[]{:S(2)}, u32[]{:S(2)}) collective-permute-start(f32[8,8,512]{2,1,0:T(8,128)S(1)} %get-tuple-element.30), channel_id=1, source_target_pairs={{0,2},{1,3},{2,0},{3,1},{4,6},{5,7},{6,4},{7,5},{8,10},{9,11},{10,... | collective-permute-start | bytes 393224 | tf_op jit(solution)/shard_map/ppermute | solution.py:491
  48.4 15.9 %collective-permute-start.8 = (f32[8,8,512]{2,1,0:T(8,128)S(1)}, f32[8,8,512]{2,1,0:T(8,128)S(1)}, u32[]{:S(2)}, u32[]{:S(2)}) collective-permute-start(f32[8,8,512]{2,1,0:T(8,128)S(1)} %get-tuple-element.31), channel_id=1, source_target_pairs={{0,3},{1,2},{2,1},{3,0},{4,7},{5,6},{6,5},{7,4},{8,11},{9,10},{10,... | collective-permute-start | bytes 393224 | tf_op jit(solution)/shard_map/ppermute | solution.py:491
  49.9 4.1 %collective-permute-start.16 = (f32[8,512]{1,0:T(8,128)S(1)}, f32[8,512]{1,0:T(8,128)S(1)}, u32[]{:S(2)}, u32[]{:S(2)}) collective-permute-start(f32[8,512]{1,0:T(8,128)S(1)} %get-tuple-element.38.refs_0_), channel_id=1, source_target_pairs={{4,0},{5,1},{6,2},{7,3},{8,4},{9,5},{10,6},{11,7},{12,8},{13,9},{1... | collective-permute-start | bytes 49160 | tf_op jit(solution)/shard_map/ppermute | solution.py:509
  52.5 11.7 %collective-permute-start.17 = (f32[8,512]{1,0:T(8,128)S(1)}, f32[8,512]{1,0:T(8,128)S(1)}, u32[]{:S(2)}, u32[]{:S(2)}) collective-permute-start(f32[8,512]{1,0:T(8,128)S(1)} %get-tuple-element.38.refs_0_), channel_id=1, source_target_pairs={{8,0},{9,1},{10,2},{11,3},{12,4},{13,5},{14,6},{15,7},{0,8},{1,9},... | collective-permute-start | bytes 49160 | tf_op jit(solution)/shard_map/ppermute | solution.py:509
  54.0 10.3 %collective-permute-start.18 = (f32[8,512]{1,0:T(8,128)S(1)}, f32[8,512]{1,0:T(8,128)S(1)}, u32[]{:S(2)}, u32[]{:S(2)}) collective-permute-start(f32[8,512]{1,0:T(8,128)S(1)} %get-tuple-element.38.refs_0_), channel_id=1, source_target_pairs={{12,0},{13,1},{14,2},{15,3},{0,4},{1,5},{2,6},{3,7},{4,8},{5,9},{6... | collective-permute-start | bytes 49160 | tf_op jit(solution)/shard_map/ppermute | solution.py:509
  64.3 4.3 %collective-permute-start.19 = (f32[16,512]{1,0:T(8,128)S(1)}, f32[16,512]{1,0:T(8,128)S(1)}, u32[]{:S(2)}, u32[]{:S(2)}) collective-permute-start(f32[16,512]{1,0:T(8,128)S(1)} %get-tuple-element.41), channel_id=1, source_target_pairs={{0,2},{1,3},{2,0},{3,1},{4,6},{5,7},{6,4},{7,5},{8,10},{9,11},{10,... | collective-permute-start | bytes 98312 | tf_op jit(solution)/shard_map/ppermute | solution.py:491
  64.9 3.7 %collective-permute-start.20 = (f32[16,512]{1,0:T(8,128)S(1)}, f32[16,512]{1,0:T(8,128)S(1)}, u32[]{:S(2)}, u32[]{:S(2)}) collective-permute-start(f32[16,512]{1,0:T(8,128)S(1)} %get-tuple-element.41), channel_id=1, source_target_pairs={{0,3},{1,2},{2,1},{3,0},{4,7},{5,6},{6,5},{7,4},{8,11},{9,10},{10,... | collective-permute-start | bytes 98312 | tf_op jit(solution)/shard_map/ppermute | solution.py:491
  65.2 3.4 %collective-permute-start.21 = (f32[16,512]{1,0:T(8,128)S(1)}, f32[16,512]{1,0:T(8,128)S(1)}, u32[]{:S(2)}, u32[]{:S(2)}) collective-permute-start(f32[16,512]{1,0:T(8,128)S(1)} %get-tuple-element.41), channel_id=1, source_target_pairs={{0,1},{1,0},{2,3},{3,2},{4,5},{5,4},{6,7},{7,6},{8,9},{9,8},{10,11... | collective-permute-start | bytes 98312 | tf_op jit(solution)/shard_map/ppermute | solution.py:491
  66.5 6.3 %collective-permute-start.13 = (f32[8,8,512]{2,1,0:T(8,128)S(1)}, f32[8,8,512]{2,1,0:T(8,128)S(1)}, u32[]{:S(2)}, u32[]{:S(2)}) collective-permute-start(f32[8,8,512]{2,1,0:T(8,128)S(1)} %get-tuple-element.35), channel_id=1, source_target_pairs={{0,1},{1,0},{2,3},{3,2},{4,5},{5,4},{6,7},{7,6},{8,9},{9,8},{10,11... | collective-permute-start | bytes 393224 | tf_op jit(solution)/shard_map/ppermute | solution.py:491
  66.5 8.8 %collective-permute-start.14 = (f32[8,8,512]{2,1,0:T(8,128)S(1)}, f32[8,8,512]{2,1,0:T(8,128)S(1)}, u32[]{:S(2)}, u32[]{:S(2)}) collective-permute-start(f32[8,8,512]{2,1,0:T(8,128)S(1)} %get-tuple-element.36), channel_id=1, source_target_pairs={{0,2},{1,3},{2,0},{3,1},{4,6},{5,7},{6,4},{7,5},{8,10},{9,11},{10,... | collective-permute-start | bytes 393224 | tf_op jit(solution)/shard_map/ppermute | solution.py:491
  68.6 6.7 %collective-permute-start.15 = (f32[8,8,512]{2,1,0:T(8,128)S(1)}, f32[8,8,512]{2,1,0:T(8,128)S(1)}, u32[]{:S(2)}, u32[]{:S(2)}) collective-permute-start(f32[8,8,512]{2,1,0:T(8,128)S(1)} %get-tuple-element.37), channel_id=1, source_target_pairs={{0,3},{1,2},{2,1},{3,0},{4,7},{5,6},{6,5},{7,4},{8,11},{9,10},{10,... | collective-permute-start | bytes 393224 | tf_op jit(solution)/shard_map/ppermute | solution.py:491
  68.7 7.7 %collective-permute-start.22 = (f32[1,16,512]{2,1,0:T(8,128)S(1)}, f32[1,16,512]{2,1,0:T(8,128)S(1)}, u32[]{:S(2)}, u32[]{:S(2)}) collective-permute-start(f32[1,16,512]{2,1,0:T(8,128)S(1)} %add_bitcast_fusion.refs_0_), channel_id=1, source_target_pairs={{4,0},{5,1},{6,2},{7,3},{8,4},{9,5},{10,6},{11,7},{12,8},{13,9},{1... | collective-permute-start | bytes 98312 | tf_op jit(solution)/shard_map/ppermute | solution.py:509
  72.2 5.6 %collective-permute-start.23 = (f32[1,16,512]{2,1,0:T(8,128)S(1)}, f32[1,16,512]{2,1,0:T(8,128)S(1)}, u32[]{:S(2)}, u32[]{:S(2)}) collective-permute-start(f32[1,16,512]{2,1,0:T(8,128)S(1)} %add_bitcast_fusion.refs_0_), channel_id=1, source_target_pairs={{8,0},{9,1},{10,2},{11,3},{12,4},{13,5},{14,6},{15,7},{0,8},{1,9},... | collective-permute-start | bytes 98312 | tf_op jit(solution)/shard_map/ppermute | solution.py:509
  72.8 5.8 %collective-permute-start.24 = (f32[1,16,512]{2,1,0:T(8,128)S(1)}, f32[1,16,512]{2,1,0:T(8,128)S(1)}, u32[]{:S(2)}, u32[]{:S(2)}) collective-permute-start(f32[1,16,512]{2,1,0:T(8,128)S(1)} %add_bitcast_fusion.refs_0_), channel_id=1, source_target_pairs={{12,0},{13,1},{14,2},{15,3},{0,4},{1,5},{2,6},{3,7},{4,8},{5,9},{6... | collective-permute-start | bytes 98312 | tf_op jit(solution)/shard_map/ppermute | solution.py:509
  75.3 3.3 %copy-start = (f32[512,512]{1,0:T(8,128)S(1)}, f32[512,512]{1,0:T(8,128)}, u32[]{:S(2)}) copy-start(f32[512,512]{1,0:T(8,128)} %constant.5.clone.refs_5_) | copy-start | bytes 3145732
  75.3 3.3 %copy-start.1 = (f32[16,32,64]{2,1,0:T(8,128)S(1)}, f32[16,32,64]{2,1,0:T(8,128)}, u32[]{:S(2)}) copy-start(f32[16,32,64]{2,1,0:T(8,128)} %constant.4.clone.refs_4_) | copy-start | bytes 393220

commit v6 on v5

--- a/solution.py
+++ b/solution.py
@@ -290,7 +290,7 @@
                 u_a[p, t] = scaled
                 s_a[p, t] = scaled * (1.0 / centre)
 
-        each(1, span - 1, setup, 2)
+        each(1, span - 1, setup, 5)
 
         s_now, s_next, u_now, u_next, t_now, t_next = s_a, s_b, u_a, u_b, t_a, t_b
         for step in range(STEPS - 1):
@@ -320,7 +320,7 @@
                         t_next[p, t] = t_now[p, t] + (s + new_s)
 
             margin = halo - (STEPS - 2 - step)
-            each(margin, span - margin, advance, 4)
+            each(margin, span - margin, advance, 8)
             s_now, s_next, u_now, u_next = s_next, s_now, u_next, u_now
             if step % 2 == 0:
                 t_now, t_next = t_next, t_now

time: 80.4 us -> 76.5 us (0.951)
  Pallas kernels: 25.7 us -> 21.7 us
    pallas_call x2, Pallas kernels: 18.1 us -> 14.1 us  [solve(): pl.pallas_call(kernel, out_shape=[jax.ShapeDtypeStruct((2 * planes, half,...]
  transfers between devices with their start and end apart: 25 -> 25, of which waited for: 9 -> 9; matrix products, arithmetic and copies ran while one was open for 1% -> 1% of each run, Pallas kernels for 27% -> 23%
where the time goes in v6:
time: 76.5 us; the launch traced here: 76.1 us
  starting transfers between devices  37.6 us (49%)
  Pallas kernels  21.7 us (28%)
  waiting for transfers between devices  15.4 us (20%)
  between operations  0.84 us (1%)
    ppermute x5, starting transfers between devices, along(): return lax.ppermute(value, 'gz', pairs)  15 us
    pallas_call x2, Pallas kernels, solve(): pl.pallas_call(kernel, out_shape=[jax.ShapeDtypeStruct((2 * planes, half,...  14.1 us
    ppermute x14, starting transfers between devices, swap(): return lax.ppermute(value, 'gz', [(i, i ^ m) for i in range(slabs)])  12.3 us
    ppermute x14, waiting for transfers between devices, swap(): return lax.ppermute(value, 'gz', [(i, i ^ m) for i in range(slabs)])  12.1 us
    ppermute x6, starting transfers between devices, from_teams(): heard.append(lax.ppermute(value, 'gz', pairs))  10.4 us
    pallas_call x3, Pallas kernels, prepare(): pl.pallas_call(kernel, out_shape=[jax.ShapeDtypeStruct(shape, F32) for sh...  4.99 us
    ppermute x6, waiting for transfers between devices, from_teams(): heard.append(lax.ppermute(value, 'gz', pairs))  3.3 us
  transfers between devices with their start and end apart: 25, of which 9 were waited for; matrix products, arithmetic and copies ran while one was open for 1% of the time, Pallas kernels for 23%

profile of v6, /device:TPU:0, one launch (start us, length us, event | category | flops | bytes accessed | tf_op | source)
XLA Modules:
  0.0 76.1 jit_solution(14968333971198350629)
XLA Ops:
  0.6 2.3 %prepare.3 = (f32[33,8,512]{2,1,0:T(8,128)S(1)}, f32[33,8,512]{2,1,0:T(8,128)S(1)}, f32[8,512]{1,0:T(8,128)S(1)}) custom-call(f32[8,8]{1,0:T(8,128)} %refs_1_.5, f32[8]{0:T(128)} %refs_2_.5, f32[8,4,16,512]{3,2,1,0:T(8,128)} %refs_3_.5, f32[4,16,512]{2,1,0:T(8,128)} %refs_4_.6, s32[8,4,16,512]{3,2,1,0:T(8,128)} %refs_5_.4), custom_call_target="tpu_custom_call" | custom-call | bytes 4194304 | tf_op jit(solution)/shard_map/prepare/pallas_call | solution.py:155
  2.9 0.5 collective-permute-start
  3.5 1.3 %prepare.4 = (f32[17,8,512]{2,1,0:T(8,128)S(1)}, f32[17,8,512]{2,1,0:T(8,128)S(1)}) custom-call(f32[8,512]{1,0:T(8,128)S(1)} %get-tuple-element.25.refs_0_, f32[8,8]{1,0:T(8,128)} %refs_1_.5, f32[8]{0:T(128)} %refs_2_.5, f32[8,4,16,512]{3,2,1,0:T(8,128)} %refs_3_.5, f32[4,16,512]{2,1,0:T(8,128)} %refs_4_.6, s32[8,4,16,512]{3,2,1,0:T(8,128)} %refs_5_.4), custom_call_target="tpu_custom_call" | custom-call | bytes 2097152 | tf_op jit(solution)/shard_map/prepare/pallas_call | solution.py:155
  4.8 0.2 collective-permute-done.theirs_ref.refs_7_
  5.0 0.1 merge.1.refs_0_
  5.1 1.3 %collective-permute-start.1 = (f32[2,2,16,8,512]{4,3,2,1,0:T(8,128)S(1)}, f32[2,2,16,8,512]{4,3,2,1,0:T(8,128)S(1)}, u32[]{:S(2)}, u32[]{:S(2)}) collective-permute-start(f32[2,2,16,8,512]{4,3,2,1,0:T(8,128)S(1)} %merge.1.refs_0_), channel_id=1, source_target_pairs={{2,6},{3,7},{4,0},{5,1},{6,10},{7,11},{8,4},{9,5},{10,14},{11,15},... | collective-permute-start | bytes 3145736 | tf_op jit(solution)/shard_map/ppermute | solution.py:500
  6.4 5.2 %collective-permute-start.2 = (f32[17,8,512]{2,1,0:T(8,128)S(1)}, f32[17,8,512]{2,1,0:T(8,128)S(1)}, u32[]{:S(2)}, u32[]{:S(2)}) collective-permute-start(f32[17,8,512]{2,1,0:T(8,128)S(1)} %get-tuple-element.26._), channel_id=1, source_target_pairs={{0,2},{1,3},{2,0},{3,1},{4,6},{5,7},{6,4},{7,5},{8,10},{9,11},{10,... | collective-permute-start | bytes 835592 | tf_op jit(solution)/shard_map/ppermute | solution.py:491
  11.6 0.0 collective-permute-start.3
  11.6 1.3 %prepare.5 = (f32[17,8,512]{2,1,0:T(8,128)S(1)}, f32[17,8,512]{2,1,0:T(8,128)S(1)}) custom-call(f32[8,512]{1,0:T(8,128)S(1)} %get-tuple-element.25.refs_0_, f32[8,8]{1,0:T(8,128)} %refs_1_.5, f32[8]{0:T(128)} %refs_2_.5, f32[8,4,16,512]{3,2,1,0:T(8,128)} %refs_3_.5, f32[4,16,512]{2,1,0:T(8,128)} %refs_4_.6, s32[8,4,16,512]{3,2,1,0:T(8,128)} %refs_5_.4), custom_call_target="tpu_custom_call" | custom-call | bytes 2097152 | tf_op jit(solution)/shard_map/prepare/pallas_call | solution.py:155
  12.9 1.3 %collective-permute-start.9 = (f32[17,8,512]{2,1,0:T(8,128)S(1)}, f32[17,8,512]{2,1,0:T(8,128)S(1)}, u32[]{:S(2)}, u32[]{:S(2)}) collective-permute-start(f32[17,8,512]{2,1,0:T(8,128)S(1)} %get-tuple-element.32), channel_id=1, source_target_pairs={{0,2},{1,3},{2,0},{3,1},{4,6},{5,7},{6,4},{7,5},{8,10},{9,11},{10,... | collective-permute-start | bytes 835592 | tf_op jit(solution)/shard_map/ppermute | solution.py:491
  14.2 0.6 collective-permute-start.10
  14.8 4.2 %collective-permute-done.2.refs_2_.refs_8_ = f32[17,8,512]{2,1,0:T(8,128)S(1)} collective-permute-done((f32[17,8,512]{2,1,0:T(8,128)S(1)}, f32[17,8,512]{2,1,0:T(8,128)S(1)}, u32[]{:S(2)}, u32[]{:S(2)}) %collective-permute-start.2) | collective-permute-done | bytes 278560 | tf_op jit(solution)/shard_map/ppermute | solution.py:491
  19.1 3.4 %collective-permute-start.4 = (f32[17,8,512]{2,1,0:T(8,128)S(1)}, f32[17,8,512]{2,1,0:T(8,128)S(1)}, u32[]{:S(2)}, u32[]{:S(2)}) collective-permute-start(f32[17,8,512]{2,1,0:T(8,128)S(1)} %collective-permute-done.2.refs_2_.refs_8_), channel_id=1, source_target_pairs={{0,4},{1,5},{4,8},{5,9},{6,2},{7,3},{8,12},{9,13},{10,6},{11,7},{1... | collective-permute-start | bytes 835592 | tf_op jit(solution)/shard_map/ppermute | solution.py:500
  22.5 2.1 %collective-permute-done.3.refs_3_.refs_9_ = f32[17,8,512]{2,1,0:T(8,128)S(1)} collective-permute-done((f32[17,8,512]{2,1,0:T(8,128)S(1)}, f32[17,8,512]{2,1,0:T(8,128)S(1)}, u32[]{:S(2)}, u32[]{:S(2)}) %collective-permute-start.3) | collective-permute-done | bytes 278560 | tf_op jit(solution)/shard_map/ppermute | solution.py:491
  24.6 3.4 %collective-permute-start.5 = (f32[17,8,512]{2,1,0:T(8,128)S(1)}, f32[17,8,512]{2,1,0:T(8,128)S(1)}, u32[]{:S(2)}, u32[]{:S(2)}) collective-permute-start(f32[17,8,512]{2,1,0:T(8,128)S(1)} %collective-permute-done.3.refs_3_.refs_9_), channel_id=1, source_target_pairs={{0,4},{1,5},{4,8},{5,9},{6,2},{7,3},{8,12},{9,13},{10,6},{11,7},{1... | collective-permute-start | bytes 835592 | tf_op jit(solution)/shard_map/ppermute | solution.py:500
  28.0 3.0 %collective-permute-done.9.refs_2_ = f32[17,8,512]{2,1,0:T(8,128)S(1)} collective-permute-done((f32[17,8,512]{2,1,0:T(8,128)S(1)}, f32[17,8,512]{2,1,0:T(8,128)S(1)}, u32[]{:S(2)}, u32[]{:S(2)}) %collective-permute-start.9) | collective-permute-done | bytes 278560 | tf_op jit(solution)/shard_map/ppermute | solution.py:491
  31.0 3.4 %collective-permute-start.11 = (f32[17,8,512]{2,1,0:T(8,128)S(1)}, f32[17,8,512]{2,1,0:T(8,128)S(1)}, u32[]{:S(2)}, u32[]{:S(2)}) collective-permute-start(f32[17,8,512]{2,1,0:T(8,128)S(1)} %collective-permute-done.9.refs_2_), channel_id=1, source_target_pairs={{0,4},{1,5},{4,8},{5,9},{6,2},{7,3},{8,12},{9,13},{10,6},{11,7},{1... | collective-permute-start | bytes 835592 | tf_op jit(solution)/shard_map/ppermute | solution.py:500
  34.4 1.0 %collective-permute-done.10.refs_3_ = f32[17,8,512]{2,1,0:T(8,128)S(1)} collective-permute-done((f32[17,8,512]{2,1,0:T(8,128)S(1)}, f32[17,8,512]{2,1,0:T(8,128)S(1)}, u32[]{:S(2)}, u32[]{:S(2)}) %collective-permute-start.10) | collective-permute-done | bytes 278560 | tf_op jit(solution)/shard_map/ppermute | solution.py:491
  35.4 3.4 %collective-permute-start.12 = (f32[17,8,512]{2,1,0:T(8,128)S(1)}, f32[17,8,512]{2,1,0:T(8,128)S(1)}, u32[]{:S(2)}, u32[]{:S(2)}) collective-permute-start(f32[17,8,512]{2,1,0:T(8,128)S(1)} %collective-permute-done.10.refs_3_), channel_id=1, source_target_pairs={{0,4},{1,5},{4,8},{5,9},{6,2},{7,3},{8,12},{9,13},{10,6},{11,7},{1... | collective-permute-start | bytes 835592 | tf_op jit(solution)/shard_map/ppermute | solution.py:500
  38.9 0.0 collective-permute-done.5.refs_5_
  38.9 0.0 collective-permute-done.1.refs_1_
  38.9 7.1 %solve0.1 = (f32[8,8,512]{2,1,0:T(8,128)S(1)}, f32[8,8,512]{2,1,0:T(8,128)S(1)}, f32[8,8,512]{2,1,0:T(8,128)S(1)}, f32[8,8,512]{2,1,0:T(8,128)S(1)}, f32[16,512]{1,0:T(8,128)S(1)}, /*index=5*/f32[8,512]{1,0:T(8,128)S(1)}) custom-call(f32[2,2,16,8,512]{4,3,2,1,0:T(8,128)S(1)} %merge.1.refs_0_, f32[2,2,16,8,512]{4,3,2,1,0:T(8,128)S(1)} %collective-permute-done.1.refs_1_, ...), custom_call_target="tpu_custom_call" | custom-call | bytes 23068672 | tf_op jit(solution)/shard_map/solve0/pallas_call | solution.py:338
  46.0 0.4 collective-permute-start.6
  46.4 0.0 collective-permute-start.7
  46.4 1.5 %collective-permute-start.8 = (f32[8,8,512]{2,1,0:T(8,128)S(1)}, f32[8,8,512]{2,1,0:T(8,128)S(1)}, u32[]{:S(2)}, u32[]{:S(2)}) collective-permute-start(f32[8,8,512]{2,1,0:T(8,128)S(1)} %get-tuple-element.31), channel_id=1, source_target_pairs={{0,3},{1,2},{2,1},{3,0},{4,7},{5,6},{6,5},{7,4},{8,11},{9,10},{10,... | collective-permute-start | bytes 393224 | tf_op jit(solution)/shard_map/ppermute | solution.py:491
  47.9 0.0 collective-permute-done.11.refs_4_
  47.9 2.6 %collective-permute-start.16 = (f32[8,512]{1,0:T(8,128)S(1)}, f32[8,512]{1,0:T(8,128)S(1)}, u32[]{:S(2)}, u32[]{:S(2)}) collective-permute-start(f32[8,512]{1,0:T(8,128)S(1)} %get-tuple-element.38.refs_0_), channel_id=1, source_target_pairs={{4,0},{5,1},{6,2},{7,3},{8,4},{9,5},{10,6},{11,7},{12,8},{13,9},{1... | collective-permute-start | bytes 49160 | tf_op jit(solution)/shard_map/ppermute | solution.py:509
  50.5 0.0 collective-permute-done.12.refs_5_
  50.5 0.4 collective-permute-start.17
  50.9 1.1 %collective-permute-done.16.refs_1_ = f32[8,512]{1,0:T(8,128)S(1)} collective-permute-done((f32[8,512]{1,0:T(8,128)S(1)}, f32[8,512]{1,0:T(8,128)S(1)}, u32[]{:S(2)}, u32[]{:S(2)}) %collective-permute-start.16) | collective-permute-done | bytes 16416 | tf_op jit(solution)/shard_map/ppermute | solution.py:509
  52.0 1.2 %collective-permute-start.18 = (f32[8,512]{1,0:T(8,128)S(1)}, f32[8,512]{1,0:T(8,128)S(1)}, u32[]{:S(2)}, u32[]{:S(2)}) collective-permute-start(f32[8,512]{1,0:T(8,128)S(1)} %get-tuple-element.38.refs_0_), channel_id=1, source_target_pairs={{12,0},{13,1},{14,2},{15,3},{0,4},{1,5},{2,6},{3,7},{4,8},{5,9},{6... | collective-permute-start | bytes 49160 | tf_op jit(solution)/shard_map/ppermute | solution.py:509
  53.2 7.1 %solve1.1 = (f32[8,8,512]{2,1,0:T(8,128)S(1)}, f32[8,8,512]{2,1,0:T(8,128)S(1)}, f32[8,8,512]{2,1,0:T(8,128)S(1)}, f32[8,8,512]{2,1,0:T(8,128)S(1)}, f32[16,512]{1,0:T(8,128)S(1)}) custom-call(f32[2,2,16,8,512]{4,3,2,1,0:T(8,128)S(1)} %merge.1.refs_0_, f32[2,2,16,8,512]{4,3,2,1,0:T(8,128)S(1)} %collective-permute-done.1.refs_1_, ...), custom_call_target="tpu_custom_call" | custom-call | bytes 23068672 | tf_op jit(solution)/shard_map/solve1/pallas_call | solution.py:338
  60.3 0.0 collective-permute-done.17.refs_2_
  60.3 0.0 collective-permute-done.18.refs_3_
  60.4 0.6 collective-permute-start.19
  61.0 0.3 collective-permute-start.20
  61.3 1.3 %collective-permute-start.21 = (f32[16,512]{1,0:T(8,128)S(1)}, f32[16,512]{1,0:T(8,128)S(1)}, u32[]{:S(2)}, u32[]{:S(2)}) collective-permute-start(f32[16,512]{1,0:T(8,128)S(1)} %get-tuple-element.41), channel_id=1, source_target_pairs={{0,1},{1,0},{2,3},{3,2},{4,5},{5,4},{6,7},{7,6},{8,9},{9,8},{10,11... | collective-permute-start | bytes 98312 | tf_op jit(solution)/shard_map/ppermute | solution.py:491
  62.6 0.6 collective-permute-start.14
  63.1 1.5 %collective-permute-done.19 = f32[16,512]{1,0:T(8,128)S(1)} collective-permute-done((f32[16,512]{1,0:T(8,128)S(1)}, f32[16,512]{1,0:T(8,128)S(1)}, u32[]{:S(2)}, u32[]{:S(2)}) %collective-permute-start.19) | collective-permute-done | bytes 32800 | tf_op jit(solution)/shard_map/ppermute | solution.py:491
  64.7 3.5 %collective-permute-start.22 = (f32[1,16,512]{2,1,0:T(8,128)S(1)}, f32[1,16,512]{2,1,0:T(8,128)S(1)}, u32[]{:S(2)}, u32[]{:S(2)}) collective-permute-start(f32[1,16,512]{2,1,0:T(8,128)S(1)} %add_bitcast_fusion.refs_0_), channel_id=1, source_target_pairs={{4,0},{5,1},{6,2},{7,3},{8,4},{9,5},{10,6},{11,7},{12,8},{13,9},{1... | collective-permute-start | bytes 98312 | tf_op jit(solution)/shard_map/ppermute | solution.py:509
  68.2 0.6 collective-permute-start.23
  68.9 1.9 %collective-permute-start.24 = (f32[1,16,512]{2,1,0:T(8,128)S(1)}, f32[1,16,512]{2,1,0:T(8,128)S(1)}, u32[]{:S(2)}, u32[]{:S(2)}) collective-permute-start(f32[1,16,512]{2,1,0:T(8,128)S(1)} %add_bitcast_fusion.refs_0_), channel_id=1, source_target_pairs={{12,0},{13,1},{14,2},{15,3},{0,4},{1,5},{2,6},{3,7},{4,8},{5,9},{6... | collective-permute-start | bytes 98312 | tf_op jit(solution)/shard_map/ppermute | solution.py:509
  70.8 0.5 slice_bitcast_fusion
  71.3 0.0 copy-start.1
  71.4 1.1 %gather_adjoint.1 = f32[8,4,16,512]{3,2,1,0:T(8,128)} custom-call(f32[8,8,512]{2,1,0:T(8,128)S(1)} %get-tuple-element.28.refs_0_, f32[8,8,512]{2,1,0:T(8,128)S(1)} %collective-permute-done.6.refs_1_.refs_6_, f32[8,8,512]{2,1,0:T(8,128)S(1)} %collective-permute-done.7.refs_2_.refs_7_, f32[8,8,512]{2,1,0:T(8,128)S(1)} %collective-permute-done.8.refs_3_.refs_8_, ...), custom_call_target="tpu_custom_call" | custom-call | bytes 4194304 | tf_op jit(solution)/shard_map/gather_adjoint/pallas_call | solution.py:420
  72.4 1.4 %collective-permute-done.23.refs_2_ = f32[1,16,512]{2,1,0:T(8,128)S(1)} collective-permute-done((f32[1,16,512]{2,1,0:T(8,128)S(1)}, f32[1,16,512]{2,1,0:T(8,128)S(1)}, u32[]{:S(2)}, u32[]{:S(2)}) %collective-permute-start.23) | collective-permute-done | bytes 32800 | tf_op jit(solution)/shard_map/ppermute | solution.py:509
  73.8 0.8 %collective-permute-done.24.refs_3_ = f32[1,16,512]{2,1,0:T(8,128)S(1)} collective-permute-done((f32[1,16,512]{2,1,0:T(8,128)S(1)}, f32[1,16,512]{2,1,0:T(8,128)S(1)}, u32[]{:S(2)}, u32[]{:S(2)}) %collective-permute-start.24) | collective-permute-done | bytes 32800 | tf_op jit(solution)/shard_map/ppermute | solution.py:509
  74.7 1.4 %control.1 = f32[32,512]{1,0:T(8,128)} custom-call(f32[1,16,512]{2,1,0:T(8,128)S(1)} %add_bitcast_fusion.refs_0_, f32[1,16,512]{2,1,0:T(8,128)S(1)} %collective-permute-done.22.refs_1_, f32[1,16,512]{2,1,0:T(8,128)S(1)} %collective-permute-done.23.refs_2_, f32[1,16,512]{2,1,0:T(8,128)S(1)} %collective-permute-done.24.refs_3_, f32[16,32,64]{2,1,0:T(8,128)S(1)} %copy-done.1, ...), custom_call_target="tpu_custom_call" | custom-call | tf_op jit(solution)/shard_map/control/pallas_call | solution.py:463
  (17 shorter events, 0.1 us)
Async XLA Ops:
  2.9 2.1 %collective-permute-start = (f32[33,8,512]{2,1,0:T(8,128)S(1)}, f32[33,8,512]{2,1,0:T(8,128)S(1)}, u32[]{:S(2)}, u32[]{:S(2)}) collective-permute-start(f32[33,8,512]{2,1,0:T(8,128)S(1)} %get-tuple-element.24), channel_id=1, source_target_pairs={{0,1},{1,0},{2,3},{3,2},{4,5},{5,4},{6,7},{7,6},{8,9},{9,8},{10,11... | collective-permute-start | bytes 1622024 | tf_op jit(solution)/shard_map/ppermute | solution.py:491
  5.1 33.8 %collective-permute-start.1 = (f32[2,2,16,8,512]{4,3,2,1,0:T(8,128)S(1)}, f32[2,2,16,8,512]{4,3,2,1,0:T(8,128)S(1)}, u32[]{:S(2)}, u32[]{:S(2)}) collective-permute-start(f32[2,2,16,8,512]{4,3,2,1,0:T(8,128)S(1)} %merge.1.refs_0_), channel_id=1, source_target_pairs={{2,6},{3,7},{4,0},{5,1},{6,10},{7,11},{8,4},{9,5},{10,14},{11,15},... | collective-permute-start | bytes 3145736 | tf_op jit(solution)/shard_map/ppermute | solution.py:500
  6.4 12.7 %collective-permute-start.2 = (f32[17,8,512]{2,1,0:T(8,128)S(1)}, f32[17,8,512]{2,1,0:T(8,128)S(1)}, u32[]{:S(2)}, u32[]{:S(2)}) collective-permute-start(f32[17,8,512]{2,1,0:T(8,128)S(1)} %get-tuple-element.26._), channel_id=1, source_target_pairs={{0,2},{1,3},{2,0},{3,1},{4,6},{5,7},{6,4},{7,5},{8,10},{9,11},{10,... | collective-permute-start | bytes 835592 | tf_op jit(solution)/shard_map/ppermute | solution.py:491
  11.6 13.0 %collective-permute-start.3 = (f32[17,8,512]{2,1,0:T(8,128)S(1)}, f32[17,8,512]{2,1,0:T(8,128)S(1)}, u32[]{:S(2)}, u32[]{:S(2)}) collective-permute-start(f32[17,8,512]{2,1,0:T(8,128)S(1)} %get-tuple-element.27), channel_id=1, source_target_pairs={{0,3},{1,2},{2,1},{3,0},{4,7},{5,6},{6,5},{7,4},{8,11},{9,10},{10,... | collective-permute-start | bytes 835592 | tf_op jit(solution)/shard_map/ppermute | solution.py:491
  12.9 18.1 %collective-permute-start.9 = (f32[17,8,512]{2,1,0:T(8,128)S(1)}, f32[17,8,512]{2,1,0:T(8,128)S(1)}, u32[]{:S(2)}, u32[]{:S(2)}) collective-permute-start(f32[17,8,512]{2,1,0:T(8,128)S(1)} %get-tuple-element.32), channel_id=1, source_target_pairs={{0,2},{1,3},{2,0},{3,1},{4,6},{5,7},{6,4},{7,5},{8,10},{9,11},{10,... | collective-permute-start | bytes 835592 | tf_op jit(solution)/shard_map/ppermute | solution.py:491
  14.2 21.2 %collective-permute-start.10 = (f32[17,8,512]{2,1,0:T(8,128)S(1)}, f32[17,8,512]{2,1,0:T(8,128)S(1)}, u32[]{:S(2)}, u32[]{:S(2)}) collective-permute-start(f32[17,8,512]{2,1,0:T(8,128)S(1)} %get-tuple-element.33), channel_id=1, source_target_pairs={{0,3},{1,2},{2,1},{3,0},{4,7},{5,6},{6,5},{7,4},{8,11},{9,10},{10,... | collective-permute-start | bytes 835592 | tf_op jit(solution)/shard_map/ppermute | solution.py:491
  19.1 19.8 %collective-permute-start.4 = (f32[17,8,512]{2,1,0:T(8,128)S(1)}, f32[17,8,512]{2,1,0:T(8,128)S(1)}, u32[]{:S(2)}, u32[]{:S(2)}) collective-permute-start(f32[17,8,512]{2,1,0:T(8,128)S(1)} %collective-permute-done.2.refs_2_.refs_8_), channel_id=1, source_target_pairs={{0,4},{1,5},{4,8},{5,9},{6,2},{7,3},{8,12},{9,13},{10,6},{11,7},{1... | collective-permute-start | bytes 835592 | tf_op jit(solution)/shard_map/ppermute | solution.py:500
  24.6 14.3 %collective-permute-start.5 = (f32[17,8,512]{2,1,0:T(8,128)S(1)}, f32[17,8,512]{2,1,0:T(8,128)S(1)}, u32[]{:S(2)}, u32[]{:S(2)}) collective-permute-start(f32[17,8,512]{2,1,0:T(8,128)S(1)} %collective-permute-done.3.refs_3_.refs_9_), channel_id=1, source_target_pairs={{0,4},{1,5},{4,8},{5,9},{6,2},{7,3},{8,12},{9,13},{10,6},{11,7},{1... | collective-permute-start | bytes 835592 | tf_op jit(solution)/shard_map/ppermute | solution.py:500
  31.0 16.9 %collective-permute-start.11 = (f32[17,8,512]{2,1,0:T(8,128)S(1)}, f32[17,8,512]{2,1,0:T(8,128)S(1)}, u32[]{:S(2)}, u32[]{:S(2)}) collective-permute-start(f32[17,8,512]{2,1,0:T(8,128)S(1)} %collective-permute-done.9.refs_2_), channel_id=1, source_target_pairs={{0,4},{1,5},{4,8},{5,9},{6,2},{7,3},{8,12},{9,13},{10,6},{11,7},{1... | collective-permute-start | bytes 835592 | tf_op jit(solution)/shard_map/ppermute | solution.py:500
  35.4 15.1 %collective-permute-start.12 = (f32[17,8,512]{2,1,0:T(8,128)S(1)}, f32[17,8,512]{2,1,0:T(8,128)S(1)}, u32[]{:S(2)}, u32[]{:S(2)}) collective-permute-start(f32[17,8,512]{2,1,0:T(8,128)S(1)} %collective-permute-done.10.refs_3_), channel_id=1, source_target_pairs={{0,4},{1,5},{4,8},{5,9},{6,2},{7,3},{8,12},{9,13},{10,6},{11,7},{1... | collective-permute-start | bytes 835592 | tf_op jit(solution)/shard_map/ppermute | solution.py:500
  46.0 14.3 %collective-permute-start.6 = (f32[8,8,512]{2,1,0:T(8,128)S(1)}, f32[8,8,512]{2,1,0:T(8,128)S(1)}, u32[]{:S(2)}, u32[]{:S(2)}) collective-permute-start(f32[8,8,512]{2,1,0:T(8,128)S(1)} %get-tuple-element.29), channel_id=1, source_target_pairs={{0,1},{1,0},{2,3},{3,2},{4,5},{5,4},{6,7},{7,6},{8,9},{9,8},{10,11... | collective-permute-start | bytes 393224 | tf_op jit(solution)/shard_map/ppermute | solution.py:491
  46.4 13.9 %collective-permute-start.7 = (f32[8,8,512]{2,1,0:T(8,128)S(1)}, f32[8,8,512]{2,1,0:T(8,128)S(1)}, u32[]{:S(2)}, u32[]{:S(2)}) collective-permute-start(f32[8,8,512]{2,1,0:T(8,128)S(1)} %get-tuple-element.30), channel_id=1, source_target_pairs={{0,2},{1,3},{2,0},{3,1},{4,6},{5,7},{6,4},{7,5},{8,10},{9,11},{10,... | collective-permute-start | bytes 393224 | tf_op jit(solution)/shard_map/ppermute | solution.py:491
  46.4 13.9 %collective-permute-start.8 = (f32[8,8,512]{2,1,0:T(8,128)S(1)}, f32[8,8,512]{2,1,0:T(8,128)S(1)}, u32[]{:S(2)}, u32[]{:S(2)}) collective-permute-start(f32[8,8,512]{2,1,0:T(8,128)S(1)} %get-tuple-element.31), channel_id=1, source_target_pairs={{0,3},{1,2},{2,1},{3,0},{4,7},{5,6},{6,5},{7,4},{8,11},{9,10},{10,... | collective-permute-start | bytes 393224 | tf_op jit(solution)/shard_map/ppermute | solution.py:491
  47.9 4.1 %collective-permute-start.16 = (f32[8,512]{1,0:T(8,128)S(1)}, f32[8,512]{1,0:T(8,128)S(1)}, u32[]{:S(2)}, u32[]{:S(2)}) collective-permute-start(f32[8,512]{1,0:T(8,128)S(1)} %get-tuple-element.38.refs_0_), channel_id=1, source_target_pairs={{4,0},{5,1},{6,2},{7,3},{8,4},{9,5},{10,6},{11,7},{12,8},{13,9},{1... | collective-permute-start | bytes 49160 | tf_op jit(solution)/shard_map/ppermute | solution.py:509
  50.5 9.7 %collective-permute-start.17 = (f32[8,512]{1,0:T(8,128)S(1)}, f32[8,512]{1,0:T(8,128)S(1)}, u32[]{:S(2)}, u32[]{:S(2)}) collective-permute-start(f32[8,512]{1,0:T(8,128)S(1)} %get-tuple-element.38.refs_0_), channel_id=1, source_target_pairs={{8,0},{9,1},{10,2},{11,3},{12,4},{13,5},{14,6},{15,7},{0,8},{1,9},... | collective-permute-start | bytes 49160 | tf_op jit(solution)/shard_map/ppermute | solution.py:509
  52.0 8.3 %collective-permute-start.18 = (f32[8,512]{1,0:T(8,128)S(1)}, f32[8,512]{1,0:T(8,128)S(1)}, u32[]{:S(2)}, u32[]{:S(2)}) collective-permute-start(f32[8,512]{1,0:T(8,128)S(1)} %get-tuple-element.38.refs_0_), channel_id=1, source_target_pairs={{12,0},{13,1},{14,2},{15,3},{0,4},{1,5},{2,6},{3,7},{4,8},{5,9},{6... | collective-permute-start | bytes 49160 | tf_op jit(solution)/shard_map/ppermute | solution.py:509
  60.4 4.3 %collective-permute-start.19 = (f32[16,512]{1,0:T(8,128)S(1)}, f32[16,512]{1,0:T(8,128)S(1)}, u32[]{:S(2)}, u32[]{:S(2)}) collective-permute-start(f32[16,512]{1,0:T(8,128)S(1)} %get-tuple-element.41), channel_id=1, source_target_pairs={{0,2},{1,3},{2,0},{3,1},{4,6},{5,7},{6,4},{7,5},{8,10},{9,11},{10,... | collective-permute-start | bytes 98312 | tf_op jit(solution)/shard_map/ppermute | solution.py:491
  61.0 3.7 %collective-permute-start.20 = (f32[16,512]{1,0:T(8,128)S(1)}, f32[16,512]{1,0:T(8,128)S(1)}, u32[]{:S(2)}, u32[]{:S(2)}) collective-permute-start(f32[16,512]{1,0:T(8,128)S(1)} %get-tuple-element.41), channel_id=1, source_target_pairs={{0,3},{1,2},{2,1},{3,0},{4,7},{5,6},{6,5},{7,4},{8,11},{9,10},{10,... | collective-permute-start | bytes 98312 | tf_op jit(solution)/shard_map/ppermute | solution.py:491
  61.3 3.4 %collective-permute-start.21 = (f32[16,512]{1,0:T(8,128)S(1)}, f32[16,512]{1,0:T(8,128)S(1)}, u32[]{:S(2)}, u32[]{:S(2)}) collective-permute-start(f32[16,512]{1,0:T(8,128)S(1)} %get-tuple-element.41), channel_id=1, source_target_pairs={{0,1},{1,0},{2,3},{3,2},{4,5},{5,4},{6,7},{7,6},{8,9},{9,8},{10,11... | collective-permute-start | bytes 98312 | tf_op jit(solution)/shard_map/ppermute | solution.py:491
  62.6 6.3 %collective-permute-start.13 = (f32[8,8,512]{2,1,0:T(8,128)S(1)}, f32[8,8,512]{2,1,0:T(8,128)S(1)}, u32[]{:S(2)}, u32[]{:S(2)}) collective-permute-start(f32[8,8,512]{2,1,0:T(8,128)S(1)} %get-tuple-element.35), channel_id=1, source_target_pairs={{0,1},{1,0},{2,3},{3,2},{4,5},{5,4},{6,7},{7,6},{8,9},{9,8},{10,11... | collective-permute-start | bytes 393224 | tf_op jit(solution)/shard_map/ppermute | solution.py:491
  62.6 8.8 %collective-permute-start.14 = (f32[8,8,512]{2,1,0:T(8,128)S(1)}, f32[8,8,512]{2,1,0:T(8,128)S(1)}, u32[]{:S(2)}, u32[]{:S(2)}) collective-permute-start(f32[8,8,512]{2,1,0:T(8,128)S(1)} %get-tuple-element.36), channel_id=1, source_target_pairs={{0,2},{1,3},{2,0},{3,1},{4,6},{5,7},{6,4},{7,5},{8,10},{9,11},{10,... | collective-permute-start | bytes 393224 | tf_op jit(solution)/shard_map/ppermute | solution.py:491
  64.7 6.7 %collective-permute-start.15 = (f32[8,8,512]{2,1,0:T(8,128)S(1)}, f32[8,8,512]{2,1,0:T(8,128)S(1)}, u32[]{:S(2)}, u32[]{:S(2)}) collective-permute-start(f32[8,8,512]{2,1,0:T(8,128)S(1)} %get-tuple-element.37), channel_id=1, source_target_pairs={{0,3},{1,2},{2,1},{3,0},{4,7},{5,6},{6,5},{7,4},{8,11},{9,10},{10,... | collective-permute-start | bytes 393224 | tf_op jit(solution)/shard_map/ppermute | solution.py:491
  64.7 7.7 %collective-permute-start.22 = (f32[1,16,512]{2,1,0:T(8,128)S(1)}, f32[1,16,512]{2,1,0:T(8,128)S(1)}, u32[]{:S(2)}, u32[]{:S(2)}) collective-permute-start(f32[1,16,512]{2,1,0:T(8,128)S(1)} %add_bitcast_fusion.refs_0_), channel_id=1, source_target_pairs={{4,0},{5,1},{6,2},{7,3},{8,4},{9,5},{10,6},{11,7},{12,8},{13,9},{1... | collective-permute-start | bytes 98312 | tf_op jit(solution)/shard_map/ppermute | solution.py:509
  68.2 5.6 %collective-permute-start.23 = (f32[1,16,512]{2,1,0:T(8,128)S(1)}, f32[1,16,512]{2,1,0:T(8,128)S(1)}, u32[]{:S(2)}, u32[]{:S(2)}) collective-permute-start(f32[1,16,512]{2,1,0:T(8,128)S(1)} %add_bitcast_fusion.refs_0_), channel_id=1, source_target_pairs={{8,0},{9,1},{10,2},{11,3},{12,4},{13,5},{14,6},{15,7},{0,8},{1,9},... | collective-permute-start | bytes 98312 | tf_op jit(solution)/shard_map/ppermute | solution.py:509
  68.9 5.8 %collective-permute-start.24 = (f32[1,16,512]{2,1,0:T(8,128)S(1)}, f32[1,16,512]{2,1,0:T(8,128)S(1)}, u32[]{:S(2)}, u32[]{:S(2)}) collective-permute-start(f32[1,16,512]{2,1,0:T(8,128)S(1)} %add_bitcast_fusion.refs_0_), channel_id=1, source_target_pairs={{12,0},{13,1},{14,2},{15,3},{0,4},{1,5},{2,6},{3,7},{4,8},{5,9},{6... | collective-permute-start | bytes 98312 | tf_op jit(solution)/shard_map/ppermute | solution.py:509
  71.3 3.3 %copy-start = (f32[512,512]{1,0:T(8,128)S(1)}, f32[512,512]{1,0:T(8,128)}, u32[]{:S(2)}) copy-start(f32[512,512]{1,0:T(8,128)} %constant.5.clone.refs_5_) | copy-start | bytes 3145732
  71.3 3.3 %copy-start.1 = (f32[16,32,64]{2,1,0:T(8,128)S(1)}, f32[16,32,64]{2,1,0:T(8,128)}, u32[]{:S(2)}) copy-start(f32[16,32,64]{2,1,0:T(8,128)} %constant.4.clone.refs_4_) | copy-start | bytes 393220

commit v7 on v6

--- a/solution.py
+++ b/solution.py
@@ -63,12 +63,12 @@
     depth_total = planes * lax.axis_size("gz")
     flat = [(o, i, job) for o, group in enumerate(jobs) for i, job in enumerate(group)]
     count = len(flat)
-    shapes = [(len(group) * size + 1, half, columns) for group in jobs]
     given = [] if sums is None else [sums]
+    shapes = [(len(group) * size + 1 - len(given), half, columns) for group in jobs]
     states = count if given else samples
 
     def kernel(*refs):
-        before, refs = refs[: len(given)], refs[len(given) :]
+        refs = refs[len(given) :]
         (table_ref, scale_ref, state_ref, target_ref, rock_ref), refs = refs[:5], refs[5:]
         outs, refs = refs[: len(jobs)], refs[len(jobs) :]
         if not given:
@@ -146,8 +146,8 @@
                             outs[o][at, :, c * 128 : (c + 1) * 128] = mixed[
                                 n % 2, p, a, c, pl.ds(t, half, stride=2), :
                             ]
-        for o, group in enumerate(jobs):
-            outs[o][len(group) * size] = before[0][...] if given else sums_ref[...]
+        for o, group in enumerate([] if given else jobs):
+            outs[o][len(group) * size] = sums_ref[...]
 
     hbm = pl.BlockSpec(memory_space=pltpu.HBM)
     vmem = pl.BlockSpec(memory_space=pltpu.VMEM)
@@ -156,7 +156,7 @@
         kernel,
         out_shape=[jax.ShapeDtypeStruct(shape, F32) for shape in shapes]
         + ([] if given else [jax.ShapeDtypeStruct(sums_shape, F32)]),
-        in_specs=[vmem] * len(given) + [hbm] * 5,
+        in_specs=[pl.BlockSpec(memory_space=pl.ANY)] * len(given) + [hbm] * 5,
         out_specs=[vmem] * (len(shapes) + 1 - len(given)),
         scratch_shapes=[
             pltpu.SMEM(log_table.shape, F32),
@@ -173,10 +173,38 @@
     )(*given, log_table, obs_scale, state, target, rock_type)
 
 
-def merge(mine, theirs, slots, after):
-    size = (mine.shape[0] - 1) // slots
-
-    def kernel(mine_ref, theirs_ref, _, out_ref):
+def merge_far(mine, theirs, slots, size):
+    tile = mine.shape[1:]
+
+    def kernel(mine_ref, theirs_ref, sums_ref, *outs):
+        core = lax.rem(team_place(), 2)
+        for ref, at in ((mine_ref, core), (theirs_ref, 1 - core)):
+            for slot in range(slots):
+                for n in range(size):
+                    outs[slot][at * size + n] = ref[slot * size + n]
+        outs[0][2 * size] = sums_ref[...] + theirs_ref[slots * size]
+
+    vmem = pl.BlockSpec(memory_space=pltpu.VMEM)
+
+    def call(sums):
+        return pl.pallas_call(
+            kernel,
+            out_shape=[
+                jax.ShapeDtypeStruct((2 * size + (slot == 0),) + tile, F32) for slot in range(slots)
+            ],
+            in_specs=[vmem] * 3,
+            out_specs=[vmem] * slots,
+            compiler_params=pltpu.CompilerParams(vmem_limit_bytes=4 * MIB),
+            name="merge_far",
+        )(mine, theirs, sums)
+
+    return call
+
+
+def merge_near(mine, theirs, slots, size):
+    tile = mine.shape[1:]
+
+    def kernel(mine_ref, theirs_ref, out_ref):
         core = lax.rem(team_place(), 2)
         for ref, at in ((mine_ref, core), (theirs_ref, 1 - core)):
             for slot in range(slots):
@@ -186,12 +214,12 @@
     vmem = pl.BlockSpec(memory_space=pltpu.VMEM)
     return pl.pallas_call(
         kernel,
-        out_shape=jax.ShapeDtypeStruct((2, slots, size) + mine.shape[1:], F32),
-        in_specs=[vmem] * 2 + [pl.BlockSpec(memory_space=pl.ANY)],
+        out_shape=jax.ShapeDtypeStruct((2, slots, size) + tile, F32),
+        in_specs=[vmem] * 2,
         out_specs=vmem,
         compiler_params=pltpu.CompilerParams(vmem_limit_bytes=4 * MIB),
-        name="merge",
-    )(mine, theirs, after)
+        name="merge_near",
+    )(mine, theirs)
 
 
 def reciprocal(x):
@@ -216,9 +244,10 @@
         body(p)
 
 
-def solve(slot, near, far, near_halo, far_halo, sums, planes):
-    inputs = [near, near_halo, *far, *far_halo, *sums]
-    half, columns = far[0].shape[1:]
+def solve(slot, near, far, near_halo, far_halo, planes):
+    inputs = [near, near_halo, *far, *far_halo]
+    half, columns = far[0].shape[-2:]
+    part = 2 * planes
     halo = 2 * planes
     own = TEAM * planes
     span = own + 2 * halo
@@ -226,31 +255,30 @@
     assert halo >= STEPS
 
     def kernel(*refs):
-        ins, refs = refs[:6], refs[6:]
-        sum_refs, refs = refs[: len(sums)], refs[len(sums) :]
+        ins, refs = refs[: len(inputs)], refs[len(inputs) :]
         outs, face_ref, refs = refs[:TEAM], refs[TEAM], refs[TEAM + 1 :]
-        if sums:
-            summed_ref, refs = refs[0], refs[1:]
-            summed = sum_refs[0][sums[0].shape[0] - 1]
-            for n, ref in enumerate(sum_refs[1:], 1):
-                summed = summed + ref[sums[n].shape[0] - 1]
-            summed_ref[...] = summed
         cond, u_a, u_b, s_a, s_b, zp, zm, yp, ym, xp, xm, t_a, t_b = refs
         place = team_place()
-        column, side = lax.rem(place, 2), place // 2
+        side = place // 2
         upper, lower = halo + own, 0
         near_base = jnp.where(side == 0, upper, lower)
         far_base = jnp.where(side == 0, lower, upper)
-        blocks = [(ins[0].at[core, slot], halo + planes * (2 * side + core)) for core in range(2)]
-        blocks += [(ins[1].at[core, slot], near_base + planes * core) for core in range(2)]
-        blocks += [(ins[m], halo + planes * (place ^ m)) for m in (2, 3)]
-        blocks += [(ins[4], far_base + planes * column)]
-        blocks += [(ins[5], far_base + planes * (1 - column))]
-        for block, base in blocks:
+        for core in range(2):
             for j in range(planes):
                 for t in range(2):
-                    cond[base + j, t] = jnp.maximum(block[2 * j + t], 1e-30)
-                    t_a[base + j, t] = block[2 * (planes + j) + t]
+                    n = 2 * j + t
+                    own_base = halo + planes * core + j
+                    for ref, base in ((ins[0], own_base + part * side), (ins[1], near_base + planes * core + j)):
+                        cond[base, t] = jnp.maximum(ref[core, slot, n], 1e-30)
+                        t_a[base, t] = ref[core, slot, part + n]
+                    for i, base in ((0, own_base + part * (1 - side)), (1, far_base + planes * core + j)):
+                        refs = ins[2 + i * len(far) : 2 + (i + 1) * len(far)]
+                        if len(far) == 1:
+                            first, second = refs[0][core * 2 * part + n], refs[0][(core * 2 + 1) * part + n]
+                        else:
+                            first, second = refs[0][core * part + n], refs[1][core * part + n]
+                        cond[base, t] = jnp.maximum(first, 1e-30)
+                        t_a[base, t] = second
 
         last_row = lax.broadcasted_iota(jnp.int32, (half, columns), 0) == half - 1
         last_column = lax.broadcasted_iota(jnp.int32, (half, columns), 1) == columns - 1
@@ -290,7 +318,7 @@
                 u_a[p, t] = scaled
                 s_a[p, t] = scaled * (1.0 / centre)
 
-        each(1, span - 1, setup, 5)
+        each(1, span - 1, setup, (span - 2) // 2)
 
         s_now, s_next, u_now, u_next, t_now, t_next = s_a, s_b, u_a, u_b, t_a, t_b
         for step in range(STEPS - 1):
@@ -320,7 +348,7 @@
                         t_next[p, t] = t_now[p, t] + (s + new_s)
 
             margin = halo - (STEPS - 2 - step)
-            each(margin, span - margin, advance, 8)
+            each(margin, span - margin, advance, span // 2 - margin)
             s_now, s_next, u_now, u_next = s_next, s_now, u_next, u_now
             if step % 2 == 0:
                 t_now, t_next = t_next, t_now
@@ -338,10 +366,9 @@
     return pl.pallas_call(
         kernel,
         out_shape=[jax.ShapeDtypeStruct((2 * planes, half, columns), F32)] * TEAM
-        + [jax.ShapeDtypeStruct((own, columns), F32)]
-        + [jax.ShapeDtypeStruct(sums[0].shape[1:], F32) for _ in sums[:1]],
+        + [jax.ShapeDtypeStruct((own, columns), F32)],
         in_specs=[vmem] * len(inputs),
-        out_specs=[vmem] * (TEAM + 1 + len(sums[:1])),
+        out_specs=[vmem] * (TEAM + 1),
         scratch_shapes=[field] * 13,
         compiler_params=pltpu.CompilerParams(vmem_limit_bytes=16 * MIB),
         cost_estimate=pl.CostEstimate(flops=0, bytes_accessed=22 * MIB, transcendentals=0),
@@ -513,33 +540,30 @@
         pltpu.with_memory_space_constraint(field, pltpu.HBM)
         for field in (state, target, rock_type, log_table, obs_scale)
     ]
-    jobs = [[(slot, m) for slot in range(slots)] for m in range(2)]
-    mine, theirs, sums = prepare(jobs, fields)
-    theirs = swap(theirs, 1)
-    far = []
-    for slot in range(slots):
-        blocks = prepare([[(slot, 2)], [(slot, 3)]], fields, sums)
-        far.append([swap(blocks[0], 2), swap(blocks[1], 3)])
-        if slot == 0:
-            near = merge(mine, theirs, slots, blocks[0])
+    size = 4 * planes
+    jobs = [[(slot, m) for slot in range(slots)] for m in range(TEAM)]
+    mine, theirs, sums = prepare(jobs[2:], fields)
+    across = merge_far(mine, swap(theirs, 1), slots, size)(sums)
+    far = [[swap(value, 2)] for value in across]
+    mine, theirs = prepare(jobs[:2], fields, sums)
+    near = merge_near(mine, swap(theirs, 1), slots, size)
     near_halo = along(near, True)
+
+    sums = across[0][2 * size] + far[0][0][2 * size]
+    stride = 1
+    while stride * TEAM < slabs:
+        radix = next(r for r in range(2, slabs) if slabs // (stride * TEAM) % r == 0)
+        sums = sum(from_teams(sums, stride, radix), sums)
+        stride *= radix
 
     pieces, faces = [], []
     for slot in range(slots):
         far_halo = [along(block, False) for block in far[slot]]
-        known = [mine, theirs, *far[0]] if slot == 0 else []
-        solved = solve(slot, near, far[slot], near_halo, far_halo, known, planes)
+        solved = solve(slot, near, far[slot], near_halo, far_halo, planes)
         pieces.append([solved[0]] + [swap(solved[m], m) for m in (1, 2, 3)])
         faces.append(solved[TEAM])
-        if slot == 0:
-            sums = [solved[TEAM + 1]]
-            stride = 1
-            for radix in radices:
-                held = sum(sums[1:], sums[0])
-                sums = [held] + from_teams(held, stride, radix)
-                stride *= radix
-
-    face, moments = weigh(sums, faces, depth_total * rows_y * columns, pieces[0][1:])
+
+    face, moments = weigh([sums], faces, depth_total * rows_y * columns, pieces[0][1:])
     heard = [sum((swap(face, m) for m in (2, 3, 1)), face)[None]]
     stride = 1
     for radix in radices:

time: 76.5 us -> 76.9 us (level)
  waiting for transfers between devices: 15.4 us -> 21.9 us
  starting transfers between devices: 37.6 us -> 32.3 us
    ppermute x5 -> x3, starting transfers between devices: 15 us -> 9.11 us  [along(): return lax.ppermute(value, 'gz', pairs)]
    ppermute x14 -> x13, waiting for transfers between devices: 12.1 us -> 15.8 us  [swap(): return lax.ppermute(value, 'gz', [(i, i ^ m) for i in range(slabs)])]
    ppermute x6 -> x5, waiting for transfers between devices: 3.3 us -> 6.17 us  [from_teams(): heard.append(lax.ppermute(value, 'gz', pairs))]
    ppermute x14 -> x13, starting transfers between devices: 12.3 us -> 13.8 us  [swap(): return lax.ppermute(value, 'gz', [(i, i ^ m) for i in range(slabs)])]
    ppermute x6 -> x5, starting transfers between devices: 10.4 us -> 9.3 us  [from_teams(): heard.append(lax.ppermute(value, 'gz', pairs))]
    pallas_call x3 -> x2, Pallas kernels: 4.99 us -> 3.96 us  [prepare(): pl.pallas_call(kernel, out_shape=[jax.ShapeDtypeStruct(shape, F32) for sh...]
  transfers between devices with their start and end apart: 25 -> 21, of which waited for: 9 -> 8; matrix products, arithmetic and copies ran while one was open for 1% -> 1% of each run, Pallas kernels for 23% -> 23%
where the time goes in v7:
time: 76.9 us; the launch traced here: 76.6 us
  starting transfers between devices  32.3 us (42%)
  waiting for transfers between devices  21.9 us (28%)
  Pallas kernels  21.1 us (27%)
  between operations  0.79 us (1%)
    ppermute x13, waiting for transfers between devices, swap(): return lax.ppermute(value, 'gz', [(i, i ^ m) for i in range(slabs)])  15.8 us
    pallas_call x2, Pallas kernels, solve(): pl.pallas_call(kernel, out_shape=[jax.ShapeDtypeStruct((2 * planes, half,...  14.5 us
    ppermute x13, starting transfers between devices, swap(): return lax.ppermute(value, 'gz', [(i, i ^ m) for i in range(slabs)])  13.8 us
    ppermute x5, starting transfers between devices, from_teams(): heard.append(lax.ppermute(value, 'gz', pairs))  9.3 us
    ppermute x3, starting transfers between devices, along(): return lax.ppermute(value, 'gz', pairs)  9.11 us
    ppermute x5, waiting for transfers between devices, from_teams(): heard.append(lax.ppermute(value, 'gz', pairs))  6.17 us
    pallas_call x2, Pallas kernels, prepare(): pl.pallas_call(kernel, out_shape=[jax.ShapeDtypeStruct(shape, F32) for sh...  3.96 us
  transfers between devices with their start and end apart: 21, of which 8 were waited for; matrix products, arithmetic and copies ran while one was open for 1% of the time, Pallas kernels for 23%

profile of v7, /device:TPU:0, one launch (start us, length us, event | category | flops | bytes accessed | tf_op | source)
XLA Modules:
  0.0 76.6 jit_solution(12113336523583090810)
XLA Ops:
  0.6 2.3 %prepare.2 = (f32[33,8,512]{2,1,0:T(8,128)S(1)}, f32[33,8,512]{2,1,0:T(8,128)S(1)}, f32[8,512]{1,0:T(8,128)S(1)}) custom-call(f32[8,8]{1,0:T(8,128)} %refs_1_.3, f32[8]{0:T(128)} %refs_2_.3, f32[8,4,16,512]{3,2,1,0:T(8,128)} %refs_3_.3, f32[4,16,512]{2,1,0:T(8,128)} %refs_4_.4, s32[8,4,16,512]{3,2,1,0:T(8,128)} %refs_5_.2), custom_call_target="tpu_custom_call" | custom-call | bytes 4194304 | tf_op jit(solution)/shard_map/prepare/pallas_call | solution.py:155
  2.9 0.5 collective-permute-start.2
  3.5 1.7 %prepare.3 = (f32[32,8,512]{2,1,0:T(8,128)S(1)}, f32[32,8,512]{2,1,0:T(8,128)S(1)}) custom-call(f32[8,512]{1,0:T(8,128)S(1)} %get-tuple-element.22.refs_0_.sums_ref, f32[8,8]{1,0:T(8,128)} %refs_1_.3, f32[8]{0:T(128)} %refs_2_.3, f32[8,4,16,512]{3,2,1,0:T(8,128)} %refs_3_.3, f32[4,16,512]{2,1,0:T(8,128)} %refs_4_.4, s32[8,4,16,512]{3,2,1,0:T(8,128)} %refs_5_.2), custom_call_target="tpu_custom_call" | custom-call | bytes 4194304 | tf_op jit(solution)/shard_map/prepare/pallas_call | solution.py:155
  5.1 0.1 collective-permute-start
  5.2 0.0 collective-permute-done.2.theirs_ref
  5.2 0.1 merge_far.1
  5.3 3.0 %collective-permute-start.3 = (f32[33,8,512]{2,1,0:T(8,128)S(1)}, f32[33,8,512]{2,1,0:T(8,128)S(1)}, u32[]{:S(2)}, u32[]{:S(2)}) collective-permute-start(f32[33,8,512]{2,1,0:T(8,128)S(1)} %get-tuple-element.27), channel_id=1, source_target_pairs={{0,2},{1,3},{2,0},{3,1},{4,6},{5,7},{6,4},{7,5},{8,10},{9,11},{10,... | collective-permute-start | bytes 1622024 | tf_op jit(solution)/shard_map/ppermute | solution.py:518
  8.3 0.0 collective-permute-done.theirs_ref
  8.3 0.1 merge_near.1.refs_0_
  8.4 1.3 %collective-permute-start.1 = (f32[2,2,16,8,512]{4,3,2,1,0:T(8,128)S(1)}, f32[2,2,16,8,512]{4,3,2,1,0:T(8,128)S(1)}, u32[]{:S(2)}, u32[]{:S(2)}) collective-permute-start(f32[2,2,16,8,512]{4,3,2,1,0:T(8,128)S(1)} %merge_near.1.refs_0_), channel_id=1, source_target_pairs={{2,6},{3,7},{4,0},{5,1},{6,10},{7,11},{8,4},{9,5},{10,14},{11,15},... | collective-permute-start | bytes 3145736 | tf_op jit(solution)/shard_map/ppermute | solution.py:527
  9.7 3.7 %collective-permute-start.8 = (f32[32,8,512]{2,1,0:T(8,128)S(1)}, f32[32,8,512]{2,1,0:T(8,128)S(1)}, u32[]{:S(2)}, u32[]{:S(2)}) collective-permute-start(f32[32,8,512]{2,1,0:T(8,128)S(1)} %get-tuple-element.32), channel_id=1, source_target_pairs={{0,2},{1,3},{2,0},{3,1},{4,6},{5,7},{6,4},{7,5},{8,10},{9,11},{10,... | collective-permute-start | bytes 1572872 | tf_op jit(solution)/shard_map/ppermute | solution.py:518
  13.4 8.0 %collective-permute-done.3.refs_2_ = f32[33,8,512]{2,1,0:T(8,128)S(1)} collective-permute-done((f32[33,8,512]{2,1,0:T(8,128)S(1)}, f32[33,8,512]{2,1,0:T(8,128)S(1)}, u32[]{:S(2)}, u32[]{:S(2)}) %collective-permute-start.3) | collective-permute-done | bytes 540704 | tf_op jit(solution)/shard_map/ppermute | solution.py:518
  21.4 4.1 %collective-permute-start.4 = (f32[33,8,512]{2,1,0:T(8,128)S(1)}, f32[33,8,512]{2,1,0:T(8,128)S(1)}, u32[]{:S(2)}, u32[]{:S(2)}) collective-permute-start(f32[33,8,512]{2,1,0:T(8,128)S(1)} %collective-permute-done.3.refs_2_), channel_id=1, source_target_pairs={{0,4},{1,5},{4,8},{5,9},{6,2},{7,3},{8,12},{9,13},{10,6},{11,7},{1... | collective-permute-start | bytes 1622024 | tf_op jit(solution)/shard_map/ppermute | solution.py:527
  25.5 6.5 %collective-permute-done.8.refs_2_ = f32[32,8,512]{2,1,0:T(8,128)S(1)} collective-permute-done((f32[32,8,512]{2,1,0:T(8,128)S(1)}, f32[32,8,512]{2,1,0:T(8,128)S(1)}, u32[]{:S(2)}, u32[]{:S(2)}) %collective-permute-start.8) | collective-permute-done | bytes 524320 | tf_op jit(solution)/shard_map/ppermute | solution.py:518
  32.0 3.8 %collective-permute-start.9 = (f32[32,8,512]{2,1,0:T(8,128)S(1)}, f32[32,8,512]{2,1,0:T(8,128)S(1)}, u32[]{:S(2)}, u32[]{:S(2)}) collective-permute-start(f32[32,8,512]{2,1,0:T(8,128)S(1)} %collective-permute-done.8.refs_2_), channel_id=1, source_target_pairs={{0,4},{1,5},{4,8},{5,9},{6,2},{7,3},{8,12},{9,13},{10,6},{11,7},{1... | collective-permute-start | bytes 1572872 | tf_op jit(solution)/shard_map/ppermute | solution.py:527
  35.8 0.0 collective-permute-done.1.refs_1_
  35.8 0.0 collective-permute-done.4.refs_3_
  35.8 7.2 %solve0.1 = (f32[8,8,512]{2,1,0:T(8,128)S(1)}, f32[8,8,512]{2,1,0:T(8,128)S(1)}, f32[8,8,512]{2,1,0:T(8,128)S(1)}, f32[8,8,512]{2,1,0:T(8,128)S(1)}, f32[16,512]{1,0:T(8,128)S(1)}) custom-call(f32[2,2,16,8,512]{4,3,2,1,0:T(8,128)S(1)} %merge_near.1.refs_0_, f32[2,2,16,8,512]{4,3,2,1,0:T(8,128)S(1)} %collective-permute-done.1.refs_1_, ...), custom_call_target="tpu_custom_call" | custom-call | bytes 23068672 | tf_op jit(solution)/shard_map/solve0/pallas_call | solution.py:366
  43.1 0.1 collective-permute-start.5
  43.1 2.3 %collective-permute-start.6 = (f32[8,8,512]{2,1,0:T(8,128)S(1)}, f32[8,8,512]{2,1,0:T(8,128)S(1)}, u32[]{:S(2)}, u32[]{:S(2)}) collective-permute-start(f32[8,8,512]{2,1,0:T(8,128)S(1)} %get-tuple-element.30), channel_id=1, source_target_pairs={{0,2},{1,3},{2,0},{3,1},{4,6},{5,7},{6,4},{7,5},{8,10},{9,11},{10,... | collective-permute-start | bytes 393224 | tf_op jit(solution)/shard_map/ppermute | solution.py:518
  45.4 0.1 collective-permute-start.7
  45.5 1.8 %collective-permute-start.13 = (f32[8,512]{1,0:T(8,128)S(1)}, f32[8,512]{1,0:T(8,128)S(1)}, u32[]{:S(2)}, u32[]{:S(2)}) collective-permute-start(f32[8,512]{1,0:T(8,128)S(1)} %fusion), channel_id=1, source_target_pairs={{4,0},{5,1},{6,2},{7,3},{0,4},{1,5},{2,6},{3,7},{12,8},{13,9},{14,... | collective-permute-start | bytes 49160 | tf_op jit(solution)/shard_map/ppermute | solution.py:536
  47.3 1.9 %collective-permute-done.13 = f32[8,512]{1,0:T(8,128)S(1)} collective-permute-done((f32[8,512]{1,0:T(8,128)S(1)}, f32[8,512]{1,0:T(8,128)S(1)}, u32[]{:S(2)}, u32[]{:S(2)}) %collective-permute-start.13) | collective-permute-done | bytes 16416 | tf_op jit(solution)/shard_map/ppermute | solution.py:536
  49.3 2.8 %collective-permute-start.14 = (f32[8,512]{1,0:T(8,128)S(1)}, f32[8,512]{1,0:T(8,128)S(1)}, u32[]{:S(2)}, u32[]{:S(2)}) collective-permute-start(f32[8,512]{1,0:T(8,128)S(1)} %add.23), channel_id=1, source_target_pairs={{8,0},{9,1},{10,2},{11,3},{12,4},{13,5},{14,6},{15,7},{0,8},{1,9},... | collective-permute-start | bytes 49160 | tf_op jit(solution)/shard_map/ppermute | solution.py:536
  52.1 1.8 %collective-permute-done.14 = f32[8,512]{1,0:T(8,128)S(1)} collective-permute-done((f32[8,512]{1,0:T(8,128)S(1)}, f32[8,512]{1,0:T(8,128)S(1)}, u32[]{:S(2)}, u32[]{:S(2)}) %collective-permute-start.14) | collective-permute-done | bytes 16416 | tf_op jit(solution)/shard_map/ppermute | solution.py:536
  53.9 0.0 collective-permute-done.9.refs_3_
  53.9 7.2 %solve1.1 = (f32[8,8,512]{2,1,0:T(8,128)S(1)}, f32[8,8,512]{2,1,0:T(8,128)S(1)}, f32[8,8,512]{2,1,0:T(8,128)S(1)}, f32[8,8,512]{2,1,0:T(8,128)S(1)}, f32[16,512]{1,0:T(8,128)S(1)}) custom-call(f32[2,2,16,8,512]{4,3,2,1,0:T(8,128)S(1)} %merge_near.1.refs_0_, f32[2,2,16,8,512]{4,3,2,1,0:T(8,128)S(1)} %collective-permute-done.1.refs_1_, ...), custom_call_target="tpu_custom_call" | custom-call | bytes 23068672 | tf_op jit(solution)/shard_map/solve1/pallas_call | solution.py:366
  61.1 0.0 collective-permute-done.5.refs_1_.refs_3_
  61.2 0.0 collective-permute-done.7.refs_3_.refs_5_
  61.2 1.8 %collective-permute-start.15 = (f32[16,512]{1,0:T(8,128)S(1)}, f32[16,512]{1,0:T(8,128)S(1)}, u32[]{:S(2)}, u32[]{:S(2)}) collective-permute-start(f32[16,512]{1,0:T(8,128)S(1)} %get-tuple-element.39), channel_id=1, source_target_pairs={{0,2},{1,3},{2,0},{3,1},{4,6},{5,7},{6,4},{7,5},{8,10},{9,11},{10,... | collective-permute-start | bytes 98312 | tf_op jit(solution)/shard_map/ppermute | solution.py:518
  63.0 0.4 collective-permute-start.17
  63.4 0.1 collective-permute-start.10
  63.5 1.6 %collective-permute-start.11 = (f32[8,8,512]{2,1,0:T(8,128)S(1)}, f32[8,8,512]{2,1,0:T(8,128)S(1)}, u32[]{:S(2)}, u32[]{:S(2)}) collective-permute-start(f32[8,8,512]{2,1,0:T(8,128)S(1)} %get-tuple-element.35), channel_id=1, source_target_pairs={{0,2},{1,3},{2,0},{3,1},{4,6},{5,7},{6,4},{7,5},{8,10},{9,11},{10,... | collective-permute-start | bytes 393224 | tf_op jit(solution)/shard_map/ppermute | solution.py:518
  65.1 0.0 collective-permute-done.15
  65.2 0.1 collective-permute-start.12
  65.3 1.0 %collective-permute-done.16 = f32[16,512]{1,0:T(8,128)S(1)} collective-permute-done((f32[16,512]{1,0:T(8,128)S(1)}, f32[16,512]{1,0:T(8,128)S(1)}, u32[]{:S(2)}, u32[]{:S(2)}) %collective-permute-start.16) | collective-permute-done | bytes 32800 | tf_op jit(solution)/shard_map/ppermute | solution.py:518
  66.3 0.0 collective-permute-done.17
  66.4 3.1 %collective-permute-start.18 = (f32[1,16,512]{2,1,0:T(8,128)S(1)}, f32[1,16,512]{2,1,0:T(8,128)S(1)}, u32[]{:S(2)}, u32[]{:S(2)}) collective-permute-start(f32[1,16,512]{2,1,0:T(8,128)S(1)} %add_bitcast_fusion.refs_0_), channel_id=1, source_target_pairs={{4,0},{5,1},{6,2},{7,3},{8,4},{9,5},{10,6},{11,7},{12,8},{13,9},{1... | collective-permute-start | bytes 98312 | tf_op jit(solution)/shard_map/ppermute | solution.py:536
  69.5 0.0 collective-permute-start.19
  69.5 0.0 collective-permute-done.10.refs_5_
  69.5 1.6 %collective-permute-start.20 = (f32[1,16,512]{2,1,0:T(8,128)S(1)}, f32[1,16,512]{2,1,0:T(8,128)S(1)}, u32[]{:S(2)}, u32[]{:S(2)}) collective-permute-start(f32[1,16,512]{2,1,0:T(8,128)S(1)} %add_bitcast_fusion.refs_0_), channel_id=1, source_target_pairs={{12,0},{13,1},{14,2},{15,3},{0,4},{1,5},{2,6},{3,7},{4,8},{5,9},{6... | collective-permute-start | bytes 98312 | tf_op jit(solution)/shard_map/ppermute | solution.py:536
  71.0 0.5 slice_bitcast_fusion
  71.5 0.0 collective-permute-done.11.refs_6_
  71.5 0.1 collective-permute-done.12.refs_7_
  71.7 1.0 %gather_adjoint.1 = f32[8,4,16,512]{3,2,1,0:T(8,128)} custom-call(f32[8,8,512]{2,1,0:T(8,128)S(1)} %get-tuple-element.28.refs_0_, f32[8,8,512]{2,1,0:T(8,128)S(1)} %collective-permute-done.5.refs_1_.refs_3_, f32[8,8,512]{2,1,0:T(8,128)S(1)} %collective-permute-done.6.refs_2_.refs_4_, f32[8,8,512]{2,1,0:T(8,128)S(1)} %collective-permute-done.7.refs_3_.refs_5_, ...), custom_call_target="tpu_custom_call" | custom-call | bytes 4194304 | tf_op jit(solution)/shard_map/gather_adjoint/pallas_call | solution.py:447
  72.7 1.5 %collective-permute-done.19.refs_2_ = f32[1,16,512]{2,1,0:T(8,128)S(1)} collective-permute-done((f32[1,16,512]{2,1,0:T(8,128)S(1)}, f32[1,16,512]{2,1,0:T(8,128)S(1)}, u32[]{:S(2)}, u32[]{:S(2)}) %collective-permute-start.19) | collective-permute-done | bytes 32800 | tf_op jit(solution)/shard_map/ppermute | solution.py:536
  74.3 0.9 %collective-permute-done.20.refs_3_ = f32[1,16,512]{2,1,0:T(8,128)S(1)} collective-permute-done((f32[1,16,512]{2,1,0:T(8,128)S(1)}, f32[1,16,512]{2,1,0:T(8,128)S(1)}, u32[]{:S(2)}, u32[]{:S(2)}) %collective-permute-start.20) | collective-permute-done | bytes 32800 | tf_op jit(solution)/shard_map/ppermute | solution.py:536
  75.2 1.4 %control.1 = f32[32,512]{1,0:T(8,128)} custom-call(f32[1,16,512]{2,1,0:T(8,128)S(1)} %add_bitcast_fusion.refs_0_, f32[1,16,512]{2,1,0:T(8,128)S(1)} %collective-permute-done.18.refs_1_, f32[1,16,512]{2,1,0:T(8,128)S(1)} %collective-permute-done.19.refs_2_, f32[1,16,512]{2,1,0:T(8,128)S(1)} %collective-permute-done.20.refs_3_, f32[16,32,64]{2,1,0:T(8,128)S(1)} %copy-done.1, ...), custom_call_target="tpu_custom_call" | custom-call | tf_op jit(solution)/shard_map/control/pallas_call | solution.py:490
  (12 shorter events, 0.1 us)
Async XLA Ops:
  2.9 2.3 %collective-permute-start.2 = (f32[33,8,512]{2,1,0:T(8,128)S(1)}, f32[33,8,512]{2,1,0:T(8,128)S(1)}, u32[]{:S(2)}, u32[]{:S(2)}) collective-permute-start(f32[33,8,512]{2,1,0:T(8,128)S(1)} %get-tuple-element.26), channel_id=1, source_target_pairs={{0,1},{1,0},{2,3},{3,2},{4,5},{5,4},{6,7},{7,6},{8,9},{9,8},{10,11... | collective-permute-start | bytes 1622024 | tf_op jit(solution)/shard_map/ppermute | solution.py:518
  5.1 3.2 %collective-permute-start = (f32[32,8,512]{2,1,0:T(8,128)S(1)}, f32[32,8,512]{2,1,0:T(8,128)S(1)}, u32[]{:S(2)}, u32[]{:S(2)}) collective-permute-start(f32[32,8,512]{2,1,0:T(8,128)S(1)} %get-tuple-element.24), channel_id=1, source_target_pairs={{0,1},{1,0},{2,3},{3,2},{4,5},{5,4},{6,7},{7,6},{8,9},{9,8},{10,11... | collective-permute-start | bytes 1572872 | tf_op jit(solution)/shard_map/ppermute | solution.py:518
  5.3 16.1 %collective-permute-start.3 = (f32[33,8,512]{2,1,0:T(8,128)S(1)}, f32[33,8,512]{2,1,0:T(8,128)S(1)}, u32[]{:S(2)}, u32[]{:S(2)}) collective-permute-start(f32[33,8,512]{2,1,0:T(8,128)S(1)} %get-tuple-element.27), channel_id=1, source_target_pairs={{0,2},{1,3},{2,0},{3,1},{4,6},{5,7},{6,4},{7,5},{8,10},{9,11},{10,... | collective-permute-start | bytes 1622024 | tf_op jit(solution)/shard_map/ppermute | solution.py:518
  8.4 27.4 %collective-permute-start.1 = (f32[2,2,16,8,512]{4,3,2,1,0:T(8,128)S(1)}, f32[2,2,16,8,512]{4,3,2,1,0:T(8,128)S(1)}, u32[]{:S(2)}, u32[]{:S(2)}) collective-permute-start(f32[2,2,16,8,512]{4,3,2,1,0:T(8,128)S(1)} %merge_near.1.refs_0_), channel_id=1, source_target_pairs={{2,6},{3,7},{4,0},{5,1},{6,10},{7,11},{8,4},{9,5},{10,14},{11,15},... | collective-permute-start | bytes 3145736 | tf_op jit(solution)/shard_map/ppermute | solution.py:527
  9.7 22.3 %collective-permute-start.8 = (f32[32,8,512]{2,1,0:T(8,128)S(1)}, f32[32,8,512]{2,1,0:T(8,128)S(1)}, u32[]{:S(2)}, u32[]{:S(2)}) collective-permute-start(f32[32,8,512]{2,1,0:T(8,128)S(1)} %get-tuple-element.32), channel_id=1, source_target_pairs={{0,2},{1,3},{2,0},{3,1},{4,6},{5,7},{6,4},{7,5},{8,10},{9,11},{10,... | collective-permute-start | bytes 1572872 | tf_op jit(solution)/shard_map/ppermute | solution.py:518
  21.4 14.4 %collective-permute-start.4 = (f32[33,8,512]{2,1,0:T(8,128)S(1)}, f32[33,8,512]{2,1,0:T(8,128)S(1)}, u32[]{:S(2)}, u32[]{:S(2)}) collective-permute-start(f32[33,8,512]{2,1,0:T(8,128)S(1)} %collective-permute-done.3.refs_2_), channel_id=1, source_target_pairs={{0,4},{1,5},{4,8},{5,9},{6,2},{7,3},{8,12},{9,13},{10,6},{11,7},{1... | collective-permute-start | bytes 1622024 | tf_op jit(solution)/shard_map/ppermute | solution.py:527
  32.0 21.9 %collective-permute-start.9 = (f32[32,8,512]{2,1,0:T(8,128)S(1)}, f32[32,8,512]{2,1,0:T(8,128)S(1)}, u32[]{:S(2)}, u32[]{:S(2)}) collective-permute-start(f32[32,8,512]{2,1,0:T(8,128)S(1)} %collective-permute-done.8.refs_2_), channel_id=1, source_target_pairs={{0,4},{1,5},{4,8},{5,9},{6,2},{7,3},{8,12},{9,13},{10,6},{11,7},{1... | collective-permute-start | bytes 1572872 | tf_op jit(solution)/shard_map/ppermute | solution.py:527
  43.1 18.1 %collective-permute-start.5 = (f32[8,8,512]{2,1,0:T(8,128)S(1)}, f32[8,8,512]{2,1,0:T(8,128)S(1)}, u32[]{:S(2)}, u32[]{:S(2)}) collective-permute-start(f32[8,8,512]{2,1,0:T(8,128)S(1)} %get-tuple-element.29), channel_id=1, source_target_pairs={{0,1},{1,0},{2,3},{3,2},{4,5},{5,4},{6,7},{7,6},{8,9},{9,8},{10,11... | collective-permute-start | bytes 393224 | tf_op jit(solution)/shard_map/ppermute | solution.py:518
  43.1 18.0 %collective-permute-start.6 = (f32[8,8,512]{2,1,0:T(8,128)S(1)}, f32[8,8,512]{2,1,0:T(8,128)S(1)}, u32[]{:S(2)}, u32[]{:S(2)}) collective-permute-start(f32[8,8,512]{2,1,0:T(8,128)S(1)} %get-tuple-element.30), channel_id=1, source_target_pairs={{0,2},{1,3},{2,0},{3,1},{4,6},{5,7},{6,4},{7,5},{8,10},{9,11},{10,... | collective-permute-start | bytes 393224 | tf_op jit(solution)/shard_map/ppermute | solution.py:518
  45.4 15.7 %collective-permute-start.7 = (f32[8,8,512]{2,1,0:T(8,128)S(1)}, f32[8,8,512]{2,1,0:T(8,128)S(1)}, u32[]{:S(2)}, u32[]{:S(2)}) collective-permute-start(f32[8,8,512]{2,1,0:T(8,128)S(1)} %get-tuple-element.31), channel_id=1, source_target_pairs={{0,3},{1,2},{2,1},{3,0},{4,7},{5,6},{6,5},{7,4},{8,11},{9,10},{10,... | collective-permute-start | bytes 393224 | tf_op jit(solution)/shard_map/ppermute | solution.py:518
  45.5 3.7 %collective-permute-start.13 = (f32[8,512]{1,0:T(8,128)S(1)}, f32[8,512]{1,0:T(8,128)S(1)}, u32[]{:S(2)}, u32[]{:S(2)}) collective-permute-start(f32[8,512]{1,0:T(8,128)S(1)} %fusion), channel_id=1, source_target_pairs={{4,0},{5,1},{6,2},{7,3},{0,4},{1,5},{2,6},{3,7},{12,8},{13,9},{14,... | collective-permute-start | bytes 49160 | tf_op jit(solution)/shard_map/ppermute | solution.py:536
  49.3 4.6 %collective-permute-start.14 = (f32[8,512]{1,0:T(8,128)S(1)}, f32[8,512]{1,0:T(8,128)S(1)}, u32[]{:S(2)}, u32[]{:S(2)}) collective-permute-start(f32[8,512]{1,0:T(8,128)S(1)} %add.23), channel_id=1, source_target_pairs={{8,0},{9,1},{10,2},{11,3},{12,4},{13,5},{14,6},{15,7},{0,8},{1,9},... | collective-permute-start | bytes 49160 | tf_op jit(solution)/shard_map/ppermute | solution.py:536
  61.2 4.0 %collective-permute-start.15 = (f32[16,512]{1,0:T(8,128)S(1)}, f32[16,512]{1,0:T(8,128)S(1)}, u32[]{:S(2)}, u32[]{:S(2)}) collective-permute-start(f32[16,512]{1,0:T(8,128)S(1)} %get-tuple-element.39), channel_id=1, source_target_pairs={{0,2},{1,3},{2,0},{3,1},{4,6},{5,7},{6,4},{7,5},{8,10},{9,11},{10,... | collective-permute-start | bytes 98312 | tf_op jit(solution)/shard_map/ppermute | solution.py:518
  63.0 3.3 %collective-permute-start.16 = (f32[16,512]{1,0:T(8,128)S(1)}, f32[16,512]{1,0:T(8,128)S(1)}, u32[]{:S(2)}, u32[]{:S(2)}) collective-permute-start(f32[16,512]{1,0:T(8,128)S(1)} %get-tuple-element.39), channel_id=1, source_target_pairs={{0,3},{1,2},{2,1},{3,0},{4,7},{5,6},{6,5},{7,4},{8,11},{9,10},{10,... | collective-permute-start | bytes 98312 | tf_op jit(solution)/shard_map/ppermute | solution.py:518
  63.0 3.3 %collective-permute-start.17 = (f32[16,512]{1,0:T(8,128)S(1)}, f32[16,512]{1,0:T(8,128)S(1)}, u32[]{:S(2)}, u32[]{:S(2)}) collective-permute-start(f32[16,512]{1,0:T(8,128)S(1)} %get-tuple-element.39), channel_id=1, source_target_pairs={{0,1},{1,0},{2,3},{3,2},{4,5},{5,4},{6,7},{7,6},{8,9},{9,8},{10,11... | collective-permute-start | bytes 98312 | tf_op jit(solution)/shard_map/ppermute | solution.py:518
  63.4 6.0 %collective-permute-start.10 = (f32[8,8,512]{2,1,0:T(8,128)S(1)}, f32[8,8,512]{2,1,0:T(8,128)S(1)}, u32[]{:S(2)}, u32[]{:S(2)}) collective-permute-start(f32[8,8,512]{2,1,0:T(8,128)S(1)} %get-tuple-element.34), channel_id=1, source_target_pairs={{0,1},{1,0},{2,3},{3,2},{4,5},{5,4},{6,7},{7,6},{8,9},{9,8},{10,11... | collective-permute-start | bytes 393224 | tf_op jit(solution)/shard_map/ppermute | solution.py:518
  63.5 8.0 %collective-permute-start.11 = (f32[8,8,512]{2,1,0:T(8,128)S(1)}, f32[8,8,512]{2,1,0:T(8,128)S(1)}, u32[]{:S(2)}, u32[]{:S(2)}) collective-permute-start(f32[8,8,512]{2,1,0:T(8,128)S(1)} %get-tuple-element.35), channel_id=1, source_target_pairs={{0,2},{1,3},{2,0},{3,1},{4,6},{5,7},{6,4},{7,5},{8,10},{9,11},{10,... | collective-permute-start | bytes 393224 | tf_op jit(solution)/shard_map/ppermute | solution.py:518
  65.2 6.5 %collective-permute-start.12 = (f32[8,8,512]{2,1,0:T(8,128)S(1)}, f32[8,8,512]{2,1,0:T(8,128)S(1)}, u32[]{:S(2)}, u32[]{:S(2)}) collective-permute-start(f32[8,8,512]{2,1,0:T(8,128)S(1)} %get-tuple-element.36), channel_id=1, source_target_pairs={{0,3},{1,2},{2,1},{3,0},{4,7},{5,6},{6,5},{7,4},{8,11},{9,10},{10,... | collective-permute-start | bytes 393224 | tf_op jit(solution)/shard_map/ppermute | solution.py:518
  66.4 6.4 %collective-permute-start.18 = (f32[1,16,512]{2,1,0:T(8,128)S(1)}, f32[1,16,512]{2,1,0:T(8,128)S(1)}, u32[]{:S(2)}, u32[]{:S(2)}) collective-permute-start(f32[1,16,512]{2,1,0:T(8,128)S(1)} %add_bitcast_fusion.refs_0_), channel_id=1, source_target_pairs={{4,0},{5,1},{6,2},{7,3},{8,4},{9,5},{10,6},{11,7},{12,8},{13,9},{1... | collective-permute-start | bytes 98312 | tf_op jit(solution)/shard_map/ppermute | solution.py:536
  69.5 4.8 %collective-permute-start.19 = (f32[1,16,512]{2,1,0:T(8,128)S(1)}, f32[1,16,512]{2,1,0:T(8,128)S(1)}, u32[]{:S(2)}, u32[]{:S(2)}) collective-permute-start(f32[1,16,512]{2,1,0:T(8,128)S(1)} %add_bitcast_fusion.refs_0_), channel_id=1, source_target_pairs={{8,0},{9,1},{10,2},{11,3},{12,4},{13,5},{14,6},{15,7},{0,8},{1,9},... | collective-permute-start | bytes 98312 | tf_op jit(solution)/shard_map/ppermute | solution.py:536
  69.5 5.7 %collective-permute-start.20 = (f32[1,16,512]{2,1,0:T(8,128)S(1)}, f32[1,16,512]{2,1,0:T(8,128)S(1)}, u32[]{:S(2)}, u32[]{:S(2)}) collective-permute-start(f32[1,16,512]{2,1,0:T(8,128)S(1)} %add_bitcast_fusion.refs_0_), channel_id=1, source_target_pairs={{12,0},{13,1},{14,2},{15,3},{0,4},{1,5},{2,6},{3,7},{4,8},{5,9},{6... | collective-permute-start | bytes 98312 | tf_op jit(solution)/shard_map/ppermute | solution.py:536
  71.7 3.5 %copy-start = (f32[512,512]{1,0:T(8,128)S(1)}, f32[512,512]{1,0:T(8,128)}, u32[]{:S(2)}) copy-start(f32[512,512]{1,0:T(8,128)} %constant.5.clone.refs_5_) | copy-start | bytes 3145732
  71.7 3.5 %copy-start.1 = (f32[16,32,64]{2,1,0:T(8,128)S(1)}, f32[16,32,64]{2,1,0:T(8,128)}, u32[]{:S(2)}) copy-start(f32[16,32,64]{2,1,0:T(8,128)} %constant.4.clone.refs_4_) | copy-start | bytes 393220

commit v8 on v7

--- a/solution.py
+++ b/solution.py
@@ -376,17 +376,30 @@
     )(*inputs)
 
 
+def hold(value, after):
+    def kernel(value_ref, _, out_ref):
+        for n in range(value.shape[0]):
+            out_ref[n] = value_ref[n]
+
+    vmem = pl.BlockSpec(memory_space=pltpu.VMEM)
+    return pl.pallas_call(
+        kernel,
+        out_shape=jax.ShapeDtypeStruct(value.shape, F32),
+        in_specs=[vmem, pl.BlockSpec(memory_space=pl.ANY)],
+        out_specs=vmem,
+        compiler_params=pltpu.CompilerParams(vmem_limit_bytes=2 * MIB),
+        name="hold",
+    )(value, after)
+
+
 def weigh(sums, faces, cells, after):
     slots = len(faces)
-    samples, columns = sums[0].shape
-
-    def kernel(*refs):
-        sum_refs, refs = refs[: len(sums)], refs[len(sums) :]
+    teams, samples, columns = sums.shape
+
+    def kernel(sums_ref, *refs):
         face_refs, (out_ref, moments_ref, weights) = refs[:slots], refs[slots + len(after) :]
         place = team_place()
-        summed = sum_refs[0][...]
-        for ref in sum_refs[1:]:
-            summed = summed + ref[...]
+        summed = jnp.sum(sums_ref[...], axis=0)
         misfit = summed * (1.0 / (2.0 * cells))
         mean = jnp.sum(misfit, axis=0, keepdims=True) * (1.0 / samples)
         deviation = misfit - mean
@@ -406,13 +419,13 @@
             jax.ShapeDtypeStruct(faces[0].shape, F32),
             jax.ShapeDtypeStruct((1, columns), F32),
         ],
-        in_specs=[vmem] * (len(sums) + slots)
+        in_specs=[vmem] * (1 + slots)
         + [pl.BlockSpec(memory_space=pl.ANY)] * len(after),
         out_specs=[vmem, vmem],
         scratch_shapes=[pltpu.VMEM((samples, columns), F32)],
         compiler_params=pltpu.CompilerParams(vmem_limit_bytes=2 * MIB),
         name="weigh",
-    )(*sums, *faces, *after)
+    )(sums, *faces, *after)
 
 
 def gather_adjoint(pieces, planes):
@@ -460,25 +473,13 @@
     )(*[piece for group in pieces for piece in group])
 
 
-def control(faces, radices, basis_z, basis_x):
-    slabs, own_count, depth_total = basis_z.shape
-    own, columns = faces[0].shape[1:]
-    teams = depth_total // own
-
-    def kernel(*refs):
-        parts, (z_ref, x_ref, out_ref, whole) = refs[: len(faces)], refs[len(faces) :]
-        rank = lax.axis_index("gz")
-        team = rank // TEAM
-        for n in range(teams):
-            at, left, stride = 0, n, 1
-            for radix in radices:
-                digit = lax.rem(team // stride + left % radix, radix)
-                at, left, stride = at + digit * stride, left // radix, stride * radix
-            inner = teams // len(faces)
-            whole[at] = parts[n // inner][n % inner]
+def control(faces, basis_z, basis_x):
+    own_count = basis_z.shape[1]
+
+    def kernel(face_ref, z_ref, x_ref, out_ref):
         along_z = jnp.dot(
-            z_ref[rank],
-            whole[...].reshape(depth_total, columns),
+            z_ref[lax.axis_index("gz")],
+            face_ref[...],
             precision=lax.Precision.HIGHEST,
             preferred_element_type=F32,
         )
@@ -490,21 +491,11 @@
     return pl.pallas_call(
         kernel,
         out_shape=jax.ShapeDtypeStruct((own_count, basis_x.shape[1]), F32),
-        in_specs=[vmem] * (len(faces) + 2),
+        in_specs=[vmem] * 3,
         out_specs=vmem,
-        scratch_shapes=[pltpu.VMEM((teams, own, columns), F32)],
         compiler_params=pltpu.CompilerParams(vmem_limit_bytes=8 * MIB),
         name="control",
-    )(*faces, basis_z, basis_x)
-
-
-def radices_of(teams):
-    radices = []
-    while teams > 1:
-        radix = next(r for r in (4, 2, 3, *range(5, teams + 1)) if teams % r == 0)
-        radices.append(radix)
-        teams //= radix
-    return radices
+    )(faces, basis_z, basis_x)
 
 
 def on_device(state, target, rock_type, log_table, obs_scale):
@@ -512,7 +503,6 @@
     slabs = lax.axis_size("gz")
     slots = samples // TEAM
     depth_total = planes * slabs
-    radices = radices_of(slabs // TEAM)
 
     def swap(value, m):
         return lax.ppermute(value, "gz", [(i, i ^ m) for i in range(slabs)])
@@ -526,15 +516,17 @@
                 pairs.append((i, to))
         return lax.ppermute(value, "gz", pairs)
 
-    def from_teams(value, stride, radix):
-        heard = []
-        for k in range(1, radix):
-            pairs = []
-            for i in range(slabs):
-                digit = i // (TEAM * stride) % radix
-                pairs.append((i + ((digit + k) % radix - digit) * stride * TEAM, i))
-            heard.append(lax.ppermute(value, "gz", pairs))
-        return heard
+    def of_teams(value):
+        columns_of_teams = [list(range(place, slabs, TEAM)) for place in range(TEAM)]
+        repeated = jnp.broadcast_to(value[None], (slabs // TEAM,) + value.shape)
+        return lax.all_to_all(
+            repeated,
+            "gz",
+            split_axis=0,
+            concat_axis=0,
+            axis_index_groups=columns_of_teams,
+            tiled=True,
+        )
 
     fields = [
         pltpu.with_memory_space_constraint(field, pltpu.HBM)
@@ -550,11 +542,8 @@
     near_halo = along(near, True)
 
     sums = across[0][2 * size] + far[0][0][2 * size]
-    stride = 1
-    while stride * TEAM < slabs:
-        radix = next(r for r in range(2, slabs) if slabs // (stride * TEAM) % r == 0)
-        sums = sum(from_teams(sums, stride, radix), sums)
-        stride *= radix
+    sums = of_teams(sums)
+    far[1:] = [[hold(value, sums) for value in values] for values in far[1:]]
 
     pieces, faces = [], []
     for slot in range(slots):
@@ -563,18 +552,12 @@
         pieces.append([solved[0]] + [swap(solved[m], m) for m in (1, 2, 3)])
         faces.append(solved[TEAM])
 
-    face, moments = weigh([sums], faces, depth_total * rows_y * columns, pieces[0][1:])
-    heard = [sum((swap(face, m) for m in (2, 3, 1)), face)[None]]
-    stride = 1
-    for radix in radices:
-        held = heard[0] if len(heard) == 1 else jnp.concatenate(heard)
-        heard = [held] + from_teams(held, stride, radix)
-        stride *= radix
+    face, moments = weigh(sums, faces, depth_total * rows_y * columns, pieces[0][1:])
+    heard = of_teams(sum((swap(face, m) for m in (2, 3, 1)), face))
     adjoint = gather_adjoint(pieces, planes)
     own_count = MA // slabs
     gradient = control(
-        heard,
-        radices,
+        heard.reshape(depth_total, columns),
         jnp.asarray(cosine_basis(depth_total, MA).T.reshape(slabs, own_count, depth_total)),
         jnp.asarray(cosine_basis(columns, MB)),
     )

time: 76.9 us -> 78.5 us (1.021)
  starting transfers between devices: 32.3 us -> 28.5 us
  Pallas kernels: 21.1 us -> 23.7 us
  waiting for transfers between devices: 21.9 us -> 23.3 us
  local copies, waits for them, and re-layouts: 0.52 us -> 1.8 us
    all_to_all x0 -> x2, waiting for transfers between devices: none -> 9.72 us  [of_teams(): lax.all_to_all(repeated, 'gz', split_axis=0, concat_axis=0, axis_index_gr...]
    ppermute x5 -> x0, starting transfers between devices: 9.3 us -> none  [from_teams(): heard.append(lax.ppermute(value, 'gz', pairs))]
    all_to_all x0 -> x2, starting transfers between devices: none -> 7.15 us  [of_teams(): lax.all_to_all(repeated, 'gz', split_axis=0, concat_axis=0, axis_index_gr...]
    ppermute x5 -> x0, waiting for transfers between devices: 6.17 us -> none  [from_teams(): heard.append(lax.ppermute(value, 'gz', pairs))]
    ppermute x13, waiting for transfers between devices: 15.8 us -> 12.9 us  [swap(): return lax.ppermute(value, 'gz', [(i, i ^ m) for i in range(slabs)])]
    broadcast_in_dim x0 -> x2, local copies, waits for them, and re-layouts: none -> 1.28 us  [of_teams(): repeated = jnp.broadcast_to(value[None], (slabs // TEAM,) + value.shape)]
    pallas_call x0 -> x1, Pallas kernels: none -> 1.08 us  [hold(): pl.pallas_call(kernel, out_shape=jax.ShapeDtypeStruct(value.shape, F32),...]
    ppermute x3, starting transfers between devices: 9.11 us -> 8.22 us  [along(): return lax.ppermute(value, 'gz', pairs)]
  transfers between devices with their start and end apart: 21 -> 18, of which waited for: 8 -> 7; matrix products, arithmetic and copies ran while one was open for 1% -> 2% of each run, Pallas kernels for 23% -> 25%
where the time goes in v8:
time: 78.5 us; the launch traced here: 78.1 us
  starting transfers between devices  28.5 us (36%)
  Pallas kernels  23.7 us (30%)
  waiting for transfers between devices  23.3 us (30%)
  local copies, waits for them, and re-layouts  1.8 us (2%)
    pallas_call x2, Pallas kernels, solve(): pl.pallas_call(kernel, out_shape=[jax.ShapeDtypeStruct((2 * planes, half,...  15.1 us
    ppermute x13, starting transfers between devices, swap(): return lax.ppermute(value, 'gz', [(i, i ^ m) for i in range(slabs)])  13.2 us
    ppermute x13, waiting for transfers between devices, swap(): return lax.ppermute(value, 'gz', [(i, i ^ m) for i in range(slabs)])  12.9 us
    all_to_all x2, waiting for transfers between devices, of_teams(): lax.all_to_all(repeated, 'gz', split_axis=0, concat_axis=0, axis_index_gr...  9.72 us
    ppermute x3, starting transfers between devices, along(): return lax.ppermute(value, 'gz', pairs)  8.22 us
    all_to_all x2, starting transfers between devices, of_teams(): lax.all_to_all(repeated, 'gz', split_axis=0, concat_axis=0, axis_index_gr...  7.15 us
    pallas_call x2, Pallas kernels, prepare(): pl.pallas_call(kernel, out_shape=[jax.ShapeDtypeStruct(shape, F32) for sh...  3.96 us
  transfers between devices with their start and end apart: 18, of which 7 were waited for; matrix products, arithmetic and copies ran while one was open for 2% of the time, Pallas kernels for 25%

profile of v8, /device:TPU:0, one launch (start us, length us, event | category | flops | bytes accessed | tf_op | source)
XLA Modules:
  0.0 78.1 jit_solution(9220985162688933435)
XLA Ops:
  0.6 2.3 %prepare.2 = (f32[33,8,512]{2,1,0:T(8,128)S(1)}, f32[33,8,512]{2,1,0:T(8,128)S(1)}, f32[8,512]{1,0:T(8,128)S(1)}) custom-call(f32[8,8]{1,0:T(8,128)} %refs_1_.3, f32[8]{0:T(128)} %refs_2_.3, f32[8,4,16,512]{3,2,1,0:T(8,128)} %refs_3_.3, f32[4,16,512]{2,1,0:T(8,128)} %refs_4_.3, s32[8,4,16,512]{3,2,1,0:T(8,128)} %refs_5_.1), custom_call_target="tpu_custom_call" | custom-call | bytes 4194304 | tf_op jit(solution)/shard_map/prepare/pallas_call | solution.py:155
  2.9 0.5 collective-permute-start.2
  3.5 1.7 %prepare.3 = (f32[32,8,512]{2,1,0:T(8,128)S(1)}, f32[32,8,512]{2,1,0:T(8,128)S(1)}) custom-call(f32[8,512]{1,0:T(8,128)S(1)} %get-tuple-element.22.refs_0_.sums_ref, f32[8,8]{1,0:T(8,128)} %refs_1_.3, f32[8]{0:T(128)} %refs_2_.3, f32[8,4,16,512]{3,2,1,0:T(8,128)} %refs_3_.3, f32[4,16,512]{2,1,0:T(8,128)} %refs_4_.3, s32[8,4,16,512]{3,2,1,0:T(8,128)} %refs_5_.1), custom_call_target="tpu_custom_call" | custom-call | bytes 4194304 | tf_op jit(solution)/shard_map/prepare/pallas_call | solution.py:155
  5.1 0.1 collective-permute-start
  5.2 0.0 collective-permute-done.2.theirs_ref
  5.2 0.9 %merge_far.1 = (f32[33,8,512]{2,1,0:T(8,128)S(1)}, f32[32,8,512]{2,1,0:T(8,128)}) custom-call(f32[33,8,512]{2,1,0:T(8,128)S(1)} %get-tuple-element.25.mine_ref, f32[33,8,512]{2,1,0:T(8,128)S(1)} %collective-permute-done.2.theirs_ref, f32[8,512]{1,0:T(8,128)S(1)} %get-tuple-element.22.refs_0_.sums_ref), custom_call_target="tpu_custom_call" | custom-call | tf_op jit(solution)/shard_map/merge_far/pallas_call | solution.py:190
  6.1 2.9 %collective-permute-start.3 = (f32[33,8,512]{2,1,0:T(8,128)S(1)}, f32[33,8,512]{2,1,0:T(8,128)S(1)}, u32[]{:S(2)}, u32[]{:S(2)}) collective-permute-start(f32[33,8,512]{2,1,0:T(8,128)S(1)} %get-tuple-element.27), channel_id=1, source_target_pairs={{0,2},{1,3},{2,0},{3,1},{4,6},{5,7},{6,4},{7,5},{8,10},{9,11},{10,... | collective-permute-start | bytes 1622024 | tf_op jit(solution)/shard_map/ppermute | solution.py:508
  9.1 0.0 collective-permute-done.theirs_ref
  9.1 0.1 merge_near.1.refs_0_
  9.2 1.3 %collective-permute-start.1 = (f32[2,2,16,8,512]{4,3,2,1,0:T(8,128)S(1)}, f32[2,2,16,8,512]{4,3,2,1,0:T(8,128)S(1)}, u32[]{:S(2)}, u32[]{:S(2)}) collective-permute-start(f32[2,2,16,8,512]{4,3,2,1,0:T(8,128)S(1)} %merge_near.1.refs_0_), channel_id=1, source_target_pairs={{2,6},{3,7},{4,0},{5,1},{6,10},{7,11},{8,4},{9,5},{10,14},{11,15},... | collective-permute-start | bytes 3145736 | tf_op jit(solution)/shard_map/ppermute | solution.py:517
  10.5 3.0 %collective-permute-start.8 = (f32[32,8,512]{2,1,0:T(8,128)}, f32[32,8,512]{2,1,0:T(8,128)}, u32[]{:S(2)}, u32[]{:S(2)}) collective-permute-start(f32[32,8,512]{2,1,0:T(8,128)} %get-tuple-element.32), channel_id=1, source_target_pairs={{0,2},{1,3},{2,0},{3,1},{4,6},{5,7},{6,4},{7,5},{8,10},{9,11},{10,... | collective-permute-start | bytes 1572872 | tf_op jit(solution)/shard_map/ppermute | solution.py:508
  13.4 8.7 %collective-permute-done.3.refs_2_ = f32[33,8,512]{2,1,0:T(8,128)S(1)} collective-permute-done((f32[33,8,512]{2,1,0:T(8,128)S(1)}, f32[33,8,512]{2,1,0:T(8,128)S(1)}, u32[]{:S(2)}, u32[]{:S(2)}) %collective-permute-start.3) | collective-permute-done | bytes 540704 | tf_op jit(solution)/shard_map/ppermute | solution.py:508
  22.1 4.1 %collective-permute-start.4 = (f32[33,8,512]{2,1,0:T(8,128)S(1)}, f32[33,8,512]{2,1,0:T(8,128)S(1)}, u32[]{:S(2)}, u32[]{:S(2)}) collective-permute-start(f32[33,8,512]{2,1,0:T(8,128)S(1)} %collective-permute-done.3.refs_2_), channel_id=1, source_target_pairs={{0,4},{1,5},{4,8},{5,9},{6,2},{7,3},{8,12},{9,13},{10,6},{11,7},{1... | collective-permute-start | bytes 1622024 | tf_op jit(solution)/shard_map/ppermute | solution.py:517
  26.2 0.6 broadcast_in_dim.7
  26.9 3.8 %all-to-all-start = ((f32[4,8,512]{2,1,0:T(8,128)}), f32[4,8,512]{2,1,0:T(8,128)S(1)}, u32[]{:S(2)}, u32[]{:S(2)}) async-start(f32[4,8,512]{2,1,0:T(8,128)} %broadcast_in_dim.7), calls=%async_computation | async-start | bytes 131072 | tf_op jit(solution)/shard_map/all_to_all | solution.py:522
  30.7 2.2 %collective-permute-done.8.value_ref = f32[32,8,512]{2,1,0:T(8,128)} collective-permute-done((f32[32,8,512]{2,1,0:T(8,128)}, f32[32,8,512]{2,1,0:T(8,128)}, u32[]{:S(2)}, u32[]{:S(2)}) %collective-permute-start.8) | collective-permute-done | bytes 524320 | tf_op jit(solution)/shard_map/ppermute | solution.py:508
  32.9 5.7 %all-to-all-done._.sums_ref = f32[4,8,512]{2,1,0:T(8,128)S(1)} async-done(((f32[4,8,512]{2,1,0:T(8,128)}), f32[4,8,512]{2,1,0:T(8,128)S(1)}, u32[]{:S(2)}, u32[]{:S(2)}) %all-to-all-start) | async-done | bytes 65568 | tf_op jit(solution)/shard_map/all_to_all | solution.py:522
  38.6 1.1 %hold.1.refs_2_ = f32[32,8,512]{2,1,0:T(8,128)S(1)} custom-call(f32[32,8,512]{2,1,0:T(8,128)} %collective-permute-done.8.value_ref, f32[4,8,512]{2,1,0:T(8,128)S(1)} %all-to-all-done._.sums_ref), custom_call_target="tpu_custom_call" | custom-call | tf_op jit(solution)/shard_map/hold/pallas_call | solution.py:385
  39.7 2.9 %collective-permute-start.9 = (f32[32,8,512]{2,1,0:T(8,128)S(1)}, f32[32,8,512]{2,1,0:T(8,128)S(1)}, u32[]{:S(2)}, u32[]{:S(2)}) collective-permute-start(f32[32,8,512]{2,1,0:T(8,128)S(1)} %hold.1.refs_2_), channel_id=1, source_target_pairs={{0,4},{1,5},{4,8},{5,9},{6,2},{7,3},{8,12},{9,13},{10,6},{11,7},{1... | collective-permute-start | bytes 1572872 | tf_op jit(solution)/shard_map/ppermute | solution.py:517
  42.5 0.0 collective-permute-done.1.refs_1_
  42.5 0.0 collective-permute-done.4.refs_3_
  42.5 7.2 %solve0.1 = (f32[8,8,512]{2,1,0:T(8,128)S(1)}, f32[8,8,512]{2,1,0:T(8,128)S(1)}, f32[8,8,512]{2,1,0:T(8,128)S(1)}, f32[8,8,512]{2,1,0:T(8,128)S(1)}, f32[16,512]{1,0:T(8,128)S(1)}) custom-call(f32[2,2,16,8,512]{4,3,2,1,0:T(8,128)S(1)} %merge_near.1.refs_0_, f32[2,2,16,8,512]{4,3,2,1,0:T(8,128)S(1)} %collective-permute-done.1.refs_1_, ...), custom_call_target="tpu_custom_call" | custom-call | bytes 23068672 | tf_op jit(solution)/shard_map/solve0/pallas_call | solution.py:366
  49.8 0.1 collective-permute-start.5
  49.9 1.2 %collective-permute-start.6 = (f32[8,8,512]{2,1,0:T(8,128)S(1)}, f32[8,8,512]{2,1,0:T(8,128)S(1)}, u32[]{:S(2)}, u32[]{:S(2)}) collective-permute-start(f32[8,8,512]{2,1,0:T(8,128)S(1)} %get-tuple-element.30), channel_id=1, source_target_pairs={{0,2},{1,3},{2,0},{3,1},{4,6},{5,7},{6,4},{7,5},{8,10},{9,11},{10,... | collective-permute-start | bytes 393224 | tf_op jit(solution)/shard_map/ppermute | solution.py:508
  51.0 0.7 collective-permute-start.7
  51.7 0.7 collective-permute-done.9.refs_3_
  52.4 7.9 %solve1.1 = (f32[8,8,512]{2,1,0:T(8,128)S(1)}, f32[8,8,512]{2,1,0:T(8,128)}, f32[8,8,512]{2,1,0:T(8,128)}, f32[8,8,512]{2,1,0:T(8,128)S(1)}, f32[16,512]{1,0:T(8,128)S(1)}) custom-call(f32[2,2,16,8,512]{4,3,2,1,0:T(8,128)S(1)} %merge_near.1.refs_0_, f32[2,2,16,8,512]{4,3,2,1,0:T(8,128)S(1)} %collective-permute-done.1.refs_1_, ...), custom_call_target="tpu_custom_call" | custom-call | bytes 23068672 | tf_op jit(solution)/shard_map/solve1/pallas_call | solution.py:366
  60.3 0.0 collective-permute-done.5.refs_1_.refs_2_
  60.3 0.0 collective-permute-done.6.refs_2_.refs_3_
  60.3 0.0 collective-permute-done.7.refs_3_.refs_4_
  60.4 2.4 %collective-permute-start.13 = (f32[16,512]{1,0:T(8,128)S(1)}, f32[16,512]{1,0:T(8,128)S(1)}, u32[]{:S(2)}, u32[]{:S(2)}) collective-permute-start(f32[16,512]{1,0:T(8,128)S(1)} %get-tuple-element.39), channel_id=1, source_target_pairs={{0,2},{1,3},{2,0},{3,1},{4,6},{5,7},{6,4},{7,5},{8,10},{9,11},{10,... | collective-permute-start | bytes 98312 | tf_op jit(solution)/shard_map/ppermute | solution.py:508
  62.8 0.0 collective-permute-start.14
  62.8 0.2 collective-permute-start.15
  62.9 0.3 collective-permute-start.10
  63.3 1.6 %collective-permute-start.11 = (f32[8,8,512]{2,1,0:T(8,128)}, f32[8,8,512]{2,1,0:T(8,128)S(1)}, u32[]{:S(2)}, u32[]{:S(2)}) collective-permute-start(f32[8,8,512]{2,1,0:T(8,128)} %get-tuple-element.35), channel_id=1, source_target_pairs={{0,2},{1,3},{2,0},{3,1},{4,6},{5,7},{6,4},{7,5},{8,10},{9,11},{10,... | collective-permute-start | bytes 393224 | tf_op jit(solution)/shard_map/ppermute | solution.py:508
  64.9 0.0 collective-permute-done.13
  64.9 0.1 collective-permute-start.12
  65.0 1.0 %collective-permute-done.14 = f32[16,512]{1,0:T(8,128)S(1)} collective-permute-done((f32[16,512]{1,0:T(8,128)S(1)}, f32[16,512]{1,0:T(8,128)S(1)}, u32[]{:S(2)}, u32[]{:S(2)}) %collective-permute-start.14) | collective-permute-done | bytes 32800 | tf_op jit(solution)/shard_map/ppermute | solution.py:508
  66.1 0.0 collective-permute-done.15
  66.1 0.6 broadcast_in_dim.16
  66.8 3.3 %all-to-all-start.1 = ((f32[4,16,512]{2,1,0:T(8,128)}), f32[4,16,512]{2,1,0:T(8,128)S(1)}, u32[]{:S(2)}, u32[]{:S(2)}) async-start(f32[4,16,512]{2,1,0:T(8,128)} %broadcast_in_dim.16), calls=%async_computation.1 | async-start | bytes 262144 | tf_op jit(solution)/shard_map/all_to_all | solution.py:522
  70.1 0.5 slice_bitcast_fusion
  70.6 0.0 collective-permute-done.10.refs_5_
  70.6 0.0 collective-permute-done.11.refs_6_
  70.6 1.0 %collective-permute-done.12.refs_7_ = f32[8,8,512]{2,1,0:T(8,128)S(1)} collective-permute-done((f32[8,8,512]{2,1,0:T(8,128)S(1)}, f32[8,8,512]{2,1,0:T(8,128)S(1)}, u32[]{:S(2)}, u32[]{:S(2)}) %collective-permute-start.12) | collective-permute-done | bytes 131104 | tf_op jit(solution)/shard_map/ppermute | solution.py:508
  71.6 1.0 %gather_adjoint.1 = f32[8,4,16,512]{3,2,1,0:T(8,128)} custom-call(f32[8,8,512]{2,1,0:T(8,128)S(1)} %get-tuple-element.28.refs_0_, f32[8,8,512]{2,1,0:T(8,128)S(1)} %collective-permute-done.5.refs_1_.refs_2_, f32[8,8,512]{2,1,0:T(8,128)S(1)} %collective-permute-done.6.refs_2_.refs_3_, f32[8,8,512]{2,1,0:T(8,128)S(1)} %collective-permute-done.7.refs_3_.refs_4_, ...), custom_call_target="tpu_custom_call" | custom-call | bytes 4194304 | tf_op jit(solution)/shard_map/gather_adjoint/pallas_call | solution.py:460
  72.6 4.0 %all-to-all-done.1 = f32[4,16,512]{2,1,0:T(8,128)S(1)} async-done(((f32[4,16,512]{2,1,0:T(8,128)}), f32[4,16,512]{2,1,0:T(8,128)S(1)}, u32[]{:S(2)}, u32[]{:S(2)}) %all-to-all-start.1) | async-done | bytes 131104 | tf_op jit(solution)/shard_map/all_to_all | solution.py:522
  76.6 1.4 %control.1 = f32[32,512]{1,0:T(8,128)} custom-call(f32[64,512]{1,0:T(8,128)S(1)} %bitcast.5, f32[16,32,64]{2,1,0:T(8,128)S(1)} %copy-done.1, f32[512,512]{1,0:T(8,128)S(1)} %copy-done), custom_call_target="tpu_custom_call" | custom-call | tf_op jit(solution)/shard_map/control/pallas_call | solution.py:491
  (7 shorter events, 0.1 us)
Async XLA Ops:
  2.9 2.3 %collective-permute-start.2 = (f32[33,8,512]{2,1,0:T(8,128)S(1)}, f32[33,8,512]{2,1,0:T(8,128)S(1)}, u32[]{:S(2)}, u32[]{:S(2)}) collective-permute-start(f32[33,8,512]{2,1,0:T(8,128)S(1)} %get-tuple-element.26), channel_id=1, source_target_pairs={{0,1},{1,0},{2,3},{3,2},{4,5},{5,4},{6,7},{7,6},{8,9},{9,8},{10,11... | collective-permute-start | bytes 1622024 | tf_op jit(solution)/shard_map/ppermute | solution.py:508
  5.1 3.9 %collective-permute-start = (f32[32,8,512]{2,1,0:T(8,128)S(1)}, f32[32,8,512]{2,1,0:T(8,128)S(1)}, u32[]{:S(2)}, u32[]{:S(2)}) collective-permute-start(f32[32,8,512]{2,1,0:T(8,128)S(1)} %get-tuple-element.24), channel_id=1, source_target_pairs={{0,1},{1,0},{2,3},{3,2},{4,5},{5,4},{6,7},{7,6},{8,9},{9,8},{10,11... | collective-permute-start | bytes 1572872 | tf_op jit(solution)/shard_map/ppermute | solution.py:508
  6.1 16.0 %collective-permute-start.3 = (f32[33,8,512]{2,1,0:T(8,128)S(1)}, f32[33,8,512]{2,1,0:T(8,128)S(1)}, u32[]{:S(2)}, u32[]{:S(2)}) collective-permute-start(f32[33,8,512]{2,1,0:T(8,128)S(1)} %get-tuple-element.27), channel_id=1, source_target_pairs={{0,2},{1,3},{2,0},{3,1},{4,6},{5,7},{6,4},{7,5},{8,10},{9,11},{10,... | collective-permute-start | bytes 1622024 | tf_op jit(solution)/shard_map/ppermute | solution.py:508
  9.2 33.4 %collective-permute-start.1 = (f32[2,2,16,8,512]{4,3,2,1,0:T(8,128)S(1)}, f32[2,2,16,8,512]{4,3,2,1,0:T(8,128)S(1)}, u32[]{:S(2)}, u32[]{:S(2)}) collective-permute-start(f32[2,2,16,8,512]{4,3,2,1,0:T(8,128)S(1)} %merge_near.1.refs_0_), channel_id=1, source_target_pairs={{2,6},{3,7},{4,0},{5,1},{6,10},{7,11},{8,4},{9,5},{10,14},{11,15},... | collective-permute-start | bytes 3145736 | tf_op jit(solution)/shard_map/ppermute | solution.py:517
  10.5 22.4 %collective-permute-start.8 = (f32[32,8,512]{2,1,0:T(8,128)}, f32[32,8,512]{2,1,0:T(8,128)}, u32[]{:S(2)}, u32[]{:S(2)}) collective-permute-start(f32[32,8,512]{2,1,0:T(8,128)} %get-tuple-element.32), channel_id=1, source_target_pairs={{0,2},{1,3},{2,0},{3,1},{4,6},{5,7},{6,4},{7,5},{8,10},{9,11},{10,... | collective-permute-start | bytes 1572872 | tf_op jit(solution)/shard_map/ppermute | solution.py:508
  22.1 20.4 %collective-permute-start.4 = (f32[33,8,512]{2,1,0:T(8,128)S(1)}, f32[33,8,512]{2,1,0:T(8,128)S(1)}, u32[]{:S(2)}, u32[]{:S(2)}) collective-permute-start(f32[33,8,512]{2,1,0:T(8,128)S(1)} %collective-permute-done.3.refs_2_), channel_id=1, source_target_pairs={{0,4},{1,5},{4,8},{5,9},{6,2},{7,3},{8,12},{9,13},{10,6},{11,7},{1... | collective-permute-start | bytes 1622024 | tf_op jit(solution)/shard_map/ppermute | solution.py:517
  26.9 11.7 %all-to-all-start = ((f32[4,8,512]{2,1,0:T(8,128)}), f32[4,8,512]{2,1,0:T(8,128)S(1)}, u32[]{:S(2)}, u32[]{:S(2)}) async-start(f32[4,8,512]{2,1,0:T(8,128)} %broadcast_in_dim.7), calls=%async_computation | async-start | bytes 131072 | tf_op jit(solution)/shard_map/all_to_all | solution.py:522
  39.7 12.7 %collective-permute-start.9 = (f32[32,8,512]{2,1,0:T(8,128)S(1)}, f32[32,8,512]{2,1,0:T(8,128)S(1)}, u32[]{:S(2)}, u32[]{:S(2)}) collective-permute-start(f32[32,8,512]{2,1,0:T(8,128)S(1)} %hold.1.refs_2_), channel_id=1, source_target_pairs={{0,4},{1,5},{4,8},{5,9},{6,2},{7,3},{8,12},{9,13},{10,6},{11,7},{1... | collective-permute-start | bytes 1572872 | tf_op jit(solution)/shard_map/ppermute | solution.py:517
  49.8 10.5 %collective-permute-start.5 = (f32[8,8,512]{2,1,0:T(8,128)S(1)}, f32[8,8,512]{2,1,0:T(8,128)S(1)}, u32[]{:S(2)}, u32[]{:S(2)}) collective-permute-start(f32[8,8,512]{2,1,0:T(8,128)S(1)} %get-tuple-element.29), channel_id=1, source_target_pairs={{0,1},{1,0},{2,3},{3,2},{4,5},{5,4},{6,7},{7,6},{8,9},{9,8},{10,11... | collective-permute-start | bytes 393224 | tf_op jit(solution)/shard_map/ppermute | solution.py:508
  49.9 10.4 %collective-permute-start.6 = (f32[8,8,512]{2,1,0:T(8,128)S(1)}, f32[8,8,512]{2,1,0:T(8,128)S(1)}, u32[]{:S(2)}, u32[]{:S(2)}) collective-permute-start(f32[8,8,512]{2,1,0:T(8,128)S(1)} %get-tuple-element.30), channel_id=1, source_target_pairs={{0,2},{1,3},{2,0},{3,1},{4,6},{5,7},{6,4},{7,5},{8,10},{9,11},{10,... | collective-permute-start | bytes 393224 | tf_op jit(solution)/shard_map/ppermute | solution.py:508
  51.0 9.3 %collective-permute-start.7 = (f32[8,8,512]{2,1,0:T(8,128)S(1)}, f32[8,8,512]{2,1,0:T(8,128)S(1)}, u32[]{:S(2)}, u32[]{:S(2)}) collective-permute-start(f32[8,8,512]{2,1,0:T(8,128)S(1)} %get-tuple-element.31), channel_id=1, source_target_pairs={{0,3},{1,2},{2,1},{3,0},{4,7},{5,6},{6,5},{7,4},{8,11},{9,10},{10,... | collective-permute-start | bytes 393224 | tf_op jit(solution)/shard_map/ppermute | solution.py:508
  60.4 4.5 %collective-permute-start.13 = (f32[16,512]{1,0:T(8,128)S(1)}, f32[16,512]{1,0:T(8,128)S(1)}, u32[]{:S(2)}, u32[]{:S(2)}) collective-permute-start(f32[16,512]{1,0:T(8,128)S(1)} %get-tuple-element.39), channel_id=1, source_target_pairs={{0,2},{1,3},{2,0},{3,1},{4,6},{5,7},{6,4},{7,5},{8,10},{9,11},{10,... | collective-permute-start | bytes 98312 | tf_op jit(solution)/shard_map/ppermute | solution.py:508
  62.8 3.3 %collective-permute-start.14 = (f32[16,512]{1,0:T(8,128)S(1)}, f32[16,512]{1,0:T(8,128)S(1)}, u32[]{:S(2)}, u32[]{:S(2)}) collective-permute-start(f32[16,512]{1,0:T(8,128)S(1)} %get-tuple-element.39), channel_id=1, source_target_pairs={{0,3},{1,2},{2,1},{3,0},{4,7},{5,6},{6,5},{7,4},{8,11},{9,10},{10,... | collective-permute-start | bytes 98312 | tf_op jit(solution)/shard_map/ppermute | solution.py:508
  62.8 3.3 %collective-permute-start.15 = (f32[16,512]{1,0:T(8,128)S(1)}, f32[16,512]{1,0:T(8,128)S(1)}, u32[]{:S(2)}, u32[]{:S(2)}) collective-permute-start(f32[16,512]{1,0:T(8,128)S(1)} %get-tuple-element.39), channel_id=1, source_target_pairs={{0,1},{1,0},{2,3},{3,2},{4,5},{5,4},{6,7},{7,6},{8,9},{9,8},{10,11... | collective-permute-start | bytes 98312 | tf_op jit(solution)/shard_map/ppermute | solution.py:508
  62.9 7.7 %collective-permute-start.10 = (f32[8,8,512]{2,1,0:T(8,128)}, f32[8,8,512]{2,1,0:T(8,128)S(1)}, u32[]{:S(2)}, u32[]{:S(2)}) collective-permute-start(f32[8,8,512]{2,1,0:T(8,128)} %get-tuple-element.34), channel_id=1, source_target_pairs={{0,1},{1,0},{2,3},{3,2},{4,5},{5,4},{6,7},{7,6},{8,9},{9,8},{10,11... | collective-permute-start | bytes 393224 | tf_op jit(solution)/shard_map/ppermute | solution.py:508
  63.3 7.3 %collective-permute-start.11 = (f32[8,8,512]{2,1,0:T(8,128)}, f32[8,8,512]{2,1,0:T(8,128)S(1)}, u32[]{:S(2)}, u32[]{:S(2)}) collective-permute-start(f32[8,8,512]{2,1,0:T(8,128)} %get-tuple-element.35), channel_id=1, source_target_pairs={{0,2},{1,3},{2,0},{3,1},{4,6},{5,7},{6,4},{7,5},{8,10},{9,11},{10,... | collective-permute-start | bytes 393224 | tf_op jit(solution)/shard_map/ppermute | solution.py:508
  64.9 6.7 %collective-permute-start.12 = (f32[8,8,512]{2,1,0:T(8,128)S(1)}, f32[8,8,512]{2,1,0:T(8,128)S(1)}, u32[]{:S(2)}, u32[]{:S(2)}) collective-permute-start(f32[8,8,512]{2,1,0:T(8,128)S(1)} %get-tuple-element.36), channel_id=1, source_target_pairs={{0,3},{1,2},{2,1},{3,0},{4,7},{5,6},{6,5},{7,4},{8,11},{9,10},{10,... | collective-permute-start | bytes 393224 | tf_op jit(solution)/shard_map/ppermute | solution.py:508
  66.8 9.9 %all-to-all-start.1 = ((f32[4,16,512]{2,1,0:T(8,128)}), f32[4,16,512]{2,1,0:T(8,128)S(1)}, u32[]{:S(2)}, u32[]{:S(2)}) async-start(f32[4,16,512]{2,1,0:T(8,128)} %broadcast_in_dim.16), calls=%async_computation.1 | async-start | bytes 262144 | tf_op jit(solution)/shard_map/all_to_all | solution.py:522
  71.6 5.1 %copy-start = (f32[512,512]{1,0:T(8,128)S(1)}, f32[512,512]{1,0:T(8,128)}, u32[]{:S(2)}) copy-start(f32[512,512]{1,0:T(8,128)} %constant.5.clone.x_ref) | copy-start | bytes 3145732
  71.6 5.1 %copy-start.1 = (f32[16,32,64]{2,1,0:T(8,128)S(1)}, f32[16,32,64]{2,1,0:T(8,128)}, u32[]{:S(2)}) copy-start(f32[16,32,64]{2,1,0:T(8,128)} %constant.4.clone.z_ref) | copy-start | bytes 393220

commit v9 on v7

--- a/solution.py
+++ b/solution.py
@@ -53,7 +53,7 @@
     return lax.rem(lax.axis_index("gz"), TEAM)
 
 
-def prepare(jobs, fields, sums=None):
+def prepare(jobs, fields, with_sums=False):
     state, target, rock_type, log_table, obs_scale = fields
     samples, planes, rows_y, columns = state.shape
     slots = samples // TEAM
@@ -63,15 +63,13 @@
     depth_total = planes * lax.axis_size("gz")
     flat = [(o, i, job) for o, group in enumerate(jobs) for i, job in enumerate(group)]
     count = len(flat)
-    given = [] if sums is None else [sums]
-    shapes = [(len(group) * size + 1 - len(given), half, columns) for group in jobs]
-    states = count if given else samples
+    shapes = [(len(group) * size + with_sums, half, columns) for group in jobs]
+    states = samples if with_sums else count
 
     def kernel(*refs):
-        refs = refs[len(given) :]
         (table_ref, scale_ref, state_ref, target_ref, rock_ref), refs = refs[:5], refs[5:]
         outs, refs = refs[: len(jobs)], refs[len(jobs) :]
-        if not given:
+        if with_sums:
             sums_ref, refs = refs[0], refs[1:]
         table, scale, state_buf, rock_buf, target_buf, mixed, sems = refs
         place = team_place()
@@ -90,7 +88,7 @@
         ]
         loads = [
             pltpu.make_async_copy(
-                state_ref.at[members[n] if given else n], state_buf.at[n], sems.at[0, n]
+                state_ref.at[n if with_sums else members[n]], state_buf.at[n], sems.at[0, n]
             )
             for n in range(states)
         ]
@@ -101,7 +99,7 @@
         ]
         for copy in small:
             copy.wait()
-        if not given:
+        if with_sums:
             for copy in loads:
                 copy.wait()
             for n in range(samples):
@@ -117,12 +115,12 @@
                 sums_ref[n : n + 1, :] = jnp.broadcast_to(summed, (1, columns))
         for n, (o, i, _) in enumerate(flat):
             rocks[n].wait()
-            if given:
+            if not with_sums:
                 loads[n].wait()
             member = members[n]
-            own_state = n if given else member
+            own_state = member if with_sums else n
             values = [
-                jnp.exp(jnp.full((8, columns), table[member, code], F32)) for code in range(NR)
+                jnp.exp(jnp.full((8, columns), -table[member, code], F32)) for code in range(NR)
             ]
             for p in range(planes):
                 factor = scale[member] * depth_weights[p]
@@ -146,18 +144,17 @@
                             outs[o][at, :, c * 128 : (c + 1) * 128] = mixed[
                                 n % 2, p, a, c, pl.ds(t, half, stride=2), :
                             ]
-        for o, group in enumerate([] if given else jobs):
+        for o, group in enumerate(jobs if with_sums else []):
             outs[o][len(group) * size] = sums_ref[...]
 
     hbm = pl.BlockSpec(memory_space=pltpu.HBM)
     vmem = pl.BlockSpec(memory_space=pltpu.VMEM)
-    sums_shape = (samples, columns)
     return pl.pallas_call(
         kernel,
         out_shape=[jax.ShapeDtypeStruct(shape, F32) for shape in shapes]
-        + ([] if given else [jax.ShapeDtypeStruct(sums_shape, F32)]),
-        in_specs=[pl.BlockSpec(memory_space=pl.ANY)] * len(given) + [hbm] * 5,
-        out_specs=[vmem] * (len(shapes) + 1 - len(given)),
+        + [jax.ShapeDtypeStruct((samples, columns), F32)] * with_sums,
+        in_specs=[hbm] * 5,
+        out_specs=[vmem] * (len(shapes) + with_sums),
         scratch_shapes=[
             pltpu.SMEM(log_table.shape, F32),
             pltpu.SMEM(obs_scale.shape, F32),
@@ -170,35 +167,52 @@
         compiler_params=pltpu.CompilerParams(vmem_limit_bytes=6 * MIB),
         cost_estimate=pl.CostEstimate(flops=0, bytes_accessed=count * MIB, transcendentals=0),
         name="prepare",
-    )(*given, log_table, obs_scale, state, target, rock_type)
-
-
-def merge_far(mine, theirs, slots, size):
+    )(log_table, obs_scale, state, target, rock_type)
+
+
+def merge_far(mine, theirs, slot, size, sums=None, with_sums=None):
+    given = [] if sums is None else [sums, with_sums]
     tile = mine.shape[1:]
 
-    def kernel(mine_ref, theirs_ref, sums_ref, *outs):
+    def kernel(mine_ref, theirs_ref, *refs):
         core = lax.rem(team_place(), 2)
+        out_ref = refs[len(given)]
         for ref, at in ((mine_ref, core), (theirs_ref, 1 - core)):
-            for slot in range(slots):
-                for n in range(size):
-                    outs[slot][at * size + n] = ref[slot * size + n]
-        outs[0][2 * size] = sums_ref[...] + theirs_ref[slots * size]
+            for n in range(size):
+                out_ref[at * size + n] = ref[slot * size + n]
+        if given:
+            total = refs[0][...] + refs[1][with_sums.shape[0] - 1]
+            out_ref[2 * size] = total
+            refs[-1][...] = total
 
     vmem = pl.BlockSpec(memory_space=pltpu.VMEM)
-
-    def call(sums):
-        return pl.pallas_call(
-            kernel,
-            out_shape=[
-                jax.ShapeDtypeStruct((2 * size + (slot == 0),) + tile, F32) for slot in range(slots)
-            ],
-            in_specs=[vmem] * 3,
-            out_specs=[vmem] * slots,
-            compiler_params=pltpu.CompilerParams(vmem_limit_bytes=4 * MIB),
-            name="merge_far",
-        )(mine, theirs, sums)
-
-    return call
+    shapes = [(2 * size + 1,) + tile, tile] if given else [(2 * size,) + tile]
+    outs = pl.pallas_call(
+        kernel,
+        out_shape=[jax.ShapeDtypeStruct(shape, F32) for shape in shapes],
+        in_specs=[vmem] * (2 + len(given)),
+        out_specs=[vmem] * len(shapes),
+        compiler_params=pltpu.CompilerParams(vmem_limit_bytes=4 * MIB),
+        name="merge_far",
+    )(mine, theirs, *given)
+    return outs if given else outs[0]
+
+
+def team_sums(mine, theirs, count):
+    def kernel(mine_ref, theirs_ref, out_ref):
+        total = mine_ref[...] + theirs_ref[theirs.shape[0] - 1]
+        for n in range(count):
+            out_ref[n] = total
+
+    vmem = pl.BlockSpec(memory_space=pltpu.VMEM)
+    return pl.pallas_call(
+        kernel,
+        out_shape=jax.ShapeDtypeStruct((count,) + mine.shape, F32),
+        in_specs=[vmem] * 2,
+        out_specs=vmem,
+        compiler_params=pltpu.CompilerParams(vmem_limit_bytes=4 * MIB),
+        name="team_sums",
+    )(mine, theirs)
 
 
 def merge_near(mine, theirs, slots, size):
@@ -228,7 +242,9 @@
 
 
 def harmonic(a, b):
-    return (a * b) * (2.0 * reciprocal(a + b))
+    x = a + b
+    guess = pl.reciprocal(x, approx=True)
+    return guess * (4.0 - (2.0 * x) * guess)
 
 
 def each(start, stop, body, width):
@@ -263,13 +279,16 @@
         upper, lower = halo + own, 0
         near_base = jnp.where(side == 0, upper, lower)
         far_base = jnp.where(side == 0, lower, upper)
+        def outside(v):
+            return jnp.where(v > 0.0, v, 1e30)
+
         for core in range(2):
             for j in range(planes):
                 for t in range(2):
                     n = 2 * j + t
                     own_base = halo + planes * core + j
                     for ref, base in ((ins[0], own_base + part * side), (ins[1], near_base + planes * core + j)):
-                        cond[base, t] = jnp.maximum(ref[core, slot, n], 1e-30)
+                        cond[base, t] = outside(ref[core, slot, n])
                         t_a[base, t] = ref[core, slot, part + n]
                     for i, base in ((0, own_base + part * (1 - side)), (1, far_base + planes * core + j)):
                         refs = ins[2 + i * len(far) : 2 + (i + 1) * len(far)]
@@ -277,7 +296,7 @@
                             first, second = refs[0][core * 2 * part + n], refs[0][(core * 2 + 1) * part + n]
                         else:
                             first, second = refs[0][core * part + n], refs[1][core * part + n]
-                        cond[base, t] = jnp.maximum(first, 1e-30)
+                        cond[base, t] = outside(first)
                         t_a[base, t] = second
 
         last_row = lax.broadcasted_iota(jnp.int32, (half, columns), 0) == half - 1
@@ -295,13 +314,15 @@
         def behind_y(v):
             return pltpu.roll(v, 1, 0)
 
-        def setup(p):
+        def setup(p, w_z_before):
             even, odd = cond[p, 0], cond[p, 1]
             w_pair = harmonic(even, odd)
             w_next = jnp.where(last_row, 0.0, harmonic(odd, ahead_y(even)))
+            w_z_here = []
             for t, here in enumerate((even, odd)):
                 w_z = harmonic(here, cond[p + 1, t])
-                w_z_behind = harmonic(here, cond[p - 1, t])
+                w_z_here.append(w_z)
+                w_z_behind = w_z_before[t]
                 w_y = w_next if t else w_pair
                 w_y_behind = w_pair if t else behind_y(w_next)
                 w_x = jnp.where(last_column, 0.0, harmonic(here, ahead_x(here)))
@@ -317,8 +338,19 @@
                 scaled = t_a[p, t] * inverse
                 u_a[p, t] = scaled
                 s_a[p, t] = scaled * (1.0 / centre)
-
-        each(1, span - 1, setup, (span - 2) // 2)
+            return w_z_here
+
+        width = (span - 2) // 3
+
+        def setup_group(n, carry):
+            start = 1 + n * width
+            w_z = [harmonic(cond[start - 1, t], cond[start, t]) for t in range(2)]
+            for k in range(width):
+                w_z = setup(start + k, w_z)
+            return carry
+
+        assert (span - 2) % width == 0
+        lax.fori_loop(0, (span - 2) // width, setup_group, 0)
 
         s_now, s_next, u_now, u_next, t_now, t_next = s_a, s_b, u_a, u_b, t_a, t_b
         for step in range(STEPS - 1):
@@ -348,7 +380,7 @@
                         t_next[p, t] = t_now[p, t] + (s + new_s)
 
             margin = halo - (STEPS - 2 - step)
-            each(margin, span - margin, advance, span // 2 - margin)
+            each(margin, span - margin, advance, 8)
             s_now, s_next, u_now, u_next = s_next, s_now, u_next, u_now
             if step % 2 == 0:
                 t_now, t_next = t_next, t_now
@@ -378,15 +410,12 @@
 
 def weigh(sums, faces, cells, after):
     slots = len(faces)
-    samples, columns = sums[0].shape
-
-    def kernel(*refs):
-        sum_refs, refs = refs[: len(sums)], refs[len(sums) :]
+    teams, samples, columns = sums.shape
+
+    def kernel(sums_ref, *refs):
         face_refs, (out_ref, moments_ref, weights) = refs[:slots], refs[slots + len(after) :]
         place = team_place()
-        summed = sum_refs[0][...]
-        for ref in sum_refs[1:]:
-            summed = summed + ref[...]
+        summed = jnp.sum(sums_ref[...], axis=0)
         misfit = summed * (1.0 / (2.0 * cells))
         mean = jnp.sum(misfit, axis=0, keepdims=True) * (1.0 / samples)
         deviation = misfit - mean
@@ -406,13 +435,13 @@
             jax.ShapeDtypeStruct(faces[0].shape, F32),
             jax.ShapeDtypeStruct((1, columns), F32),
         ],
-        in_specs=[vmem] * (len(sums) + slots)
+        in_specs=[vmem] * (1 + slots)
         + [pl.BlockSpec(memory_space=pl.ANY)] * len(after),
         out_specs=[vmem, vmem],
         scratch_shapes=[pltpu.VMEM((samples, columns), F32)],
         compiler_params=pltpu.CompilerParams(vmem_limit_bytes=2 * MIB),
         name="weigh",
-    )(*sums, *faces, *after)
+    )(sums, *faces, *after)
 
 
 def gather_adjoint(pieces, planes):
@@ -536,25 +565,33 @@
             heard.append(lax.ppermute(value, "gz", pairs))
         return heard
 
+    def of_teams(repeated):
+        columns_of_teams = [list(range(place, slabs, TEAM)) for place in range(TEAM)]
+        return lax.all_to_all(
+            repeated,
+            "gz",
+            split_axis=0,
+            concat_axis=0,
+            axis_index_groups=columns_of_teams,
+            tiled=True,
+        )
+
     fields = [
         pltpu.with_memory_space_constraint(field, pltpu.HBM)
         for field in (state, target, rock_type, log_table, obs_scale)
     ]
     size = 4 * planes
     jobs = [[(slot, m) for slot in range(slots)] for m in range(TEAM)]
-    mine, theirs, sums = prepare(jobs[2:], fields)
-    across = merge_far(mine, swap(theirs, 1), slots, size)(sums)
-    far = [[swap(value, 2)] for value in across]
-    mine, theirs = prepare(jobs[:2], fields, sums)
-    near = merge_near(mine, swap(theirs, 1), slots, size)
+    mine, theirs = prepare(jobs[2:], fields)
+    theirs = swap(theirs, 1)
+    far = [[swap(merge_far(mine, theirs, slot, size), 2)] for slot in range(slots - 1)]
+    mine_near, theirs_near, sums = prepare(jobs[:2], fields, with_sums=True)
+    theirs_near = swap(theirs_near, 1)
+    near = merge_near(mine_near, theirs_near, slots, size)
     near_halo = along(near, True)
-
-    sums = across[0][2 * size] + far[0][0][2 * size]
-    stride = 1
-    while stride * TEAM < slabs:
-        radix = next(r for r in range(2, slabs) if slabs // (stride * TEAM) % r == 0)
-        sums = sum(from_teams(sums, stride, radix), sums)
-        stride *= radix
+    last, chip_sums = merge_far(mine, theirs, slots - 1, size, sums, theirs_near)
+    far.append([swap(last, 2)])
+    all_sums = of_teams(team_sums(chip_sums, far[-1][0], slabs // TEAM))
 
     pieces, faces = [], []
     for slot in range(slots):
@@ -563,7 +600,7 @@
         pieces.append([solved[0]] + [swap(solved[m], m) for m in (1, 2, 3)])
         faces.append(solved[TEAM])
 
-    face, moments = weigh([sums], faces, depth_total * rows_y * columns, pieces[0][1:])
+    face, moments = weigh(all_sums, faces, depth_total * rows_y * columns, pieces[0][1:])
     heard = [sum((swap(face, m) for m in (2, 3, 1)), face)[None]]
     stride = 1
     for radix in radices:

time: 76.9 us -> 79 us (1.027)
  local copies, waits for them, and re-layouts: 0.52 us -> 5.17 us
  starting transfers between devices: 32.3 us -> 29.9 us
  waiting for transfers between devices: 21.9 us -> 21.1 us
    all_to_all x0 -> x1, starting transfers between devices: none -> 5.02 us  [of_teams(): lax.all_to_all(repeated, 'gz', split_axis=0, concat_axis=0, axis_index_gr...]
    ppermute x5 -> x3, waiting for transfers between devices: 6.17 us -> 1.32 us  [from_teams(): heard.append(lax.ppermute(value, 'gz', pairs))]
    unnamed x4 -> x28, local copies, waits for them, and re-layouts: 0.01 us -> 4.66 us
    ppermute x5 -> x3, starting transfers between devices: 9.3 us -> 5 us  [from_teams(): heard.append(lax.ppermute(value, 'gz', pairs))]
    ppermute x13, waiting for transfers between devices: 15.8 us -> 19.7 us  [swap(): return lax.ppermute(value, 'gz', [(i, i ^ m) for i in range(slabs)])]
    ppermute x13, starting transfers between devices: 13.8 us -> 10.8 us  [swap(): return lax.ppermute(value, 'gz', [(i, i ^ m) for i in range(slabs)])]
    pallas_call x2, Pallas kernels: 14.5 us -> 13.3 us  [solve(): pl.pallas_call(kernel, out_shape=[jax.ShapeDtypeStruct((2 * planes, half,...]
    pallas_call x1, Pallas kernels: 1.05 us -> 2.06 us  [gather_adjoint(): pl.pallas_call(kernel, out_shape=jax.ShapeDtypeStruct((slots * TEAM,) + b...]
  transfers between devices with their start and end apart: 21 -> 20, of which waited for: 8 -> 7; matrix products, arithmetic and copies ran while one was open for 1% -> 1% of each run, Pallas kernels for 23% -> 23%
where the time goes in v9:
time: 79 us; the launch traced here: 78.6 us
  starting transfers between devices  29.9 us (38%)
  Pallas kernels  21.6 us (27%)
  waiting for transfers between devices  21.1 us (27%)
  local copies, waits for them, and re-layouts  5.17 us (7%)
  between operations  0.82 us (1%)
    ppermute x13, waiting for transfers between devices, swap(): return lax.ppermute(value, 'gz', [(i, i ^ m) for i in range(slabs)])  19.7 us
    pallas_call x2, Pallas kernels, solve(): pl.pallas_call(kernel, out_shape=[jax.ShapeDtypeStruct((2 * planes, half,...  13.3 us
    ppermute x13, starting transfers between devices, swap(): return lax.ppermute(value, 'gz', [(i, i ^ m) for i in range(slabs)])  10.8 us
    ppermute x3, starting transfers between devices, along(): return lax.ppermute(value, 'gz', pairs)  9.04 us
    all_to_all x1, starting transfers between devices, of_teams(): lax.all_to_all(repeated, 'gz', split_axis=0, concat_axis=0, axis_index_gr...  5.02 us
    ppermute x3, starting transfers between devices, from_teams(): heard.append(lax.ppermute(value, 'gz', pairs))  5 us
    unnamed x28, local copies, waits for them, and re-layouts  4.66 us
    pallas_call x2, Pallas kernels, prepare(): pl.pallas_call(kernel, out_shape=[jax.ShapeDtypeStruct(shape, F32) for sh...  3.97 us
  transfers between devices with their start and end apart: 20, of which 7 were waited for; matrix products, arithmetic and copies ran while one was open for 1% of the time, Pallas kernels for 23%

profile of v9, /device:TPU:0, one launch (start us, length us, event | category | flops | bytes accessed | tf_op | source)
XLA Modules:
  0.0 78.6 jit_solution(17340936982716301759)
XLA Ops:
  0.6 2.3 %prepare.2 = (f32[33,8,512]{2,1,0:T(8,128)S(1)}, f32[33,8,512]{2,1,0:T(8,128)S(1)}, f32[8,512]{1,0:T(8,128)S(1)}) custom-call(f32[8,8]{1,0:T(8,128)} %refs_0_.3, f32[8]{0:T(128)} %refs_1_.3, f32[8,4,16,512]{3,2,1,0:T(8,128)} %refs_2_.3, f32[4,16,512]{2,1,0:T(8,128)} %refs_3_.3, s32[8,4,16,512]{3,2,1,0:T(8,128)} %refs_4_.4), custom_call_target="tpu_custom_call" | custom-call | bytes 4194304 | tf_op jit(solution)/shard_map/prepare/pallas_call | solution.py:152
  2.9 0.5 collective-permute-start
  3.5 1.7 %prepare.3 = (f32[32,8,512]{2,1,0:T(8,128)S(1)}, f32[32,8,512]{2,1,0:T(8,128)S(1)}) custom-call(f32[8,8]{1,0:T(8,128)} %refs_0_.3, f32[8]{0:T(128)} %refs_1_.3, f32[8,4,16,512]{3,2,1,0:T(8,128)} %refs_2_.3, f32[4,16,512]{2,1,0:T(8,128)} %refs_3_.3, s32[8,4,16,512]{3,2,1,0:T(8,128)} %refs_4_.4), custom_call_target="tpu_custom_call" | custom-call | bytes 4194304 | tf_op jit(solution)/shard_map/prepare/pallas_call | solution.py:152
  5.1 0.1 collective-permute-start.2
  5.3 1.9 %collective-permute-done.2.theirs_ref = f32[32,8,512]{2,1,0:T(8,128)S(1)} collective-permute-done((f32[32,8,512]{2,1,0:T(8,128)S(1)}, f32[32,8,512]{2,1,0:T(8,128)S(1)}, u32[]{:S(2)}, u32[]{:S(2)}) %collective-permute-start.2) | collective-permute-done | bytes 524320 | tf_op jit(solution)/shard_map/ppermute | solution.py:547
  7.1 0.1 merge_far.2
  7.2 2.7 %collective-permute-start.3 = (f32[32,8,512]{2,1,0:T(8,128)S(1)}, f32[32,8,512]{2,1,0:T(8,128)S(1)}, u32[]{:S(2)}, u32[]{:S(2)}) collective-permute-start(f32[32,8,512]{2,1,0:T(8,128)S(1)} %merge_far.2), channel_id=1, source_target_pairs={{0,2},{1,3},{2,0},{3,1},{4,6},{5,7},{6,4},{7,5},{8,10},{9,11},{10,... | collective-permute-start | bytes 1572872 | tf_op jit(solution)/shard_map/ppermute | solution.py:547
  9.9 0.0 collective-permute-done.theirs_ref.refs_1_
  9.9 0.1 merge_near.1.refs_0_
  10.0 1.3 %collective-permute-start.1 = (f32[2,2,16,8,512]{4,3,2,1,0:T(8,128)S(1)}, f32[2,2,16,8,512]{4,3,2,1,0:T(8,128)S(1)}, u32[]{:S(2)}, u32[]{:S(2)}) collective-permute-start(f32[2,2,16,8,512]{4,3,2,1,0:T(8,128)S(1)} %merge_near.1.refs_0_), channel_id=1, source_target_pairs={{2,6},{3,7},{4,0},{5,1},{6,10},{7,11},{8,4},{9,5},{10,14},{11,15},... | collective-permute-start | bytes 3145736 | tf_op jit(solution)/shard_map/ppermute | solution.py:556
  11.3 0.1 merge_far.3
  11.3 2.9 %collective-permute-start.8 = (f32[33,8,512]{2,1,0:T(8,128)S(1)}, f32[33,8,512]{2,1,0:T(8,128)S(1)}, u32[]{:S(2)}, u32[]{:S(2)}) collective-permute-start(f32[33,8,512]{2,1,0:T(8,128)S(1)} %get-tuple-element.31), channel_id=1, source_target_pairs={{0,2},{1,3},{2,0},{3,1},{4,6},{5,7},{6,4},{7,5},{8,10},{9,11},{10,... | collective-permute-start | bytes 1622024 | tf_op jit(solution)/shard_map/ppermute | solution.py:547
  14.2 8.4 %collective-permute-done.3.refs_2_ = f32[32,8,512]{2,1,0:T(8,128)S(1)} collective-permute-done((f32[32,8,512]{2,1,0:T(8,128)S(1)}, f32[32,8,512]{2,1,0:T(8,128)S(1)}, u32[]{:S(2)}, u32[]{:S(2)}) %collective-permute-start.3) | collective-permute-done | bytes 524320 | tf_op jit(solution)/shard_map/ppermute | solution.py:547
  22.6 4.0 %collective-permute-start.4 = (f32[32,8,512]{2,1,0:T(8,128)S(1)}, f32[32,8,512]{2,1,0:T(8,128)S(1)}, u32[]{:S(2)}, u32[]{:S(2)}) collective-permute-start(f32[32,8,512]{2,1,0:T(8,128)S(1)} %collective-permute-done.3.refs_2_), channel_id=1, source_target_pairs={{0,4},{1,5},{4,8},{5,9},{6,2},{7,3},{8,12},{9,13},{10,6},{11,7},{1... | collective-permute-start | bytes 1572872 | tf_op jit(solution)/shard_map/ppermute | solution.py:556
  26.6 7.3 %collective-permute-done.8.refs_2_.theirs_ref = f32[33,8,512]{2,1,0:T(8,128)S(1)} collective-permute-done((f32[33,8,512]{2,1,0:T(8,128)S(1)}, f32[33,8,512]{2,1,0:T(8,128)S(1)}, u32[]{:S(2)}, u32[]{:S(2)}) %collective-permute-start.8) | collective-permute-done | bytes 540704 | tf_op jit(solution)/shard_map/ppermute | solution.py:547
  33.9 3.8 %collective-permute-start.9 = (f32[33,8,512]{2,1,0:T(8,128)S(1)}, f32[33,8,512]{2,1,0:T(8,128)S(1)}, u32[]{:S(2)}, u32[]{:S(2)}) collective-permute-start(f32[33,8,512]{2,1,0:T(8,128)S(1)} %collective-permute-done.8.refs_2_.theirs_ref), channel_id=1, source_target_pairs={{0,4},{1,5},{4,8},{5,9},{6,2},{7,3},{8,12},{9,13},{10,6},{11,7},{1... | collective-permute-start | bytes 1622024 | tf_op jit(solution)/shard_map/ppermute | solution.py:556
  37.7 0.0 collective-permute-done.1.refs_1_
  37.7 7.0 %solve0.1 = (f32[8,8,512]{2,1,0:T(8,128)S(1)}, f32[8,8,512]{2,1,0:T(8,128)}, f32[8,8,512]{2,1,0:T(8,128)}, f32[8,8,512]{2,1,0:T(8,128)}, f32[16,512]{1,0:T(8,128)S(1)}) custom-call(f32[2,2,16,8,512]{4,3,2,1,0:T(8,128)S(1)} %merge_near.1.refs_0_, f32[2,2,16,8,512]{4,3,2,1,0:T(8,128)S(1)} %collective-permute-done.1.refs_1_, ...), custom_call_target="tpu_custom_call" | custom-call | bytes 23068672 | tf_op jit(solution)/shard_map/solve0/pallas_call | solution.py:398
  44.7 0.7 copy-done.2
  45.4 1.6 %collective-permute-start.6 = (f32[8,8,512]{2,1,0:T(8,128)}, f32[8,8,512]{2,1,0:T(8,128)S(1)}, u32[]{:S(2)}, u32[]{:S(2)}) collective-permute-start(f32[8,8,512]{2,1,0:T(8,128)} %get-tuple-element.28), channel_id=1, source_target_pairs={{0,2},{1,3},{2,0},{3,1},{4,6},{5,7},{6,4},{7,5},{8,10},{9,11},{10,... | collective-permute-start | bytes 393224 | tf_op jit(solution)/shard_map/ppermute | solution.py:547
  47.0 0.2 collective-permute-start.7
  47.2 0.6 team_sums.1
  47.8 5.0 %all-to-all-start = ((f32[4,8,512]{2,1,0:T(8,128)}), f32[4,8,512]{2,1,0:T(8,128)S(1)}, u32[]{:S(2)}, u32[]{:S(2)}) async-start(f32[4,8,512]{2,1,0:T(8,128)} %team_sums.1), calls=%async_computation | async-start | bytes 131072 | tf_op jit(solution)/shard_map/all_to_all | solution.py:570
  52.9 6.3 %solve1.1 = (f32[8,8,512]{2,1,0:T(8,128)S(1)}, f32[8,8,512]{2,1,0:T(8,128)S(1)}, f32[8,8,512]{2,1,0:T(8,128)S(1)}, f32[8,8,512]{2,1,0:T(8,128)S(1)}, f32[16,512]{1,0:T(8,128)S(1)}) custom-call(f32[2,2,16,8,512]{4,3,2,1,0:T(8,128)S(1)} %merge_near.1.refs_0_, f32[2,2,16,8,512]{4,3,2,1,0:T(8,128)S(1)} %collective-permute-done.1.refs_1_, ...), custom_call_target="tpu_custom_call" | custom-call | bytes 23068672 | tf_op jit(solution)/shard_map/solve1/pallas_call | solution.py:398
  59.2 0.6 copy-done.4
  59.8 0.6 copy-done.6
  60.4 0.7 copy-done.8
  61.1 0.7 copy-done.10
  61.7 0.6 copy-done.12
  62.4 0.0 collective-permute-done.6.refs_2_.refs_3_
  62.4 0.7 copy-done.7
  63.2 0.5 collective-permute-start.13
  63.8 0.9 %collective-permute-start.14 = (f32[16,512]{1,0:T(8,128)S(1)}, f32[16,512]{1,0:T(8,128)S(1)}, u32[]{:S(2)}, u32[]{:S(2)}) collective-permute-start(f32[16,512]{1,0:T(8,128)S(1)} %get-tuple-element.39), channel_id=1, source_target_pairs={{0,3},{1,2},{2,1},{3,0},{4,7},{5,6},{6,5},{7,4},{8,11},{9,10},{10,... | collective-permute-start | bytes 98312 | tf_op jit(solution)/shard_map/ppermute | solution.py:547
  64.7 0.8 %collective-permute-start.15 = (f32[16,512]{1,0:T(8,128)S(1)}, f32[16,512]{1,0:T(8,128)S(1)}, u32[]{:S(2)}, u32[]{:S(2)}) collective-permute-start(f32[16,512]{1,0:T(8,128)S(1)} %get-tuple-element.39), channel_id=1, source_target_pairs={{0,1},{1,0},{2,3},{3,2},{4,5},{5,4},{6,7},{7,6},{8,9},{9,8},{10,11... | collective-permute-start | bytes 98312 | tf_op jit(solution)/shard_map/ppermute | solution.py:547
  65.4 0.0 collective-permute-start.10
  65.5 0.5 collective-permute-start.11
  66.0 1.5 %collective-permute-done.13 = f32[16,512]{1,0:T(8,128)S(1)} collective-permute-done((f32[16,512]{1,0:T(8,128)S(1)}, f32[16,512]{1,0:T(8,128)S(1)}, u32[]{:S(2)}, u32[]{:S(2)}) %collective-permute-start.13) | collective-permute-done | bytes 32800 | tf_op jit(solution)/shard_map/ppermute | solution.py:547
  67.5 0.0 collective-permute-start.12
  67.5 0.0 collective-permute-done.14
  67.5 0.0 collective-permute-done.15
  67.5 3.9 %collective-permute-start.16 = (f32[1,16,512]{2,1,0:T(8,128)S(1)}, f32[1,16,512]{2,1,0:T(8,128)S(1)}, u32[]{:S(2)}, u32[]{:S(2)}) collective-permute-start(f32[1,16,512]{2,1,0:T(8,128)S(1)} %add_bitcast_fusion.refs_0_), channel_id=1, source_target_pairs={{4,0},{5,1},{6,2},{7,3},{8,4},{9,5},{10,6},{11,7},{12,8},{13,9},{1... | collective-permute-start | bytes 98312 | tf_op jit(solution)/shard_map/ppermute | solution.py:565
  71.4 1.1 %collective-permute-start.18 = (f32[1,16,512]{2,1,0:T(8,128)S(1)}, f32[1,16,512]{2,1,0:T(8,128)S(1)}, u32[]{:S(2)}, u32[]{:S(2)}) collective-permute-start(f32[1,16,512]{2,1,0:T(8,128)S(1)} %add_bitcast_fusion.refs_0_), channel_id=1, source_target_pairs={{12,0},{13,1},{14,2},{15,3},{0,4},{1,5},{2,6},{3,7},{4,8},{5,9},{6... | collective-permute-start | bytes 98312 | tf_op jit(solution)/shard_map/ppermute | solution.py:565
  72.5 0.5 slice_bitcast_fusion
  73.0 0.7 collective-permute-done.12.refs_7_
  73.7 2.1 %gather_adjoint.1 = f32[8,4,16,512]{3,2,1,0:T(8,128)} custom-call(f32[8,8,512]{2,1,0:T(8,128)S(1)} %copy-done.3, f32[8,8,512]{2,1,0:T(8,128)S(1)} %collective-permute-done.5.refs_1_.refs_2_, f32[8,8,512]{2,1,0:T(8,128)S(1)} %collective-permute-done.6.refs_2_.refs_3_, f32[8,8,512]{2,1,0:T(8,128)} %collective-permute-done.7.refs_3_.refs_4_, ...), custom_call_target="tpu_custom_call" | custom-call | bytes 4194304 | tf_op jit(solution)/shard_map/gather_adjoint/pallas_call | solution.py:476
  75.8 0.7 collective-permute-done.17.refs_2_
  76.5 0.6 collective-permute-done.18.refs_3_
  77.1 1.4 %control.1 = f32[32,512]{1,0:T(8,128)} custom-call(f32[1,16,512]{2,1,0:T(8,128)S(1)} %add_bitcast_fusion.refs_0_, f32[1,16,512]{2,1,0:T(8,128)S(1)} %collective-permute-done.16.refs_1_, f32[1,16,512]{2,1,0:T(8,128)S(1)} %collective-permute-done.17.refs_2_, f32[1,16,512]{2,1,0:T(8,128)S(1)} %collective-permute-done.18.refs_3_, f32[16,32,64]{2,1,0:T(8,128)S(1)} %copy-done.1, ...), custom_call_target="tpu_custom_call" | custom-call | tf_op jit(solution)/shard_map/control/pallas_call | solution.py:519
  (33 shorter events, 0.1 us)
Async XLA Ops:
  2.9 6.9 %collective-permute-start = (f32[33,8,512]{2,1,0:T(8,128)S(1)}, f32[33,8,512]{2,1,0:T(8,128)S(1)}, u32[]{:S(2)}, u32[]{:S(2)}) collective-permute-start(f32[33,8,512]{2,1,0:T(8,128)S(1)} %get-tuple-element.23), channel_id=1, source_target_pairs={{0,1},{1,0},{2,3},{3,2},{4,5},{5,4},{6,7},{7,6},{8,9},{9,8},{10,11... | collective-permute-start | bytes 1622024 | tf_op jit(solution)/shard_map/ppermute | solution.py:547
  5.1 2.0 %collective-permute-start.2 = (f32[32,8,512]{2,1,0:T(8,128)S(1)}, f32[32,8,512]{2,1,0:T(8,128)S(1)}, u32[]{:S(2)}, u32[]{:S(2)}) collective-permute-start(f32[32,8,512]{2,1,0:T(8,128)S(1)} %get-tuple-element.25), channel_id=1, source_target_pairs={{0,1},{1,0},{2,3},{3,2},{4,5},{5,4},{6,7},{7,6},{8,9},{9,8},{10,11... | collective-permute-start | bytes 1572872 | tf_op jit(solution)/shard_map/ppermute | solution.py:547
  7.2 15.5 %collective-permute-start.3 = (f32[32,8,512]{2,1,0:T(8,128)S(1)}, f32[32,8,512]{2,1,0:T(8,128)S(1)}, u32[]{:S(2)}, u32[]{:S(2)}) collective-permute-start(f32[32,8,512]{2,1,0:T(8,128)S(1)} %merge_far.2), channel_id=1, source_target_pairs={{0,2},{1,3},{2,0},{3,1},{4,6},{5,7},{6,4},{7,5},{8,10},{9,11},{10,... | collective-permute-start | bytes 1572872 | tf_op jit(solution)/shard_map/ppermute | solution.py:547
  10.0 27.7 %collective-permute-start.1 = (f32[2,2,16,8,512]{4,3,2,1,0:T(8,128)S(1)}, f32[2,2,16,8,512]{4,3,2,1,0:T(8,128)S(1)}, u32[]{:S(2)}, u32[]{:S(2)}) collective-permute-start(f32[2,2,16,8,512]{4,3,2,1,0:T(8,128)S(1)} %merge_near.1.refs_0_), channel_id=1, source_target_pairs={{2,6},{3,7},{4,0},{5,1},{6,10},{7,11},{8,4},{9,5},{10,14},{11,15},... | collective-permute-start | bytes 3145736 | tf_op jit(solution)/shard_map/ppermute | solution.py:556
  11.3 22.6 %collective-permute-start.8 = (f32[33,8,512]{2,1,0:T(8,128)S(1)}, f32[33,8,512]{2,1,0:T(8,128)S(1)}, u32[]{:S(2)}, u32[]{:S(2)}) collective-permute-start(f32[33,8,512]{2,1,0:T(8,128)S(1)} %get-tuple-element.31), channel_id=1, source_target_pairs={{0,2},{1,3},{2,0},{3,1},{4,6},{5,7},{6,4},{7,5},{8,10},{9,11},{10,... | collective-permute-start | bytes 1622024 | tf_op jit(solution)/shard_map/ppermute | solution.py:547
  22.6 15.0 %collective-permute-start.4 = (f32[32,8,512]{2,1,0:T(8,128)S(1)}, f32[32,8,512]{2,1,0:T(8,128)S(1)}, u32[]{:S(2)}, u32[]{:S(2)}) collective-permute-start(f32[32,8,512]{2,1,0:T(8,128)S(1)} %collective-permute-done.3.refs_2_), channel_id=1, source_target_pairs={{0,4},{1,5},{4,8},{5,9},{6,2},{7,3},{8,12},{9,13},{10,6},{11,7},{1... | collective-permute-start | bytes 1572872 | tf_op jit(solution)/shard_map/ppermute | solution.py:556
  33.9 19.0 %collective-permute-start.9 = (f32[33,8,512]{2,1,0:T(8,128)S(1)}, f32[33,8,512]{2,1,0:T(8,128)S(1)}, u32[]{:S(2)}, u32[]{:S(2)}) collective-permute-start(f32[33,8,512]{2,1,0:T(8,128)S(1)} %collective-permute-done.8.refs_2_.theirs_ref), channel_id=1, source_target_pairs={{0,4},{1,5},{4,8},{5,9},{6,2},{7,3},{8,12},{9,13},{10,6},{11,7},{1... | collective-permute-start | bytes 1622024 | tf_op jit(solution)/shard_map/ppermute | solution.py:556
  44.7 0.7 copy-start.2
  45.3 17.1 %collective-permute-start.5 = (f32[8,8,512]{2,1,0:T(8,128)}, f32[8,8,512]{2,1,0:T(8,128)S(1)}, u32[]{:S(2)}, u32[]{:S(2)}) collective-permute-start(f32[8,8,512]{2,1,0:T(8,128)} %get-tuple-element.27), channel_id=1, source_target_pairs={{0,1},{1,0},{2,3},{3,2},{4,5},{5,4},{6,7},{7,6},{8,9},{9,8},{10,11... | collective-permute-start | bytes 393224 | tf_op jit(solution)/shard_map/ppermute | solution.py:547
  45.4 17.1 %collective-permute-start.6 = (f32[8,8,512]{2,1,0:T(8,128)}, f32[8,8,512]{2,1,0:T(8,128)S(1)}, u32[]{:S(2)}, u32[]{:S(2)}) collective-permute-start(f32[8,8,512]{2,1,0:T(8,128)} %get-tuple-element.28), channel_id=1, source_target_pairs={{0,2},{1,3},{2,0},{3,1},{4,6},{5,7},{6,4},{7,5},{8,10},{9,11},{10,... | collective-permute-start | bytes 393224 | tf_op jit(solution)/shard_map/ppermute | solution.py:547
  47.0 15.4 %collective-permute-start.7 = (f32[8,8,512]{2,1,0:T(8,128)}, f32[8,8,512]{2,1,0:T(8,128)}, u32[]{:S(2)}, u32[]{:S(2)}) collective-permute-start(f32[8,8,512]{2,1,0:T(8,128)} %get-tuple-element.29), channel_id=1, source_target_pairs={{0,3},{1,2},{2,1},{3,0},{4,7},{5,6},{6,5},{7,4},{8,11},{9,10},{10,... | collective-permute-start | bytes 393224 | tf_op jit(solution)/shard_map/ppermute | solution.py:547
  47.8 14.6 %all-to-all-start = ((f32[4,8,512]{2,1,0:T(8,128)}), f32[4,8,512]{2,1,0:T(8,128)S(1)}, u32[]{:S(2)}, u32[]{:S(2)}) async-start(f32[4,8,512]{2,1,0:T(8,128)} %team_sums.1), calls=%async_computation | async-start | bytes 131072 | tf_op jit(solution)/shard_map/all_to_all | solution.py:570
  59.2 0.7 copy-start.4
  59.8 0.6 copy-start.6
  60.4 0.7 copy-start.8
  61.1 0.7 copy-start.10
  61.7 0.6 copy-start.12
  62.4 0.8 copy-start.7
  63.2 2.3 %copy-start.13 = (f32[8,8,512]{2,1,0:T(8,128)S(1)}, f32[8,8,512]{2,1,0:T(8,128)}, u32[]{:S(2)}) copy-start(f32[8,8,512]{2,1,0:T(8,128)} %copy-done.12) | copy-start | bytes 393220
  63.2 2.3 %copy-start.11 = (f32[8,8,512]{2,1,0:T(8,128)S(1)}, f32[8,8,512]{2,1,0:T(8,128)}, u32[]{:S(2)}) copy-start(f32[8,8,512]{2,1,0:T(8,128)} %copy-done.10) | copy-start | bytes 393220
  63.2 4.3 %copy-start.9 = (f32[8,8,512]{2,1,0:T(8,128)S(1)}, f32[8,8,512]{2,1,0:T(8,128)}, u32[]{:S(2)}) copy-start(f32[8,8,512]{2,1,0:T(8,128)} %copy-done.8) | copy-start | bytes 393220
  63.2 10.5 %copy-start.5 = (f32[8,8,512]{2,1,0:T(8,128)S(1)}, f32[8,8,512]{2,1,0:T(8,128)}, u32[]{:S(2)}) copy-start(f32[8,8,512]{2,1,0:T(8,128)} %copy-done.4) | copy-start | bytes 393220
  63.2 10.5 %copy-start.3 = (f32[8,8,512]{2,1,0:T(8,128)S(1)}, f32[8,8,512]{2,1,0:T(8,128)}, u32[]{:S(2)}) copy-start(f32[8,8,512]{2,1,0:T(8,128)} %copy-done.2) | copy-start | bytes 393220
  63.2 4.2 %collective-permute-start.13 = (f32[16,512]{1,0:T(8,128)S(1)}, f32[16,512]{1,0:T(8,128)S(1)}, u32[]{:S(2)}, u32[]{:S(2)}) collective-permute-start(f32[16,512]{1,0:T(8,128)S(1)} %get-tuple-element.39), channel_id=1, source_target_pairs={{0,2},{1,3},{2,0},{3,1},{4,6},{5,7},{6,4},{7,5},{8,10},{9,11},{10,... | collective-permute-start | bytes 98312 | tf_op jit(solution)/shard_map/ppermute | solution.py:547
  63.8 3.7 %collective-permute-start.14 = (f32[16,512]{1,0:T(8,128)S(1)}, f32[16,512]{1,0:T(8,128)S(1)}, u32[]{:S(2)}, u32[]{:S(2)}) collective-permute-start(f32[16,512]{1,0:T(8,128)S(1)} %get-tuple-element.39), channel_id=1, source_target_pairs={{0,3},{1,2},{2,1},{3,0},{4,7},{5,6},{6,5},{7,4},{8,11},{9,10},{10,... | collective-permute-start | bytes 98312 | tf_op jit(solution)/shard_map/ppermute | solution.py:547
  64.7 2.8 %collective-permute-start.15 = (f32[16,512]{1,0:T(8,128)S(1)}, f32[16,512]{1,0:T(8,128)S(1)}, u32[]{:S(2)}, u32[]{:S(2)}) collective-permute-start(f32[16,512]{1,0:T(8,128)S(1)} %get-tuple-element.39), channel_id=1, source_target_pairs={{0,1},{1,0},{2,3},{3,2},{4,5},{5,4},{6,7},{7,6},{8,9},{9,8},{10,11... | collective-permute-start | bytes 98312 | tf_op jit(solution)/shard_map/ppermute | solution.py:547
  65.4 5.9 %collective-permute-start.10 = (f32[8,8,512]{2,1,0:T(8,128)S(1)}, f32[8,8,512]{2,1,0:T(8,128)S(1)}, u32[]{:S(2)}, u32[]{:S(2)}) collective-permute-start(f32[8,8,512]{2,1,0:T(8,128)S(1)} %copy-done.13), channel_id=1, source_target_pairs={{0,1},{1,0},{2,3},{3,2},{4,5},{5,4},{6,7},{7,6},{8,9},{9,8},{10,11... | collective-permute-start | bytes 393224 | tf_op jit(solution)/shard_map/ppermute | solution.py:547
  65.5 7.6 %collective-permute-start.11 = (f32[8,8,512]{2,1,0:T(8,128)S(1)}, f32[8,8,512]{2,1,0:T(8,128)S(1)}, u32[]{:S(2)}, u32[]{:S(2)}) collective-permute-start(f32[8,8,512]{2,1,0:T(8,128)S(1)} %copy-done.11), channel_id=1, source_target_pairs={{0,2},{1,3},{2,0},{3,1},{4,6},{5,7},{6,4},{7,5},{8,10},{9,11},{10,... | collective-permute-start | bytes 393224 | tf_op jit(solution)/shard_map/ppermute | solution.py:547
  67.5 6.2 %collective-permute-start.12 = (f32[8,8,512]{2,1,0:T(8,128)S(1)}, f32[8,8,512]{2,1,0:T(8,128)S(1)}, u32[]{:S(2)}, u32[]{:S(2)}) collective-permute-start(f32[8,8,512]{2,1,0:T(8,128)S(1)} %copy-done.9), channel_id=1, source_target_pairs={{0,3},{1,2},{2,1},{3,0},{4,7},{5,6},{6,5},{7,4},{8,11},{9,10},{10,... | collective-permute-start | bytes 393224 | tf_op jit(solution)/shard_map/ppermute | solution.py:547
  67.5 8.3 %collective-permute-start.16 = (f32[1,16,512]{2,1,0:T(8,128)S(1)}, f32[1,16,512]{2,1,0:T(8,128)S(1)}, u32[]{:S(2)}, u32[]{:S(2)}) collective-permute-start(f32[1,16,512]{2,1,0:T(8,128)S(1)} %add_bitcast_fusion.refs_0_), channel_id=1, source_target_pairs={{4,0},{5,1},{6,2},{7,3},{8,4},{9,5},{10,6},{11,7},{12,8},{13,9},{1... | collective-permute-start | bytes 98312 | tf_op jit(solution)/shard_map/ppermute | solution.py:565
  71.4 5.1 %collective-permute-start.17 = (f32[1,16,512]{2,1,0:T(8,128)S(1)}, f32[1,16,512]{2,1,0:T(8,128)S(1)}, u32[]{:S(2)}, u32[]{:S(2)}) collective-permute-start(f32[1,16,512]{2,1,0:T(8,128)S(1)} %add_bitcast_fusion.refs_0_), channel_id=1, source_target_pairs={{8,0},{9,1},{10,2},{11,3},{12,4},{13,5},{14,6},{15,7},{0,8},{1,9},... | collective-permute-start | bytes 98312 | tf_op jit(solution)/shard_map/ppermute | solution.py:565
  71.4 5.7 %collective-permute-start.18 = (f32[1,16,512]{2,1,0:T(8,128)S(1)}, f32[1,16,512]{2,1,0:T(8,128)S(1)}, u32[]{:S(2)}, u32[]{:S(2)}) collective-permute-start(f32[1,16,512]{2,1,0:T(8,128)S(1)} %add_bitcast_fusion.refs_0_), channel_id=1, source_target_pairs={{12,0},{13,1},{14,2},{15,3},{0,4},{1,5},{2,6},{3,7},{4,8},{5,9},{6... | collective-permute-start | bytes 98312 | tf_op jit(solution)/shard_map/ppermute | solution.py:565
  73.7 3.4 %copy-start = (f32[512,512]{1,0:T(8,128)S(1)}, f32[512,512]{1,0:T(8,128)}, u32[]{:S(2)}) copy-start(f32[512,512]{1,0:T(8,128)} %constant.5.clone.refs_5_) | copy-start | bytes 3145732
  73.7 3.4 %copy-start.1 = (f32[16,32,64]{2,1,0:T(8,128)S(1)}, f32[16,32,64]{2,1,0:T(8,128)}, u32[]{:S(2)}) copy-start(f32[16,32,64]{2,1,0:T(8,128)} %constant.4.clone.refs_4_) | copy-start | bytes 393220

commit v10 on v9

--- a/solution.py
+++ b/solution.py
@@ -170,8 +170,8 @@
     )(log_table, obs_scale, state, target, rock_type)
 
 
-def merge_far(mine, theirs, slot, size, sums=None, with_sums=None):
-    given = [] if sums is None else [sums, with_sums]
+def merge_far(mine, theirs, slot, size, sums=None):
+    given = [] if sums is None else [sums]
     tile = mine.shape[1:]
 
     def kernel(mine_ref, theirs_ref, *refs):
@@ -181,7 +181,7 @@
             for n in range(size):
                 out_ref[at * size + n] = ref[slot * size + n]
         if given:
-            total = refs[0][...] + refs[1][with_sums.shape[0] - 1]
+            total = refs[0][...] + theirs_ref[theirs.shape[0] - 1]
             out_ref[2 * size] = total
             refs[-1][...] = total
 
@@ -198,21 +198,38 @@
     return outs if given else outs[0]
 
 
-def team_sums(mine, theirs, count):
-    def kernel(mine_ref, theirs_ref, out_ref):
-        total = mine_ref[...] + theirs_ref[theirs.shape[0] - 1]
-        for n in range(count):
-            out_ref[n] = total
-
-    vmem = pl.BlockSpec(memory_space=pltpu.VMEM)
-    return pl.pallas_call(
-        kernel,
-        out_shape=jax.ShapeDtypeStruct((count,) + mine.shape, F32),
-        in_specs=[vmem] * 2,
+def hold(value, after):
+    def kernel(value_ref, _, out_ref):
+        for n in range(value.shape[0]):
+            out_ref[n] = value_ref[n]
+
+    vmem = pl.BlockSpec(memory_space=pltpu.VMEM)
+    return pl.pallas_call(
+        kernel,
+        out_shape=jax.ShapeDtypeStruct(value.shape, F32),
+        in_specs=[vmem, pl.BlockSpec(memory_space=pl.ANY)],
         out_specs=vmem,
-        compiler_params=pltpu.CompilerParams(vmem_limit_bytes=4 * MIB),
-        name="team_sums",
-    )(mine, theirs)
+        compiler_params=pltpu.CompilerParams(vmem_limit_bytes=2 * MIB),
+        name="hold",
+    )(value, after)
+
+
+def add_up(values, after):
+    def kernel(*refs):
+        total = refs[0][...]
+        for ref in refs[1 : len(values)]:
+            total = total + ref[...]
+        refs[-1][...] = total
+
+    vmem = pl.BlockSpec(memory_space=pltpu.VMEM)
+    return pl.pallas_call(
+        kernel,
+        out_shape=jax.ShapeDtypeStruct(values[0].shape, F32),
+        in_specs=[vmem] * len(values) + [pl.BlockSpec(memory_space=pl.ANY)],
+        out_specs=vmem,
+        compiler_params=pltpu.CompilerParams(vmem_limit_bytes=MIB),
+        name="add_up",
+    )(*values, after)
 
 
 def merge_near(mine, theirs, slots, size):
@@ -261,8 +278,8 @@
 
 
 def solve(slot, near, far, near_halo, far_halo, planes):
-    inputs = [near, near_halo, *far, *far_halo]
-    half, columns = far[0].shape[-2:]
+    inputs = [near, near_halo, far, far_halo]
+    half, columns = far.shape[-2:]
     part = 2 * planes
     halo = 2 * planes
     own = TEAM * planes
@@ -291,13 +308,8 @@
                         cond[base, t] = outside(ref[core, slot, n])
                         t_a[base, t] = ref[core, slot, part + n]
                     for i, base in ((0, own_base + part * (1 - side)), (1, far_base + planes * core + j)):
-                        refs = ins[2 + i * len(far) : 2 + (i + 1) * len(far)]
-                        if len(far) == 1:
-                            first, second = refs[0][core * 2 * part + n], refs[0][(core * 2 + 1) * part + n]
-                        else:
-                            first, second = refs[0][core * part + n], refs[1][core * part + n]
-                        cond[base, t] = outside(first)
-                        t_a[base, t] = second
+                        cond[base, t] = outside(ins[2 + i][core * 2 * part + n])
+                        t_a[base, t] = ins[2 + i][(core * 2 + 1) * part + n]
 
         last_row = lax.broadcasted_iota(jnp.int32, (half, columns), 0) == half - 1
         last_column = lax.broadcasted_iota(jnp.int32, (half, columns), 1) == columns - 1
@@ -410,12 +422,15 @@
 
 def weigh(sums, faces, cells, after):
     slots = len(faces)
-    teams, samples, columns = sums.shape
-
-    def kernel(sums_ref, *refs):
+    samples, columns = sums[0].shape
+
+    def kernel(*refs):
+        sum_refs, refs = refs[: len(sums)], refs[len(sums) :]
         face_refs, (out_ref, moments_ref, weights) = refs[:slots], refs[slots + len(after) :]
         place = team_place()
-        summed = jnp.sum(sums_ref[...], axis=0)
+        summed = sum_refs[0][...]
+        for ref in sum_refs[1:]:
+            summed = summed + ref[...]
         misfit = summed * (1.0 / (2.0 * cells))
         mean = jnp.sum(misfit, axis=0, keepdims=True) * (1.0 / samples)
         deviation = misfit - mean
@@ -435,13 +450,13 @@
             jax.ShapeDtypeStruct(faces[0].shape, F32),
             jax.ShapeDtypeStruct((1, columns), F32),
         ],
-        in_specs=[vmem] * (1 + slots)
+        in_specs=[vmem] * (len(sums) + slots)
         + [pl.BlockSpec(memory_space=pl.ANY)] * len(after),
         out_specs=[vmem, vmem],
         scratch_shapes=[pltpu.VMEM((samples, columns), F32)],
         compiler_params=pltpu.CompilerParams(vmem_limit_bytes=2 * MIB),
         name="weigh",
-    )(sums, *faces, *after)
+    )(*sums, *faces, *after)
 
 
 def gather_adjoint(pieces, planes):
@@ -565,42 +580,44 @@
             heard.append(lax.ppermute(value, "gz", pairs))
         return heard
 
-    def of_teams(repeated):
-        columns_of_teams = [list(range(place, slabs, TEAM)) for place in range(TEAM)]
-        return lax.all_to_all(
-            repeated,
-            "gz",
-            split_axis=0,
-            concat_axis=0,
-            axis_index_groups=columns_of_teams,
-            tiled=True,
-        )
-
     fields = [
         pltpu.with_memory_space_constraint(field, pltpu.HBM)
         for field in (state, target, rock_type, log_table, obs_scale)
     ]
     size = 4 * planes
     jobs = [[(slot, m) for slot in range(slots)] for m in range(TEAM)]
-    mine, theirs = prepare(jobs[2:], fields)
+    mine, theirs, sums = prepare(jobs[2:], fields, with_sums=True)
     theirs = swap(theirs, 1)
-    far = [[swap(merge_far(mine, theirs, slot, size), 2)] for slot in range(slots - 1)]
-    mine_near, theirs_near, sums = prepare(jobs[:2], fields, with_sums=True)
+    first, chip_sums = merge_far(mine, theirs, 0, size, sums)
+    far = [swap(first, 2)]
+    mine_near, theirs_near = prepare(jobs[:2], fields)
     theirs_near = swap(theirs_near, 1)
     near = merge_near(mine_near, theirs_near, slots, size)
     near_halo = along(near, True)
-    last, chip_sums = merge_far(mine, theirs, slots - 1, size, sums, theirs_near)
-    far.append([swap(last, 2)])
-    all_sums = of_teams(team_sums(chip_sums, far[-1][0], slabs // TEAM))
+    far += [swap(merge_far(mine, theirs, slot, size), 2) for slot in range(1, slots)]
+    teams = slabs // TEAM
+    rounds, stride = [], 1
+    while stride < teams:
+        radix = next(r for r in range(2, teams + 1) if teams // stride % r == 0)
+        rounds.append((stride, radix))
+        stride *= radix
+    sums = [chip_sums + far[0][2 * size]]
+    for stride, radix in rounds[:1]:
+        sums = [sum(from_teams(sums[0], stride, radix), sums[0])]
+    far[1:] = [hold(value, sums[0]) for value in far[1:]]
 
     pieces, faces = [], []
     for slot in range(slots):
-        far_halo = [along(block, False) for block in far[slot]]
+        far_halo = along(far[slot], False)
         solved = solve(slot, near, far[slot], near_halo, far_halo, planes)
         pieces.append([solved[0]] + [swap(solved[m], m) for m in (1, 2, 3)])
         faces.append(solved[TEAM])
-
-    face, moments = weigh(all_sums, faces, depth_total * rows_y * columns, pieces[0][1:])
+        if slot == 0:
+            for stride, radix in rounds[1:]:
+                sums = [add_up(sums, solved[TEAM])]
+                sums += from_teams(sums[0], stride, radix)
+
+    face, moments = weigh(sums, faces, depth_total * rows_y * columns, pieces[0][1:])
     heard = [sum((swap(face, m) for m in (2, 3, 1)), face)[None]]
     stride = 1
     for radix in radices:

time: 79 us -> 72.3 us (0.915)
  local copies, waits for them, and re-layouts: 5.17 us -> 0.52 us
  Pallas kernels: 21.6 us -> 19.3 us
  starting transfers between devices: 29.9 us -> 31.9 us
  waiting for transfers between devices: 21.1 us -> 19.4 us
    ppermute x13, waiting for transfers between devices: 19.7 us -> 10 us  [swap(): return lax.ppermute(value, 'gz', [(i, i ^ m) for i in range(slabs)])]
    ppermute x3 -> x5, waiting for transfers between devices: 1.32 us -> 9.39 us  [from_teams(): heard.append(lax.ppermute(value, 'gz', pairs))]
    all_to_all x1 -> x0, starting transfers between devices: 5.02 us -> none  [of_teams(): lax.all_to_all(repeated, 'gz', split_axis=0, concat_axis=0, axis_index_gr...]
    unnamed x28 -> x4, local copies, waits for them, and re-layouts: 4.66 us -> 0.01 us
    ppermute x3 -> x5, starting transfers between devices: 5 us -> 8.76 us  [from_teams(): heard.append(lax.ppermute(value, 'gz', pairs))]
    ppermute x13, starting transfers between devices: 10.8 us -> 13.5 us  [swap(): return lax.ppermute(value, 'gz', [(i, i ^ m) for i in range(slabs)])]
    pallas_call x1, Pallas kernels: 2.06 us -> 1.05 us  [gather_adjoint(): pl.pallas_call(kernel, out_shape=jax.ShapeDtypeStruct((slots * TEAM,) + b...]
  transfers between devices with their start and end apart: 20 -> 21, of which waited for: 7 -> 4; matrix products, arithmetic and copies ran while one was open for 1% -> 1% of each run, Pallas kernels for 23% -> 22%
where the time goes in v10:
time: 72.3 us; the launch traced here: 72 us
  starting transfers between devices  31.9 us (44%)
  waiting for transfers between devices  19.4 us (27%)
  Pallas kernels  19.3 us (27%)
  between operations  0.84 us (1%)
    ppermute x13, starting transfers between devices, swap(): return lax.ppermute(value, 'gz', [(i, i ^ m) for i in range(slabs)])  13.5 us
    pallas_call x2, Pallas kernels, solve(): pl.pallas_call(kernel, out_shape=[jax.ShapeDtypeStruct((2 * planes, half,...  12.6 us
    ppermute x13, waiting for transfers between devices, swap(): return lax.ppermute(value, 'gz', [(i, i ^ m) for i in range(slabs)])  10 us
    ppermute x3, starting transfers between devices, along(): return lax.ppermute(value, 'gz', pairs)  9.65 us
    ppermute x5, waiting for transfers between devices, from_teams(): heard.append(lax.ppermute(value, 'gz', pairs))  9.39 us
    ppermute x5, starting transfers between devices, from_teams(): heard.append(lax.ppermute(value, 'gz', pairs))  8.76 us
    pallas_call x2, Pallas kernels, prepare(): pl.pallas_call(kernel, out_shape=[jax.ShapeDtypeStruct(shape, F32) for sh...  3.97 us
    pallas_call x1, Pallas kernels, control(): pl.pallas_call(kernel, out_shape=jax.ShapeDtypeStruct((own_count, basis_x...  1.45 us
  transfers between devices with their start and end apart: 21, of which 4 were waited for; matrix products, arithmetic and copies ran while one was open for 1% of the time, Pallas kernels for 22%

profile of v10, /device:TPU:0, one launch (start us, length us, event | category | flops | bytes accessed | tf_op | source)
XLA Modules:
  0.0 72.0 jit_solution(3402197165060604696)
XLA Ops:
  0.6 2.3 %prepare.3 = (f32[33,8,512]{2,1,0:T(8,128)S(1)}, f32[33,8,512]{2,1,0:T(8,128)S(1)}, f32[8,512]{1,0:T(8,128)S(1)}) custom-call(f32[8,8]{1,0:T(8,128)} %refs_0_.3, f32[8]{0:T(128)} %refs_1_.3, f32[8,4,16,512]{3,2,1,0:T(8,128)} %refs_2_.3, f32[4,16,512]{2,1,0:T(8,128)} %refs_3_.3, s32[8,4,16,512]{3,2,1,0:T(8,128)} %refs_4_.4), custom_call_target="tpu_custom_call" | custom-call | bytes 4194304 | tf_op jit(solution)/shard_map/prepare/pallas_call | solution.py:152
  2.9 0.5 collective-permute-start.2
  3.5 1.7 %prepare.2 = (f32[32,8,512]{2,1,0:T(8,128)S(1)}, f32[32,8,512]{2,1,0:T(8,128)S(1)}) custom-call(f32[8,8]{1,0:T(8,128)} %refs_0_.3, f32[8]{0:T(128)} %refs_1_.3, f32[8,4,16,512]{3,2,1,0:T(8,128)} %refs_2_.3, f32[4,16,512]{2,1,0:T(8,128)} %refs_3_.3, s32[8,4,16,512]{3,2,1,0:T(8,128)} %refs_4_.4), custom_call_target="tpu_custom_call" | custom-call | bytes 4194304 | tf_op jit(solution)/shard_map/prepare/pallas_call | solution.py:152
  5.1 0.1 collective-permute-start
  5.3 0.0 collective-permute-done.2.theirs_ref
  5.3 0.1 merge_far.2
  5.3 3.0 %collective-permute-start.3 = (f32[33,8,512]{2,1,0:T(8,128)S(1)}, f32[33,8,512]{2,1,0:T(8,128)S(1)}, u32[]{:S(2)}, u32[]{:S(2)}) collective-permute-start(f32[33,8,512]{2,1,0:T(8,128)S(1)} %get-tuple-element.27), channel_id=1, source_target_pairs={{0,2},{1,3},{2,0},{3,1},{4,6},{5,7},{6,4},{7,5},{8,10},{9,11},{10,... | collective-permute-start | bytes 1622024 | tf_op jit(solution)/shard_map/ppermute | solution.py:562
  8.3 0.0 collective-permute-done.theirs_ref
  8.3 0.1 merge_near.1.refs_0_
  8.4 1.3 %collective-permute-start.1 = (f32[2,2,16,8,512]{4,3,2,1,0:T(8,128)S(1)}, f32[2,2,16,8,512]{4,3,2,1,0:T(8,128)S(1)}, u32[]{:S(2)}, u32[]{:S(2)}) collective-permute-start(f32[2,2,16,8,512]{4,3,2,1,0:T(8,128)S(1)} %merge_near.1.refs_0_), channel_id=1, source_target_pairs={{2,6},{3,7},{4,0},{5,1},{6,10},{7,11},{8,4},{9,5},{10,14},{11,15},... | collective-permute-start | bytes 3145736 | tf_op jit(solution)/shard_map/ppermute | solution.py:571
  9.7 0.1 merge_far.3
  9.8 3.7 %collective-permute-start.8 = (f32[32,8,512]{2,1,0:T(8,128)S(1)}, f32[32,8,512]{2,1,0:T(8,128)S(1)}, u32[]{:S(2)}, u32[]{:S(2)}) collective-permute-start(f32[32,8,512]{2,1,0:T(8,128)S(1)} %merge_far.3), channel_id=1, source_target_pairs={{0,2},{1,3},{2,0},{3,1},{4,6},{5,7},{6,4},{7,5},{8,10},{9,11},{10,... | collective-permute-start | bytes 1572872 | tf_op jit(solution)/shard_map/ppermute | solution.py:562
  13.5 7.9 %collective-permute-done.3.refs_2_ = f32[33,8,512]{2,1,0:T(8,128)S(1)} collective-permute-done((f32[33,8,512]{2,1,0:T(8,128)S(1)}, f32[33,8,512]{2,1,0:T(8,128)S(1)}, u32[]{:S(2)}, u32[]{:S(2)}) %collective-permute-start.3) | collective-permute-done | bytes 540704 | tf_op jit(solution)/shard_map/ppermute | solution.py:562
  21.4 4.1 %collective-permute-start.4 = (f32[33,8,512]{2,1,0:T(8,128)S(1)}, f32[33,8,512]{2,1,0:T(8,128)S(1)}, u32[]{:S(2)}, u32[]{:S(2)}) collective-permute-start(f32[33,8,512]{2,1,0:T(8,128)S(1)} %collective-permute-done.3.refs_2_), channel_id=1, source_target_pairs={{0,4},{1,5},{4,8},{5,9},{6,2},{7,3},{8,12},{9,13},{10,6},{11,7},{1... | collective-permute-start | bytes 1622024 | tf_op jit(solution)/shard_map/ppermute | solution.py:571
  25.5 1.6 %collective-permute-start.9 = (f32[8,512]{1,0:T(8,128)S(1)}, f32[8,512]{1,0:T(8,128)S(1)}, u32[]{:S(2)}, u32[]{:S(2)}) collective-permute-start(f32[8,512]{1,0:T(8,128)S(1)} %fusion), channel_id=1, source_target_pairs={{4,0},{5,1},{6,2},{7,3},{0,4},{1,5},{2,6},{3,7},{12,8},{13,9},{14,... | collective-permute-start | bytes 49160 | tf_op jit(solution)/shard_map/ppermute | solution.py:580
  27.1 8.8 %collective-permute-done.9 = f32[8,512]{1,0:T(8,128)S(1)} collective-permute-done((f32[8,512]{1,0:T(8,128)S(1)}, f32[8,512]{1,0:T(8,128)S(1)}, u32[]{:S(2)}, u32[]{:S(2)}) %collective-permute-start.9) | collective-permute-done | bytes 16416 | tf_op jit(solution)/shard_map/ppermute | solution.py:580
  35.9 0.0 collective-permute-done.8.value_ref
  35.9 4.3 %collective-permute-start.10 = (f32[32,8,512]{2,1,0:T(8,128)S(1)}, f32[32,8,512]{2,1,0:T(8,128)S(1)}, u32[]{:S(2)}, u32[]{:S(2)}) collective-permute-start(f32[32,8,512]{2,1,0:T(8,128)S(1)} %hold.1.refs_2_), channel_id=1, source_target_pairs={{0,4},{1,5},{4,8},{5,9},{6,2},{7,3},{8,12},{9,13},{10,6},{11,7},{1... | collective-permute-start | bytes 1572872 | tf_op jit(solution)/shard_map/ppermute | solution.py:571
  40.2 0.0 collective-permute-done.1.refs_1_
  40.2 0.0 collective-permute-done.4.refs_3_
  40.2 6.3 %solve0.1 = (f32[8,8,512]{2,1,0:T(8,128)S(1)}, f32[8,8,512]{2,1,0:T(8,128)S(1)}, f32[8,8,512]{2,1,0:T(8,128)S(1)}, f32[8,8,512]{2,1,0:T(8,128)S(1)}, f32[16,512]{1,0:T(8,128)S(1)}) custom-call(f32[2,2,16,8,512]{4,3,2,1,0:T(8,128)S(1)} %merge_near.1.refs_0_, f32[2,2,16,8,512]{4,3,2,1,0:T(8,128)S(1)} %collective-permute-done.1.refs_1_, ...), custom_call_target="tpu_custom_call" | custom-call | bytes 23068672 | tf_op jit(solution)/shard_map/solve0/pallas_call | solution.py:410
  46.5 0.1 collective-permute-start.5
  46.6 0.1 collective-permute-start.6
  46.7 1.8 %collective-permute-start.7 = (f32[8,8,512]{2,1,0:T(8,128)S(1)}, f32[8,8,512]{2,1,0:T(8,128)S(1)}, u32[]{:S(2)}, u32[]{:S(2)}) collective-permute-start(f32[8,8,512]{2,1,0:T(8,128)S(1)} %get-tuple-element.31), channel_id=1, source_target_pairs={{0,3},{1,2},{2,1},{3,0},{4,7},{5,6},{6,5},{7,4},{8,11},{9,10},{10,... | collective-permute-start | bytes 393224 | tf_op jit(solution)/shard_map/ppermute | solution.py:562
  48.5 2.6 %collective-permute-start.14 = (f32[8,512]{1,0:T(8,128)S(1)}, f32[8,512]{1,0:T(8,128)S(1)}, u32[]{:S(2)}, u32[]{:S(2)}) collective-permute-start(f32[8,512]{1,0:T(8,128)S(1)} %add_up.1.refs_0_), channel_id=1, source_target_pairs={{8,0},{9,1},{10,2},{11,3},{12,4},{13,5},{14,6},{15,7},{0,8},{1,9},... | collective-permute-start | bytes 49160 | tf_op jit(solution)/shard_map/ppermute | solution.py:580
  51.0 0.0 collective-permute-done.10.refs_3_
  51.0 6.3 %solve1.1 = (f32[8,8,512]{2,1,0:T(8,128)S(1)}, f32[8,8,512]{2,1,0:T(8,128)S(1)}, f32[8,8,512]{2,1,0:T(8,128)S(1)}, f32[8,8,512]{2,1,0:T(8,128)S(1)}, f32[16,512]{1,0:T(8,128)S(1)}) custom-call(f32[2,2,16,8,512]{4,3,2,1,0:T(8,128)S(1)} %merge_near.1.refs_0_, f32[2,2,16,8,512]{4,3,2,1,0:T(8,128)S(1)} %collective-permute-done.1.refs_1_, ...), custom_call_target="tpu_custom_call" | custom-call | bytes 23068672 | tf_op jit(solution)/shard_map/solve1/pallas_call | solution.py:410
  57.3 0.0 collective-permute-done.14.refs_1_
  57.3 0.0 collective-permute-done.5.refs_1_.refs_4_
  57.3 0.0 collective-permute-done.6.refs_2_.refs_5_
  57.4 0.1 collective-permute-start.17
  57.5 1.9 %collective-permute-start.16 = (f32[16,512]{1,0:T(8,128)S(1)}, f32[16,512]{1,0:T(8,128)S(1)}, u32[]{:S(2)}, u32[]{:S(2)}) collective-permute-start(f32[16,512]{1,0:T(8,128)S(1)} %get-tuple-element.39), channel_id=1, source_target_pairs={{0,3},{1,2},{2,1},{3,0},{4,7},{5,6},{6,5},{7,4},{8,11},{9,10},{10,... | collective-permute-start | bytes 98312 | tf_op jit(solution)/shard_map/ppermute | solution.py:562
  59.4 0.2 collective-permute-start.15
  59.6 1.8 %collective-permute-start.12 = (f32[8,8,512]{2,1,0:T(8,128)S(1)}, f32[8,8,512]{2,1,0:T(8,128)S(1)}, u32[]{:S(2)}, u32[]{:S(2)}) collective-permute-start(f32[8,8,512]{2,1,0:T(8,128)S(1)} %get-tuple-element.35), channel_id=1, source_target_pairs={{0,2},{1,3},{2,0},{3,1},{4,6},{5,7},{6,4},{7,5},{8,10},{9,11},{10,... | collective-permute-start | bytes 393224 | tf_op jit(solution)/shard_map/ppermute | solution.py:562
  61.4 0.0 collective-permute-done.17
  61.4 0.1 collective-permute-start.13
  61.6 2.1 %collective-permute-done.15 = f32[16,512]{1,0:T(8,128)S(1)} collective-permute-done((f32[16,512]{1,0:T(8,128)S(1)}, f32[16,512]{1,0:T(8,128)S(1)}, u32[]{:S(2)}, u32[]{:S(2)}) %collective-permute-start.15) | collective-permute-done | bytes 32800 | tf_op jit(solution)/shard_map/ppermute | solution.py:562
  63.7 2.0 %collective-permute-start.20 = (f32[1,16,512]{2,1,0:T(8,128)S(1)}, f32[1,16,512]{2,1,0:T(8,128)S(1)}, u32[]{:S(2)}, u32[]{:S(2)}) collective-permute-start(f32[1,16,512]{2,1,0:T(8,128)S(1)} %add_bitcast_fusion.refs_0_), channel_id=1, source_target_pairs={{12,0},{13,1},{14,2},{15,3},{0,4},{1,5},{2,6},{3,7},{4,8},{5,9},{6... | collective-permute-start | bytes 98312 | tf_op jit(solution)/shard_map/ppermute | solution.py:580
  65.7 0.0 collective-permute-start.19
  65.7 0.0 collective-permute-done.11.refs_5_
  65.7 2.6 %collective-permute-start.18 = (f32[1,16,512]{2,1,0:T(8,128)S(1)}, f32[1,16,512]{2,1,0:T(8,128)S(1)}, u32[]{:S(2)}, u32[]{:S(2)}) collective-permute-start(f32[1,16,512]{2,1,0:T(8,128)S(1)} %add_bitcast_fusion.refs_0_), channel_id=1, source_target_pairs={{4,0},{5,1},{6,2},{7,3},{8,4},{9,5},{10,6},{11,7},{12,8},{13,9},{1... | collective-permute-start | bytes 98312 | tf_op jit(solution)/shard_map/ppermute | solution.py:580
  68.3 0.5 slice_bitcast_fusion.1
  68.8 0.0 copy-start.1
  68.8 1.1 %gather_adjoint.1 = f32[8,4,16,512]{3,2,1,0:T(8,128)} custom-call(f32[8,8,512]{2,1,0:T(8,128)S(1)} %get-tuple-element.28.refs_0_, f32[8,8,512]{2,1,0:T(8,128)S(1)} %collective-permute-done.5.refs_1_.refs_4_, f32[8,8,512]{2,1,0:T(8,128)S(1)} %collective-permute-done.6.refs_2_.refs_5_, f32[8,8,512]{2,1,0:T(8,128)S(1)} %collective-permute-done.7.refs_3_.refs_6_, ...), custom_call_target="tpu_custom_call" | custom-call | bytes 4194304 | tf_op jit(solution)/shard_map/gather_adjoint/pallas_call | solution.py:491
  69.9 0.0 collective-permute-done.20.refs_3_
  69.9 0.6 collective-permute-done.19.refs_2_
  70.5 0.0 collective-permute-done.18.refs_1_
  70.5 1.5 %control.1 = f32[32,512]{1,0:T(8,128)} custom-call(f32[1,16,512]{2,1,0:T(8,128)S(1)} %add_bitcast_fusion.refs_0_, f32[1,16,512]{2,1,0:T(8,128)S(1)} %collective-permute-done.18.refs_1_, f32[1,16,512]{2,1,0:T(8,128)S(1)} %collective-permute-done.19.refs_2_, f32[1,16,512]{2,1,0:T(8,128)S(1)} %collective-permute-done.20.refs_3_, f32[16,32,64]{2,1,0:T(8,128)S(1)} %copy-done.1, ...), custom_call_target="tpu_custom_call" | custom-call | tf_op jit(solution)/shard_map/control/pallas_call | solution.py:534
  (14 shorter events, 0.1 us)
Async XLA Ops:
  2.9 2.3 %collective-permute-start.2 = (f32[33,8,512]{2,1,0:T(8,128)S(1)}, f32[33,8,512]{2,1,0:T(8,128)S(1)}, u32[]{:S(2)}, u32[]{:S(2)}) collective-permute-start(f32[33,8,512]{2,1,0:T(8,128)S(1)} %get-tuple-element.25), channel_id=1, source_target_pairs={{0,1},{1,0},{2,3},{3,2},{4,5},{5,4},{6,7},{7,6},{8,9},{9,8},{10,11... | collective-permute-start | bytes 1622024 | tf_op jit(solution)/shard_map/ppermute | solution.py:562
  5.1 3.2 %collective-permute-start = (f32[32,8,512]{2,1,0:T(8,128)S(1)}, f32[32,8,512]{2,1,0:T(8,128)S(1)}, u32[]{:S(2)}, u32[]{:S(2)}) collective-permute-start(f32[32,8,512]{2,1,0:T(8,128)S(1)} %get-tuple-element.23), channel_id=1, source_target_pairs={{0,1},{1,0},{2,3},{3,2},{4,5},{5,4},{6,7},{7,6},{8,9},{9,8},{10,11... | collective-permute-start | bytes 1572872 | tf_op jit(solution)/shard_map/ppermute | solution.py:562
  5.3 16.1 %collective-permute-start.3 = (f32[33,8,512]{2,1,0:T(8,128)S(1)}, f32[33,8,512]{2,1,0:T(8,128)S(1)}, u32[]{:S(2)}, u32[]{:S(2)}) collective-permute-start(f32[33,8,512]{2,1,0:T(8,128)S(1)} %get-tuple-element.27), channel_id=1, source_target_pairs={{0,2},{1,3},{2,0},{3,1},{4,6},{5,7},{6,4},{7,5},{8,10},{9,11},{10,... | collective-permute-start | bytes 1622024 | tf_op jit(solution)/shard_map/ppermute | solution.py:562
  8.4 31.8 %collective-permute-start.1 = (f32[2,2,16,8,512]{4,3,2,1,0:T(8,128)S(1)}, f32[2,2,16,8,512]{4,3,2,1,0:T(8,128)S(1)}, u32[]{:S(2)}, u32[]{:S(2)}) collective-permute-start(f32[2,2,16,8,512]{4,3,2,1,0:T(8,128)S(1)} %merge_near.1.refs_0_), channel_id=1, source_target_pairs={{2,6},{3,7},{4,0},{5,1},{6,10},{7,11},{8,4},{9,5},{10,14},{11,15},... | collective-permute-start | bytes 3145736 | tf_op jit(solution)/shard_map/ppermute | solution.py:571
  9.8 26.1 %collective-permute-start.8 = (f32[32,8,512]{2,1,0:T(8,128)S(1)}, f32[32,8,512]{2,1,0:T(8,128)S(1)}, u32[]{:S(2)}, u32[]{:S(2)}) collective-permute-start(f32[32,8,512]{2,1,0:T(8,128)S(1)} %merge_far.3), channel_id=1, source_target_pairs={{0,2},{1,3},{2,0},{3,1},{4,6},{5,7},{6,4},{7,5},{8,10},{9,11},{10,... | collective-permute-start | bytes 1572872 | tf_op jit(solution)/shard_map/ppermute | solution.py:562
  21.4 18.8 %collective-permute-start.4 = (f32[33,8,512]{2,1,0:T(8,128)S(1)}, f32[33,8,512]{2,1,0:T(8,128)S(1)}, u32[]{:S(2)}, u32[]{:S(2)}) collective-permute-start(f32[33,8,512]{2,1,0:T(8,128)S(1)} %collective-permute-done.3.refs_2_), channel_id=1, source_target_pairs={{0,4},{1,5},{4,8},{5,9},{6,2},{7,3},{8,12},{9,13},{10,6},{11,7},{1... | collective-permute-start | bytes 1622024 | tf_op jit(solution)/shard_map/ppermute | solution.py:571
  25.5 10.4 %collective-permute-start.9 = (f32[8,512]{1,0:T(8,128)S(1)}, f32[8,512]{1,0:T(8,128)S(1)}, u32[]{:S(2)}, u32[]{:S(2)}) collective-permute-start(f32[8,512]{1,0:T(8,128)S(1)} %fusion), channel_id=1, source_target_pairs={{4,0},{5,1},{6,2},{7,3},{0,4},{1,5},{2,6},{3,7},{12,8},{13,9},{14,... | collective-permute-start | bytes 49160 | tf_op jit(solution)/shard_map/ppermute | solution.py:580
  35.9 15.1 %collective-permute-start.10 = (f32[32,8,512]{2,1,0:T(8,128)S(1)}, f32[32,8,512]{2,1,0:T(8,128)S(1)}, u32[]{:S(2)}, u32[]{:S(2)}) collective-permute-start(f32[32,8,512]{2,1,0:T(8,128)S(1)} %hold.1.refs_2_), channel_id=1, source_target_pairs={{0,4},{1,5},{4,8},{5,9},{6,2},{7,3},{8,12},{9,13},{10,6},{11,7},{1... | collective-permute-start | bytes 1572872 | tf_op jit(solution)/shard_map/ppermute | solution.py:571
  46.5 10.8 %collective-permute-start.5 = (f32[8,8,512]{2,1,0:T(8,128)S(1)}, f32[8,8,512]{2,1,0:T(8,128)S(1)}, u32[]{:S(2)}, u32[]{:S(2)}) collective-permute-start(f32[8,8,512]{2,1,0:T(8,128)S(1)} %get-tuple-element.29), channel_id=1, source_target_pairs={{0,1},{1,0},{2,3},{3,2},{4,5},{5,4},{6,7},{7,6},{8,9},{9,8},{10,11... | collective-permute-start | bytes 393224 | tf_op jit(solution)/shard_map/ppermute | solution.py:562
  46.6 10.7 %collective-permute-start.6 = (f32[8,8,512]{2,1,0:T(8,128)S(1)}, f32[8,8,512]{2,1,0:T(8,128)S(1)}, u32[]{:S(2)}, u32[]{:S(2)}) collective-permute-start(f32[8,8,512]{2,1,0:T(8,128)S(1)} %get-tuple-element.30), channel_id=1, source_target_pairs={{0,2},{1,3},{2,0},{3,1},{4,6},{5,7},{6,4},{7,5},{8,10},{9,11},{10,... | collective-permute-start | bytes 393224 | tf_op jit(solution)/shard_map/ppermute | solution.py:562
  46.7 10.7 %collective-permute-start.7 = (f32[8,8,512]{2,1,0:T(8,128)S(1)}, f32[8,8,512]{2,1,0:T(8,128)S(1)}, u32[]{:S(2)}, u32[]{:S(2)}) collective-permute-start(f32[8,8,512]{2,1,0:T(8,128)S(1)} %get-tuple-element.31), channel_id=1, source_target_pairs={{0,3},{1,2},{2,1},{3,0},{4,7},{5,6},{6,5},{7,4},{8,11},{9,10},{10,... | collective-permute-start | bytes 393224 | tf_op jit(solution)/shard_map/ppermute | solution.py:562
  48.5 8.8 %collective-permute-start.14 = (f32[8,512]{1,0:T(8,128)S(1)}, f32[8,512]{1,0:T(8,128)S(1)}, u32[]{:S(2)}, u32[]{:S(2)}) collective-permute-start(f32[8,512]{1,0:T(8,128)S(1)} %add_up.1.refs_0_), channel_id=1, source_target_pairs={{8,0},{9,1},{10,2},{11,3},{12,4},{13,5},{14,6},{15,7},{0,8},{1,9},... | collective-permute-start | bytes 49160 | tf_op jit(solution)/shard_map/ppermute | solution.py:580
  57.4 4.1 %collective-permute-start.17 = (f32[16,512]{1,0:T(8,128)S(1)}, f32[16,512]{1,0:T(8,128)S(1)}, u32[]{:S(2)}, u32[]{:S(2)}) collective-permute-start(f32[16,512]{1,0:T(8,128)S(1)} %get-tuple-element.39), channel_id=1, source_target_pairs={{0,1},{1,0},{2,3},{3,2},{4,5},{5,4},{6,7},{7,6},{8,9},{9,8},{10,11... | collective-permute-start | bytes 98312 | tf_op jit(solution)/shard_map/ppermute | solution.py:562
  57.5 4.1 %collective-permute-start.16 = (f32[16,512]{1,0:T(8,128)S(1)}, f32[16,512]{1,0:T(8,128)S(1)}, u32[]{:S(2)}, u32[]{:S(2)}) collective-permute-start(f32[16,512]{1,0:T(8,128)S(1)} %get-tuple-element.39), channel_id=1, source_target_pairs={{0,3},{1,2},{2,1},{3,0},{4,7},{5,6},{6,5},{7,4},{8,11},{9,10},{10,... | collective-permute-start | bytes 98312 | tf_op jit(solution)/shard_map/ppermute | solution.py:562
  59.4 4.3 %collective-permute-start.15 = (f32[16,512]{1,0:T(8,128)S(1)}, f32[16,512]{1,0:T(8,128)S(1)}, u32[]{:S(2)}, u32[]{:S(2)}) collective-permute-start(f32[16,512]{1,0:T(8,128)S(1)} %get-tuple-element.39), channel_id=1, source_target_pairs={{0,2},{1,3},{2,0},{3,1},{4,6},{5,7},{6,4},{7,5},{8,10},{9,11},{10,... | collective-permute-start | bytes 98312 | tf_op jit(solution)/shard_map/ppermute | solution.py:562
  59.6 6.1 %collective-permute-start.11 = (f32[8,8,512]{2,1,0:T(8,128)S(1)}, f32[8,8,512]{2,1,0:T(8,128)S(1)}, u32[]{:S(2)}, u32[]{:S(2)}) collective-permute-start(f32[8,8,512]{2,1,0:T(8,128)S(1)} %get-tuple-element.34), channel_id=1, source_target_pairs={{0,1},{1,0},{2,3},{3,2},{4,5},{5,4},{6,7},{7,6},{8,9},{9,8},{10,11... | collective-permute-start | bytes 393224 | tf_op jit(solution)/shard_map/ppermute | solution.py:562
  59.6 9.2 %collective-permute-start.12 = (f32[8,8,512]{2,1,0:T(8,128)S(1)}, f32[8,8,512]{2,1,0:T(8,128)S(1)}, u32[]{:S(2)}, u32[]{:S(2)}) collective-permute-start(f32[8,8,512]{2,1,0:T(8,128)S(1)} %get-tuple-element.35), channel_id=1, source_target_pairs={{0,2},{1,3},{2,0},{3,1},{4,6},{5,7},{6,4},{7,5},{8,10},{9,11},{10,... | collective-permute-start | bytes 393224 | tf_op jit(solution)/shard_map/ppermute | solution.py:562
  61.4 7.4 %collective-permute-start.13 = (f32[8,8,512]{2,1,0:T(8,128)S(1)}, f32[8,8,512]{2,1,0:T(8,128)S(1)}, u32[]{:S(2)}, u32[]{:S(2)}) collective-permute-start(f32[8,8,512]{2,1,0:T(8,128)S(1)} %get-tuple-element.36), channel_id=1, source_target_pairs={{0,3},{1,2},{2,1},{3,0},{4,7},{5,6},{6,5},{7,4},{8,11},{9,10},{10,... | collective-permute-start | bytes 393224 | tf_op jit(solution)/shard_map/ppermute | solution.py:562
  63.7 6.2 %collective-permute-start.20 = (f32[1,16,512]{2,1,0:T(8,128)S(1)}, f32[1,16,512]{2,1,0:T(8,128)S(1)}, u32[]{:S(2)}, u32[]{:S(2)}) collective-permute-start(f32[1,16,512]{2,1,0:T(8,128)S(1)} %add_bitcast_fusion.refs_0_), channel_id=1, source_target_pairs={{12,0},{13,1},{14,2},{15,3},{0,4},{1,5},{2,6},{3,7},{4,8},{5,9},{6... | collective-permute-start | bytes 98312 | tf_op jit(solution)/shard_map/ppermute | solution.py:580
  65.7 4.9 %collective-permute-start.19 = (f32[1,16,512]{2,1,0:T(8,128)S(1)}, f32[1,16,512]{2,1,0:T(8,128)S(1)}, u32[]{:S(2)}, u32[]{:S(2)}) collective-permute-start(f32[1,16,512]{2,1,0:T(8,128)S(1)} %add_bitcast_fusion.refs_0_), channel_id=1, source_target_pairs={{8,0},{9,1},{10,2},{11,3},{12,4},{13,5},{14,6},{15,7},{0,8},{1,9},... | collective-permute-start | bytes 98312 | tf_op jit(solution)/shard_map/ppermute | solution.py:580
  65.7 4.9 %collective-permute-start.18 = (f32[1,16,512]{2,1,0:T(8,128)S(1)}, f32[1,16,512]{2,1,0:T(8,128)S(1)}, u32[]{:S(2)}, u32[]{:S(2)}) collective-permute-start(f32[1,16,512]{2,1,0:T(8,128)S(1)} %add_bitcast_fusion.refs_0_), channel_id=1, source_target_pairs={{4,0},{5,1},{6,2},{7,3},{8,4},{9,5},{10,6},{11,7},{12,8},{13,9},{1... | collective-permute-start | bytes 98312 | tf_op jit(solution)/shard_map/ppermute | solution.py:580
  68.8 1.7 %copy-start = (f32[512,512]{1,0:T(8,128)S(1)}, f32[512,512]{1,0:T(8,128)}, u32[]{:S(2)}) copy-start(f32[512,512]{1,0:T(8,128)} %constant.5.clone.refs_5_) | copy-start | bytes 3145732
  68.8 1.7 %copy-start.1 = (f32[16,32,64]{2,1,0:T(8,128)S(1)}, f32[16,32,64]{2,1,0:T(8,128)}, u32[]{:S(2)}) copy-start(f32[16,32,64]{2,1,0:T(8,128)} %constant.4.clone.refs_4_) | copy-start | bytes 393220

commit v11 on v10

--- a/solution.py
+++ b/solution.py
@@ -170,87 +170,49 @@
     )(log_table, obs_scale, state, target, rock_type)
 
 
-def merge_far(mine, theirs, slot, size, sums=None):
-    given = [] if sums is None else [sums]
+def merge_far(mine, theirs, slot, size, sums, add=False):
     tile = mine.shape[1:]
 
-    def kernel(mine_ref, theirs_ref, *refs):
+    def kernel(mine_ref, theirs_ref, sums_ref, out_ref, *more):
         core = lax.rem(team_place(), 2)
-        out_ref = refs[len(given)]
         for ref, at in ((mine_ref, core), (theirs_ref, 1 - core)):
             for n in range(size):
                 out_ref[at * size + n] = ref[slot * size + n]
-        if given:
-            total = refs[0][...] + theirs_ref[theirs.shape[0] - 1]
-            out_ref[2 * size] = total
-            refs[-1][...] = total
+        if add:
+            more[0][...] = sums_ref[...] + theirs_ref[theirs.shape[0] - 1]
+        else:
+            out_ref[2 * size] = sums_ref[...]
 
     vmem = pl.BlockSpec(memory_space=pltpu.VMEM)
-    shapes = [(2 * size + 1,) + tile, tile] if given else [(2 * size,) + tile]
+    shapes = [(2 * size,) + tile, tile] if add else [(2 * size + 1,) + tile]
     outs = pl.pallas_call(
         kernel,
         out_shape=[jax.ShapeDtypeStruct(shape, F32) for shape in shapes],
-        in_specs=[vmem] * (2 + len(given)),
+        in_specs=[vmem] * 3,
         out_specs=[vmem] * len(shapes),
         compiler_params=pltpu.CompilerParams(vmem_limit_bytes=4 * MIB),
         name="merge_far",
-    )(mine, theirs, *given)
-    return outs if given else outs[0]
-
-
-def hold(value, after):
-    def kernel(value_ref, _, out_ref):
-        for n in range(value.shape[0]):
-            out_ref[n] = value_ref[n]
+    )(mine, theirs, sums)
+    return outs if add else outs[0]
+
+
+def merge_near(mine, theirs, slot, size, sums):
+    def kernel(mine_ref, theirs_ref, sums_ref, out_ref):
+        core = lax.rem(team_place(), 2)
+        for ref, at in ((mine_ref, core), (theirs_ref, 1 - core)):
+            for n in range(size):
+                out_ref[at * size + n] = ref[slot * size + n]
+        out_ref[2 * size] = sums_ref[...]
 
     vmem = pl.BlockSpec(memory_space=pltpu.VMEM)
     return pl.pallas_call(
         kernel,
-        out_shape=jax.ShapeDtypeStruct(value.shape, F32),
-        in_specs=[vmem, pl.BlockSpec(memory_space=pl.ANY)],
-        out_specs=vmem,
-        compiler_params=pltpu.CompilerParams(vmem_limit_bytes=2 * MIB),
-        name="hold",
-    )(value, after)
-
-
-def add_up(values, after):
-    def kernel(*refs):
-        total = refs[0][...]
-        for ref in refs[1 : len(values)]:
-            total = total + ref[...]
-        refs[-1][...] = total
-
-    vmem = pl.BlockSpec(memory_space=pltpu.VMEM)
-    return pl.pallas_call(
-        kernel,
-        out_shape=jax.ShapeDtypeStruct(values[0].shape, F32),
-        in_specs=[vmem] * len(values) + [pl.BlockSpec(memory_space=pl.ANY)],
-        out_specs=vmem,
-        compiler_params=pltpu.CompilerParams(vmem_limit_bytes=MIB),
-        name="add_up",
-    )(*values, after)
-
-
-def merge_near(mine, theirs, slots, size):
-    tile = mine.shape[1:]
-
-    def kernel(mine_ref, theirs_ref, out_ref):
-        core = lax.rem(team_place(), 2)
-        for ref, at in ((mine_ref, core), (theirs_ref, 1 - core)):
-            for slot in range(slots):
-                for n in range(size):
-                    out_ref[at, slot, n] = ref[slot * size + n]
-
-    vmem = pl.BlockSpec(memory_space=pltpu.VMEM)
-    return pl.pallas_call(
-        kernel,
-        out_shape=jax.ShapeDtypeStruct((2, slots, size) + tile, F32),
-        in_specs=[vmem] * 2,
+        out_shape=jax.ShapeDtypeStruct((2 * size + 1,) + mine.shape[1:], F32),
+        in_specs=[vmem] * 3,
         out_specs=vmem,
         compiler_params=pltpu.CompilerParams(vmem_limit_bytes=4 * MIB),
         name="merge_near",
-    )(mine, theirs)
+    )(mine, theirs, sums)
 
 
 def reciprocal(x):
@@ -277,7 +239,7 @@
         body(p)
 
 
-def solve(slot, near, far, near_halo, far_halo, planes):
+def solve(near, far, near_halo, far_halo, planes):
     inputs = [near, near_halo, far, far_halo]
     half, columns = far.shape[-2:]
     part = 2 * planes
@@ -304,12 +266,14 @@
                 for t in range(2):
                     n = 2 * j + t
                     own_base = halo + planes * core + j
-                    for ref, base in ((ins[0], own_base + part * side), (ins[1], near_base + planes * core + j)):
-                        cond[base, t] = outside(ref[core, slot, n])
-                        t_a[base, t] = ref[core, slot, part + n]
-                    for i, base in ((0, own_base + part * (1 - side)), (1, far_base + planes * core + j)):
-                        cond[base, t] = outside(ins[2 + i][core * 2 * part + n])
-                        t_a[base, t] = ins[2 + i][(core * 2 + 1) * part + n]
+                    for ref, base in (
+                        (ins[0], own_base + part * side),
+                        (ins[1], near_base + planes * core + j),
+                        (ins[2], own_base + part * (1 - side)),
+                        (ins[3], far_base + planes * core + j),
+                    ):
+                        cond[base, t] = outside(ref[core * 2 * part + n])
+                        t_a[base, t] = ref[(core * 2 + 1) * part + n]
 
         last_row = lax.broadcasted_iota(jnp.int32, (half, columns), 0) == half - 1
         last_column = lax.broadcasted_iota(jnp.int32, (half, columns), 1) == columns - 1
@@ -416,7 +380,7 @@
         scratch_shapes=[field] * 13,
         compiler_params=pltpu.CompilerParams(vmem_limit_bytes=16 * MIB),
         cost_estimate=pl.CostEstimate(flops=0, bytes_accessed=22 * MIB, transcendentals=0),
-        name=f"solve{slot}",
+        name="solve",
     )(*inputs)
 
 
@@ -466,7 +430,8 @@
     block = (planes, 2 * half, columns)
 
     def kernel(*refs):
-        blocks, out, held, mixed, sems = refs[: slots * TEAM], *refs[slots * TEAM :]
+        blocks, out, mark, held, mixed, sems = refs[: slots * TEAM], *refs[slots * TEAM :]
+        mark[...] = blocks[0][0, :, :LANES]
         place = team_place()
         copies = []
         for slot in range(slots):
@@ -490,9 +455,15 @@
 
     return pl.pallas_call(
         kernel,
-        out_shape=jax.ShapeDtypeStruct((slots * TEAM,) + block, F32),
+        out_shape=[
+            jax.ShapeDtypeStruct((slots * TEAM,) + block, F32),
+            jax.ShapeDtypeStruct((half, LANES), F32),
+        ],
         in_specs=[pl.BlockSpec(memory_space=pltpu.VMEM)] * (slots * TEAM),
-        out_specs=pl.BlockSpec(memory_space=pltpu.HBM),
+        out_specs=[
+            pl.BlockSpec(memory_space=pltpu.HBM),
+            pl.BlockSpec(memory_space=pltpu.VMEM),
+        ],
         scratch_shapes=[
             pltpu.VMEM((slots * TEAM,) + block, F32),
             pltpu.VMEM((2, planes, tiles, 2 * half, 128), F32),
@@ -504,13 +475,13 @@
     )(*[piece for group in pieces for piece in group])
 
 
-def control(faces, radices, basis_z, basis_x):
+def control(faces, radices, basis_z, basis_x, after):
     slabs, own_count, depth_total = basis_z.shape
     own, columns = faces[0].shape[1:]
     teams = depth_total // own
 
     def kernel(*refs):
-        parts, (z_ref, x_ref, out_ref, whole) = refs[: len(faces)], refs[len(faces) :]
+        parts, (z_ref, x_ref, _, out_ref, whole) = refs[: len(faces)], refs[len(faces) :]
         rank = lax.axis_index("gz")
         team = rank // TEAM
         for n in range(teams):
@@ -534,12 +505,12 @@
     return pl.pallas_call(
         kernel,
         out_shape=jax.ShapeDtypeStruct((own_count, basis_x.shape[1]), F32),
-        in_specs=[vmem] * (len(faces) + 2),
+        in_specs=[vmem] * (len(faces) + 2) + [pl.BlockSpec(memory_space=pl.ANY)],
         out_specs=vmem,
         scratch_shapes=[pltpu.VMEM((teams, own, columns), F32)],
         compiler_params=pltpu.CompilerParams(vmem_limit_bytes=8 * MIB),
         name="control",
-    )(*faces, basis_z, basis_x)
+    )(*faces, basis_z, basis_x, after)
 
 
 def radices_of(teams):
@@ -588,34 +559,27 @@
     jobs = [[(slot, m) for slot in range(slots)] for m in range(TEAM)]
     mine, theirs, sums = prepare(jobs[2:], fields, with_sums=True)
     theirs = swap(theirs, 1)
-    first, chip_sums = merge_far(mine, theirs, 0, size, sums)
+    first, sums = merge_far(mine, theirs, 0, size, sums, add=True)
     far = [swap(first, 2)]
+    stride, teams = 1, slabs // TEAM
+    while stride < teams:
+        radix = next(r for r in range(2, teams + 1) if teams // stride % r == 0)
+        sums = sum(from_teams(sums, stride, radix), sums)
+        stride *= radix
+
     mine_near, theirs_near = prepare(jobs[:2], fields)
     theirs_near = swap(theirs_near, 1)
-    near = merge_near(mine_near, theirs_near, slots, size)
-    near_halo = along(near, True)
-    far += [swap(merge_far(mine, theirs, slot, size), 2) for slot in range(1, slots)]
-    teams = slabs // TEAM
-    rounds, stride = [], 1
-    while stride < teams:
-        radix = next(r for r in range(2, teams + 1) if teams // stride % r == 0)
-        rounds.append((stride, radix))
-        stride *= radix
-    sums = [chip_sums + far[0][2 * size]]
-    for stride, radix in rounds[:1]:
-        sums = [sum(from_teams(sums[0], stride, radix), sums[0])]
-    far[1:] = [hold(value, sums[0]) for value in far[1:]]
+    near = [merge_near(mine_near, theirs_near, slot, size, sums) for slot in range(slots)]
+    near_halo = [along(value, True) for value in near]
+    far += [swap(merge_far(mine, theirs, slot, size, sums), 2) for slot in range(1, slots)]
+    sums = [sums, far[-1][2 * size]]
 
     pieces, faces = [], []
     for slot in range(slots):
         far_halo = along(far[slot], False)
-        solved = solve(slot, near, far[slot], near_halo, far_halo, planes)
+        solved = solve(near[slot], far[slot], near_halo[slot], far_halo, planes)
         pieces.append([solved[0]] + [swap(solved[m], m) for m in (1, 2, 3)])
         faces.append(solved[TEAM])
-        if slot == 0:
-            for stride, radix in rounds[1:]:
-                sums = [add_up(sums, solved[TEAM])]
-                sums += from_teams(sums[0], stride, radix)
 
     face, moments = weigh(sums, faces, depth_total * rows_y * columns, pieces[0][1:])
     heard = [sum((swap(face, m) for m in (2, 3, 1)), face)[None]]
@@ -624,13 +588,14 @@
         held = heard[0] if len(heard) == 1 else jnp.concatenate(heard)
         heard = [held] + from_teams(held, stride, radix)
         stride *= radix
-    adjoint = gather_adjoint(pieces, planes)
+    adjoint, mark = gather_adjoint(pieces, planes)
     own_count = MA // slabs
     gradient = control(
         heard,
         radices,
         jnp.asarray(cosine_basis(depth_total, MA).T.reshape(slabs, own_count, depth_total)),
         jnp.asarray(cosine_basis(columns, MB)),
+        mark,
     )
     return (adjoint, gradient, moments[0, :2])
 

time: 72.3 us -> 68.7 us (0.950)
  waiting for transfers between devices: 19.4 us -> 17.1 us
  starting transfers between devices: 31.9 us -> 30.7 us
    ppermute x5, waiting for transfers between devices: 9.39 us -> 4.22 us  [from_teams(): heard.append(lax.ppermute(value, 'gz', pairs))]
    ppermute x13, starting transfers between devices: 13.5 us -> 10.6 us  [swap(): return lax.ppermute(value, 'gz', [(i, i ^ m) for i in range(slabs)])]
    ppermute x3 -> x4, waiting for transfers between devices: 0.01 us -> 2.58 us  [along(): return lax.ppermute(value, 'gz', pairs)]
    ppermute x5, starting transfers between devices: 8.76 us -> 9.66 us  [from_teams(): heard.append(lax.ppermute(value, 'gz', pairs))]
    ppermute x3 -> x4, starting transfers between devices: 9.65 us -> 10.4 us  [along(): return lax.ppermute(value, 'gz', pairs)]
  transfers between devices with their start and end apart: 21 -> 22, of which waited for: 4 -> 6; matrix products, arithmetic and copies ran while one was open for 1% -> 1% of each run, Pallas kernels for 22% -> 23%
where the time goes in v11:
time: 68.7 us; the launch traced here: 68.4 us
  starting transfers between devices  30.7 us (45%)
  Pallas kernels  19.3 us (28%)
  waiting for transfers between devices  17.1 us (25%)
  between operations  0.85 us (1%)
    pallas_call x2, Pallas kernels, solve(): pl.pallas_call(kernel, out_shape=[jax.ShapeDtypeStruct((2 * planes, half,...  12.6 us
    ppermute x13, starting transfers between devices, swap(): return lax.ppermute(value, 'gz', [(i, i ^ m) for i in range(slabs)])  10.6 us
    ppermute x4, starting transfers between devices, along(): return lax.ppermute(value, 'gz', pairs)  10.4 us
    ppermute x13, waiting for transfers between devices, swap(): return lax.ppermute(value, 'gz', [(i, i ^ m) for i in range(slabs)])  10.3 us
    ppermute x5, starting transfers between devices, from_teams(): heard.append(lax.ppermute(value, 'gz', pairs))  9.66 us
    ppermute x5, waiting for transfers between devices, from_teams(): heard.append(lax.ppermute(value, 'gz', pairs))  4.22 us
    pallas_call x2, Pallas kernels, prepare(): pl.pallas_call(kernel, out_shape=[jax.ShapeDtypeStruct(shape, F32) for sh...  3.97 us
    ppermute x4, waiting for transfers between devices, along(): return lax.ppermute(value, 'gz', pairs)  2.58 us
  transfers between devices with their start and end apart: 22, of which 6 were waited for; matrix products, arithmetic and copies ran while one was open for 1% of the time, Pallas kernels for 23%

profile of v11, /device:TPU:0, one launch (start us, length us, event | category | flops | bytes accessed | tf_op | source)
XLA Modules:
  0.0 68.4 jit_solution(2707891047540498802)
XLA Ops:
  0.6 2.3 %prepare.3 = (f32[33,8,512]{2,1,0:T(8,128)S(1)}, f32[33,8,512]{2,1,0:T(8,128)S(1)}, f32[8,512]{1,0:T(8,128)S(1)}) custom-call(f32[8,8]{1,0:T(8,128)} %refs_0_.3, f32[8]{0:T(128)} %refs_1_.3, f32[8,4,16,512]{3,2,1,0:T(8,128)} %refs_2_.3, f32[4,16,512]{2,1,0:T(8,128)} %refs_3_.3, s32[8,4,16,512]{3,2,1,0:T(8,128)} %refs_4_.4), custom_call_target="tpu_custom_call" | custom-call | bytes 4194304 | tf_op jit(solution)/shard_map/prepare/pallas_call | solution.py:152
  2.9 0.5 collective-permute-start.1
  3.5 1.7 %prepare.2 = (f32[32,8,512]{2,1,0:T(8,128)S(1)}, f32[32,8,512]{2,1,0:T(8,128)S(1)}) custom-call(f32[8,8]{1,0:T(8,128)} %refs_0_.3, f32[8]{0:T(128)} %refs_1_.3, f32[8,4,16,512]{3,2,1,0:T(8,128)} %refs_2_.3, f32[4,16,512]{2,1,0:T(8,128)} %refs_3_.3, s32[8,4,16,512]{3,2,1,0:T(8,128)} %refs_4_.4), custom_call_target="tpu_custom_call" | custom-call | bytes 4194304 | tf_op jit(solution)/shard_map/prepare/pallas_call | solution.py:152
  5.1 0.1 collective-permute-start
  5.3 0.0 collective-permute-done.1.theirs_ref
  5.3 0.1 merge_far.2
  5.3 3.0 %collective-permute-start.5 = (f32[32,8,512]{2,1,0:T(8,128)S(1)}, f32[32,8,512]{2,1,0:T(8,128)S(1)}, u32[]{:S(2)}, u32[]{:S(2)}) collective-permute-start(f32[32,8,512]{2,1,0:T(8,128)S(1)} %get-tuple-element.30), channel_id=1, source_target_pairs={{0,2},{1,3},{2,0},{3,1},{4,6},{5,7},{6,4},{7,5},{8,10},{9,11},{10,... | collective-permute-start | bytes 1572872 | tf_op jit(solution)/shard_map/ppermute | solution.py:533
  8.3 1.6 %collective-permute-start.2 = (f32[8,512]{1,0:T(8,128)S(1)}, f32[8,512]{1,0:T(8,128)S(1)}, u32[]{:S(2)}, u32[]{:S(2)}) collective-permute-start(f32[8,512]{1,0:T(8,128)S(1)} %get-tuple-element.29), channel_id=1, source_target_pairs={{4,0},{5,1},{6,2},{7,3},{0,4},{1,5},{2,6},{3,7},{12,8},{13,9},{14,... | collective-permute-start | bytes 49160 | tf_op jit(solution)/shard_map/ppermute | solution.py:551
  9.9 2.2 %collective-permute-done.2 = f32[8,512]{1,0:T(8,128)S(1)} collective-permute-done((f32[8,512]{1,0:T(8,128)S(1)}, f32[8,512]{1,0:T(8,128)S(1)}, u32[]{:S(2)}, u32[]{:S(2)}) %collective-permute-start.2) | collective-permute-done | bytes 16416 | tf_op jit(solution)/shard_map/ppermute | solution.py:551
  12.1 2.6 %collective-permute-start.3 = (f32[8,512]{1,0:T(8,128)S(1)}, f32[8,512]{1,0:T(8,128)S(1)}, u32[]{:S(2)}, u32[]{:S(2)}) collective-permute-start(f32[8,512]{1,0:T(8,128)S(1)} %add.15), channel_id=1, source_target_pairs={{8,0},{9,1},{10,2},{11,3},{12,4},{13,5},{14,6},{15,7},{0,8},{1,9},... | collective-permute-start | bytes 49160 | tf_op jit(solution)/shard_map/ppermute | solution.py:551
  14.7 2.0 %collective-permute-done.3 = f32[8,512]{1,0:T(8,128)S(1)} collective-permute-done((f32[8,512]{1,0:T(8,128)S(1)}, f32[8,512]{1,0:T(8,128)S(1)}, u32[]{:S(2)}, u32[]{:S(2)}) %collective-permute-start.3) | collective-permute-done | bytes 16416 | tf_op jit(solution)/shard_map/ppermute | solution.py:551
  16.7 0.1 merge_far.3
  16.8 0.3 collective-permute-start.11
  17.0 0.0 collective-permute-done.theirs_ref
  17.0 0.1 merge_near.2.refs_0_
  17.1 1.3 %collective-permute-start.4 = (f32[33,8,512]{2,1,0:T(8,128)S(1)}, f32[33,8,512]{2,1,0:T(8,128)S(1)}, u32[]{:S(2)}, u32[]{:S(2)}) collective-permute-start(f32[33,8,512]{2,1,0:T(8,128)S(1)} %merge_near.2.refs_0_), channel_id=1, source_target_pairs={{2,6},{3,7},{4,0},{5,1},{6,10},{7,11},{8,4},{9,5},{10,14},{11,15},... | collective-permute-start | bytes 1622024 | tf_op jit(solution)/shard_map/ppermute | solution.py:542
  18.4 2.7 %collective-permute-done.5.refs_2_ = f32[32,8,512]{2,1,0:T(8,128)S(1)} collective-permute-done((f32[32,8,512]{2,1,0:T(8,128)S(1)}, f32[32,8,512]{2,1,0:T(8,128)S(1)}, u32[]{:S(2)}, u32[]{:S(2)}) %collective-permute-start.5) | collective-permute-done | bytes 524320 | tf_op jit(solution)/shard_map/ppermute | solution.py:533
  21.0 4.1 %collective-permute-start.6 = (f32[32,8,512]{2,1,0:T(8,128)S(1)}, f32[32,8,512]{2,1,0:T(8,128)S(1)}, u32[]{:S(2)}, u32[]{:S(2)}) collective-permute-start(f32[32,8,512]{2,1,0:T(8,128)S(1)} %collective-permute-done.5.refs_2_), channel_id=1, source_target_pairs={{0,4},{1,5},{4,8},{5,9},{6,2},{7,3},{8,12},{9,13},{10,6},{11,7},{1... | collective-permute-start | bytes 1572872 | tf_op jit(solution)/shard_map/ppermute | solution.py:542
  25.1 0.1 merge_near.3.refs_0_
  25.2 1.3 %collective-permute-start.10 = (f32[33,8,512]{2,1,0:T(8,128)S(1)}, f32[33,8,512]{2,1,0:T(8,128)S(1)}, u32[]{:S(2)}, u32[]{:S(2)}) collective-permute-start(f32[33,8,512]{2,1,0:T(8,128)S(1)} %merge_near.3.refs_0_), channel_id=1, source_target_pairs={{2,6},{3,7},{4,0},{5,1},{6,10},{7,11},{8,4},{9,5},{10,14},{11,15},... | collective-permute-start | bytes 1622024 | tf_op jit(solution)/shard_map/ppermute | solution.py:542
  26.5 5.5 %collective-permute-done.11.refs_2_ = f32[33,8,512]{2,1,0:T(8,128)S(1)} collective-permute-done((f32[33,8,512]{2,1,0:T(8,128)S(1)}, f32[33,8,512]{2,1,0:T(8,128)S(1)}, u32[]{:S(2)}, u32[]{:S(2)}) %collective-permute-start.11) | collective-permute-done | bytes 540704 | tf_op jit(solution)/shard_map/ppermute | solution.py:533
  32.0 3.8 %collective-permute-start.12 = (f32[33,8,512]{2,1,0:T(8,128)S(1)}, f32[33,8,512]{2,1,0:T(8,128)S(1)}, u32[]{:S(2)}, u32[]{:S(2)}) collective-permute-start(f32[33,8,512]{2,1,0:T(8,128)S(1)} %collective-permute-done.11.refs_2_), channel_id=1, source_target_pairs={{0,4},{1,5},{4,8},{5,9},{6,2},{7,3},{8,12},{9,13},{10,6},{11,7},{1... | collective-permute-start | bytes 1622024 | tf_op jit(solution)/shard_map/ppermute | solution.py:542
  35.8 0.0 collective-permute-done.4.refs_1_
  35.8 6.3 %solve.2 = (f32[8,8,512]{2,1,0:T(8,128)S(1)}, f32[8,8,512]{2,1,0:T(8,128)S(1)}, f32[8,8,512]{2,1,0:T(8,128)S(1)}, f32[8,8,512]{2,1,0:T(8,128)S(1)}, f32[16,512]{1,0:T(8,128)S(1)}) custom-call(f32[33,8,512]{2,1,0:T(8,128)S(1)} %merge_near.2.refs_0_, f32[33,8,512]{2,1,0:T(8,128)S(1)} %collective-permute-done.4.refs_1_, ...), custom_call_target="tpu_custom_call" | custom-call | bytes 23068672 | tf_op jit(solution)/shard_map/solve/pallas_call | solution.py:374
  42.1 0.1 collective-permute-start.7
  42.2 1.3 %collective-permute-start.8 = (f32[8,8,512]{2,1,0:T(8,128)S(1)}, f32[8,8,512]{2,1,0:T(8,128)S(1)}, u32[]{:S(2)}, u32[]{:S(2)}) collective-permute-start(f32[8,8,512]{2,1,0:T(8,128)S(1)} %get-tuple-element.33), channel_id=1, source_target_pairs={{0,2},{1,3},{2,0},{3,1},{4,6},{5,7},{6,4},{7,5},{8,10},{9,11},{10,... | collective-permute-start | bytes 393224 | tf_op jit(solution)/shard_map/ppermute | solution.py:533
  43.5 0.5 collective-permute-start.9
  44.0 0.0 collective-permute-done.10.refs_1_
  44.0 2.6 %collective-permute-done.12.refs_3_ = f32[33,8,512]{2,1,0:T(8,128)S(1)} collective-permute-done((f32[33,8,512]{2,1,0:T(8,128)S(1)}, f32[33,8,512]{2,1,0:T(8,128)S(1)}, u32[]{:S(2)}, u32[]{:S(2)}) %collective-permute-start.12) | collective-permute-done | bytes 540704 | tf_op jit(solution)/shard_map/ppermute | solution.py:542
  46.6 6.3 %solve.3 = (f32[8,8,512]{2,1,0:T(8,128)S(1)}, f32[8,8,512]{2,1,0:T(8,128)S(1)}, f32[8,8,512]{2,1,0:T(8,128)S(1)}, f32[8,8,512]{2,1,0:T(8,128)S(1)}, f32[16,512]{1,0:T(8,128)S(1)}) custom-call(f32[33,8,512]{2,1,0:T(8,128)S(1)} %merge_near.3.refs_0_, f32[33,8,512]{2,1,0:T(8,128)S(1)} %collective-permute-done.10.refs_1_, ...), custom_call_target="tpu_custom_call" | custom-call | bytes 23068672 | tf_op jit(solution)/shard_map/solve/pallas_call | solution.py:374
  52.9 0.0 copy-start
  52.9 0.0 collective-permute-done.7.refs_1_.refs_4_
  52.9 0.0 collective-permute-done.8.refs_2_.refs_5_
  53.0 0.1 collective-permute-start.18
  53.0 2.5 %collective-permute-start.17 = (f32[16,512]{1,0:T(8,128)S(1)}, f32[16,512]{1,0:T(8,128)S(1)}, u32[]{:S(2)}, u32[]{:S(2)}) collective-permute-start(f32[16,512]{1,0:T(8,128)S(1)} %get-tuple-element.42), channel_id=1, source_target_pairs={{0,3},{1,2},{2,1},{3,0},{4,7},{5,6},{6,5},{7,4},{8,11},{9,10},{10,... | collective-permute-start | bytes 98312 | tf_op jit(solution)/shard_map/ppermute | solution.py:533
  55.6 0.0 collective-permute-start.16
  55.6 0.1 collective-permute-start.13
  55.7 1.9 %collective-permute-start.14 = (f32[8,8,512]{2,1,0:T(8,128)S(1)}, f32[8,8,512]{2,1,0:T(8,128)S(1)}, u32[]{:S(2)}, u32[]{:S(2)}) collective-permute-start(f32[8,8,512]{2,1,0:T(8,128)S(1)} %get-tuple-element.37), channel_id=1, source_target_pairs={{0,2},{1,3},{2,0},{3,1},{4,6},{5,7},{6,4},{7,5},{8,10},{9,11},{10,... | collective-permute-start | bytes 393224 | tf_op jit(solution)/shard_map/ppermute | solution.py:533
  57.6 0.1 collective-permute-start.15
  57.7 0.0 collective-permute-done.17
  57.7 2.1 %collective-permute-done.16 = f32[16,512]{1,0:T(8,128)S(1)} collective-permute-done((f32[16,512]{1,0:T(8,128)S(1)}, f32[16,512]{1,0:T(8,128)S(1)}, u32[]{:S(2)}, u32[]{:S(2)}) %collective-permute-start.16) | collective-permute-done | bytes 32800 | tf_op jit(solution)/shard_map/ppermute | solution.py:533
  59.8 1.6 %collective-permute-start.21 = (f32[1,16,512]{2,1,0:T(8,128)S(1)}, f32[1,16,512]{2,1,0:T(8,128)S(1)}, u32[]{:S(2)}, u32[]{:S(2)}) collective-permute-start(f32[1,16,512]{2,1,0:T(8,128)S(1)} %add_bitcast_fusion.refs_0_), channel_id=1, source_target_pairs={{12,0},{13,1},{14,2},{15,3},{0,4},{1,5},{2,6},{3,7},{4,8},{5,9},{6... | collective-permute-start | bytes 98312 | tf_op jit(solution)/shard_map/ppermute | solution.py:551
  61.4 1.3 %collective-permute-start.20 = (f32[1,16,512]{2,1,0:T(8,128)S(1)}, f32[1,16,512]{2,1,0:T(8,128)S(1)}, u32[]{:S(2)}, u32[]{:S(2)}) collective-permute-start(f32[1,16,512]{2,1,0:T(8,128)S(1)} %add_bitcast_fusion.refs_0_), channel_id=1, source_target_pairs={{8,0},{9,1},{10,2},{11,3},{12,4},{13,5},{14,6},{15,7},{0,8},{1,9},... | collective-permute-start | bytes 98312 | tf_op jit(solution)/shard_map/ppermute | solution.py:551
  62.6 0.0 collective-permute-done.13.refs_5_
  62.6 2.7 %collective-permute-start.19 = (f32[1,16,512]{2,1,0:T(8,128)S(1)}, f32[1,16,512]{2,1,0:T(8,128)S(1)}, u32[]{:S(2)}, u32[]{:S(2)}) collective-permute-start(f32[1,16,512]{2,1,0:T(8,128)S(1)} %add_bitcast_fusion.refs_0_), channel_id=1, source_target_pairs={{4,0},{5,1},{6,2},{7,3},{8,4},{9,5},{10,6},{11,7},{12,8},{13,9},{1... | collective-permute-start | bytes 98312 | tf_op jit(solution)/shard_map/ppermute | solution.py:551
  65.3 0.5 slice_bitcast_fusion.1
  65.9 1.1 %gather_adjoint.1 = (f32[8,4,16,512]{3,2,1,0:T(8,128)}, f32[8,128]{1,0:T(8,128)S(1)}) custom-call(f32[8,8,512]{2,1,0:T(8,128)S(1)} %get-tuple-element.31.refs_0_, f32[8,8,512]{2,1,0:T(8,128)S(1)} %collective-permute-done.7.refs_1_.refs_4_, f32[8,8,512]{2,1,0:T(8,128)S(1)} %collective-permute-done.8.refs_2_.refs_5_, ...), custom_call_target="tpu_custom_call" | custom-call | bytes 4194304 | tf_op jit(solution)/shard_map/gather_adjoint/pallas_call | solution.py:456
  67.0 1.5 %control.1 = f32[32,512]{1,0:T(8,128)} custom-call(f32[1,16,512]{2,1,0:T(8,128)S(1)} %add_bitcast_fusion.refs_0_, f32[1,16,512]{2,1,0:T(8,128)S(1)} %collective-permute-done.19.refs_1_, f32[1,16,512]{2,1,0:T(8,128)S(1)} %collective-permute-done.20.refs_2_, f32[1,16,512]{2,1,0:T(8,128)S(1)} %collective-permute-done.21.refs_3_, f32[16,32,64]{2,1,0:T(8,128)S(1)} %copy-done.1, ...), custom_call_target="tpu_custom_call" | custom-call | tf_op jit(solution)/shard_map/control/pallas_call | solution.py:505
  (16 shorter events, 0.1 us)
Async XLA Ops:
  2.9 2.3 %collective-permute-start.1 = (f32[33,8,512]{2,1,0:T(8,128)S(1)}, f32[33,8,512]{2,1,0:T(8,128)S(1)}, u32[]{:S(2)}, u32[]{:S(2)}) collective-permute-start(f32[33,8,512]{2,1,0:T(8,128)S(1)} %get-tuple-element.27), channel_id=1, source_target_pairs={{0,1},{1,0},{2,3},{3,2},{4,5},{5,4},{6,7},{7,6},{8,9},{9,8},{10,11... | collective-permute-start | bytes 1622024 | tf_op jit(solution)/shard_map/ppermute | solution.py:533
  5.1 11.9 %collective-permute-start = (f32[32,8,512]{2,1,0:T(8,128)S(1)}, f32[32,8,512]{2,1,0:T(8,128)S(1)}, u32[]{:S(2)}, u32[]{:S(2)}) collective-permute-start(f32[32,8,512]{2,1,0:T(8,128)S(1)} %get-tuple-element.25), channel_id=1, source_target_pairs={{0,1},{1,0},{2,3},{3,2},{4,5},{5,4},{6,7},{7,6},{8,9},{9,8},{10,11... | collective-permute-start | bytes 1572872 | tf_op jit(solution)/shard_map/ppermute | solution.py:533
  5.3 15.7 %collective-permute-start.5 = (f32[32,8,512]{2,1,0:T(8,128)S(1)}, f32[32,8,512]{2,1,0:T(8,128)S(1)}, u32[]{:S(2)}, u32[]{:S(2)}) collective-permute-start(f32[32,8,512]{2,1,0:T(8,128)S(1)} %get-tuple-element.30), channel_id=1, source_target_pairs={{0,2},{1,3},{2,0},{3,1},{4,6},{5,7},{6,4},{7,5},{8,10},{9,11},{10,... | collective-permute-start | bytes 1572872 | tf_op jit(solution)/shard_map/ppermute | solution.py:533
  8.3 3.7 %collective-permute-start.2 = (f32[8,512]{1,0:T(8,128)S(1)}, f32[8,512]{1,0:T(8,128)S(1)}, u32[]{:S(2)}, u32[]{:S(2)}) collective-permute-start(f32[8,512]{1,0:T(8,128)S(1)} %get-tuple-element.29), channel_id=1, source_target_pairs={{4,0},{5,1},{6,2},{7,3},{0,4},{1,5},{2,6},{3,7},{12,8},{13,9},{14,... | collective-permute-start | bytes 49160 | tf_op jit(solution)/shard_map/ppermute | solution.py:551
  12.1 4.6 %collective-permute-start.3 = (f32[8,512]{1,0:T(8,128)S(1)}, f32[8,512]{1,0:T(8,128)S(1)}, u32[]{:S(2)}, u32[]{:S(2)}) collective-permute-start(f32[8,512]{1,0:T(8,128)S(1)} %add.15), channel_id=1, source_target_pairs={{8,0},{9,1},{10,2},{11,3},{12,4},{13,5},{14,6},{15,7},{0,8},{1,9},... | collective-permute-start | bytes 49160 | tf_op jit(solution)/shard_map/ppermute | solution.py:551
  16.8 15.3 %collective-permute-start.11 = (f32[33,8,512]{2,1,0:T(8,128)S(1)}, f32[33,8,512]{2,1,0:T(8,128)S(1)}, u32[]{:S(2)}, u32[]{:S(2)}) collective-permute-start(f32[33,8,512]{2,1,0:T(8,128)S(1)} %merge_far.3), channel_id=1, source_target_pairs={{0,2},{1,3},{2,0},{3,1},{4,6},{5,7},{6,4},{7,5},{8,10},{9,11},{10,... | collective-permute-start | bytes 1622024 | tf_op jit(solution)/shard_map/ppermute | solution.py:533
  17.1 18.7 %collective-permute-start.4 = (f32[33,8,512]{2,1,0:T(8,128)S(1)}, f32[33,8,512]{2,1,0:T(8,128)S(1)}, u32[]{:S(2)}, u32[]{:S(2)}) collective-permute-start(f32[33,8,512]{2,1,0:T(8,128)S(1)} %merge_near.2.refs_0_), channel_id=1, source_target_pairs={{2,6},{3,7},{4,0},{5,1},{6,10},{7,11},{8,4},{9,5},{10,14},{11,15},... | collective-permute-start | bytes 1622024 | tf_op jit(solution)/shard_map/ppermute | solution.py:542
  21.0 14.7 %collective-permute-start.6 = (f32[32,8,512]{2,1,0:T(8,128)S(1)}, f32[32,8,512]{2,1,0:T(8,128)S(1)}, u32[]{:S(2)}, u32[]{:S(2)}) collective-permute-start(f32[32,8,512]{2,1,0:T(8,128)S(1)} %collective-permute-done.5.refs_2_), channel_id=1, source_target_pairs={{0,4},{1,5},{4,8},{5,9},{6,2},{7,3},{8,12},{9,13},{10,6},{11,7},{1... | collective-permute-start | bytes 1572872 | tf_op jit(solution)/shard_map/ppermute | solution.py:542
  25.2 18.9 %collective-permute-start.10 = (f32[33,8,512]{2,1,0:T(8,128)S(1)}, f32[33,8,512]{2,1,0:T(8,128)S(1)}, u32[]{:S(2)}, u32[]{:S(2)}) collective-permute-start(f32[33,8,512]{2,1,0:T(8,128)S(1)} %merge_near.3.refs_0_), channel_id=1, source_target_pairs={{2,6},{3,7},{4,0},{5,1},{6,10},{7,11},{8,4},{9,5},{10,14},{11,15},... | collective-permute-start | bytes 1622024 | tf_op jit(solution)/shard_map/ppermute | solution.py:542
  32.0 14.6 %collective-permute-start.12 = (f32[33,8,512]{2,1,0:T(8,128)S(1)}, f32[33,8,512]{2,1,0:T(8,128)S(1)}, u32[]{:S(2)}, u32[]{:S(2)}) collective-permute-start(f32[33,8,512]{2,1,0:T(8,128)S(1)} %collective-permute-done.11.refs_2_), channel_id=1, source_target_pairs={{0,4},{1,5},{4,8},{5,9},{6,2},{7,3},{8,12},{9,13},{10,6},{11,7},{1... | collective-permute-start | bytes 1622024 | tf_op jit(solution)/shard_map/ppermute | solution.py:542
  42.1 10.8 %collective-permute-start.7 = (f32[8,8,512]{2,1,0:T(8,128)S(1)}, f32[8,8,512]{2,1,0:T(8,128)S(1)}, u32[]{:S(2)}, u32[]{:S(2)}) collective-permute-start(f32[8,8,512]{2,1,0:T(8,128)S(1)} %get-tuple-element.32), channel_id=1, source_target_pairs={{0,1},{1,0},{2,3},{3,2},{4,5},{5,4},{6,7},{7,6},{8,9},{9,8},{10,11... | collective-permute-start | bytes 393224 | tf_op jit(solution)/shard_map/ppermute | solution.py:533
  42.2 10.7 %collective-permute-start.8 = (f32[8,8,512]{2,1,0:T(8,128)S(1)}, f32[8,8,512]{2,1,0:T(8,128)S(1)}, u32[]{:S(2)}, u32[]{:S(2)}) collective-permute-start(f32[8,8,512]{2,1,0:T(8,128)S(1)} %get-tuple-element.33), channel_id=1, source_target_pairs={{0,2},{1,3},{2,0},{3,1},{4,6},{5,7},{6,4},{7,5},{8,10},{9,11},{10,... | collective-permute-start | bytes 393224 | tf_op jit(solution)/shard_map/ppermute | solution.py:533
  43.5 9.4 %collective-permute-start.9 = (f32[8,8,512]{2,1,0:T(8,128)S(1)}, f32[8,8,512]{2,1,0:T(8,128)S(1)}, u32[]{:S(2)}, u32[]{:S(2)}) collective-permute-start(f32[8,8,512]{2,1,0:T(8,128)S(1)} %get-tuple-element.34), channel_id=1, source_target_pairs={{0,3},{1,2},{2,1},{3,0},{4,7},{5,6},{6,5},{7,4},{8,11},{9,10},{10,... | collective-permute-start | bytes 393224 | tf_op jit(solution)/shard_map/ppermute | solution.py:533
  52.9 14.1 %copy-start = (f32[512,512]{1,0:T(8,128)S(1)}, f32[512,512]{1,0:T(8,128)}, u32[]{:S(2)}) copy-start(f32[512,512]{1,0:T(8,128)} %constant.5.clone.refs_5_) | copy-start | bytes 3145732
  53.0 4.6 %collective-permute-start.18 = (f32[16,512]{1,0:T(8,128)S(1)}, f32[16,512]{1,0:T(8,128)S(1)}, u32[]{:S(2)}, u32[]{:S(2)}) collective-permute-start(f32[16,512]{1,0:T(8,128)S(1)} %get-tuple-element.42), channel_id=1, source_target_pairs={{0,1},{1,0},{2,3},{3,2},{4,5},{5,4},{6,7},{7,6},{8,9},{9,8},{10,11... | collective-permute-start | bytes 98312 | tf_op jit(solution)/shard_map/ppermute | solution.py:533
  53.0 4.7 %collective-permute-start.17 = (f32[16,512]{1,0:T(8,128)S(1)}, f32[16,512]{1,0:T(8,128)S(1)}, u32[]{:S(2)}, u32[]{:S(2)}) collective-permute-start(f32[16,512]{1,0:T(8,128)S(1)} %get-tuple-element.42), channel_id=1, source_target_pairs={{0,3},{1,2},{2,1},{3,0},{4,7},{5,6},{6,5},{7,4},{8,11},{9,10},{10,... | collective-permute-start | bytes 98312 | tf_op jit(solution)/shard_map/ppermute | solution.py:533
  55.6 4.3 %collective-permute-start.16 = (f32[16,512]{1,0:T(8,128)S(1)}, f32[16,512]{1,0:T(8,128)S(1)}, u32[]{:S(2)}, u32[]{:S(2)}) collective-permute-start(f32[16,512]{1,0:T(8,128)S(1)} %get-tuple-element.42), channel_id=1, source_target_pairs={{0,2},{1,3},{2,0},{3,1},{4,6},{5,7},{6,4},{7,5},{8,10},{9,11},{10,... | collective-permute-start | bytes 98312 | tf_op jit(solution)/shard_map/ppermute | solution.py:533
  55.6 7.0 %collective-permute-start.13 = (f32[8,8,512]{2,1,0:T(8,128)S(1)}, f32[8,8,512]{2,1,0:T(8,128)S(1)}, u32[]{:S(2)}, u32[]{:S(2)}) collective-permute-start(f32[8,8,512]{2,1,0:T(8,128)S(1)} %get-tuple-element.36), channel_id=1, source_target_pairs={{0,1},{1,0},{2,3},{3,2},{4,5},{5,4},{6,7},{7,6},{8,9},{9,8},{10,11... | collective-permute-start | bytes 393224 | tf_op jit(solution)/shard_map/ppermute | solution.py:533
  55.7 10.2 %collective-permute-start.14 = (f32[8,8,512]{2,1,0:T(8,128)S(1)}, f32[8,8,512]{2,1,0:T(8,128)S(1)}, u32[]{:S(2)}, u32[]{:S(2)}) collective-permute-start(f32[8,8,512]{2,1,0:T(8,128)S(1)} %get-tuple-element.37), channel_id=1, source_target_pairs={{0,2},{1,3},{2,0},{3,1},{4,6},{5,7},{6,4},{7,5},{8,10},{9,11},{10,... | collective-permute-start | bytes 393224 | tf_op jit(solution)/shard_map/ppermute | solution.py:533
  57.6 8.3 %collective-permute-start.15 = (f32[8,8,512]{2,1,0:T(8,128)S(1)}, f32[8,8,512]{2,1,0:T(8,128)S(1)}, u32[]{:S(2)}, u32[]{:S(2)}) collective-permute-start(f32[8,8,512]{2,1,0:T(8,128)S(1)} %get-tuple-element.38), channel_id=1, source_target_pairs={{0,3},{1,2},{2,1},{3,0},{4,7},{5,6},{6,5},{7,4},{8,11},{9,10},{10,... | collective-permute-start | bytes 393224 | tf_op jit(solution)/shard_map/ppermute | solution.py:533
  59.8 7.1 %collective-permute-start.21 = (f32[1,16,512]{2,1,0:T(8,128)S(1)}, f32[1,16,512]{2,1,0:T(8,128)S(1)}, u32[]{:S(2)}, u32[]{:S(2)}) collective-permute-start(f32[1,16,512]{2,1,0:T(8,128)S(1)} %add_bitcast_fusion.refs_0_), channel_id=1, source_target_pairs={{12,0},{13,1},{14,2},{15,3},{0,4},{1,5},{2,6},{3,7},{4,8},{5,9},{6... | collective-permute-start | bytes 98312 | tf_op jit(solution)/shard_map/ppermute | solution.py:551
  61.4 5.5 %collective-permute-start.20 = (f32[1,16,512]{2,1,0:T(8,128)S(1)}, f32[1,16,512]{2,1,0:T(8,128)S(1)}, u32[]{:S(2)}, u32[]{:S(2)}) collective-permute-start(f32[1,16,512]{2,1,0:T(8,128)S(1)} %add_bitcast_fusion.refs_0_), channel_id=1, source_target_pairs={{8,0},{9,1},{10,2},{11,3},{12,4},{13,5},{14,6},{15,7},{0,8},{1,9},... | collective-permute-start | bytes 98312 | tf_op jit(solution)/shard_map/ppermute | solution.py:551
  62.6 4.3 %collective-permute-start.19 = (f32[1,16,512]{2,1,0:T(8,128)S(1)}, f32[1,16,512]{2,1,0:T(8,128)S(1)}, u32[]{:S(2)}, u32[]{:S(2)}) collective-permute-start(f32[1,16,512]{2,1,0:T(8,128)S(1)} %add_bitcast_fusion.refs_0_), channel_id=1, source_target_pairs={{4,0},{5,1},{6,2},{7,3},{8,4},{9,5},{10,6},{11,7},{12,8},{13,9},{1... | collective-permute-start | bytes 98312 | tf_op jit(solution)/shard_map/ppermute | solution.py:551
  65.9 1.1 %copy-start.1 = (f32[16,32,64]{2,1,0:T(8,128)S(1)}, f32[16,32,64]{2,1,0:T(8,128)}, u32[]{:S(2)}) copy-start(f32[16,32,64]{2,1,0:T(8,128)} %constant.4.clone.refs_4_) | copy-start | bytes 393220

commit v12 on v11

--- a/solution.py
+++ b/solution.py
@@ -47,6 +47,11 @@
     )
     angle = product_index.astype(np.float64) * (math.pi / (4 * length_total))
     return (math.sqrt(2.0 / length_total) * np.cos(angle)).astype(np.float32)
+
+
+def in_halves(values):
+    high = values.astype(jnp.bfloat16)
+    return high, (values - high.astype(F32)).astype(jnp.bfloat16)
 
 
 def team_place():
@@ -170,49 +175,81 @@
     )(log_table, obs_scale, state, target, rock_type)
 
 
-def merge_far(mine, theirs, slot, size, sums, add=False):
+def merge(mine, theirs, slot, size, behind=None, add=None):
+    given = [value for value in (behind, add) if value is not None]
+
+    def kernel(mine_ref, theirs_ref, *refs):
+        core = lax.rem(team_place(), 2)
+        tail, (out_ref, *more) = refs[: len(given)], refs[len(given) :]
+        for ref, at in ((mine_ref, core), (theirs_ref, 1 - core)):
+            for n in range(size):
+                out_ref[at * size + n] = ref[slot * size + n]
+        if behind is not None:
+            out_ref[2 * size] = tail[0][...]
+        if add is not None:
+            more[0][...] = tail[-1][...] + theirs_ref[theirs.shape[0] - 1]
+
+    vmem = pl.BlockSpec(memory_space=pltpu.VMEM)
     tile = mine.shape[1:]
-
-    def kernel(mine_ref, theirs_ref, sums_ref, out_ref, *more):
+    outs = pl.pallas_call(
+        kernel,
+        out_shape=[jax.ShapeDtypeStruct((2 * size + (behind is not None),) + tile, F32)]
+        + [jax.ShapeDtypeStruct(tile, F32)] * (add is not None),
+        in_specs=[vmem] * (2 + len(given)),
+        out_specs=[vmem] * (1 + (add is not None)),
+        compiler_params=pltpu.CompilerParams(vmem_limit_bytes=4 * MIB),
+        name="merge",
+    )(mine, theirs, *given)
+    return outs if add is not None else outs[0]
+
+
+def copy_trimmed(ref, out_ref, size, below):
+    part = size // 2
+    for core in range(2):
+        for n in range(part):
+            out_ref[core * part + n] = ref[core * size + n]
+    for n in range(size - 2):
+        at = n + jnp.where(below, 2, 0)
+        out_ref[size + n] = ref[(at // part) * size + part + lax.rem(at, part)]
+
+
+def trim(blocks, size):
+    def kernel(ref, out_ref):
+        copy_trimmed(ref, out_ref, size, team_place() < 2)
+
+    vmem = pl.BlockSpec(memory_space=pltpu.VMEM)
+    return pl.pallas_call(
+        kernel,
+        out_shape=jax.ShapeDtypeStruct((2 * size - 2,) + blocks.shape[1:], F32),
+        in_specs=[vmem],
+        out_specs=vmem,
+        compiler_params=pltpu.CompilerParams(vmem_limit_bytes=4 * MIB),
+        name="trim",
+    )(blocks)
+
+
+def merge_near(mine, theirs, slot, size, after):
+    tile = mine.shape[1:]
+
+    def kernel(mine_ref, theirs_ref, _, out_ref, trimmed_ref):
         core = lax.rem(team_place(), 2)
         for ref, at in ((mine_ref, core), (theirs_ref, 1 - core)):
             for n in range(size):
                 out_ref[at * size + n] = ref[slot * size + n]
-        if add:
-            more[0][...] = sums_ref[...] + theirs_ref[theirs.shape[0] - 1]
-        else:
-            out_ref[2 * size] = sums_ref[...]
-
-    vmem = pl.BlockSpec(memory_space=pltpu.VMEM)
-    shapes = [(2 * size,) + tile, tile] if add else [(2 * size + 1,) + tile]
-    outs = pl.pallas_call(
-        kernel,
-        out_shape=[jax.ShapeDtypeStruct(shape, F32) for shape in shapes],
-        in_specs=[vmem] * 3,
-        out_specs=[vmem] * len(shapes),
-        compiler_params=pltpu.CompilerParams(vmem_limit_bytes=4 * MIB),
-        name="merge_far",
-    )(mine, theirs, sums)
-    return outs if add else outs[0]
-
-
-def merge_near(mine, theirs, slot, size, sums):
-    def kernel(mine_ref, theirs_ref, sums_ref, out_ref):
-        core = lax.rem(team_place(), 2)
-        for ref, at in ((mine_ref, core), (theirs_ref, 1 - core)):
-            for n in range(size):
-                out_ref[at * size + n] = ref[slot * size + n]
-        out_ref[2 * size] = sums_ref[...]
+        copy_trimmed(out_ref, trimmed_ref, size, team_place() >= 2)
 
     vmem = pl.BlockSpec(memory_space=pltpu.VMEM)
     return pl.pallas_call(
         kernel,
-        out_shape=jax.ShapeDtypeStruct((2 * size + 1,) + mine.shape[1:], F32),
-        in_specs=[vmem] * 3,
-        out_specs=vmem,
+        out_shape=[
+            jax.ShapeDtypeStruct((2 * size,) + tile, F32),
+            jax.ShapeDtypeStruct((2 * size - 2,) + tile, F32),
+        ],
+        in_specs=[vmem] * 2 + [pl.BlockSpec(memory_space=pl.ANY)],
+        out_specs=[vmem] * 2,
         compiler_params=pltpu.CompilerParams(vmem_limit_bytes=4 * MIB),
         name="merge_near",
-    )(mine, theirs, sums)
+    )(mine, theirs, after)
 
 
 def reciprocal(x):
@@ -262,18 +299,17 @@
             return jnp.where(v > 0.0, v, 1e30)
 
         for core in range(2):
-            for j in range(planes):
-                for t in range(2):
-                    n = 2 * j + t
-                    own_base = halo + planes * core + j
-                    for ref, base in (
-                        (ins[0], own_base + part * side),
-                        (ins[1], near_base + planes * core + j),
-                        (ins[2], own_base + part * (1 - side)),
-                        (ins[3], far_base + planes * core + j),
-                    ):
-                        cond[base, t] = outside(ref[core * 2 * part + n])
-                        t_a[base, t] = ref[(core * 2 + 1) * part + n]
+            for n in range(part):
+                base = halo + planes * core + n // 2
+                for ref, at in ((ins[0], base + part * side), (ins[2], base + part * (1 - side))):
+                    cond[at, n % 2] = outside(ref[core * 2 * part + n])
+                    t_a[at, n % 2] = ref[(core * 2 + 1) * part + n]
+        for ref, at in ((ins[1], near_base), (ins[3], far_base)):
+            skip = jnp.where(at == lower, 1, 0)
+            for n in range(2 * part):
+                cond[at + n // 2, n % 2] = outside(ref[n])
+            for n in range(2 * part - 2):
+                t_a[at + skip + n // 2, n % 2] = ref[2 * part + n]
 
         last_row = lax.broadcasted_iota(jnp.int32, (half, columns), 0) == half - 1
         last_column = lax.broadcasted_iota(jnp.int32, (half, columns), 1) == columns - 1
@@ -497,9 +533,12 @@
             precision=lax.Precision.HIGHEST,
             preferred_element_type=F32,
         )
-        out_ref[...] = jnp.dot(
-            along_z, x_ref[...], precision=lax.Precision.HIGHEST, preferred_element_type=F32
-        )
+        high, low = in_halves(along_z)
+        x_high, x_low = in_halves(x_ref[...])
+        both = jnp.concatenate([high, low], axis=0)
+        first = jnp.dot(both, x_high, preferred_element_type=F32)
+        second = jnp.dot(high, x_low, preferred_element_type=F32)
+        out_ref[...] = (first[:own_count] + first[own_count:]) + second
 
     vmem = pl.BlockSpec(memory_space=pltpu.VMEM)
     return pl.pallas_call(
@@ -559,7 +598,7 @@
     jobs = [[(slot, m) for slot in range(slots)] for m in range(TEAM)]
     mine, theirs, sums = prepare(jobs[2:], fields, with_sums=True)
     theirs = swap(theirs, 1)
-    first, sums = merge_far(mine, theirs, 0, size, sums, add=True)
+    first, sums = merge(mine, theirs, 0, size, add=sums)
     far = [swap(first, 2)]
     stride, teams = 1, slabs // TEAM
     while stride < teams:
@@ -569,14 +608,18 @@
 
     mine_near, theirs_near = prepare(jobs[:2], fields)
     theirs_near = swap(theirs_near, 1)
-    near = [merge_near(mine_near, theirs_near, slot, size, sums) for slot in range(slots)]
-    near_halo = [along(value, True) for value in near]
-    far += [swap(merge_far(mine, theirs, slot, size, sums), 2) for slot in range(1, slots)]
+    near, near_halo = [], []
+    for slot in range(slots):
+        blocks, trimmed = merge_near(mine_near, theirs_near, slot, size, sums)
+        near.append(blocks)
+        near_halo.append(along(trimmed, True))
+    for slot in range(1, slots):
+        far.append(swap(merge(mine, theirs, slot, size, sums), 2))
     sums = [sums, far[-1][2 * size]]
 
     pieces, faces = [], []
     for slot in range(slots):
-        far_halo = along(far[slot], False)
+        far_halo = along(trim(far[slot], size), False)
         solved = solve(near[slot], far[slot], near_halo[slot], far_halo, planes)
         pieces.append([solved[0]] + [swap(solved[m], m) for m in (1, 2, 3)])
         faces.append(solved[TEAM])

time: 68.7 us -> 68 us (0.990)
  starting transfers between devices: 30.7 us -> 29.8 us
    ppermute x5, waiting for transfers between devices: 4.22 us -> 6.71 us  [from_teams(): heard.append(lax.ppermute(value, 'gz', pairs))]
    ppermute x13, waiting for transfers between devices: 10.3 us -> 9.18 us  [swap(): return lax.ppermute(value, 'gz', [(i, i ^ m) for i in range(slabs)])]
    ppermute x4, waiting for transfers between devices: 2.58 us -> 1.53 us  [along(): return lax.ppermute(value, 'gz', pairs)]
    ppermute x5, starting transfers between devices: 9.66 us -> 8.83 us  [from_teams(): heard.append(lax.ppermute(value, 'gz', pairs))]
  transfers between devices with their start and end apart: 22 -> 22, of which waited for: 6 -> 9; matrix products, arithmetic and copies ran while one was open for 1% -> 1% of each run, Pallas kernels for 23% -> 23%
where the time goes in v12:
time: 68 us; the launch traced here: 67.8 us
  starting transfers between devices  29.8 us (44%)
  Pallas kernels  19.1 us (28%)
  waiting for transfers between devices  17.4 us (26%)
  between operations  0.84 us (1%)
    pallas_call x2, Pallas kernels, solve(): pl.pallas_call(kernel, out_shape=[jax.ShapeDtypeStruct((2 * planes, half,...  12.6 us
    ppermute x13, starting transfers between devices, swap(): return lax.ppermute(value, 'gz', [(i, i ^ m) for i in range(slabs)])  10.6 us
    ppermute x4, starting transfers between devices, along(): return lax.ppermute(value, 'gz', pairs)  10.4 us
    ppermute x13, waiting for transfers between devices, swap(): return lax.ppermute(value, 'gz', [(i, i ^ m) for i in range(slabs)])  9.18 us
    ppermute x5, starting transfers between devices, from_teams(): heard.append(lax.ppermute(value, 'gz', pairs))  8.83 us
    ppermute x5, waiting for transfers between devices, from_teams(): heard.append(lax.ppermute(value, 'gz', pairs))  6.71 us
    pallas_call x2, Pallas kernels, prepare(): pl.pallas_call(kernel, out_shape=[jax.ShapeDtypeStruct(shape, F32) for sh...  3.97 us
    ppermute x4, waiting for transfers between devices, along(): return lax.ppermute(value, 'gz', pairs)  1.53 us
  transfers between devices with their start and end apart: 22, of which 9 were waited for; matrix products, arithmetic and copies ran while one was open for 1% of the time, Pallas kernels for 23%

profile of v12, /device:TPU:0, one launch (start us, length us, event | category | flops | bytes accessed | tf_op | source)
XLA Modules:
  0.0 67.8 jit_solution(2914253921591439523)
XLA Ops:
  0.6 2.3 %prepare.3 = (f32[33,8,512]{2,1,0:T(8,128)S(1)}, f32[33,8,512]{2,1,0:T(8,128)S(1)}, f32[8,512]{1,0:T(8,128)S(1)}) custom-call(f32[8,8]{1,0:T(8,128)} %refs_0_.3, f32[8]{0:T(128)} %refs_1_.3, f32[8,4,16,512]{3,2,1,0:T(8,128)} %refs_2_.3, f32[4,16,512]{2,1,0:T(8,128)} %refs_3_.3, s32[8,4,16,512]{3,2,1,0:T(8,128)} %refs_4_.4), custom_call_target="tpu_custom_call" | custom-call | bytes 4194304 | tf_op jit(solution)/shard_map/prepare/pallas_call | solution.py:157
  2.9 0.5 collective-permute-start.1
  3.5 1.7 %prepare.2 = (f32[32,8,512]{2,1,0:T(8,128)S(1)}, f32[32,8,512]{2,1,0:T(8,128)S(1)}) custom-call(f32[8,8]{1,0:T(8,128)} %refs_0_.3, f32[8]{0:T(128)} %refs_1_.3, f32[8,4,16,512]{3,2,1,0:T(8,128)} %refs_2_.3, f32[4,16,512]{2,1,0:T(8,128)} %refs_3_.3, s32[8,4,16,512]{3,2,1,0:T(8,128)} %refs_4_.4), custom_call_target="tpu_custom_call" | custom-call | bytes 4194304 | tf_op jit(solution)/shard_map/prepare/pallas_call | solution.py:157
  5.1 0.1 collective-permute-start
  5.3 0.1 merge.2
  5.3 3.0 %collective-permute-start.5 = (f32[32,8,512]{2,1,0:T(8,128)S(1)}, f32[32,8,512]{2,1,0:T(8,128)S(1)}, u32[]{:S(2)}, u32[]{:S(2)}) collective-permute-start(f32[32,8,512]{2,1,0:T(8,128)S(1)} %get-tuple-element.36), channel_id=1, source_target_pairs={{0,2},{1,3},{2,0},{3,1},{4,6},{5,7},{6,4},{7,5},{8,10},{9,11},{10,... | collective-permute-start | bytes 1572872 | tf_op jit(solution)/shard_map/ppermute | solution.py:572
  8.3 1.6 %collective-permute-start.2 = (f32[8,512]{1,0:T(8,128)S(1)}, f32[8,512]{1,0:T(8,128)S(1)}, u32[]{:S(2)}, u32[]{:S(2)}) collective-permute-start(f32[8,512]{1,0:T(8,128)S(1)} %get-tuple-element.33), channel_id=1, source_target_pairs={{4,0},{5,1},{6,2},{7,3},{0,4},{1,5},{2,6},{3,7},{12,8},{13,9},{14,... | collective-permute-start | bytes 49160 | tf_op jit(solution)/shard_map/ppermute | solution.py:590
  9.9 2.2 %collective-permute-done.2 = f32[8,512]{1,0:T(8,128)S(1)} collective-permute-done((f32[8,512]{1,0:T(8,128)S(1)}, f32[8,512]{1,0:T(8,128)S(1)}, u32[]{:S(2)}, u32[]{:S(2)}) %collective-permute-start.2) | collective-permute-done | bytes 16416 | tf_op jit(solution)/shard_map/ppermute | solution.py:590
  12.1 2.6 %collective-permute-start.3 = (f32[8,512]{1,0:T(8,128)S(1)}, f32[8,512]{1,0:T(8,128)S(1)}, u32[]{:S(2)}, u32[]{:S(2)}) collective-permute-start(f32[8,512]{1,0:T(8,128)S(1)} %add.15), channel_id=1, source_target_pairs={{8,0},{9,1},{10,2},{11,3},{12,4},{13,5},{14,6},{15,7},{0,8},{1,9},... | collective-permute-start | bytes 49160 | tf_op jit(solution)/shard_map/ppermute | solution.py:590
  14.7 2.0 %collective-permute-done.3 = f32[8,512]{1,0:T(8,128)S(1)} collective-permute-done((f32[8,512]{1,0:T(8,128)S(1)}, f32[8,512]{1,0:T(8,128)S(1)}, u32[]{:S(2)}, u32[]{:S(2)}) %collective-permute-start.3) | collective-permute-done | bytes 16416 | tf_op jit(solution)/shard_map/ppermute | solution.py:590
  16.7 0.1 merge.3
  16.8 0.3 collective-permute-start.11
  17.0 0.0 collective-permute-done.theirs_ref
  17.0 0.1 merge_near.2
  17.1 1.3 %collective-permute-start.4 = (f32[30,8,512]{2,1,0:T(8,128)S(1)}, f32[30,8,512]{2,1,0:T(8,128)S(1)}, u32[]{:S(2)}, u32[]{:S(2)}) collective-permute-start(f32[30,8,512]{2,1,0:T(8,128)S(1)} %get-tuple-element.35), channel_id=1, source_target_pairs={{2,6},{3,7},{4,0},{5,1},{6,10},{7,11},{8,4},{9,5},{10,14},{11,15},... | collective-permute-start | bytes 1474568 | tf_op jit(solution)/shard_map/ppermute | solution.py:581
  18.4 2.6 %collective-permute-done.5.ref.refs_2_ = f32[32,8,512]{2,1,0:T(8,128)S(1)} collective-permute-done((f32[32,8,512]{2,1,0:T(8,128)S(1)}, f32[32,8,512]{2,1,0:T(8,128)S(1)}, u32[]{:S(2)}, u32[]{:S(2)}) %collective-permute-start.5) | collective-permute-done | bytes 524320 | tf_op jit(solution)/shard_map/ppermute | solution.py:572
  21.1 4.1 %collective-permute-start.6 = (f32[30,8,512]{2,1,0:T(8,128)S(1)}, f32[30,8,512]{2,1,0:T(8,128)S(1)}, u32[]{:S(2)}, u32[]{:S(2)}) collective-permute-start(f32[30,8,512]{2,1,0:T(8,128)S(1)} %trim.2), channel_id=1, source_target_pairs={{0,4},{1,5},{4,8},{5,9},{6,2},{7,3},{8,12},{9,13},{10,6},{11,7},{1... | collective-permute-start | bytes 1474568 | tf_op jit(solution)/shard_map/ppermute | solution.py:581
  25.2 0.1 merge_near.3
  25.3 1.3 %collective-permute-start.10 = (f32[30,8,512]{2,1,0:T(8,128)S(1)}, f32[30,8,512]{2,1,0:T(8,128)S(1)}, u32[]{:S(2)}, u32[]{:S(2)}) collective-permute-start(f32[30,8,512]{2,1,0:T(8,128)S(1)} %get-tuple-element.42), channel_id=1, source_target_pairs={{2,6},{3,7},{4,0},{5,1},{6,10},{7,11},{8,4},{9,5},{10,14},{11,15},... | collective-permute-start | bytes 1474568 | tf_op jit(solution)/shard_map/ppermute | solution.py:581
  26.6 5.4 %collective-permute-done.11.ref.refs_2_ = f32[33,8,512]{2,1,0:T(8,128)S(1)} collective-permute-done((f32[33,8,512]{2,1,0:T(8,128)S(1)}, f32[33,8,512]{2,1,0:T(8,128)S(1)}, u32[]{:S(2)}, u32[]{:S(2)}) %collective-permute-start.11) | collective-permute-done | bytes 540704 | tf_op jit(solution)/shard_map/ppermute | solution.py:572
  32.1 3.8 %collective-permute-start.12 = (f32[30,8,512]{2,1,0:T(8,128)S(1)}, f32[30,8,512]{2,1,0:T(8,128)S(1)}, u32[]{:S(2)}, u32[]{:S(2)}) collective-permute-start(f32[30,8,512]{2,1,0:T(8,128)S(1)} %trim.3), channel_id=1, source_target_pairs={{0,4},{1,5},{4,8},{5,9},{6,2},{7,3},{8,12},{9,13},{10,6},{11,7},{1... | collective-permute-start | bytes 1474568 | tf_op jit(solution)/shard_map/ppermute | solution.py:581
  35.8 0.0 collective-permute-done.4.refs_1_
  35.9 0.0 collective-permute-done.6.refs_3_
  35.9 6.3 %solve.2 = (f32[8,8,512]{2,1,0:T(8,128)S(1)}, f32[8,8,512]{2,1,0:T(8,128)S(1)}, f32[8,8,512]{2,1,0:T(8,128)S(1)}, f32[8,8,512]{2,1,0:T(8,128)S(1)}, f32[16,512]{1,0:T(8,128)S(1)}) custom-call(f32[32,8,512]{2,1,0:T(8,128)S(1)} %get-tuple-element.34.refs_0_, f32[30,8,512]{2,1,0:T(8,128)S(1)} %collective-permute-done.4.refs_1_, ...), custom_call_target="tpu_custom_call" | custom-call | bytes 23068672 | tf_op jit(solution)/shard_map/solve/pallas_call | solution.py:410
  42.1 0.1 collective-permute-start.7
  42.2 0.6 collective-permute-start.8
  42.9 1.2 %collective-permute-start.9 = (f32[8,8,512]{2,1,0:T(8,128)S(1)}, f32[8,8,512]{2,1,0:T(8,128)S(1)}, u32[]{:S(2)}, u32[]{:S(2)}) collective-permute-start(f32[8,8,512]{2,1,0:T(8,128)S(1)} %get-tuple-element.40), channel_id=1, source_target_pairs={{0,3},{1,2},{2,1},{3,0},{4,7},{5,6},{6,5},{7,4},{8,11},{9,10},{10,... | collective-permute-start | bytes 393224 | tf_op jit(solution)/shard_map/ppermute | solution.py:572
  44.1 0.0 collective-permute-done.10.refs_1_
  44.1 1.5 %collective-permute-done.12.refs_3_ = f32[30,8,512]{2,1,0:T(8,128)S(1)} collective-permute-done((f32[30,8,512]{2,1,0:T(8,128)S(1)}, f32[30,8,512]{2,1,0:T(8,128)S(1)}, u32[]{:S(2)}, u32[]{:S(2)}) %collective-permute-start.12) | collective-permute-done | bytes 491552 | tf_op jit(solution)/shard_map/ppermute | solution.py:581
  45.6 6.3 %solve.3 = (f32[8,8,512]{2,1,0:T(8,128)S(1)}, f32[8,8,512]{2,1,0:T(8,128)S(1)}, f32[8,8,512]{2,1,0:T(8,128)S(1)}, f32[8,8,512]{2,1,0:T(8,128)S(1)}, f32[16,512]{1,0:T(8,128)S(1)}) custom-call(f32[32,8,512]{2,1,0:T(8,128)S(1)} %get-tuple-element.41.refs_0_, f32[30,8,512]{2,1,0:T(8,128)S(1)} %collective-permute-done.10.refs_1_, ...), custom_call_target="tpu_custom_call" | custom-call | bytes 23068672 | tf_op jit(solution)/shard_map/solve/pallas_call | solution.py:410
  51.9 0.0 copy-start
  51.9 0.0 collective-permute-done.8.refs_2_.refs_5_
  51.9 0.0 collective-permute-done.9.refs_3_.refs_6_
  52.0 2.5 %collective-permute-start.16 = (f32[16,512]{1,0:T(8,128)S(1)}, f32[16,512]{1,0:T(8,128)S(1)}, u32[]{:S(2)}, u32[]{:S(2)}) collective-permute-start(f32[16,512]{1,0:T(8,128)S(1)} %get-tuple-element.50), channel_id=1, source_target_pairs={{0,2},{1,3},{2,0},{3,1},{4,6},{5,7},{6,4},{7,5},{8,10},{9,11},{10,... | collective-permute-start | bytes 98312 | tf_op jit(solution)/shard_map/ppermute | solution.py:572
  54.4 0.2 collective-permute-start.18
  54.6 0.3 collective-permute-start.13
  55.0 1.6 %collective-permute-start.14 = (f32[8,8,512]{2,1,0:T(8,128)S(1)}, f32[8,8,512]{2,1,0:T(8,128)S(1)}, u32[]{:S(2)}, u32[]{:S(2)}) collective-permute-start(f32[8,8,512]{2,1,0:T(8,128)S(1)} %get-tuple-element.45), channel_id=1, source_target_pairs={{0,2},{1,3},{2,0},{3,1},{4,6},{5,7},{6,4},{7,5},{8,10},{9,11},{10,... | collective-permute-start | bytes 393224 | tf_op jit(solution)/shard_map/ppermute | solution.py:572
  56.6 0.1 collective-permute-start.15
  56.7 1.0 %collective-permute-done.17 = f32[16,512]{1,0:T(8,128)S(1)} collective-permute-done((f32[16,512]{1,0:T(8,128)S(1)}, f32[16,512]{1,0:T(8,128)S(1)}, u32[]{:S(2)}, u32[]{:S(2)}) %collective-permute-start.17) | collective-permute-done | bytes 32800 | tf_op jit(solution)/shard_map/ppermute | solution.py:572
  57.8 2.8 %collective-permute-start.19 = (f32[1,16,512]{2,1,0:T(8,128)S(1)}, f32[1,16,512]{2,1,0:T(8,128)S(1)}, u32[]{:S(2)}, u32[]{:S(2)}) collective-permute-start(f32[1,16,512]{2,1,0:T(8,128)S(1)} %add_bitcast_fusion.refs_0_), channel_id=1, source_target_pairs={{4,0},{5,1},{6,2},{7,3},{8,4},{9,5},{10,6},{11,7},{12,8},{13,9},{1... | collective-permute-start | bytes 98312 | tf_op jit(solution)/shard_map/ppermute | solution.py:590
  60.6 0.3 collective-permute-start.20
  60.9 1.6 %collective-permute-start.21 = (f32[1,16,512]{2,1,0:T(8,128)S(1)}, f32[1,16,512]{2,1,0:T(8,128)S(1)}, u32[]{:S(2)}, u32[]{:S(2)}) collective-permute-start(f32[1,16,512]{2,1,0:T(8,128)S(1)} %add_bitcast_fusion.refs_0_), channel_id=1, source_target_pairs={{12,0},{13,1},{14,2},{15,3},{0,4},{1,5},{2,6},{3,7},{4,8},{5,9},{6... | collective-permute-start | bytes 98312 | tf_op jit(solution)/shard_map/ppermute | solution.py:590
  62.5 0.5 slice_bitcast_fusion.1
  63.0 0.1 collective-permute-done.15.refs_7_
  63.0 1.0 %gather_adjoint.1 = (f32[8,4,16,512]{3,2,1,0:T(8,128)}, f32[8,128]{1,0:T(8,128)S(1)}) custom-call(f32[8,8,512]{2,1,0:T(8,128)S(1)} %get-tuple-element.37.refs_0_, f32[8,8,512]{2,1,0:T(8,128)S(1)} %collective-permute-done.7.refs_1_.refs_4_, f32[8,8,512]{2,1,0:T(8,128)S(1)} %collective-permute-done.8.refs_2_.refs_5_, ...), custom_call_target="tpu_custom_call" | custom-call | bytes 4194304 | tf_op jit(solution)/shard_map/gather_adjoint/pallas_call | solution.py:492
  64.1 1.4 %collective-permute-done.20.refs_2_ = f32[1,16,512]{2,1,0:T(8,128)S(1)} collective-permute-done((f32[1,16,512]{2,1,0:T(8,128)S(1)}, f32[1,16,512]{2,1,0:T(8,128)S(1)}, u32[]{:S(2)}, u32[]{:S(2)}) %collective-permute-start.20) | collective-permute-done | bytes 32800 | tf_op jit(solution)/shard_map/ppermute | solution.py:590
  65.5 1.1 %collective-permute-done.21.refs_3_ = f32[1,16,512]{2,1,0:T(8,128)S(1)} collective-permute-done((f32[1,16,512]{2,1,0:T(8,128)S(1)}, f32[1,16,512]{2,1,0:T(8,128)S(1)}, u32[]{:S(2)}, u32[]{:S(2)}) %collective-permute-start.21) | collective-permute-done | bytes 32800 | tf_op jit(solution)/shard_map/ppermute | solution.py:590
  66.6 1.1 %control.1 = f32[32,512]{1,0:T(8,128)} custom-call(f32[1,16,512]{2,1,0:T(8,128)S(1)} %add_bitcast_fusion.refs_0_, f32[1,16,512]{2,1,0:T(8,128)S(1)} %collective-permute-done.19.refs_1_, f32[1,16,512]{2,1,0:T(8,128)S(1)} %collective-permute-done.20.refs_2_, f32[1,16,512]{2,1,0:T(8,128)S(1)} %collective-permute-done.21.refs_3_, f32[16,32,64]{2,1,0:T(8,128)S(1)} %copy-done.1, ...), custom_call_target="tpu_custom_call" | custom-call | tf_op jit(solution)/shard_map/control/pallas_call | solution.py:544
  (18 shorter events, 0.2 us)
Async XLA Ops:
  2.9 2.3 %collective-permute-start.1 = (f32[33,8,512]{2,1,0:T(8,128)S(1)}, f32[33,8,512]{2,1,0:T(8,128)S(1)}, u32[]{:S(2)}, u32[]{:S(2)}) collective-permute-start(f32[33,8,512]{2,1,0:T(8,128)S(1)} %get-tuple-element.31), channel_id=1, source_target_pairs={{0,1},{1,0},{2,3},{3,2},{4,5},{5,4},{6,7},{7,6},{8,9},{9,8},{10,11... | collective-permute-start | bytes 1622024 | tf_op jit(solution)/shard_map/ppermute | solution.py:572
  5.1 11.9 %collective-permute-start = (f32[32,8,512]{2,1,0:T(8,128)S(1)}, f32[32,8,512]{2,1,0:T(8,128)S(1)}, u32[]{:S(2)}, u32[]{:S(2)}) collective-permute-start(f32[32,8,512]{2,1,0:T(8,128)S(1)} %get-tuple-element.29), channel_id=1, source_target_pairs={{0,1},{1,0},{2,3},{3,2},{4,5},{5,4},{6,7},{7,6},{8,9},{9,8},{10,11... | collective-permute-start | bytes 1572872 | tf_op jit(solution)/shard_map/ppermute | solution.py:572
  5.3 15.7 %collective-permute-start.5 = (f32[32,8,512]{2,1,0:T(8,128)S(1)}, f32[32,8,512]{2,1,0:T(8,128)S(1)}, u32[]{:S(2)}, u32[]{:S(2)}) collective-permute-start(f32[32,8,512]{2,1,0:T(8,128)S(1)} %get-tuple-element.36), channel_id=1, source_target_pairs={{0,2},{1,3},{2,0},{3,1},{4,6},{5,7},{6,4},{7,5},{8,10},{9,11},{10,... | collective-permute-start | bytes 1572872 | tf_op jit(solution)/shard_map/ppermute | solution.py:572
  8.3 3.7 %collective-permute-start.2 = (f32[8,512]{1,0:T(8,128)S(1)}, f32[8,512]{1,0:T(8,128)S(1)}, u32[]{:S(2)}, u32[]{:S(2)}) collective-permute-start(f32[8,512]{1,0:T(8,128)S(1)} %get-tuple-element.33), channel_id=1, source_target_pairs={{4,0},{5,1},{6,2},{7,3},{0,4},{1,5},{2,6},{3,7},{12,8},{13,9},{14,... | collective-permute-start | bytes 49160 | tf_op jit(solution)/shard_map/ppermute | solution.py:590
  12.1 4.6 %collective-permute-start.3 = (f32[8,512]{1,0:T(8,128)S(1)}, f32[8,512]{1,0:T(8,128)S(1)}, u32[]{:S(2)}, u32[]{:S(2)}) collective-permute-start(f32[8,512]{1,0:T(8,128)S(1)} %add.15), channel_id=1, source_target_pairs={{8,0},{9,1},{10,2},{11,3},{12,4},{13,5},{14,6},{15,7},{0,8},{1,9},... | collective-permute-start | bytes 49160 | tf_op jit(solution)/shard_map/ppermute | solution.py:590
  16.8 15.3 %collective-permute-start.11 = (f32[33,8,512]{2,1,0:T(8,128)S(1)}, f32[33,8,512]{2,1,0:T(8,128)S(1)}, u32[]{:S(2)}, u32[]{:S(2)}) collective-permute-start(f32[33,8,512]{2,1,0:T(8,128)S(1)} %merge.3), channel_id=1, source_target_pairs={{0,2},{1,3},{2,0},{3,1},{4,6},{5,7},{6,4},{7,5},{8,10},{9,11},{10,... | collective-permute-start | bytes 1622024 | tf_op jit(solution)/shard_map/ppermute | solution.py:572
  17.1 18.7 %collective-permute-start.4 = (f32[30,8,512]{2,1,0:T(8,128)S(1)}, f32[30,8,512]{2,1,0:T(8,128)S(1)}, u32[]{:S(2)}, u32[]{:S(2)}) collective-permute-start(f32[30,8,512]{2,1,0:T(8,128)S(1)} %get-tuple-element.35), channel_id=1, source_target_pairs={{2,6},{3,7},{4,0},{5,1},{6,10},{7,11},{8,4},{9,5},{10,14},{11,15},... | collective-permute-start | bytes 1474568 | tf_op jit(solution)/shard_map/ppermute | solution.py:581
  21.1 14.8 %collective-permute-start.6 = (f32[30,8,512]{2,1,0:T(8,128)S(1)}, f32[30,8,512]{2,1,0:T(8,128)S(1)}, u32[]{:S(2)}, u32[]{:S(2)}) collective-permute-start(f32[30,8,512]{2,1,0:T(8,128)S(1)} %trim.2), channel_id=1, source_target_pairs={{0,4},{1,5},{4,8},{5,9},{6,2},{7,3},{8,12},{9,13},{10,6},{11,7},{1... | collective-permute-start | bytes 1474568 | tf_op jit(solution)/shard_map/ppermute | solution.py:581
  25.3 18.8 %collective-permute-start.10 = (f32[30,8,512]{2,1,0:T(8,128)S(1)}, f32[30,8,512]{2,1,0:T(8,128)S(1)}, u32[]{:S(2)}, u32[]{:S(2)}) collective-permute-start(f32[30,8,512]{2,1,0:T(8,128)S(1)} %get-tuple-element.42), channel_id=1, source_target_pairs={{2,6},{3,7},{4,0},{5,1},{6,10},{7,11},{8,4},{9,5},{10,14},{11,15},... | collective-permute-start | bytes 1474568 | tf_op jit(solution)/shard_map/ppermute | solution.py:581
  32.1 13.5 %collective-permute-start.12 = (f32[30,8,512]{2,1,0:T(8,128)S(1)}, f32[30,8,512]{2,1,0:T(8,128)S(1)}, u32[]{:S(2)}, u32[]{:S(2)}) collective-permute-start(f32[30,8,512]{2,1,0:T(8,128)S(1)} %trim.3), channel_id=1, source_target_pairs={{0,4},{1,5},{4,8},{5,9},{6,2},{7,3},{8,12},{9,13},{10,6},{11,7},{1... | collective-permute-start | bytes 1474568 | tf_op jit(solution)/shard_map/ppermute | solution.py:581
  42.1 9.8 %collective-permute-start.7 = (f32[8,8,512]{2,1,0:T(8,128)S(1)}, f32[8,8,512]{2,1,0:T(8,128)S(1)}, u32[]{:S(2)}, u32[]{:S(2)}) collective-permute-start(f32[8,8,512]{2,1,0:T(8,128)S(1)} %get-tuple-element.38), channel_id=1, source_target_pairs={{0,1},{1,0},{2,3},{3,2},{4,5},{5,4},{6,7},{7,6},{8,9},{9,8},{10,11... | collective-permute-start | bytes 393224 | tf_op jit(solution)/shard_map/ppermute | solution.py:572
  42.2 9.7 %collective-permute-start.8 = (f32[8,8,512]{2,1,0:T(8,128)S(1)}, f32[8,8,512]{2,1,0:T(8,128)S(1)}, u32[]{:S(2)}, u32[]{:S(2)}) collective-permute-start(f32[8,8,512]{2,1,0:T(8,128)S(1)} %get-tuple-element.39), channel_id=1, source_target_pairs={{0,2},{1,3},{2,0},{3,1},{4,6},{5,7},{6,4},{7,5},{8,10},{9,11},{10,... | collective-permute-start | bytes 393224 | tf_op jit(solution)/shard_map/ppermute | solution.py:572
  42.9 9.1 %collective-permute-start.9 = (f32[8,8,512]{2,1,0:T(8,128)S(1)}, f32[8,8,512]{2,1,0:T(8,128)S(1)}, u32[]{:S(2)}, u32[]{:S(2)}) collective-permute-start(f32[8,8,512]{2,1,0:T(8,128)S(1)} %get-tuple-element.40), channel_id=1, source_target_pairs={{0,3},{1,2},{2,1},{3,0},{4,7},{5,6},{6,5},{7,4},{8,11},{9,10},{10,... | collective-permute-start | bytes 393224 | tf_op jit(solution)/shard_map/ppermute | solution.py:572
  51.9 14.7 %copy-start = (f32[512,512]{1,0:T(8,128)S(1)}, f32[512,512]{1,0:T(8,128)}, u32[]{:S(2)}) copy-start(f32[512,512]{1,0:T(8,128)} %constant.5.clone.refs_5_) | copy-start | bytes 3145732
  52.0 4.6 %collective-permute-start.16 = (f32[16,512]{1,0:T(8,128)S(1)}, f32[16,512]{1,0:T(8,128)S(1)}, u32[]{:S(2)}, u32[]{:S(2)}) collective-permute-start(f32[16,512]{1,0:T(8,128)S(1)} %get-tuple-element.50), channel_id=1, source_target_pairs={{0,2},{1,3},{2,0},{3,1},{4,6},{5,7},{6,4},{7,5},{8,10},{9,11},{10,... | collective-permute-start | bytes 98312 | tf_op jit(solution)/shard_map/ppermute | solution.py:572
  54.4 3.3 %collective-permute-start.17 = (f32[16,512]{1,0:T(8,128)S(1)}, f32[16,512]{1,0:T(8,128)S(1)}, u32[]{:S(2)}, u32[]{:S(2)}) collective-permute-start(f32[16,512]{1,0:T(8,128)S(1)} %get-tuple-element.50), channel_id=1, source_target_pairs={{0,3},{1,2},{2,1},{3,0},{4,7},{5,6},{6,5},{7,4},{8,11},{9,10},{10,... | collective-permute-start | bytes 98312 | tf_op jit(solution)/shard_map/ppermute | solution.py:572
  54.4 3.3 %collective-permute-start.18 = (f32[16,512]{1,0:T(8,128)S(1)}, f32[16,512]{1,0:T(8,128)S(1)}, u32[]{:S(2)}, u32[]{:S(2)}) collective-permute-start(f32[16,512]{1,0:T(8,128)S(1)} %get-tuple-element.50), channel_id=1, source_target_pairs={{0,1},{1,0},{2,3},{3,2},{4,5},{5,4},{6,7},{7,6},{8,9},{9,8},{10,11... | collective-permute-start | bytes 98312 | tf_op jit(solution)/shard_map/ppermute | solution.py:572
  54.6 6.3 %collective-permute-start.13 = (f32[8,8,512]{2,1,0:T(8,128)S(1)}, f32[8,8,512]{2,1,0:T(8,128)S(1)}, u32[]{:S(2)}, u32[]{:S(2)}) collective-permute-start(f32[8,8,512]{2,1,0:T(8,128)S(1)} %get-tuple-element.44), channel_id=1, source_target_pairs={{0,1},{1,0},{2,3},{3,2},{4,5},{5,4},{6,7},{7,6},{8,9},{9,8},{10,11... | collective-permute-start | bytes 393224 | tf_op jit(solution)/shard_map/ppermute | solution.py:572
  55.0 8.0 %collective-permute-start.14 = (f32[8,8,512]{2,1,0:T(8,128)S(1)}, f32[8,8,512]{2,1,0:T(8,128)S(1)}, u32[]{:S(2)}, u32[]{:S(2)}) collective-permute-start(f32[8,8,512]{2,1,0:T(8,128)S(1)} %get-tuple-element.45), channel_id=1, source_target_pairs={{0,2},{1,3},{2,0},{3,1},{4,6},{5,7},{6,4},{7,5},{8,10},{9,11},{10,... | collective-permute-start | bytes 393224 | tf_op jit(solution)/shard_map/ppermute | solution.py:572
  56.6 6.5 %collective-permute-start.15 = (f32[8,8,512]{2,1,0:T(8,128)S(1)}, f32[8,8,512]{2,1,0:T(8,128)S(1)}, u32[]{:S(2)}, u32[]{:S(2)}) collective-permute-start(f32[8,8,512]{2,1,0:T(8,128)S(1)} %get-tuple-element.46), channel_id=1, source_target_pairs={{0,3},{1,2},{2,1},{3,0},{4,7},{5,6},{6,5},{7,4},{8,11},{9,10},{10,... | collective-permute-start | bytes 393224 | tf_op jit(solution)/shard_map/ppermute | solution.py:572
  57.8 6.3 %collective-permute-start.19 = (f32[1,16,512]{2,1,0:T(8,128)S(1)}, f32[1,16,512]{2,1,0:T(8,128)S(1)}, u32[]{:S(2)}, u32[]{:S(2)}) collective-permute-start(f32[1,16,512]{2,1,0:T(8,128)S(1)} %add_bitcast_fusion.refs_0_), channel_id=1, source_target_pairs={{4,0},{5,1},{6,2},{7,3},{8,4},{9,5},{10,6},{11,7},{12,8},{13,9},{1... | collective-permute-start | bytes 98312 | tf_op jit(solution)/shard_map/ppermute | solution.py:590
  60.6 4.9 %collective-permute-start.20 = (f32[1,16,512]{2,1,0:T(8,128)S(1)}, f32[1,16,512]{2,1,0:T(8,128)S(1)}, u32[]{:S(2)}, u32[]{:S(2)}) collective-permute-start(f32[1,16,512]{2,1,0:T(8,128)S(1)} %add_bitcast_fusion.refs_0_), channel_id=1, source_target_pairs={{8,0},{9,1},{10,2},{11,3},{12,4},{13,5},{14,6},{15,7},{0,8},{1,9},... | collective-permute-start | bytes 98312 | tf_op jit(solution)/shard_map/ppermute | solution.py:590
  60.9 5.7 %collective-permute-start.21 = (f32[1,16,512]{2,1,0:T(8,128)S(1)}, f32[1,16,512]{2,1,0:T(8,128)S(1)}, u32[]{:S(2)}, u32[]{:S(2)}) collective-permute-start(f32[1,16,512]{2,1,0:T(8,128)S(1)} %add_bitcast_fusion.refs_0_), channel_id=1, source_target_pairs={{12,0},{13,1},{14,2},{15,3},{0,4},{1,5},{2,6},{3,7},{4,8},{5,9},{6... | collective-permute-start | bytes 98312 | tf_op jit(solution)/shard_map/ppermute | solution.py:590
  63.0 3.6 %copy-start.1 = (f32[16,32,64]{2,1,0:T(8,128)S(1)}, f32[16,32,64]{2,1,0:T(8,128)}, u32[]{:S(2)}) copy-start(f32[16,32,64]{2,1,0:T(8,128)} %constant.4.clone.refs_4_) | copy-start | bytes 393220

commit v13 on v12

--- a/solution.py
+++ b/solution.py
@@ -175,7 +175,7 @@
     )(log_table, obs_scale, state, target, rock_type)
 
 
-def merge(mine, theirs, slot, size, behind=None, add=None):
+def merge(mine, theirs, slot, size, behind=None, add=None, spare=0):
     given = [value for value in (behind, add) if value is not None]
 
     def kernel(mine_ref, theirs_ref, *refs):
@@ -186,6 +186,8 @@
                 out_ref[at * size + n] = ref[slot * size + n]
         if behind is not None:
             out_ref[2 * size] = tail[0][...]
+        for n in range(spare):
+            out_ref[2 * size + n] = mine_ref[slot * size]
         if add is not None:
             more[0][...] = tail[-1][...] + theirs_ref[theirs.shape[0] - 1]
 
@@ -193,7 +195,7 @@
     tile = mine.shape[1:]
     outs = pl.pallas_call(
         kernel,
-        out_shape=[jax.ShapeDtypeStruct((2 * size + (behind is not None),) + tile, F32)]
+        out_shape=[jax.ShapeDtypeStruct((2 * size + (behind is not None) + spare,) + tile, F32)]
         + [jax.ShapeDtypeStruct(tile, F32)] * (add is not None),
         in_specs=[vmem] * (2 + len(given)),
         out_specs=[vmem] * (1 + (add is not None)),
@@ -263,17 +265,22 @@
     return guess * (4.0 - (2.0 * x) * guess)
 
 
-def each(start, stop, body, width):
+def each(start, stop, body, width, field):
     whole = (stop - start) // width
 
+    def planes(first, count):
+        window = [[field[first + n, t] for t in range(2)] for n in (-1, 0)]
+        for k in range(count):
+            window.append([field[first + k + 1, t] for t in range(2)])
+            body(first + k, window)
+            window.pop(0)
+
     def group(n, carry):
-        for k in range(width):
-            body(start + n * width + k)
+        planes(start + n * width, width)
         return carry
 
     lax.fori_loop(0, whole, group, 0)
-    for p in range(start + whole * width, stop):
-        body(p)
+    planes(start + whole * width, stop - start - whole * width)
 
 
 def solve(near, far, near_halo, far_halo, planes):
@@ -326,13 +333,13 @@
         def behind_y(v):
             return pltpu.roll(v, 1, 0)
 
-        def setup(p, w_z_before):
-            even, odd = cond[p, 0], cond[p, 1]
+        def setup(p, w_z_before, window):
+            even, odd = window[0]
             w_pair = harmonic(even, odd)
             w_next = jnp.where(last_row, 0.0, harmonic(odd, ahead_y(even)))
             w_z_here = []
             for t, here in enumerate((even, odd)):
-                w_z = harmonic(here, cond[p + 1, t])
+                w_z = harmonic(here, window[1][t])
                 w_z_here.append(w_z)
                 w_z_behind = w_z_before[t]
                 w_y = w_next if t else w_pair
@@ -356,9 +363,12 @@
 
         def setup_group(n, carry):
             start = 1 + n * width
-            w_z = [harmonic(cond[start - 1, t], cond[start, t]) for t in range(2)]
+            here = [cond[start, t] for t in range(2)]
+            w_z = [harmonic(cond[start - 1, t], here[t]) for t in range(2)]
             for k in range(width):
-                w_z = setup(start + k, w_z)
+                above = [cond[start + k + 1, t] for t in range(2)]
+                w_z = setup(start + k, w_z, (here, above))
+                here = above
             return carry
 
         assert (span - 2) % width == 0
@@ -373,12 +383,12 @@
                 keep, mix = 0.0, 1.0 / centre
             last = step == STEPS - 2
 
-            def advance(p):
-                even, odd = s_now[p, 0], s_now[p, 1]
+            def advance(p, window):
+                below, (even, odd), above = window
                 for t, s in enumerate((even, odd)):
                     ahead = ahead_y(even) if t else odd
                     behind = even if t else behind_y(odd)
-                    moved = zp[p, t] * s_now[p + 1, t] + zm[p, t] * s_now[p - 1, t]
+                    moved = zp[p, t] * above[t] + zm[p, t] * below[t]
                     moved += yp[p, t] * ahead + ym[p, t] * behind
                     moved += xp[p, t] * ahead_x(s) + xm[p, t] * behind_x(s)
                     new_u = (u_now[p, t] - s) + moved
@@ -392,7 +402,7 @@
                         t_next[p, t] = t_now[p, t] + (s + new_s)
 
             margin = halo - (STEPS - 2 - step)
-            each(margin, span - margin, advance, 8)
+            each(margin, span - margin, advance, 8, s_now)
             s_now, s_next, u_now, u_next = s_next, s_now, u_next, u_now
             if step % 2 == 0:
                 t_now, t_next = t_next, t_now
@@ -598,7 +608,7 @@
     jobs = [[(slot, m) for slot in range(slots)] for m in range(TEAM)]
     mine, theirs, sums = prepare(jobs[2:], fields, with_sums=True)
     theirs = swap(theirs, 1)
-    first, sums = merge(mine, theirs, 0, size, add=sums)
+    first, sums = merge(mine, theirs, 0, size, add=sums, spare=1)
     far = [swap(first, 2)]
     stride, teams = 1, slabs // TEAM
     while stride < teams:

time: 68 us -> 68.3 us (level)
  transfers between devices with their start and end apart: 22 -> 22, of which waited for: 9 -> 10; matrix products, arithmetic and copies ran while one was open for 1% -> 1% of each run, Pallas kernels for 23% -> 23%
where the time goes in v13:
time: 68.3 us; the launch traced here: 68 us
  starting transfers between devices  30.2 us (44%)
  Pallas kernels  19 us (28%)
  waiting for transfers between devices  17.3 us (25%)
  between operations  0.84 us (1%)
    pallas_call x2, Pallas kernels, solve(): pl.pallas_call(kernel, out_shape=[jax.ShapeDtypeStruct((2 * planes, half,...  12.4 us
    ppermute x13, starting transfers between devices, swap(): return lax.ppermute(value, 'gz', [(i, i ^ m) for i in range(slabs)])  10.9 us
    ppermute x4, starting transfers between devices, along(): return lax.ppermute(value, 'gz', pairs)  10.4 us
    ppermute x13, waiting for transfers between devices, swap(): return lax.ppermute(value, 'gz', [(i, i ^ m) for i in range(slabs)])  9.24 us
    ppermute x5, starting transfers between devices, from_teams(): heard.append(lax.ppermute(value, 'gz', pairs))  8.9 us
    ppermute x5, waiting for transfers between devices, from_teams(): heard.append(lax.ppermute(value, 'gz', pairs))  6.71 us
    pallas_call x2, Pallas kernels, prepare(): pl.pallas_call(kernel, out_shape=[jax.ShapeDtypeStruct(shape, F32) for sh...  3.97 us
    ppermute x4, waiting for transfers between devices, along(): return lax.ppermute(value, 'gz', pairs)  1.39 us
  transfers between devices with their start and end apart: 22, of which 10 were waited for; matrix products, arithmetic and copies ran while one was open for 1% of the time, Pallas kernels for 23%

profile of v13, /device:TPU:0, one launch (start us, length us, event | category | flops | bytes accessed | tf_op | source)
XLA Modules:
  0.0 68.0 jit_solution(18344250357054464642)
XLA Ops:
  0.6 2.3 %prepare.3 = (f32[33,8,512]{2,1,0:T(8,128)S(1)}, f32[33,8,512]{2,1,0:T(8,128)S(1)}, f32[8,512]{1,0:T(8,128)S(1)}) custom-call(f32[8,8]{1,0:T(8,128)} %refs_0_.3, f32[8]{0:T(128)} %refs_1_.3, f32[8,4,16,512]{3,2,1,0:T(8,128)} %refs_2_.3, f32[4,16,512]{2,1,0:T(8,128)} %refs_3_.3, s32[8,4,16,512]{3,2,1,0:T(8,128)} %refs_4_.4), custom_call_target="tpu_custom_call" | custom-call | bytes 4194304 | tf_op jit(solution)/shard_map/prepare/pallas_call | solution.py:157
  2.9 0.5 collective-permute-start.1
  3.5 1.6 %collective-permute-done.1.theirs_ref = f32[33,8,512]{2,1,0:T(8,128)S(1)} collective-permute-done((f32[33,8,512]{2,1,0:T(8,128)S(1)}, f32[33,8,512]{2,1,0:T(8,128)S(1)}, u32[]{:S(2)}, u32[]{:S(2)}) %collective-permute-start.1) | collective-permute-done | bytes 540704 | tf_op jit(solution)/shard_map/ppermute | solution.py:582
  5.0 0.1 merge.2
  5.1 2.9 %collective-permute-start.5 = (f32[33,8,512]{2,1,0:T(8,128)S(1)}, f32[33,8,512]{2,1,0:T(8,128)S(1)}, u32[]{:S(2)}, u32[]{:S(2)}) collective-permute-start(f32[33,8,512]{2,1,0:T(8,128)S(1)} %get-tuple-element.36), channel_id=1, source_target_pairs={{0,2},{1,3},{2,0},{3,1},{4,6},{5,7},{6,4},{7,5},{8,10},{9,11},{10,... | collective-permute-start | bytes 1622024 | tf_op jit(solution)/shard_map/ppermute | solution.py:582
  8.0 1.7 %prepare.2 = (f32[32,8,512]{2,1,0:T(8,128)S(1)}, f32[32,8,512]{2,1,0:T(8,128)S(1)}) custom-call(f32[8,8]{1,0:T(8,128)} %refs_0_.3, f32[8]{0:T(128)} %refs_1_.3, f32[8,4,16,512]{3,2,1,0:T(8,128)} %refs_2_.3, f32[4,16,512]{2,1,0:T(8,128)} %refs_3_.3, s32[8,4,16,512]{3,2,1,0:T(8,128)} %refs_4_.4), custom_call_target="tpu_custom_call" | custom-call | bytes 4194304 | tf_op jit(solution)/shard_map/prepare/pallas_call | solution.py:157
  9.7 0.1 collective-permute-start
  9.8 1.6 %collective-permute-start.2 = (f32[8,512]{1,0:T(8,128)S(1)}, f32[8,512]{1,0:T(8,128)S(1)}, u32[]{:S(2)}, u32[]{:S(2)}) collective-permute-start(f32[8,512]{1,0:T(8,128)S(1)} %get-tuple-element.33), channel_id=1, source_target_pairs={{4,0},{5,1},{6,2},{7,3},{0,4},{1,5},{2,6},{3,7},{12,8},{13,9},{14,... | collective-permute-start | bytes 49160 | tf_op jit(solution)/shard_map/ppermute | solution.py:600
  11.4 2.2 %collective-permute-done.2 = f32[8,512]{1,0:T(8,128)S(1)} collective-permute-done((f32[8,512]{1,0:T(8,128)S(1)}, f32[8,512]{1,0:T(8,128)S(1)}, u32[]{:S(2)}, u32[]{:S(2)}) %collective-permute-start.2) | collective-permute-done | bytes 16416 | tf_op jit(solution)/shard_map/ppermute | solution.py:600
  13.6 2.6 %collective-permute-start.3 = (f32[8,512]{1,0:T(8,128)S(1)}, f32[8,512]{1,0:T(8,128)S(1)}, u32[]{:S(2)}, u32[]{:S(2)}) collective-permute-start(f32[8,512]{1,0:T(8,128)S(1)} %add.15), channel_id=1, source_target_pairs={{8,0},{9,1},{10,2},{11,3},{12,4},{13,5},{14,6},{15,7},{0,8},{1,9},... | collective-permute-start | bytes 49160 | tf_op jit(solution)/shard_map/ppermute | solution.py:600
  16.2 2.0 %collective-permute-done.3 = f32[8,512]{1,0:T(8,128)S(1)} collective-permute-done((f32[8,512]{1,0:T(8,128)S(1)}, f32[8,512]{1,0:T(8,128)S(1)}, u32[]{:S(2)}, u32[]{:S(2)}) %collective-permute-start.3) | collective-permute-done | bytes 16416 | tf_op jit(solution)/shard_map/ppermute | solution.py:600
  18.2 0.1 merge.3
  18.3 0.4 collective-permute-start.11
  18.7 0.1 merge_near.2
  18.8 1.3 %collective-permute-start.4 = (f32[30,8,512]{2,1,0:T(8,128)S(1)}, f32[30,8,512]{2,1,0:T(8,128)S(1)}, u32[]{:S(2)}, u32[]{:S(2)}) collective-permute-start(f32[30,8,512]{2,1,0:T(8,128)S(1)} %get-tuple-element.35), channel_id=1, source_target_pairs={{2,6},{3,7},{4,0},{5,1},{6,10},{7,11},{8,4},{9,5},{10,14},{11,15},... | collective-permute-start | bytes 1474568 | tf_op jit(solution)/shard_map/ppermute | solution.py:591
  20.1 1.0 %collective-permute-done.5.ref.refs_2_ = f32[33,8,512]{2,1,0:T(8,128)S(1)} collective-permute-done((f32[33,8,512]{2,1,0:T(8,128)S(1)}, f32[33,8,512]{2,1,0:T(8,128)S(1)}, u32[]{:S(2)}, u32[]{:S(2)}) %collective-permute-start.5) | collective-permute-done | bytes 540704 | tf_op jit(solution)/shard_map/ppermute | solution.py:582
  21.1 4.1 %collective-permute-start.6 = (f32[30,8,512]{2,1,0:T(8,128)S(1)}, f32[30,8,512]{2,1,0:T(8,128)S(1)}, u32[]{:S(2)}, u32[]{:S(2)}) collective-permute-start(f32[30,8,512]{2,1,0:T(8,128)S(1)} %trim.2), channel_id=1, source_target_pairs={{0,4},{1,5},{4,8},{5,9},{6,2},{7,3},{8,12},{9,13},{10,6},{11,7},{1... | collective-permute-start | bytes 1474568 | tf_op jit(solution)/shard_map/ppermute | solution.py:591
  25.2 0.1 merge_near.3
  25.3 1.3 %collective-permute-start.10 = (f32[30,8,512]{2,1,0:T(8,128)S(1)}, f32[30,8,512]{2,1,0:T(8,128)S(1)}, u32[]{:S(2)}, u32[]{:S(2)}) collective-permute-start(f32[30,8,512]{2,1,0:T(8,128)S(1)} %get-tuple-element.42), channel_id=1, source_target_pairs={{2,6},{3,7},{4,0},{5,1},{6,10},{7,11},{8,4},{9,5},{10,14},{11,15},... | collective-permute-start | bytes 1474568 | tf_op jit(solution)/shard_map/ppermute | solution.py:591
  26.6 5.6 %collective-permute-done.11.ref.refs_2_ = f32[33,8,512]{2,1,0:T(8,128)S(1)} collective-permute-done((f32[33,8,512]{2,1,0:T(8,128)S(1)}, f32[33,8,512]{2,1,0:T(8,128)S(1)}, u32[]{:S(2)}, u32[]{:S(2)}) %collective-permute-start.11) | collective-permute-done | bytes 540704 | tf_op jit(solution)/shard_map/ppermute | solution.py:582
  32.2 3.8 %collective-permute-start.12 = (f32[30,8,512]{2,1,0:T(8,128)S(1)}, f32[30,8,512]{2,1,0:T(8,128)S(1)}, u32[]{:S(2)}, u32[]{:S(2)}) collective-permute-start(f32[30,8,512]{2,1,0:T(8,128)S(1)} %trim.3), channel_id=1, source_target_pairs={{0,4},{1,5},{4,8},{5,9},{6,2},{7,3},{8,12},{9,13},{10,6},{11,7},{1... | collective-permute-start | bytes 1474568 | tf_op jit(solution)/shard_map/ppermute | solution.py:591
  36.0 0.0 collective-permute-done.6.refs_3_
  36.0 6.2 %solve.2 = (f32[8,8,512]{2,1,0:T(8,128)S(1)}, f32[8,8,512]{2,1,0:T(8,128)S(1)}, f32[8,8,512]{2,1,0:T(8,128)S(1)}, f32[8,8,512]{2,1,0:T(8,128)S(1)}, f32[16,512]{1,0:T(8,128)S(1)}) custom-call(f32[32,8,512]{2,1,0:T(8,128)S(1)} %get-tuple-element.34.refs_0_, f32[30,8,512]{2,1,0:T(8,128)S(1)} %collective-permute-done.4.refs_1_, ...), custom_call_target="tpu_custom_call" | custom-call | bytes 23068672 | tf_op jit(solution)/shard_map/solve/pallas_call | solution.py:420
  42.2 0.1 collective-permute-start.7
  42.3 1.0 %collective-permute-start.8 = (f32[8,8,512]{2,1,0:T(8,128)S(1)}, f32[8,8,512]{2,1,0:T(8,128)S(1)}, u32[]{:S(2)}, u32[]{:S(2)}) collective-permute-start(f32[8,8,512]{2,1,0:T(8,128)S(1)} %get-tuple-element.39), channel_id=1, source_target_pairs={{0,2},{1,3},{2,0},{3,1},{4,6},{5,7},{6,4},{7,5},{8,10},{9,11},{10,... | collective-permute-start | bytes 393224 | tf_op jit(solution)/shard_map/ppermute | solution.py:582
  43.3 0.9 %collective-permute-start.9 = (f32[8,8,512]{2,1,0:T(8,128)S(1)}, f32[8,8,512]{2,1,0:T(8,128)S(1)}, u32[]{:S(2)}, u32[]{:S(2)}) collective-permute-start(f32[8,8,512]{2,1,0:T(8,128)S(1)} %get-tuple-element.40), channel_id=1, source_target_pairs={{0,3},{1,2},{2,1},{3,0},{4,7},{5,6},{6,5},{7,4},{8,11},{9,10},{10,... | collective-permute-start | bytes 393224 | tf_op jit(solution)/shard_map/ppermute | solution.py:582
  44.2 1.4 %collective-permute-done.12.refs_3_ = f32[30,8,512]{2,1,0:T(8,128)S(1)} collective-permute-done((f32[30,8,512]{2,1,0:T(8,128)S(1)}, f32[30,8,512]{2,1,0:T(8,128)S(1)}, u32[]{:S(2)}, u32[]{:S(2)}) %collective-permute-start.12) | collective-permute-done | bytes 491552 | tf_op jit(solution)/shard_map/ppermute | solution.py:591
  45.6 6.2 %solve.3 = (f32[8,8,512]{2,1,0:T(8,128)S(1)}, f32[8,8,512]{2,1,0:T(8,128)S(1)}, f32[8,8,512]{2,1,0:T(8,128)S(1)}, f32[8,8,512]{2,1,0:T(8,128)S(1)}, f32[16,512]{1,0:T(8,128)S(1)}) custom-call(f32[32,8,512]{2,1,0:T(8,128)S(1)} %get-tuple-element.41.refs_0_, f32[30,8,512]{2,1,0:T(8,128)S(1)} %collective-permute-done.10.refs_1_, ...), custom_call_target="tpu_custom_call" | custom-call | bytes 23068672 | tf_op jit(solution)/shard_map/solve/pallas_call | solution.py:420
  51.8 0.0 copy-start
  51.8 0.0 collective-permute-done.7.refs_1_.refs_4_
  51.8 0.0 collective-permute-done.8.refs_2_.refs_5_
  51.9 2.8 %collective-permute-start.16 = (f32[16,512]{1,0:T(8,128)S(1)}, f32[16,512]{1,0:T(8,128)S(1)}, u32[]{:S(2)}, u32[]{:S(2)}) collective-permute-start(f32[16,512]{1,0:T(8,128)S(1)} %get-tuple-element.50), channel_id=1, source_target_pairs={{0,2},{1,3},{2,0},{3,1},{4,6},{5,7},{6,4},{7,5},{8,10},{9,11},{10,... | collective-permute-start | bytes 98312 | tf_op jit(solution)/shard_map/ppermute | solution.py:582
  54.7 0.0 collective-permute-start.17
  54.7 0.2 collective-permute-start.18
  54.9 0.3 collective-permute-start.13
  55.2 1.6 %collective-permute-start.14 = (f32[8,8,512]{2,1,0:T(8,128)S(1)}, f32[8,8,512]{2,1,0:T(8,128)S(1)}, u32[]{:S(2)}, u32[]{:S(2)}) collective-permute-start(f32[8,8,512]{2,1,0:T(8,128)S(1)} %get-tuple-element.45), channel_id=1, source_target_pairs={{0,2},{1,3},{2,0},{3,1},{4,6},{5,7},{6,4},{7,5},{8,10},{9,11},{10,... | collective-permute-start | bytes 393224 | tf_op jit(solution)/shard_map/ppermute | solution.py:582
  56.8 0.1 collective-permute-start.15
  57.0 1.0 %collective-permute-done.17 = f32[16,512]{1,0:T(8,128)S(1)} collective-permute-done((f32[16,512]{1,0:T(8,128)S(1)}, f32[16,512]{1,0:T(8,128)S(1)}, u32[]{:S(2)}, u32[]{:S(2)}) %collective-permute-start.17) | collective-permute-done | bytes 32800 | tf_op jit(solution)/shard_map/ppermute | solution.py:582
  58.0 0.0 collective-permute-done.18
  58.0 2.5 %collective-permute-start.19 = (f32[1,16,512]{2,1,0:T(8,128)S(1)}, f32[1,16,512]{2,1,0:T(8,128)S(1)}, u32[]{:S(2)}, u32[]{:S(2)}) collective-permute-start(f32[1,16,512]{2,1,0:T(8,128)S(1)} %add_bitcast_fusion.refs_0_), channel_id=1, source_target_pairs={{4,0},{5,1},{6,2},{7,3},{8,4},{9,5},{10,6},{11,7},{12,8},{13,9},{1... | collective-permute-start | bytes 98312 | tf_op jit(solution)/shard_map/ppermute | solution.py:600
  60.5 0.6 collective-permute-start.20
  61.1 1.6 %collective-permute-start.21 = (f32[1,16,512]{2,1,0:T(8,128)S(1)}, f32[1,16,512]{2,1,0:T(8,128)S(1)}, u32[]{:S(2)}, u32[]{:S(2)}) collective-permute-start(f32[1,16,512]{2,1,0:T(8,128)S(1)} %add_bitcast_fusion.refs_0_), channel_id=1, source_target_pairs={{12,0},{13,1},{14,2},{15,3},{0,4},{1,5},{2,6},{3,7},{4,8},{5,9},{6... | collective-permute-start | bytes 98312 | tf_op jit(solution)/shard_map/ppermute | solution.py:600
  62.7 0.5 slice_bitcast_fusion.1
  63.2 0.1 collective-permute-done.15.refs_7_
  63.3 1.0 %gather_adjoint.1 = (f32[8,4,16,512]{3,2,1,0:T(8,128)}, f32[8,128]{1,0:T(8,128)S(1)}) custom-call(f32[8,8,512]{2,1,0:T(8,128)S(1)} %get-tuple-element.37.refs_0_, f32[8,8,512]{2,1,0:T(8,128)S(1)} %collective-permute-done.7.refs_1_.refs_4_, f32[8,8,512]{2,1,0:T(8,128)S(1)} %collective-permute-done.8.refs_2_.refs_5_, ...), custom_call_target="tpu_custom_call" | custom-call | bytes 4194304 | tf_op jit(solution)/shard_map/gather_adjoint/pallas_call | solution.py:502
  64.3 1.0 %collective-permute-done.20.refs_2_ = f32[1,16,512]{2,1,0:T(8,128)S(1)} collective-permute-done((f32[1,16,512]{2,1,0:T(8,128)S(1)}, f32[1,16,512]{2,1,0:T(8,128)S(1)}, u32[]{:S(2)}, u32[]{:S(2)}) %collective-permute-start.20) | collective-permute-done | bytes 32800 | tf_op jit(solution)/shard_map/ppermute | solution.py:600
  65.3 1.5 %collective-permute-done.21.refs_3_ = f32[1,16,512]{2,1,0:T(8,128)S(1)} collective-permute-done((f32[1,16,512]{2,1,0:T(8,128)S(1)}, f32[1,16,512]{2,1,0:T(8,128)S(1)}, u32[]{:S(2)}, u32[]{:S(2)}) %collective-permute-start.21) | collective-permute-done | bytes 32800 | tf_op jit(solution)/shard_map/ppermute | solution.py:600
  66.8 1.1 %control.1 = f32[32,512]{1,0:T(8,128)} custom-call(f32[1,16,512]{2,1,0:T(8,128)S(1)} %add_bitcast_fusion.refs_0_, f32[1,16,512]{2,1,0:T(8,128)S(1)} %collective-permute-done.19.refs_1_, f32[1,16,512]{2,1,0:T(8,128)S(1)} %collective-permute-done.20.refs_2_, f32[1,16,512]{2,1,0:T(8,128)S(1)} %collective-permute-done.21.refs_3_, f32[16,32,64]{2,1,0:T(8,128)S(1)} %copy-done.1, ...), custom_call_target="tpu_custom_call" | custom-call | tf_op jit(solution)/shard_map/control/pallas_call | solution.py:554
  (18 shorter events, 0.2 us)
Async XLA Ops:
  2.9 2.1 %collective-permute-start.1 = (f32[33,8,512]{2,1,0:T(8,128)S(1)}, f32[33,8,512]{2,1,0:T(8,128)S(1)}, u32[]{:S(2)}, u32[]{:S(2)}) collective-permute-start(f32[33,8,512]{2,1,0:T(8,128)S(1)} %get-tuple-element.31), channel_id=1, source_target_pairs={{0,1},{1,0},{2,3},{3,2},{4,5},{5,4},{6,7},{7,6},{8,9},{9,8},{10,11... | collective-permute-start | bytes 1622024 | tf_op jit(solution)/shard_map/ppermute | solution.py:582
  5.1 16.0 %collective-permute-start.5 = (f32[33,8,512]{2,1,0:T(8,128)S(1)}, f32[33,8,512]{2,1,0:T(8,128)S(1)}, u32[]{:S(2)}, u32[]{:S(2)}) collective-permute-start(f32[33,8,512]{2,1,0:T(8,128)S(1)} %get-tuple-element.36), channel_id=1, source_target_pairs={{0,2},{1,3},{2,0},{3,1},{4,6},{5,7},{6,4},{7,5},{8,10},{9,11},{10,... | collective-permute-start | bytes 1622024 | tf_op jit(solution)/shard_map/ppermute | solution.py:582
  9.7 9.0 %collective-permute-start = (f32[32,8,512]{2,1,0:T(8,128)S(1)}, f32[32,8,512]{2,1,0:T(8,128)S(1)}, u32[]{:S(2)}, u32[]{:S(2)}) collective-permute-start(f32[32,8,512]{2,1,0:T(8,128)S(1)} %get-tuple-element.29), channel_id=1, source_target_pairs={{0,1},{1,0},{2,3},{3,2},{4,5},{5,4},{6,7},{7,6},{8,9},{9,8},{10,11... | collective-permute-start | bytes 1572872 | tf_op jit(solution)/shard_map/ppermute | solution.py:582
  9.8 3.8 %collective-permute-start.2 = (f32[8,512]{1,0:T(8,128)S(1)}, f32[8,512]{1,0:T(8,128)S(1)}, u32[]{:S(2)}, u32[]{:S(2)}) collective-permute-start(f32[8,512]{1,0:T(8,128)S(1)} %get-tuple-element.33), channel_id=1, source_target_pairs={{4,0},{5,1},{6,2},{7,3},{0,4},{1,5},{2,6},{3,7},{12,8},{13,9},{14,... | collective-permute-start | bytes 49160 | tf_op jit(solution)/shard_map/ppermute | solution.py:600
  13.6 4.6 %collective-permute-start.3 = (f32[8,512]{1,0:T(8,128)S(1)}, f32[8,512]{1,0:T(8,128)S(1)}, u32[]{:S(2)}, u32[]{:S(2)}) collective-permute-start(f32[8,512]{1,0:T(8,128)S(1)} %add.15), channel_id=1, source_target_pairs={{8,0},{9,1},{10,2},{11,3},{12,4},{13,5},{14,6},{15,7},{0,8},{1,9},... | collective-permute-start | bytes 49160 | tf_op jit(solution)/shard_map/ppermute | solution.py:600
  18.3 13.9 %collective-permute-start.11 = (f32[33,8,512]{2,1,0:T(8,128)S(1)}, f32[33,8,512]{2,1,0:T(8,128)S(1)}, u32[]{:S(2)}, u32[]{:S(2)}) collective-permute-start(f32[33,8,512]{2,1,0:T(8,128)S(1)} %merge.3), channel_id=1, source_target_pairs={{0,2},{1,3},{2,0},{3,1},{4,6},{5,7},{6,4},{7,5},{8,10},{9,11},{10,... | collective-permute-start | bytes 1622024 | tf_op jit(solution)/shard_map/ppermute | solution.py:582
  18.8 17.2 %collective-permute-start.4 = (f32[30,8,512]{2,1,0:T(8,128)S(1)}, f32[30,8,512]{2,1,0:T(8,128)S(1)}, u32[]{:S(2)}, u32[]{:S(2)}) collective-permute-start(f32[30,8,512]{2,1,0:T(8,128)S(1)} %get-tuple-element.35), channel_id=1, source_target_pairs={{2,6},{3,7},{4,0},{5,1},{6,10},{7,11},{8,4},{9,5},{10,14},{11,15},... | collective-permute-start | bytes 1474568 | tf_op jit(solution)/shard_map/ppermute | solution.py:591
  21.1 14.9 %collective-permute-start.6 = (f32[30,8,512]{2,1,0:T(8,128)S(1)}, f32[30,8,512]{2,1,0:T(8,128)S(1)}, u32[]{:S(2)}, u32[]{:S(2)}) collective-permute-start(f32[30,8,512]{2,1,0:T(8,128)S(1)} %trim.2), channel_id=1, source_target_pairs={{0,4},{1,5},{4,8},{5,9},{6,2},{7,3},{8,12},{9,13},{10,6},{11,7},{1... | collective-permute-start | bytes 1474568 | tf_op jit(solution)/shard_map/ppermute | solution.py:591
  25.3 18.9 %collective-permute-start.10 = (f32[30,8,512]{2,1,0:T(8,128)S(1)}, f32[30,8,512]{2,1,0:T(8,128)S(1)}, u32[]{:S(2)}, u32[]{:S(2)}) collective-permute-start(f32[30,8,512]{2,1,0:T(8,128)S(1)} %get-tuple-element.42), channel_id=1, source_target_pairs={{2,6},{3,7},{4,0},{5,1},{6,10},{7,11},{8,4},{9,5},{10,14},{11,15},... | collective-permute-start | bytes 1474568 | tf_op jit(solution)/shard_map/ppermute | solution.py:591
  32.2 13.3 %collective-permute-start.12 = (f32[30,8,512]{2,1,0:T(8,128)S(1)}, f32[30,8,512]{2,1,0:T(8,128)S(1)}, u32[]{:S(2)}, u32[]{:S(2)}) collective-permute-start(f32[30,8,512]{2,1,0:T(8,128)S(1)} %trim.3), channel_id=1, source_target_pairs={{0,4},{1,5},{4,8},{5,9},{6,2},{7,3},{8,12},{9,13},{10,6},{11,7},{1... | collective-permute-start | bytes 1474568 | tf_op jit(solution)/shard_map/ppermute | solution.py:591
  42.2 9.6 %collective-permute-start.7 = (f32[8,8,512]{2,1,0:T(8,128)S(1)}, f32[8,8,512]{2,1,0:T(8,128)S(1)}, u32[]{:S(2)}, u32[]{:S(2)}) collective-permute-start(f32[8,8,512]{2,1,0:T(8,128)S(1)} %get-tuple-element.38), channel_id=1, source_target_pairs={{0,1},{1,0},{2,3},{3,2},{4,5},{5,4},{6,7},{7,6},{8,9},{9,8},{10,11... | collective-permute-start | bytes 393224 | tf_op jit(solution)/shard_map/ppermute | solution.py:582
  42.3 9.5 %collective-permute-start.8 = (f32[8,8,512]{2,1,0:T(8,128)S(1)}, f32[8,8,512]{2,1,0:T(8,128)S(1)}, u32[]{:S(2)}, u32[]{:S(2)}) collective-permute-start(f32[8,8,512]{2,1,0:T(8,128)S(1)} %get-tuple-element.39), channel_id=1, source_target_pairs={{0,2},{1,3},{2,0},{3,1},{4,6},{5,7},{6,4},{7,5},{8,10},{9,11},{10,... | collective-permute-start | bytes 393224 | tf_op jit(solution)/shard_map/ppermute | solution.py:582
  43.3 8.5 %collective-permute-start.9 = (f32[8,8,512]{2,1,0:T(8,128)S(1)}, f32[8,8,512]{2,1,0:T(8,128)S(1)}, u32[]{:S(2)}, u32[]{:S(2)}) collective-permute-start(f32[8,8,512]{2,1,0:T(8,128)S(1)} %get-tuple-element.40), channel_id=1, source_target_pairs={{0,3},{1,2},{2,1},{3,0},{4,7},{5,6},{6,5},{7,4},{8,11},{9,10},{10,... | collective-permute-start | bytes 393224 | tf_op jit(solution)/shard_map/ppermute | solution.py:582
  51.8 15.0 %copy-start = (f32[512,512]{1,0:T(8,128)S(1)}, f32[512,512]{1,0:T(8,128)}, u32[]{:S(2)}) copy-start(f32[512,512]{1,0:T(8,128)} %constant.5.clone.refs_5_) | copy-start | bytes 3145732
  51.9 4.9 %collective-permute-start.16 = (f32[16,512]{1,0:T(8,128)S(1)}, f32[16,512]{1,0:T(8,128)S(1)}, u32[]{:S(2)}, u32[]{:S(2)}) collective-permute-start(f32[16,512]{1,0:T(8,128)S(1)} %get-tuple-element.50), channel_id=1, source_target_pairs={{0,2},{1,3},{2,0},{3,1},{4,6},{5,7},{6,4},{7,5},{8,10},{9,11},{10,... | collective-permute-start | bytes 98312 | tf_op jit(solution)/shard_map/ppermute | solution.py:582
  54.7 3.3 %collective-permute-start.17 = (f32[16,512]{1,0:T(8,128)S(1)}, f32[16,512]{1,0:T(8,128)S(1)}, u32[]{:S(2)}, u32[]{:S(2)}) collective-permute-start(f32[16,512]{1,0:T(8,128)S(1)} %get-tuple-element.50), channel_id=1, source_target_pairs={{0,3},{1,2},{2,1},{3,0},{4,7},{5,6},{6,5},{7,4},{8,11},{9,10},{10,... | collective-permute-start | bytes 98312 | tf_op jit(solution)/shard_map/ppermute | solution.py:582
  54.7 3.3 %collective-permute-start.18 = (f32[16,512]{1,0:T(8,128)S(1)}, f32[16,512]{1,0:T(8,128)S(1)}, u32[]{:S(2)}, u32[]{:S(2)}) collective-permute-start(f32[16,512]{1,0:T(8,128)S(1)} %get-tuple-element.50), channel_id=1, source_target_pairs={{0,1},{1,0},{2,3},{3,2},{4,5},{5,4},{6,7},{7,6},{8,9},{9,8},{10,11... | collective-permute-start | bytes 98312 | tf_op jit(solution)/shard_map/ppermute | solution.py:582
  54.9 6.3 %collective-permute-start.13 = (f32[8,8,512]{2,1,0:T(8,128)S(1)}, f32[8,8,512]{2,1,0:T(8,128)S(1)}, u32[]{:S(2)}, u32[]{:S(2)}) collective-permute-start(f32[8,8,512]{2,1,0:T(8,128)S(1)} %get-tuple-element.44), channel_id=1, source_target_pairs={{0,1},{1,0},{2,3},{3,2},{4,5},{5,4},{6,7},{7,6},{8,9},{9,8},{10,11... | collective-permute-start | bytes 393224 | tf_op jit(solution)/shard_map/ppermute | solution.py:582
  55.2 8.0 %collective-permute-start.14 = (f32[8,8,512]{2,1,0:T(8,128)S(1)}, f32[8,8,512]{2,1,0:T(8,128)S(1)}, u32[]{:S(2)}, u32[]{:S(2)}) collective-permute-start(f32[8,8,512]{2,1,0:T(8,128)S(1)} %get-tuple-element.45), channel_id=1, source_target_pairs={{0,2},{1,3},{2,0},{3,1},{4,6},{5,7},{6,4},{7,5},{8,10},{9,11},{10,... | collective-permute-start | bytes 393224 | tf_op jit(solution)/shard_map/ppermute | solution.py:582
  56.8 6.5 %collective-permute-start.15 = (f32[8,8,512]{2,1,0:T(8,128)S(1)}, f32[8,8,512]{2,1,0:T(8,128)S(1)}, u32[]{:S(2)}, u32[]{:S(2)}) collective-permute-start(f32[8,8,512]{2,1,0:T(8,128)S(1)} %get-tuple-element.46), channel_id=1, source_target_pairs={{0,3},{1,2},{2,1},{3,0},{4,7},{5,6},{6,5},{7,4},{8,11},{9,10},{10,... | collective-permute-start | bytes 393224 | tf_op jit(solution)/shard_map/ppermute | solution.py:582
  58.0 6.3 %collective-permute-start.19 = (f32[1,16,512]{2,1,0:T(8,128)S(1)}, f32[1,16,512]{2,1,0:T(8,128)S(1)}, u32[]{:S(2)}, u32[]{:S(2)}) collective-permute-start(f32[1,16,512]{2,1,0:T(8,128)S(1)} %add_bitcast_fusion.refs_0_), channel_id=1, source_target_pairs={{4,0},{5,1},{6,2},{7,3},{8,4},{9,5},{10,6},{11,7},{12,8},{13,9},{1... | collective-permute-start | bytes 98312 | tf_op jit(solution)/shard_map/ppermute | solution.py:600
  60.5 4.8 %collective-permute-start.20 = (f32[1,16,512]{2,1,0:T(8,128)S(1)}, f32[1,16,512]{2,1,0:T(8,128)S(1)}, u32[]{:S(2)}, u32[]{:S(2)}) collective-permute-start(f32[1,16,512]{2,1,0:T(8,128)S(1)} %add_bitcast_fusion.refs_0_), channel_id=1, source_target_pairs={{8,0},{9,1},{10,2},{11,3},{12,4},{13,5},{14,6},{15,7},{0,8},{1,9},... | collective-permute-start | bytes 98312 | tf_op jit(solution)/shard_map/ppermute | solution.py:600
  61.1 5.7 %collective-permute-start.21 = (f32[1,16,512]{2,1,0:T(8,128)S(1)}, f32[1,16,512]{2,1,0:T(8,128)S(1)}, u32[]{:S(2)}, u32[]{:S(2)}) collective-permute-start(f32[1,16,512]{2,1,0:T(8,128)S(1)} %add_bitcast_fusion.refs_0_), channel_id=1, source_target_pairs={{12,0},{13,1},{14,2},{15,3},{0,4},{1,5},{2,6},{3,7},{4,8},{5,9},{6... | collective-permute-start | bytes 98312 | tf_op jit(solution)/shard_map/ppermute | solution.py:600
  63.3 3.6 %copy-start.1 = (f32[16,32,64]{2,1,0:T(8,128)S(1)}, f32[16,32,64]{2,1,0:T(8,128)}, u32[]{:S(2)}) copy-start(f32[16,32,64]{2,1,0:T(8,128)} %constant.4.clone.refs_4_) | copy-start | bytes 393220

commit v14 on v12

--- a/solution.py
+++ b/solution.py
@@ -459,56 +459,55 @@
     )(*sums, *faces, *after)
 
 
-def gather_adjoint(pieces, planes):
-    slots = len(pieces)
-    _, half, columns = pieces[0][0].shape
+def gather_adjoint(pieces, slot, slots, planes, adjoint):
+    _, half, columns = pieces[0].shape
     tiles = columns // 128
     block = (planes, 2 * half, columns)
+    given = [] if adjoint is None else [adjoint]
 
     def kernel(*refs):
-        blocks, out, mark, held, mixed, sems = refs[: slots * TEAM], *refs[slots * TEAM :]
+        blocks, refs = refs[:TEAM], refs[TEAM + len(given) :]
+        out, mark, held, mixed, sems = refs
         mark[...] = blocks[0][0, :, :LANES]
         place = team_place()
         copies = []
-        for slot in range(slots):
-            for m in range(TEAM):
-                i = slot * TEAM + m
-                for j in range(planes):
-                    for t in range(2):
-                        for c in range(tiles):
-                            mixed[i % 2, j, c, pl.ds(t, half, stride=2), :] = blocks[i][
-                                2 * j + t, :, c * 128 : (c + 1) * 128
-                            ]
+        for m in range(TEAM):
+            for j in range(planes):
+                for t in range(2):
                     for c in range(tiles):
-                        held[i, j, :, c * 128 : (c + 1) * 128] = mixed[i % 2, j, c]
-                copy = pltpu.make_async_copy(
-                    held.at[i], out.at[slots * (place ^ m) + slot], sems.at[i]
-                )
-                copy.start()
-                copies.append(copy)
+                        mixed[m, j, c, pl.ds(t, half, stride=2), :] = blocks[m][
+                            2 * j + t, :, c * 128 : (c + 1) * 128
+                        ]
+                for c in range(tiles):
+                    held[m, j, :, c * 128 : (c + 1) * 128] = mixed[m, j, c]
+            copy = pltpu.make_async_copy(
+                held.at[m], out.at[slots * (place ^ m) + slot], sems.at[m]
+            )
+            copy.start()
+            copies.append(copy)
         for copy in copies:
             copy.wait()
 
+    vmem = pl.BlockSpec(memory_space=pltpu.VMEM)
+    hbm = pl.BlockSpec(memory_space=pltpu.HBM)
     return pl.pallas_call(
         kernel,
         out_shape=[
             jax.ShapeDtypeStruct((slots * TEAM,) + block, F32),
             jax.ShapeDtypeStruct((half, LANES), F32),
         ],
-        in_specs=[pl.BlockSpec(memory_space=pltpu.VMEM)] * (slots * TEAM),
-        out_specs=[
-            pl.BlockSpec(memory_space=pltpu.HBM),
-            pl.BlockSpec(memory_space=pltpu.VMEM),
+        in_specs=[vmem] * TEAM + [hbm] * len(given),
+        out_specs=[hbm, vmem],
+        scratch_shapes=[
+            pltpu.VMEM((TEAM,) + block, F32),
+            pltpu.VMEM((TEAM, planes, tiles, 2 * half, 128), F32),
+            pltpu.SemaphoreType.DMA((TEAM,)),
         ],
-        scratch_shapes=[
-            pltpu.VMEM((slots * TEAM,) + block, F32),
-            pltpu.VMEM((2, planes, tiles, 2 * half, 128), F32),
-            pltpu.SemaphoreType.DMA((slots * TEAM,)),
-        ],
+        input_output_aliases={TEAM: 0} if given else {},
         compiler_params=pltpu.CompilerParams(vmem_limit_bytes=4 * MIB),
-        cost_estimate=pl.CostEstimate(flops=0, bytes_accessed=4 * MIB, transcendentals=0),
+        cost_estimate=pl.CostEstimate(flops=0, bytes_accessed=2 * MIB, transcendentals=0),
         name="gather_adjoint",
-    )(*[piece for group in pieces for piece in group])
+    )(*pieces, *given)
 
 
 def control(faces, radices, basis_z, basis_x, after):
@@ -523,7 +522,7 @@
         for n in range(teams):
             at, left, stride = 0, n, 1
             for radix in radices:
-                digit = lax.rem(team // stride + left % radix, radix)
+                digit = turned(lax.rem(team // stride, radix), left % radix, radix)
                 at, left, stride = at + digit * stride, left // radix, stride * radix
             inner = teams // len(faces)
             whole[at] = parts[n // inner][n % inner]
@@ -552,6 +551,10 @@
     )(*faces, basis_z, basis_x, after)
 
 
+def turned(digit, k, radix):
+    return digit ^ k if radix in (2, 4) else (digit + k) % radix
+
+
 def radices_of(teams):
     radices = []
     while teams > 1:
@@ -581,14 +584,14 @@
         return lax.ppermute(value, "gz", pairs)
 
     def from_teams(value, stride, radix):
-        heard = []
-        for k in range(1, radix):
+        heard = {}
+        for k in reversed(range(1, radix)):
             pairs = []
             for i in range(slabs):
                 digit = i // (TEAM * stride) % radix
-                pairs.append((i + ((digit + k) % radix - digit) * stride * TEAM, i))
-            heard.append(lax.ppermute(value, "gz", pairs))
-        return heard
+                pairs.append((i + (turned(digit, k, radix) - digit) * stride * TEAM, i))
+            heard[k] = lax.ppermute(value, "gz", pairs)
+        return [heard[k] for k in range(1, radix)]
 
     fields = [
         pltpu.with_memory_space_constraint(field, pltpu.HBM)
@@ -621,7 +624,8 @@
     for slot in range(slots):
         far_halo = along(trim(far[slot], size), False)
         solved = solve(near[slot], far[slot], near_halo[slot], far_halo, planes)
-        pieces.append([solved[0]] + [swap(solved[m], m) for m in (1, 2, 3)])
+        traded = {m: swap(solved[m], m) for m in (2, 3, 1)}
+        pieces.append([solved[0]] + [traded[m] for m in (1, 2, 3)])
         faces.append(solved[TEAM])
 
     face, moments = weigh(sums, faces, depth_total * rows_y * columns, pieces[0][1:])
@@ -631,7 +635,9 @@
         held = heard[0] if len(heard) == 1 else jnp.concatenate(heard)
         heard = [held] + from_teams(held, stride, radix)
         stride *= radix
-    adjoint, mark = gather_adjoint(pieces, planes)
+    adjoint = None
+    for slot in range(slots):
+        adjoint, mark = gather_adjoint(pieces[slot], slot, slots, planes, adjoint)
     own_count = MA // slabs
     gradient = control(
         heard,

time: 68 us -> 68.8 us (1.012)
  Pallas kernels: 19.1 us -> 20.3 us
    ppermute x5, waiting for transfers between devices: 6.71 us -> 5.43 us  [from_teams(): heard[k] = lax.ppermute(value, 'gz', pairs)]
    pallas_call x1 -> x2, Pallas kernels: 1.05 us -> 2.28 us  [gather_adjoint(): pl.pallas_call(kernel, out_shape=[jax.ShapeDtypeStruct((slots * TEAM,) +...]
    ppermute x13, waiting for transfers between devices: 9.18 us -> 10.2 us  [swap(): return lax.ppermute(value, 'gz', [(i, i ^ m) for i in range(slabs)])]
  transfers between devices with their start and end apart: 22 -> 22, of which waited for: 9 -> 7; matrix products, arithmetic and copies ran while one was open for 1% -> 1% of each run, Pallas kernels for 23% -> 25%
where the time goes in v14:
time: 68.8 us; the launch traced here: 68.5 us
  starting transfers between devices  29.6 us (43%)
  Pallas kernels  20.3 us (30%)
  waiting for transfers between devices  17.1 us (25%)
  between operations  0.87 us (1%)
    pallas_call x2, Pallas kernels, solve(): pl.pallas_call(kernel, out_shape=[jax.ShapeDtypeStruct((2 * planes, half,...  12.6 us
    ppermute x13, starting transfers between devices, swap(): return lax.ppermute(value, 'gz', [(i, i ^ m) for i in range(slabs)])  10.6 us
    ppermute x4, starting transfers between devices, along(): return lax.ppermute(value, 'gz', pairs)  10.4 us
    ppermute x13, waiting for transfers between devices, swap(): return lax.ppermute(value, 'gz', [(i, i ^ m) for i in range(slabs)])  10.2 us
    ppermute x5, starting transfers between devices, from_teams(): heard[k] = lax.ppermute(value, 'gz', pairs)  8.62 us
    ppermute x5, waiting for transfers between devices, from_teams(): heard[k] = lax.ppermute(value, 'gz', pairs)  5.43 us
    pallas_call x2, Pallas kernels, prepare(): pl.pallas_call(kernel, out_shape=[jax.ShapeDtypeStruct(shape, F32) for sh...  3.97 us
    pallas_call x2, Pallas kernels, gather_adjoint(): pl.pallas_call(kernel, out_shape=[jax.ShapeDtypeStruct((slots * TEAM,) +...  2.28 us
  transfers between devices with their start and end apart: 22, of which 7 were waited for; matrix products, arithmetic and copies ran while one was open for 1% of the time, Pallas kernels for 25%

profile of v14, /device:TPU:0, one launch (start us, length us, event | category | flops | bytes accessed | tf_op | source)
XLA Modules:
  0.0 68.5 jit_solution(3694770388433496937)
XLA Ops:
  0.6 2.3 %prepare.3 = (f32[33,8,512]{2,1,0:T(8,128)S(1)}, f32[33,8,512]{2,1,0:T(8,128)S(1)}, f32[8,512]{1,0:T(8,128)S(1)}) custom-call(f32[8,8]{1,0:T(8,128)} %refs_0_.3, f32[8]{0:T(128)} %refs_1_.3, f32[8,4,16,512]{3,2,1,0:T(8,128)} %refs_2_.3, f32[4,16,512]{2,1,0:T(8,128)} %refs_3_.3, s32[8,4,16,512]{3,2,1,0:T(8,128)} %refs_4_.4), custom_call_target="tpu_custom_call" | custom-call | bytes 4194304 | tf_op jit(solution)/shard_map/prepare/pallas_call | solution.py:157
  2.9 0.5 collective-permute-start.1
  3.5 1.7 %prepare.2 = (f32[32,8,512]{2,1,0:T(8,128)S(1)}, f32[32,8,512]{2,1,0:T(8,128)S(1)}) custom-call(f32[8,8]{1,0:T(8,128)} %refs_0_.3, f32[8]{0:T(128)} %refs_1_.3, f32[8,4,16,512]{3,2,1,0:T(8,128)} %refs_2_.3, f32[4,16,512]{2,1,0:T(8,128)} %refs_3_.3, s32[8,4,16,512]{3,2,1,0:T(8,128)} %refs_4_.4), custom_call_target="tpu_custom_call" | custom-call | bytes 4194304 | tf_op jit(solution)/shard_map/prepare/pallas_call | solution.py:157
  5.1 0.1 collective-permute-start
  5.3 0.0 collective-permute-done.1.theirs_ref
  5.3 0.1 merge.2
  5.3 3.0 %collective-permute-start.11 = (f32[32,8,512]{2,1,0:T(8,128)S(1)}, f32[32,8,512]{2,1,0:T(8,128)S(1)}, u32[]{:S(2)}, u32[]{:S(2)}) collective-permute-start(f32[32,8,512]{2,1,0:T(8,128)S(1)} %get-tuple-element.43), channel_id=1, source_target_pairs={{0,2},{1,3},{2,0},{3,1},{4,6},{5,7},{6,4},{7,5},{8,10},{9,11},{10,... | collective-permute-start | bytes 1572872 | tf_op jit(solution)/shard_map/ppermute | solution.py:575
  8.3 1.6 %collective-permute-start.2 = (f32[8,512]{1,0:T(8,128)S(1)}, f32[8,512]{1,0:T(8,128)S(1)}, u32[]{:S(2)}, u32[]{:S(2)}) collective-permute-start(f32[8,512]{1,0:T(8,128)S(1)} %get-tuple-element.34), channel_id=1, source_target_pairs={{4,0},{5,1},{6,2},{7,3},{0,4},{1,5},{2,6},{3,7},{12,8},{13,9},{14,... | collective-permute-start | bytes 49160 | tf_op jit(solution)/shard_map/ppermute | solution.py:593
  9.9 2.2 %collective-permute-done.2 = f32[8,512]{1,0:T(8,128)S(1)} collective-permute-done((f32[8,512]{1,0:T(8,128)S(1)}, f32[8,512]{1,0:T(8,128)S(1)}, u32[]{:S(2)}, u32[]{:S(2)}) %collective-permute-start.2) | collective-permute-done | bytes 16416 | tf_op jit(solution)/shard_map/ppermute | solution.py:593
  12.1 2.6 %collective-permute-start.3 = (f32[8,512]{1,0:T(8,128)S(1)}, f32[8,512]{1,0:T(8,128)S(1)}, u32[]{:S(2)}, u32[]{:S(2)}) collective-permute-start(f32[8,512]{1,0:T(8,128)S(1)} %add.15), channel_id=1, source_target_pairs={{8,0},{9,1},{10,2},{11,3},{12,4},{13,5},{14,6},{15,7},{0,8},{1,9},... | collective-permute-start | bytes 49160 | tf_op jit(solution)/shard_map/ppermute | solution.py:593
  14.7 2.0 %collective-permute-done.3 = f32[8,512]{1,0:T(8,128)S(1)} collective-permute-done((f32[8,512]{1,0:T(8,128)S(1)}, f32[8,512]{1,0:T(8,128)S(1)}, u32[]{:S(2)}, u32[]{:S(2)}) %collective-permute-start.3) | collective-permute-done | bytes 16416 | tf_op jit(solution)/shard_map/ppermute | solution.py:593
  16.7 0.1 merge.3
  16.8 0.3 collective-permute-start.5
  17.0 0.0 collective-permute-done.theirs_ref
  17.0 0.1 merge_near.3
  17.1 1.3 %collective-permute-start.10 = (f32[30,8,512]{2,1,0:T(8,128)S(1)}, f32[30,8,512]{2,1,0:T(8,128)S(1)}, u32[]{:S(2)}, u32[]{:S(2)}) collective-permute-start(f32[30,8,512]{2,1,0:T(8,128)S(1)} %get-tuple-element.42), channel_id=1, source_target_pairs={{2,6},{3,7},{4,0},{5,1},{6,10},{7,11},{8,4},{9,5},{10,14},{11,15},... | collective-permute-start | bytes 1474568 | tf_op jit(solution)/shard_map/ppermute | solution.py:584
  18.4 2.6 %collective-permute-done.11.ref.refs_2_ = f32[32,8,512]{2,1,0:T(8,128)S(1)} collective-permute-done((f32[32,8,512]{2,1,0:T(8,128)S(1)}, f32[32,8,512]{2,1,0:T(8,128)S(1)}, u32[]{:S(2)}, u32[]{:S(2)}) %collective-permute-start.11) | collective-permute-done | bytes 524320 | tf_op jit(solution)/shard_map/ppermute | solution.py:575
  21.1 4.1 %collective-permute-start.12 = (f32[30,8,512]{2,1,0:T(8,128)S(1)}, f32[30,8,512]{2,1,0:T(8,128)S(1)}, u32[]{:S(2)}, u32[]{:S(2)}) collective-permute-start(f32[30,8,512]{2,1,0:T(8,128)S(1)} %trim.3), channel_id=1, source_target_pairs={{0,4},{1,5},{4,8},{5,9},{6,2},{7,3},{8,12},{9,13},{10,6},{11,7},{1... | collective-permute-start | bytes 1474568 | tf_op jit(solution)/shard_map/ppermute | solution.py:584
  25.2 0.1 merge_near.2
  25.3 1.3 %collective-permute-start.4 = (f32[30,8,512]{2,1,0:T(8,128)S(1)}, f32[30,8,512]{2,1,0:T(8,128)S(1)}, u32[]{:S(2)}, u32[]{:S(2)}) collective-permute-start(f32[30,8,512]{2,1,0:T(8,128)S(1)} %get-tuple-element.36), channel_id=1, source_target_pairs={{2,6},{3,7},{4,0},{5,1},{6,10},{7,11},{8,4},{9,5},{10,14},{11,15},... | collective-permute-start | bytes 1474568 | tf_op jit(solution)/shard_map/ppermute | solution.py:584
  26.6 5.4 %collective-permute-done.5.ref.refs_2_ = f32[33,8,512]{2,1,0:T(8,128)S(1)} collective-permute-done((f32[33,8,512]{2,1,0:T(8,128)S(1)}, f32[33,8,512]{2,1,0:T(8,128)S(1)}, u32[]{:S(2)}, u32[]{:S(2)}) %collective-permute-start.5) | collective-permute-done | bytes 540704 | tf_op jit(solution)/shard_map/ppermute | solution.py:575
  32.1 3.8 %collective-permute-start.6 = (f32[30,8,512]{2,1,0:T(8,128)S(1)}, f32[30,8,512]{2,1,0:T(8,128)S(1)}, u32[]{:S(2)}, u32[]{:S(2)}) collective-permute-start(f32[30,8,512]{2,1,0:T(8,128)S(1)} %trim.2), channel_id=1, source_target_pairs={{0,4},{1,5},{4,8},{5,9},{6,2},{7,3},{8,12},{9,13},{10,6},{11,7},{1... | collective-permute-start | bytes 1474568 | tf_op jit(solution)/shard_map/ppermute | solution.py:584
  35.8 0.0 collective-permute-done.10.refs_1_
  35.9 0.0 collective-permute-done.12.refs_3_
  35.9 6.3 %solve.3 = (f32[8,8,512]{2,1,0:T(8,128)S(1)}, f32[8,8,512]{2,1,0:T(8,128)S(1)}, f32[8,8,512]{2,1,0:T(8,128)S(1)}, f32[8,8,512]{2,1,0:T(8,128)S(1)}, f32[16,512]{1,0:T(8,128)S(1)}) custom-call(f32[32,8,512]{2,1,0:T(8,128)S(1)} %get-tuple-element.41.refs_0_, f32[30,8,512]{2,1,0:T(8,128)S(1)} %collective-permute-done.10.refs_1_, ...), custom_call_target="tpu_custom_call" | custom-call | bytes 23068672 | tf_op jit(solution)/shard_map/solve/pallas_call | solution.py:410
  42.1 0.1 collective-permute-start.13
  42.2 0.6 collective-permute-start.14
  42.9 1.2 %collective-permute-start.15 = (f32[8,8,512]{2,1,0:T(8,128)S(1)}, f32[8,8,512]{2,1,0:T(8,128)S(1)}, u32[]{:S(2)}, u32[]{:S(2)}) collective-permute-start(f32[8,8,512]{2,1,0:T(8,128)S(1)} %get-tuple-element.47), channel_id=1, source_target_pairs={{0,3},{1,2},{2,1},{3,0},{4,7},{5,6},{6,5},{7,4},{8,11},{9,10},{10,... | collective-permute-start | bytes 393224 | tf_op jit(solution)/shard_map/ppermute | solution.py:575
  44.1 0.0 collective-permute-done.4.refs_1_
  44.1 1.5 %collective-permute-done.6.refs_3_ = f32[30,8,512]{2,1,0:T(8,128)S(1)} collective-permute-done((f32[30,8,512]{2,1,0:T(8,128)S(1)}, f32[30,8,512]{2,1,0:T(8,128)S(1)}, u32[]{:S(2)}, u32[]{:S(2)}) %collective-permute-start.6) | collective-permute-done | bytes 491552 | tf_op jit(solution)/shard_map/ppermute | solution.py:584
  45.6 6.3 %solve.2 = (f32[8,8,512]{2,1,0:T(8,128)S(1)}, f32[8,8,512]{2,1,0:T(8,128)S(1)}, f32[8,8,512]{2,1,0:T(8,128)S(1)}, f32[8,8,512]{2,1,0:T(8,128)S(1)}, f32[16,512]{1,0:T(8,128)S(1)}) custom-call(f32[32,8,512]{2,1,0:T(8,128)S(1)} %get-tuple-element.35.refs_0_, f32[30,8,512]{2,1,0:T(8,128)S(1)} %collective-permute-done.4.refs_1_, ...), custom_call_target="tpu_custom_call" | custom-call | bytes 23068672 | tf_op jit(solution)/shard_map/solve/pallas_call | solution.py:410
  51.9 0.0 collective-permute-done.13.refs_1_.refs_4_
  52.0 0.1 collective-permute-start.18
  52.0 2.5 %collective-permute-start.17 = (f32[16,512]{1,0:T(8,128)S(1)}, f32[16,512]{1,0:T(8,128)S(1)}, u32[]{:S(2)}, u32[]{:S(2)}) collective-permute-start(f32[16,512]{1,0:T(8,128)S(1)} %get-tuple-element.52), channel_id=1, source_target_pairs={{0,3},{1,2},{2,1},{3,0},{4,7},{5,6},{6,5},{7,4},{8,11},{9,10},{10,... | collective-permute-start | bytes 98312 | tf_op jit(solution)/shard_map/ppermute | solution.py:575
  54.6 0.0 collective-permute-start.16
  54.6 0.1 collective-permute-start.7
  54.7 1.9 %collective-permute-start.8 = (f32[8,8,512]{2,1,0:T(8,128)S(1)}, f32[8,8,512]{2,1,0:T(8,128)S(1)}, u32[]{:S(2)}, u32[]{:S(2)}) collective-permute-start(f32[8,8,512]{2,1,0:T(8,128)S(1)} %get-tuple-element.39), channel_id=1, source_target_pairs={{0,2},{1,3},{2,0},{3,1},{4,6},{5,7},{6,4},{7,5},{8,10},{9,11},{10,... | collective-permute-start | bytes 393224 | tf_op jit(solution)/shard_map/ppermute | solution.py:575
  56.6 0.1 collective-permute-start.9
  56.7 2.1 %collective-permute-done.16 = f32[16,512]{1,0:T(8,128)S(1)} collective-permute-done((f32[16,512]{1,0:T(8,128)S(1)}, f32[16,512]{1,0:T(8,128)S(1)}, u32[]{:S(2)}, u32[]{:S(2)}) %collective-permute-start.16) | collective-permute-done | bytes 32800 | tf_op jit(solution)/shard_map/ppermute | solution.py:575
  58.8 1.6 %collective-permute-start.19 = (f32[1,16,512]{2,1,0:T(8,128)S(1)}, f32[1,16,512]{2,1,0:T(8,128)S(1)}, u32[]{:S(2)}, u32[]{:S(2)}) collective-permute-start(f32[1,16,512]{2,1,0:T(8,128)S(1)} %add_bitcast_fusion.refs_0_), channel_id=1, source_target_pairs={{4,0},{5,1},{6,2},{7,3},{0,4},{1,5},{2,6},{3,7},{12,8},{13,9},{14,... | collective-permute-start | bytes 98312 | tf_op jit(solution)/shard_map/ppermute | solution.py:593
  60.4 1.3 %collective-permute-start.20 = (f32[1,16,512]{2,1,0:T(8,128)S(1)}, f32[1,16,512]{2,1,0:T(8,128)S(1)}, u32[]{:S(2)}, u32[]{:S(2)}) collective-permute-start(f32[1,16,512]{2,1,0:T(8,128)S(1)} %add_bitcast_fusion.refs_0_), channel_id=1, source_target_pairs={{8,0},{9,1},{10,2},{11,3},{12,4},{13,5},{14,6},{15,7},{0,8},{1,9},... | collective-permute-start | bytes 98312 | tf_op jit(solution)/shard_map/ppermute | solution.py:593
  61.7 1.6 %collective-permute-start.21 = (f32[1,16,512]{2,1,0:T(8,128)S(1)}, f32[1,16,512]{2,1,0:T(8,128)S(1)}, u32[]{:S(2)}, u32[]{:S(2)}) collective-permute-start(f32[1,16,512]{2,1,0:T(8,128)S(1)} %add_bitcast_fusion.refs_0_), channel_id=1, source_target_pairs={{12,0},{13,1},{14,2},{15,3},{8,4},{9,5},{10,6},{11,7},{4,8},{5,9},... | collective-permute-start | bytes 98312 | tf_op jit(solution)/shard_map/ppermute | solution.py:593
  63.3 0.5 slice_bitcast_fusion.1
  63.8 1.4 %gather_adjoint.2 = (f32[8,4,16,512]{3,2,1,0:T(8,128)}, f32[8,128]{1,0:T(8,128)}) custom-call(f32[8,8,512]{2,1,0:T(8,128)S(1)} %get-tuple-element.44.refs_0_, f32[8,8,512]{2,1,0:T(8,128)S(1)} %collective-permute-done.13.refs_1_.refs_4_, f32[8,8,512]{2,1,0:T(8,128)S(1)} %collective-permute-done.14.refs_2_.refs_5_, ...), custom_call_target="tpu_custom_call" | custom-call | bytes 2097152 | tf_op jit(solution)/shard_map/gather_adjoint/pallas_call | solution.py:493
  65.3 0.0 copy-start.1
  65.3 0.8 %gather_adjoint.3 = (f32[8,4,16,512]{3,2,1,0:T(8,128)}, f32[8,128]{1,0:T(8,128)S(1)}) custom-call(f32[8,8,512]{2,1,0:T(8,128)S(1)} %get-tuple-element.37.refs_0_, f32[8,8,512]{2,1,0:T(8,128)S(1)} %collective-permute-done.7.refs_1_, f32[8,8,512]{2,1,0:T(8,128)S(1)} %collective-permute-done.8.refs_2_, ...), custom_call_target="tpu_custom_call", output_to_operand_aliasing={{0}: (4, {})} | custom-call | bytes 2097152 | tf_op jit(solution)/shard_map/gather_adjoint/pallas_call | solution.py:493
  66.2 1.2 %collective-permute-done.21.refs_3_ = f32[1,16,512]{2,1,0:T(8,128)S(1)} collective-permute-done((f32[1,16,512]{2,1,0:T(8,128)S(1)}, f32[1,16,512]{2,1,0:T(8,128)S(1)}, u32[]{:S(2)}, u32[]{:S(2)}) %collective-permute-start.21) | collective-permute-done | bytes 32800 | tf_op jit(solution)/shard_map/ppermute | solution.py:593
  67.4 1.1 %control.1 = f32[32,512]{1,0:T(8,128)} custom-call(f32[1,16,512]{2,1,0:T(8,128)S(1)} %add_bitcast_fusion.refs_0_, f32[1,16,512]{2,1,0:T(8,128)S(1)} %collective-permute-done.19.refs_1_, f32[1,16,512]{2,1,0:T(8,128)S(1)} %collective-permute-done.20.refs_2_, f32[1,16,512]{2,1,0:T(8,128)S(1)} %collective-permute-done.21.refs_3_, f32[16,32,64]{2,1,0:T(8,128)S(1)} %copy-done.1, ...), custom_call_target="tpu_custom_call" | custom-call | tf_op jit(solution)/shard_map/control/pallas_call | solution.py:543
  (19 shorter events, 0.2 us)
Async XLA Ops:
  2.9 2.3 %collective-permute-start.1 = (f32[33,8,512]{2,1,0:T(8,128)S(1)}, f32[33,8,512]{2,1,0:T(8,128)S(1)}, u32[]{:S(2)}, u32[]{:S(2)}) collective-permute-start(f32[33,8,512]{2,1,0:T(8,128)S(1)} %get-tuple-element.32), channel_id=1, source_target_pairs={{0,1},{1,0},{2,3},{3,2},{4,5},{5,4},{6,7},{7,6},{8,9},{9,8},{10,11... | collective-permute-start | bytes 1622024 | tf_op jit(solution)/shard_map/ppermute | solution.py:575
  5.1 11.9 %collective-permute-start = (f32[32,8,512]{2,1,0:T(8,128)S(1)}, f32[32,8,512]{2,1,0:T(8,128)S(1)}, u32[]{:S(2)}, u32[]{:S(2)}) collective-permute-start(f32[32,8,512]{2,1,0:T(8,128)S(1)} %get-tuple-element.30), channel_id=1, source_target_pairs={{0,1},{1,0},{2,3},{3,2},{4,5},{5,4},{6,7},{7,6},{8,9},{9,8},{10,11... | collective-permute-start | bytes 1572872 | tf_op jit(solution)/shard_map/ppermute | solution.py:575
  5.3 15.7 %collective-permute-start.11 = (f32[32,8,512]{2,1,0:T(8,128)S(1)}, f32[32,8,512]{2,1,0:T(8,128)S(1)}, u32[]{:S(2)}, u32[]{:S(2)}) collective-permute-start(f32[32,8,512]{2,1,0:T(8,128)S(1)} %get-tuple-element.43), channel_id=1, source_target_pairs={{0,2},{1,3},{2,0},{3,1},{4,6},{5,7},{6,4},{7,5},{8,10},{9,11},{10,... | collective-permute-start | bytes 1572872 | tf_op jit(solution)/shard_map/ppermute | solution.py:575
  8.3 3.7 %collective-permute-start.2 = (f32[8,512]{1,0:T(8,128)S(1)}, f32[8,512]{1,0:T(8,128)S(1)}, u32[]{:S(2)}, u32[]{:S(2)}) collective-permute-start(f32[8,512]{1,0:T(8,128)S(1)} %get-tuple-element.34), channel_id=1, source_target_pairs={{4,0},{5,1},{6,2},{7,3},{0,4},{1,5},{2,6},{3,7},{12,8},{13,9},{14,... | collective-permute-start | bytes 49160 | tf_op jit(solution)/shard_map/ppermute | solution.py:593
  12.1 4.6 %collective-permute-start.3 = (f32[8,512]{1,0:T(8,128)S(1)}, f32[8,512]{1,0:T(8,128)S(1)}, u32[]{:S(2)}, u32[]{:S(2)}) collective-permute-start(f32[8,512]{1,0:T(8,128)S(1)} %add.15), channel_id=1, source_target_pairs={{8,0},{9,1},{10,2},{11,3},{12,4},{13,5},{14,6},{15,7},{0,8},{1,9},... | collective-permute-start | bytes 49160 | tf_op jit(solution)/shard_map/ppermute | solution.py:593
  16.8 15.3 %collective-permute-start.5 = (f32[33,8,512]{2,1,0:T(8,128)S(1)}, f32[33,8,512]{2,1,0:T(8,128)S(1)}, u32[]{:S(2)}, u32[]{:S(2)}) collective-permute-start(f32[33,8,512]{2,1,0:T(8,128)S(1)} %merge.3), channel_id=1, source_target_pairs={{0,2},{1,3},{2,0},{3,1},{4,6},{5,7},{6,4},{7,5},{8,10},{9,11},{10,... | collective-permute-start | bytes 1622024 | tf_op jit(solution)/shard_map/ppermute | solution.py:575
  17.1 18.7 %collective-permute-start.10 = (f32[30,8,512]{2,1,0:T(8,128)S(1)}, f32[30,8,512]{2,1,0:T(8,128)S(1)}, u32[]{:S(2)}, u32[]{:S(2)}) collective-permute-start(f32[30,8,512]{2,1,0:T(8,128)S(1)} %get-tuple-element.42), channel_id=1, source_target_pairs={{2,6},{3,7},{4,0},{5,1},{6,10},{7,11},{8,4},{9,5},{10,14},{11,15},... | collective-permute-start | bytes 1474568 | tf_op jit(solution)/shard_map/ppermute | solution.py:584
  21.1 14.8 %collective-permute-start.12 = (f32[30,8,512]{2,1,0:T(8,128)S(1)}, f32[30,8,512]{2,1,0:T(8,128)S(1)}, u32[]{:S(2)}, u32[]{:S(2)}) collective-permute-start(f32[30,8,512]{2,1,0:T(8,128)S(1)} %trim.3), channel_id=1, source_target_pairs={{0,4},{1,5},{4,8},{5,9},{6,2},{7,3},{8,12},{9,13},{10,6},{11,7},{1... | collective-permute-start | bytes 1474568 | tf_op jit(solution)/shard_map/ppermute | solution.py:584
  25.3 18.8 %collective-permute-start.4 = (f32[30,8,512]{2,1,0:T(8,128)S(1)}, f32[30,8,512]{2,1,0:T(8,128)S(1)}, u32[]{:S(2)}, u32[]{:S(2)}) collective-permute-start(f32[30,8,512]{2,1,0:T(8,128)S(1)} %get-tuple-element.36), channel_id=1, source_target_pairs={{2,6},{3,7},{4,0},{5,1},{6,10},{7,11},{8,4},{9,5},{10,14},{11,15},... | collective-permute-start | bytes 1474568 | tf_op jit(solution)/shard_map/ppermute | solution.py:584
  32.1 13.5 %collective-permute-start.6 = (f32[30,8,512]{2,1,0:T(8,128)S(1)}, f32[30,8,512]{2,1,0:T(8,128)S(1)}, u32[]{:S(2)}, u32[]{:S(2)}) collective-permute-start(f32[30,8,512]{2,1,0:T(8,128)S(1)} %trim.2), channel_id=1, source_target_pairs={{0,4},{1,5},{4,8},{5,9},{6,2},{7,3},{8,12},{9,13},{10,6},{11,7},{1... | collective-permute-start | bytes 1474568 | tf_op jit(solution)/shard_map/ppermute | solution.py:584
  42.1 9.8 %collective-permute-start.13 = (f32[8,8,512]{2,1,0:T(8,128)S(1)}, f32[8,8,512]{2,1,0:T(8,128)S(1)}, u32[]{:S(2)}, u32[]{:S(2)}) collective-permute-start(f32[8,8,512]{2,1,0:T(8,128)S(1)} %get-tuple-element.45), channel_id=1, source_target_pairs={{0,1},{1,0},{2,3},{3,2},{4,5},{5,4},{6,7},{7,6},{8,9},{9,8},{10,11... | collective-permute-start | bytes 393224 | tf_op jit(solution)/shard_map/ppermute | solution.py:575
  42.2 9.7 %collective-permute-start.14 = (f32[8,8,512]{2,1,0:T(8,128)S(1)}, f32[8,8,512]{2,1,0:T(8,128)S(1)}, u32[]{:S(2)}, u32[]{:S(2)}) collective-permute-start(f32[8,8,512]{2,1,0:T(8,128)S(1)} %get-tuple-element.46), channel_id=1, source_target_pairs={{0,2},{1,3},{2,0},{3,1},{4,6},{5,7},{6,4},{7,5},{8,10},{9,11},{10,... | collective-permute-start | bytes 393224 | tf_op jit(solution)/shard_map/ppermute | solution.py:575
  42.9 9.1 %collective-permute-start.15 = (f32[8,8,512]{2,1,0:T(8,128)S(1)}, f32[8,8,512]{2,1,0:T(8,128)S(1)}, u32[]{:S(2)}, u32[]{:S(2)}) collective-permute-start(f32[8,8,512]{2,1,0:T(8,128)S(1)} %get-tuple-element.47), channel_id=1, source_target_pairs={{0,3},{1,2},{2,1},{3,0},{4,7},{5,6},{6,5},{7,4},{8,11},{9,10},{10,... | collective-permute-start | bytes 393224 | tf_op jit(solution)/shard_map/ppermute | solution.py:575
  52.0 4.6 %collective-permute-start.18 = (f32[16,512]{1,0:T(8,128)S(1)}, f32[16,512]{1,0:T(8,128)S(1)}, u32[]{:S(2)}, u32[]{:S(2)}) collective-permute-start(f32[16,512]{1,0:T(8,128)S(1)} %get-tuple-element.52), channel_id=1, source_target_pairs={{0,1},{1,0},{2,3},{3,2},{4,5},{5,4},{6,7},{7,6},{8,9},{9,8},{10,11... | collective-permute-start | bytes 98312 | tf_op jit(solution)/shard_map/ppermute | solution.py:575
  52.0 4.7 %collective-permute-start.17 = (f32[16,512]{1,0:T(8,128)S(1)}, f32[16,512]{1,0:T(8,128)S(1)}, u32[]{:S(2)}, u32[]{:S(2)}) collective-permute-start(f32[16,512]{1,0:T(8,128)S(1)} %get-tuple-element.52), channel_id=1, source_target_pairs={{0,3},{1,2},{2,1},{3,0},{4,7},{5,6},{6,5},{7,4},{8,11},{9,10},{10,... | collective-permute-start | bytes 98312 | tf_op jit(solution)/shard_map/ppermute | solution.py:575
  54.6 4.3 %collective-permute-start.16 = (f32[16,512]{1,0:T(8,128)S(1)}, f32[16,512]{1,0:T(8,128)S(1)}, u32[]{:S(2)}, u32[]{:S(2)}) collective-permute-start(f32[16,512]{1,0:T(8,128)S(1)} %get-tuple-element.52), channel_id=1, source_target_pairs={{0,2},{1,3},{2,0},{3,1},{4,6},{5,7},{6,4},{7,5},{8,10},{9,11},{10,... | collective-permute-start | bytes 98312 | tf_op jit(solution)/shard_map/ppermute | solution.py:575
  54.6 7.1 %collective-permute-start.7 = (f32[8,8,512]{2,1,0:T(8,128)S(1)}, f32[8,8,512]{2,1,0:T(8,128)S(1)}, u32[]{:S(2)}, u32[]{:S(2)}) collective-permute-start(f32[8,8,512]{2,1,0:T(8,128)S(1)} %get-tuple-element.38), channel_id=1, source_target_pairs={{0,1},{1,0},{2,3},{3,2},{4,5},{5,4},{6,7},{7,6},{8,9},{9,8},{10,11... | collective-permute-start | bytes 393224 | tf_op jit(solution)/shard_map/ppermute | solution.py:575
  54.7 10.6 %collective-permute-start.8 = (f32[8,8,512]{2,1,0:T(8,128)S(1)}, f32[8,8,512]{2,1,0:T(8,128)S(1)}, u32[]{:S(2)}, u32[]{:S(2)}) collective-permute-start(f32[8,8,512]{2,1,0:T(8,128)S(1)} %get-tuple-element.39), channel_id=1, source_target_pairs={{0,2},{1,3},{2,0},{3,1},{4,6},{5,7},{6,4},{7,5},{8,10},{9,11},{10,... | collective-permute-start | bytes 393224 | tf_op jit(solution)/shard_map/ppermute | solution.py:575
  56.6 8.7 %collective-permute-start.9 = (f32[8,8,512]{2,1,0:T(8,128)S(1)}, f32[8,8,512]{2,1,0:T(8,128)S(1)}, u32[]{:S(2)}, u32[]{:S(2)}) collective-permute-start(f32[8,8,512]{2,1,0:T(8,128)S(1)} %get-tuple-element.40), channel_id=1, source_target_pairs={{0,3},{1,2},{2,1},{3,0},{4,7},{5,6},{6,5},{7,4},{8,11},{9,10},{10,... | collective-permute-start | bytes 393224 | tf_op jit(solution)/shard_map/ppermute | solution.py:575
  58.8 7.3 %collective-permute-start.19 = (f32[1,16,512]{2,1,0:T(8,128)S(1)}, f32[1,16,512]{2,1,0:T(8,128)S(1)}, u32[]{:S(2)}, u32[]{:S(2)}) collective-permute-start(f32[1,16,512]{2,1,0:T(8,128)S(1)} %add_bitcast_fusion.refs_0_), channel_id=1, source_target_pairs={{4,0},{5,1},{6,2},{7,3},{0,4},{1,5},{2,6},{3,7},{12,8},{13,9},{14,... | collective-permute-start | bytes 98312 | tf_op jit(solution)/shard_map/ppermute | solution.py:593
  60.4 5.7 %collective-permute-start.20 = (f32[1,16,512]{2,1,0:T(8,128)S(1)}, f32[1,16,512]{2,1,0:T(8,128)S(1)}, u32[]{:S(2)}, u32[]{:S(2)}) collective-permute-start(f32[1,16,512]{2,1,0:T(8,128)S(1)} %add_bitcast_fusion.refs_0_), channel_id=1, source_target_pairs={{8,0},{9,1},{10,2},{11,3},{12,4},{13,5},{14,6},{15,7},{0,8},{1,9},... | collective-permute-start | bytes 98312 | tf_op jit(solution)/shard_map/ppermute | solution.py:593
  61.7 5.7 %collective-permute-start.21 = (f32[1,16,512]{2,1,0:T(8,128)S(1)}, f32[1,16,512]{2,1,0:T(8,128)S(1)}, u32[]{:S(2)}, u32[]{:S(2)}) collective-permute-start(f32[1,16,512]{2,1,0:T(8,128)S(1)} %add_bitcast_fusion.refs_0_), channel_id=1, source_target_pairs={{12,0},{13,1},{14,2},{15,3},{8,4},{9,5},{10,6},{11,7},{4,8},{5,9},... | collective-permute-start | bytes 98312 | tf_op jit(solution)/shard_map/ppermute | solution.py:593
  63.8 3.6 %copy-start = (f32[512,512]{1,0:T(8,128)S(1)}, f32[512,512]{1,0:T(8,128)}, u32[]{:S(2)}) copy-start(f32[512,512]{1,0:T(8,128)} %constant.5.clone.refs_5_) | copy-start | bytes 3145732
  65.3 2.1 %copy-start.1 = (f32[16,32,64]{2,1,0:T(8,128)S(1)}, f32[16,32,64]{2,1,0:T(8,128)}, u32[]{:S(2)}) copy-start(f32[16,32,64]{2,1,0:T(8,128)} %constant.4.clone.refs_4_) | copy-start | bytes 393220

commit v15 on v12

--- a/solution.py
+++ b/solution.py
@@ -276,93 +276,154 @@
         body(p)
 
 
-def solve(near, far, near_halo, far_halo, planes):
-    inputs = [near, near_halo, far, far_halo]
+def ahead_x(v):
+    return pltpu.roll(v, v.shape[1] - 1, 1)
+
+
+def behind_x(v):
+    return pltpu.roll(v, 1, 1)
+
+
+def ahead_y(v):
+    return pltpu.roll(v, v.shape[0] - 1, 0)
+
+
+def behind_y(v):
+    return pltpu.roll(v, 1, 0)
+
+
+def set_up(planes, conductance, source, store):
+    centre, _ = chebyshev_constants(DEGREE)
+    here = [conductance(planes[0], t) for t in range(2)]
+    half, columns = here[0].shape
+    last_row = lax.broadcasted_iota(jnp.int32, (half, columns), 0) == half - 1
+    last_column = lax.broadcasted_iota(jnp.int32, (half, columns), 1) == columns - 1
+    w_below = [harmonic(conductance(planes[0] - 1, t), here[t]) for t in range(2)]
+    for p in planes:
+        above = [conductance(p + 1, t) for t in range(2)]
+        even, odd = here
+        w_pair = harmonic(even, odd)
+        w_next = jnp.where(last_row, 0.0, harmonic(odd, ahead_y(even)))
+        w_above = [harmonic(here[t], above[t]) for t in range(2)]
+        for t in range(2):
+            w_y = w_next if t else w_pair
+            w_y_behind = w_pair if t else behind_y(w_next)
+            w_x = jnp.where(last_column, 0.0, harmonic(here[t], ahead_x(here[t])))
+            w_x_behind = behind_x(w_x)
+            diagonal = (w_above[t] + w_below[t]) + (w_y + w_y_behind) + (w_x + w_x_behind) + STORAGE
+            inverse = reciprocal(diagonal)
+            weights = (w_above[t], w_below[t], w_y, w_y_behind, w_x, w_x_behind)
+            scaled = source(p, t) * inverse
+            store(p, t, [w * inverse for w in weights] + [scaled, scaled * (1.0 / centre)])
+        here, w_below = above, w_above
+
+
+def outside(v):
+    return jnp.where(v > 0.0, v, 1e30)
+
+
+def prepare_planes(near, far, near_halo, planes, after):
     half, columns = far.shape[-2:]
-    part = 2 * planes
-    halo = 2 * planes
-    own = TEAM * planes
+    halo, own, part = 2 * planes, TEAM * planes, 2 * planes
     span = own + 2 * halo
-    centre, coefficients = chebyshev_constants(DEGREE)
-    assert halo >= STEPS
-
-    def kernel(*refs):
-        ins, refs = refs[: len(inputs)], refs[len(inputs) :]
-        outs, face_ref, refs = refs[:TEAM], refs[TEAM], refs[TEAM + 1 :]
-        cond, u_a, u_b, s_a, s_b, zp, zm, yp, ym, xp, xm, t_a, t_b = refs
-        place = team_place()
-        side = place // 2
-        upper, lower = halo + own, 0
-        near_base = jnp.where(side == 0, upper, lower)
-        far_base = jnp.where(side == 0, lower, upper)
-        def outside(v):
-            return jnp.where(v > 0.0, v, 1e30)
+    first, count = halo + 1, own + halo - 2
+
+    def kernel(near_ref, halo_ref, far_ref, *refs):
+        refs = refs[len(after) :]
+        outs, edge_ref, (cond, start) = refs[:8], refs[8], refs[9:]
+        side = team_place() // 2
+
+        def place(natural):
+            return jnp.where(side == 0, natural, span - 1 - natural) - halo
 
         for core in range(2):
             for n in range(part):
                 base = halo + planes * core + n // 2
-                for ref, at in ((ins[0], base + part * side), (ins[2], base + part * (1 - side))):
-                    cond[at, n % 2] = outside(ref[core * 2 * part + n])
-                    t_a[at, n % 2] = ref[(core * 2 + 1) * part + n]
-        for ref, at in ((ins[1], near_base), (ins[3], far_base)):
-            skip = jnp.where(at == lower, 1, 0)
-            for n in range(2 * part):
-                cond[at + n // 2, n % 2] = outside(ref[n])
-            for n in range(2 * part - 2):
-                t_a[at + skip + n // 2, n % 2] = ref[2 * part + n]
-
-        last_row = lax.broadcasted_iota(jnp.int32, (half, columns), 0) == half - 1
-        last_column = lax.broadcasted_iota(jnp.int32, (half, columns), 1) == columns - 1
-
-        def ahead_x(v):
-            return pltpu.roll(v, columns - 1, 1)
-
-        def behind_x(v):
-            return pltpu.roll(v, 1, 1)
-
-        def ahead_y(v):
-            return pltpu.roll(v, half - 1, 0)
-
-        def behind_y(v):
-            return pltpu.roll(v, 1, 0)
-
-        def setup(p, w_z_before):
-            even, odd = cond[p, 0], cond[p, 1]
-            w_pair = harmonic(even, odd)
-            w_next = jnp.where(last_row, 0.0, harmonic(odd, ahead_y(even)))
-            w_z_here = []
-            for t, here in enumerate((even, odd)):
-                w_z = harmonic(here, cond[p + 1, t])
-                w_z_here.append(w_z)
-                w_z_behind = w_z_before[t]
-                w_y = w_next if t else w_pair
-                w_y_behind = w_pair if t else behind_y(w_next)
-                w_x = jnp.where(last_column, 0.0, harmonic(here, ahead_x(here)))
-                w_x_behind = behind_x(w_x)
-                diagonal = (w_z + w_z_behind) + (w_y + w_y_behind) + (w_x + w_x_behind) + STORAGE
-                inverse = reciprocal(diagonal)
-                zp[p, t] = w_z * inverse
-                zm[p, t] = w_z_behind * inverse
-                yp[p, t] = w_y * inverse
-                ym[p, t] = w_y_behind * inverse
-                xp[p, t] = w_x * inverse
-                xm[p, t] = w_x_behind * inverse
-                scaled = t_a[p, t] * inverse
-                u_a[p, t] = scaled
-                s_a[p, t] = scaled * (1.0 / centre)
-            return w_z_here
-
-        width = (span - 2) // 3
-
-        def setup_group(n, carry):
-            start = 1 + n * width
-            w_z = [harmonic(cond[start - 1, t], cond[start, t]) for t in range(2)]
-            for k in range(width):
-                w_z = setup(start + k, w_z)
+                for ref, at in ((near_ref, base + part * side), (far_ref, base + part * (1 - side))):
+                    cond[place(at), n % 2] = ref[core * 2 * part + n]
+                    start[place(at), n % 2] = ref[(core * 2 + 1) * part + n]
+        near_base = jnp.where(side == 0, halo + own, 0)
+        for n in range(2 * part):
+            cond[place(near_base + n // 2), n % 2] = outside(halo_ref[n])
+        for n in range(2 * part - 2):
+            start[place(near_base + side + n // 2), n % 2] = halo_ref[2 * part + n]
+        for p in range(2):
+            for t in range(2):
+                edge_ref[0, p, t] = cond[p, t]
+                edge_ref[1, p, t] = start[p, t]
+
+        width = count // 2
+
+        def group(n, carry):
+            begin = 1 + n * width
+
+            def store(p, t, values):
+                for ref, value in zip(outs, values):
+                    ref[p - 1, t] = value
+
+            set_up(
+                [begin + k for k in range(width)],
+                lambda p, t: cond[p, t],
+                lambda p, t: start[p, t],
+                store,
+            )
             return carry
 
-        assert (span - 2) % width == 0
-        lax.fori_loop(0, (span - 2) // width, setup_group, 0)
+        lax.fori_loop(0, 2, group, 0)
+
+    assert count % 2 == 0
+    vmem = pl.BlockSpec(memory_space=pltpu.VMEM)
+    results = pl.pallas_call(
+        kernel,
+        out_shape=[jax.ShapeDtypeStruct((count, 2, half, columns), F32)] * 8
+        + [jax.ShapeDtypeStruct((2, 2, 2, half, columns), F32)],
+        in_specs=[vmem] * 3 + [pl.BlockSpec(memory_space=pl.ANY)] * len(after),
+        out_specs=[vmem] * 9,
+        scratch_shapes=[pltpu.VMEM((own + halo, 2, half, columns), F32)] * 2,
+        compiler_params=pltpu.CompilerParams(vmem_limit_bytes=4 * MIB),
+        cost_estimate=pl.CostEstimate(flops=0, bytes_accessed=8 * MIB, transcendentals=0),
+        name="prepare_planes",
+    )(near, near_halo, far, *after)
+    return results[:8], results[8]
+
+
+def solve(made, edge, far_halo, planes):
+    half, columns = far_halo.shape[-2:]
+    halo, own, part = 2 * planes, TEAM * planes, 2 * planes
+    span = own + 2 * halo
+    cut = halo + 1
+    centre, coefficients = chebyshev_constants(DEGREE)
+    assert halo >= STEPS
+
+    def kernel(*refs):
+        high, (edge_ref, halo_ref), refs = refs[:8], refs[8:10], refs[10:]
+        outs, face_ref, refs = refs[:TEAM], refs[TEAM], refs[TEAM + 1 :]
+        low, (cond, start, u_a, u_b, s_a, s_b, t_a, t_b) = refs[:6], refs[6:]
+        place = team_place()
+        side = place // 2
+
+        def at(natural):
+            return jnp.where(side == 0, natural, span - 1 - natural)
+
+        far_base = jnp.where(side == 0, 0, halo + own)
+        for n in range(2 * part):
+            cond[at(far_base + n // 2), n % 2] = outside(halo_ref[n])
+        for n in range(2 * part - 2):
+            start[at(far_base + (1 - side) + n // 2), n % 2] = halo_ref[2 * part + n]
+        for p in range(2):
+            for t in range(2):
+                cond[halo + p, t] = edge_ref[0, p, t]
+                start[halo + p, t] = edge_ref[1, p, t]
+
+        def store(p, t, values):
+            for ref, value in zip((*low, u_a, s_a), values):
+                ref[p, t] = value
+
+        set_up(range(1, cut), lambda p, t: cond[p, t], lambda p, t: start[p, t], store)
+        for p in range(cut, span - 1):
+            for t in range(2):
+                u_a[p, t] = high[6][p - cut, t]
+                s_a[p, t] = high[7][p - cut, t]
 
         s_now, s_next, u_now, u_next, t_now, t_next = s_a, s_b, u_a, u_b, t_a, t_b
         for step in range(STEPS - 1):
@@ -373,14 +434,16 @@
                 keep, mix = 0.0, 1.0 / centre
             last = step == STEPS - 2
 
-            def advance(p):
+            def advance(p, fields, first):
+                zp, zm, yp, ym, xp, xm = fields
+                q = p - first
                 even, odd = s_now[p, 0], s_now[p, 1]
                 for t, s in enumerate((even, odd)):
                     ahead = ahead_y(even) if t else odd
                     behind = even if t else behind_y(odd)
-                    moved = zp[p, t] * s_now[p + 1, t] + zm[p, t] * s_now[p - 1, t]
-                    moved += yp[p, t] * ahead + ym[p, t] * behind
-                    moved += xp[p, t] * ahead_x(s) + xm[p, t] * behind_x(s)
+                    moved = zp[q, t] * s_now[p + 1, t] + zm[q, t] * s_now[p - 1, t]
+                    moved += yp[q, t] * ahead + ym[q, t] * behind
+                    moved += xp[q, t] * ahead_x(s) + xm[q, t] * behind_x(s)
                     new_u = (u_now[p, t] - s) + moved
                     new_s = mix * new_u if keep == 0.0 else keep * s + mix * new_u
                     if not last:
@@ -392,7 +455,8 @@
                         t_next[p, t] = t_now[p, t] + (s + new_s)
 
             margin = halo - (STEPS - 2 - step)
-            each(margin, span - margin, advance, 8)
+            each(cut, span - margin, lambda p: advance(p, high[:6], cut), 8)
+            each(margin, cut, lambda p: advance(p, low, 0), 8)
             s_now, s_next, u_now, u_next = s_next, s_now, u_next, u_now
             if step % 2 == 0:
                 t_now, t_next = t_next, t_now
@@ -401,23 +465,24 @@
             base = halo + planes * (place ^ m)
             for j in range(planes):
                 for t in range(2):
-                    outs[m][2 * j + t] = t_now[base + j, t]
+                    outs[m][2 * j + t] = t_now[at(base + j), t]
         for p in range(own):
-            face_ref[p : p + 1, :] = t_now[halo + p, 0, 0:1, :]
+            face_ref[p : p + 1, :] = t_now[at(halo + p), 0, 0:1, :]
 
     vmem = pl.BlockSpec(memory_space=pltpu.VMEM)
     field = pltpu.VMEM((span, 2, half, columns), F32)
+    small = pltpu.VMEM((halo + 2, 2, half, columns), F32)
     return pl.pallas_call(
         kernel,
         out_shape=[jax.ShapeDtypeStruct((2 * planes, half, columns), F32)] * TEAM
         + [jax.ShapeDtypeStruct((own, columns), F32)],
-        in_specs=[vmem] * len(inputs),
+        in_specs=[vmem] * 10,
         out_specs=[vmem] * (TEAM + 1),
-        scratch_shapes=[field] * 13,
-        compiler_params=pltpu.CompilerParams(vmem_limit_bytes=16 * MIB),
-        cost_estimate=pl.CostEstimate(flops=0, bytes_accessed=22 * MIB, transcendentals=0),
+        scratch_shapes=[small] * 8 + [field] * 6,
+        compiler_params=pltpu.CompilerParams(vmem_limit_bytes=10 * MIB),
+        cost_estimate=pl.CostEstimate(flops=0, bytes_accessed=16 * MIB, transcendentals=0),
         name="solve",
-    )(*inputs)
+    )(*made, edge, far_halo)
 
 
 def weigh(sums, faces, cells, after):
@@ -620,7 +685,8 @@
     pieces, faces = [], []
     for slot in range(slots):
         far_halo = along(trim(far[slot], size), False)
-        solved = solve(near[slot], far[slot], near_halo[slot], far_halo, planes)
+        made, edge = prepare_planes(near[slot], far[slot], near_halo[slot], planes, faces[-1:])
+        solved = solve(made, edge, far_halo, planes)
         pieces.append([solved[0]] + [swap(solved[m], m) for m in (1, 2, 3)])
         faces.append(solved[TEAM])
 

time: 68 us -> 66.6 us (0.979)
  waiting for transfers between devices: 17.4 us -> 16 us
    pallas_call x0 -> x2, Pallas kernels: none -> 2.74 us  [prepare_planes(): pl.pallas_call(kernel, out_shape=[jax.ShapeDtypeStruct((count, 2, half, c...]
    pallas_call x2, Pallas kernels: 12.6 us -> 10 us  [solve(): pl.pallas_call(kernel, out_shape=[jax.ShapeDtypeStruct((2 * planes, half,...]
    ppermute x4, waiting for transfers between devices: 1.53 us -> 0.01 us  [along(): return lax.ppermute(value, 'gz', pairs)]
  transfers between devices with their start and end apart: 22 -> 22, of which waited for: 9 -> 9; matrix products, arithmetic and copies ran while one was open for 1% -> 1% of each run, Pallas kernels for 23% -> 24%
where the time goes in v15:
time: 66.6 us; the launch traced here: 66.3 us
  starting transfers between devices  29.6 us (44%)
  Pallas kernels  19.3 us (29%)
  waiting for transfers between devices  16 us (24%)
  between operations  0.85 us (1%)
    ppermute x4, starting transfers between devices, along(): return lax.ppermute(value, 'gz', pairs)  10.4 us
    ppermute x13, starting transfers between devices, swap(): return lax.ppermute(value, 'gz', [(i, i ^ m) for i in range(slabs)])  10.3 us
    pallas_call x2, Pallas kernels, solve(): pl.pallas_call(kernel, out_shape=[jax.ShapeDtypeStruct((2 * planes, half,...  10 us
    ppermute x13, waiting for transfers between devices, swap(): return lax.ppermute(value, 'gz', [(i, i ^ m) for i in range(slabs)])  9.31 us
    ppermute x5, starting transfers between devices, from_teams(): heard.append(lax.ppermute(value, 'gz', pairs))  8.83 us
    ppermute x5, waiting for transfers between devices, from_teams(): heard.append(lax.ppermute(value, 'gz', pairs))  6.71 us
    pallas_call x2, Pallas kernels, prepare(): pl.pallas_call(kernel, out_shape=[jax.ShapeDtypeStruct(shape, F32) for sh...  3.97 us
    pallas_call x2, Pallas kernels, prepare_planes(): pl.pallas_call(kernel, out_shape=[jax.ShapeDtypeStruct((count, 2, half, c...  2.74 us
  transfers between devices with their start and end apart: 22, of which 9 were waited for; matrix products, arithmetic and copies ran while one was open for 1% of the time, Pallas kernels for 24%

profile of v15, /device:TPU:0, one launch (start us, length us, event | category | flops | bytes accessed | tf_op | source)
XLA Modules:
  0.0 66.3 jit_solution(2829254247134371893)
XLA Ops:
  0.6 2.3 %prepare.3 = (f32[33,8,512]{2,1,0:T(8,128)S(1)}, f32[33,8,512]{2,1,0:T(8,128)S(1)}, f32[8,512]{1,0:T(8,128)S(1)}) custom-call(f32[8,8]{1,0:T(8,128)} %refs_0_.3, f32[8]{0:T(128)} %refs_1_.3, f32[8,4,16,512]{3,2,1,0:T(8,128)} %refs_2_.3, f32[4,16,512]{2,1,0:T(8,128)} %refs_3_.3, s32[8,4,16,512]{3,2,1,0:T(8,128)} %refs_4_.4), custom_call_target="tpu_custom_call" | custom-call | bytes 4194304 | tf_op jit(solution)/shard_map/prepare/pallas_call | solution.py:157
  2.9 0.5 collective-permute-start.1
  3.5 1.7 %prepare.2 = (f32[32,8,512]{2,1,0:T(8,128)S(1)}, f32[32,8,512]{2,1,0:T(8,128)S(1)}) custom-call(f32[8,8]{1,0:T(8,128)} %refs_0_.3, f32[8]{0:T(128)} %refs_1_.3, f32[8,4,16,512]{3,2,1,0:T(8,128)} %refs_2_.3, f32[4,16,512]{2,1,0:T(8,128)} %refs_3_.3, s32[8,4,16,512]{3,2,1,0:T(8,128)} %refs_4_.4), custom_call_target="tpu_custom_call" | custom-call | bytes 4194304 | tf_op jit(solution)/shard_map/prepare/pallas_call | solution.py:157
  5.1 0.1 collective-permute-start
  5.3 0.0 collective-permute-done.1.theirs_ref
  5.3 0.1 merge.2
  5.3 3.0 %collective-permute-start.5 = (f32[32,8,512]{2,1,0:T(8,128)S(1)}, f32[32,8,512]{2,1,0:T(8,128)S(1)}, u32[]{:S(2)}, u32[]{:S(2)}) collective-permute-start(f32[32,8,512]{2,1,0:T(8,128)S(1)} %get-tuple-element.54), channel_id=1, source_target_pairs={{0,2},{1,3},{2,0},{3,1},{4,6},{5,7},{6,4},{7,5},{8,10},{9,11},{10,... | collective-permute-start | bytes 1572872 | tf_op jit(solution)/shard_map/ppermute | solution.py:637
  8.3 1.6 %collective-permute-start.2 = (f32[8,512]{1,0:T(8,128)S(1)}, f32[8,512]{1,0:T(8,128)S(1)}, u32[]{:S(2)}, u32[]{:S(2)}) collective-permute-start(f32[8,512]{1,0:T(8,128)S(1)} %get-tuple-element.51), channel_id=1, source_target_pairs={{4,0},{5,1},{6,2},{7,3},{0,4},{1,5},{2,6},{3,7},{12,8},{13,9},{14,... | collective-permute-start | bytes 49160 | tf_op jit(solution)/shard_map/ppermute | solution.py:655
  9.9 2.2 %collective-permute-done.2 = f32[8,512]{1,0:T(8,128)S(1)} collective-permute-done((f32[8,512]{1,0:T(8,128)S(1)}, f32[8,512]{1,0:T(8,128)S(1)}, u32[]{:S(2)}, u32[]{:S(2)}) %collective-permute-start.2) | collective-permute-done | bytes 16416 | tf_op jit(solution)/shard_map/ppermute | solution.py:655
  12.1 2.6 %collective-permute-start.3 = (f32[8,512]{1,0:T(8,128)S(1)}, f32[8,512]{1,0:T(8,128)S(1)}, u32[]{:S(2)}, u32[]{:S(2)}) collective-permute-start(f32[8,512]{1,0:T(8,128)S(1)} %add.15), channel_id=1, source_target_pairs={{8,0},{9,1},{10,2},{11,3},{12,4},{13,5},{14,6},{15,7},{0,8},{1,9},... | collective-permute-start | bytes 49160 | tf_op jit(solution)/shard_map/ppermute | solution.py:655
  14.7 2.0 %collective-permute-done.3 = f32[8,512]{1,0:T(8,128)S(1)} collective-permute-done((f32[8,512]{1,0:T(8,128)S(1)}, f32[8,512]{1,0:T(8,128)S(1)}, u32[]{:S(2)}, u32[]{:S(2)}) %collective-permute-start.3) | collective-permute-done | bytes 16416 | tf_op jit(solution)/shard_map/ppermute | solution.py:655
  16.7 0.1 merge.3
  16.8 0.3 collective-permute-start.11
  17.0 0.1 merge_near.2
  17.1 1.3 %collective-permute-start.4 = (f32[30,8,512]{2,1,0:T(8,128)S(1)}, f32[30,8,512]{2,1,0:T(8,128)S(1)}, u32[]{:S(2)}, u32[]{:S(2)}) collective-permute-start(f32[30,8,512]{2,1,0:T(8,128)S(1)} %get-tuple-element.53), channel_id=1, source_target_pairs={{2,6},{3,7},{4,0},{5,1},{6,10},{7,11},{8,4},{9,5},{10,14},{11,15},... | collective-permute-start | bytes 1474568 | tf_op jit(solution)/shard_map/ppermute | solution.py:646
  18.4 2.6 %collective-permute-done.5.far_ref.ref = f32[32,8,512]{2,1,0:T(8,128)S(1)} collective-permute-done((f32[32,8,512]{2,1,0:T(8,128)S(1)}, f32[32,8,512]{2,1,0:T(8,128)S(1)}, u32[]{:S(2)}, u32[]{:S(2)}) %collective-permute-start.5) | collective-permute-done | bytes 524320 | tf_op jit(solution)/shard_map/ppermute | solution.py:637
  21.1 4.1 %collective-permute-start.6 = (f32[30,8,512]{2,1,0:T(8,128)S(1)}, f32[30,8,512]{2,1,0:T(8,128)S(1)}, u32[]{:S(2)}, u32[]{:S(2)}) collective-permute-start(f32[30,8,512]{2,1,0:T(8,128)S(1)} %trim.2), channel_id=1, source_target_pairs={{0,4},{1,5},{4,8},{5,9},{6,2},{7,3},{8,12},{9,13},{10,6},{11,7},{1... | collective-permute-start | bytes 1474568 | tf_op jit(solution)/shard_map/ppermute | solution.py:646
  25.2 0.1 merge_near.3
  25.3 1.3 %collective-permute-start.10 = (f32[30,8,512]{2,1,0:T(8,128)S(1)}, f32[30,8,512]{2,1,0:T(8,128)S(1)}, u32[]{:S(2)}, u32[]{:S(2)}) collective-permute-start(f32[30,8,512]{2,1,0:T(8,128)S(1)} %get-tuple-element.69), channel_id=1, source_target_pairs={{2,6},{3,7},{4,0},{5,1},{6,10},{7,11},{8,4},{9,5},{10,14},{11,15},... | collective-permute-start | bytes 1474568 | tf_op jit(solution)/shard_map/ppermute | solution.py:646
  26.6 5.4 %collective-permute-done.11.far_ref.ref = f32[33,8,512]{2,1,0:T(8,128)S(1)} collective-permute-done((f32[33,8,512]{2,1,0:T(8,128)S(1)}, f32[33,8,512]{2,1,0:T(8,128)S(1)}, u32[]{:S(2)}, u32[]{:S(2)}) %collective-permute-start.11) | collective-permute-done | bytes 540704 | tf_op jit(solution)/shard_map/ppermute | solution.py:637
  32.1 3.8 %collective-permute-start.12 = (f32[30,8,512]{2,1,0:T(8,128)S(1)}, f32[30,8,512]{2,1,0:T(8,128)S(1)}, u32[]{:S(2)}, u32[]{:S(2)}) collective-permute-start(f32[30,8,512]{2,1,0:T(8,128)S(1)} %trim.3), channel_id=1, source_target_pairs={{0,4},{1,5},{4,8},{5,9},{6,2},{7,3},{8,12},{9,13},{10,6},{11,7},{1... | collective-permute-start | bytes 1474568 | tf_op jit(solution)/shard_map/ppermute | solution.py:646
  35.9 1.4 %prepare_planes.2 = (f32[22,2,8,512]{3,2,1,0:T(8,128)S(1)}, f32[22,2,8,512]{3,2,1,0:T(8,128)S(1)}, f32[22,2,8,512]{3,2,1,0:T(8,128)S(1)}, f32[22,2,8,512]{3,2,1,...) custom-call(f32[32,8,512]{2,1,0:T(8,128)S(1)} %get-tuple-element.52., ...), custom_call_target="tpu_custom_call" | custom-call | bytes 8388608 | tf_op jit(solution)/shard_map/prepare_planes/pallas_call | solution.py:376
  37.2 0.0 collective-permute-done.6.refs_9_
  37.2 5.2 %solve.2 = (f32[8,8,512]{2,1,0:T(8,128)S(1)}, f32[8,8,512]{2,1,0:T(8,128)S(1)}, f32[8,8,512]{2,1,0:T(8,128)S(1)}, f32[8,8,512]{2,1,0:T(8,128)S(1)}, f32[16,512]{1,0:T(8,128)S(1)}) custom-call(f32[22,2,8,512]{3,2,1,0:T(8,128)S(1)} %get-tuple-element.55.refs_0_, f32[22,2,8,512]{3,2,1,0:T(8,128)S(1)} %get-tuple-element.56.refs_1_, ...), custom_call_target="tpu_custom_call" | custom-call | bytes 16777216 | tf_op jit(solution)/shard_map/solve/pallas_call | solution.py:475
  42.4 0.1 collective-permute-start.7
  42.5 0.1 collective-permute-start.8
  42.6 1.8 %collective-permute-start.9 = (f32[8,8,512]{2,1,0:T(8,128)S(1)}, f32[8,8,512]{2,1,0:T(8,128)S(1)}, u32[]{:S(2)}, u32[]{:S(2)}) collective-permute-start(f32[8,8,512]{2,1,0:T(8,128)S(1)} %get-tuple-element.67), channel_id=1, source_target_pairs={{0,3},{1,2},{2,1},{3,0},{4,7},{5,6},{6,5},{7,4},{8,11},{9,10},{10,... | collective-permute-start | bytes 393224 | tf_op jit(solution)/shard_map/ppermute | solution.py:637
  44.3 0.0 collective-permute-done.10.halo_ref
  44.4 1.4 %prepare_planes.3 = (f32[22,2,8,512]{3,2,1,0:T(8,128)S(1)}, f32[22,2,8,512]{3,2,1,0:T(8,128)S(1)}, f32[22,2,8,512]{3,2,1,0:T(8,128)S(1)}, f32[22,2,8,512]{3,2,1,...) custom-call(f32[32,8,512]{2,1,0:T(8,128)S(1)} %get-tuple-element.68., ...), custom_call_target="tpu_custom_call" | custom-call | bytes 8388608 | tf_op jit(solution)/shard_map/prepare_planes/pallas_call | solution.py:376
  45.7 0.0 collective-permute-done.12.refs_9_
  45.8 4.8 %solve.3 = (f32[8,8,512]{2,1,0:T(8,128)S(1)}, f32[8,8,512]{2,1,0:T(8,128)S(1)}, f32[8,8,512]{2,1,0:T(8,128)S(1)}, f32[8,8,512]{2,1,0:T(8,128)S(1)}, f32[16,512]{1,0:T(8,128)S(1)}) custom-call(f32[22,2,8,512]{3,2,1,0:T(8,128)S(1)} %get-tuple-element.71.refs_0_, f32[22,2,8,512]{3,2,1,0:T(8,128)S(1)} %get-tuple-element.72.refs_1_, ...), custom_call_target="tpu_custom_call" | custom-call | bytes 16777216 | tf_op jit(solution)/shard_map/solve/pallas_call | solution.py:475
  50.6 0.0 copy-start
  50.6 0.1 collective-permute-done.9.refs_3_.refs_6_
  50.8 2.2 %collective-permute-start.16 = (f32[16,512]{1,0:T(8,128)S(1)}, f32[16,512]{1,0:T(8,128)S(1)}, u32[]{:S(2)}, u32[]{:S(2)}) collective-permute-start(f32[16,512]{1,0:T(8,128)S(1)} %get-tuple-element.86), channel_id=1, source_target_pairs={{0,2},{1,3},{2,0},{3,1},{4,6},{5,7},{6,4},{7,5},{8,10},{9,11},{10,... | collective-permute-start | bytes 98312 | tf_op jit(solution)/shard_map/ppermute | solution.py:637
  53.0 0.2 collective-permute-start.18
  53.2 0.3 collective-permute-start.13
  53.5 1.6 %collective-permute-start.14 = (f32[8,8,512]{2,1,0:T(8,128)S(1)}, f32[8,8,512]{2,1,0:T(8,128)S(1)}, u32[]{:S(2)}, u32[]{:S(2)}) collective-permute-start(f32[8,8,512]{2,1,0:T(8,128)S(1)} %get-tuple-element.82), channel_id=1, source_target_pairs={{0,2},{1,3},{2,0},{3,1},{4,6},{5,7},{6,4},{7,5},{8,10},{9,11},{10,... | collective-permute-start | bytes 393224 | tf_op jit(solution)/shard_map/ppermute | solution.py:637
  55.1 0.1 collective-permute-start.15
  55.3 1.0 %collective-permute-done.17 = f32[16,512]{1,0:T(8,128)S(1)} collective-permute-done((f32[16,512]{1,0:T(8,128)S(1)}, f32[16,512]{1,0:T(8,128)S(1)}, u32[]{:S(2)}, u32[]{:S(2)}) %collective-permute-start.17) | collective-permute-done | bytes 32800 | tf_op jit(solution)/shard_map/ppermute | solution.py:637
  56.3 2.8 %collective-permute-start.19 = (f32[1,16,512]{2,1,0:T(8,128)S(1)}, f32[1,16,512]{2,1,0:T(8,128)S(1)}, u32[]{:S(2)}, u32[]{:S(2)}) collective-permute-start(f32[1,16,512]{2,1,0:T(8,128)S(1)} %add_bitcast_fusion.refs_0_), channel_id=1, source_target_pairs={{4,0},{5,1},{6,2},{7,3},{8,4},{9,5},{10,6},{11,7},{12,8},{13,9},{1... | collective-permute-start | bytes 98312 | tf_op jit(solution)/shard_map/ppermute | solution.py:655
  59.2 0.3 collective-permute-start.20
  59.4 1.6 %collective-permute-start.21 = (f32[1,16,512]{2,1,0:T(8,128)S(1)}, f32[1,16,512]{2,1,0:T(8,128)S(1)}, u32[]{:S(2)}, u32[]{:S(2)}) collective-permute-start(f32[1,16,512]{2,1,0:T(8,128)S(1)} %add_bitcast_fusion.refs_0_), channel_id=1, source_target_pairs={{12,0},{13,1},{14,2},{15,3},{0,4},{1,5},{2,6},{3,7},{4,8},{5,9},{6... | collective-permute-start | bytes 98312 | tf_op jit(solution)/shard_map/ppermute | solution.py:655
  61.0 0.5 slice_bitcast_fusion.1
  61.5 0.1 collective-permute-done.15.refs_7_
  61.6 1.0 %gather_adjoint.1 = (f32[8,4,16,512]{3,2,1,0:T(8,128)}, f32[8,128]{1,0:T(8,128)S(1)}) custom-call(f32[8,8,512]{2,1,0:T(8,128)S(1)} %get-tuple-element.64.refs_0_, f32[8,8,512]{2,1,0:T(8,128)S(1)} %collective-permute-done.7.refs_1_.refs_4_, f32[8,8,512]{2,1,0:T(8,128)S(1)} %collective-permute-done.8.refs_2_.refs_5_, ...), custom_call_target="tpu_custom_call" | custom-call | bytes 4194304 | tf_op jit(solution)/shard_map/gather_adjoint/pallas_call | solution.py:557
  62.7 1.4 %collective-permute-done.20.refs_2_ = f32[1,16,512]{2,1,0:T(8,128)S(1)} collective-permute-done((f32[1,16,512]{2,1,0:T(8,128)S(1)}, f32[1,16,512]{2,1,0:T(8,128)S(1)}, u32[]{:S(2)}, u32[]{:S(2)}) %collective-permute-start.20) | collective-permute-done | bytes 32800 | tf_op jit(solution)/shard_map/ppermute | solution.py:655
  64.1 1.1 %collective-permute-done.21.refs_3_ = f32[1,16,512]{2,1,0:T(8,128)S(1)} collective-permute-done((f32[1,16,512]{2,1,0:T(8,128)S(1)}, f32[1,16,512]{2,1,0:T(8,128)S(1)}, u32[]{:S(2)}, u32[]{:S(2)}) %collective-permute-start.21) | collective-permute-done | bytes 32800 | tf_op jit(solution)/shard_map/ppermute | solution.py:655
  65.2 1.1 %control.1 = f32[32,512]{1,0:T(8,128)} custom-call(f32[1,16,512]{2,1,0:T(8,128)S(1)} %add_bitcast_fusion.refs_0_, f32[1,16,512]{2,1,0:T(8,128)S(1)} %collective-permute-done.19.refs_1_, f32[1,16,512]{2,1,0:T(8,128)S(1)} %collective-permute-done.20.refs_2_, f32[1,16,512]{2,1,0:T(8,128)S(1)} %collective-permute-done.21.refs_3_, f32[16,32,64]{2,1,0:T(8,128)S(1)} %copy-done.1, ...), custom_call_target="tpu_custom_call" | custom-call | tf_op jit(solution)/shard_map/control/pallas_call | solution.py:609
  (20 shorter events, 0.2 us)
Async XLA Ops:
  2.9 2.3 %collective-permute-start.1 = (f32[33,8,512]{2,1,0:T(8,128)S(1)}, f32[33,8,512]{2,1,0:T(8,128)S(1)}, u32[]{:S(2)}, u32[]{:S(2)}) collective-permute-start(f32[33,8,512]{2,1,0:T(8,128)S(1)} %get-tuple-element.49), channel_id=1, source_target_pairs={{0,1},{1,0},{2,3},{3,2},{4,5},{5,4},{6,7},{7,6},{8,9},{9,8},{10,11... | collective-permute-start | bytes 1622024 | tf_op jit(solution)/shard_map/ppermute | solution.py:637
  5.1 11.9 %collective-permute-start = (f32[32,8,512]{2,1,0:T(8,128)S(1)}, f32[32,8,512]{2,1,0:T(8,128)S(1)}, u32[]{:S(2)}, u32[]{:S(2)}) collective-permute-start(f32[32,8,512]{2,1,0:T(8,128)S(1)} %get-tuple-element.47), channel_id=1, source_target_pairs={{0,1},{1,0},{2,3},{3,2},{4,5},{5,4},{6,7},{7,6},{8,9},{9,8},{10,11... | collective-permute-start | bytes 1572872 | tf_op jit(solution)/shard_map/ppermute | solution.py:637
  5.3 15.7 %collective-permute-start.5 = (f32[32,8,512]{2,1,0:T(8,128)S(1)}, f32[32,8,512]{2,1,0:T(8,128)S(1)}, u32[]{:S(2)}, u32[]{:S(2)}) collective-permute-start(f32[32,8,512]{2,1,0:T(8,128)S(1)} %get-tuple-element.54), channel_id=1, source_target_pairs={{0,2},{1,3},{2,0},{3,1},{4,6},{5,7},{6,4},{7,5},{8,10},{9,11},{10,... | collective-permute-start | bytes 1572872 | tf_op jit(solution)/shard_map/ppermute | solution.py:637
  8.3 3.7 %collective-permute-start.2 = (f32[8,512]{1,0:T(8,128)S(1)}, f32[8,512]{1,0:T(8,128)S(1)}, u32[]{:S(2)}, u32[]{:S(2)}) collective-permute-start(f32[8,512]{1,0:T(8,128)S(1)} %get-tuple-element.51), channel_id=1, source_target_pairs={{4,0},{5,1},{6,2},{7,3},{0,4},{1,5},{2,6},{3,7},{12,8},{13,9},{14,... | collective-permute-start | bytes 49160 | tf_op jit(solution)/shard_map/ppermute | solution.py:655
  12.1 4.6 %collective-permute-start.3 = (f32[8,512]{1,0:T(8,128)S(1)}, f32[8,512]{1,0:T(8,128)S(1)}, u32[]{:S(2)}, u32[]{:S(2)}) collective-permute-start(f32[8,512]{1,0:T(8,128)S(1)} %add.15), channel_id=1, source_target_pairs={{8,0},{9,1},{10,2},{11,3},{12,4},{13,5},{14,6},{15,7},{0,8},{1,9},... | collective-permute-start | bytes 49160 | tf_op jit(solution)/shard_map/ppermute | solution.py:655
  16.8 15.3 %collective-permute-start.11 = (f32[33,8,512]{2,1,0:T(8,128)S(1)}, f32[33,8,512]{2,1,0:T(8,128)S(1)}, u32[]{:S(2)}, u32[]{:S(2)}) collective-permute-start(f32[33,8,512]{2,1,0:T(8,128)S(1)} %merge.3), channel_id=1, source_target_pairs={{0,2},{1,3},{2,0},{3,1},{4,6},{5,7},{6,4},{7,5},{8,10},{9,11},{10,... | collective-permute-start | bytes 1622024 | tf_op jit(solution)/shard_map/ppermute | solution.py:637
  17.1 18.7 %collective-permute-start.4 = (f32[30,8,512]{2,1,0:T(8,128)S(1)}, f32[30,8,512]{2,1,0:T(8,128)S(1)}, u32[]{:S(2)}, u32[]{:S(2)}) collective-permute-start(f32[30,8,512]{2,1,0:T(8,128)S(1)} %get-tuple-element.53), channel_id=1, source_target_pairs={{2,6},{3,7},{4,0},{5,1},{6,10},{7,11},{8,4},{9,5},{10,14},{11,15},... | collective-permute-start | bytes 1474568 | tf_op jit(solution)/shard_map/ppermute | solution.py:646
  21.1 16.1 %collective-permute-start.6 = (f32[30,8,512]{2,1,0:T(8,128)S(1)}, f32[30,8,512]{2,1,0:T(8,128)S(1)}, u32[]{:S(2)}, u32[]{:S(2)}) collective-permute-start(f32[30,8,512]{2,1,0:T(8,128)S(1)} %trim.2), channel_id=1, source_target_pairs={{0,4},{1,5},{4,8},{5,9},{6,2},{7,3},{8,12},{9,13},{10,6},{11,7},{1... | collective-permute-start | bytes 1474568 | tf_op jit(solution)/shard_map/ppermute | solution.py:646
  25.3 19.1 %collective-permute-start.10 = (f32[30,8,512]{2,1,0:T(8,128)S(1)}, f32[30,8,512]{2,1,0:T(8,128)S(1)}, u32[]{:S(2)}, u32[]{:S(2)}) collective-permute-start(f32[30,8,512]{2,1,0:T(8,128)S(1)} %get-tuple-element.69), channel_id=1, source_target_pairs={{2,6},{3,7},{4,0},{5,1},{6,10},{7,11},{8,4},{9,5},{10,14},{11,15},... | collective-permute-start | bytes 1474568 | tf_op jit(solution)/shard_map/ppermute | solution.py:646
  32.1 13.7 %collective-permute-start.12 = (f32[30,8,512]{2,1,0:T(8,128)S(1)}, f32[30,8,512]{2,1,0:T(8,128)S(1)}, u32[]{:S(2)}, u32[]{:S(2)}) collective-permute-start(f32[30,8,512]{2,1,0:T(8,128)S(1)} %trim.3), channel_id=1, source_target_pairs={{0,4},{1,5},{4,8},{5,9},{6,2},{7,3},{8,12},{9,13},{10,6},{11,7},{1... | collective-permute-start | bytes 1474568 | tf_op jit(solution)/shard_map/ppermute | solution.py:646
  42.4 8.2 %collective-permute-start.7 = (f32[8,8,512]{2,1,0:T(8,128)S(1)}, f32[8,8,512]{2,1,0:T(8,128)S(1)}, u32[]{:S(2)}, u32[]{:S(2)}) collective-permute-start(f32[8,8,512]{2,1,0:T(8,128)S(1)} %get-tuple-element.65), channel_id=1, source_target_pairs={{0,1},{1,0},{2,3},{3,2},{4,5},{5,4},{6,7},{7,6},{8,9},{9,8},{10,11... | collective-permute-start | bytes 393224 | tf_op jit(solution)/shard_map/ppermute | solution.py:637
  42.5 8.1 %collective-permute-start.8 = (f32[8,8,512]{2,1,0:T(8,128)S(1)}, f32[8,8,512]{2,1,0:T(8,128)S(1)}, u32[]{:S(2)}, u32[]{:S(2)}) collective-permute-start(f32[8,8,512]{2,1,0:T(8,128)S(1)} %get-tuple-element.66), channel_id=1, source_target_pairs={{0,2},{1,3},{2,0},{3,1},{4,6},{5,7},{6,4},{7,5},{8,10},{9,11},{10,... | collective-permute-start | bytes 393224 | tf_op jit(solution)/shard_map/ppermute | solution.py:637
  42.6 8.2 %collective-permute-start.9 = (f32[8,8,512]{2,1,0:T(8,128)S(1)}, f32[8,8,512]{2,1,0:T(8,128)S(1)}, u32[]{:S(2)}, u32[]{:S(2)}) collective-permute-start(f32[8,8,512]{2,1,0:T(8,128)S(1)} %get-tuple-element.67), channel_id=1, source_target_pairs={{0,3},{1,2},{2,1},{3,0},{4,7},{5,6},{6,5},{7,4},{8,11},{9,10},{10,... | collective-permute-start | bytes 393224 | tf_op jit(solution)/shard_map/ppermute | solution.py:637
  50.6 14.6 %copy-start = (f32[512,512]{1,0:T(8,128)S(1)}, f32[512,512]{1,0:T(8,128)}, u32[]{:S(2)}) copy-start(f32[512,512]{1,0:T(8,128)} %constant.5.clone.refs_5_) | copy-start | bytes 3145732
  50.8 4.4 %collective-permute-start.16 = (f32[16,512]{1,0:T(8,128)S(1)}, f32[16,512]{1,0:T(8,128)S(1)}, u32[]{:S(2)}, u32[]{:S(2)}) collective-permute-start(f32[16,512]{1,0:T(8,128)S(1)} %get-tuple-element.86), channel_id=1, source_target_pairs={{0,2},{1,3},{2,0},{3,1},{4,6},{5,7},{6,4},{7,5},{8,10},{9,11},{10,... | collective-permute-start | bytes 98312 | tf_op jit(solution)/shard_map/ppermute | solution.py:637
  53.0 3.3 %collective-permute-start.17 = (f32[16,512]{1,0:T(8,128)S(1)}, f32[16,512]{1,0:T(8,128)S(1)}, u32[]{:S(2)}, u32[]{:S(2)}) collective-permute-start(f32[16,512]{1,0:T(8,128)S(1)} %get-tuple-element.86), channel_id=1, source_target_pairs={{0,3},{1,2},{2,1},{3,0},{4,7},{5,6},{6,5},{7,4},{8,11},{9,10},{10,... | collective-permute-start | bytes 98312 | tf_op jit(solution)/shard_map/ppermute | solution.py:637
  53.0 3.3 %collective-permute-start.18 = (f32[16,512]{1,0:T(8,128)S(1)}, f32[16,512]{1,0:T(8,128)S(1)}, u32[]{:S(2)}, u32[]{:S(2)}) collective-permute-start(f32[16,512]{1,0:T(8,128)S(1)} %get-tuple-element.86), channel_id=1, source_target_pairs={{0,1},{1,0},{2,3},{3,2},{4,5},{5,4},{6,7},{7,6},{8,9},{9,8},{10,11... | collective-permute-start | bytes 98312 | tf_op jit(solution)/shard_map/ppermute | solution.py:637
  53.2 6.3 %collective-permute-start.13 = (f32[8,8,512]{2,1,0:T(8,128)S(1)}, f32[8,8,512]{2,1,0:T(8,128)S(1)}, u32[]{:S(2)}, u32[]{:S(2)}) collective-permute-start(f32[8,8,512]{2,1,0:T(8,128)S(1)} %get-tuple-element.81), channel_id=1, source_target_pairs={{0,1},{1,0},{2,3},{3,2},{4,5},{5,4},{6,7},{7,6},{8,9},{9,8},{10,11... | collective-permute-start | bytes 393224 | tf_op jit(solution)/shard_map/ppermute | solution.py:637
  53.5 8.0 %collective-permute-start.14 = (f32[8,8,512]{2,1,0:T(8,128)S(1)}, f32[8,8,512]{2,1,0:T(8,128)S(1)}, u32[]{:S(2)}, u32[]{:S(2)}) collective-permute-start(f32[8,8,512]{2,1,0:T(8,128)S(1)} %get-tuple-element.82), channel_id=1, source_target_pairs={{0,2},{1,3},{2,0},{3,1},{4,6},{5,7},{6,4},{7,5},{8,10},{9,11},{10,... | collective-permute-start | bytes 393224 | tf_op jit(solution)/shard_map/ppermute | solution.py:637
  55.1 6.5 %collective-permute-start.15 = (f32[8,8,512]{2,1,0:T(8,128)S(1)}, f32[8,8,512]{2,1,0:T(8,128)S(1)}, u32[]{:S(2)}, u32[]{:S(2)}) collective-permute-start(f32[8,8,512]{2,1,0:T(8,128)S(1)} %get-tuple-element.83), channel_id=1, source_target_pairs={{0,3},{1,2},{2,1},{3,0},{4,7},{5,6},{6,5},{7,4},{8,11},{9,10},{10,... | collective-permute-start | bytes 393224 | tf_op jit(solution)/shard_map/ppermute | solution.py:637
  56.3 6.3 %collective-permute-start.19 = (f32[1,16,512]{2,1,0:T(8,128)S(1)}, f32[1,16,512]{2,1,0:T(8,128)S(1)}, u32[]{:S(2)}, u32[]{:S(2)}) collective-permute-start(f32[1,16,512]{2,1,0:T(8,128)S(1)} %add_bitcast_fusion.refs_0_), channel_id=1, source_target_pairs={{4,0},{5,1},{6,2},{7,3},{8,4},{9,5},{10,6},{11,7},{12,8},{13,9},{1... | collective-permute-start | bytes 98312 | tf_op jit(solution)/shard_map/ppermute | solution.py:655
  59.2 4.9 %collective-permute-start.20 = (f32[1,16,512]{2,1,0:T(8,128)S(1)}, f32[1,16,512]{2,1,0:T(8,128)S(1)}, u32[]{:S(2)}, u32[]{:S(2)}) collective-permute-start(f32[1,16,512]{2,1,0:T(8,128)S(1)} %add_bitcast_fusion.refs_0_), channel_id=1, source_target_pairs={{8,0},{9,1},{10,2},{11,3},{12,4},{13,5},{14,6},{15,7},{0,8},{1,9},... | collective-permute-start | bytes 98312 | tf_op jit(solution)/shard_map/ppermute | solution.py:655
  59.4 5.7 %collective-permute-start.21 = (f32[1,16,512]{2,1,0:T(8,128)S(1)}, f32[1,16,512]{2,1,0:T(8,128)S(1)}, u32[]{:S(2)}, u32[]{:S(2)}) collective-permute-start(f32[1,16,512]{2,1,0:T(8,128)S(1)} %add_bitcast_fusion.refs_0_), channel_id=1, source_target_pairs={{12,0},{13,1},{14,2},{15,3},{0,4},{1,5},{2,6},{3,7},{4,8},{5,9},{6... | collective-permute-start | bytes 98312 | tf_op jit(solution)/shard_map/ppermute | solution.py:655
  61.6 3.6 %copy-start.1 = (f32[16,32,64]{2,1,0:T(8,128)S(1)}, f32[16,32,64]{2,1,0:T(8,128)}, u32[]{:S(2)}) copy-start(f32[16,32,64]{2,1,0:T(8,128)} %constant.4.clone.refs_4_) | copy-start | bytes 393220

commit v16 on v15

--- a/solution.py
+++ b/solution.py
@@ -24,6 +24,7 @@
 F32 = jnp.float32
 MIB = 1024 * 1024
 LANES = 128
+OUT_ORDER = (0, 2, 3, 1)
 
 
 def chebyshev_constants(number_steps):
@@ -536,8 +537,8 @@
         place = team_place()
         copies = []
         for slot in range(slots):
-            for m in range(TEAM):
-                i = slot * TEAM + m
+            for n, m in enumerate(OUT_ORDER):
+                i = slot * TEAM + n
                 for j in range(planes):
                     for t in range(2):
                         for c in range(tiles):
@@ -573,7 +574,7 @@
         compiler_params=pltpu.CompilerParams(vmem_limit_bytes=4 * MIB),
         cost_estimate=pl.CostEstimate(flops=0, bytes_accessed=4 * MIB, transcendentals=0),
         name="gather_adjoint",
-    )(*[piece for group in pieces for piece in group])
+    )(*[group[m] for group in pieces for m in OUT_ORDER])
 
 
 def control(faces, radices, basis_z, basis_x, after):

time: 66.6 us -> 66.9 us (level)
  starting transfers between devices: 29.6 us -> 30.3 us
  transfers between devices with their start and end apart: 22 -> 22, of which waited for: 9 -> 8; matrix products, arithmetic and copies ran while one was open for 1% -> 1% of each run, Pallas kernels for 24% -> 24%
where the time goes in v16:
time: 66.9 us; the launch traced here: 66.6 us
  starting transfers between devices  30.3 us (45%)
  Pallas kernels  19.3 us (29%)
  waiting for transfers between devices  15.6 us (23%)
  between operations  0.86 us (1%)
    ppermute x13, starting transfers between devices, swap(): return lax.ppermute(value, 'gz', [(i, i ^ m) for i in range(slabs)])  10.5 us
    ppermute x4, starting transfers between devices, along(): return lax.ppermute(value, 'gz', pairs)  10.4 us
    pallas_call x2, Pallas kernels, solve(): pl.pallas_call(kernel, out_shape=[jax.ShapeDtypeStruct((2 * planes, half,...  10 us
    ppermute x5, starting transfers between devices, from_teams(): heard.append(lax.ppermute(value, 'gz', pairs))  9.38 us
    ppermute x13, waiting for transfers between devices, swap(): return lax.ppermute(value, 'gz', [(i, i ^ m) for i in range(slabs)])  9.12 us
    ppermute x5, waiting for transfers between devices, from_teams(): heard.append(lax.ppermute(value, 'gz', pairs))  6.5 us
    pallas_call x2, Pallas kernels, prepare(): pl.pallas_call(kernel, out_shape=[jax.ShapeDtypeStruct(shape, F32) for sh...  3.97 us
    pallas_call x2, Pallas kernels, prepare_planes(): pl.pallas_call(kernel, out_shape=[jax.ShapeDtypeStruct((count, 2, half, c...  2.74 us
  transfers between devices with their start and end apart: 22, of which 8 were waited for; matrix products, arithmetic and copies ran while one was open for 1% of the time, Pallas kernels for 24%

profile of v16, /device:TPU:0, one launch (start us, length us, event | category | flops | bytes accessed | tf_op | source)
XLA Modules:
  0.0 66.6 jit_solution(4087892063945687837)
XLA Ops:
  0.6 2.3 %prepare.3 = (f32[33,8,512]{2,1,0:T(8,128)S(1)}, f32[33,8,512]{2,1,0:T(8,128)S(1)}, f32[8,512]{1,0:T(8,128)S(1)}) custom-call(f32[8,8]{1,0:T(8,128)} %refs_0_.3, f32[8]{0:T(128)} %refs_1_.3, f32[8,4,16,512]{3,2,1,0:T(8,128)} %refs_2_.3, f32[4,16,512]{2,1,0:T(8,128)} %refs_3_.3, s32[8,4,16,512]{3,2,1,0:T(8,128)} %refs_4_.4), custom_call_target="tpu_custom_call" | custom-call | bytes 4194304 | tf_op jit(solution)/shard_map/prepare/pallas_call | solution.py:158
  2.9 0.5 collective-permute-start.1
  3.5 1.7 %prepare.2 = (f32[32,8,512]{2,1,0:T(8,128)S(1)}, f32[32,8,512]{2,1,0:T(8,128)S(1)}) custom-call(f32[8,8]{1,0:T(8,128)} %refs_0_.3, f32[8]{0:T(128)} %refs_1_.3, f32[8,4,16,512]{3,2,1,0:T(8,128)} %refs_2_.3, f32[4,16,512]{2,1,0:T(8,128)} %refs_3_.3, s32[8,4,16,512]{3,2,1,0:T(8,128)} %refs_4_.4), custom_call_target="tpu_custom_call" | custom-call | bytes 4194304 | tf_op jit(solution)/shard_map/prepare/pallas_call | solution.py:158
  5.1 0.1 collective-permute-start
  5.3 0.0 collective-permute-done.1.theirs_ref
  5.3 0.1 merge.2
  5.3 3.0 %collective-permute-start.5 = (f32[32,8,512]{2,1,0:T(8,128)S(1)}, f32[32,8,512]{2,1,0:T(8,128)S(1)}, u32[]{:S(2)}, u32[]{:S(2)}) collective-permute-start(f32[32,8,512]{2,1,0:T(8,128)S(1)} %get-tuple-element.54), channel_id=1, source_target_pairs={{0,2},{1,3},{2,0},{3,1},{4,6},{5,7},{6,4},{7,5},{8,10},{9,11},{10,... | collective-permute-start | bytes 1572872 | tf_op jit(solution)/shard_map/ppermute | solution.py:638
  8.3 1.6 %collective-permute-start.2 = (f32[8,512]{1,0:T(8,128)S(1)}, f32[8,512]{1,0:T(8,128)S(1)}, u32[]{:S(2)}, u32[]{:S(2)}) collective-permute-start(f32[8,512]{1,0:T(8,128)S(1)} %get-tuple-element.51), channel_id=1, source_target_pairs={{4,0},{5,1},{6,2},{7,3},{0,4},{1,5},{2,6},{3,7},{12,8},{13,9},{14,... | collective-permute-start | bytes 49160 | tf_op jit(solution)/shard_map/ppermute | solution.py:656
  9.9 2.2 %collective-permute-done.2 = f32[8,512]{1,0:T(8,128)S(1)} collective-permute-done((f32[8,512]{1,0:T(8,128)S(1)}, f32[8,512]{1,0:T(8,128)S(1)}, u32[]{:S(2)}, u32[]{:S(2)}) %collective-permute-start.2) | collective-permute-done | bytes 16416 | tf_op jit(solution)/shard_map/ppermute | solution.py:656
  12.1 2.6 %collective-permute-start.3 = (f32[8,512]{1,0:T(8,128)S(1)}, f32[8,512]{1,0:T(8,128)S(1)}, u32[]{:S(2)}, u32[]{:S(2)}) collective-permute-start(f32[8,512]{1,0:T(8,128)S(1)} %add.15), channel_id=1, source_target_pairs={{8,0},{9,1},{10,2},{11,3},{12,4},{13,5},{14,6},{15,7},{0,8},{1,9},... | collective-permute-start | bytes 49160 | tf_op jit(solution)/shard_map/ppermute | solution.py:656
  14.7 2.0 %collective-permute-done.3 = f32[8,512]{1,0:T(8,128)S(1)} collective-permute-done((f32[8,512]{1,0:T(8,128)S(1)}, f32[8,512]{1,0:T(8,128)S(1)}, u32[]{:S(2)}, u32[]{:S(2)}) %collective-permute-start.3) | collective-permute-done | bytes 16416 | tf_op jit(solution)/shard_map/ppermute | solution.py:656
  16.7 0.1 merge.3
  16.8 0.3 collective-permute-start.11
  17.0 0.0 collective-permute-done.theirs_ref
  17.0 0.1 merge_near.2
  17.1 1.3 %collective-permute-start.4 = (f32[30,8,512]{2,1,0:T(8,128)S(1)}, f32[30,8,512]{2,1,0:T(8,128)S(1)}, u32[]{:S(2)}, u32[]{:S(2)}) collective-permute-start(f32[30,8,512]{2,1,0:T(8,128)S(1)} %get-tuple-element.53), channel_id=1, source_target_pairs={{2,6},{3,7},{4,0},{5,1},{6,10},{7,11},{8,4},{9,5},{10,14},{11,15},... | collective-permute-start | bytes 1474568 | tf_op jit(solution)/shard_map/ppermute | solution.py:647
  18.4 2.6 %collective-permute-done.5.far_ref.ref = f32[32,8,512]{2,1,0:T(8,128)S(1)} collective-permute-done((f32[32,8,512]{2,1,0:T(8,128)S(1)}, f32[32,8,512]{2,1,0:T(8,128)S(1)}, u32[]{:S(2)}, u32[]{:S(2)}) %collective-permute-start.5) | collective-permute-done | bytes 524320 | tf_op jit(solution)/shard_map/ppermute | solution.py:638
  21.1 4.1 %collective-permute-start.6 = (f32[30,8,512]{2,1,0:T(8,128)S(1)}, f32[30,8,512]{2,1,0:T(8,128)S(1)}, u32[]{:S(2)}, u32[]{:S(2)}) collective-permute-start(f32[30,8,512]{2,1,0:T(8,128)S(1)} %trim.2), channel_id=1, source_target_pairs={{0,4},{1,5},{4,8},{5,9},{6,2},{7,3},{8,12},{9,13},{10,6},{11,7},{1... | collective-permute-start | bytes 1474568 | tf_op jit(solution)/shard_map/ppermute | solution.py:647
  25.2 0.1 merge_near.3
  25.3 1.3 %collective-permute-start.10 = (f32[30,8,512]{2,1,0:T(8,128)S(1)}, f32[30,8,512]{2,1,0:T(8,128)S(1)}, u32[]{:S(2)}, u32[]{:S(2)}) collective-permute-start(f32[30,8,512]{2,1,0:T(8,128)S(1)} %get-tuple-element.69), channel_id=1, source_target_pairs={{2,6},{3,7},{4,0},{5,1},{6,10},{7,11},{8,4},{9,5},{10,14},{11,15},... | collective-permute-start | bytes 1474568 | tf_op jit(solution)/shard_map/ppermute | solution.py:647
  26.6 5.4 %collective-permute-done.11.far_ref.ref = f32[33,8,512]{2,1,0:T(8,128)S(1)} collective-permute-done((f32[33,8,512]{2,1,0:T(8,128)S(1)}, f32[33,8,512]{2,1,0:T(8,128)S(1)}, u32[]{:S(2)}, u32[]{:S(2)}) %collective-permute-start.11) | collective-permute-done | bytes 540704 | tf_op jit(solution)/shard_map/ppermute | solution.py:638
  32.1 3.8 %collective-permute-start.12 = (f32[30,8,512]{2,1,0:T(8,128)S(1)}, f32[30,8,512]{2,1,0:T(8,128)S(1)}, u32[]{:S(2)}, u32[]{:S(2)}) collective-permute-start(f32[30,8,512]{2,1,0:T(8,128)S(1)} %trim.3), channel_id=1, source_target_pairs={{0,4},{1,5},{4,8},{5,9},{6,2},{7,3},{8,12},{9,13},{10,6},{11,7},{1... | collective-permute-start | bytes 1474568 | tf_op jit(solution)/shard_map/ppermute | solution.py:647
  35.9 1.4 %prepare_planes.2 = (f32[22,2,8,512]{3,2,1,0:T(8,128)S(1)}, f32[22,2,8,512]{3,2,1,0:T(8,128)S(1)}, f32[22,2,8,512]{3,2,1,0:T(8,128)S(1)}, f32[22,2,8,512]{3,2,1,...) custom-call(f32[32,8,512]{2,1,0:T(8,128)S(1)} %get-tuple-element.52., ...), custom_call_target="tpu_custom_call" | custom-call | bytes 8388608 | tf_op jit(solution)/shard_map/prepare_planes/pallas_call | solution.py:377
  37.2 0.0 collective-permute-done.6.refs_9_
  37.2 5.2 %solve.2 = (f32[8,8,512]{2,1,0:T(8,128)S(1)}, f32[8,8,512]{2,1,0:T(8,128)S(1)}, f32[8,8,512]{2,1,0:T(8,128)S(1)}, f32[8,8,512]{2,1,0:T(8,128)S(1)}, f32[16,512]{1,0:T(8,128)S(1)}) custom-call(f32[22,2,8,512]{3,2,1,0:T(8,128)S(1)} %get-tuple-element.55.refs_0_, f32[22,2,8,512]{3,2,1,0:T(8,128)S(1)} %get-tuple-element.56.refs_1_, ...), custom_call_target="tpu_custom_call" | custom-call | bytes 16777216 | tf_op jit(solution)/shard_map/solve/pallas_call | solution.py:476
  42.4 0.1 collective-permute-start.7
  42.5 0.2 collective-permute-start.8
  42.7 1.9 %collective-permute-start.9 = (f32[8,8,512]{2,1,0:T(8,128)S(1)}, f32[8,8,512]{2,1,0:T(8,128)S(1)}, u32[]{:S(2)}, u32[]{:S(2)}) collective-permute-start(f32[8,8,512]{2,1,0:T(8,128)S(1)} %get-tuple-element.67), channel_id=1, source_target_pairs={{0,1},{1,0},{2,3},{3,2},{4,5},{5,4},{6,7},{7,6},{8,9},{9,8},{10,11... | collective-permute-start | bytes 393224 | tf_op jit(solution)/shard_map/ppermute | solution.py:638
  44.6 0.0 collective-permute-done.10.halo_ref
  44.6 1.4 %prepare_planes.3 = (f32[22,2,8,512]{3,2,1,0:T(8,128)S(1)}, f32[22,2,8,512]{3,2,1,0:T(8,128)S(1)}, f32[22,2,8,512]{3,2,1,0:T(8,128)S(1)}, f32[22,2,8,512]{3,2,1,...) custom-call(f32[32,8,512]{2,1,0:T(8,128)S(1)} %get-tuple-element.68., ...), custom_call_target="tpu_custom_call" | custom-call | bytes 8388608 | tf_op jit(solution)/shard_map/prepare_planes/pallas_call | solution.py:377
  46.0 4.8 %solve.3 = (f32[8,8,512]{2,1,0:T(8,128)S(1)}, f32[8,8,512]{2,1,0:T(8,128)S(1)}, f32[8,8,512]{2,1,0:T(8,128)S(1)}, f32[8,8,512]{2,1,0:T(8,128)S(1)}, f32[16,512]{1,0:T(8,128)S(1)}) custom-call(f32[22,2,8,512]{3,2,1,0:T(8,128)S(1)} %get-tuple-element.71.refs_0_, f32[22,2,8,512]{3,2,1,0:T(8,128)S(1)} %get-tuple-element.72.refs_1_, ...), custom_call_target="tpu_custom_call" | custom-call | bytes 16777216 | tf_op jit(solution)/shard_map/solve/pallas_call | solution.py:476
  50.9 0.0 copy-start
  50.9 0.0 collective-permute-done.7.refs_1_.refs_5_
  50.9 0.0 collective-permute-done.9.refs_3_.refs_4_
  50.9 2.1 %collective-permute-start.16 = (f32[16,512]{1,0:T(8,128)S(1)}, f32[16,512]{1,0:T(8,128)S(1)}, u32[]{:S(2)}, u32[]{:S(2)}) collective-permute-start(f32[16,512]{1,0:T(8,128)S(1)} %get-tuple-element.86), channel_id=1, source_target_pairs={{0,2},{1,3},{2,0},{3,1},{4,6},{5,7},{6,4},{7,5},{8,10},{9,11},{10,... | collective-permute-start | bytes 98312 | tf_op jit(solution)/shard_map/ppermute | solution.py:638
  53.0 0.0 collective-permute-start.17
  53.0 0.2 collective-permute-start.18
  53.2 1.9 %collective-permute-start.13 = (f32[8,8,512]{2,1,0:T(8,128)S(1)}, f32[8,8,512]{2,1,0:T(8,128)S(1)}, u32[]{:S(2)}, u32[]{:S(2)}) collective-permute-start(f32[8,8,512]{2,1,0:T(8,128)S(1)} %get-tuple-element.81), channel_id=1, source_target_pairs={{0,2},{1,3},{2,0},{3,1},{4,6},{5,7},{6,4},{7,5},{8,10},{9,11},{10,... | collective-permute-start | bytes 393224 | tf_op jit(solution)/shard_map/ppermute | solution.py:638
  55.1 0.2 collective-permute-start.15
  55.3 1.0 %collective-permute-done.17 = f32[16,512]{1,0:T(8,128)S(1)} collective-permute-done((f32[16,512]{1,0:T(8,128)S(1)}, f32[16,512]{1,0:T(8,128)S(1)}, u32[]{:S(2)}, u32[]{:S(2)}) %collective-permute-start.17) | collective-permute-done | bytes 32800 | tf_op jit(solution)/shard_map/ppermute | solution.py:638
  56.3 3.1 %collective-permute-start.19 = (f32[1,16,512]{2,1,0:T(8,128)S(1)}, f32[1,16,512]{2,1,0:T(8,128)S(1)}, u32[]{:S(2)}, u32[]{:S(2)}) collective-permute-start(f32[1,16,512]{2,1,0:T(8,128)S(1)} %add_bitcast_fusion.refs_0_), channel_id=1, source_target_pairs={{4,0},{5,1},{6,2},{7,3},{8,4},{9,5},{10,6},{11,7},{12,8},{13,9},{1... | collective-permute-start | bytes 98312 | tf_op jit(solution)/shard_map/ppermute | solution.py:656
  59.5 0.1 collective-permute-done.13.refs_5_
  59.5 2.1 %collective-permute-start.21 = (f32[1,16,512]{2,1,0:T(8,128)S(1)}, f32[1,16,512]{2,1,0:T(8,128)S(1)}, u32[]{:S(2)}, u32[]{:S(2)}) collective-permute-start(f32[1,16,512]{2,1,0:T(8,128)S(1)} %add_bitcast_fusion.refs_0_), channel_id=1, source_target_pairs={{12,0},{13,1},{14,2},{15,3},{0,4},{1,5},{2,6},{3,7},{4,8},{5,9},{6... | collective-permute-start | bytes 98312 | tf_op jit(solution)/shard_map/ppermute | solution.py:656
  61.6 0.5 slice_bitcast_fusion.1
  62.1 1.1 %gather_adjoint.1 = (f32[8,4,16,512]{3,2,1,0:T(8,128)}, f32[8,128]{1,0:T(8,128)S(1)}) custom-call(f32[8,8,512]{2,1,0:T(8,128)S(1)} %get-tuple-element.64.refs_0_, f32[8,8,512]{2,1,0:T(8,128)S(1)} %collective-permute-done.7.refs_1_.refs_5_, f32[8,8,512]{2,1,0:T(8,128)S(1)} %collective-permute-done.8.refs_2_.refs_6_, ...), custom_call_target="tpu_custom_call" | custom-call | bytes 4194304 | tf_op jit(solution)/shard_map/gather_adjoint/pallas_call | solution.py:558
  63.2 1.2 %collective-permute-done.20.refs_2_ = f32[1,16,512]{2,1,0:T(8,128)S(1)} collective-permute-done((f32[1,16,512]{2,1,0:T(8,128)S(1)}, f32[1,16,512]{2,1,0:T(8,128)S(1)}, u32[]{:S(2)}, u32[]{:S(2)}) %collective-permute-start.20) | collective-permute-done | bytes 32800 | tf_op jit(solution)/shard_map/ppermute | solution.py:656
  64.4 1.1 %collective-permute-done.21.refs_3_ = f32[1,16,512]{2,1,0:T(8,128)S(1)} collective-permute-done((f32[1,16,512]{2,1,0:T(8,128)S(1)}, f32[1,16,512]{2,1,0:T(8,128)S(1)}, u32[]{:S(2)}, u32[]{:S(2)}) %collective-permute-start.21) | collective-permute-done | bytes 32800 | tf_op jit(solution)/shard_map/ppermute | solution.py:656
  65.5 1.1 %control.1 = f32[32,512]{1,0:T(8,128)} custom-call(f32[1,16,512]{2,1,0:T(8,128)S(1)} %add_bitcast_fusion.refs_0_, f32[1,16,512]{2,1,0:T(8,128)S(1)} %collective-permute-done.19.refs_1_, f32[1,16,512]{2,1,0:T(8,128)S(1)} %collective-permute-done.20.refs_2_, f32[1,16,512]{2,1,0:T(8,128)S(1)} %collective-permute-done.21.refs_3_, f32[16,32,64]{2,1,0:T(8,128)S(1)} %copy-done.1, ...), custom_call_target="tpu_custom_call" | custom-call | tf_op jit(solution)/shard_map/control/pallas_call | solution.py:610
  (20 shorter events, 0.2 us)
Async XLA Ops:
  2.9 2.3 %collective-permute-start.1 = (f32[33,8,512]{2,1,0:T(8,128)S(1)}, f32[33,8,512]{2,1,0:T(8,128)S(1)}, u32[]{:S(2)}, u32[]{:S(2)}) collective-permute-start(f32[33,8,512]{2,1,0:T(8,128)S(1)} %get-tuple-element.49), channel_id=1, source_target_pairs={{0,1},{1,0},{2,3},{3,2},{4,5},{5,4},{6,7},{7,6},{8,9},{9,8},{10,11... | collective-permute-start | bytes 1622024 | tf_op jit(solution)/shard_map/ppermute | solution.py:638
  5.1 11.9 %collective-permute-start = (f32[32,8,512]{2,1,0:T(8,128)S(1)}, f32[32,8,512]{2,1,0:T(8,128)S(1)}, u32[]{:S(2)}, u32[]{:S(2)}) collective-permute-start(f32[32,8,512]{2,1,0:T(8,128)S(1)} %get-tuple-element.47), channel_id=1, source_target_pairs={{0,1},{1,0},{2,3},{3,2},{4,5},{5,4},{6,7},{7,6},{8,9},{9,8},{10,11... | collective-permute-start | bytes 1572872 | tf_op jit(solution)/shard_map/ppermute | solution.py:638
  5.3 15.7 %collective-permute-start.5 = (f32[32,8,512]{2,1,0:T(8,128)S(1)}, f32[32,8,512]{2,1,0:T(8,128)S(1)}, u32[]{:S(2)}, u32[]{:S(2)}) collective-permute-start(f32[32,8,512]{2,1,0:T(8,128)S(1)} %get-tuple-element.54), channel_id=1, source_target_pairs={{0,2},{1,3},{2,0},{3,1},{4,6},{5,7},{6,4},{7,5},{8,10},{9,11},{10,... | collective-permute-start | bytes 1572872 | tf_op jit(solution)/shard_map/ppermute | solution.py:638
  8.3 3.7 %collective-permute-start.2 = (f32[8,512]{1,0:T(8,128)S(1)}, f32[8,512]{1,0:T(8,128)S(1)}, u32[]{:S(2)}, u32[]{:S(2)}) collective-permute-start(f32[8,512]{1,0:T(8,128)S(1)} %get-tuple-element.51), channel_id=1, source_target_pairs={{4,0},{5,1},{6,2},{7,3},{0,4},{1,5},{2,6},{3,7},{12,8},{13,9},{14,... | collective-permute-start | bytes 49160 | tf_op jit(solution)/shard_map/ppermute | solution.py:656
  12.1 4.6 %collective-permute-start.3 = (f32[8,512]{1,0:T(8,128)S(1)}, f32[8,512]{1,0:T(8,128)S(1)}, u32[]{:S(2)}, u32[]{:S(2)}) collective-permute-start(f32[8,512]{1,0:T(8,128)S(1)} %add.15), channel_id=1, source_target_pairs={{8,0},{9,1},{10,2},{11,3},{12,4},{13,5},{14,6},{15,7},{0,8},{1,9},... | collective-permute-start | bytes 49160 | tf_op jit(solution)/shard_map/ppermute | solution.py:656
  16.8 15.3 %collective-permute-start.11 = (f32[33,8,512]{2,1,0:T(8,128)S(1)}, f32[33,8,512]{2,1,0:T(8,128)S(1)}, u32[]{:S(2)}, u32[]{:S(2)}) collective-permute-start(f32[33,8,512]{2,1,0:T(8,128)S(1)} %merge.3), channel_id=1, source_target_pairs={{0,2},{1,3},{2,0},{3,1},{4,6},{5,7},{6,4},{7,5},{8,10},{9,11},{10,... | collective-permute-start | bytes 1622024 | tf_op jit(solution)/shard_map/ppermute | solution.py:638
  17.1 18.7 %collective-permute-start.4 = (f32[30,8,512]{2,1,0:T(8,128)S(1)}, f32[30,8,512]{2,1,0:T(8,128)S(1)}, u32[]{:S(2)}, u32[]{:S(2)}) collective-permute-start(f32[30,8,512]{2,1,0:T(8,128)S(1)} %get-tuple-element.53), channel_id=1, source_target_pairs={{2,6},{3,7},{4,0},{5,1},{6,10},{7,11},{8,4},{9,5},{10,14},{11,15},... | collective-permute-start | bytes 1474568 | tf_op jit(solution)/shard_map/ppermute | solution.py:647
  21.1 16.1 %collective-permute-start.6 = (f32[30,8,512]{2,1,0:T(8,128)S(1)}, f32[30,8,512]{2,1,0:T(8,128)S(1)}, u32[]{:S(2)}, u32[]{:S(2)}) collective-permute-start(f32[30,8,512]{2,1,0:T(8,128)S(1)} %trim.2), channel_id=1, source_target_pairs={{0,4},{1,5},{4,8},{5,9},{6,2},{7,3},{8,12},{9,13},{10,6},{11,7},{1... | collective-permute-start | bytes 1474568 | tf_op jit(solution)/shard_map/ppermute | solution.py:647
  25.3 19.3 %collective-permute-start.10 = (f32[30,8,512]{2,1,0:T(8,128)S(1)}, f32[30,8,512]{2,1,0:T(8,128)S(1)}, u32[]{:S(2)}, u32[]{:S(2)}) collective-permute-start(f32[30,8,512]{2,1,0:T(8,128)S(1)} %get-tuple-element.69), channel_id=1, source_target_pairs={{2,6},{3,7},{4,0},{5,1},{6,10},{7,11},{8,4},{9,5},{10,14},{11,15},... | collective-permute-start | bytes 1474568 | tf_op jit(solution)/shard_map/ppermute | solution.py:647
  32.1 13.9 %collective-permute-start.12 = (f32[30,8,512]{2,1,0:T(8,128)S(1)}, f32[30,8,512]{2,1,0:T(8,128)S(1)}, u32[]{:S(2)}, u32[]{:S(2)}) collective-permute-start(f32[30,8,512]{2,1,0:T(8,128)S(1)} %trim.3), channel_id=1, source_target_pairs={{0,4},{1,5},{4,8},{5,9},{6,2},{7,3},{8,12},{9,13},{10,6},{11,7},{1... | collective-permute-start | bytes 1474568 | tf_op jit(solution)/shard_map/ppermute | solution.py:647
  42.4 8.5 %collective-permute-start.7 = (f32[8,8,512]{2,1,0:T(8,128)S(1)}, f32[8,8,512]{2,1,0:T(8,128)S(1)}, u32[]{:S(2)}, u32[]{:S(2)}) collective-permute-start(f32[8,8,512]{2,1,0:T(8,128)S(1)} %get-tuple-element.65), channel_id=1, source_target_pairs={{0,2},{1,3},{2,0},{3,1},{4,6},{5,7},{6,4},{7,5},{8,10},{9,11},{10,... | collective-permute-start | bytes 393224 | tf_op jit(solution)/shard_map/ppermute | solution.py:638
  42.5 8.4 %collective-permute-start.8 = (f32[8,8,512]{2,1,0:T(8,128)S(1)}, f32[8,8,512]{2,1,0:T(8,128)S(1)}, u32[]{:S(2)}, u32[]{:S(2)}) collective-permute-start(f32[8,8,512]{2,1,0:T(8,128)S(1)} %get-tuple-element.66), channel_id=1, source_target_pairs={{0,3},{1,2},{2,1},{3,0},{4,7},{5,6},{6,5},{7,4},{8,11},{9,10},{10,... | collective-permute-start | bytes 393224 | tf_op jit(solution)/shard_map/ppermute | solution.py:638
  42.7 8.2 %collective-permute-start.9 = (f32[8,8,512]{2,1,0:T(8,128)S(1)}, f32[8,8,512]{2,1,0:T(8,128)S(1)}, u32[]{:S(2)}, u32[]{:S(2)}) collective-permute-start(f32[8,8,512]{2,1,0:T(8,128)S(1)} %get-tuple-element.67), channel_id=1, source_target_pairs={{0,1},{1,0},{2,3},{3,2},{4,5},{5,4},{6,7},{7,6},{8,9},{9,8},{10,11... | collective-permute-start | bytes 393224 | tf_op jit(solution)/shard_map/ppermute | solution.py:638
  50.9 14.6 %copy-start = (f32[512,512]{1,0:T(8,128)S(1)}, f32[512,512]{1,0:T(8,128)}, u32[]{:S(2)}) copy-start(f32[512,512]{1,0:T(8,128)} %constant.5.clone.refs_5_) | copy-start | bytes 3145732
  50.9 4.2 %collective-permute-start.16 = (f32[16,512]{1,0:T(8,128)S(1)}, f32[16,512]{1,0:T(8,128)S(1)}, u32[]{:S(2)}, u32[]{:S(2)}) collective-permute-start(f32[16,512]{1,0:T(8,128)S(1)} %get-tuple-element.86), channel_id=1, source_target_pairs={{0,2},{1,3},{2,0},{3,1},{4,6},{5,7},{6,4},{7,5},{8,10},{9,11},{10,... | collective-permute-start | bytes 98312 | tf_op jit(solution)/shard_map/ppermute | solution.py:638
  53.0 3.3 %collective-permute-start.17 = (f32[16,512]{1,0:T(8,128)S(1)}, f32[16,512]{1,0:T(8,128)S(1)}, u32[]{:S(2)}, u32[]{:S(2)}) collective-permute-start(f32[16,512]{1,0:T(8,128)S(1)} %get-tuple-element.86), channel_id=1, source_target_pairs={{0,3},{1,2},{2,1},{3,0},{4,7},{5,6},{6,5},{7,4},{8,11},{9,10},{10,... | collective-permute-start | bytes 98312 | tf_op jit(solution)/shard_map/ppermute | solution.py:638
  53.0 3.3 %collective-permute-start.18 = (f32[16,512]{1,0:T(8,128)S(1)}, f32[16,512]{1,0:T(8,128)S(1)}, u32[]{:S(2)}, u32[]{:S(2)}) collective-permute-start(f32[16,512]{1,0:T(8,128)S(1)} %get-tuple-element.86), channel_id=1, source_target_pairs={{0,1},{1,0},{2,3},{3,2},{4,5},{5,4},{6,7},{7,6},{8,9},{9,8},{10,11... | collective-permute-start | bytes 98312 | tf_op jit(solution)/shard_map/ppermute | solution.py:638
  53.2 6.3 %collective-permute-start.13 = (f32[8,8,512]{2,1,0:T(8,128)S(1)}, f32[8,8,512]{2,1,0:T(8,128)S(1)}, u32[]{:S(2)}, u32[]{:S(2)}) collective-permute-start(f32[8,8,512]{2,1,0:T(8,128)S(1)} %get-tuple-element.81), channel_id=1, source_target_pairs={{0,2},{1,3},{2,0},{3,1},{4,6},{5,7},{6,4},{7,5},{8,10},{9,11},{10,... | collective-permute-start | bytes 393224 | tf_op jit(solution)/shard_map/ppermute | solution.py:638
  55.1 7.0 %collective-permute-start.14 = (f32[8,8,512]{2,1,0:T(8,128)S(1)}, f32[8,8,512]{2,1,0:T(8,128)S(1)}, u32[]{:S(2)}, u32[]{:S(2)}) collective-permute-start(f32[8,8,512]{2,1,0:T(8,128)S(1)} %get-tuple-element.82), channel_id=1, source_target_pairs={{0,3},{1,2},{2,1},{3,0},{4,7},{5,6},{6,5},{7,4},{8,11},{9,10},{10,... | collective-permute-start | bytes 393224 | tf_op jit(solution)/shard_map/ppermute | solution.py:638
  55.1 7.0 %collective-permute-start.15 = (f32[8,8,512]{2,1,0:T(8,128)S(1)}, f32[8,8,512]{2,1,0:T(8,128)S(1)}, u32[]{:S(2)}, u32[]{:S(2)}) collective-permute-start(f32[8,8,512]{2,1,0:T(8,128)S(1)} %get-tuple-element.83), channel_id=1, source_target_pairs={{0,1},{1,0},{2,3},{3,2},{4,5},{5,4},{6,7},{7,6},{8,9},{9,8},{10,11... | collective-permute-start | bytes 393224 | tf_op jit(solution)/shard_map/ppermute | solution.py:638
  56.3 6.9 %collective-permute-start.19 = (f32[1,16,512]{2,1,0:T(8,128)S(1)}, f32[1,16,512]{2,1,0:T(8,128)S(1)}, u32[]{:S(2)}, u32[]{:S(2)}) collective-permute-start(f32[1,16,512]{2,1,0:T(8,128)S(1)} %add_bitcast_fusion.refs_0_), channel_id=1, source_target_pairs={{4,0},{5,1},{6,2},{7,3},{8,4},{9,5},{10,6},{11,7},{12,8},{13,9},{1... | collective-permute-start | bytes 98312 | tf_op jit(solution)/shard_map/ppermute | solution.py:656
  59.5 5.0 %collective-permute-start.20 = (f32[1,16,512]{2,1,0:T(8,128)S(1)}, f32[1,16,512]{2,1,0:T(8,128)S(1)}, u32[]{:S(2)}, u32[]{:S(2)}) collective-permute-start(f32[1,16,512]{2,1,0:T(8,128)S(1)} %add_bitcast_fusion.refs_0_), channel_id=1, source_target_pairs={{8,0},{9,1},{10,2},{11,3},{12,4},{13,5},{14,6},{15,7},{0,8},{1,9},... | collective-permute-start | bytes 98312 | tf_op jit(solution)/shard_map/ppermute | solution.py:656
  59.5 6.0 %collective-permute-start.21 = (f32[1,16,512]{2,1,0:T(8,128)S(1)}, f32[1,16,512]{2,1,0:T(8,128)S(1)}, u32[]{:S(2)}, u32[]{:S(2)}) collective-permute-start(f32[1,16,512]{2,1,0:T(8,128)S(1)} %add_bitcast_fusion.refs_0_), channel_id=1, source_target_pairs={{12,0},{13,1},{14,2},{15,3},{0,4},{1,5},{2,6},{3,7},{4,8},{5,9},{6... | collective-permute-start | bytes 98312 | tf_op jit(solution)/shard_map/ppermute | solution.py:656
  62.1 3.4 %copy-start.1 = (f32[16,32,64]{2,1,0:T(8,128)S(1)}, f32[16,32,64]{2,1,0:T(8,128)}, u32[]{:S(2)}) copy-start(f32[16,32,64]{2,1,0:T(8,128)} %constant.4.clone.refs_4_) | copy-start | bytes 393220

commit v17 on v15

--- a/solution.py
+++ b/solution.py
@@ -691,7 +691,9 @@
         faces.append(solved[TEAM])
 
     face, moments = weigh(sums, faces, depth_total * rows_y * columns, pieces[0][1:])
-    heard = [sum((swap(face, m) for m in (2, 3, 1)), face)[None]]
+    for m in (1, 2):
+        face = face + swap(face, m)
+    heard = [face[None]]
     stride = 1
     for radix in radices:
         held = heard[0] if len(heard) == 1 else jnp.concatenate(heard)

time: 66.6 us -> 67.7 us (1.017)
  waiting for transfers between devices: 16 us -> 16.8 us
    ppermute x13 -> x12, waiting for transfers between devices: 9.31 us -> 9.92 us  [swap(): return lax.ppermute(value, 'gz', [(i, i ^ m) for i in range(slabs)])]
    ppermute x13 -> x12, starting transfers between devices: 10.3 us -> 10.2 us  [swap(): return lax.ppermute(value, 'gz', [(i, i ^ m) for i in range(slabs)])]
  transfers between devices with their start and end apart: 22 -> 21, of which waited for: 9 -> 9; matrix products, arithmetic and copies ran while one was open for 1% -> 1% of each run, Pallas kernels for 24% -> 23%
where the time goes in v17:
time: 67.7 us; the launch traced here: 67.4 us
  starting transfers between devices  29.9 us (44%)
  Pallas kernels  19.3 us (29%)
  waiting for transfers between devices  16.8 us (25%)
  between operations  0.85 us (1%)
    ppermute x4, starting transfers between devices, along(): return lax.ppermute(value, 'gz', pairs)  10.4 us
    ppermute x12, starting transfers between devices, swap(): return lax.ppermute(value, 'gz', [(i, i ^ m) for i in range(slabs)])  10.2 us
    pallas_call x2, Pallas kernels, solve(): pl.pallas_call(kernel, out_shape=[jax.ShapeDtypeStruct((2 * planes, half,...  10 us
    ppermute x12, waiting for transfers between devices, swap(): return lax.ppermute(value, 'gz', [(i, i ^ m) for i in range(slabs)])  9.92 us
    ppermute x5, starting transfers between devices, from_teams(): heard.append(lax.ppermute(value, 'gz', pairs))  9.32 us
    ppermute x5, waiting for transfers between devices, from_teams(): heard.append(lax.ppermute(value, 'gz', pairs))  6.92 us
    pallas_call x2, Pallas kernels, prepare(): pl.pallas_call(kernel, out_shape=[jax.ShapeDtypeStruct(shape, F32) for sh...  3.97 us
    pallas_call x2, Pallas kernels, prepare_planes(): pl.pallas_call(kernel, out_shape=[jax.ShapeDtypeStruct((count, 2, half, c...  2.74 us
  transfers between devices with their start and end apart: 21, of which 9 were waited for; matrix products, arithmetic and copies ran while one was open for 1% of the time, Pallas kernels for 23%

profile of v17, /device:TPU:0, one launch (start us, length us, event | category | flops | bytes accessed | tf_op | source)
XLA Modules:
  0.0 67.4 jit_solution(11484937292598429983)
XLA Ops:
  0.6 2.3 %prepare.3 = (f32[33,8,512]{2,1,0:T(8,128)S(1)}, f32[33,8,512]{2,1,0:T(8,128)S(1)}, f32[8,512]{1,0:T(8,128)S(1)}) custom-call(f32[8,8]{1,0:T(8,128)} %refs_0_.3, f32[8]{0:T(128)} %refs_1_.3, f32[8,4,16,512]{3,2,1,0:T(8,128)} %refs_2_.3, f32[4,16,512]{2,1,0:T(8,128)} %refs_3_.3, s32[8,4,16,512]{3,2,1,0:T(8,128)} %refs_4_.4), custom_call_target="tpu_custom_call" | custom-call | bytes 4194304 | tf_op jit(solution)/shard_map/prepare/pallas_call | solution.py:157
  2.9 0.5 collective-permute-start.1
  3.5 1.7 %prepare.2 = (f32[32,8,512]{2,1,0:T(8,128)S(1)}, f32[32,8,512]{2,1,0:T(8,128)S(1)}) custom-call(f32[8,8]{1,0:T(8,128)} %refs_0_.3, f32[8]{0:T(128)} %refs_1_.3, f32[8,4,16,512]{3,2,1,0:T(8,128)} %refs_2_.3, f32[4,16,512]{2,1,0:T(8,128)} %refs_3_.3, s32[8,4,16,512]{3,2,1,0:T(8,128)} %refs_4_.4), custom_call_target="tpu_custom_call" | custom-call | bytes 4194304 | tf_op jit(solution)/shard_map/prepare/pallas_call | solution.py:157
  5.1 0.1 collective-permute-start
  5.3 0.0 collective-permute-done.1.theirs_ref
  5.3 0.1 merge.2
  5.3 3.0 %collective-permute-start.5 = (f32[32,8,512]{2,1,0:T(8,128)S(1)}, f32[32,8,512]{2,1,0:T(8,128)S(1)}, u32[]{:S(2)}, u32[]{:S(2)}) collective-permute-start(f32[32,8,512]{2,1,0:T(8,128)S(1)} %get-tuple-element.54), channel_id=1, source_target_pairs={{0,2},{1,3},{2,0},{3,1},{4,6},{5,7},{6,4},{7,5},{8,10},{9,11},{10,... | collective-permute-start | bytes 1572872 | tf_op jit(solution)/shard_map/ppermute | solution.py:637
  8.3 1.6 %collective-permute-start.2 = (f32[8,512]{1,0:T(8,128)S(1)}, f32[8,512]{1,0:T(8,128)S(1)}, u32[]{:S(2)}, u32[]{:S(2)}) collective-permute-start(f32[8,512]{1,0:T(8,128)S(1)} %get-tuple-element.51), channel_id=1, source_target_pairs={{4,0},{5,1},{6,2},{7,3},{0,4},{1,5},{2,6},{3,7},{12,8},{13,9},{14,... | collective-permute-start | bytes 49160 | tf_op jit(solution)/shard_map/ppermute | solution.py:655
  9.9 2.2 %collective-permute-done.2 = f32[8,512]{1,0:T(8,128)S(1)} collective-permute-done((f32[8,512]{1,0:T(8,128)S(1)}, f32[8,512]{1,0:T(8,128)S(1)}, u32[]{:S(2)}, u32[]{:S(2)}) %collective-permute-start.2) | collective-permute-done | bytes 16416 | tf_op jit(solution)/shard_map/ppermute | solution.py:655
  12.1 2.6 %collective-permute-start.3 = (f32[8,512]{1,0:T(8,128)S(1)}, f32[8,512]{1,0:T(8,128)S(1)}, u32[]{:S(2)}, u32[]{:S(2)}) collective-permute-start(f32[8,512]{1,0:T(8,128)S(1)} %add.12), channel_id=1, source_target_pairs={{8,0},{9,1},{10,2},{11,3},{12,4},{13,5},{14,6},{15,7},{0,8},{1,9},... | collective-permute-start | bytes 49160 | tf_op jit(solution)/shard_map/ppermute | solution.py:655
  14.7 2.0 %collective-permute-done.3 = f32[8,512]{1,0:T(8,128)S(1)} collective-permute-done((f32[8,512]{1,0:T(8,128)S(1)}, f32[8,512]{1,0:T(8,128)S(1)}, u32[]{:S(2)}, u32[]{:S(2)}) %collective-permute-start.3) | collective-permute-done | bytes 16416 | tf_op jit(solution)/shard_map/ppermute | solution.py:655
  16.7 0.1 merge.3
  16.8 0.3 collective-permute-start.11
  17.0 0.0 collective-permute-done.theirs_ref
  17.0 0.1 merge_near.2
  17.1 1.3 %collective-permute-start.4 = (f32[30,8,512]{2,1,0:T(8,128)S(1)}, f32[30,8,512]{2,1,0:T(8,128)S(1)}, u32[]{:S(2)}, u32[]{:S(2)}) collective-permute-start(f32[30,8,512]{2,1,0:T(8,128)S(1)} %get-tuple-element.53), channel_id=1, source_target_pairs={{2,6},{3,7},{4,0},{5,1},{6,10},{7,11},{8,4},{9,5},{10,14},{11,15},... | collective-permute-start | bytes 1474568 | tf_op jit(solution)/shard_map/ppermute | solution.py:646
  18.4 2.6 %collective-permute-done.5.far_ref.ref = f32[32,8,512]{2,1,0:T(8,128)S(1)} collective-permute-done((f32[32,8,512]{2,1,0:T(8,128)S(1)}, f32[32,8,512]{2,1,0:T(8,128)S(1)}, u32[]{:S(2)}, u32[]{:S(2)}) %collective-permute-start.5) | collective-permute-done | bytes 524320 | tf_op jit(solution)/shard_map/ppermute | solution.py:637
  21.1 4.1 %collective-permute-start.6 = (f32[30,8,512]{2,1,0:T(8,128)S(1)}, f32[30,8,512]{2,1,0:T(8,128)S(1)}, u32[]{:S(2)}, u32[]{:S(2)}) collective-permute-start(f32[30,8,512]{2,1,0:T(8,128)S(1)} %trim.2), channel_id=1, source_target_pairs={{0,4},{1,5},{4,8},{5,9},{6,2},{7,3},{8,12},{9,13},{10,6},{11,7},{1... | collective-permute-start | bytes 1474568 | tf_op jit(solution)/shard_map/ppermute | solution.py:646
  25.2 0.1 merge_near.3
  25.3 1.3 %collective-permute-start.10 = (f32[30,8,512]{2,1,0:T(8,128)S(1)}, f32[30,8,512]{2,1,0:T(8,128)S(1)}, u32[]{:S(2)}, u32[]{:S(2)}) collective-permute-start(f32[30,8,512]{2,1,0:T(8,128)S(1)} %get-tuple-element.69), channel_id=1, source_target_pairs={{2,6},{3,7},{4,0},{5,1},{6,10},{7,11},{8,4},{9,5},{10,14},{11,15},... | collective-permute-start | bytes 1474568 | tf_op jit(solution)/shard_map/ppermute | solution.py:646
  26.6 5.4 %collective-permute-done.11.far_ref.ref = f32[33,8,512]{2,1,0:T(8,128)S(1)} collective-permute-done((f32[33,8,512]{2,1,0:T(8,128)S(1)}, f32[33,8,512]{2,1,0:T(8,128)S(1)}, u32[]{:S(2)}, u32[]{:S(2)}) %collective-permute-start.11) | collective-permute-done | bytes 540704 | tf_op jit(solution)/shard_map/ppermute | solution.py:637
  32.1 3.8 %collective-permute-start.12 = (f32[30,8,512]{2,1,0:T(8,128)S(1)}, f32[30,8,512]{2,1,0:T(8,128)S(1)}, u32[]{:S(2)}, u32[]{:S(2)}) collective-permute-start(f32[30,8,512]{2,1,0:T(8,128)S(1)} %trim.3), channel_id=1, source_target_pairs={{0,4},{1,5},{4,8},{5,9},{6,2},{7,3},{8,12},{9,13},{10,6},{11,7},{1... | collective-permute-start | bytes 1474568 | tf_op jit(solution)/shard_map/ppermute | solution.py:646
  35.8 0.0 collective-permute-done.4.halo_ref
  35.9 1.4 %prepare_planes.2 = (f32[22,2,8,512]{3,2,1,0:T(8,128)S(1)}, f32[22,2,8,512]{3,2,1,0:T(8,128)S(1)}, f32[22,2,8,512]{3,2,1,0:T(8,128)S(1)}, f32[22,2,8,512]{3,2,1,...) custom-call(f32[32,8,512]{2,1,0:T(8,128)S(1)} %get-tuple-element.52., ...), custom_call_target="tpu_custom_call" | custom-call | bytes 8388608 | tf_op jit(solution)/shard_map/prepare_planes/pallas_call | solution.py:376
  37.2 5.2 %solve.2 = (f32[8,8,512]{2,1,0:T(8,128)S(1)}, f32[8,8,512]{2,1,0:T(8,128)S(1)}, f32[8,8,512]{2,1,0:T(8,128)S(1)}, f32[8,8,512]{2,1,0:T(8,128)S(1)}, f32[16,512]{1,0:T(8,128)S(1)}) custom-call(f32[22,2,8,512]{3,2,1,0:T(8,128)S(1)} %get-tuple-element.55.refs_0_, f32[22,2,8,512]{3,2,1,0:T(8,128)S(1)} %get-tuple-element.56.refs_1_, ...), custom_call_target="tpu_custom_call" | custom-call | bytes 16777216 | tf_op jit(solution)/shard_map/solve/pallas_call | solution.py:475
  42.4 0.1 collective-permute-start.7
  42.5 0.1 collective-permute-start.8
  42.6 1.8 %collective-permute-start.9 = (f32[8,8,512]{2,1,0:T(8,128)S(1)}, f32[8,8,512]{2,1,0:T(8,128)S(1)}, u32[]{:S(2)}, u32[]{:S(2)}) collective-permute-start(f32[8,8,512]{2,1,0:T(8,128)S(1)} %get-tuple-element.67), channel_id=1, source_target_pairs={{0,3},{1,2},{2,1},{3,0},{4,7},{5,6},{6,5},{7,4},{8,11},{9,10},{10,... | collective-permute-start | bytes 393224 | tf_op jit(solution)/shard_map/ppermute | solution.py:637
  44.3 0.0 collective-permute-done.10.halo_ref
  44.4 1.4 %prepare_planes.3 = (f32[22,2,8,512]{3,2,1,0:T(8,128)S(1)}, f32[22,2,8,512]{3,2,1,0:T(8,128)S(1)}, f32[22,2,8,512]{3,2,1,0:T(8,128)S(1)}, f32[22,2,8,512]{3,2,1,...) custom-call(f32[32,8,512]{2,1,0:T(8,128)S(1)} %get-tuple-element.68., ...), custom_call_target="tpu_custom_call" | custom-call | bytes 8388608 | tf_op jit(solution)/shard_map/prepare_planes/pallas_call | solution.py:376
  45.8 4.8 %solve.3 = (f32[8,8,512]{2,1,0:T(8,128)S(1)}, f32[8,8,512]{2,1,0:T(8,128)S(1)}, f32[8,8,512]{2,1,0:T(8,128)S(1)}, f32[8,8,512]{2,1,0:T(8,128)S(1)}, f32[16,512]{1,0:T(8,128)S(1)}) custom-call(f32[22,2,8,512]{3,2,1,0:T(8,128)S(1)} %get-tuple-element.71.refs_0_, f32[22,2,8,512]{3,2,1,0:T(8,128)S(1)} %get-tuple-element.72.refs_1_, ...), custom_call_target="tpu_custom_call" | custom-call | bytes 16777216 | tf_op jit(solution)/shard_map/solve/pallas_call | solution.py:475
  50.6 0.0 copy-start
  50.6 0.0 collective-permute-done.7.refs_1_.refs_4_
  50.6 0.1 collective-permute-done.9.refs_3_.refs_6_
  50.8 0.3 collective-permute-start.16
  51.1 0.9 %collective-permute-done.16 = f32[16,512]{1,0:T(8,128)S(1)} collective-permute-done((f32[16,512]{1,0:T(8,128)S(1)}, f32[16,512]{1,0:T(8,128)S(1)}, u32[]{:S(2)}, u32[]{:S(2)}) %collective-permute-start.16) | collective-permute-done | bytes 32800 | tf_op jit(solution)/shard_map/ppermute | solution.py:637
  52.1 2.1 %collective-permute-start.17 = (f32[16,512]{1,0:T(8,128)S(1)}, f32[16,512]{1,0:T(8,128)S(1)}, u32[]{:S(2)}, u32[]{:S(2)}) collective-permute-start(f32[16,512]{1,0:T(8,128)S(1)} %add.14), channel_id=1, source_target_pairs={{0,2},{1,3},{2,0},{3,1},{4,6},{5,7},{6,4},{7,5},{8,10},{9,11},{10,... | collective-permute-start | bytes 98312 | tf_op jit(solution)/shard_map/ppermute | solution.py:637
  54.2 0.2 collective-permute-start.14
  54.4 1.6 %collective-permute-start.15 = (f32[8,8,512]{2,1,0:T(8,128)S(1)}, f32[8,8,512]{2,1,0:T(8,128)S(1)}, u32[]{:S(2)}, u32[]{:S(2)}) collective-permute-start(f32[8,8,512]{2,1,0:T(8,128)S(1)} %get-tuple-element.83), channel_id=1, source_target_pairs={{0,3},{1,2},{2,1},{3,0},{4,7},{5,6},{6,5},{7,4},{8,11},{9,10},{10,... | collective-permute-start | bytes 393224 | tf_op jit(solution)/shard_map/ppermute | solution.py:637
  56.1 0.0 collective-permute-done.17
  56.1 4.5 %collective-permute-start.18 = (f32[1,16,512]{2,1,0:T(8,128)S(1)}, f32[1,16,512]{2,1,0:T(8,128)S(1)}, u32[]{:S(2)}, u32[]{:S(2)}) collective-permute-start(f32[1,16,512]{2,1,0:T(8,128)S(1)} %add_bitcast_fusion.refs_0_), channel_id=1, source_target_pairs={{4,0},{5,1},{6,2},{7,3},{8,4},{9,5},{10,6},{11,7},{12,8},{13,9},{1... | collective-permute-start | bytes 98312 | tf_op jit(solution)/shard_map/ppermute | solution.py:655
  60.6 0.7 collective-permute-start.20
  61.3 0.5 slice_bitcast_fusion.1
  61.8 0.8 %collective-permute-done.15.refs_7_ = f32[8,8,512]{2,1,0:T(8,128)S(1)} collective-permute-done((f32[8,8,512]{2,1,0:T(8,128)S(1)}, f32[8,8,512]{2,1,0:T(8,128)S(1)}, u32[]{:S(2)}, u32[]{:S(2)}) %collective-permute-start.15) | collective-permute-done | bytes 131104 | tf_op jit(solution)/shard_map/ppermute | solution.py:637
  62.5 1.0 %gather_adjoint.1 = (f32[8,4,16,512]{3,2,1,0:T(8,128)}, f32[8,128]{1,0:T(8,128)S(1)}) custom-call(f32[8,8,512]{2,1,0:T(8,128)S(1)} %get-tuple-element.64.refs_0_, f32[8,8,512]{2,1,0:T(8,128)S(1)} %collective-permute-done.7.refs_1_.refs_4_, f32[8,8,512]{2,1,0:T(8,128)S(1)} %collective-permute-done.8.refs_2_.refs_5_, ...), custom_call_target="tpu_custom_call" | custom-call | bytes 4194304 | tf_op jit(solution)/shard_map/gather_adjoint/pallas_call | solution.py:557
  63.6 1.8 %collective-permute-done.19.refs_2_ = f32[1,16,512]{2,1,0:T(8,128)S(1)} collective-permute-done((f32[1,16,512]{2,1,0:T(8,128)S(1)}, f32[1,16,512]{2,1,0:T(8,128)S(1)}, u32[]{:S(2)}, u32[]{:S(2)}) %collective-permute-start.19) | collective-permute-done | bytes 32800 | tf_op jit(solution)/shard_map/ppermute | solution.py:655
  65.4 0.9 %collective-permute-done.20.refs_3_ = f32[1,16,512]{2,1,0:T(8,128)S(1)} collective-permute-done((f32[1,16,512]{2,1,0:T(8,128)S(1)}, f32[1,16,512]{2,1,0:T(8,128)S(1)}, u32[]{:S(2)}, u32[]{:S(2)}) %collective-permute-start.20) | collective-permute-done | bytes 32800 | tf_op jit(solution)/shard_map/ppermute | solution.py:655
  66.3 1.1 %control.1 = f32[32,512]{1,0:T(8,128)} custom-call(f32[1,16,512]{2,1,0:T(8,128)S(1)} %add_bitcast_fusion.refs_0_, f32[1,16,512]{2,1,0:T(8,128)S(1)} %collective-permute-done.18.refs_1_, f32[1,16,512]{2,1,0:T(8,128)S(1)} %collective-permute-done.19.refs_2_, f32[1,16,512]{2,1,0:T(8,128)S(1)} %collective-permute-done.20.refs_3_, f32[16,32,64]{2,1,0:T(8,128)S(1)} %copy-done.1, ...), custom_call_target="tpu_custom_call" | custom-call | tf_op jit(solution)/shard_map/control/pallas_call | solution.py:609
  (19 shorter events, 0.2 us)
Async XLA Ops:
  2.9 2.3 %collective-permute-start.1 = (f32[33,8,512]{2,1,0:T(8,128)S(1)}, f32[33,8,512]{2,1,0:T(8,128)S(1)}, u32[]{:S(2)}, u32[]{:S(2)}) collective-permute-start(f32[33,8,512]{2,1,0:T(8,128)S(1)} %get-tuple-element.49), channel_id=1, source_target_pairs={{0,1},{1,0},{2,3},{3,2},{4,5},{5,4},{6,7},{7,6},{8,9},{9,8},{10,11... | collective-permute-start | bytes 1622024 | tf_op jit(solution)/shard_map/ppermute | solution.py:637
  5.1 11.9 %collective-permute-start = (f32[32,8,512]{2,1,0:T(8,128)S(1)}, f32[32,8,512]{2,1,0:T(8,128)S(1)}, u32[]{:S(2)}, u32[]{:S(2)}) collective-permute-start(f32[32,8,512]{2,1,0:T(8,128)S(1)} %get-tuple-element.47), channel_id=1, source_target_pairs={{0,1},{1,0},{2,3},{3,2},{4,5},{5,4},{6,7},{7,6},{8,9},{9,8},{10,11... | collective-permute-start | bytes 1572872 | tf_op jit(solution)/shard_map/ppermute | solution.py:637
  5.3 15.7 %collective-permute-start.5 = (f32[32,8,512]{2,1,0:T(8,128)S(1)}, f32[32,8,512]{2,1,0:T(8,128)S(1)}, u32[]{:S(2)}, u32[]{:S(2)}) collective-permute-start(f32[32,8,512]{2,1,0:T(8,128)S(1)} %get-tuple-element.54), channel_id=1, source_target_pairs={{0,2},{1,3},{2,0},{3,1},{4,6},{5,7},{6,4},{7,5},{8,10},{9,11},{10,... | collective-permute-start | bytes 1572872 | tf_op jit(solution)/shard_map/ppermute | solution.py:637
  8.3 3.7 %collective-permute-start.2 = (f32[8,512]{1,0:T(8,128)S(1)}, f32[8,512]{1,0:T(8,128)S(1)}, u32[]{:S(2)}, u32[]{:S(2)}) collective-permute-start(f32[8,512]{1,0:T(8,128)S(1)} %get-tuple-element.51), channel_id=1, source_target_pairs={{4,0},{5,1},{6,2},{7,3},{0,4},{1,5},{2,6},{3,7},{12,8},{13,9},{14,... | collective-permute-start | bytes 49160 | tf_op jit(solution)/shard_map/ppermute | solution.py:655
  12.1 4.6 %collective-permute-start.3 = (f32[8,512]{1,0:T(8,128)S(1)}, f32[8,512]{1,0:T(8,128)S(1)}, u32[]{:S(2)}, u32[]{:S(2)}) collective-permute-start(f32[8,512]{1,0:T(8,128)S(1)} %add.12), channel_id=1, source_target_pairs={{8,0},{9,1},{10,2},{11,3},{12,4},{13,5},{14,6},{15,7},{0,8},{1,9},... | collective-permute-start | bytes 49160 | tf_op jit(solution)/shard_map/ppermute | solution.py:655
  16.8 15.3 %collective-permute-start.11 = (f32[33,8,512]{2,1,0:T(8,128)S(1)}, f32[33,8,512]{2,1,0:T(8,128)S(1)}, u32[]{:S(2)}, u32[]{:S(2)}) collective-permute-start(f32[33,8,512]{2,1,0:T(8,128)S(1)} %merge.3), channel_id=1, source_target_pairs={{0,2},{1,3},{2,0},{3,1},{4,6},{5,7},{6,4},{7,5},{8,10},{9,11},{10,... | collective-permute-start | bytes 1622024 | tf_op jit(solution)/shard_map/ppermute | solution.py:637
  17.1 18.7 %collective-permute-start.4 = (f32[30,8,512]{2,1,0:T(8,128)S(1)}, f32[30,8,512]{2,1,0:T(8,128)S(1)}, u32[]{:S(2)}, u32[]{:S(2)}) collective-permute-start(f32[30,8,512]{2,1,0:T(8,128)S(1)} %get-tuple-element.53), channel_id=1, source_target_pairs={{2,6},{3,7},{4,0},{5,1},{6,10},{7,11},{8,4},{9,5},{10,14},{11,15},... | collective-permute-start | bytes 1474568 | tf_op jit(solution)/shard_map/ppermute | solution.py:646
  21.1 16.1 %collective-permute-start.6 = (f32[30,8,512]{2,1,0:T(8,128)S(1)}, f32[30,8,512]{2,1,0:T(8,128)S(1)}, u32[]{:S(2)}, u32[]{:S(2)}) collective-permute-start(f32[30,8,512]{2,1,0:T(8,128)S(1)} %trim.2), channel_id=1, source_target_pairs={{0,4},{1,5},{4,8},{5,9},{6,2},{7,3},{8,12},{9,13},{10,6},{11,7},{1... | collective-permute-start | bytes 1474568 | tf_op jit(solution)/shard_map/ppermute | solution.py:646
  25.3 19.1 %collective-permute-start.10 = (f32[30,8,512]{2,1,0:T(8,128)S(1)}, f32[30,8,512]{2,1,0:T(8,128)S(1)}, u32[]{:S(2)}, u32[]{:S(2)}) collective-permute-start(f32[30,8,512]{2,1,0:T(8,128)S(1)} %get-tuple-element.69), channel_id=1, source_target_pairs={{2,6},{3,7},{4,0},{5,1},{6,10},{7,11},{8,4},{9,5},{10,14},{11,15},... | collective-permute-start | bytes 1474568 | tf_op jit(solution)/shard_map/ppermute | solution.py:646
  32.1 13.7 %collective-permute-start.12 = (f32[30,8,512]{2,1,0:T(8,128)S(1)}, f32[30,8,512]{2,1,0:T(8,128)S(1)}, u32[]{:S(2)}, u32[]{:S(2)}) collective-permute-start(f32[30,8,512]{2,1,0:T(8,128)S(1)} %trim.3), channel_id=1, source_target_pairs={{0,4},{1,5},{4,8},{5,9},{6,2},{7,3},{8,12},{9,13},{10,6},{11,7},{1... | collective-permute-start | bytes 1474568 | tf_op jit(solution)/shard_map/ppermute | solution.py:646
  42.4 8.2 %collective-permute-start.7 = (f32[8,8,512]{2,1,0:T(8,128)S(1)}, f32[8,8,512]{2,1,0:T(8,128)S(1)}, u32[]{:S(2)}, u32[]{:S(2)}) collective-permute-start(f32[8,8,512]{2,1,0:T(8,128)S(1)} %get-tuple-element.65), channel_id=1, source_target_pairs={{0,1},{1,0},{2,3},{3,2},{4,5},{5,4},{6,7},{7,6},{8,9},{9,8},{10,11... | collective-permute-start | bytes 393224 | tf_op jit(solution)/shard_map/ppermute | solution.py:637
  42.5 8.1 %collective-permute-start.8 = (f32[8,8,512]{2,1,0:T(8,128)S(1)}, f32[8,8,512]{2,1,0:T(8,128)S(1)}, u32[]{:S(2)}, u32[]{:S(2)}) collective-permute-start(f32[8,8,512]{2,1,0:T(8,128)S(1)} %get-tuple-element.66), channel_id=1, source_target_pairs={{0,2},{1,3},{2,0},{3,1},{4,6},{5,7},{6,4},{7,5},{8,10},{9,11},{10,... | collective-permute-start | bytes 393224 | tf_op jit(solution)/shard_map/ppermute | solution.py:637
  42.6 8.2 %collective-permute-start.9 = (f32[8,8,512]{2,1,0:T(8,128)S(1)}, f32[8,8,512]{2,1,0:T(8,128)S(1)}, u32[]{:S(2)}, u32[]{:S(2)}) collective-permute-start(f32[8,8,512]{2,1,0:T(8,128)S(1)} %get-tuple-element.67), channel_id=1, source_target_pairs={{0,3},{1,2},{2,1},{3,0},{4,7},{5,6},{6,5},{7,4},{8,11},{9,10},{10,... | collective-permute-start | bytes 393224 | tf_op jit(solution)/shard_map/ppermute | solution.py:637
  50.6 15.7 %copy-start = (f32[512,512]{1,0:T(8,128)S(1)}, f32[512,512]{1,0:T(8,128)}, u32[]{:S(2)}) copy-start(f32[512,512]{1,0:T(8,128)} %constant.5.clone.refs_5_) | copy-start | bytes 3145732
  50.8 1.3 %collective-permute-start.16 = (f32[16,512]{1,0:T(8,128)S(1)}, f32[16,512]{1,0:T(8,128)S(1)}, u32[]{:S(2)}, u32[]{:S(2)}) collective-permute-start(f32[16,512]{1,0:T(8,128)S(1)} %get-tuple-element.86), channel_id=1, source_target_pairs={{0,1},{1,0},{2,3},{3,2},{4,5},{5,4},{6,7},{7,6},{8,9},{9,8},{10,11... | collective-permute-start | bytes 98312 | tf_op jit(solution)/shard_map/ppermute | solution.py:637
  52.1 4.0 %collective-permute-start.17 = (f32[16,512]{1,0:T(8,128)S(1)}, f32[16,512]{1,0:T(8,128)S(1)}, u32[]{:S(2)}, u32[]{:S(2)}) collective-permute-start(f32[16,512]{1,0:T(8,128)S(1)} %add.14), channel_id=1, source_target_pairs={{0,2},{1,3},{2,0},{3,1},{4,6},{5,7},{6,4},{7,5},{8,10},{9,11},{10,... | collective-permute-start | bytes 98312 | tf_op jit(solution)/shard_map/ppermute | solution.py:637
  54.2 6.4 %collective-permute-start.13 = (f32[8,8,512]{2,1,0:T(8,128)S(1)}, f32[8,8,512]{2,1,0:T(8,128)S(1)}, u32[]{:S(2)}, u32[]{:S(2)}) collective-permute-start(f32[8,8,512]{2,1,0:T(8,128)S(1)} %get-tuple-element.81), channel_id=1, source_target_pairs={{0,1},{1,0},{2,3},{3,2},{4,5},{5,4},{6,7},{7,6},{8,9},{9,8},{10,11... | collective-permute-start | bytes 393224 | tf_op jit(solution)/shard_map/ppermute | solution.py:637
  54.2 7.6 %collective-permute-start.14 = (f32[8,8,512]{2,1,0:T(8,128)S(1)}, f32[8,8,512]{2,1,0:T(8,128)S(1)}, u32[]{:S(2)}, u32[]{:S(2)}) collective-permute-start(f32[8,8,512]{2,1,0:T(8,128)S(1)} %get-tuple-element.82), channel_id=1, source_target_pairs={{0,2},{1,3},{2,0},{3,1},{4,6},{5,7},{6,4},{7,5},{8,10},{9,11},{10,... | collective-permute-start | bytes 393224 | tf_op jit(solution)/shard_map/ppermute | solution.py:637
  54.4 8.1 %collective-permute-start.15 = (f32[8,8,512]{2,1,0:T(8,128)S(1)}, f32[8,8,512]{2,1,0:T(8,128)S(1)}, u32[]{:S(2)}, u32[]{:S(2)}) collective-permute-start(f32[8,8,512]{2,1,0:T(8,128)S(1)} %get-tuple-element.83), channel_id=1, source_target_pairs={{0,3},{1,2},{2,1},{3,0},{4,7},{5,6},{6,5},{7,4},{8,11},{9,10},{10,... | collective-permute-start | bytes 393224 | tf_op jit(solution)/shard_map/ppermute | solution.py:637
  56.1 7.5 %collective-permute-start.18 = (f32[1,16,512]{2,1,0:T(8,128)S(1)}, f32[1,16,512]{2,1,0:T(8,128)S(1)}, u32[]{:S(2)}, u32[]{:S(2)}) collective-permute-start(f32[1,16,512]{2,1,0:T(8,128)S(1)} %add_bitcast_fusion.refs_0_), channel_id=1, source_target_pairs={{4,0},{5,1},{6,2},{7,3},{8,4},{9,5},{10,6},{11,7},{12,8},{13,9},{1... | collective-permute-start | bytes 98312 | tf_op jit(solution)/shard_map/ppermute | solution.py:655
  60.6 4.8 %collective-permute-start.19 = (f32[1,16,512]{2,1,0:T(8,128)S(1)}, f32[1,16,512]{2,1,0:T(8,128)S(1)}, u32[]{:S(2)}, u32[]{:S(2)}) collective-permute-start(f32[1,16,512]{2,1,0:T(8,128)S(1)} %add_bitcast_fusion.refs_0_), channel_id=1, source_target_pairs={{8,0},{9,1},{10,2},{11,3},{12,4},{13,5},{14,6},{15,7},{0,8},{1,9},... | collective-permute-start | bytes 98312 | tf_op jit(solution)/shard_map/ppermute | solution.py:655
  60.6 5.7 %collective-permute-start.20 = (f32[1,16,512]{2,1,0:T(8,128)S(1)}, f32[1,16,512]{2,1,0:T(8,128)S(1)}, u32[]{:S(2)}, u32[]{:S(2)}) collective-permute-start(f32[1,16,512]{2,1,0:T(8,128)S(1)} %add_bitcast_fusion.refs_0_), channel_id=1, source_target_pairs={{12,0},{13,1},{14,2},{15,3},{0,4},{1,5},{2,6},{3,7},{4,8},{5,9},{6... | collective-permute-start | bytes 98312 | tf_op jit(solution)/shard_map/ppermute | solution.py:655
  62.5 3.8 %copy-start.1 = (f32[16,32,64]{2,1,0:T(8,128)S(1)}, f32[16,32,64]{2,1,0:T(8,128)}, u32[]{:S(2)}) copy-start(f32[16,32,64]{2,1,0:T(8,128)} %constant.4.clone.refs_4_) | copy-start | bytes 393220

commit v18 on v15

--- a/solution.py
+++ b/solution.py
@@ -271,7 +271,8 @@
             body(start + n * width + k)
         return carry
 
-    lax.fori_loop(0, whole, group, 0)
+    if whole > 0:
+        lax.fori_loop(0, whole, group, 0)
     for p in range(start + whole * width, stop):
         body(p)
 

time: 66.6 us -> 66.6 us (level)
  no operation moved by 1% of the time
where the time goes in v18:
time: 66.6 us; the launch traced here: 66.3 us
  starting transfers between devices  29.6 us (44%)
  Pallas kernels  19.3 us (29%)
  waiting for transfers between devices  16 us (24%)
  between operations  0.85 us (1%)
    ppermute x4, starting transfers between devices, along(): return lax.ppermute(value, 'gz', pairs)  10.4 us
    ppermute x13, starting transfers between devices, swap(): return lax.ppermute(value, 'gz', [(i, i ^ m) for i in range(slabs)])  10.3 us
    pallas_call x2, Pallas kernels, solve(): pl.pallas_call(kernel, out_shape=[jax.ShapeDtypeStruct((2 * planes, half,...  10 us
    ppermute x13, waiting for transfers between devices, swap(): return lax.ppermute(value, 'gz', [(i, i ^ m) for i in range(slabs)])  9.31 us
    ppermute x5, starting transfers between devices, from_teams(): heard.append(lax.ppermute(value, 'gz', pairs))  8.83 us
    ppermute x5, waiting for transfers between devices, from_teams(): heard.append(lax.ppermute(value, 'gz', pairs))  6.71 us
    pallas_call x2, Pallas kernels, prepare(): pl.pallas_call(kernel, out_shape=[jax.ShapeDtypeStruct(shape, F32) for sh...  3.97 us
    pallas_call x2, Pallas kernels, prepare_planes(): pl.pallas_call(kernel, out_shape=[jax.ShapeDtypeStruct((count, 2, half, c...  2.74 us
  transfers between devices with their start and end apart: 22, of which 9 were waited for; matrix products, arithmetic and copies ran while one was open for 1% of the time, Pallas kernels for 24%

profile of v18, /device:TPU:0, one launch (start us, length us, event | category | flops | bytes accessed | tf_op | source)
XLA Modules:
  0.0 66.3 jit_solution(2829254247134371893)
XLA Ops:
  0.6 2.3 %prepare.3 = (f32[33,8,512]{2,1,0:T(8,128)S(1)}, f32[33,8,512]{2,1,0:T(8,128)S(1)}, f32[8,512]{1,0:T(8,128)S(1)}) custom-call(f32[8,8]{1,0:T(8,128)} %refs_0_.3, f32[8]{0:T(128)} %refs_1_.3, f32[8,4,16,512]{3,2,1,0:T(8,128)} %refs_2_.3, f32[4,16,512]{2,1,0:T(8,128)} %refs_3_.3, s32[8,4,16,512]{3,2,1,0:T(8,128)} %refs_4_.4), custom_call_target="tpu_custom_call" | custom-call | bytes 4194304 | tf_op jit(solution)/shard_map/prepare/pallas_call | solution.py:157
  2.9 0.5 collective-permute-start.1
  3.5 1.7 %prepare.2 = (f32[32,8,512]{2,1,0:T(8,128)S(1)}, f32[32,8,512]{2,1,0:T(8,128)S(1)}) custom-call(f32[8,8]{1,0:T(8,128)} %refs_0_.3, f32[8]{0:T(128)} %refs_1_.3, f32[8,4,16,512]{3,2,1,0:T(8,128)} %refs_2_.3, f32[4,16,512]{2,1,0:T(8,128)} %refs_3_.3, s32[8,4,16,512]{3,2,1,0:T(8,128)} %refs_4_.4), custom_call_target="tpu_custom_call" | custom-call | bytes 4194304 | tf_op jit(solution)/shard_map/prepare/pallas_call | solution.py:157
  5.1 0.1 collective-permute-start
  5.3 0.0 collective-permute-done.1.theirs_ref
  5.3 0.1 merge.2
  5.3 3.0 %collective-permute-start.5 = (f32[32,8,512]{2,1,0:T(8,128)S(1)}, f32[32,8,512]{2,1,0:T(8,128)S(1)}, u32[]{:S(2)}, u32[]{:S(2)}) collective-permute-start(f32[32,8,512]{2,1,0:T(8,128)S(1)} %get-tuple-element.54), channel_id=1, source_target_pairs={{0,2},{1,3},{2,0},{3,1},{4,6},{5,7},{6,4},{7,5},{8,10},{9,11},{10,... | collective-permute-start | bytes 1572872 | tf_op jit(solution)/shard_map/ppermute | solution.py:638
  8.3 1.6 %collective-permute-start.2 = (f32[8,512]{1,0:T(8,128)S(1)}, f32[8,512]{1,0:T(8,128)S(1)}, u32[]{:S(2)}, u32[]{:S(2)}) collective-permute-start(f32[8,512]{1,0:T(8,128)S(1)} %get-tuple-element.51), channel_id=1, source_target_pairs={{4,0},{5,1},{6,2},{7,3},{0,4},{1,5},{2,6},{3,7},{12,8},{13,9},{14,... | collective-permute-start | bytes 49160 | tf_op jit(solution)/shard_map/ppermute | solution.py:656
  9.9 2.2 %collective-permute-done.2 = f32[8,512]{1,0:T(8,128)S(1)} collective-permute-done((f32[8,512]{1,0:T(8,128)S(1)}, f32[8,512]{1,0:T(8,128)S(1)}, u32[]{:S(2)}, u32[]{:S(2)}) %collective-permute-start.2) | collective-permute-done | bytes 16416 | tf_op jit(solution)/shard_map/ppermute | solution.py:656
  12.1 2.6 %collective-permute-start.3 = (f32[8,512]{1,0:T(8,128)S(1)}, f32[8,512]{1,0:T(8,128)S(1)}, u32[]{:S(2)}, u32[]{:S(2)}) collective-permute-start(f32[8,512]{1,0:T(8,128)S(1)} %add.15), channel_id=1, source_target_pairs={{8,0},{9,1},{10,2},{11,3},{12,4},{13,5},{14,6},{15,7},{0,8},{1,9},... | collective-permute-start | bytes 49160 | tf_op jit(solution)/shard_map/ppermute | solution.py:656
  14.7 2.0 %collective-permute-done.3 = f32[8,512]{1,0:T(8,128)S(1)} collective-permute-done((f32[8,512]{1,0:T(8,128)S(1)}, f32[8,512]{1,0:T(8,128)S(1)}, u32[]{:S(2)}, u32[]{:S(2)}) %collective-permute-start.3) | collective-permute-done | bytes 16416 | tf_op jit(solution)/shard_map/ppermute | solution.py:656
  16.7 0.1 merge.3
  16.8 0.3 collective-permute-start.11
  17.0 0.1 merge_near.2
  17.1 1.3 %collective-permute-start.4 = (f32[30,8,512]{2,1,0:T(8,128)S(1)}, f32[30,8,512]{2,1,0:T(8,128)S(1)}, u32[]{:S(2)}, u32[]{:S(2)}) collective-permute-start(f32[30,8,512]{2,1,0:T(8,128)S(1)} %get-tuple-element.53), channel_id=1, source_target_pairs={{2,6},{3,7},{4,0},{5,1},{6,10},{7,11},{8,4},{9,5},{10,14},{11,15},... | collective-permute-start | bytes 1474568 | tf_op jit(solution)/shard_map/ppermute | solution.py:647
  18.4 2.6 %collective-permute-done.5.far_ref.ref = f32[32,8,512]{2,1,0:T(8,128)S(1)} collective-permute-done((f32[32,8,512]{2,1,0:T(8,128)S(1)}, f32[32,8,512]{2,1,0:T(8,128)S(1)}, u32[]{:S(2)}, u32[]{:S(2)}) %collective-permute-start.5) | collective-permute-done | bytes 524320 | tf_op jit(solution)/shard_map/ppermute | solution.py:638
  21.1 4.1 %collective-permute-start.6 = (f32[30,8,512]{2,1,0:T(8,128)S(1)}, f32[30,8,512]{2,1,0:T(8,128)S(1)}, u32[]{:S(2)}, u32[]{:S(2)}) collective-permute-start(f32[30,8,512]{2,1,0:T(8,128)S(1)} %trim.2), channel_id=1, source_target_pairs={{0,4},{1,5},{4,8},{5,9},{6,2},{7,3},{8,12},{9,13},{10,6},{11,7},{1... | collective-permute-start | bytes 1474568 | tf_op jit(solution)/shard_map/ppermute | solution.py:647
  25.2 0.1 merge_near.3
  25.3 1.3 %collective-permute-start.10 = (f32[30,8,512]{2,1,0:T(8,128)S(1)}, f32[30,8,512]{2,1,0:T(8,128)S(1)}, u32[]{:S(2)}, u32[]{:S(2)}) collective-permute-start(f32[30,8,512]{2,1,0:T(8,128)S(1)} %get-tuple-element.69), channel_id=1, source_target_pairs={{2,6},{3,7},{4,0},{5,1},{6,10},{7,11},{8,4},{9,5},{10,14},{11,15},... | collective-permute-start | bytes 1474568 | tf_op jit(solution)/shard_map/ppermute | solution.py:647
  26.6 5.4 %collective-permute-done.11.far_ref.ref = f32[33,8,512]{2,1,0:T(8,128)S(1)} collective-permute-done((f32[33,8,512]{2,1,0:T(8,128)S(1)}, f32[33,8,512]{2,1,0:T(8,128)S(1)}, u32[]{:S(2)}, u32[]{:S(2)}) %collective-permute-start.11) | collective-permute-done | bytes 540704 | tf_op jit(solution)/shard_map/ppermute | solution.py:638
  32.1 3.8 %collective-permute-start.12 = (f32[30,8,512]{2,1,0:T(8,128)S(1)}, f32[30,8,512]{2,1,0:T(8,128)S(1)}, u32[]{:S(2)}, u32[]{:S(2)}) collective-permute-start(f32[30,8,512]{2,1,0:T(8,128)S(1)} %trim.3), channel_id=1, source_target_pairs={{0,4},{1,5},{4,8},{5,9},{6,2},{7,3},{8,12},{9,13},{10,6},{11,7},{1... | collective-permute-start | bytes 1474568 | tf_op jit(solution)/shard_map/ppermute | solution.py:647
  35.9 1.4 %prepare_planes.2 = (f32[22,2,8,512]{3,2,1,0:T(8,128)S(1)}, f32[22,2,8,512]{3,2,1,0:T(8,128)S(1)}, f32[22,2,8,512]{3,2,1,0:T(8,128)S(1)}, f32[22,2,8,512]{3,2,1,...) custom-call(f32[32,8,512]{2,1,0:T(8,128)S(1)} %get-tuple-element.52., ...), custom_call_target="tpu_custom_call" | custom-call | bytes 8388608 | tf_op jit(solution)/shard_map/prepare_planes/pallas_call | solution.py:377
  37.2 0.0 collective-permute-done.6.refs_9_
  37.2 5.2 %solve.2 = (f32[8,8,512]{2,1,0:T(8,128)S(1)}, f32[8,8,512]{2,1,0:T(8,128)S(1)}, f32[8,8,512]{2,1,0:T(8,128)S(1)}, f32[8,8,512]{2,1,0:T(8,128)S(1)}, f32[16,512]{1,0:T(8,128)S(1)}) custom-call(f32[22,2,8,512]{3,2,1,0:T(8,128)S(1)} %get-tuple-element.55.refs_0_, f32[22,2,8,512]{3,2,1,0:T(8,128)S(1)} %get-tuple-element.56.refs_1_, ...), custom_call_target="tpu_custom_call" | custom-call | bytes 16777216 | tf_op jit(solution)/shard_map/solve/pallas_call | solution.py:476
  42.4 0.1 collective-permute-start.7
  42.5 0.1 collective-permute-start.8
  42.6 1.8 %collective-permute-start.9 = (f32[8,8,512]{2,1,0:T(8,128)S(1)}, f32[8,8,512]{2,1,0:T(8,128)S(1)}, u32[]{:S(2)}, u32[]{:S(2)}) collective-permute-start(f32[8,8,512]{2,1,0:T(8,128)S(1)} %get-tuple-element.67), channel_id=1, source_target_pairs={{0,3},{1,2},{2,1},{3,0},{4,7},{5,6},{6,5},{7,4},{8,11},{9,10},{10,... | collective-permute-start | bytes 393224 | tf_op jit(solution)/shard_map/ppermute | solution.py:638
  44.3 0.0 collective-permute-done.10.halo_ref
  44.4 1.4 %prepare_planes.3 = (f32[22,2,8,512]{3,2,1,0:T(8,128)S(1)}, f32[22,2,8,512]{3,2,1,0:T(8,128)S(1)}, f32[22,2,8,512]{3,2,1,0:T(8,128)S(1)}, f32[22,2,8,512]{3,2,1,...) custom-call(f32[32,8,512]{2,1,0:T(8,128)S(1)} %get-tuple-element.68., ...), custom_call_target="tpu_custom_call" | custom-call | bytes 8388608 | tf_op jit(solution)/shard_map/prepare_planes/pallas_call | solution.py:377
  45.7 0.0 collective-permute-done.12.refs_9_
  45.8 4.8 %solve.3 = (f32[8,8,512]{2,1,0:T(8,128)S(1)}, f32[8,8,512]{2,1,0:T(8,128)S(1)}, f32[8,8,512]{2,1,0:T(8,128)S(1)}, f32[8,8,512]{2,1,0:T(8,128)S(1)}, f32[16,512]{1,0:T(8,128)S(1)}) custom-call(f32[22,2,8,512]{3,2,1,0:T(8,128)S(1)} %get-tuple-element.71.refs_0_, f32[22,2,8,512]{3,2,1,0:T(8,128)S(1)} %get-tuple-element.72.refs_1_, ...), custom_call_target="tpu_custom_call" | custom-call | bytes 16777216 | tf_op jit(solution)/shard_map/solve/pallas_call | solution.py:476
  50.6 0.0 copy-start
  50.6 0.1 collective-permute-done.9.refs_3_.refs_6_
  50.8 2.2 %collective-permute-start.16 = (f32[16,512]{1,0:T(8,128)S(1)}, f32[16,512]{1,0:T(8,128)S(1)}, u32[]{:S(2)}, u32[]{:S(2)}) collective-permute-start(f32[16,512]{1,0:T(8,128)S(1)} %get-tuple-element.86), channel_id=1, source_target_pairs={{0,2},{1,3},{2,0},{3,1},{4,6},{5,7},{6,4},{7,5},{8,10},{9,11},{10,... | collective-permute-start | bytes 98312 | tf_op jit(solution)/shard_map/ppermute | solution.py:638
  53.0 0.2 collective-permute-start.18
  53.2 0.3 collective-permute-start.13
  53.5 1.6 %collective-permute-start.14 = (f32[8,8,512]{2,1,0:T(8,128)S(1)}, f32[8,8,512]{2,1,0:T(8,128)S(1)}, u32[]{:S(2)}, u32[]{:S(2)}) collective-permute-start(f32[8,8,512]{2,1,0:T(8,128)S(1)} %get-tuple-element.82), channel_id=1, source_target_pairs={{0,2},{1,3},{2,0},{3,1},{4,6},{5,7},{6,4},{7,5},{8,10},{9,11},{10,... | collective-permute-start | bytes 393224 | tf_op jit(solution)/shard_map/ppermute | solution.py:638
  55.1 0.1 collective-permute-start.15
  55.3 1.0 %collective-permute-done.17 = f32[16,512]{1,0:T(8,128)S(1)} collective-permute-done((f32[16,512]{1,0:T(8,128)S(1)}, f32[16,512]{1,0:T(8,128)S(1)}, u32[]{:S(2)}, u32[]{:S(2)}) %collective-permute-start.17) | collective-permute-done | bytes 32800 | tf_op jit(solution)/shard_map/ppermute | solution.py:638
  56.3 2.8 %collective-permute-start.19 = (f32[1,16,512]{2,1,0:T(8,128)S(1)}, f32[1,16,512]{2,1,0:T(8,128)S(1)}, u32[]{:S(2)}, u32[]{:S(2)}) collective-permute-start(f32[1,16,512]{2,1,0:T(8,128)S(1)} %add_bitcast_fusion.refs_0_), channel_id=1, source_target_pairs={{4,0},{5,1},{6,2},{7,3},{8,4},{9,5},{10,6},{11,7},{12,8},{13,9},{1... | collective-permute-start | bytes 98312 | tf_op jit(solution)/shard_map/ppermute | solution.py:656
  59.2 0.3 collective-permute-start.20
  59.4 1.6 %collective-permute-start.21 = (f32[1,16,512]{2,1,0:T(8,128)S(1)}, f32[1,16,512]{2,1,0:T(8,128)S(1)}, u32[]{:S(2)}, u32[]{:S(2)}) collective-permute-start(f32[1,16,512]{2,1,0:T(8,128)S(1)} %add_bitcast_fusion.refs_0_), channel_id=1, source_target_pairs={{12,0},{13,1},{14,2},{15,3},{0,4},{1,5},{2,6},{3,7},{4,8},{5,9},{6... | collective-permute-start | bytes 98312 | tf_op jit(solution)/shard_map/ppermute | solution.py:656
  61.0 0.5 slice_bitcast_fusion.1
  61.5 0.1 collective-permute-done.15.refs_7_
  61.6 1.0 %gather_adjoint.1 = (f32[8,4,16,512]{3,2,1,0:T(8,128)}, f32[8,128]{1,0:T(8,128)S(1)}) custom-call(f32[8,8,512]{2,1,0:T(8,128)S(1)} %get-tuple-element.64.refs_0_, f32[8,8,512]{2,1,0:T(8,128)S(1)} %collective-permute-done.7.refs_1_.refs_4_, f32[8,8,512]{2,1,0:T(8,128)S(1)} %collective-permute-done.8.refs_2_.refs_5_, ...), custom_call_target="tpu_custom_call" | custom-call | bytes 4194304 | tf_op jit(solution)/shard_map/gather_adjoint/pallas_call | solution.py:558
  62.7 1.4 %collective-permute-done.20.refs_2_ = f32[1,16,512]{2,1,0:T(8,128)S(1)} collective-permute-done((f32[1,16,512]{2,1,0:T(8,128)S(1)}, f32[1,16,512]{2,1,0:T(8,128)S(1)}, u32[]{:S(2)}, u32[]{:S(2)}) %collective-permute-start.20) | collective-permute-done | bytes 32800 | tf_op jit(solution)/shard_map/ppermute | solution.py:656
  64.1 1.1 %collective-permute-done.21.refs_3_ = f32[1,16,512]{2,1,0:T(8,128)S(1)} collective-permute-done((f32[1,16,512]{2,1,0:T(8,128)S(1)}, f32[1,16,512]{2,1,0:T(8,128)S(1)}, u32[]{:S(2)}, u32[]{:S(2)}) %collective-permute-start.21) | collective-permute-done | bytes 32800 | tf_op jit(solution)/shard_map/ppermute | solution.py:656
  65.2 1.1 %control.1 = f32[32,512]{1,0:T(8,128)} custom-call(f32[1,16,512]{2,1,0:T(8,128)S(1)} %add_bitcast_fusion.refs_0_, f32[1,16,512]{2,1,0:T(8,128)S(1)} %collective-permute-done.19.refs_1_, f32[1,16,512]{2,1,0:T(8,128)S(1)} %collective-permute-done.20.refs_2_, f32[1,16,512]{2,1,0:T(8,128)S(1)} %collective-permute-done.21.refs_3_, f32[16,32,64]{2,1,0:T(8,128)S(1)} %copy-done.1, ...), custom_call_target="tpu_custom_call" | custom-call | tf_op jit(solution)/shard_map/control/pallas_call | solution.py:610
  (20 shorter events, 0.2 us)
Async XLA Ops:
  2.9 2.3 %collective-permute-start.1 = (f32[33,8,512]{2,1,0:T(8,128)S(1)}, f32[33,8,512]{2,1,0:T(8,128)S(1)}, u32[]{:S(2)}, u32[]{:S(2)}) collective-permute-start(f32[33,8,512]{2,1,0:T(8,128)S(1)} %get-tuple-element.49), channel_id=1, source_target_pairs={{0,1},{1,0},{2,3},{3,2},{4,5},{5,4},{6,7},{7,6},{8,9},{9,8},{10,11... | collective-permute-start | bytes 1622024 | tf_op jit(solution)/shard_map/ppermute | solution.py:638
  5.1 11.9 %collective-permute-start = (f32[32,8,512]{2,1,0:T(8,128)S(1)}, f32[32,8,512]{2,1,0:T(8,128)S(1)}, u32[]{:S(2)}, u32[]{:S(2)}) collective-permute-start(f32[32,8,512]{2,1,0:T(8,128)S(1)} %get-tuple-element.47), channel_id=1, source_target_pairs={{0,1},{1,0},{2,3},{3,2},{4,5},{5,4},{6,7},{7,6},{8,9},{9,8},{10,11... | collective-permute-start | bytes 1572872 | tf_op jit(solution)/shard_map/ppermute | solution.py:638
  5.3 15.7 %collective-permute-start.5 = (f32[32,8,512]{2,1,0:T(8,128)S(1)}, f32[32,8,512]{2,1,0:T(8,128)S(1)}, u32[]{:S(2)}, u32[]{:S(2)}) collective-permute-start(f32[32,8,512]{2,1,0:T(8,128)S(1)} %get-tuple-element.54), channel_id=1, source_target_pairs={{0,2},{1,3},{2,0},{3,1},{4,6},{5,7},{6,4},{7,5},{8,10},{9,11},{10,... | collective-permute-start | bytes 1572872 | tf_op jit(solution)/shard_map/ppermute | solution.py:638
  8.3 3.7 %collective-permute-start.2 = (f32[8,512]{1,0:T(8,128)S(1)}, f32[8,512]{1,0:T(8,128)S(1)}, u32[]{:S(2)}, u32[]{:S(2)}) collective-permute-start(f32[8,512]{1,0:T(8,128)S(1)} %get-tuple-element.51), channel_id=1, source_target_pairs={{4,0},{5,1},{6,2},{7,3},{0,4},{1,5},{2,6},{3,7},{12,8},{13,9},{14,... | collective-permute-start | bytes 49160 | tf_op jit(solution)/shard_map/ppermute | solution.py:656
  12.1 4.6 %collective-permute-start.3 = (f32[8,512]{1,0:T(8,128)S(1)}, f32[8,512]{1,0:T(8,128)S(1)}, u32[]{:S(2)}, u32[]{:S(2)}) collective-permute-start(f32[8,512]{1,0:T(8,128)S(1)} %add.15), channel_id=1, source_target_pairs={{8,0},{9,1},{10,2},{11,3},{12,4},{13,5},{14,6},{15,7},{0,8},{1,9},... | collective-permute-start | bytes 49160 | tf_op jit(solution)/shard_map/ppermute | solution.py:656
  16.8 15.3 %collective-permute-start.11 = (f32[33,8,512]{2,1,0:T(8,128)S(1)}, f32[33,8,512]{2,1,0:T(8,128)S(1)}, u32[]{:S(2)}, u32[]{:S(2)}) collective-permute-start(f32[33,8,512]{2,1,0:T(8,128)S(1)} %merge.3), channel_id=1, source_target_pairs={{0,2},{1,3},{2,0},{3,1},{4,6},{5,7},{6,4},{7,5},{8,10},{9,11},{10,... | collective-permute-start | bytes 1622024 | tf_op jit(solution)/shard_map/ppermute | solution.py:638
  17.1 18.7 %collective-permute-start.4 = (f32[30,8,512]{2,1,0:T(8,128)S(1)}, f32[30,8,512]{2,1,0:T(8,128)S(1)}, u32[]{:S(2)}, u32[]{:S(2)}) collective-permute-start(f32[30,8,512]{2,1,0:T(8,128)S(1)} %get-tuple-element.53), channel_id=1, source_target_pairs={{2,6},{3,7},{4,0},{5,1},{6,10},{7,11},{8,4},{9,5},{10,14},{11,15},... | collective-permute-start | bytes 1474568 | tf_op jit(solution)/shard_map/ppermute | solution.py:647
  21.1 16.1 %collective-permute-start.6 = (f32[30,8,512]{2,1,0:T(8,128)S(1)}, f32[30,8,512]{2,1,0:T(8,128)S(1)}, u32[]{:S(2)}, u32[]{:S(2)}) collective-permute-start(f32[30,8,512]{2,1,0:T(8,128)S(1)} %trim.2), channel_id=1, source_target_pairs={{0,4},{1,5},{4,8},{5,9},{6,2},{7,3},{8,12},{9,13},{10,6},{11,7},{1... | collective-permute-start | bytes 1474568 | tf_op jit(solution)/shard_map/ppermute | solution.py:647
  25.3 19.1 %collective-permute-start.10 = (f32[30,8,512]{2,1,0:T(8,128)S(1)}, f32[30,8,512]{2,1,0:T(8,128)S(1)}, u32[]{:S(2)}, u32[]{:S(2)}) collective-permute-start(f32[30,8,512]{2,1,0:T(8,128)S(1)} %get-tuple-element.69), channel_id=1, source_target_pairs={{2,6},{3,7},{4,0},{5,1},{6,10},{7,11},{8,4},{9,5},{10,14},{11,15},... | collective-permute-start | bytes 1474568 | tf_op jit(solution)/shard_map/ppermute | solution.py:647
  32.1 13.7 %collective-permute-start.12 = (f32[30,8,512]{2,1,0:T(8,128)S(1)}, f32[30,8,512]{2,1,0:T(8,128)S(1)}, u32[]{:S(2)}, u32[]{:S(2)}) collective-permute-start(f32[30,8,512]{2,1,0:T(8,128)S(1)} %trim.3), channel_id=1, source_target_pairs={{0,4},{1,5},{4,8},{5,9},{6,2},{7,3},{8,12},{9,13},{10,6},{11,7},{1... | collective-permute-start | bytes 1474568 | tf_op jit(solution)/shard_map/ppermute | solution.py:647
  42.4 8.2 %collective-permute-start.7 = (f32[8,8,512]{2,1,0:T(8,128)S(1)}, f32[8,8,512]{2,1,0:T(8,128)S(1)}, u32[]{:S(2)}, u32[]{:S(2)}) collective-permute-start(f32[8,8,512]{2,1,0:T(8,128)S(1)} %get-tuple-element.65), channel_id=1, source_target_pairs={{0,1},{1,0},{2,3},{3,2},{4,5},{5,4},{6,7},{7,6},{8,9},{9,8},{10,11... | collective-permute-start | bytes 393224 | tf_op jit(solution)/shard_map/ppermute | solution.py:638
  42.5 8.1 %collective-permute-start.8 = (f32[8,8,512]{2,1,0:T(8,128)S(1)}, f32[8,8,512]{2,1,0:T(8,128)S(1)}, u32[]{:S(2)}, u32[]{:S(2)}) collective-permute-start(f32[8,8,512]{2,1,0:T(8,128)S(1)} %get-tuple-element.66), channel_id=1, source_target_pairs={{0,2},{1,3},{2,0},{3,1},{4,6},{5,7},{6,4},{7,5},{8,10},{9,11},{10,... | collective-permute-start | bytes 393224 | tf_op jit(solution)/shard_map/ppermute | solution.py:638
  42.6 8.2 %collective-permute-start.9 = (f32[8,8,512]{2,1,0:T(8,128)S(1)}, f32[8,8,512]{2,1,0:T(8,128)S(1)}, u32[]{:S(2)}, u32[]{:S(2)}) collective-permute-start(f32[8,8,512]{2,1,0:T(8,128)S(1)} %get-tuple-element.67), channel_id=1, source_target_pairs={{0,3},{1,2},{2,1},{3,0},{4,7},{5,6},{6,5},{7,4},{8,11},{9,10},{10,... | collective-permute-start | bytes 393224 | tf_op jit(solution)/shard_map/ppermute | solution.py:638
  50.6 14.6 %copy-start = (f32[512,512]{1,0:T(8,128)S(1)}, f32[512,512]{1,0:T(8,128)}, u32[]{:S(2)}) copy-start(f32[512,512]{1,0:T(8,128)} %constant.5.clone.refs_5_) | copy-start | bytes 3145732
  50.8 4.4 %collective-permute-start.16 = (f32[16,512]{1,0:T(8,128)S(1)}, f32[16,512]{1,0:T(8,128)S(1)}, u32[]{:S(2)}, u32[]{:S(2)}) collective-permute-start(f32[16,512]{1,0:T(8,128)S(1)} %get-tuple-element.86), channel_id=1, source_target_pairs={{0,2},{1,3},{2,0},{3,1},{4,6},{5,7},{6,4},{7,5},{8,10},{9,11},{10,... | collective-permute-start | bytes 98312 | tf_op jit(solution)/shard_map/ppermute | solution.py:638
  53.0 3.3 %collective-permute-start.17 = (f32[16,512]{1,0:T(8,128)S(1)}, f32[16,512]{1,0:T(8,128)S(1)}, u32[]{:S(2)}, u32[]{:S(2)}) collective-permute-start(f32[16,512]{1,0:T(8,128)S(1)} %get-tuple-element.86), channel_id=1, source_target_pairs={{0,3},{1,2},{2,1},{3,0},{4,7},{5,6},{6,5},{7,4},{8,11},{9,10},{10,... | collective-permute-start | bytes 98312 | tf_op jit(solution)/shard_map/ppermute | solution.py:638
  53.0 3.3 %collective-permute-start.18 = (f32[16,512]{1,0:T(8,128)S(1)}, f32[16,512]{1,0:T(8,128)S(1)}, u32[]{:S(2)}, u32[]{:S(2)}) collective-permute-start(f32[16,512]{1,0:T(8,128)S(1)} %get-tuple-element.86), channel_id=1, source_target_pairs={{0,1},{1,0},{2,3},{3,2},{4,5},{5,4},{6,7},{7,6},{8,9},{9,8},{10,11... | collective-permute-start | bytes 98312 | tf_op jit(solution)/shard_map/ppermute | solution.py:638
  53.2 6.3 %collective-permute-start.13 = (f32[8,8,512]{2,1,0:T(8,128)S(1)}, f32[8,8,512]{2,1,0:T(8,128)S(1)}, u32[]{:S(2)}, u32[]{:S(2)}) collective-permute-start(f32[8,8,512]{2,1,0:T(8,128)S(1)} %get-tuple-element.81), channel_id=1, source_target_pairs={{0,1},{1,0},{2,3},{3,2},{4,5},{5,4},{6,7},{7,6},{8,9},{9,8},{10,11... | collective-permute-start | bytes 393224 | tf_op jit(solution)/shard_map/ppermute | solution.py:638
  53.5 8.0 %collective-permute-start.14 = (f32[8,8,512]{2,1,0:T(8,128)S(1)}, f32[8,8,512]{2,1,0:T(8,128)S(1)}, u32[]{:S(2)}, u32[]{:S(2)}) collective-permute-start(f32[8,8,512]{2,1,0:T(8,128)S(1)} %get-tuple-element.82), channel_id=1, source_target_pairs={{0,2},{1,3},{2,0},{3,1},{4,6},{5,7},{6,4},{7,5},{8,10},{9,11},{10,... | collective-permute-start | bytes 393224 | tf_op jit(solution)/shard_map/ppermute | solution.py:638
  55.1 6.5 %collective-permute-start.15 = (f32[8,8,512]{2,1,0:T(8,128)S(1)}, f32[8,8,512]{2,1,0:T(8,128)S(1)}, u32[]{:S(2)}, u32[]{:S(2)}) collective-permute-start(f32[8,8,512]{2,1,0:T(8,128)S(1)} %get-tuple-element.83), channel_id=1, source_target_pairs={{0,3},{1,2},{2,1},{3,0},{4,7},{5,6},{6,5},{7,4},{8,11},{9,10},{10,... | collective-permute-start | bytes 393224 | tf_op jit(solution)/shard_map/ppermute | solution.py:638
  56.3 6.3 %collective-permute-start.19 = (f32[1,16,512]{2,1,0:T(8,128)S(1)}, f32[1,16,512]{2,1,0:T(8,128)S(1)}, u32[]{:S(2)}, u32[]{:S(2)}) collective-permute-start(f32[1,16,512]{2,1,0:T(8,128)S(1)} %add_bitcast_fusion.refs_0_), channel_id=1, source_target_pairs={{4,0},{5,1},{6,2},{7,3},{8,4},{9,5},{10,6},{11,7},{12,8},{13,9},{1... | collective-permute-start | bytes 98312 | tf_op jit(solution)/shard_map/ppermute | solution.py:656
  59.2 4.9 %collective-permute-start.20 = (f32[1,16,512]{2,1,0:T(8,128)S(1)}, f32[1,16,512]{2,1,0:T(8,128)S(1)}, u32[]{:S(2)}, u32[]{:S(2)}) collective-permute-start(f32[1,16,512]{2,1,0:T(8,128)S(1)} %add_bitcast_fusion.refs_0_), channel_id=1, source_target_pairs={{8,0},{9,1},{10,2},{11,3},{12,4},{13,5},{14,6},{15,7},{0,8},{1,9},... | collective-permute-start | bytes 98312 | tf_op jit(solution)/shard_map/ppermute | solution.py:656
  59.4 5.7 %collective-permute-start.21 = (f32[1,16,512]{2,1,0:T(8,128)S(1)}, f32[1,16,512]{2,1,0:T(8,128)S(1)}, u32[]{:S(2)}, u32[]{:S(2)}) collective-permute-start(f32[1,16,512]{2,1,0:T(8,128)S(1)} %add_bitcast_fusion.refs_0_), channel_id=1, source_target_pairs={{12,0},{13,1},{14,2},{15,3},{0,4},{1,5},{2,6},{3,7},{4,8},{5,9},{6... | collective-permute-start | bytes 98312 | tf_op jit(solution)/shard_map/ppermute | solution.py:656
  61.6 3.6 %copy-start.1 = (f32[16,32,64]{2,1,0:T(8,128)S(1)}, f32[16,32,64]{2,1,0:T(8,128)}, u32[]{:S(2)}) copy-start(f32[16,32,64]{2,1,0:T(8,128)} %constant.4.clone.refs_4_) | copy-start | bytes 393220

commit v19 on v15

--- a/solution.py
+++ b/solution.py
@@ -576,13 +576,28 @@
     )(*[piece for group in pieces for piece in group])
 
 
+def split_basis(basis):
+    def kernel(ref, high_ref, low_ref):
+        high_ref[...], low_ref[...] = in_halves(ref[...])
+
+    vmem = pl.BlockSpec(memory_space=pltpu.VMEM)
+    return pl.pallas_call(
+        kernel,
+        out_shape=[jax.ShapeDtypeStruct(basis.shape, jnp.bfloat16)] * 2,
+        in_specs=[vmem],
+        out_specs=[vmem] * 2,
+        compiler_params=pltpu.CompilerParams(vmem_limit_bytes=4 * MIB),
+        name="split_basis",
+    )(basis)
+
+
 def control(faces, radices, basis_z, basis_x, after):
     slabs, own_count, depth_total = basis_z.shape
     own, columns = faces[0].shape[1:]
     teams = depth_total // own
 
     def kernel(*refs):
-        parts, (z_ref, x_ref, _, out_ref, whole) = refs[: len(faces)], refs[len(faces) :]
+        parts, (z_ref, x_ref, low_ref, _, out_ref, whole) = refs[: len(faces)], refs[len(faces) :]
         rank = lax.axis_index("gz")
         team = rank // TEAM
         for n in range(teams):
@@ -599,22 +614,21 @@
             preferred_element_type=F32,
         )
         high, low = in_halves(along_z)
-        x_high, x_low = in_halves(x_ref[...])
         both = jnp.concatenate([high, low], axis=0)
-        first = jnp.dot(both, x_high, preferred_element_type=F32)
-        second = jnp.dot(high, x_low, preferred_element_type=F32)
+        first = jnp.dot(both, x_ref[...], preferred_element_type=F32)
+        second = jnp.dot(high, low_ref[...], preferred_element_type=F32)
         out_ref[...] = (first[:own_count] + first[own_count:]) + second
 
     vmem = pl.BlockSpec(memory_space=pltpu.VMEM)
     return pl.pallas_call(
         kernel,
-        out_shape=jax.ShapeDtypeStruct((own_count, basis_x.shape[1]), F32),
-        in_specs=[vmem] * (len(faces) + 2) + [pl.BlockSpec(memory_space=pl.ANY)],
+        out_shape=jax.ShapeDtypeStruct((own_count, columns), F32),
+        in_specs=[vmem] * (len(faces) + 3) + [pl.BlockSpec(memory_space=pl.ANY)],
         out_specs=vmem,
         scratch_shapes=[pltpu.VMEM((teams, own, columns), F32)],
         compiler_params=pltpu.CompilerParams(vmem_limit_bytes=8 * MIB),
         name="control",
-    )(*faces, basis_z, basis_x, after)
+    )(*faces, basis_z, *basis_x, after)
 
 
 def radices_of(teams):
@@ -682,10 +696,11 @@
         far.append(swap(merge(mine, theirs, slot, size, sums), 2))
     sums = [sums, far[-1][2 * size]]
 
+    basis_x = split_basis(jnp.asarray(cosine_basis(columns, MB)))
     pieces, faces = [], []
     for slot in range(slots):
         far_halo = along(trim(far[slot], size), False)
-        made, edge = prepare_planes(near[slot], far[slot], near_halo[slot], planes, faces[-1:])
+        made, edge = prepare_planes(near[slot], far[slot], near_halo[slot], planes, [*faces[-1:], basis_x[0]] if slot else [])
         solved = solve(made, edge, far_halo, planes)
         pieces.append([solved[0]] + [swap(solved[m], m) for m in (1, 2, 3)])
         faces.append(solved[TEAM])
@@ -703,7 +718,7 @@
         heard,
         radices,
         jnp.asarray(cosine_basis(depth_total, MA).T.reshape(slabs, own_count, depth_total)),
-        jnp.asarray(cosine_basis(columns, MB)),
+        basis_x,
         mark,
     )
     return (adjoint, gradient, moments[0, :2])

time: 66.6 us -> 66.5 us (level)
  no operation moved by 1% of the time
where the time goes in v19:
time: 66.5 us; the launch traced here: 66.2 us
  starting transfers between devices  29.5 us (44%)
  Pallas kernels  19.4 us (29%)
  waiting for transfers between devices  15.9 us (24%)
  between operations  0.86 us (1%)
    ppermute x4, starting transfers between devices, along(): return lax.ppermute(value, 'gz', pairs)  10.6 us
    ppermute x13, starting transfers between devices, swap(): return lax.ppermute(value, 'gz', [(i, i ^ m) for i in range(slabs)])  10.1 us
    pallas_call x2, Pallas kernels, solve(): pl.pallas_call(kernel, out_shape=[jax.ShapeDtypeStruct((2 * planes, half,...  10 us
    ppermute x13, waiting for transfers between devices, swap(): return lax.ppermute(value, 'gz', [(i, i ^ m) for i in range(slabs)])  9.18 us
    ppermute x5, starting transfers between devices, from_teams(): heard.append(lax.ppermute(value, 'gz', pairs))  8.83 us
    ppermute x5, waiting for transfers between devices, from_teams(): heard.append(lax.ppermute(value, 'gz', pairs))  6.71 us
    pallas_call x2, Pallas kernels, prepare(): pl.pallas_call(kernel, out_shape=[jax.ShapeDtypeStruct(shape, F32) for sh...  3.97 us
    pallas_call x2, Pallas kernels, prepare_planes(): pl.pallas_call(kernel, out_shape=[jax.ShapeDtypeStruct((count, 2, half, c...  2.74 us
  transfers between devices with their start and end apart: 22, of which 9 were waited for; matrix products, arithmetic and copies ran while one was open for 1% of the time, Pallas kernels for 24%

profile of v19, /device:TPU:0, one launch (start us, length us, event | category | flops | bytes accessed | tf_op | source)
XLA Modules:
  0.0 66.2 jit_solution(18029903462951335833)
XLA Ops:
  0.6 2.3 %prepare.3 = (f32[33,8,512]{2,1,0:T(8,128)S(1)}, f32[33,8,512]{2,1,0:T(8,128)S(1)}, f32[8,512]{1,0:T(8,128)S(1)}) custom-call(f32[8,8]{1,0:T(8,128)} %refs_0_.3, f32[8]{0:T(128)} %refs_1_.3, f32[8,4,16,512]{3,2,1,0:T(8,128)} %refs_2_.3, f32[4,16,512]{2,1,0:T(8,128)} %refs_3_.3, s32[8,4,16,512]{3,2,1,0:T(8,128)} %refs_4_.4), custom_call_target="tpu_custom_call" | custom-call | bytes 4194304 | tf_op jit(solution)/shard_map/prepare/pallas_call | solution.py:157
  2.9 0.5 collective-permute-start.1
  3.5 1.7 %prepare.2 = (f32[32,8,512]{2,1,0:T(8,128)S(1)}, f32[32,8,512]{2,1,0:T(8,128)S(1)}) custom-call(f32[8,8]{1,0:T(8,128)} %refs_0_.3, f32[8]{0:T(128)} %refs_1_.3, f32[8,4,16,512]{3,2,1,0:T(8,128)} %refs_2_.3, f32[4,16,512]{2,1,0:T(8,128)} %refs_3_.3, s32[8,4,16,512]{3,2,1,0:T(8,128)} %refs_4_.4), custom_call_target="tpu_custom_call" | custom-call | bytes 4194304 | tf_op jit(solution)/shard_map/prepare/pallas_call | solution.py:157
  5.1 0.1 collective-permute-start
  5.3 0.0 collective-permute-done.1.theirs_ref
  5.3 0.1 merge.2
  5.3 3.0 %collective-permute-start.5 = (f32[32,8,512]{2,1,0:T(8,128)S(1)}, f32[32,8,512]{2,1,0:T(8,128)S(1)}, u32[]{:S(2)}, u32[]{:S(2)}) collective-permute-start(f32[32,8,512]{2,1,0:T(8,128)S(1)} %get-tuple-element.56), channel_id=1, source_target_pairs={{0,2},{1,3},{2,0},{3,1},{4,6},{5,7},{6,4},{7,5},{8,10},{9,11},{10,... | collective-permute-start | bytes 1572872 | tf_op jit(solution)/shard_map/ppermute | solution.py:651
  8.3 1.6 %collective-permute-start.2 = (f32[8,512]{1,0:T(8,128)S(1)}, f32[8,512]{1,0:T(8,128)S(1)}, u32[]{:S(2)}, u32[]{:S(2)}) collective-permute-start(f32[8,512]{1,0:T(8,128)S(1)} %get-tuple-element.53), channel_id=1, source_target_pairs={{4,0},{5,1},{6,2},{7,3},{0,4},{1,5},{2,6},{3,7},{12,8},{13,9},{14,... | collective-permute-start | bytes 49160 | tf_op jit(solution)/shard_map/ppermute | solution.py:669
  9.9 2.2 %collective-permute-done.2 = f32[8,512]{1,0:T(8,128)S(1)} collective-permute-done((f32[8,512]{1,0:T(8,128)S(1)}, f32[8,512]{1,0:T(8,128)S(1)}, u32[]{:S(2)}, u32[]{:S(2)}) %collective-permute-start.2) | collective-permute-done | bytes 16416 | tf_op jit(solution)/shard_map/ppermute | solution.py:669
  12.1 2.6 %collective-permute-start.3 = (f32[8,512]{1,0:T(8,128)S(1)}, f32[8,512]{1,0:T(8,128)S(1)}, u32[]{:S(2)}, u32[]{:S(2)}) collective-permute-start(f32[8,512]{1,0:T(8,128)S(1)} %add.15), channel_id=1, source_target_pairs={{8,0},{9,1},{10,2},{11,3},{12,4},{13,5},{14,6},{15,7},{0,8},{1,9},... | collective-permute-start | bytes 49160 | tf_op jit(solution)/shard_map/ppermute | solution.py:669
  14.7 2.0 %collective-permute-done.3 = f32[8,512]{1,0:T(8,128)S(1)} collective-permute-done((f32[8,512]{1,0:T(8,128)S(1)}, f32[8,512]{1,0:T(8,128)S(1)}, u32[]{:S(2)}, u32[]{:S(2)}) %collective-permute-start.3) | collective-permute-done | bytes 16416 | tf_op jit(solution)/shard_map/ppermute | solution.py:669
  16.7 0.1 merge.3
  16.8 0.3 collective-permute-start.11
  17.0 0.1 merge_near.2
  17.1 1.3 %collective-permute-start.4 = (f32[30,8,512]{2,1,0:T(8,128)S(1)}, f32[30,8,512]{2,1,0:T(8,128)S(1)}, u32[]{:S(2)}, u32[]{:S(2)}) collective-permute-start(f32[30,8,512]{2,1,0:T(8,128)S(1)} %get-tuple-element.55), channel_id=1, source_target_pairs={{2,6},{3,7},{4,0},{5,1},{6,10},{7,11},{8,4},{9,5},{10,14},{11,15},... | collective-permute-start | bytes 1474568 | tf_op jit(solution)/shard_map/ppermute | solution.py:660
  18.4 2.6 %collective-permute-done.5.far_ref.ref = f32[32,8,512]{2,1,0:T(8,128)S(1)} collective-permute-done((f32[32,8,512]{2,1,0:T(8,128)S(1)}, f32[32,8,512]{2,1,0:T(8,128)S(1)}, u32[]{:S(2)}, u32[]{:S(2)}) %collective-permute-start.5) | collective-permute-done | bytes 524320 | tf_op jit(solution)/shard_map/ppermute | solution.py:651
  21.1 0.0 copy-start
  21.1 4.2 %collective-permute-start.6 = (f32[30,8,512]{2,1,0:T(8,128)S(1)}, f32[30,8,512]{2,1,0:T(8,128)S(1)}, u32[]{:S(2)}, u32[]{:S(2)}) collective-permute-start(f32[30,8,512]{2,1,0:T(8,128)S(1)} %trim.2), channel_id=1, source_target_pairs={{0,4},{1,5},{4,8},{5,9},{6,2},{7,3},{8,12},{9,13},{10,6},{11,7},{1... | collective-permute-start | bytes 1474568 | tf_op jit(solution)/shard_map/ppermute | solution.py:660
  25.3 0.1 merge_near.3
  25.4 1.3 %collective-permute-start.10 = (f32[30,8,512]{2,1,0:T(8,128)S(1)}, f32[30,8,512]{2,1,0:T(8,128)S(1)}, u32[]{:S(2)}, u32[]{:S(2)}) collective-permute-start(f32[30,8,512]{2,1,0:T(8,128)S(1)} %get-tuple-element.71), channel_id=1, source_target_pairs={{2,6},{3,7},{4,0},{5,1},{6,10},{7,11},{8,4},{9,5},{10,14},{11,15},... | collective-permute-start | bytes 1474568 | tf_op jit(solution)/shard_map/ppermute | solution.py:660
  26.7 5.3 %collective-permute-done.11.far_ref.ref = f32[33,8,512]{2,1,0:T(8,128)S(1)} collective-permute-done((f32[33,8,512]{2,1,0:T(8,128)S(1)}, f32[33,8,512]{2,1,0:T(8,128)S(1)}, u32[]{:S(2)}, u32[]{:S(2)}) %collective-permute-start.11) | collective-permute-done | bytes 540704 | tf_op jit(solution)/shard_map/ppermute | solution.py:651
  32.1 3.8 %collective-permute-start.12 = (f32[30,8,512]{2,1,0:T(8,128)S(1)}, f32[30,8,512]{2,1,0:T(8,128)S(1)}, u32[]{:S(2)}, u32[]{:S(2)}) collective-permute-start(f32[30,8,512]{2,1,0:T(8,128)S(1)} %trim.3), channel_id=1, source_target_pairs={{0,4},{1,5},{4,8},{5,9},{6,2},{7,3},{8,12},{9,13},{10,6},{11,7},{1... | collective-permute-start | bytes 1474568 | tf_op jit(solution)/shard_map/ppermute | solution.py:660
  35.9 0.2 split_basis.1
  36.0 0.0 collective-permute-done.4.halo_ref
  36.0 1.4 %prepare_planes.2 = (f32[22,2,8,512]{3,2,1,0:T(8,128)S(1)}, f32[22,2,8,512]{3,2,1,0:T(8,128)S(1)}, f32[22,2,8,512]{3,2,1,0:T(8,128)S(1)}, f32[22,2,8,512]{3,2,1,...) custom-call(f32[32,8,512]{2,1,0:T(8,128)S(1)} %get-tuple-element.54., ...), custom_call_target="tpu_custom_call" | custom-call | bytes 8388608 | tf_op jit(solution)/shard_map/prepare_planes/pallas_call | solution.py:376
  37.4 5.2 %solve.2 = (f32[8,8,512]{2,1,0:T(8,128)S(1)}, f32[8,8,512]{2,1,0:T(8,128)S(1)}, f32[8,8,512]{2,1,0:T(8,128)S(1)}, f32[8,8,512]{2,1,0:T(8,128)S(1)}, f32[16,512]{1,0:T(8,128)S(1)}) custom-call(f32[22,2,8,512]{3,2,1,0:T(8,128)S(1)} %get-tuple-element.57.refs_0_, f32[22,2,8,512]{3,2,1,0:T(8,128)S(1)} %get-tuple-element.58.refs_1_, ...), custom_call_target="tpu_custom_call" | custom-call | bytes 16777216 | tf_op jit(solution)/shard_map/solve/pallas_call | solution.py:475
  42.6 0.1 collective-permute-start.7
  42.6 0.1 collective-permute-start.8
  42.7 1.8 %collective-permute-start.9 = (f32[8,8,512]{2,1,0:T(8,128)S(1)}, f32[8,8,512]{2,1,0:T(8,128)S(1)}, u32[]{:S(2)}, u32[]{:S(2)}) collective-permute-start(f32[8,8,512]{2,1,0:T(8,128)S(1)} %get-tuple-element.69), channel_id=1, source_target_pairs={{0,3},{1,2},{2,1},{3,0},{4,7},{5,6},{6,5},{7,4},{8,11},{9,10},{10,... | collective-permute-start | bytes 393224 | tf_op jit(solution)/shard_map/ppermute | solution.py:651
  44.5 0.0 collective-permute-done.10.halo_ref
  44.5 1.4 %prepare_planes.3 = (f32[22,2,8,512]{3,2,1,0:T(8,128)S(1)}, f32[22,2,8,512]{3,2,1,0:T(8,128)S(1)}, f32[22,2,8,512]{3,2,1,0:T(8,128)S(1)}, f32[22,2,8,512]{3,2,1,...) custom-call(f32[32,8,512]{2,1,0:T(8,128)S(1)} %get-tuple-element.70., ...), custom_call_target="tpu_custom_call" | custom-call | bytes 8388608 | tf_op jit(solution)/shard_map/prepare_planes/pallas_call | solution.py:376
  45.9 4.8 %solve.3 = (f32[8,8,512]{2,1,0:T(8,128)S(1)}, f32[8,8,512]{2,1,0:T(8,128)S(1)}, f32[8,8,512]{2,1,0:T(8,128)S(1)}, f32[8,8,512]{2,1,0:T(8,128)S(1)}, f32[16,512]{1,0:T(8,128)S(1)}) custom-call(f32[22,2,8,512]{3,2,1,0:T(8,128)S(1)} %get-tuple-element.74.refs_0_, f32[22,2,8,512]{3,2,1,0:T(8,128)S(1)} %get-tuple-element.75.refs_1_, ...), custom_call_target="tpu_custom_call" | custom-call | bytes 16777216 | tf_op jit(solution)/shard_map/solve/pallas_call | solution.py:475
  50.8 0.1 collective-permute-done.9.refs_3_.refs_6_
  50.9 2.0 %collective-permute-start.16 = (f32[16,512]{1,0:T(8,128)S(1)}, f32[16,512]{1,0:T(8,128)S(1)}, u32[]{:S(2)}, u32[]{:S(2)}) collective-permute-start(f32[16,512]{1,0:T(8,128)S(1)} %get-tuple-element.89), channel_id=1, source_target_pairs={{0,2},{1,3},{2,0},{3,1},{4,6},{5,7},{6,4},{7,5},{8,10},{9,11},{10,... | collective-permute-start | bytes 98312 | tf_op jit(solution)/shard_map/ppermute | solution.py:651
  53.0 0.2 collective-permute-start.18
  53.2 0.3 collective-permute-start.13
  53.5 1.6 %collective-permute-start.14 = (f32[8,8,512]{2,1,0:T(8,128)S(1)}, f32[8,8,512]{2,1,0:T(8,128)S(1)}, u32[]{:S(2)}, u32[]{:S(2)}) collective-permute-start(f32[8,8,512]{2,1,0:T(8,128)S(1)} %get-tuple-element.85), channel_id=1, source_target_pairs={{0,2},{1,3},{2,0},{3,1},{4,6},{5,7},{6,4},{7,5},{8,10},{9,11},{10,... | collective-permute-start | bytes 393224 | tf_op jit(solution)/shard_map/ppermute | solution.py:651
  55.1 0.1 collective-permute-start.15
  55.3 1.0 %collective-permute-done.17 = f32[16,512]{1,0:T(8,128)S(1)} collective-permute-done((f32[16,512]{1,0:T(8,128)S(1)}, f32[16,512]{1,0:T(8,128)S(1)}, u32[]{:S(2)}, u32[]{:S(2)}) %collective-permute-start.17) | collective-permute-done | bytes 32800 | tf_op jit(solution)/shard_map/ppermute | solution.py:651
  56.3 2.8 %collective-permute-start.19 = (f32[1,16,512]{2,1,0:T(8,128)S(1)}, f32[1,16,512]{2,1,0:T(8,128)S(1)}, u32[]{:S(2)}, u32[]{:S(2)}) collective-permute-start(f32[1,16,512]{2,1,0:T(8,128)S(1)} %add_bitcast_fusion.refs_0_), channel_id=1, source_target_pairs={{4,0},{5,1},{6,2},{7,3},{8,4},{9,5},{10,6},{11,7},{12,8},{13,9},{1... | collective-permute-start | bytes 98312 | tf_op jit(solution)/shard_map/ppermute | solution.py:669
  59.2 0.3 collective-permute-start.20
  59.4 1.6 %collective-permute-start.21 = (f32[1,16,512]{2,1,0:T(8,128)S(1)}, f32[1,16,512]{2,1,0:T(8,128)S(1)}, u32[]{:S(2)}, u32[]{:S(2)}) collective-permute-start(f32[1,16,512]{2,1,0:T(8,128)S(1)} %add_bitcast_fusion.refs_0_), channel_id=1, source_target_pairs={{12,0},{13,1},{14,2},{15,3},{0,4},{1,5},{2,6},{3,7},{4,8},{5,9},{6... | collective-permute-start | bytes 98312 | tf_op jit(solution)/shard_map/ppermute | solution.py:669
  61.0 0.5 slice_bitcast_fusion.1
  61.5 0.1 collective-permute-done.15.refs_7_
  61.6 1.0 %gather_adjoint.1 = (f32[8,4,16,512]{3,2,1,0:T(8,128)}, f32[8,128]{1,0:T(8,128)S(1)}) custom-call(f32[8,8,512]{2,1,0:T(8,128)S(1)} %get-tuple-element.66.refs_0_, f32[8,8,512]{2,1,0:T(8,128)S(1)} %collective-permute-done.7.refs_1_.refs_4_, f32[8,8,512]{2,1,0:T(8,128)S(1)} %collective-permute-done.8.refs_2_.refs_5_, ...), custom_call_target="tpu_custom_call" | custom-call | bytes 4194304 | tf_op jit(solution)/shard_map/gather_adjoint/pallas_call | solution.py:557
  62.6 1.4 %collective-permute-done.20.refs_2_ = f32[1,16,512]{2,1,0:T(8,128)S(1)} collective-permute-done((f32[1,16,512]{2,1,0:T(8,128)S(1)}, f32[1,16,512]{2,1,0:T(8,128)S(1)}, u32[]{:S(2)}, u32[]{:S(2)}) %collective-permute-start.20) | collective-permute-done | bytes 32800 | tf_op jit(solution)/shard_map/ppermute | solution.py:669
  64.1 1.1 %collective-permute-done.21.refs_3_ = f32[1,16,512]{2,1,0:T(8,128)S(1)} collective-permute-done((f32[1,16,512]{2,1,0:T(8,128)S(1)}, f32[1,16,512]{2,1,0:T(8,128)S(1)}, u32[]{:S(2)}, u32[]{:S(2)}) %collective-permute-start.21) | collective-permute-done | bytes 32800 | tf_op jit(solution)/shard_map/ppermute | solution.py:669
  65.1 1.1 %control.1 = f32[32,512]{1,0:T(8,128)} custom-call(f32[1,16,512]{2,1,0:T(8,128)S(1)} %add_bitcast_fusion.refs_0_, f32[1,16,512]{2,1,0:T(8,128)S(1)} %collective-permute-done.19.refs_1_, f32[1,16,512]{2,1,0:T(8,128)S(1)} %collective-permute-done.20.refs_2_, f32[1,16,512]{2,1,0:T(8,128)S(1)} %collective-permute-done.21.refs_3_, f32[16,32,64]{2,1,0:T(8,128)S(1)} %copy-done.1, ...), custom_call_target="tpu_custom_call" | custom-call | tf_op jit(solution)/shard_map/control/pallas_call | solution.py:623
  (21 shorter events, 0.2 us)
Async XLA Ops:
  2.9 2.3 %collective-permute-start.1 = (f32[33,8,512]{2,1,0:T(8,128)S(1)}, f32[33,8,512]{2,1,0:T(8,128)S(1)}, u32[]{:S(2)}, u32[]{:S(2)}) collective-permute-start(f32[33,8,512]{2,1,0:T(8,128)S(1)} %get-tuple-element.51), channel_id=1, source_target_pairs={{0,1},{1,0},{2,3},{3,2},{4,5},{5,4},{6,7},{7,6},{8,9},{9,8},{10,11... | collective-permute-start | bytes 1622024 | tf_op jit(solution)/shard_map/ppermute | solution.py:651
  5.1 11.9 %collective-permute-start = (f32[32,8,512]{2,1,0:T(8,128)S(1)}, f32[32,8,512]{2,1,0:T(8,128)S(1)}, u32[]{:S(2)}, u32[]{:S(2)}) collective-permute-start(f32[32,8,512]{2,1,0:T(8,128)S(1)} %get-tuple-element.49), channel_id=1, source_target_pairs={{0,1},{1,0},{2,3},{3,2},{4,5},{5,4},{6,7},{7,6},{8,9},{9,8},{10,11... | collective-permute-start | bytes 1572872 | tf_op jit(solution)/shard_map/ppermute | solution.py:651
  5.3 15.7 %collective-permute-start.5 = (f32[32,8,512]{2,1,0:T(8,128)S(1)}, f32[32,8,512]{2,1,0:T(8,128)S(1)}, u32[]{:S(2)}, u32[]{:S(2)}) collective-permute-start(f32[32,8,512]{2,1,0:T(8,128)S(1)} %get-tuple-element.56), channel_id=1, source_target_pairs={{0,2},{1,3},{2,0},{3,1},{4,6},{5,7},{6,4},{7,5},{8,10},{9,11},{10,... | collective-permute-start | bytes 1572872 | tf_op jit(solution)/shard_map/ppermute | solution.py:651
  8.3 3.7 %collective-permute-start.2 = (f32[8,512]{1,0:T(8,128)S(1)}, f32[8,512]{1,0:T(8,128)S(1)}, u32[]{:S(2)}, u32[]{:S(2)}) collective-permute-start(f32[8,512]{1,0:T(8,128)S(1)} %get-tuple-element.53), channel_id=1, source_target_pairs={{4,0},{5,1},{6,2},{7,3},{0,4},{1,5},{2,6},{3,7},{12,8},{13,9},{14,... | collective-permute-start | bytes 49160 | tf_op jit(solution)/shard_map/ppermute | solution.py:669
  12.1 4.6 %collective-permute-start.3 = (f32[8,512]{1,0:T(8,128)S(1)}, f32[8,512]{1,0:T(8,128)S(1)}, u32[]{:S(2)}, u32[]{:S(2)}) collective-permute-start(f32[8,512]{1,0:T(8,128)S(1)} %add.15), channel_id=1, source_target_pairs={{8,0},{9,1},{10,2},{11,3},{12,4},{13,5},{14,6},{15,7},{0,8},{1,9},... | collective-permute-start | bytes 49160 | tf_op jit(solution)/shard_map/ppermute | solution.py:669
  16.8 15.3 %collective-permute-start.11 = (f32[33,8,512]{2,1,0:T(8,128)S(1)}, f32[33,8,512]{2,1,0:T(8,128)S(1)}, u32[]{:S(2)}, u32[]{:S(2)}) collective-permute-start(f32[33,8,512]{2,1,0:T(8,128)S(1)} %merge.3), channel_id=1, source_target_pairs={{0,2},{1,3},{2,0},{3,1},{4,6},{5,7},{6,4},{7,5},{8,10},{9,11},{10,... | collective-permute-start | bytes 1622024 | tf_op jit(solution)/shard_map/ppermute | solution.py:651
  17.1 18.9 %collective-permute-start.4 = (f32[30,8,512]{2,1,0:T(8,128)S(1)}, f32[30,8,512]{2,1,0:T(8,128)S(1)}, u32[]{:S(2)}, u32[]{:S(2)}) collective-permute-start(f32[30,8,512]{2,1,0:T(8,128)S(1)} %get-tuple-element.55), channel_id=1, source_target_pairs={{2,6},{3,7},{4,0},{5,1},{6,10},{7,11},{8,4},{9,5},{10,14},{11,15},... | collective-permute-start | bytes 1474568 | tf_op jit(solution)/shard_map/ppermute | solution.py:660
  21.1 14.7 %copy-start = (f32[512,512]{1,0:T(8,128)S(1)}, f32[512,512]{1,0:T(8,128)}, u32[]{:S(2)}) copy-start(f32[512,512]{1,0:T(8,128)} %constant.4.clone.ref) | copy-start | bytes 3145732
  21.1 16.3 %collective-permute-start.6 = (f32[30,8,512]{2,1,0:T(8,128)S(1)}, f32[30,8,512]{2,1,0:T(8,128)S(1)}, u32[]{:S(2)}, u32[]{:S(2)}) collective-permute-start(f32[30,8,512]{2,1,0:T(8,128)S(1)} %trim.2), channel_id=1, source_target_pairs={{0,4},{1,5},{4,8},{5,9},{6,2},{7,3},{8,12},{9,13},{10,6},{11,7},{1... | collective-permute-start | bytes 1474568 | tf_op jit(solution)/shard_map/ppermute | solution.py:660
  25.4 19.1 %collective-permute-start.10 = (f32[30,8,512]{2,1,0:T(8,128)S(1)}, f32[30,8,512]{2,1,0:T(8,128)S(1)}, u32[]{:S(2)}, u32[]{:S(2)}) collective-permute-start(f32[30,8,512]{2,1,0:T(8,128)S(1)} %get-tuple-element.71), channel_id=1, source_target_pairs={{2,6},{3,7},{4,0},{5,1},{6,10},{7,11},{8,4},{9,5},{10,14},{11,15},... | collective-permute-start | bytes 1474568 | tf_op jit(solution)/shard_map/ppermute | solution.py:660
  32.1 13.8 %collective-permute-start.12 = (f32[30,8,512]{2,1,0:T(8,128)S(1)}, f32[30,8,512]{2,1,0:T(8,128)S(1)}, u32[]{:S(2)}, u32[]{:S(2)}) collective-permute-start(f32[30,8,512]{2,1,0:T(8,128)S(1)} %trim.3), channel_id=1, source_target_pairs={{0,4},{1,5},{4,8},{5,9},{6,2},{7,3},{8,12},{9,13},{10,6},{11,7},{1... | collective-permute-start | bytes 1474568 | tf_op jit(solution)/shard_map/ppermute | solution.py:660
  42.6 8.2 %collective-permute-start.7 = (f32[8,8,512]{2,1,0:T(8,128)S(1)}, f32[8,8,512]{2,1,0:T(8,128)S(1)}, u32[]{:S(2)}, u32[]{:S(2)}) collective-permute-start(f32[8,8,512]{2,1,0:T(8,128)S(1)} %get-tuple-element.67), channel_id=1, source_target_pairs={{0,1},{1,0},{2,3},{3,2},{4,5},{5,4},{6,7},{7,6},{8,9},{9,8},{10,11... | collective-permute-start | bytes 393224 | tf_op jit(solution)/shard_map/ppermute | solution.py:651
  42.6 8.1 %collective-permute-start.8 = (f32[8,8,512]{2,1,0:T(8,128)S(1)}, f32[8,8,512]{2,1,0:T(8,128)S(1)}, u32[]{:S(2)}, u32[]{:S(2)}) collective-permute-start(f32[8,8,512]{2,1,0:T(8,128)S(1)} %get-tuple-element.68), channel_id=1, source_target_pairs={{0,2},{1,3},{2,0},{3,1},{4,6},{5,7},{6,4},{7,5},{8,10},{9,11},{10,... | collective-permute-start | bytes 393224 | tf_op jit(solution)/shard_map/ppermute | solution.py:651
  42.7 8.2 %collective-permute-start.9 = (f32[8,8,512]{2,1,0:T(8,128)S(1)}, f32[8,8,512]{2,1,0:T(8,128)S(1)}, u32[]{:S(2)}, u32[]{:S(2)}) collective-permute-start(f32[8,8,512]{2,1,0:T(8,128)S(1)} %get-tuple-element.69), channel_id=1, source_target_pairs={{0,3},{1,2},{2,1},{3,0},{4,7},{5,6},{6,5},{7,4},{8,11},{9,10},{10,... | collective-permute-start | bytes 393224 | tf_op jit(solution)/shard_map/ppermute | solution.py:651
  50.9 4.2 %collective-permute-start.16 = (f32[16,512]{1,0:T(8,128)S(1)}, f32[16,512]{1,0:T(8,128)S(1)}, u32[]{:S(2)}, u32[]{:S(2)}) collective-permute-start(f32[16,512]{1,0:T(8,128)S(1)} %get-tuple-element.89), channel_id=1, source_target_pairs={{0,2},{1,3},{2,0},{3,1},{4,6},{5,7},{6,4},{7,5},{8,10},{9,11},{10,... | collective-permute-start | bytes 98312 | tf_op jit(solution)/shard_map/ppermute | solution.py:651
  53.0 3.3 %collective-permute-start.17 = (f32[16,512]{1,0:T(8,128)S(1)}, f32[16,512]{1,0:T(8,128)S(1)}, u32[]{:S(2)}, u32[]{:S(2)}) collective-permute-start(f32[16,512]{1,0:T(8,128)S(1)} %get-tuple-element.89), channel_id=1, source_target_pairs={{0,3},{1,2},{2,1},{3,0},{4,7},{5,6},{6,5},{7,4},{8,11},{9,10},{10,... | collective-permute-start | bytes 98312 | tf_op jit(solution)/shard_map/ppermute | solution.py:651
  53.0 3.3 %collective-permute-start.18 = (f32[16,512]{1,0:T(8,128)S(1)}, f32[16,512]{1,0:T(8,128)S(1)}, u32[]{:S(2)}, u32[]{:S(2)}) collective-permute-start(f32[16,512]{1,0:T(8,128)S(1)} %get-tuple-element.89), channel_id=1, source_target_pairs={{0,1},{1,0},{2,3},{3,2},{4,5},{5,4},{6,7},{7,6},{8,9},{9,8},{10,11... | collective-permute-start | bytes 98312 | tf_op jit(solution)/shard_map/ppermute | solution.py:651
  53.2 6.3 %collective-permute-start.13 = (f32[8,8,512]{2,1,0:T(8,128)S(1)}, f32[8,8,512]{2,1,0:T(8,128)S(1)}, u32[]{:S(2)}, u32[]{:S(2)}) collective-permute-start(f32[8,8,512]{2,1,0:T(8,128)S(1)} %get-tuple-element.84), channel_id=1, source_target_pairs={{0,1},{1,0},{2,3},{3,2},{4,5},{5,4},{6,7},{7,6},{8,9},{9,8},{10,11... | collective-permute-start | bytes 393224 | tf_op jit(solution)/shard_map/ppermute | solution.py:651
  53.5 8.0 %collective-permute-start.14 = (f32[8,8,512]{2,1,0:T(8,128)S(1)}, f32[8,8,512]{2,1,0:T(8,128)S(1)}, u32[]{:S(2)}, u32[]{:S(2)}) collective-permute-start(f32[8,8,512]{2,1,0:T(8,128)S(1)} %get-tuple-element.85), channel_id=1, source_target_pairs={{0,2},{1,3},{2,0},{3,1},{4,6},{5,7},{6,4},{7,5},{8,10},{9,11},{10,... | collective-permute-start | bytes 393224 | tf_op jit(solution)/shard_map/ppermute | solution.py:651
  55.1 6.5 %collective-permute-start.15 = (f32[8,8,512]{2,1,0:T(8,128)S(1)}, f32[8,8,512]{2,1,0:T(8,128)S(1)}, u32[]{:S(2)}, u32[]{:S(2)}) collective-permute-start(f32[8,8,512]{2,1,0:T(8,128)S(1)} %get-tuple-element.86), channel_id=1, source_target_pairs={{0,3},{1,2},{2,1},{3,0},{4,7},{5,6},{6,5},{7,4},{8,11},{9,10},{10,... | collective-permute-start | bytes 393224 | tf_op jit(solution)/shard_map/ppermute | solution.py:651
  56.3 6.3 %collective-permute-start.19 = (f32[1,16,512]{2,1,0:T(8,128)S(1)}, f32[1,16,512]{2,1,0:T(8,128)S(1)}, u32[]{:S(2)}, u32[]{:S(2)}) collective-permute-start(f32[1,16,512]{2,1,0:T(8,128)S(1)} %add_bitcast_fusion.refs_0_), channel_id=1, source_target_pairs={{4,0},{5,1},{6,2},{7,3},{8,4},{9,5},{10,6},{11,7},{12,8},{13,9},{1... | collective-permute-start | bytes 98312 | tf_op jit(solution)/shard_map/ppermute | solution.py:669
  59.2 4.9 %collective-permute-start.20 = (f32[1,16,512]{2,1,0:T(8,128)S(1)}, f32[1,16,512]{2,1,0:T(8,128)S(1)}, u32[]{:S(2)}, u32[]{:S(2)}) collective-permute-start(f32[1,16,512]{2,1,0:T(8,128)S(1)} %add_bitcast_fusion.refs_0_), channel_id=1, source_target_pairs={{8,0},{9,1},{10,2},{11,3},{12,4},{13,5},{14,6},{15,7},{0,8},{1,9},... | collective-permute-start | bytes 98312 | tf_op jit(solution)/shard_map/ppermute | solution.py:669
  59.4 5.7 %collective-permute-start.21 = (f32[1,16,512]{2,1,0:T(8,128)S(1)}, f32[1,16,512]{2,1,0:T(8,128)S(1)}, u32[]{:S(2)}, u32[]{:S(2)}) collective-permute-start(f32[1,16,512]{2,1,0:T(8,128)S(1)} %add_bitcast_fusion.refs_0_), channel_id=1, source_target_pairs={{12,0},{13,1},{14,2},{15,3},{0,4},{1,5},{2,6},{3,7},{4,8},{5,9},{6... | collective-permute-start | bytes 98312 | tf_op jit(solution)/shard_map/ppermute | solution.py:669
  61.6 3.6 %copy-start.1 = (f32[16,32,64]{2,1,0:T(8,128)S(1)}, f32[16,32,64]{2,1,0:T(8,128)}, u32[]{:S(2)}) copy-start(f32[16,32,64]{2,1,0:T(8,128)} %constant.5.clone.refs_4_) | copy-start | bytes 393220
